TPU v7x, 32 devices: a whole 2x2x4 slice. The times are simulated.
32 devices in a mesh: scen: 8 (over z, core), row: 4 (over y, x).
Axes of the slice: x: 2, y: 2, z: 4, core: 2. Of those that a mesh axis runs over, the one named last changes fastest.
Arguments:
- coupling: bfloat16 [8, 1536, 4096], P('scen', None, 'row'), may hold values from -40 to 40
- solves: bfloat16 [8, 1536, 512], P('scen', 'row'), may hold values from -1.25 to 1.25
- border_diagonal: float32 [1024, 4], P('scen', 'row'), may hold values from 32 to 64
- panel_rows: int32 [512], replicated, may hold values from 0 to 4095, as said below
Outputs:
- first_factor: float32 [1024, 4, 256], P('scen', 'row')
- second_factor: float32 [1024, 4, 256], P('scen', 'row')
Inputs may be any that keep to these rules, and one draw needn't show every extreme that they name: `panel_rows`: 512 distinct border rows; the first 256 are the first panel's pivot rows and columns, the rest the second's.
All inputs are finite; a program needn't handle non-finite values. Where the computation divides by a largest or mean magnitude, that divisor is 1e-20 or more.
Results may differ from a plain program's by a relative error of at most 0.0003.
Values may be sent and summed in bfloat16 or wider, within the bound.
No kernel may reach another device: no remote copies, remote signals or barrier semaphores. Data moves between devices by JAX's collectives and lax.ppermute only.
A program may use at most 64 MiB of HBM per device.

v0:
```python
import jax
import jax.numpy as jnp
from jax import lax
from jax.sharding import PartitionSpec as P

HALF = 256
NEWTON = 8


def pick_rows(local, panel_rows, base):
    offset = panel_rows - base
    owned = (offset >= 0) & (offset < local.shape[0])
    taken = jnp.take(local, jnp.clip(offset, 0, local.shape[0] - 1), axis=0)
    return jnp.where(owned[:, None], taken, jnp.float32(0.0))


def newton_start(pivot):
    norm_one = jnp.max(jnp.sum(jnp.abs(pivot), axis=0))
    norm_inf = jnp.max(jnp.sum(jnp.abs(pivot), axis=1))
    return pivot.T / (norm_one * norm_inf)


def invert(pivot):
    start_guess = newton_start(pivot)
    approx = start_guess
    for step in range(NEWTON):
        left = jnp.dot(approx, pivot, precision=lax.Precision.HIGHEST)
        approx = 2.0 * approx - jnp.dot(left, approx, precision=lax.Precision.HIGHEST)
    return approx


def shards(coupling, solves, border_diagonal, panel_rows):
    half_cols = HALF
    full_solves = lax.all_gather(solves, "row", axis=1, tiled=True)
    row_count = coupling.shape[2]
    share = row_count // lax.axis_size("scen")
    base = lax.axis_index("row") * row_count + lax.axis_index("scen") * share
    glob = base + jnp.arange(share, dtype=jnp.int32)
    diag_part = jnp.where(
        glob[:, None] == panel_rows[None, :], border_diagonal[:, 0][:, None], jnp.float32(0.0)
    )
    both = (
        lax.psum_scatter(
            jnp.einsum("snr,snc->rc", coupling, full_solves, preferred_element_type=jnp.float32),
            "scen",
            scatter_dimension=0,
            tiled=True,
        )
        + diag_part
    )
    pivots = lax.psum(pick_rows(both, panel_rows, base), ("scen", "row"))
    first = both[:, :half_cols]
    second = both[:, half_cols:]
    pivots_first = pivots[:, :half_cols]
    pivots_second = pivots[:, half_cols:]
    inverse_first = invert(pivots_first[:half_cols])
    first_factor = jnp.dot(first, inverse_first, precision=lax.Precision.HIGHEST)
    upper = pivots_second[:half_cols]
    updated = second - jnp.dot(first_factor, upper, precision=lax.Precision.HIGHEST)
    lower_factor = jnp.dot(pivots_first[half_cols:], inverse_first, precision=lax.Precision.HIGHEST)
    pivot_two = pivots_second[half_cols:] - jnp.dot(
        lower_factor, upper, precision=lax.Precision.HIGHEST
    )
    inverse_second = invert(pivot_two)
    second_factor = jnp.dot(updated, inverse_second, precision=lax.Precision.HIGHEST)
    return (first_factor[:, None, :], second_factor[:, None, :])


def solution(mesh):
    placed = (P("scen", None, "row"), P("scen", "row", None), P("scen", "row"), P())
    return jax.shard_map(
        shards,
        mesh=mesh,
        in_specs=placed,
        out_specs=(P("scen", "row", None), P("scen", "row", None)),
        check_vma=False,
    )
```

profile of v0, /device:TPU:0, one launch (start us, length us, event | category | flops | bytes accessed | tf_op | source)
XLA Modules:
  0.0 256.6 jit_solution(12977961193365737765)
XLA Ops:
  7.2 0.0 copy-start
  7.2 0.0 all-gather.2.cloned.1.call-start
  7.2 0.7 all-gather.2.cloned.1.call-update
  7.9 0.0 reduce-scatter.2.cloned.1.call-start
  8.0 35.6 %all-gather.2.cloned.1.call-done = bf16[1,1536,512]{2,1,0:T(8,128)(2,1)} async-done(((bf16[1,384,512]{2,1,0:T(8,128)(2,1)}), bf16[1,1536,512]{2,1,0:T(8,128)(2,1)}) %all-gather.2.cloned.1.call-update) | async-done | bytes 1572880 | tf_op jit(solution)/shard_map/all_gather | solution.py:34
  43.6 0.0 copy-done
  43.6 4.6 %fusion = f32[1024,512]{1,0:T(8,128)} fusion(bf16[1,1536,1024]{2,1,0:T(8,128)(2,1)S(1)} %copy-done, bf16[1,1536,512]{2,1,0:T(8,128)(2,1)} %all-gather.2.cloned.1.call-done), kind=kOutput, calls=%fused_computation.1 | convolution fusion | flops 1610612736 | bytes 6815744 | tf_op jit(solution)/shard_map/snr,snc->rc/dot_general | solution.py:44
  48.1 0.0 reduce-scatter.2.cloned.1.call-update
  48.2 0.0 all-reduce.2.cloned.1.call-start
  48.2 0.6 copy-done.3
  48.9 35.3 %reduce-scatter.2.cloned.1.call-done = f32[128,512]{1,0:T(8,128)} async-done(((f32[1024,512]{1,0:T(8,128)}), f32[128,512]{1,0:T(8,128)}) %reduce-scatter.2.cloned.1.call-update) | async-done | bytes 262160 | tf_op jit(solution)/shard_map/reduce_scatter | solution.py:43
  84.2 0.0 copy-done.4
  84.2 1.1 select_add_fusion
  85.2 2.3 gather_fusion
  87.6 2.6 %copy.6 = f32[512,512]{0,1:T(8,128)} copy(f32[512,512]{1,0:T(8,128)} %gather_fusion) | data formatting | bytes 2097152 | tf_op jit(solution)/shard_map/jit(_take)/gather | solution.py:13
  90.2 2.4 select_select_fusion
  92.6 0.0 all-reduce.2.cloned.1.call-update
  92.6 128.7 %all-reduce.2.cloned.1.call-done = f32[512,512]{0,1:T(8,128)} async-done(((f32[512,512]{0,1:T(8,128)}), f32[512,512]{0,1:T(8,128)}) %all-reduce.2.cloned.1.call-update) | async-done | bytes 1048592 | tf_op jit(solution)/shard_map/psum | solution.py:51
  221.3 1.1 abs_reduce_fusion.2
  222.3 0.6 reduce_max.36
  223.0 0.6 reduce_max.37
  224.9 0.0 copy-start.2
  224.9 1.5 fusion.10
  226.4 1.4 convolution_subtract_fusion.16
  227.8 0.0 copy-done.2
  227.8 0.4 fusion.31
  228.3 0.4 convolution_subtract_fusion.15
  228.6 0.4 fusion.29
  229.1 0.4 convolution_subtract_fusion.14
  229.5 0.4 fusion.27
  229.9 0.4 convolution_subtract_fusion.13
  230.3 0.4 fusion.25
  230.7 0.4 convolution_subtract_fusion.12
  231.1 0.4 fusion.23
  231.5 0.4 convolution_subtract_fusion.11
  231.9 0.4 fusion.21
  232.3 0.4 convolution_subtract_fusion.10
  232.7 0.4 fusion.19
  233.1 0.4 convolution_subtract_fusion.9
  233.5 0.3 fusion.13
  233.8 0.8 copy.10
  234.6 0.6 fusion.3
  235.2 1.1 abs_reduce_fusion
  236.3 0.6 reduce_max.38
  236.9 0.6 reduce_max.39
  238.8 1.5 fusion.7
  240.3 1.4 convolution_subtract_fusion.7
  241.8 0.4 fusion.35
  242.2 0.4 convolution_subtract_fusion.6
  242.6 0.4 fusion.36
  243.0 0.4 convolution_subtract_fusion.5
  243.4 0.4 fusion.37
  243.8 0.4 convolution_subtract_fusion.4
  244.2 0.4 fusion.38
  244.6 0.4 convolution_subtract_fusion.3
  245.0 0.6 fusion.39
  245.6 0.4 convolution_subtract_fusion.2
  246.0 0.4 fusion.40
  246.4 0.4 convolution_subtract_fusion.1
  246.8 0.4 fusion.41
  247.2 0.4 convolution_subtract_fusion
  247.6 1.3 convolution_subtract_fusion.17
  249.0 0.3 convolution_bitcast_fusion
  249.3 0.8 copy.11
  (7 shorter events, 0.0 us)
Async XLA Ops:
  7.2 36.4 %copy-start = (bf16[1,1536,1024]{2,1,0:T(8,128)(2,1)S(1)}, bf16[1,1536,1024]{2,1,0:T(8,128)(2,1)}, u32[]{:S(2)}) copy-start(bf16[1,1536,1024]{2,1,0:T(8,128)(2,1)} %param.4) | copy-start | bytes 9437188
  7.2 36.4 %all-gather.2.cloned.1.call-start = ((), (), s32[]{:S(2)}) async-start(), calls=%async_computation.1 | async-start | bytes 1966080 | tf_op jit(solution)/shard_map/all_gather | solution.py:34
  7.9 76.2 %reduce-scatter.2.cloned.1.call-start = ((), (), s32[]{:S(2)}) async-start(), calls=%async_computation.2 | async-start | bytes 2359296 | tf_op jit(solution)/shard_map/reduce_scatter | solution.py:43
  48.1 0.7 copy-start.3
  48.1 36.0 %copy-start.4 = (f32[128,1]{0,1:T(1,128)S(1)}, f32[128,1]{0,1:T(1,128)}, u32[]{:S(2)}) copy-start(f32[128,1]{0,1:T(1,128)} %param.6) | copy-start | bytes 1540
  48.2 173.1 %all-reduce.2.cloned.1.call-start = ((), (), s32[]{:S(2)}) async-start(), calls=%async_computation.3 | async-start | bytes 2097152 | tf_op jit(solution)/shard_map/psum | solution.py:51
  224.9 3.0 %copy-start.2 = (f32[512,512]{0,1:T(8,128)S(1)}, f32[512,512]{0,1:T(8,128)}, u32[]{:S(2)}) copy-start(f32[512,512]{0,1:T(8,128)} %all-reduce.2.cloned.1.call-done) | copy-start | bytes 3145732
  238.8 2.9 %copy-start.1 = (f32[256,256]{0,1:T(8,128)S(1)}, f32[256,256]{0,1:T(8,128)}, u32[]{:S(2)}) copy-start(f32[256,256]{0,1:T(8,128)} %get-tuple-element.11) | copy-start | bytes 786436
Sparse Core Ops, SparseCore 0:
  9.9 33.6 all-gather.1
  48.3 35.8 reduce-scatter.1
  92.7 128.5 all-reduce.1
where the time goes:
time: 257 us
  waiting for transfers between devices  200 us (78%)
  matrix products  25.4 us (10%)
  between operations  16.7 us (6%)
  local copies, waits for them, and re-layouts  7.13 us (3%)
  other arithmetic  6.97 us (3%)
    psum x1, waiting for transfers between devices, shards(): pivots = lax.psum(pick_rows(both, panel_rows, base), ('scen', 'row'))  129 us
    all_gather x1, waiting for transfers between devices, shards(): full_solves = lax.all_gather(solves, 'row', axis=1, tiled=True)  35.6 us
    reduce_scatter x1, waiting for transfers between devices, shards(): lax.psum_scatter(jnp.einsum('snr,snc->rc', coupling, full_solves, preferr...  35.3 us
    dot_general x16, matrix products, invert(): left = jnp.dot(approx, pivot, precision=lax.Precision.HIGHEST)  8.99 us
    dot_general x16, matrix products, invert(): jnp.dot(left, approx, precision=lax.Precision.HIGHEST)  8.16 us
  transfers between devices with their start and end apart: 3, of which 3 were waited for; matrix products, arithmetic and copies ran while one was open for 0% of the time, Pallas kernels for 0%

commit v1 on v0

v1 whole, which is shorter than its diff:
```python
import functools

import jax
import jax.numpy as jnp
from jax import lax
from jax.experimental import pallas as pl
from jax.experimental.pallas import tpu as pltpu
from jax.sharding import PartitionSpec as P

HALF = 256
NEWTON = 8
BOTH = ("scen", "row")
F32 = jnp.float32
BF16 = jnp.bfloat16


def halves(a):
    high = a.astype(BF16)
    low = (a - high.astype(F32)).astype(BF16)
    return high, low


def left_of(a):
    high, low = halves(a)
    return jnp.concatenate([high, high, low], axis=1)


def right_of(b):
    high, low = halves(b)
    return jnp.concatenate([high, low, high], axis=0)


def dot(a, b):
    return jnp.dot(a, b, preferred_element_type=F32)


def product(a, b):
    return dot(left_of(a), right_of(b))


def newton(pivot):
    size = jnp.abs(pivot)
    norm_one = jnp.max(jnp.sum(size, axis=0, keepdims=True))
    norm_inf = jnp.max(jnp.sum(size, axis=1, keepdims=True))
    approx = pivot.T / (norm_one * norm_inf)
    pivot_right = right_of(pivot)
    for step in range(NEWTON):
        left = dot(left_of(approx), pivot_right)
        approx = 2.0 * approx - product(left, approx)
    return approx


def first_kernel(pivot_ref, inverse_ref):
    inverse_ref[...] = newton(pivot_ref[...])


def second_kernel(inverse_first_ref, upper_ref, lower_ref, corner_ref, inverse_ref):
    lower_factor = product(lower_ref[...], inverse_first_ref[...])
    inverse_ref[...] = newton(corner_ref[...] - product(lower_factor, upper_ref[...]))


def factor_kernel(first_ref, second_ref, inverse_first_ref, inverse_second_ref, upper_ref, first_out, second_out):
    first_factor = product(first_ref[...], inverse_first_ref[...])
    updated = second_ref[...] - product(first_factor, upper_ref[...])
    first_out[...] = first_factor[:, None, :]
    second_out[...] = product(updated, inverse_second_ref[...])[:, None, :]


def in_vmem(kernel, out_shape, flops, *args):
    spec = pl.BlockSpec(memory_space=pltpu.VMEM)
    return pl.pallas_call(
        kernel,
        out_shape=out_shape,
        in_specs=[spec] * len(args),
        out_specs=jax.tree.map(lambda _: spec, out_shape),
        compiler_params=pltpu.CompilerParams(vmem_limit_bytes=24 * 1024 * 1024),
        cost_estimate=pl.CostEstimate(flops=flops, bytes_accessed=1 << 20, transcendentals=0),
    )(*args)


def swap(x, axis, bit):
    count = lax.axis_size(axis)
    return lax.ppermute(x, axis, [(i, i ^ bit) for i in range(count)])


def gather_rows(block, flip):
    count = lax.axis_size("row")
    bits = [1 << i for i in range(count.bit_length() - 1)]
    held = {0: block}
    for bit in reversed(bits) if flip else bits:
        keys = sorted(held)
        sent = held[keys[0]] if len(keys) == 1 else jnp.concatenate([held[k] for k in keys], axis=0)
        got = jnp.split(swap(sent, "row", bit), len(keys), axis=0)
        held.update({k ^ bit: piece for k, piece in zip(keys, got)})
    return jnp.concatenate([held[k] for k in range(count)], axis=0)


def exchange_sum(x, axis, step=1):
    count = x.shape[0]
    place = lax.axis_index(axis) // step
    total = lax.dynamic_index_in_dim(x, place, 0, keepdims=False)
    for k in range(1, count):
        total = total + swap(lax.dynamic_index_in_dim(x, place ^ k, 0, keepdims=False), axis, k * step)
    return total


def exchange_gather(piece, axis, count, step=1):
    place = lax.axis_index(axis) // step
    out = jnp.zeros((count,) + piece.shape, piece.dtype)
    out = lax.dynamic_update_index_in_dim(out, piece, place, 0)
    for k in range(1, count):
        out = lax.dynamic_update_index_in_dim(out, swap(piece, axis, k * step), place ^ k, 0)
    return out


def sum_at_once(x):
    devices = lax.axis_size("scen") * lax.axis_size("row")
    rows = x.shape[0]
    if rows % (8 * devices):
        return lax.psum(x, BOTH)
    pieces = x.reshape(devices, rows // devices, -1)
    own = jnp.sum(lax.all_to_all(pieces, BOTH, 0, 0, tiled=True), axis=0)
    everyone = jnp.broadcast_to(own[None], (devices,) + own.shape)
    return lax.all_to_all(everyone, BOTH, 0, 0, tiled=True).reshape(x.shape)


def sum_in_stages(x):
    scen, row = lax.axis_size("scen"), lax.axis_size("row")
    rows = x.shape[0]
    if rows % (8 * scen * row):
        return lax.psum(x, BOTH)
    core = lax.axis_index("scen") % 2
    pair = x.reshape(2, rows // 2, -1)
    part = lax.dynamic_index_in_dim(pair, core, 0, keepdims=False)
    part = part + swap(lax.dynamic_index_in_dim(pair, 1 - core, 0, keepdims=False), "scen", 1)
    part = exchange_sum(part.reshape(row, part.shape[0] // row, -1), "row")
    layers = scen // 2
    part = exchange_sum(part.reshape(layers, part.shape[0] // layers, -1), "scen", 2)
    part = exchange_gather(part, "scen", layers, 2).reshape(-1, x.shape[1])
    part = exchange_gather(part, "row", row).reshape(-1, x.shape[1])
    other = swap(part, "scen", 1)
    return jnp.where(core == 0, jnp.concatenate([part, other]), jnp.concatenate([other, part]))


def scatter_sum(x):
    scen = lax.axis_size("scen")
    layers = scen // 2
    place = lax.axis_index("scen")
    layer, core = place // 2, place % 2
    pieces = x.reshape(layers, 2, x.shape[0] // scen, -1)
    mine = lax.dynamic_index_in_dim(pieces, core, 1, keepdims=False)
    theirs = lax.dynamic_index_in_dim(pieces, 1 - core, 1, keepdims=False)
    mine = mine + swap(theirs, "scen", 1)
    total = lax.dynamic_index_in_dim(mine, layer, 0, keepdims=False)
    for way in (1, -1):
        carried = None
        for step in range(1, layers):
            index = jnp.clip(layer + way * (layers - step), 0, layers - 1)
            sent = lax.dynamic_index_in_dim(mine, index, 0, keepdims=False)
            if carried is not None:
                sent = sent + carried
            senders = range(step) if way == 1 else range(layers - step, layers)
            pairs = [(2 * i + c, 2 * (i + way) + c) for i in senders for c in range(2)]
            carried = lax.ppermute(sent, "scen", pairs)
        total = total + carried
    return total


def shards(coupling, solves, border_diagonal, panel_rows):
    half = HALF
    coupling, solves = coupling[0], solves[0]
    local, row_count = coupling.shape
    block = solves.shape[0]
    panel = solves.shape[1]
    scen, rows = lax.axis_size("scen"), lax.axis_size("row")
    row = lax.axis_index("row")
    share = row_count // scen
    base = row * row_count + lax.axis_index("scen") * share
    quarter = half // 2

    gathered = [gather_rows(solves[:, i * quarter:(i + 1) * quarter], i % 2 == 1) for i in range(panel // quarter)]
    solves_first = jnp.concatenate(gathered[:2], axis=1)
    solves_second = jnp.concatenate(gathered[2:], axis=1)

    coupling_t = jnp.concatenate(
        [lax.dynamic_slice_in_dim(coupling, (row ^ k) * block, block, 0) for k in range(rows)], axis=0
    ).T
    columns = row * row_count + jnp.arange(row_count, dtype=jnp.int32)
    chosen = (panel_rows[:, None] == columns[None, :]).astype(BF16)
    picked = dot(chosen, coupling_t).astype(BF16)

    glob = base + jnp.arange(share, dtype=jnp.int32)
    at_diagonal = panel_rows[:, None] == glob[None, :]
    diagonal = jnp.sum(jnp.where(at_diagonal, border_diagonal[:, 0][None, :], F32(0.0)), axis=1)
    on_diagonal = jnp.where(jnp.eye(panel, dtype=bool), diagonal[:, None], F32(0.0))

    pivots_left = dot(picked, solves_first) + on_diagonal[:, :half]
    pivot_first = sum_at_once(pivots_left[:half])
    lower = sum_in_stages(pivots_left[half:])
    right = sum_in_stages(dot(picked, solves_second) + on_diagonal[:, half:])
    upper, corner = right[:half], right[half:]

    diag_part = jnp.where(at_diagonal.T, border_diagonal[:, 0][:, None], F32(0.0))
    first = scatter_sum(dot(coupling_t, solves_first)) + diag_part[:, :half]
    second = scatter_sum(dot(coupling_t, solves_second)) + diag_part[:, half:]

    square = jax.ShapeDtypeStruct((half, half), F32)
    inverse_first = in_vmem(first_kernel, square, 2 * 16 * 3 * half**3, pivot_first)
    inverse_second = in_vmem(second_kernel, square, 2 * 18 * 3 * half**3, inverse_first, upper, lower, corner)
    out = jax.ShapeDtypeStruct((share, 1, half), F32)
    return in_vmem(
        factor_kernel, (out, out), 2 * 9 * share * half**2, first, second, inverse_first, inverse_second, upper
    )


def solution(mesh):
    placed = (P("scen", None, "row"), P("scen", "row", None), P("scen", "row"), P())
    return jax.shard_map(
        shards,
        mesh=mesh,
        in_specs=placed,
        out_specs=(P("scen", "row", None), P("scen", "row", None)),
        check_vma=False,
    )
```

time: 257 us -> 142 us (0.55)
  waiting for transfers between devices: 200 us -> 23 us
  starting transfers between devices: 0.12 us -> 77.2 us
  between operations: 16.7 us -> 1.61 us
  matrix products: 25.4 us -> 11 us
  Pallas kernels: 0 us -> 10.5 us
    psum x1 -> x0, waiting for transfers between devices: 129 us -> none  [shards(): pivots = lax.psum(pick_rows(both, panel_rows, base), ('scen', 'row'))]
    ppermute x0 -> x50, starting transfers between devices: none -> 68.8 us  [the longest x38 43.3 us: swap(): return lax.ppermute(x, axis, [(i, i ^ bit) for i in range(count)])]
    all_gather x1 -> x0, waiting for transfers between devices: 35.6 us -> none  [shards(): full_solves = lax.all_gather(solves, 'row', axis=1, tiled=True)]
    reduce_scatter x1 -> x0, waiting for transfers between devices: 35.3 us -> none  [shards(): lax.psum_scatter(jnp.einsum('snr,snc->rc', coupling, full_solves, preferr...]
    ppermute x0 -> x50, waiting for transfers between devices: none -> 23 us  [the longest x38 23 us: swap(): return lax.ppermute(x, axis, [(i, i ^ bit) for i in range(count)])]
    dot_general x38 -> x5, matrix products: 25.4 us -> 11 us  [dot(): return jnp.dot(a, b, preferred_element_type=F32)]
    pallas_call x0 -> x3, Pallas kernels: none -> 10.5 us  [in_vmem(): pl.pallas_call(kernel, out_shape=out_shape, in_specs=[spec] * len(args),...]
    all_to_all x0 -> x2, starting transfers between devices: none -> 8.45 us  [the longest x1 5.6 us: sum_at_once(): own = jnp.sum(lax.all_to_all(pieces, BOTH, 0, 0, tiled=True), axis=0)]
  transfers between devices with their start and end apart: 3 -> 52, of which waited for: 3 -> 15; matrix products, arithmetic and copies ran while one was open for 0% -> 18% of each run, Pallas kernels for 0% -> 7%
where the time goes in v1:
time: 142 us; the launch traced here: 140 us
  starting transfers between devices  77.2 us (54%)
  waiting for transfers between devices  23 us (16%)
  matrix products  11 us (8%)
  Pallas kernels  10.5 us (7%)
  other arithmetic  8.43 us (6%)
  local copies, waits for them, and re-layouts  8.05 us (6%)
  between operations  1.61 us (1%)
    ppermute x38, starting transfers between devices, swap(): return lax.ppermute(x, axis, [(i, i ^ bit) for i in range(count)])  43.3 us
    ppermute x12, starting transfers between devices, scatter_sum(): carried = lax.ppermute(sent, 'scen', pairs)  25.4 us
    ppermute x38, waiting for transfers between devices, swap(): return lax.ppermute(x, axis, [(i, i ^ bit) for i in range(count)])  23 us
    dot_general x5, matrix products, dot(): return jnp.dot(a, b, preferred_element_type=F32)  11 us
    pallas_call x3, Pallas kernels, in_vmem(): pl.pallas_call(kernel, out_shape=out_shape, in_specs=[spec] * len(args),...  10.5 us
    all_to_all x1, starting transfers between devices, sum_at_once(): own = jnp.sum(lax.all_to_all(pieces, BOTH, 0, 0, tiled=True), axis=0)  5.6 us
    all_to_all x1, starting transfers between devices, sum_at_once(): return lax.all_to_all(everyone, BOTH, 0, 0, tiled=True).reshape(x.shape)  2.85 us
  transfers between devices with their start and end apart: 52, of which 15 were waited for; matrix products, arithmetic and copies ran while one was open for 18% of the time, Pallas kernels for 7%

profile of v1, /device:TPU:0, one launch (start us, length us, event | category | flops | bytes accessed | tf_op | source)
XLA Modules:
  0.0 139.7 jit_solution(10872817315447486335)
XLA Ops:
  0.6 1.1 fusion.26
  1.7 3.0 %collective-permute-start.13 = (bf16[384,128]{1,0:T(8,128)(2,1)S(1)}, bf16[384,128]{1,0:T(8,128)(2,1)S(1)}, u32[]{:S(2)}, u32[]{:S(2)}) collective-permute-start(bf16[384,128]{1,0:T(8,128)(2,1)S(1)} %get-tuple-element.23), channel_id=1, source_target_pairs={{0,2},{1,3},{2,0},{3,1},{4,6},{5,7},{6,4},{7,5},{8,10},{9,11},{10,... | collective-permute-start | bytes 294920 | tf_op jit(solution)/shard_map/ppermute | solution.py:83
  4.8 1.5 %collective-permute-start.11 = (bf16[384,128]{1,0:T(8,128)(2,1)S(1)}, bf16[384,128]{1,0:T(8,128)(2,1)}, u32[]{:S(2)}, u32[]{:S(2)}) collective-permute-start(bf16[384,128]{1,0:T(8,128)(2,1)S(1)} %get-tuple-element.22), channel_id=1, source_target_pairs={{0,1},{1,0},{2,3},{3,2},{4,5},{5,4},{6,7},{7,6},{8,9},{9,8},{10,11... | collective-permute-start | bytes 294920 | tf_op jit(solution)/shard_map/ppermute | solution.py:83
  6.9 0.9 select_reduce_fusion
  8.0 2.2 %dynamic-slice_bitcast_fusion.3 = (bf16[384,1024]{1,0:T(8,128)(2,1)S(1)}, bf16[384,1024]{1,0:T(8,128)(2,1)S(1)}, bf16[384,1024]{1,0:T(8,128)(2,1)S(1)}, bf16[384,1024]{1,0:T(8,128)(2,1)S(1)}) fusion(bf16[1,1536,1024]{2,1,0:T(8,128)(2,1)} %param.4, s32[]{:T(128)S(6)} %select_n.152, s32[]{:T(128)S(6)} %select_n.153, s32[]{:T(128)S(6)} %select_n.155, ...), kind=kLoop, calls=%fused_computation.14 | loop fusion | bytes 6291472 | tf_op jit(solution)/shard_map/dynamic_slice | solution.py:186
  10.3 3.0 %convolution_convert_fusion = bf16[512,1536]{1,0:T(8,128)(2,1)} fusion(s32[1024]{0:T(1024)S(1)} %iota_add_fusion, s32[512]{0:T(512)S(1)} %copy-done.15, bf16[384,1024]{1,0:T(8,128)(2,1)S(1)} %get-tuple-element.8, bf16[384,1024]{1,0:T(8,128)(2,1)S(1)} %get-tuple-element.9, bf16[384,1024]{1,0:T(8,128)(2,1)S(1)} %get-tuple-element.7, ...), kind=kOutput, calls=%fused_computation.1 | convolution fusion | flops 1624506368 | bytes 4724736 | tf_op jit(solution)/shard_map/dot_general | solution.py:34
  13.6 2.0 %collective-permute-start.14 = (bf16[768,128]{1,0:T(8,128)(2,1)S(1)}, bf16[768,128]{1,0:T(8,128)(2,1)S(1)}, u32[]{:S(2)}, u32[]{:S(2)}) collective-permute-start(bf16[768,128]{1,0:T(8,128)(2,1)S(1)} %pad_maximum_fusion.4), channel_id=1, source_target_pairs={{0,1},{1,0},{2,3},{3,2},{4,5},{5,4},{6,7},{7,6},{8,9},{9,8},{10,11... | collective-permute-start | bytes 589832 | tf_op jit(solution)/shard_map/ppermute | solution.py:83
  15.5 0.9 pad_maximum_fusion.3
  16.5 1.6 %collective-permute-start.12 = (bf16[768,128]{1,0:T(8,128)(2,1)S(1)}, bf16[768,128]{1,0:T(8,128)(2,1)S(1)}, u32[]{:S(2)}, u32[]{:S(2)}) collective-permute-start(bf16[768,128]{1,0:T(8,128)(2,1)S(1)} %pad_maximum_fusion.3), channel_id=1, source_target_pairs={{0,2},{1,3},{2,0},{3,1},{4,6},{5,7},{6,4},{7,5},{8,10},{9,11},{10,... | collective-permute-start | bytes 589832 | tf_op jit(solution)/shard_map/ppermute | solution.py:83
  18.0 0.9 pad_maximum_fusion.2
  19.6 0.9 pad_maximum_fusion.1
  20.8 2.4 %collective-permute-done.12 = bf16[768,128]{1,0:T(8,128)(2,1)S(1)} collective-permute-done((bf16[768,128]{1,0:T(8,128)(2,1)S(1)}, bf16[768,128]{1,0:T(8,128)(2,1)S(1)}, u32[]{:S(2)}, u32[]{:S(2)}) %collective-permute-start.12) | collective-permute-done | bytes 196640 | tf_op jit(solution)/shard_map/ppermute | solution.py:83
  23.3 2.3 %fusion.20 = f32[1024,256]{1,0:T(8,128)S(1)} fusion(bf16[384,128]{1,0:T(8,128)(2,1)S(1)} %get-tuple-element.32, bf16[384,128]{1,0:T(8,128)(2,1)} %copy-done.11, bf16[384,128]{1,0:T(8,128)(2,1)S(1)} %get-tuple-element.31, bf16[384,128]{1,0:T(8,128)(2,1)S(1)} %get-tuple-element.23, bf16[768,128]{1,0:T(8,128)(2,1)S(1)} %collective-permute-done.12, ...), kind=kOutput, calls=%fused_computation.98 | convolution fusion | flops 823394304 | bytes 4980736 | tf_op jit(solution)/shard_map/dot_general | solution.py:34
  25.6 0.8 dynamic-slice_bitcast_fusion.4
  26.5 1.6 %convolution_add_fusion.1 = f32[512,256]{1,0:T(8,128)S(1)} fusion(bf16[512,1536]{1,0:T(8,128)(2,1)S(1)} %copy-done.18, f32[512,512]{1,0:T(8,128)S(1)} %fusion.3, bf16[384,128]{1,0:T(8,128)(2,1)S(1)} %get-tuple-element.34, bf16[384,128]{1,0:T(8,128)(2,1)} %collective-permute-done.2, bf16[384,128]{1,0:T(8,128)(2,1)S(1)} %get-tuple-element.33, ...), kind=kOutput, calls=%fused_computation.4 | convolution fusion | flops 408289280 | bytes 3407872 | tf_op jit(solution)/shard_map/dot_general | solution.py:34
  29.5 2.0 %fusion.21 = f32[1024,256]{1,0:T(8,128)S(1)} fusion(bf16[384,128]{1,0:T(8,128)(2,1)S(1)} %get-tuple-element.34, bf16[384,128]{1,0:T(8,128)(2,1)} %collective-permute-done.2, bf16[384,128]{1,0:T(8,128)(2,1)S(1)} %get-tuple-element.33, bf16[384,128]{1,0:T(8,128)(2,1)S(1)} %get-tuple-element.24, bf16[768,128]{1,0:T(8,128)(2,1)S(1)} %collective-permute-done.1, ...), kind=kOutput, calls=%fused_computation.99 | convolution fusion | flops 823394304 | bytes 4980736 | tf_op jit(solution)/shard_map/dot_general | solution.py:34
  32.2 1.7 %collective-permute-start.39 = (f32[32,256]{1,0:T(8,128)}, f32[32,256]{1,0:T(8,128)S(1)}, u32[]{:S(2)}, u32[]{:S(2)}) collective-permute-start(f32[32,256]{1,0:T(8,128)} %get-tuple-element.36), channel_id=1, source_target_pairs={{0,3},{1,2},{2,1},{3,0},{4,7},{5,6},{6,5},{7,4},{8,11},{9,10},{10,... | collective-permute-start | bytes 98312 | tf_op jit(solution)/shard_map/ppermute | solution.py:83
  33.8 0.8 collective-permute-start.38
  34.6 1.5 %collective-permute-start.37 = (f32[32,256]{1,0:T(8,128)}, f32[32,256]{1,0:T(8,128)}, u32[]{:S(2)}, u32[]{:S(2)}) collective-permute-start(f32[32,256]{1,0:T(8,128)} %get-tuple-element.35), channel_id=1, source_target_pairs={{0,1},{1,0},{2,3},{3,2},{4,5},{5,4},{6,7},{7,6},{8,9},{9,8},{10,11... | collective-permute-start | bytes 98312 | tf_op jit(solution)/shard_map/ppermute | solution.py:83
  36.1 0.8 dynamic-slice_bitcast_fusion.5
  36.9 5.6 %all-to-all-start = ((f32[32,8,256]{2,1,0:T(8,128)}), f32[32,8,256]{2,1,0:T(8,128)S(1)}, u32[]{:S(2)}, u32[]{:S(2)}) async-start(f32[32,8,256]{2,1,0:T(8,128)} %get-tuple-element.13), calls=%async_computation | async-start | bytes 524288 | tf_op jit(solution)/shard_map/all_to_all | solution.py:122
  43.2 0.8 fusion.10
  44.0 3.7 %collective-permute-start.42 = (f32[8,256]{1,0:T(8,128)S(1)}, f32[8,256]{1,0:T(8,128)S(1)}, u32[]{:S(2)}, u32[]{:S(2)}) collective-permute-start(f32[8,256]{1,0:T(8,128)S(1)} %get-tuple-element.42), channel_id=1, source_target_pairs={{0,24},{4,28},{8,16},{12,20},{16,8},{20,12},{24,0},{28,4},{1,25},{... | collective-permute-start | bytes 24584 | tf_op jit(solution)/shard_map/ppermute | solution.py:83
  47.7 0.8 collective-permute-start.40
  48.4 2.1 %convolution_add_fusion = f32[512,256]{1,0:T(8,128)S(1)} fusion(bf16[512,1536]{1,0:T(8,128)(2,1)} %convolution_convert_fusion, f32[512,512]{1,0:T(8,128)S(1)} %fusion.3, bf16[384,128]{1,0:T(8,128)(2,1)} %copy-done.13, bf16[384,128]{1,0:T(8,128)(2,1)} %copy-done.11, bf16[384,128]{1,0:T(8,128)(2,1)} %copy-done.12, bf16[384,128]{1,0:T(8,128)(2,1)S(1)} %copy-done.8, ...), kind=kOutput, calls=%fused_computation.3 | convolution fusion | flops 408289280 | bytes 3407872 | tf_op jit(solution)/shard_map/dot_general | solution.py:34
  50.5 1.2 collective-permute-done.42
  51.7 0.9 collective-permute-done.41
  53.3 1.7 %collective-permute-start.44 = (f32[8,256]{1,0:T(8,128)S(1)}, f32[8,256]{1,0:T(8,128)S(1)}, u32[]{:S(2)}, u32[]{:S(2)}) collective-permute-start(f32[8,256]{1,0:T(8,128)S(1)} %get-tuple-element.3), channel_id=1, source_target_pairs={{0,16},{4,20},{8,24},{12,28},{16,0},{20,4},{24,8},{28,12},{1,17},{... | collective-permute-start | bytes 24584 | tf_op jit(solution)/shard_map/ppermute | solution.py:83
  55.0 1.4 collective-permute-done.43
  56.4 1.6 %collective-permute-start.45 = (f32[8,256]{1,0:T(8,128)S(1)}, f32[8,256]{1,0:T(8,128)S(1)}, u32[]{:S(2)}, u32[]{:S(2)}) collective-permute-start(f32[8,256]{1,0:T(8,128)S(1)} %get-tuple-element.3), channel_id=1, source_target_pairs={{0,24},{4,28},{8,16},{12,20},{16,8},{20,12},{24,0},{28,4},{1,25},{... | collective-permute-start | bytes 24584 | tf_op jit(solution)/shard_map/ppermute | solution.py:83
  57.9 3.9 %collective-permute-done.45 = f32[8,256]{1,0:T(8,128)S(1)} collective-permute-done((f32[8,256]{1,0:T(8,128)S(1)}, f32[8,256]{1,0:T(8,128)S(1)}, u32[]{:S(2)}, u32[]{:S(2)}) %collective-permute-start.45) | collective-permute-done | bytes 8224 | tf_op jit(solution)/shard_map/ppermute | solution.py:83
  61.8 1.5 %collective-permute-start.46 = (f32[32,256]{1,0:T(8,128)S(1)}, f32[32,256]{1,0:T(8,128)S(1)}, u32[]{:S(2)}, u32[]{:S(2)}) collective-permute-start(f32[32,256]{1,0:T(8,128)S(1)} %bitcast.191), channel_id=1, source_target_pairs={{0,1},{1,0},{2,3},{3,2},{4,5},{5,4},{6,7},{7,6},{8,9},{9,8},{10,11... | collective-permute-start | bytes 98312 | tf_op jit(solution)/shard_map/ppermute | solution.py:83
  63.3 1.5 %collective-permute-start.47 = (f32[32,256]{1,0:T(8,128)S(1)}, f32[32,256]{1,0:T(8,128)S(1)}, u32[]{:S(2)}, u32[]{:S(2)}) collective-permute-start(f32[32,256]{1,0:T(8,128)S(1)} %bitcast.192), channel_id=1, source_target_pairs={{0,2},{1,3},{2,0},{3,1},{4,6},{5,7},{6,4},{7,5},{8,10},{9,11},{10,... | collective-permute-start | bytes 98312 | tf_op jit(solution)/shard_map/ppermute | solution.py:83
  64.8 0.9 collective-permute-done.46
  65.8 2.7 %collective-permute-start.25 = (f32[64,256]{1,0:T(8,128)S(1)}, f32[64,256]{1,0:T(8,128)S(1)}, u32[]{:S(2)}, u32[]{:S(2)}) collective-permute-start(f32[64,256]{1,0:T(8,128)S(1)} %get-tuple-element.27), channel_id=1, source_target_pairs={{0,3},{1,2},{2,1},{3,0},{4,7},{5,6},{6,5},{7,4},{8,11},{9,10},{10,... | collective-permute-start | bytes 196616 | tf_op jit(solution)/shard_map/ppermute | solution.py:83
  69.4 2.0 %collective-permute-done.25 = f32[64,256]{1,0:T(8,128)S(1)} collective-permute-done((f32[64,256]{1,0:T(8,128)S(1)}, f32[64,256]{1,0:T(8,128)S(1)}, u32[]{:S(2)}, u32[]{:S(2)}) %collective-permute-start.25) | collective-permute-done | bytes 65568 | tf_op jit(solution)/shard_map/ppermute | solution.py:83
  71.4 2.4 %collective-permute-start.48 = (f32[32,256]{1,0:T(8,128)S(1)}, f32[32,256]{1,0:T(8,128)S(1)}, u32[]{:S(2)}, u32[]{:S(2)}) collective-permute-start(f32[32,256]{1,0:T(8,128)S(1)} %bitcast.193), channel_id=1, source_target_pairs={{0,3},{1,2},{2,1},{3,0},{4,7},{5,6},{6,5},{7,4},{8,11},{9,10},{10,... | collective-permute-start | bytes 98312 | tf_op jit(solution)/shard_map/ppermute | solution.py:83
  73.8 1.9 %collective-permute-start.28 = (f32[16,256]{1,0:T(8,128)S(1)}, f32[16,256]{1,0:T(8,128)S(1)}, u32[]{:S(2)}, u32[]{:S(2)}) collective-permute-start(f32[16,256]{1,0:T(8,128)S(1)} %get-tuple-element.39), channel_id=1, source_target_pairs={{0,24},{4,28},{8,16},{12,20},{16,8},{20,12},{24,0},{28,4},{1,25},{... | collective-permute-start | bytes 49160 | tf_op jit(solution)/shard_map/ppermute | solution.py:83
  76.2 2.0 %collective-permute-start.26 = (f32[16,256]{1,0:T(8,128)S(1)}, f32[16,256]{1,0:T(8,128)S(1)}, u32[]{:S(2)}, u32[]{:S(2)}) collective-permute-start(f32[16,256]{1,0:T(8,128)S(1)} %get-tuple-element.38), channel_id=1, source_target_pairs={{0,8},{4,12},{8,0},{12,4},{16,24},{20,28},{24,16},{28,20},{1,9},{5... | collective-permute-start | bytes 49160 | tf_op jit(solution)/shard_map/ppermute | solution.py:83
  78.3 1.1 collective-permute-done.28
  79.4 0.9 collective-permute-done.27
  80.4 1.7 %collective-permute-start.29 = (f32[16,256]{1,0:T(8,128)S(1)}, f32[16,256]{1,0:T(8,128)S(1)}, u32[]{:S(2)}, u32[]{:S(2)}) collective-permute-start(f32[16,256]{1,0:T(8,128)S(1)} %get-tuple-element.5), channel_id=1, source_target_pairs={{0,8},{4,12},{8,0},{12,4},{16,24},{20,28},{24,16},{28,20},{1,9},{5... | collective-permute-start | bytes 49160 | tf_op jit(solution)/shard_map/ppermute | solution.py:83
  82.1 0.9 collective-permute-start.30
  83.0 1.8 %collective-permute-start.31 = (f32[16,256]{1,0:T(8,128)S(1)}, f32[16,256]{1,0:T(8,128)S(1)}, u32[]{:S(2)}, u32[]{:S(2)}) collective-permute-start(f32[16,256]{1,0:T(8,128)S(1)} %get-tuple-element.5), channel_id=1, source_target_pairs={{0,24},{4,28},{8,16},{12,20},{16,8},{20,12},{24,0},{28,4},{1,25},{... | collective-permute-start | bytes 49160 | tf_op jit(solution)/shard_map/ppermute | solution.py:83
  84.9 1.9 %collective-permute-done.30 = f32[16,256]{1,0:T(8,128)S(1)} collective-permute-done((f32[16,256]{1,0:T(8,128)S(1)}, f32[16,256]{1,0:T(8,128)S(1)}, u32[]{:S(2)}, u32[]{:S(2)}) %collective-permute-start.30) | collective-permute-done | bytes 16416 | tf_op jit(solution)/shard_map/ppermute | solution.py:83
  86.8 1.8 %collective-permute-done.31 = f32[16,256]{1,0:T(8,128)S(1)} collective-permute-done((f32[16,256]{1,0:T(8,128)S(1)}, f32[16,256]{1,0:T(8,128)S(1)}, u32[]{:S(2)}, u32[]{:S(2)}) %collective-permute-start.31) | collective-permute-done | bytes 16416 | tf_op jit(solution)/shard_map/ppermute | solution.py:83
  89.2 1.7 %collective-permute-start.33 = (f32[64,256]{1,0:T(8,128)S(1)}, f32[64,256]{1,0:T(8,128)S(1)}, u32[]{:S(2)}, u32[]{:S(2)}) collective-permute-start(f32[64,256]{1,0:T(8,128)S(1)} %bitcast.188), channel_id=1, source_target_pairs={{0,2},{1,3},{2,0},{3,1},{4,6},{5,7},{6,4},{7,5},{8,10},{9,11},{10,... | collective-permute-start | bytes 196616 | tf_op jit(solution)/shard_map/ppermute | solution.py:83
  90.9 1.1 collective-permute-start.34
  93.5 2.5 %collective-permute-done.34 = f32[64,256]{1,0:T(8,128)S(1)} collective-permute-done((f32[64,256]{1,0:T(8,128)S(1)}, f32[64,256]{1,0:T(8,128)S(1)}, u32[]{:S(2)}, u32[]{:S(2)}) %collective-permute-start.34) | collective-permute-done | bytes 65568 | tf_op jit(solution)/shard_map/ppermute | solution.py:83
  96.9 2.9 %all-to-all-start.1 = ((f32[32,8,256]{2,1,0:T(8,128)}), f32[32,8,256]{2,1,0:T(8,128)S(1)}, u32[]{:S(2)}, u32[]{:S(2)}) async-start(f32[32,8,256]{2,1,0:T(8,128)} %broadcast_in_dim.120), calls=%async_computation.1 | async-start | bytes 524288 | tf_op jit(solution)/shard_map/all_to_all | solution.py:124
  99.8 1.1 bitcast_add_fusion
  101.0 3.7 %collective-permute-start.16 = (f32[128,256]{1,0:T(8,128)S(1)}, f32[128,256]{1,0:T(8,128)S(1)}, u32[]{:S(2)}, u32[]{:S(2)}) collective-permute-start(f32[128,256]{1,0:T(8,128)S(1)} %get-tuple-element.16), channel_id=1, source_target_pairs={{0,8},{4,12},{1,9},{5,13},{2,10},{6,14},{3,11},{7,15}} | collective-permute-start | bytes 393224 | tf_op jit(solution)/shard_map/ppermute | solution.py:164
  105.3 1.1 bitcast_add_fusion.1
  106.5 1.3 collective-permute-start.5
  108.5 3.6 %collective-permute-start.17 = (f32[128,256]{1,0:T(8,128)S(1)}, f32[128,256]{1,0:T(8,128)S(1)}, u32[]{:S(2)}, u32[]{:S(2)}) collective-permute-start(f32[128,256]{1,0:T(8,128)S(1)} %bitcast_add_fusion.6), channel_id=1, source_target_pairs={{0,8},{4,12},{8,16},{12,20},{1,9},{5,13},{9,17},{13,21},{2,10},{6,... | collective-permute-start | bytes 393224 | tf_op jit(solution)/shard_map/ppermute | solution.py:164
  112.2 3.1 %collective-permute-start.6 = (f32[128,256]{1,0:T(8,128)S(1)}, f32[128,256]{1,0:T(8,128)S(1)}, u32[]{:S(2)}, u32[]{:S(2)}) collective-permute-start(f32[128,256]{1,0:T(8,128)S(1)} %bitcast_add_fusion.11), channel_id=1, source_target_pairs={{0,8},{4,12},{8,16},{12,20},{1,9},{5,13},{9,17},{13,21},{2,10},{6,... | collective-permute-start | bytes 393224 | tf_op jit(solution)/shard_map/ppermute | solution.py:164
  115.3 1.1 maximum_select_fusion
  117.2 3.2 %collective-permute-start.18 = (f32[128,256]{1,0:T(8,128)S(1)}, f32[128,256]{1,0:T(8,128)S(1)}, u32[]{:S(2)}, u32[]{:S(2)}) collective-permute-start(f32[128,256]{1,0:T(8,128)S(1)} %get-tuple-element.14), channel_id=1, source_target_pairs={{0,8},{4,12},{8,16},{12,20},{16,24},{20,28},{1,9},{5,13},{9,17},{1... | collective-permute-start | bytes 393224 | tf_op jit(solution)/shard_map/ppermute | solution.py:164
  121.1 5.2 %collective-permute-start.7 = (f32[128,256]{1,0:T(8,128)S(1)}, f32[128,256]{1,0:T(8,128)S(1)}, u32[]{:S(2)}, u32[]{:S(2)}) collective-permute-start(f32[128,256]{1,0:T(8,128)S(1)} %get-tuple-element.18), channel_id=1, source_target_pairs={{0,8},{4,12},{8,16},{12,20},{16,24},{20,28},{1,9},{5,13},{9,17},{1... | collective-permute-start | bytes 393224 | tf_op jit(solution)/shard_map/ppermute | solution.py:164
  126.3 1.3 collective-permute-start.21
  127.6 1.5 %collective-permute-start.10 = (f32[128,256]{1,0:T(8,128)S(1)}, f32[128,256]{1,0:T(8,128)S(1)}, u32[]{:S(2)}, u32[]{:S(2)}) collective-permute-start(f32[128,256]{1,0:T(8,128)S(1)} %bitcast_add_fusion.10), channel_id=1, source_target_pairs={{8,0},{12,4},{16,8},{20,12},{24,16},{28,20},{9,1},{13,5},{17,9},{2... | collective-permute-start | bytes 393224 | tf_op jit(solution)/shard_map/ppermute | solution.py:164
  129.1 4.3 %shard_map.59.inverse_first_ref = f32[256,256]{1,0:T(8,128)S(1)} custom-call(f32[256,256]{1,0:T(8,128)S(1)} %bitcast.167), custom_call_target="tpu_custom_call" | custom-call | flops 1610612736 | bytes 1048576 | tf_op jit(solution)/shard_map/pallas_call | solution.py:71
  133.4 4.9 %shard_map.60.inverse_second_ref = f32[256,256]{1,0:T(8,128)S(1)} custom-call(f32[256,256]{1,0:T(8,128)S(1)} %shard_map.59.inverse_first_ref, f32[256,256]{1,0:T(8,128)S(1)} %get-tuple-element.11.upper_ref, f32[256,256]{1,0:T(8,128)S(1)} %maximum_select_fusion.1.lower_ref, f32[256,256]{1,0:T(8,128)S(1)} %get-tuple-element.10.corner_ref), custom_call_target="tpu_custom_call" | custom-call | flops 1811939328 | bytes 1048576 | tf_op jit(solution)/shard_map/pallas_call | solution.py:71
  138.4 1.3 shard_map.61
  (148 shorter events, 12.8 us)
Async XLA Ops:
  1.7 17.9 %copy-start.9 = (bf16[384,128]{1,0:T(8,128)(2,1)}, bf16[384,128]{1,0:T(8,128)(2,1)S(1)}, u32[]{:S(2)}) copy-start(bf16[384,128]{1,0:T(8,128)(2,1)S(1)} %get-tuple-element.25) | copy-start | bytes 294916
  1.7 21.5 %copy-start.7 = (bf16[384,128]{1,0:T(8,128)(2,1)}, bf16[384,128]{1,0:T(8,128)(2,1)S(1)}, u32[]{:S(2)}) copy-start(bf16[384,128]{1,0:T(8,128)(2,1)S(1)} %get-tuple-element.23) | copy-start | bytes 294916
  1.7 11.8 %collective-permute-start.13 = (bf16[384,128]{1,0:T(8,128)(2,1)S(1)}, bf16[384,128]{1,0:T(8,128)(2,1)S(1)}, u32[]{:S(2)}, u32[]{:S(2)}) collective-permute-start(bf16[384,128]{1,0:T(8,128)(2,1)S(1)} %get-tuple-element.23), channel_id=1, source_target_pairs={{0,2},{1,3},{2,0},{3,1},{4,6},{5,7},{6,4},{7,5},{8,10},{9,11},{10,... | collective-permute-start | bytes 294920 | tf_op jit(solution)/shard_map/ppermute | solution.py:83
  4.8 10.8 %collective-permute-start.11 = (bf16[384,128]{1,0:T(8,128)(2,1)S(1)}, bf16[384,128]{1,0:T(8,128)(2,1)}, u32[]{:S(2)}, u32[]{:S(2)}) collective-permute-start(bf16[384,128]{1,0:T(8,128)(2,1)S(1)} %get-tuple-element.22), channel_id=1, source_target_pairs={{0,1},{1,0},{2,3},{3,2},{4,5},{5,4},{6,7},{7,6},{8,9},{9,8},{10,11... | collective-permute-start | bytes 294920 | tf_op jit(solution)/shard_map/ppermute | solution.py:83
  6.3 11.8 %collective-permute-start.2 = (bf16[384,128]{1,0:T(8,128)(2,1)S(1)}, bf16[384,128]{1,0:T(8,128)(2,1)}, u32[]{:S(2)}, u32[]{:S(2)}) collective-permute-start(bf16[384,128]{1,0:T(8,128)(2,1)S(1)} %get-tuple-element.24), channel_id=1, source_target_pairs={{0,2},{1,3},{2,0},{3,1},{4,6},{5,7},{6,4},{7,5},{8,10},{9,11},{10,... | collective-permute-start | bytes 294920 | tf_op jit(solution)/shard_map/ppermute | solution.py:83
  6.8 12.8 %collective-permute-start = (bf16[384,128]{1,0:T(8,128)(2,1)S(1)}, bf16[384,128]{1,0:T(8,128)(2,1)}, u32[]{:S(2)}, u32[]{:S(2)}) collective-permute-start(bf16[384,128]{1,0:T(8,128)(2,1)S(1)} %get-tuple-element.25), channel_id=1, source_target_pairs={{0,1},{1,0},{2,3},{3,2},{4,5},{5,4},{6,7},{7,6},{8,9},{9,8},{10,11... | collective-permute-start | bytes 294920 | tf_op jit(solution)/shard_map/ppermute | solution.py:83
  10.2 3.0 %copy-start.1 = (bf16[384,1024]{1,0:T(8,128)(2,1)}, bf16[384,1024]{1,0:T(8,128)(2,1)S(1)}, u32[]{:S(2)}) copy-start(bf16[384,1024]{1,0:T(8,128)(2,1)S(1)} %get-tuple-element.7) | copy-start | bytes 2359300
  13.5 9.8 %copy-start.2 = (bf16[384,1024]{1,0:T(8,128)(2,1)S(1)}, bf16[384,1024]{1,0:T(8,128)(2,1)}, u32[]{:S(2)}) copy-start(bf16[384,1024]{1,0:T(8,128)(2,1)} %copy-done.1) | copy-start | bytes 2359300
  13.5 9.8 %copy-start.4 = (bf16[384,1024]{1,0:T(8,128)(2,1)S(1)}, bf16[384,1024]{1,0:T(8,128)(2,1)}, u32[]{:S(2)}) copy-start(bf16[384,1024]{1,0:T(8,128)(2,1)} %copy-done.3) | copy-start | bytes 2359300
  13.5 9.7 %copy-start.11 = (bf16[384,128]{1,0:T(8,128)(2,1)}, bf16[384,128]{1,0:T(8,128)(2,1)S(1)}, u32[]{:S(2)}) copy-start(bf16[384,128]{1,0:T(8,128)(2,1)S(1)} %collective-permute-done.13) | copy-start | bytes 294916
  13.6 7.2 %collective-permute-start.14 = (bf16[768,128]{1,0:T(8,128)(2,1)S(1)}, bf16[768,128]{1,0:T(8,128)(2,1)S(1)}, u32[]{:S(2)}, u32[]{:S(2)}) collective-permute-start(bf16[768,128]{1,0:T(8,128)(2,1)S(1)} %pad_maximum_fusion.4), channel_id=1, source_target_pairs={{0,1},{1,0},{2,3},{3,2},{4,5},{5,4},{6,7},{7,6},{8,9},{9,8},{10,11... | collective-permute-start | bytes 589832 | tf_op jit(solution)/shard_map/ppermute | solution.py:83
  16.5 6.8 %collective-permute-start.12 = (bf16[768,128]{1,0:T(8,128)(2,1)S(1)}, bf16[768,128]{1,0:T(8,128)(2,1)S(1)}, u32[]{:S(2)}, u32[]{:S(2)}) collective-permute-start(bf16[768,128]{1,0:T(8,128)(2,1)S(1)} %pad_maximum_fusion.3), channel_id=1, source_target_pairs={{0,2},{1,3},{2,0},{3,1},{4,6},{5,7},{6,4},{7,5},{8,10},{9,11},{10,... | collective-permute-start | bytes 589832 | tf_op jit(solution)/shard_map/ppermute | solution.py:83
  19.0 7.5 %collective-permute-start.3 = (bf16[768,128]{1,0:T(8,128)(2,1)S(1)}, bf16[768,128]{1,0:T(8,128)(2,1)S(1)}, u32[]{:S(2)}, u32[]{:S(2)}) collective-permute-start(bf16[768,128]{1,0:T(8,128)(2,1)S(1)} %pad_maximum_fusion.2), channel_id=1, source_target_pairs={{0,1},{1,0},{2,3},{3,2},{4,5},{5,4},{6,7},{7,6},{8,9},{9,8},{10,11... | collective-permute-start | bytes 589832 | tf_op jit(solution)/shard_map/ppermute | solution.py:83
  20.5 6.0 %collective-permute-start.1 = (bf16[768,128]{1,0:T(8,128)(2,1)S(1)}, bf16[768,128]{1,0:T(8,128)(2,1)S(1)}, u32[]{:S(2)}, u32[]{:S(2)}) collective-permute-start(bf16[768,128]{1,0:T(8,128)(2,1)S(1)} %pad_maximum_fusion.1), channel_id=1, source_target_pairs={{0,2},{1,3},{2,0},{3,1},{4,6},{5,7},{6,4},{7,5},{8,10},{9,11},{10,... | collective-permute-start | bytes 589832 | tf_op jit(solution)/shard_map/ppermute | solution.py:83
  20.8 4.8 %copy-start.12 = (bf16[384,128]{1,0:T(8,128)(2,1)}, bf16[384,128]{1,0:T(8,128)(2,1)S(1)}, u32[]{:S(2)}) copy-start(bf16[384,128]{1,0:T(8,128)(2,1)S(1)} %get-tuple-element.31) | copy-start | bytes 294916
  20.8 4.8 %copy-start.13 = (bf16[384,128]{1,0:T(8,128)(2,1)}, bf16[384,128]{1,0:T(8,128)(2,1)S(1)}, u32[]{:S(2)}) copy-start(bf16[384,128]{1,0:T(8,128)(2,1)S(1)} %get-tuple-element.32) | copy-start | bytes 294916
  23.3 3.2 %copy-start.10 = (bf16[384,128]{1,0:T(8,128)(2,1)S(1)}, bf16[384,128]{1,0:T(8,128)(2,1)}, u32[]{:S(2)}) copy-start(bf16[384,128]{1,0:T(8,128)(2,1)} %copy-done.9) | copy-start | bytes 294916
  23.3 3.2 %copy-start.18 = (bf16[512,1536]{1,0:T(8,128)(2,1)S(1)}, bf16[512,1536]{1,0:T(8,128)(2,1)}, u32[]{:S(2)}) copy-start(bf16[512,1536]{1,0:T(8,128)(2,1)} %convolution_convert_fusion) | copy-start | bytes 4718596
  26.5 73.3 %collective-permute-start.15 = (f32[4,128,256]{2,1,0:T(8,128)}, f32[4,128,256]{2,1,0:T(8,128)}, u32[]{:S(2)}, u32[]{:S(2)}) collective-permute-start(f32[4,128,256]{2,1,0:T(8,128)} %dynamic-slice_bitcast_fusion.4), channel_id=1, source_target_pairs={{0,4},{4,0},{8,12},{12,8},{16,20},{20,16},{24,28},{28,24},{1,5},{5... | collective-permute-start | bytes 1572872 | tf_op jit(solution)/shard_map/ppermute | solution.py:83
  28.9 2.6 %collective-permute-start.36 = (f32[128,256]{1,0:T(8,128)S(1)}, f32[128,256]{1,0:T(8,128)S(1)}, u32[]{:S(2)}, u32[]{:S(2)}) collective-permute-start(f32[128,256]{1,0:T(8,128)S(1)} %dynamic-slice_bitcast_fusion.7), channel_id=1, source_target_pairs={{0,4},{4,0},{8,12},{12,8},{16,20},{20,16},{24,28},{28,24},{1,5},{5... | collective-permute-start | bytes 393224 | tf_op jit(solution)/shard_map/ppermute | solution.py:83
  31.4 4.7 %copy-start = (f32[1024,256]{1,0:T(8,128)}, f32[1024,256]{1,0:T(8,128)S(1)}, u32[]{:S(2)}) copy-start(f32[1024,256]{1,0:T(8,128)S(1)} %fusion.21) | copy-start | bytes 3145732
  31.5 17.0 %copy-start.8 = (bf16[384,128]{1,0:T(8,128)(2,1)S(1)}, bf16[384,128]{1,0:T(8,128)(2,1)}, u32[]{:S(2)}) copy-start(bf16[384,128]{1,0:T(8,128)(2,1)} %copy-done.7) | copy-start | bytes 294916
  32.2 10.4 %collective-permute-start.39 = (f32[32,256]{1,0:T(8,128)}, f32[32,256]{1,0:T(8,128)S(1)}, u32[]{:S(2)}, u32[]{:S(2)}) collective-permute-start(f32[32,256]{1,0:T(8,128)} %get-tuple-element.36), channel_id=1, source_target_pairs={{0,3},{1,2},{2,1},{3,0},{4,7},{5,6},{6,5},{7,4},{8,11},{9,10},{10,... | collective-permute-start | bytes 98312 | tf_op jit(solution)/shard_map/ppermute | solution.py:83
  33.8 8.7 %collective-permute-start.38 = (f32[32,256]{1,0:T(8,128)}, f32[32,256]{1,0:T(8,128)S(1)}, u32[]{:S(2)}, u32[]{:S(2)}) collective-permute-start(f32[32,256]{1,0:T(8,128)} %get-tuple-element.37), channel_id=1, source_target_pairs={{0,2},{1,3},{2,0},{3,1},{4,6},{5,7},{6,4},{7,5},{8,10},{9,11},{10,... | collective-permute-start | bytes 98312 | tf_op jit(solution)/shard_map/ppermute | solution.py:83
  34.6 8.5 %collective-permute-start.37 = (f32[32,256]{1,0:T(8,128)}, f32[32,256]{1,0:T(8,128)}, u32[]{:S(2)}, u32[]{:S(2)}) collective-permute-start(f32[32,256]{1,0:T(8,128)} %get-tuple-element.35), channel_id=1, source_target_pairs={{0,1},{1,0},{2,3},{3,2},{4,5},{5,4},{6,7},{7,6},{8,9},{9,8},{10,11... | collective-permute-start | bytes 98312 | tf_op jit(solution)/shard_map/ppermute | solution.py:83
  36.9 68.4 %collective-permute-start.4 = (f32[4,128,256]{2,1,0:T(8,128)}, f32[4,128,256]{2,1,0:T(8,128)S(1)}, u32[]{:S(2)}, u32[]{:S(2)}) collective-permute-start(f32[4,128,256]{2,1,0:T(8,128)} %dynamic-slice_bitcast_fusion.5), channel_id=1, source_target_pairs={{0,4},{4,0},{8,12},{12,8},{16,20},{20,16},{24,28},{28,24},{1,5},{5... | collective-permute-start | bytes 1572872 | tf_op jit(solution)/shard_map/ppermute | solution.py:83
  36.9 59.2 %all-to-all-start = ((f32[32,8,256]{2,1,0:T(8,128)}), f32[32,8,256]{2,1,0:T(8,128)S(1)}, u32[]{:S(2)}, u32[]{:S(2)}) async-start(f32[32,8,256]{2,1,0:T(8,128)} %get-tuple-element.13), calls=%async_computation | async-start | bytes 524288 | tf_op jit(solution)/shard_map/all_to_all | solution.py:122
  44.0 7.7 %collective-permute-start.42 = (f32[8,256]{1,0:T(8,128)S(1)}, f32[8,256]{1,0:T(8,128)S(1)}, u32[]{:S(2)}, u32[]{:S(2)}) collective-permute-start(f32[8,256]{1,0:T(8,128)S(1)} %get-tuple-element.42), channel_id=1, source_target_pairs={{0,24},{4,28},{8,16},{12,20},{16,8},{20,12},{24,0},{28,4},{1,25},{... | collective-permute-start | bytes 24584 | tf_op jit(solution)/shard_map/ppermute | solution.py:83
  47.7 5.0 %collective-permute-start.41 = (f32[8,256]{1,0:T(8,128)S(1)}, f32[8,256]{1,0:T(8,128)S(1)}, u32[]{:S(2)}, u32[]{:S(2)}) collective-permute-start(f32[8,256]{1,0:T(8,128)S(1)} %get-tuple-element.43), channel_id=1, source_target_pairs={{0,16},{4,20},{8,24},{12,28},{16,0},{20,4},{24,8},{28,12},{1,17},{... | collective-permute-start | bytes 24584 | tf_op jit(solution)/shard_map/ppermute | solution.py:83
  47.7 5.0 %collective-permute-start.40 = (f32[8,256]{1,0:T(8,128)S(1)}, f32[8,256]{1,0:T(8,128)S(1)}, u32[]{:S(2)}, u32[]{:S(2)}) collective-permute-start(f32[8,256]{1,0:T(8,128)S(1)} %get-tuple-element.41), channel_id=1, source_target_pairs={{0,8},{4,12},{8,0},{12,4},{16,24},{20,28},{24,16},{28,20},{1,9},{5... | collective-permute-start | bytes 24584 | tf_op jit(solution)/shard_map/ppermute | solution.py:83
  52.7 3.7 %collective-permute-start.43 = (f32[8,256]{1,0:T(8,128)S(1)}, f32[8,256]{1,0:T(8,128)S(1)}, u32[]{:S(2)}, u32[]{:S(2)}) collective-permute-start(f32[8,256]{1,0:T(8,128)S(1)} %get-tuple-element.3), channel_id=1, source_target_pairs={{0,8},{4,12},{8,0},{12,4},{16,24},{20,28},{24,16},{28,20},{1,9},{5... | collective-permute-start | bytes 24584 | tf_op jit(solution)/shard_map/ppermute | solution.py:83
  53.2 12.5 %collective-permute-start.22 = (f32[256,256]{1,0:T(8,128)S(1)}, f32[256,256]{1,0:T(8,128)S(1)}, u32[]{:S(2)}, u32[]{:S(2)}) collective-permute-start(f32[256,256]{1,0:T(8,128)S(1)} %dynamic-slice_bitcast_fusion.6), channel_id=1, source_target_pairs={{0,4},{4,0},{8,12},{12,8},{16,20},{20,16},{24,28},{28,24},{1,5},{5... | collective-permute-start | bytes 786440 | tf_op jit(solution)/shard_map/ppermute | solution.py:83
  53.3 4.6 %collective-permute-start.44 = (f32[8,256]{1,0:T(8,128)S(1)}, f32[8,256]{1,0:T(8,128)S(1)}, u32[]{:S(2)}, u32[]{:S(2)}) collective-permute-start(f32[8,256]{1,0:T(8,128)S(1)} %get-tuple-element.3), channel_id=1, source_target_pairs={{0,16},{4,20},{8,24},{12,28},{16,0},{20,4},{24,8},{28,12},{1,17},{... | collective-permute-start | bytes 24584 | tf_op jit(solution)/shard_map/ppermute | solution.py:83
  56.4 5.4 %collective-permute-start.45 = (f32[8,256]{1,0:T(8,128)S(1)}, f32[8,256]{1,0:T(8,128)S(1)}, u32[]{:S(2)}, u32[]{:S(2)}) collective-permute-start(f32[8,256]{1,0:T(8,128)S(1)} %get-tuple-element.3), channel_id=1, source_target_pairs={{0,24},{4,28},{8,16},{12,20},{16,8},{20,12},{24,0},{28,4},{1,25},{... | collective-permute-start | bytes 24584 | tf_op jit(solution)/shard_map/ppermute | solution.py:83
  61.8 3.9 %collective-permute-start.46 = (f32[32,256]{1,0:T(8,128)S(1)}, f32[32,256]{1,0:T(8,128)S(1)}, u32[]{:S(2)}, u32[]{:S(2)}) collective-permute-start(f32[32,256]{1,0:T(8,128)S(1)} %bitcast.191), channel_id=1, source_target_pairs={{0,1},{1,0},{2,3},{3,2},{4,5},{5,4},{6,7},{7,6},{8,9},{9,8},{10,11... | collective-permute-start | bytes 98312 | tf_op jit(solution)/shard_map/ppermute | solution.py:83
  63.3 5.5 %collective-permute-start.47 = (f32[32,256]{1,0:T(8,128)S(1)}, f32[32,256]{1,0:T(8,128)S(1)}, u32[]{:S(2)}, u32[]{:S(2)}) collective-permute-start(f32[32,256]{1,0:T(8,128)S(1)} %bitcast.192), channel_id=1, source_target_pairs={{0,2},{1,3},{2,0},{3,1},{4,6},{5,7},{6,4},{7,5},{8,10},{9,11},{10,... | collective-permute-start | bytes 98312 | tf_op jit(solution)/shard_map/ppermute | solution.py:83
  65.8 5.6 %collective-permute-start.25 = (f32[64,256]{1,0:T(8,128)S(1)}, f32[64,256]{1,0:T(8,128)S(1)}, u32[]{:S(2)}, u32[]{:S(2)}) collective-permute-start(f32[64,256]{1,0:T(8,128)S(1)} %get-tuple-element.27), channel_id=1, source_target_pairs={{0,3},{1,2},{2,1},{3,0},{4,7},{5,6},{6,5},{7,4},{8,11},{9,10},{10,... | collective-permute-start | bytes 196616 | tf_op jit(solution)/shard_map/ppermute | solution.py:83
  68.5 5.2 %collective-permute-start.24 = (f32[64,256]{1,0:T(8,128)S(1)}, f32[64,256]{1,0:T(8,128)S(1)}, u32[]{:S(2)}, u32[]{:S(2)}) collective-permute-start(f32[64,256]{1,0:T(8,128)S(1)} %get-tuple-element.28), channel_id=1, source_target_pairs={{0,2},{1,3},{2,0},{3,1},{4,6},{5,7},{6,4},{7,5},{8,10},{9,11},{10,... | collective-permute-start | bytes 196616 | tf_op jit(solution)/shard_map/ppermute | solution.py:83
  68.8 4.9 %collective-permute-start.23 = (f32[64,256]{1,0:T(8,128)S(1)}, f32[64,256]{1,0:T(8,128)S(1)}, u32[]{:S(2)}, u32[]{:S(2)}) collective-permute-start(f32[64,256]{1,0:T(8,128)S(1)} %get-tuple-element.26), channel_id=1, source_target_pairs={{0,1},{1,0},{2,3},{3,2},{4,5},{5,4},{6,7},{7,6},{8,9},{9,8},{10,11... | collective-permute-start | bytes 196616 | tf_op jit(solution)/shard_map/ppermute | solution.py:83
  71.4 4.8 %collective-permute-start.48 = (f32[32,256]{1,0:T(8,128)S(1)}, f32[32,256]{1,0:T(8,128)S(1)}, u32[]{:S(2)}, u32[]{:S(2)}) collective-permute-start(f32[32,256]{1,0:T(8,128)S(1)} %bitcast.193), channel_id=1, source_target_pairs={{0,3},{1,2},{2,1},{3,0},{4,7},{5,6},{6,5},{7,4},{8,11},{9,10},{10,... | collective-permute-start | bytes 98312 | tf_op jit(solution)/shard_map/ppermute | solution.py:83
  73.8 5.6 %collective-permute-start.28 = (f32[16,256]{1,0:T(8,128)S(1)}, f32[16,256]{1,0:T(8,128)S(1)}, u32[]{:S(2)}, u32[]{:S(2)}) collective-permute-start(f32[16,256]{1,0:T(8,128)S(1)} %get-tuple-element.39), channel_id=1, source_target_pairs={{0,24},{4,28},{8,16},{12,20},{16,8},{20,12},{24,0},{28,4},{1,25},{... | collective-permute-start | bytes 49160 | tf_op jit(solution)/shard_map/ppermute | solution.py:83
  75.7 4.6 %collective-permute-start.27 = (f32[16,256]{1,0:T(8,128)S(1)}, f32[16,256]{1,0:T(8,128)S(1)}, u32[]{:S(2)}, u32[]{:S(2)}) collective-permute-start(f32[16,256]{1,0:T(8,128)S(1)} %get-tuple-element.40), channel_id=1, source_target_pairs={{0,16},{4,20},{8,24},{12,28},{16,0},{20,4},{24,8},{28,12},{1,17},{... | collective-permute-start | bytes 49160 | tf_op jit(solution)/shard_map/ppermute | solution.py:83
  76.2 4.1 %collective-permute-start.26 = (f32[16,256]{1,0:T(8,128)S(1)}, f32[16,256]{1,0:T(8,128)S(1)}, u32[]{:S(2)}, u32[]{:S(2)}) collective-permute-start(f32[16,256]{1,0:T(8,128)S(1)} %get-tuple-element.38), channel_id=1, source_target_pairs={{0,8},{4,12},{8,0},{12,4},{16,24},{20,28},{24,16},{28,20},{1,9},{5... | collective-permute-start | bytes 49160 | tf_op jit(solution)/shard_map/ppermute | solution.py:83
  79.4 3.6 %collective-permute-start.49 = (f32[128,256]{1,0:T(8,128)S(1)}, f32[128,256]{1,0:T(8,128)S(1)}, u32[]{:S(2)}, u32[]{:S(2)}) collective-permute-start(f32[128,256]{1,0:T(8,128)S(1)} %bitcast.178), channel_id=1, source_target_pairs={{0,4},{4,0},{8,12},{12,8},{16,20},{20,16},{24,28},{28,24},{1,5},{5... | collective-permute-start | bytes 393224 | tf_op jit(solution)/shard_map/ppermute | solution.py:83
  80.4 4.5 %collective-permute-start.29 = (f32[16,256]{1,0:T(8,128)S(1)}, f32[16,256]{1,0:T(8,128)S(1)}, u32[]{:S(2)}, u32[]{:S(2)}) collective-permute-start(f32[16,256]{1,0:T(8,128)S(1)} %get-tuple-element.5), channel_id=1, source_target_pairs={{0,8},{4,12},{8,0},{12,4},{16,24},{20,28},{24,16},{28,20},{1,9},{5... | collective-permute-start | bytes 49160 | tf_op jit(solution)/shard_map/ppermute | solution.py:83
  82.1 4.7 %collective-permute-start.30 = (f32[16,256]{1,0:T(8,128)S(1)}, f32[16,256]{1,0:T(8,128)S(1)}, u32[]{:S(2)}, u32[]{:S(2)}) collective-permute-start(f32[16,256]{1,0:T(8,128)S(1)} %get-tuple-element.5), channel_id=1, source_target_pairs={{0,16},{4,20},{8,24},{12,28},{16,0},{20,4},{24,8},{28,12},{1,17},{... | collective-permute-start | bytes 49160 | tf_op jit(solution)/shard_map/ppermute | solution.py:83
  83.0 5.5 %collective-permute-start.31 = (f32[16,256]{1,0:T(8,128)S(1)}, f32[16,256]{1,0:T(8,128)S(1)}, u32[]{:S(2)}, u32[]{:S(2)}) collective-permute-start(f32[16,256]{1,0:T(8,128)S(1)} %get-tuple-element.5), channel_id=1, source_target_pairs={{0,24},{4,28},{8,16},{12,20},{16,8},{20,12},{24,0},{28,4},{1,25},{... | collective-permute-start | bytes 49160 | tf_op jit(solution)/shard_map/ppermute | solution.py:83
  88.5 4.3 %collective-permute-start.32 = (f32[64,256]{1,0:T(8,128)S(1)}, f32[64,256]{1,0:T(8,128)S(1)}, u32[]{:S(2)}, u32[]{:S(2)}) collective-permute-start(f32[64,256]{1,0:T(8,128)S(1)} %bitcast.187), channel_id=1, source_target_pairs={{0,1},{1,0},{2,3},{3,2},{4,5},{5,4},{6,7},{7,6},{8,9},{9,8},{10,11... | collective-permute-start | bytes 196616 | tf_op jit(solution)/shard_map/ppermute | solution.py:83
  89.2 4.3 %collective-permute-start.33 = (f32[64,256]{1,0:T(8,128)S(1)}, f32[64,256]{1,0:T(8,128)S(1)}, u32[]{:S(2)}, u32[]{:S(2)}) collective-permute-start(f32[64,256]{1,0:T(8,128)S(1)} %bitcast.188), channel_id=1, source_target_pairs={{0,2},{1,3},{2,0},{3,1},{4,6},{5,7},{6,4},{7,5},{8,10},{9,11},{10,... | collective-permute-start | bytes 196616 | tf_op jit(solution)/shard_map/ppermute | solution.py:83
  90.9 5.2 %collective-permute-start.34 = (f32[64,256]{1,0:T(8,128)S(1)}, f32[64,256]{1,0:T(8,128)S(1)}, u32[]{:S(2)}, u32[]{:S(2)}) collective-permute-start(f32[64,256]{1,0:T(8,128)S(1)} %bitcast.189), channel_id=1, source_target_pairs={{0,3},{1,2},{2,1},{3,0},{4,7},{5,6},{6,5},{7,4},{8,11},{9,10},{10,... | collective-permute-start | bytes 196616 | tf_op jit(solution)/shard_map/ppermute | solution.py:83
  96.1 19.2 %collective-permute-start.35 = (f32[256,256]{1,0:T(8,128)S(1)}, f32[256,256]{1,0:T(8,128)}, u32[]{:S(2)}, u32[]{:S(2)}) collective-permute-start(f32[256,256]{1,0:T(8,128)S(1)} %bitcast.176), channel_id=1, source_target_pairs={{0,4},{4,0},{8,12},{12,8},{16,20},{20,16},{24,28},{28,24},{1,5},{5... | collective-permute-start | bytes 786440 | tf_op jit(solution)/shard_map/ppermute | solution.py:83
  96.9 32.2 %all-to-all-start.1 = ((f32[32,8,256]{2,1,0:T(8,128)}), f32[32,8,256]{2,1,0:T(8,128)S(1)}, u32[]{:S(2)}, u32[]{:S(2)}) async-start(f32[32,8,256]{2,1,0:T(8,128)} %broadcast_in_dim.120), calls=%async_computation.1 | async-start | bytes 524288 | tf_op jit(solution)/shard_map/all_to_all | solution.py:124
  101.0 7.5 %collective-permute-start.16 = (f32[128,256]{1,0:T(8,128)S(1)}, f32[128,256]{1,0:T(8,128)S(1)}, u32[]{:S(2)}, u32[]{:S(2)}) collective-permute-start(f32[128,256]{1,0:T(8,128)S(1)} %get-tuple-element.16), channel_id=1, source_target_pairs={{0,8},{4,12},{1,9},{5,13},{2,10},{6,14},{3,11},{7,15}} | collective-permute-start | bytes 393224 | tf_op jit(solution)/shard_map/ppermute | solution.py:164
  104.7 11.8 %collective-permute-start.19 = (f32[128,256]{1,0:T(8,128)S(1)}, f32[128,256]{1,0:T(8,128)S(1)}, u32[]{:S(2)}, u32[]{:S(2)}) collective-permute-start(f32[128,256]{1,0:T(8,128)S(1)} %get-tuple-element.17), channel_id=1, source_target_pairs={{24,16},{28,20},{25,17},{29,21},{26,18},{30,22},{27,19},{31,23}} | collective-permute-start | bytes 393224 | tf_op jit(solution)/shard_map/ppermute | solution.py:164
  106.5 5.6 %collective-permute-start.5 = (f32[128,256]{1,0:T(8,128)S(1)}, f32[128,256]{1,0:T(8,128)S(1)}, u32[]{:S(2)}, u32[]{:S(2)}) collective-permute-start(f32[128,256]{1,0:T(8,128)S(1)} %get-tuple-element.20), channel_id=1, source_target_pairs={{0,8},{4,12},{1,9},{5,13},{2,10},{6,14},{3,11},{7,15}} | collective-permute-start | bytes 393224 | tf_op jit(solution)/shard_map/ppermute | solution.py:164
  107.8 12.5 %collective-permute-start.8 = (f32[128,256]{1,0:T(8,128)S(1)}, f32[128,256]{1,0:T(8,128)S(1)}, u32[]{:S(2)}, u32[]{:S(2)}) collective-permute-start(f32[128,256]{1,0:T(8,128)S(1)} %get-tuple-element.21), channel_id=1, source_target_pairs={{24,16},{28,20},{25,17},{29,21},{26,18},{30,22},{27,19},{31,23}} | collective-permute-start | bytes 393224 | tf_op jit(solution)/shard_map/ppermute | solution.py:164
  108.5 7.9 %collective-permute-start.17 = (f32[128,256]{1,0:T(8,128)S(1)}, f32[128,256]{1,0:T(8,128)S(1)}, u32[]{:S(2)}, u32[]{:S(2)}) collective-permute-start(f32[128,256]{1,0:T(8,128)S(1)} %bitcast_add_fusion.6), channel_id=1, source_target_pairs={{0,8},{4,12},{8,16},{12,20},{1,9},{5,13},{9,17},{13,21},{2,10},{6,... | collective-permute-start | bytes 393224 | tf_op jit(solution)/shard_map/ppermute | solution.py:164
  112.2 8.2 %collective-permute-start.6 = (f32[128,256]{1,0:T(8,128)S(1)}, f32[128,256]{1,0:T(8,128)S(1)}, u32[]{:S(2)}, u32[]{:S(2)}) collective-permute-start(f32[128,256]{1,0:T(8,128)S(1)} %bitcast_add_fusion.11), channel_id=1, source_target_pairs={{0,8},{4,12},{8,16},{12,20},{1,9},{5,13},{9,17},{13,21},{2,10},{6,... | collective-permute-start | bytes 393224 | tf_op jit(solution)/shard_map/ppermute | solution.py:164
  116.5 9.8 %collective-permute-start.20 = (f32[128,256]{1,0:T(8,128)S(1)}, f32[128,256]{1,0:T(8,128)S(1)}, u32[]{:S(2)}, u32[]{:S(2)}) collective-permute-start(f32[128,256]{1,0:T(8,128)S(1)} %get-tuple-element.15), channel_id=1, source_target_pairs={{16,8},{20,12},{24,16},{28,20},{17,9},{21,13},{25,17},{29,21},{18,... | collective-permute-start | bytes 393224 | tf_op jit(solution)/shard_map/ppermute | solution.py:164
  117.2 21.2 %collective-permute-start.18 = (f32[128,256]{1,0:T(8,128)S(1)}, f32[128,256]{1,0:T(8,128)S(1)}, u32[]{:S(2)}, u32[]{:S(2)}) collective-permute-start(f32[128,256]{1,0:T(8,128)S(1)} %get-tuple-element.14), channel_id=1, source_target_pairs={{0,8},{4,12},{8,16},{12,20},{16,24},{20,28},{1,9},{5,13},{9,17},{1... | collective-permute-start | bytes 393224 | tf_op jit(solution)/shard_map/ppermute | solution.py:164
  120.4 7.2 %collective-permute-start.9 = (f32[128,256]{1,0:T(8,128)S(1)}, f32[128,256]{1,0:T(8,128)S(1)}, u32[]{:S(2)}, u32[]{:S(2)}) collective-permute-start(f32[128,256]{1,0:T(8,128)S(1)} %get-tuple-element.19), channel_id=1, source_target_pairs={{16,8},{20,12},{24,16},{28,20},{17,9},{21,13},{25,17},{29,21},{18,... | collective-permute-start | bytes 393224 | tf_op jit(solution)/shard_map/ppermute | solution.py:164
  121.1 17.3 %collective-permute-start.7 = (f32[128,256]{1,0:T(8,128)S(1)}, f32[128,256]{1,0:T(8,128)S(1)}, u32[]{:S(2)}, u32[]{:S(2)}) collective-permute-start(f32[128,256]{1,0:T(8,128)S(1)} %get-tuple-element.18), channel_id=1, source_target_pairs={{0,8},{4,12},{8,16},{12,20},{16,24},{20,28},{1,9},{5,13},{9,17},{1... | collective-permute-start | bytes 393224 | tf_op jit(solution)/shard_map/ppermute | solution.py:164
  126.3 12.1 %collective-permute-start.21 = (f32[128,256]{1,0:T(8,128)S(1)}, f32[128,256]{1,0:T(8,128)S(1)}, u32[]{:S(2)}, u32[]{:S(2)}) collective-permute-start(f32[128,256]{1,0:T(8,128)S(1)} %bitcast_add_fusion.5), channel_id=1, source_target_pairs={{8,0},{12,4},{16,8},{20,12},{24,16},{28,20},{9,1},{13,5},{17,9},{2... | collective-permute-start | bytes 393224 | tf_op jit(solution)/shard_map/ppermute | solution.py:164
  127.6 10.7 %collective-permute-start.10 = (f32[128,256]{1,0:T(8,128)S(1)}, f32[128,256]{1,0:T(8,128)S(1)}, u32[]{:S(2)}, u32[]{:S(2)}) collective-permute-start(f32[128,256]{1,0:T(8,128)S(1)} %bitcast_add_fusion.10), channel_id=1, source_target_pairs={{8,0},{12,4},{16,8},{20,12},{24,16},{28,20},{9,1},{13,5},{17,9},{2... | collective-permute-start | bytes 393224 | tf_op jit(solution)/shard_map/ppermute | solution.py:164
  (7 other events, 17.3 us)

commit v2 on v1

v2 whole, which is shorter than its diff:
```python
import functools

import jax
import jax.numpy as jnp
from jax import lax
from jax.experimental import pallas as pl
from jax.experimental.pallas import tpu as pltpu
from jax.sharding import PartitionSpec as P

HALF = 256
NEWTON = 8
BOTH = ("scen", "row")
F32 = jnp.float32
BF16 = jnp.bfloat16


def halves(a):
    high = a.astype(BF16)
    low = (a - high.astype(F32)).astype(BF16)
    return high, low


def left_of(a):
    high, low = halves(a)
    return jnp.concatenate([high, high, low], axis=1)


def right_of(b):
    high, low = halves(b)
    return jnp.concatenate([high, low, high], axis=0)


def dot(a, b):
    return jnp.dot(a, b, preferred_element_type=F32)


def product(a, b):
    return dot(left_of(a), right_of(b))


def newton(pivot):
    size = jnp.abs(pivot)
    norm_one = jnp.max(jnp.sum(size, axis=0, keepdims=True))
    norm_inf = jnp.max(jnp.sum(size, axis=1, keepdims=True))
    approx = pivot.T / (norm_one * norm_inf)
    pivot_right = right_of(pivot)
    for step in range(NEWTON):
        left = dot(left_of(approx), pivot_right)
        approx = 2.0 * approx - product(left, approx)
    return approx


def first_kernel(pivot_ref, inverse_ref):
    inverse_ref[...] = newton(pivot_ref[...])


def second_kernel(inverse_first_ref, upper_ref, lower_ref, corner_ref, inverse_ref):
    lower_factor = product(lower_ref[...], inverse_first_ref[...])
    inverse_ref[...] = newton(corner_ref[...] - product(lower_factor, upper_ref[...]))


def factor_kernel(first_ref, second_ref, inverse_first_ref, inverse_second_ref, upper_ref, first_out, second_out):
    first_factor = product(first_ref[...], inverse_first_ref[...])
    updated = second_ref[...] - product(first_factor, upper_ref[...])
    first_out[...] = first_factor[:, None, :]
    second_out[...] = product(updated, inverse_second_ref[...])[:, None, :]


def in_vmem(kernel, out_shape, flops, *args):
    spec = pl.BlockSpec(memory_space=pltpu.VMEM)
    return pl.pallas_call(
        kernel,
        out_shape=out_shape,
        in_specs=[spec] * len(args),
        out_specs=jax.tree.map(lambda _: spec, out_shape),
        compiler_params=pltpu.CompilerParams(vmem_limit_bytes=24 * 1024 * 1024),
        cost_estimate=pl.CostEstimate(flops=flops, bytes_accessed=1 << 20, transcendentals=0),
    )(*args)


def swap(x, axis, bit):
    count = lax.axis_size(axis)
    return lax.ppermute(x, axis, [(i, i ^ bit) for i in range(count)])


def everyone(x, count):
    return jnp.broadcast_to(x[None], (count,) + x.shape)


def by_core(rows):
    scen = lax.axis_size("scen")
    return [[s * rows + r for s in range(c, scen, 2) for r in range(rows)] for c in range(2)]


def trade(x, axis, groups=None):
    return lax.all_to_all(x, axis, 0, 0, axis_index_groups=groups, tiled=True)


def sum_at_once(x):
    devices = lax.axis_size("scen") * lax.axis_size("row")
    rows = x.shape[0]
    if rows % (8 * devices):
        return lax.psum(x, BOTH)
    own = jnp.sum(trade(x.reshape(devices, rows // devices, -1), BOTH), axis=0)
    return trade(everyone(own, devices), BOTH).reshape(x.shape)


def sum_by_core(x):
    scen, row = lax.axis_size("scen"), lax.axis_size("row")
    rows, devices = x.shape[0], scen * row // 2
    if rows % (16 * devices):
        return lax.psum(x, BOTH)
    core = lax.axis_index("scen") % 2
    pair = x.reshape(2, rows // 2, -1)
    part = lax.dynamic_index_in_dim(pair, core, 0, keepdims=False)
    part = part + swap(lax.dynamic_index_in_dim(pair, 1 - core, 0, keepdims=False), "scen", 1)
    groups = by_core(row)
    own = jnp.sum(trade(part.reshape(devices, rows // 2 // devices, -1), BOTH, groups), axis=0)
    part = trade(everyone(own, devices), BOTH, groups).reshape(part.shape)
    other = swap(part, "scen", 1)
    return jnp.where(core == 0, jnp.concatenate([part, other]), jnp.concatenate([other, part]))


def scatter_sum(x):
    scen = lax.axis_size("scen")
    core = lax.axis_index("scen") % 2
    pieces = x.reshape(scen // 2, 2, x.shape[0] // scen, -1)
    mine = lax.dynamic_index_in_dim(pieces, core, 1, keepdims=False)
    theirs = lax.dynamic_index_in_dim(pieces, 1 - core, 1, keepdims=False)
    mine = mine + swap(theirs, "scen", 1)
    groups = [list(range(c, scen, 2)) for c in range(2)]
    return jnp.sum(trade(mine, "scen", groups), axis=0)


def shards(coupling, solves, border_diagonal, panel_rows):
    half = HALF
    coupling, solves = coupling[0], solves[0]
    local, row_count = coupling.shape
    panel = solves.shape[1]
    scen, rows = lax.axis_size("scen"), lax.axis_size("row")
    row = lax.axis_index("row")
    share = row_count // scen
    base = row * row_count + lax.axis_index("scen") * share

    solves_first = trade(everyone(solves[:, :half], rows), "row").reshape(local, half)
    solves_second = trade(everyone(solves[:, half:], rows), "row").reshape(local, panel - half)

    coupling_t = coupling.T
    columns = row * row_count + jnp.arange(row_count, dtype=jnp.int32)
    chosen = (panel_rows[:, None] == columns[None, :]).astype(BF16)
    picked = dot(chosen, coupling_t).astype(BF16)

    glob = base + jnp.arange(share, dtype=jnp.int32)
    at_diagonal = panel_rows[:, None] == glob[None, :]
    diagonal = jnp.sum(jnp.where(at_diagonal, border_diagonal[:, 0][None, :], F32(0.0)), axis=1)
    on_diagonal = jnp.where(jnp.eye(panel, dtype=bool), diagonal[:, None], F32(0.0))

    pivots_left = dot(picked, solves_first) + on_diagonal[:, :half]
    pivots_right = dot(picked, solves_second) + on_diagonal[:, half:]
    pivot_first = sum_at_once(pivots_left[:half])
    rest = sum_by_core(jnp.concatenate([pivots_left[half:], pivots_right]))
    lower, upper, corner = rest[:half], rest[half:2 * half], rest[2 * half:]

    diag_part = jnp.where(at_diagonal.T, border_diagonal[:, 0][:, None], F32(0.0))
    solves_all = jnp.concatenate([solves_first, solves_second], axis=1)
    own_rows = scatter_sum(dot(coupling_t, solves_all)) + diag_part
    first, second = own_rows[:, :half], own_rows[:, half:]

    square = jax.ShapeDtypeStruct((half, half), F32)
    inverse_first = in_vmem(first_kernel, square, 2 * 16 * 3 * half**3, pivot_first)
    inverse_second = in_vmem(second_kernel, square, 2 * 18 * 3 * half**3, inverse_first, upper, lower, corner)
    out = jax.ShapeDtypeStruct((share, 1, half), F32)
    return in_vmem(
        factor_kernel, (out, out), 2 * 9 * share * half**2, first, second, inverse_first, inverse_second, upper
    )


def solution(mesh):
    placed = (P("scen", None, "row"), P("scen", "row", None), P("scen", "row"), P())
    return jax.shard_map(
        shards,
        mesh=mesh,
        in_specs=placed,
        out_specs=(P("scen", "row", None), P("scen", "row", None)),
        check_vma=False,
    )
```

time: 142 us -> 148 us (1.042)
  starting transfers between devices: 77.2 us -> 32.6 us
  waiting for transfers between devices: 23 us -> 54.7 us
  local copies, waits for them, and re-layouts: 8.05 us -> 23.6 us
  other arithmetic: 8.43 us -> 11.7 us
  matrix products: 11 us -> 12.9 us
    all_to_all x2 -> x7, waiting for transfers between devices: 0.01 us -> 54.7 us  [trade(): return lax.all_to_all(x, axis, 0, 0, axis_index_groups=groups, tiled=True)]
    ppermute x38 -> x3, starting transfers between devices: 43.3 us -> 0.08 us  [swap(): return lax.ppermute(x, axis, [(i, i ^ bit) for i in range(count)])]
    ppermute x12 -> x0, starting transfers between devices: 25.4 us -> none  [scatter_sum(): carried = lax.ppermute(sent, 'scen', pairs)]
    all_to_all x2 -> x7, starting transfers between devices: 8.45 us -> 32.6 us  [trade(): return lax.all_to_all(x, axis, 0, 0, axis_index_groups=groups, tiled=True)]
    ppermute x38 -> x3, waiting for transfers between devices: 23 us -> 0.01 us  [swap(): return lax.ppermute(x, axis, [(i, i ^ bit) for i in range(count)])]
    unnamed x38 -> x28, local copies, waits for them, and re-layouts: 0.69 us -> 5.26 us
    dynamic_slice x1 -> x2, local copies, waits for them, and re-layouts: 2.2 us -> 6.43 us  [the longest x1 5.37 us: scatter_sum(): mine = lax.dynamic_index_in_dim(pieces, core, 1, keepdims=False)]
    reduce_sum x1 -> x3, other arithmetic: 0.04 us -> 4.06 us  [the longest x1 2.04 us: scatter_sum(): return jnp.sum(trade(mine, 'scen', groups), axis=0)]
  transfers between devices with their start and end apart: 52 -> 10, of which waited for: 15 -> 6; matrix products, arithmetic and copies ran while one was open for 18% -> 21% of each run, Pallas kernels for 7% -> 6%
where the time goes in v2:
time: 148 us; the launch traced here: 147 us
  waiting for transfers between devices  54.7 us (37%)
  starting transfers between devices  32.6 us (22%)
  local copies, waits for them, and re-layouts  23.6 us (16%)
  matrix products  12.9 us (9%)
  other arithmetic  11.7 us (8%)
  Pallas kernels  10.5 us (7%)
    all_to_all x7, waiting for transfers between devices, trade(): return lax.all_to_all(x, axis, 0, 0, axis_index_groups=groups, tiled=True)  54.7 us
    all_to_all x7, starting transfers between devices, trade(): return lax.all_to_all(x, axis, 0, 0, axis_index_groups=groups, tiled=True)  32.6 us
    dot_general x4, matrix products, dot(): return jnp.dot(a, b, preferred_element_type=F32)  12.9 us
    pallas_call x3, Pallas kernels, in_vmem(): pl.pallas_call(kernel, out_shape=out_shape, in_specs=[spec] * len(args),...  10.5 us
    dynamic_slice x1, local copies, waits for them, and re-layouts, scatter_sum(): mine = lax.dynamic_index_in_dim(pieces, core, 1, keepdims=False)  5.37 us
    unnamed x28, local copies, waits for them, and re-layouts  5.26 us
    reshape x1, local copies, waits for them, and re-layouts, scatter_sum(): pieces = x.reshape(scen // 2, 2, x.shape[0] // scen, -1)  3.99 us
    broadcast_in_dim x4, local copies, waits for them, and re-layouts, everyone(): return jnp.broadcast_to(x[None], (count,) + x.shape)  3.4 us
  transfers between devices with their start and end apart: 10, of which 6 were waited for; matrix products, arithmetic and copies ran while one was open for 21% of the time, Pallas kernels for 6%

profile of v2, /device:TPU:0, one launch (start us, length us, event | category | flops | bytes accessed | tf_op | source)
XLA Modules:
  0.0 147.0 jit_solution(15962826128415805725)
XLA Ops:
  0.6 0.0 copy-start
  0.6 0.0 copy-start.10
  0.7 1.2 fusion.20
  1.9 0.9 broadcast_in_dim.68
  2.8 5.2 %all-to-all-start.1 = ((bf16[4,384,256]{2,1,0:T(8,128)(2,1)}), bf16[4,384,256]{2,1,0:T(8,128)(2,1)}, u32[]{:S(2)}, u32[]{:S(2)}) async-start(bf16[4,384,256]{2,1,0:T(8,128)(2,1)} %broadcast_in_dim.68), calls=%async_computation.1 | async-start | bytes 1572864 | tf_op jit(solution)/shard_map/all_to_all | solution.py:96
  8.0 0.0 copy-done
  8.0 0.0 copy-done.10
  8.0 3.0 %fusion.4 = bf16[512,1536]{1,0:T(8,128)(2,1)} fusion(bf16[1,1536,1024]{2,1,0:T(8,128)(2,1)S(1)} %copy-done, s32[1024]{0:T(1024)S(1)} %iota_add_fusion, s32[512]{0:T(512)S(1)} %copy-done.10), kind=kOutput, calls=%fused_computation.4 | convolution fusion | flops 1611923456 | bytes 4724736 | tf_op jit(solution)/shard_map/dot_general | solution.py:34
  11.0 8.4 %all-to-all-done.1 = bf16[4,384,256]{2,1,0:T(8,128)(2,1)} async-done(((bf16[4,384,256]{2,1,0:T(8,128)(2,1)}), bf16[4,384,256]{2,1,0:T(8,128)(2,1)}, u32[]{:S(2)}, u32[]{:S(2)}) %all-to-all-start.1) | async-done | bytes 786464 | tf_op jit(solution)/shard_map/all_to_all | solution.py:96
  19.4 0.9 broadcast_in_dim.67
  20.3 4.2 %all-to-all-start = ((bf16[4,384,256]{2,1,0:T(8,128)(2,1)}), bf16[4,384,256]{2,1,0:T(8,128)(2,1)}, u32[]{:S(2)}, u32[]{:S(2)}) async-start(bf16[4,384,256]{2,1,0:T(8,128)(2,1)} %broadcast_in_dim.67), calls=%async_computation | async-start | bytes 1572864 | tf_op jit(solution)/shard_map/all_to_all | solution.py:96
  24.5 0.0 copy-done.12
  24.5 0.2 select_reduce_fusion
  24.8 0.2 fusion.16
  25.0 1.0 copy-done.5
  25.9 3.0 %convolution_add_fusion = f32[512,256]{1,0:T(8,128)} fusion(bf16[512,1536]{1,0:T(8,128)(2,1)} %fusion.4, bf16[1536,256]{1,0:T(8,128)(2,1)} %bitcast.2, f32[512,512]{1,0:T(8,128)S(1)} %fusion.16), kind=kOutput, calls=%fused_computation.10 | convolution fusion | flops 402784256 | bytes 3407872 | tf_op jit(solution)/shard_map/dot_general | solution.py:34
  28.9 6.1 %all-to-all-done = bf16[4,384,256]{2,1,0:T(8,128)(2,1)} async-done(((bf16[4,384,256]{2,1,0:T(8,128)(2,1)}), bf16[4,384,256]{2,1,0:T(8,128)(2,1)}, u32[]{:S(2)}, u32[]{:S(2)}) %all-to-all-start) | async-done | bytes 786464 | tf_op jit(solution)/shard_map/all_to_all | solution.py:96
  35.1 2.4 %convolution_add_fusion.1 = f32[512,256]{1,0:T(8,128)S(1)} fusion(bf16[512,1536]{1,0:T(8,128)(2,1)} %fusion.4, bf16[1536,256]{1,0:T(8,128)(2,1)} %bitcast.1, f32[512,512]{1,0:T(8,128)} %copy-done.5), kind=kOutput, calls=%fused_computation.11 | convolution fusion | flops 402784256 | bytes 3407872 | tf_op jit(solution)/shard_map/dot_general | solution.py:34
  37.5 0.7 fusion.19
  38.2 0.1 pad_maximum_fusion
  38.3 0.9 copy-done.6
  39.1 0.8 dynamic-slice_bitcast_fusion
  39.9 0.0 collective-permute-start.1
  39.9 5.0 %all-to-all-start.3 = ((f32[32,8,256]{2,1,0:T(8,128)}), f32[32,8,256]{2,1,0:T(8,128)S(1)}, u32[]{:S(2)}, u32[]{:S(2)}) async-start(f32[32,8,256]{2,1,0:T(8,128)} %get-tuple-element.8), calls=%async_computation.3 | async-start | bytes 524288 | tf_op jit(solution)/shard_map/all_to_all | solution.py:96
  45.0 0.0 collective-permute-done.1
  45.0 1.9 %bitcast_add_fusion.1 = f32[384,256]{1,0:T(8,128)} fusion(f32[384,256]{1,0:T(8,128)} %collective-permute-done.1, f32[2,384,256]{2,1,0:T(8,128)} %bitcast.38, s32[]{:T(128)S(6)} %select_n.40), kind=kLoop, calls=%fused_computation.20 | loop fusion | flops 98304 | bytes 1179652 | tf_op jit(solution)/shard_map/add | solution.py:116
  46.9 9.0 %all-to-all-done.3 = f32[32,8,256]{2,1,0:T(8,128)S(1)} async-done(((f32[32,8,256]{2,1,0:T(8,128)}), f32[32,8,256]{2,1,0:T(8,128)S(1)}, u32[]{:S(2)}, u32[]{:S(2)}) %all-to-all-start.3) | async-done | bytes 262176 | tf_op jit(solution)/shard_map/all_to_all | solution.py:96
  55.9 0.7 copy-done.9
  56.6 3.6 %all-to-all-start.5 = ((f32[16,24,256]{2,1,0:T(8,128)}), f32[16,24,256]{2,1,0:T(8,128)S(1)}, u32[]{:S(2)}, u32[]{:S(2)}) async-start(f32[16,24,256]{2,1,0:T(8,128)} %bitcast.39), calls=%async_computation.5 | async-start | bytes 786432 | tf_op jit(solution)/shard_map/all_to_all | solution.py:96
  60.2 4.5 %fusion.8 = f32[1024,512]{0,1:T(8,128)} fusion(bf16[1,1536,1024]{2,1,0:T(8,128)(2,1)S(1)} %copy-done, bf16[1536,256]{1,0:T(8,128)(2,1)} %bitcast.2, bf16[1536,256]{1,0:T(8,128)(2,1)} %bitcast.1), kind=kOutput, calls=%fused_computation.6 | convolution fusion | flops 1613758464 | bytes 6815744 | tf_op jit(solution)/shard_map/dot_general | solution.py:34
  64.7 4.0 %reshape.45 = f32[4,2,128,512]{2,1,0,3:T(2,128)} reshape(f32[1024,512]{0,1:T(8,128)} %fusion.8) | data formatting | bytes 4194304 | tf_op jit(solution)/shard_map/reshape | solution.py:127
  68.7 5.4 %constant_dynamic-slice_fusion.1 = (f32[4,1,128,512]{2,1,0,3:T(1,128)}, f32[4,1,128,512]{2,1,0,3:T(1,128)S(1)}) fusion(f32[4,2,128,512]{2,1,0,3:T(2,128)} %reshape.45, s32[]{:T(128)S(6)} %select_n.40, s32[]{:T(128)S(6)} %select_n.41), kind=kLoop, calls=%fused_computation.27 | loop fusion | bytes 4194312 | tf_op jit(solution)/shard_map/jit(dynamic_index_in_dim)/dynamic_slice | solution.py:128
  74.1 1.1 copy.17
  75.1 0.0 collective-permute-start
  75.1 1.0 reduce_sum.38
  76.1 0.0 all-to-all-done.5
  76.1 0.8 broadcast_in_dim.76
  76.9 0.1 copy-done.8
  77.0 6.0 %all-to-all-start.4 = ((f32[32,8,256]{2,1,0:T(8,128)}), f32[32,8,256]{2,1,0:T(8,128)S(1)}, u32[]{:S(2)}, u32[]{:S(2)}) async-start(f32[32,8,256]{2,1,0:T(8,128)} %broadcast_in_dim.76), calls=%async_computation.4 | async-start | bytes 524288 | tf_op jit(solution)/shard_map/all_to_all | solution.py:96
  82.9 1.0 reduce_sum.39
  84.0 9.9 %all-to-all-done.4 = f32[32,8,256]{2,1,0:T(8,128)S(1)} async-done(((f32[32,8,256]{2,1,0:T(8,128)}), f32[32,8,256]{2,1,0:T(8,128)S(1)}, u32[]{:S(2)}, u32[]{:S(2)}) %all-to-all-start.4) | async-done | bytes 262176 | tf_op jit(solution)/shard_map/all_to_all | solution.py:96
  93.9 0.8 broadcast_in_dim.77
  94.7 4.2 %all-to-all-start.6 = ((f32[16,24,256]{2,1,0:T(8,128)}), f32[16,24,256]{2,1,0:T(8,128)}, u32[]{:S(2)}, u32[]{:S(2)}) async-start(f32[16,24,256]{2,1,0:T(8,128)} %broadcast_in_dim.77), calls=%async_computation.6 | async-start | bytes 786432 | tf_op jit(solution)/shard_map/all_to_all | solution.py:96
  98.9 0.0 collective-permute-done
  98.9 2.6 %bitcast_add_fusion = f32[4,128,512]{1,2,0:T(8,128)} fusion(f32[4,128,512]{1,2,0:T(8,128)} %collective-permute-done, f32[4,1,128,512]{2,1,0,3:T(1,128)} %get-tuple-element.2), kind=kLoop, calls=%fused_computation.12 | loop fusion | flops 262144 | bytes 3145728 | tf_op jit(solution)/shard_map/add | solution.py:130
  101.5 9.6 %all-to-all-done.6 = f32[16,24,256]{2,1,0:T(8,128)} async-done(((f32[16,24,256]{2,1,0:T(8,128)}), f32[16,24,256]{2,1,0:T(8,128)}, u32[]{:S(2)}, u32[]{:S(2)}) %all-to-all-start.6) | async-done | bytes 393248 | tf_op jit(solution)/shard_map/all_to_all | solution.py:96
  111.1 4.4 %all-to-all-start.2 = ((f32[4,128,512]{1,2,0:T(8,128)}), f32[4,128,512]{1,2,0:T(8,128)}, u32[]{:S(2)}, u32[]{:S(2)}) async-start(f32[4,128,512]{1,2,0:T(8,128)} %bitcast_add_fusion), calls=%async_computation.2 | async-start | bytes 2097152 | tf_op jit(solution)/shard_map/all_to_all | solution.py:96
  115.6 0.1 collective-permute-start.2
  115.7 4.3 %shard_map.59.inverse_first_ref = f32[256,256]{1,0:T(8,128)S(1)} custom-call(f32[256,256]{1,0:T(8,128)S(1)} %bitcast.36), custom_call_target="tpu_custom_call" | custom-call | flops 1610612736 | bytes 1048576 | tf_op jit(solution)/shard_map/pallas_call | solution.py:71
  120.0 0.0 copy-start.1
  120.0 0.0 collective-permute-done.2
  120.0 1.5 %maximum_select_fusion = f32[768,256]{1,0:T(8,128)S(1)} fusion(f32[384,256]{1,0:T(8,128)} %collective-permute-done.2, f32[384,256]{1,0:T(8,128)} %bitcast.14, pred[]{:T(512)S(6)} %eq.52), kind=kLoop, calls=%fused_computation.19 | loop fusion | flops 589824 | bytes 1572865 | tf_op jit(solution)/shard_map/jit(_where)/select_n | solution.py:121
  121.5 0.1 fusion.18
  121.6 0.0 copy-start.13
  121.6 4.9 %shard_map.60.inverse_second_ref = f32[256,256]{1,0:T(8,128)S(1)} custom-call(f32[256,256]{1,0:T(8,128)S(1)} %shard_map.59.inverse_first_ref, f32[256,256]{1,0:T(8,128)S(1)} %get-tuple-element.6.upper_ref, f32[256,256]{1,0:T(8,128)S(1)} %get-tuple-element.5.lower_ref, f32[256,256]{1,0:T(8,128)S(1)} %get-tuple-element.4.corner_ref), custom_call_target="tpu_custom_call" | custom-call | flops 1811939328 | bytes 1048576 | tf_op jit(solution)/shard_map/pallas_call | solution.py:71
  126.5 0.0 copy-start.3
  126.5 0.7 copy-done.3
  127.2 11.7 %all-to-all-done.2 = f32[4,128,512]{1,2,0:T(8,128)} async-done(((f32[4,128,512]{1,2,0:T(8,128)}), f32[4,128,512]{1,2,0:T(8,128)}, u32[]{:S(2)}, u32[]{:S(2)}) %all-to-all-start.2) | async-done | bytes 1048608 | tf_op jit(solution)/shard_map/all_to_all | solution.py:96
  138.9 2.0 %reduce_sum.36 = f32[128,512]{0,1:T(8,128)} reduce(f32[4,128,512]{1,2,0:T(8,128)} %all-to-all-done.2, f32[]{:T(128)} %constant.42.clone.1), dimensions={0}, to_apply=%region_0.1 | reduce | flops 196608 | bytes 1310724 | tf_op jit(solution)/shard_map/reduce_sum | solution.py:132
  140.9 1.8 %copy.13 = f32[128,512]{1,0:T(8,128)} copy(f32[128,512]{0,1:T(8,128)} %reduce_sum.36) | data formatting | bytes 524288 | tf_op jit(solution)/shard_map/reduce_sum | solution.py:132
  142.7 1.1 select_add_fusion
  143.8 0.9 copy-done.2
  144.8 0.9 copy-done.4
  145.7 1.3 shard_map.61
  (16 shorter events, 0.1 us)
Async XLA Ops:
  0.6 7.4 %copy-start = (bf16[1,1536,1024]{2,1,0:T(8,128)(2,1)S(1)}, bf16[1,1536,1024]{2,1,0:T(8,128)(2,1)}, u32[]{:S(2)}) copy-start(bf16[1,1536,1024]{2,1,0:T(8,128)(2,1)} %param.4) | copy-start | bytes 9437188
  0.6 7.3 %copy-start.10 = (s32[512]{0:T(512)S(1)}, s32[512]{0:T(512)}, u32[]{:S(2)}) copy-start(s32[512]{0:T(512)} %param.7) | copy-start | bytes 6148
  2.8 16.6 %all-to-all-start.1 = ((bf16[4,384,256]{2,1,0:T(8,128)(2,1)}), bf16[4,384,256]{2,1,0:T(8,128)(2,1)}, u32[]{:S(2)}, u32[]{:S(2)}) async-start(bf16[4,384,256]{2,1,0:T(8,128)(2,1)} %broadcast_in_dim.68), calls=%async_computation.1 | async-start | bytes 1572864 | tf_op jit(solution)/shard_map/all_to_all | solution.py:96
  8.0 16.5 %copy-start.12 = (s32[128]{0:T(128)}, s32[128]{0:T(128)S(1)}, u32[]{:S(2)}) copy-start(s32[128]{0:T(128)S(1)} %iota_add_fusion.1) | copy-start | bytes 1540
  11.0 13.5 %copy-start.11 = (f32[128,1]{0,1:T(1,128)S(1)}, f32[128,1]{0,1:T(1,128)}, u32[]{:S(2)}) copy-start(f32[128,1]{0,1:T(1,128)} %param.6) | copy-start | bytes 1540
  20.3 14.8 %all-to-all-start = ((bf16[4,384,256]{2,1,0:T(8,128)(2,1)}), bf16[4,384,256]{2,1,0:T(8,128)(2,1)}, u32[]{:S(2)}, u32[]{:S(2)}) async-start(bf16[4,384,256]{2,1,0:T(8,128)(2,1)} %broadcast_in_dim.67), calls=%async_computation | async-start | bytes 1572864 | tf_op jit(solution)/shard_map/all_to_all | solution.py:96
  24.9 1.0 copy-start.5
  35.1 3.1 %copy-start.7 = (f32[512,256]{1,0:T(8,128)S(1)}, f32[512,256]{1,0:T(8,128)}, u32[]{:S(2)}) copy-start(f32[512,256]{1,0:T(8,128)} %convolution_add_fusion) | copy-start | bytes 1572868
  38.3 0.9 copy-start.6
  39.9 5.1 %collective-permute-start.1 = (f32[384,256]{1,0:T(8,128)}, f32[384,256]{1,0:T(8,128)}, u32[]{:S(2)}, u32[]{:S(2)}) collective-permute-start(f32[384,256]{1,0:T(8,128)} %dynamic-slice_bitcast_fusion), channel_id=1, source_target_pairs={{0,4},{4,0},{8,12},{12,8},{16,20},{20,16},{24,28},{28,24},{1,5},{5... | collective-permute-start | bytes 1179656 | tf_op jit(solution)/shard_map/ppermute | solution.py:83
  39.9 16.0 %all-to-all-start.3 = ((f32[32,8,256]{2,1,0:T(8,128)}), f32[32,8,256]{2,1,0:T(8,128)S(1)}, u32[]{:S(2)}, u32[]{:S(2)}) async-start(f32[32,8,256]{2,1,0:T(8,128)} %get-tuple-element.8), calls=%async_computation.3 | async-start | bytes 524288 | tf_op jit(solution)/shard_map/all_to_all | solution.py:96
  55.9 0.7 copy-start.9
  56.6 19.5 %all-to-all-start.5 = ((f32[16,24,256]{2,1,0:T(8,128)}), f32[16,24,256]{2,1,0:T(8,128)S(1)}, u32[]{:S(2)}, u32[]{:S(2)}) async-start(f32[16,24,256]{2,1,0:T(8,128)} %bitcast.39), calls=%async_computation.5 | async-start | bytes 786432 | tf_op jit(solution)/shard_map/all_to_all | solution.py:96
  75.1 23.8 %collective-permute-start = (f32[4,128,512]{1,2,0:T(8,128)}, f32[4,128,512]{1,2,0:T(8,128)}, u32[]{:S(2)}, u32[]{:S(2)}) collective-permute-start(f32[4,128,512]{1,2,0:T(8,128)} %bitcast.35), channel_id=1, source_target_pairs={{0,4},{4,0},{8,12},{12,8},{16,20},{20,16},{24,28},{28,24},{1,5},{5... | collective-permute-start | bytes 3145736 | tf_op jit(solution)/shard_map/ppermute | solution.py:83
  76.1 0.8 copy-start.8
  77.0 16.9 %all-to-all-start.4 = ((f32[32,8,256]{2,1,0:T(8,128)}), f32[32,8,256]{2,1,0:T(8,128)S(1)}, u32[]{:S(2)}, u32[]{:S(2)}) async-start(f32[32,8,256]{2,1,0:T(8,128)} %broadcast_in_dim.76), calls=%async_computation.4 | async-start | bytes 524288 | tf_op jit(solution)/shard_map/all_to_all | solution.py:96
  94.7 16.5 %all-to-all-start.6 = ((f32[16,24,256]{2,1,0:T(8,128)}), f32[16,24,256]{2,1,0:T(8,128)}, u32[]{:S(2)}, u32[]{:S(2)}) async-start(f32[16,24,256]{2,1,0:T(8,128)} %broadcast_in_dim.77), calls=%async_computation.6 | async-start | bytes 786432 | tf_op jit(solution)/shard_map/all_to_all | solution.py:96
  111.1 27.8 %all-to-all-start.2 = ((f32[4,128,512]{1,2,0:T(8,128)}), f32[4,128,512]{1,2,0:T(8,128)}, u32[]{:S(2)}, u32[]{:S(2)}) async-start(f32[4,128,512]{1,2,0:T(8,128)} %bitcast_add_fusion), calls=%async_computation.2 | async-start | bytes 2097152 | tf_op jit(solution)/shard_map/all_to_all | solution.py:96
  115.6 4.4 %collective-permute-start.2 = (f32[384,256]{1,0:T(8,128)}, f32[384,256]{1,0:T(8,128)}, u32[]{:S(2)}, u32[]{:S(2)}) collective-permute-start(f32[384,256]{1,0:T(8,128)} %bitcast.14), channel_id=1, source_target_pairs={{0,4},{4,0},{8,12},{12,8},{16,20},{20,16},{24,28},{28,24},{1,5},{5... | collective-permute-start | bytes 1179656 | tf_op jit(solution)/shard_map/ppermute | solution.py:83
  120.0 1.6 %copy-start.1 = (f32[256,256]{1,0:T(8,128)}, f32[256,256]{1,0:T(8,128)S(1)}, u32[]{:S(2)}) copy-start(f32[256,256]{1,0:T(8,128)S(1)} %shard_map.59.inverse_first_ref) | copy-start | bytes 786436
  121.6 21.1 %copy-start.13 = (s32[128]{0:T(128)S(1)}, s32[128]{0:T(128)}, u32[]{:S(2)}) copy-start(s32[128]{0:T(128)} %copy-done.12) | copy-start | bytes 1540
  126.5 0.7 copy-start.3
  143.8 1.0 copy-start.2
  144.8 0.9 copy-start.4

commit v3 on v2

v3 whole, which is shorter than its diff:
```python
import functools

import jax
import jax.numpy as jnp
from jax import lax
from jax.experimental import pallas as pl
from jax.experimental.pallas import tpu as pltpu
from jax.sharding import PartitionSpec as P

HALF = 256
NEWTON = 8
TAIL = 16
LEVELS = 32000.0
F32 = jnp.float32
BF16 = jnp.bfloat16
I16 = jnp.int16


def halves(a):
    high = a.astype(BF16)
    low = (a - high.astype(F32)).astype(BF16)
    return high, low


def left_of(a):
    high, low = halves(a)
    return jnp.concatenate([high, high, low], axis=1)


def right_of(b):
    high, low = halves(b)
    return jnp.concatenate([high, low, high], axis=0)


def dot(a, b):
    return jnp.dot(a, b, preferred_element_type=F32)


def product(a, b):
    return dot(left_of(a), right_of(b))


def newton(pivot):
    size = jnp.abs(pivot)
    norm_one = jnp.max(jnp.sum(size, axis=0, keepdims=True))
    norm_inf = jnp.max(jnp.sum(size, axis=1, keepdims=True))
    approx = pivot.T / (norm_one * norm_inf)
    pivot_right = right_of(pivot)
    for step in range(NEWTON):
        left = dot(left_of(approx), pivot_right)
        approx = 2.0 * approx - product(left, approx)
    return approx


def aligned(index, size):
    return pl.multiple_of(index * size, size)


def encode(values, out_ref, base, diagonal=None):
    rows, lanes = values.shape
    top = jnp.maximum(jnp.max(jnp.abs(values), axis=0, keepdims=True), F32(1e-30))
    power = jnp.ceil(jnp.log2(top))
    unit = jnp.exp2(power)
    mantissa = jnp.ceil(top / unit * F32(16384.0))
    scale = mantissa * unit * F32(1.0 / (16384.0 * LEVELS))
    codes = jnp.round(values * (F32(1.0) / scale)).astype(jnp.int32)
    out_ref[base:base + rows, :] = codes.astype(I16)
    row = lax.broadcasted_iota(jnp.int32, (TAIL, lanes), 0)
    tail = jnp.where(row == 0, power, jnp.where(row == 1, mantissa, F32(0.0)))
    if diagonal is not None:
        coarse = jnp.floor(diagonal * F32(64.0))
        fine = (diagonal * F32(64.0) - coarse) * F32(4096.0)
        tail = jnp.where(row == 2, coarse, jnp.where(row == 3, fine, tail))
    out_ref[base + rows:base + rows + TAIL, :] = tail.astype(jnp.int32).astype(I16)


def decode(ref, base, rows):
    tail = ref[base + rows:base + rows + TAIL, :].astype(jnp.int32).astype(F32)
    scale = tail[1:2] * jnp.exp2(tail[0:1]) * F32(1.0 / (16384.0 * LEVELS))
    diagonal = tail[2:3] * F32(1.0 / 64.0) + tail[3:4] * F32(1.0 / (64.0 * 4096.0))
    return ref[base:base + rows, :].astype(jnp.int32).astype(F32) * scale, diagonal


def turn_kernel(solves_ref, upper_ref, lower_ref):
    turned = solves_ref[...].T
    half = upper_ref.shape[0]
    upper_ref[...] = turned[:half]
    lower_ref[...] = turned[half:]


def pick_kernel(place_ref, panel_ref, own_diagonal_ref, coupling_ref, chosen_ref, entry_ref):
    first_column, first_row = place_ref[0], place_ref[1]
    panel = panel_ref.shape[1]
    columns, share = coupling_ref.shape[1], own_diagonal_ref.shape[1]
    here = panel_ref[...] - first_column == lax.broadcasted_iota(jnp.int32, (columns, panel), 0)
    chosen = jnp.where(here, F32(1.0), F32(0.0)).astype(BF16)
    chosen_ref[...] = dot(coupling_ref[...], chosen).astype(BF16)
    owned = panel_ref[...] - first_row == lax.broadcasted_iota(jnp.int32, (share, panel), 0)
    own = jnp.broadcast_to(own_diagonal_ref[...], (8, share)).T[:, :1]
    entry = jnp.sum(jnp.where(owned, own, F32(0.0)), axis=0, keepdims=True)
    entry_ref[...] = jnp.broadcast_to(entry, entry_ref.shape)


def terms_kernel(rows, place_ref, chosen_ref, entry_ref, *refs):
    *pieces, turned_ref, keep_ref, send_ref, all_ref = refs
    row, core = place_ref[0], place_ref[1]
    if len(pieces) == 1:
        turned_ref[...] = pieces[0][...]
    else:
        half, width = pieces[0].shape
        for i, piece in enumerate(pieces):
            turned_ref[i % 2 * half:(i % 2 + 1) * half, pl.ds(aligned(row ^ (i // 2), width), width)] = piece[...]
    all_ref[...] = dot(turned_ref[...], chosen_ref[...])
    size = keep_ref.shape[0] // rows
    for out_ref, whose in ((keep_ref, core), (send_ref, 1 - core)):
        for k in range(rows):
            out_ref[k * size:(k + 1) * size, :] = all_ref[pl.ds(aligned(whose * rows + (row ^ k), size), size), :]
    send_ref[rows * size:, :] = entry_ref[...]


def pair_kernel(rows, keep_ref, got_ref, entry_ref, *out_refs):
    size = keep_ref.shape[0] // rows
    entry = entry_ref[:1, :] + got_ref[rows * size:rows * size + 1, :]
    for k, out_ref in enumerate(out_refs):
        part = slice(k * size, (k + 1) * size)
        encode(keep_ref[part, :] + got_ref[part, :], out_ref, 0, entry)


def sum_kernel(*refs):
    *in_refs, out_ref = refs
    size = out_ref.shape[0] - TAIL
    parts = [decode(ref, 0, size) for ref in in_refs]
    encode(sum(p[0] for p in parts), out_ref, 0, sum(p[1] for p in parts))


def join_kernel(*refs):
    *in_refs, out_ref = refs
    size = in_refs[0].shape[0]
    for k, ref in enumerate(in_refs):
        out_ref[k * size:(k + 1) * size, :] = ref[...]


def first_kernel(rows, place_ref, own_ref, other_ref, inverse_ref, pivots_ref):
    row, core = place_ref[0], place_ref[1]
    panel = pivots_ref.shape[0]
    size = panel // (2 * rows)
    index = lax.broadcasted_iota(jnp.int32, (size, panel), 1)
    for ref, whose in ((own_ref, core), (other_ref, 1 - core)):
        for k in range(rows):
            start = aligned(whose * rows + (row ^ k), size)
            values, diagonal = decode(ref, k * (size + TAIL), size)
            at = lax.broadcasted_iota(jnp.int32, (size, panel), 0) + start == index
            pivots_ref[pl.ds(start, size), :] = values + jnp.where(at, diagonal, F32(0.0))
    half = inverse_ref.shape[0]
    inverse_ref[...] = newton(pivots_ref[:half, :half])


def second_kernel(pivots_ref, inverse_first_ref, inverse_ref):
    half = inverse_ref.shape[0]
    lower_factor = product(inverse_first_ref[...], pivots_ref[:half, half:])
    inverse_ref[...] = newton(pivots_ref[half:, half:] - product(pivots_ref[half:, :half], lower_factor))


def schur_kernel(place_ref, coupling_ref, turned_ref, keep_ref, send_ref):
    core, layer = place_ref[1], place_ref[2]
    panel, share = turned_ref.shape[0], keep_ref.shape[1]
    layers = keep_ref.shape[0] // panel
    for position, k in enumerate(reversed_order(layers)):
        start = aligned(layer ^ k, 2 * share)
        both = dot(turned_ref[...], coupling_ref[:, pl.ds(start, 2 * share)])
        rows = slice(position * panel, (position + 1) * panel)
        one, two = both[:, :share], both[:, share:]
        keep_ref[rows, :] = jnp.where(core == 0, one, two)
        send_ref[rows, :] = jnp.where(core == 0, two, one)


def bulk_pair_kernel(panel, keep_ref, got_ref, own_ref, coded_ref):
    half = own_ref.shape[0]
    own_ref[...] = keep_ref[:half, :] + got_ref[:half, :]
    for i in range(half // panel):
        part = slice(half + i * panel, half + (i + 1) * panel)
        encode(keep_ref[part, :] + got_ref[part, :], coded_ref, i * (panel + TAIL))


def bulk_sum_kernel(panel, keep_ref, got_ref, own_ref, coded_ref):
    half = own_ref.shape[0]
    for i in range(keep_ref.shape[0] // panel):
        value = keep_ref[i * panel:(i + 1) * panel, :] + decode(got_ref, i * (panel + TAIL), panel)[0]
        if i * panel < half:
            own_ref[i * panel:(i + 1) * panel, :] = value
        else:
            encode(value, coded_ref, (i - half // panel) * (panel + TAIL))


def factor_kernel(
    place_ref, panel_ref, own_diagonal_ref, inverse_first_ref, inverse_second_ref, pivots_ref, rows_ref, *refs
):
    *got, first_out, second_out = refs
    panel, share = rows_ref.shape
    half = panel // 2
    turned = jnp.broadcast_to(panel_ref[...].astype(F32), (share, panel)).T.astype(jnp.int32)
    here = turned - place_ref[1] == lax.broadcasted_iota(jnp.int32, (panel, share), 1)
    rows = rows_ref[...] + jnp.where(here, own_diagonal_ref[...], F32(0.0))
    for ref in got:
        rows = rows + decode(ref, 0, panel)[0]
    first_factor = product(inverse_first_ref[...], rows[:half])
    updated = rows[half:] - product(pivots_ref[half:, :half], first_factor)
    first_out[...] = first_factor.T[:, None, :]
    second_out[...] = product(inverse_second_ref[...], updated).T[:, None, :]


def call(kernel, out_shape, *args, scratch=(), scalars=0, micros=0.0):
    vmem = pl.BlockSpec(memory_space=pltpu.VMEM)
    smem = pl.BlockSpec(memory_space=pltpu.SMEM)
    return pl.pallas_call(
        kernel,
        out_shape=out_shape,
        in_specs=[smem] * scalars + [vmem] * (len(args) - scalars),
        out_specs=jax.tree.map(lambda _: vmem, out_shape),
        scratch_shapes=scratch,
        compiler_params=pltpu.CompilerParams(vmem_limit_bytes=28 << 20),
        cost_estimate=pl.CostEstimate(flops=0, bytes_accessed=int(micros * 3.69e6) + 1024, transcendentals=0),
    )(*args)


def swap(x, axis, bit):
    count = lax.axis_size(axis)
    return lax.ppermute(x, axis, [(i, i ^ bit) for i in range(count)])


def after(x, *others):
    return lax.optimization_barrier((x,) + others)[0]


def bits_of(count):
    return [1 << i for i in range(count.bit_length() - 1)]


def reversed_order(count):
    width = count.bit_length() - 1
    return [int(f"{p:0{width}b}"[::-1], 2) for p in range(count)]


def gather_pieces(solves, rows, ready):
    block, panel = solves.shape
    if rows != 4:
        return [lax.all_gather(solves.T, "row", axis=1, tiled=True)]
    half = jax.ShapeDtypeStruct((panel // 2, block), BF16)
    upper, lower = call(turn_kernel, (half, half), solves)
    lower_x, upper_y = swap(lower, "row", 1), swap(upper, "row", 2)
    upper_x, lower_y = swap(upper, "row", 1), swap(lower, "row", 2)
    upper_far, lower_far = swap(after(upper_y, *ready), "row", 1), swap(after(lower_x, *ready), "row", 2)
    return [upper, lower, upper_x, lower_x, upper_y, lower_y, upper_far, lower_far]


def shards(coupling, solves, border_diagonal, panel_rows):
    half = HALF
    coupling, solves = coupling[0], solves[0]
    local, row_count = coupling.shape
    panel = solves.shape[1]
    scen, rows = lax.axis_size("scen"), lax.axis_size("row")
    layers = scen // 2
    row, place = lax.axis_index("row"), lax.axis_index("scen")
    share = row_count // scen
    size = panel // (2 * rows)
    shape = jax.ShapeDtypeStruct
    panel_row, diagonal_row = panel_rows[None, :], border_diagonal.T
    starts = jnp.stack([row * row_count, row * row_count + place * share]).astype(jnp.int32)
    at = jnp.stack([row, place % 2, place // 2]).astype(jnp.int32)

    chosen, entry = call(
        pick_kernel, (shape((local, panel), BF16), shape((8, panel), F32)),
        starts, panel_row, diagonal_row, coupling, scalars=1, micros=3.0,
    )
    pieces = gather_pieces(solves, rows, (entry,))
    turned, keep, send = call(
        functools.partial(terms_kernel, rows),
        (shape((panel, local), BF16), shape((panel // 2, panel), F32), shape((panel // 2 + 8, panel), F32)),
        at, chosen, entry, *pieces, scalars=1, scratch=[pltpu.VMEM((panel, panel), F32)],
    )
    coded = shape((size + TAIL, panel), I16)
    codes = call(
        functools.partial(pair_kernel, rows), (coded,) * rows, keep, swap(send, "scen", 1), entry
    )
    arrived = [swap(codes[k], "row", k) for k in range(1, rows)]

    if share % 128:
        terms = dot(turned, coupling)
        own, got = lax.psum_scatter(terms, "scen", scatter_dimension=1, tiled=True), []
        part = call(sum_kernel, coded, codes[0], *arrived)
        for bit in bits_of(layers):
            part = call(sum_kernel, coded, part, swap(part, "scen", 2 * bit))
    else:
        bulk = shape((layers * panel, share), F32)
        keep, send = call(schur_kernel, (bulk, bulk), at, coupling, after(turned, codes[0]), scalars=1)
        got = swap(send, "scen", 1)
        part = call(sum_kernel, coded, after(codes[0], keep), *arrived)
        steps = bits_of(layers)
        count = layers // 2
        own, bulk_codes = call(
            functools.partial(bulk_pair_kernel, panel),
            (shape((count * panel, share), F32), shape((count * (panel + TAIL), share), I16)),
            after(keep, part), got,
        )
        for bit in steps:
            other = swap(part, "scen", 2 * bit)
            part = call(sum_kernel, coded, after(part, bulk_codes), other)
        for bit in steps[:-1]:
            count //= 2
            own, bulk_codes = call(
                functools.partial(bulk_sum_kernel, panel),
                (shape((count * panel, share), F32), shape((count * (panel + TAIL), share), I16)),
                own, swap(after(bulk_codes, part), "scen", 2 * bit),
            )
        got = [swap(bulk_codes, "scen", layers)]

    joined = call(
        join_kernel, shape((rows * (size + TAIL), panel), I16), part, *[swap(part, "row", k) for k in range(1, rows)]
    )
    square = shape((half, half), F32)
    inverse_first, pivots = call(
        functools.partial(first_kernel, rows), (square, shape((panel, panel), F32)),
        at, joined, swap(joined, "scen", 1), scalars=1, micros=4.5,
    )
    inverse_second = call(second_kernel, square, pivots, inverse_first, micros=4.5)
    out = shape((share, 1, half), F32)
    return call(
        factor_kernel, (out, out),
        starts, panel_row, diagonal_row, inverse_first, inverse_second, pivots, own, *got, scalars=1,
    )


def solution(mesh):
    placed = (P("scen", None, "row"), P("scen", "row", None), P("scen", "row"), P())
    return jax.shard_map(
        shards,
        mesh=mesh,
        in_specs=placed,
        out_specs=(P("scen", "row", None), P("scen", "row", None)),
        check_vma=False,
    )
```

time: 148 us -> 70.1 us (0.47)
  waiting for transfers between devices: 54.7 us -> 20.2 us
  local copies, waits for them, and re-layouts: 23.6 us -> 4.23 us
  matrix products: 12.9 us -> 0 us
  other arithmetic: 11.7 us -> 0.15 us
  Pallas kernels: 10.5 us -> 19.7 us
  starting transfers between devices: 32.6 us -> 24.8 us
    all_to_all x7 -> x0, waiting for transfers between devices: 54.7 us -> none  [trade(): return lax.all_to_all(x, axis, 0, 0, axis_index_groups=groups, tiled=True)]
    all_to_all x7 -> x0, starting transfers between devices: 32.6 us -> none  [trade(): return lax.all_to_all(x, axis, 0, 0, axis_index_groups=groups, tiled=True)]
    ppermute x3 -> x19, starting transfers between devices: 0.08 us -> 24.8 us  [swap(): return lax.ppermute(x, axis, [(i, i ^ bit) for i in range(count)])]
    ppermute x3 -> x19, waiting for transfers between devices: 0.01 us -> 20.2 us  [swap(): return lax.ppermute(x, axis, [(i, i ^ bit) for i in range(count)])]
    dot_general x4 -> x0, matrix products: 12.9 us -> none  [dot(): return jnp.dot(a, b, preferred_element_type=F32)]
    pallas_call x3 -> x14, Pallas kernels: 10.5 us -> 19.7 us  [call(): pl.pallas_call(kernel, out_shape=out_shape, in_specs=[smem] * scalars + [...]
    dynamic_slice x2 -> x0, local copies, waits for them, and re-layouts: 6.43 us -> none  [the longest x1 5.37 us: scatter_sum(): mine = lax.dynamic_index_in_dim(pieces, core, 1, keepdims=False)]
    add x5 -> x0, other arithmetic: 5.63 us -> none  [the longest x1 2.65 us: scatter_sum(): mine = mine + swap(theirs, 'scen', 1)]
  transfers between devices with their start and end apart: 10 -> 19, of which waited for: 6 -> 13; matrix products, arithmetic and copies ran while one was open for 21% -> 0% of each run, Pallas kernels for 6% -> 19%
where the time goes in v3:
time: 70.1 us; the launch traced here: 69.9 us
  starting transfers between devices  24.8 us (35%)
  waiting for transfers between devices  20.2 us (29%)
  Pallas kernels  19.7 us (28%)
  local copies, waits for them, and re-layouts  4.23 us (6%)
  between operations  0.82 us (1%)
    ppermute x19, starting transfers between devices, swap(): return lax.ppermute(x, axis, [(i, i ^ bit) for i in range(count)])  24.8 us
    ppermute x19, waiting for transfers between devices, swap(): return lax.ppermute(x, axis, [(i, i ^ bit) for i in range(count)])  20.2 us
    pallas_call x14, Pallas kernels, call(): pl.pallas_call(kernel, out_shape=out_shape, in_specs=[smem] * scalars + [...  19.7 us
    unnamed x14, local copies, waits for them, and re-layouts  4.23 us
  transfers between devices with their start and end apart: 19, of which 13 were waited for; matrix products, arithmetic and copies ran while one was open for 0% of the time, Pallas kernels for 19%

profile of v3, /device:TPU:0, one launch (start us, length us, event | category | flops | bytes accessed | tf_op | source)
XLA Modules:
  0.0 69.9 jit_solution(14883122842582369146)
XLA Ops:
  0.6 0.0 copy-start.2
  0.6 1.0 %copy-done.2 = bf16[1,384,512]{2,1,0:T(8,128)(2,1)S(1)} copy-done((bf16[1,384,512]{2,1,0:T(8,128)(2,1)S(1)}, bf16[1,384,512]{2,1,0:T(8,128)(2,1)}, u32[]{:S(2)}) %copy-start.2) | copy-done | bytes 393240
  1.6 0.2 shard_map.60
  1.8 3.0 %collective-permute-start.1 = (bf16[256,384]{1,0:T(8,128)(2,1)S(1)}, bf16[256,384]{1,0:T(8,128)(2,1)S(1)}, u32[]{:S(2)}, u32[]{:S(2)}) collective-permute-start(bf16[256,384]{1,0:T(8,128)(2,1)S(1)} %get-tuple-element.32.refs_1_), channel_id=1, source_target_pairs={{0,1},{1,0},{2,3},{3,2},{4,5},{5,4},{6,7},{7,6},{8,9},{9,8},{10,11... | collective-permute-start | bytes 589832 | tf_op jit(solution)/shard_map/ppermute | solution.py:228
  4.8 1.5 %collective-permute-start.2 = (bf16[256,384]{1,0:T(8,128)(2,1)S(1)}, bf16[256,384]{1,0:T(8,128)(2,1)S(1)}, u32[]{:S(2)}, u32[]{:S(2)}) collective-permute-start(bf16[256,384]{1,0:T(8,128)(2,1)S(1)} %get-tuple-element.31.refs_0_), channel_id=1, source_target_pairs={{0,2},{1,3},{2,0},{3,1},{4,6},{5,7},{6,4},{7,5},{8,10},{9,11},{10,... | collective-permute-start | bytes 589832 | tf_op jit(solution)/shard_map/ppermute | solution.py:228
  6.3 0.5 collective-permute-start
  6.8 0.1 collective-permute-start.3
  6.9 0.1 pad_add_fusion.place_ref
  7.0 0.0 copy-start
  7.0 1.9 %copy-done = bf16[1,1536,1024]{2,1,0:T(8,128)(2,1)S(1)} copy-done((bf16[1,1536,1024]{2,1,0:T(8,128)(2,1)S(1)}, bf16[1,1536,1024]{2,1,0:T(8,128)(2,1)}, u32[]{:S(2)}) %copy-start) | copy-done | bytes 3145752
  8.9 0.7 copy-done.3
  9.5 0.7 copy-done.5
  10.2 2.3 %shard_map.59 = (bf16[1536,512]{1,0:T(8,128)(2,1)S(1)}, f32[8,512]{1,0:T(8,128)S(1)}) custom-call(s32[2]{0:T(128)S(1)} %pad_add_fusion.place_ref, s32[1,512]{1,0:T(1,128)S(1)} %bitcast.12, f32[1,128]{1,0:T(1,128)S(1)} %bitcast.14, bf16[1536,1024]{1,0:T(8,128)(2,1)S(1)} %bitcast.9), custom_call_target="tpu_custom_call" | custom-call | bytes 11071024 | tf_op jit(solution)/shard_map/pallas_call | solution.py:215
  12.6 0.0 collective-permute-done.1.refs_3_
  12.6 0.1 collective-permute-done.2.refs_4_
  12.6 2.0 %collective-permute-start.4 = (bf16[256,384]{1,0:T(8,128)(2,1)S(1)}, bf16[256,384]{1,0:T(8,128)(2,1)S(1)}, u32[]{:S(2)}, u32[]{:S(2)}) collective-permute-start(bf16[256,384]{1,0:T(8,128)(2,1)S(1)} %collective-permute-done.2.refs_4_), channel_id=1, source_target_pairs={{0,1},{1,0},{2,3},{3,2},{4,5},{5,4},{6,7},{7,6},{8,9},{9,8},{10,11... | collective-permute-start | bytes 589832 | tf_op jit(solution)/shard_map/ppermute | solution.py:228
  14.6 1.5 %collective-permute-start.5 = (bf16[256,384]{1,0:T(8,128)(2,1)S(1)}, bf16[256,384]{1,0:T(8,128)(2,1)S(1)}, u32[]{:S(2)}, u32[]{:S(2)}) collective-permute-start(bf16[256,384]{1,0:T(8,128)(2,1)S(1)} %collective-permute-done.1.refs_3_), channel_id=1, source_target_pairs={{0,2},{1,3},{2,0},{3,1},{4,6},{5,7},{6,4},{7,5},{8,10},{9,11},{10,... | collective-permute-start | bytes 589832 | tf_op jit(solution)/shard_map/ppermute | solution.py:228
  16.1 0.1 pad_add_fusion.1.place_ref
  16.2 0.0 collective-permute-done.refs_2_
  16.2 0.0 collective-permute-done.3.refs_5_
  16.2 2.2 %collective-permute-done.4.refs_6_ = bf16[256,384]{1,0:T(8,128)(2,1)S(1)} collective-permute-done((bf16[256,384]{1,0:T(8,128)(2,1)S(1)}, bf16[256,384]{1,0:T(8,128)(2,1)S(1)}, u32[]{:S(2)}, u32[]{:S(2)}) %collective-permute-start.4) | collective-permute-done | bytes 196640 | tf_op jit(solution)/shard_map/ppermute | solution.py:228
  18.4 1.8 %collective-permute-done.5.refs_7_ = bf16[256,384]{1,0:T(8,128)(2,1)S(1)} collective-permute-done((bf16[256,384]{1,0:T(8,128)(2,1)S(1)}, bf16[256,384]{1,0:T(8,128)(2,1)S(1)}, u32[]{:S(2)}, u32[]{:S(2)}) %collective-permute-start.5) | collective-permute-done | bytes 196640 | tf_op jit(solution)/shard_map/ppermute | solution.py:228
  20.3 1.7 %shard_map.61 = (bf16[512,1536]{1,0:T(8,128)(2,1)S(1)}, f32[256,512]{1,0:T(8,128)S(1)}, f32[264,512]{1,0:T(8,128)S(1)}) custom-call(s32[3]{0:T(128)S(1)} %pad_add_fusion.1.place_ref, bf16[1536,512]{1,0:T(8,128)(2,1)S(1)} %get-tuple-element.29.chosen_ref, f32[8,512]{1,0:T(8,128)S(1)} %get-tuple-element.30.entry_ref, ...), custom_call_target="tpu_custom_call" | custom-call | bytes 1024 | tf_op jit(solution)/shard_map/pallas_call | solution.py:215
  22.0 0.1 collective-permute-start.6
  22.1 1.9 %collective-permute-done.6.got_ref = f32[264,512]{1,0:T(8,128)S(1)} collective-permute-done((f32[264,512]{1,0:T(8,128)S(1)}, f32[264,512]{1,0:T(8,128)S(1)}, u32[]{:S(2)}, u32[]{:S(2)}) %collective-permute-start.6) | collective-permute-done | bytes 540704 | tf_op jit(solution)/shard_map/ppermute | solution.py:228
  24.0 0.2 shard_map.62
  24.1 0.0 copy-done.1
  24.2 2.4 %shard_map.63 = (f32[2048,128]{1,0:T(8,128)S(1)}, f32[2048,128]{1,0:T(8,128)S(1)}) custom-call(s32[3]{0:T(128)S(1)} %pad_add_fusion.1.place_ref, bf16[1536,1024]{1,0:T(8,128)(2,1)S(1)} %bitcast.10, bf16[512,1536]{1,0:T(8,128)(2,1)S(1)} %get-tuple-element.39.turned_ref), custom_call_target="tpu_custom_call" | custom-call | bytes 1024 | tf_op jit(solution)/shard_map/pallas_call | solution.py:215
  26.5 0.2 collective-permute-start.10
  26.7 0.1 collective-permute-start.7
  26.8 2.0 %collective-permute-start.8 = (s16[80,512]{1,0:T(8,128)(2,1)S(1)}, s16[80,512]{1,0:T(8,128)(2,1)S(1)}, u32[]{:S(2)}, u32[]{:S(2)}) collective-permute-start(s16[80,512]{1,0:T(8,128)(2,1)S(1)} %get-tuple-element.43), channel_id=1, source_target_pairs={{0,2},{1,3},{2,0},{3,1},{4,6},{5,7},{6,4},{7,5},{8,10},{9,11},{10,... | collective-permute-start | bytes 245768 | tf_op jit(solution)/shard_map/ppermute | solution.py:228
  28.8 1.4 %collective-permute-start.9 = (s16[80,512]{1,0:T(8,128)(2,1)S(1)}, s16[80,512]{1,0:T(8,128)(2,1)S(1)}, u32[]{:S(2)}, u32[]{:S(2)}) collective-permute-start(s16[80,512]{1,0:T(8,128)(2,1)S(1)} %get-tuple-element.44), channel_id=1, source_target_pairs={{0,3},{1,2},{2,1},{3,0},{4,7},{5,6},{6,5},{7,4},{8,11},{9,10},{10,... | collective-permute-start | bytes 245768 | tf_op jit(solution)/shard_map/ppermute | solution.py:228
  30.2 1.8 %collective-permute-done.7.refs_1_ = s16[80,512]{1,0:T(8,128)(2,1)S(1)} collective-permute-done((s16[80,512]{1,0:T(8,128)(2,1)S(1)}, s16[80,512]{1,0:T(8,128)(2,1)S(1)}, u32[]{:S(2)}, u32[]{:S(2)}) %collective-permute-start.7) | collective-permute-done | bytes 81952 | tf_op jit(solution)/shard_map/ppermute | solution.py:228
  32.0 0.5 collective-permute-done.8.refs_2_
  32.5 1.6 %collective-permute-done.9.refs_3_ = s16[80,512]{1,0:T(8,128)(2,1)S(1)} collective-permute-done((s16[80,512]{1,0:T(8,128)(2,1)S(1)}, s16[80,512]{1,0:T(8,128)(2,1)S(1)}, u32[]{:S(2)}, u32[]{:S(2)}) %collective-permute-start.9) | collective-permute-done | bytes 81952 | tf_op jit(solution)/shard_map/ppermute | solution.py:228
  34.2 0.1 shard_map.64.refs_0_
  34.3 1.6 %collective-permute-start.11 = (s16[80,512]{1,0:T(8,128)(2,1)S(1)}, s16[80,512]{1,0:T(8,128)(2,1)S(1)}, u32[]{:S(2)}, u32[]{:S(2)}) collective-permute-start(s16[80,512]{1,0:T(8,128)(2,1)S(1)} %shard_map.64.refs_0_), channel_id=1, source_target_pairs={{0,8},{4,12},{8,0},{12,4},{16,24},{20,28},{24,16},{28,20},{1,9},{5... | collective-permute-start | bytes 245768 | tf_op jit(solution)/shard_map/ppermute | solution.py:228
  35.9 0.0 collective-permute-done.10.got_ref
  35.9 0.2 shard_map.65
  36.1 2.7 %collective-permute-done.11.refs_1_ = s16[80,512]{1,0:T(8,128)(2,1)S(1)} collective-permute-done((s16[80,512]{1,0:T(8,128)(2,1)S(1)}, s16[80,512]{1,0:T(8,128)(2,1)S(1)}, u32[]{:S(2)}, u32[]{:S(2)}) %collective-permute-start.11) | collective-permute-done | bytes 81952 | tf_op jit(solution)/shard_map/ppermute | solution.py:228
  38.8 0.1 shard_map.66.refs_0_
  38.9 2.7 %collective-permute-start.12 = (s16[80,512]{1,0:T(8,128)(2,1)S(1)}, s16[80,512]{1,0:T(8,128)(2,1)S(1)}, u32[]{:S(2)}, u32[]{:S(2)}) collective-permute-start(s16[80,512]{1,0:T(8,128)(2,1)S(1)} %shard_map.66.refs_0_), channel_id=1, source_target_pairs={{0,16},{4,20},{8,24},{12,28},{16,0},{20,4},{24,8},{28,12},{1,17},{... | collective-permute-start | bytes 245768 | tf_op jit(solution)/shard_map/ppermute | solution.py:228
  41.6 2.8 %collective-permute-done.12.refs_1_ = s16[80,512]{1,0:T(8,128)(2,1)S(1)} collective-permute-done((s16[80,512]{1,0:T(8,128)(2,1)S(1)}, s16[80,512]{1,0:T(8,128)(2,1)S(1)}, u32[]{:S(2)}, u32[]{:S(2)}) %collective-permute-start.12) | collective-permute-done | bytes 81952 | tf_op jit(solution)/shard_map/ppermute | solution.py:228
  44.3 0.1 shard_map.67.refs_0_
  44.4 1.8 %collective-permute-start.15 = (s16[80,512]{1,0:T(8,128)(2,1)S(1)}, s16[80,512]{1,0:T(8,128)(2,1)S(1)}, u32[]{:S(2)}, u32[]{:S(2)}) collective-permute-start(s16[80,512]{1,0:T(8,128)(2,1)S(1)} %shard_map.67.refs_0_), channel_id=1, source_target_pairs={{0,3},{1,2},{2,1},{3,0},{4,7},{5,6},{6,5},{7,4},{8,11},{9,10},{10,... | collective-permute-start | bytes 245768 | tf_op jit(solution)/shard_map/ppermute | solution.py:228
  46.2 1.2 %collective-permute-start.14 = (s16[80,512]{1,0:T(8,128)(2,1)S(1)}, s16[80,512]{1,0:T(8,128)(2,1)S(1)}, u32[]{:S(2)}, u32[]{:S(2)}) collective-permute-start(s16[80,512]{1,0:T(8,128)(2,1)S(1)} %shard_map.67.refs_0_), channel_id=1, source_target_pairs={{0,2},{1,3},{2,0},{3,1},{4,6},{5,7},{6,4},{7,5},{8,10},{9,11},{10,... | collective-permute-start | bytes 245768 | tf_op jit(solution)/shard_map/ppermute | solution.py:228
  47.4 0.6 collective-permute-start.13
  48.0 1.6 %collective-permute-start.17 = (s16[1056,128]{1,0:T(8,128)(2,1)S(1)}, s16[1056,128]{1,0:T(8,128)(2,1)S(1)}, u32[]{:S(2)}, u32[]{:S(2)}) collective-permute-start(s16[1056,128]{1,0:T(8,128)(2,1)S(1)} %get-tuple-element.53), channel_id=1, source_target_pairs={{0,8},{4,12},{8,0},{12,4},{16,24},{20,28},{24,16},{28,20},{1,9},{5... | collective-permute-start | bytes 811016 | tf_op jit(solution)/shard_map/ppermute | solution.py:228
  49.5 0.3 collective-permute-done.15.refs_3_
  49.8 0.9 %collective-permute-done.14.refs_2_ = s16[80,512]{1,0:T(8,128)(2,1)S(1)} collective-permute-done((s16[80,512]{1,0:T(8,128)(2,1)S(1)}, s16[80,512]{1,0:T(8,128)(2,1)S(1)}, u32[]{:S(2)}, u32[]{:S(2)}) %collective-permute-start.14) | collective-permute-done | bytes 81952 | tf_op jit(solution)/shard_map/ppermute | solution.py:228
  50.7 1.2 %collective-permute-done.13.refs_1_ = s16[80,512]{1,0:T(8,128)(2,1)S(1)} collective-permute-done((s16[80,512]{1,0:T(8,128)(2,1)S(1)}, s16[80,512]{1,0:T(8,128)(2,1)S(1)}, u32[]{:S(2)}, u32[]{:S(2)}) %collective-permute-start.13) | collective-permute-done | bytes 81952 | tf_op jit(solution)/shard_map/ppermute | solution.py:228
  51.9 0.0 copy-start.4
  51.9 0.0 copy-start.6
  51.9 0.1 collective-permute-start.16
  52.0 2.5 %collective-permute-done.17.got_ref = s16[1056,128]{1,0:T(8,128)(2,1)S(1)} collective-permute-done((s16[1056,128]{1,0:T(8,128)(2,1)S(1)}, s16[1056,128]{1,0:T(8,128)(2,1)S(1)}, u32[]{:S(2)}, u32[]{:S(2)}) %collective-permute-start.17) | collective-permute-done | bytes 270368 | tf_op jit(solution)/shard_map/ppermute | solution.py:228
  54.4 0.2 shard_map.71
  54.6 3.0 %collective-permute-start.18 = (s16[528,128]{1,0:T(8,128)(2,1)S(1)}, s16[528,128]{1,0:T(8,128)(2,1)S(1)}, u32[]{:S(2)}, u32[]{:S(2)}) collective-permute-start(s16[528,128]{1,0:T(8,128)(2,1)S(1)} %get-tuple-element.55), channel_id=1, source_target_pairs={{0,16},{4,20},{8,24},{12,28},{16,0},{20,4},{24,8},{28,12},{1,17},{... | collective-permute-start | bytes 405512 | tf_op jit(solution)/shard_map/ppermute | solution.py:228
  57.6 0.0 collective-permute-done.16.other_ref
  57.6 5.2 %shard_map.69 = (f32[256,256]{1,0:T(8,128)S(1)}, f32[512,512]{1,0:T(8,128)S(1)}) custom-call(s32[3]{0:T(128)S(1)} %pad_add_fusion.1.place_ref, s16[320,512]{1,0:T(8,128)(2,1)S(1)} %shard_map.68.own_ref, s16[320,512]{1,0:T(8,128)(2,1)S(1)} %collective-permute-done.16.other_ref), custom_call_target="tpu_custom_call" | custom-call | bytes 16606024 | tf_op jit(solution)/shard_map/pallas_call | solution.py:215
  62.8 5.0 %shard_map.70.inverse_second_ref = f32[256,256]{1,0:T(8,128)S(1)} custom-call(f32[512,512]{1,0:T(8,128)S(1)} %get-tuple-element.51.pivots_ref, f32[256,256]{1,0:T(8,128)S(1)} %get-tuple-element.50.inverse_first_ref), custom_call_target="tpu_custom_call" | custom-call | bytes 16606024 | tf_op jit(solution)/shard_map/pallas_call | solution.py:215
  67.7 0.0 collective-permute-done.18.refs_0_
  67.7 0.0 copy-done.4
  67.7 0.0 copy-done.6
  67.8 2.2 %shard_map.72 = (f32[128,1,256]{2,1,0:T(1,128)}, f32[128,1,256]{2,1,0:T(1,128)}) custom-call(s32[2]{0:T(128)S(1)} %pad_add_fusion.place_ref, s32[1,512]{1,0:T(1,128)S(1)} %bitcast.13, f32[1,128]{1,0:T(1,128)S(1)} %bitcast.15, f32[256,256]{1,0:T(8,128)S(1)} %get-tuple-element.50.inverse_first_ref, f32[256,256]{1,0:T(8,128)S(1)} %shard_map.70.inverse_second_ref, ...), custom_call_target="tpu_custom_call" | custom-call | bytes 1024 | tf_op jit(solution)/shard_map/pallas_call | solution.py:215
  (4 shorter events, 0.0 us)
Async XLA Ops:
  0.6 1.0 %copy-start.2 = (bf16[1,384,512]{2,1,0:T(8,128)(2,1)S(1)}, bf16[1,384,512]{2,1,0:T(8,128)(2,1)}, u32[]{:S(2)}) copy-start(bf16[1,384,512]{2,1,0:T(8,128)(2,1)} %param.5) | copy-start | bytes 1179652
  1.8 10.8 %collective-permute-start.1 = (bf16[256,384]{1,0:T(8,128)(2,1)S(1)}, bf16[256,384]{1,0:T(8,128)(2,1)S(1)}, u32[]{:S(2)}, u32[]{:S(2)}) collective-permute-start(bf16[256,384]{1,0:T(8,128)(2,1)S(1)} %get-tuple-element.32.refs_1_), channel_id=1, source_target_pairs={{0,1},{1,0},{2,3},{3,2},{4,5},{5,4},{6,7},{7,6},{8,9},{9,8},{10,11... | collective-permute-start | bytes 589832 | tf_op jit(solution)/shard_map/ppermute | solution.py:228
  4.8 7.8 %collective-permute-start.2 = (bf16[256,384]{1,0:T(8,128)(2,1)S(1)}, bf16[256,384]{1,0:T(8,128)(2,1)S(1)}, u32[]{:S(2)}, u32[]{:S(2)}) collective-permute-start(bf16[256,384]{1,0:T(8,128)(2,1)S(1)} %get-tuple-element.31.refs_0_), channel_id=1, source_target_pairs={{0,2},{1,3},{2,0},{3,1},{4,6},{5,7},{6,4},{7,5},{8,10},{9,11},{10,... | collective-permute-start | bytes 589832 | tf_op jit(solution)/shard_map/ppermute | solution.py:228
  6.3 9.9 %collective-permute-start = (bf16[256,384]{1,0:T(8,128)(2,1)S(1)}, bf16[256,384]{1,0:T(8,128)(2,1)S(1)}, u32[]{:S(2)}, u32[]{:S(2)}) collective-permute-start(bf16[256,384]{1,0:T(8,128)(2,1)S(1)} %get-tuple-element.31.refs_0_), channel_id=1, source_target_pairs={{0,1},{1,0},{2,3},{3,2},{4,5},{5,4},{6,7},{7,6},{8,9},{9,8},{10,11... | collective-permute-start | bytes 589832 | tf_op jit(solution)/shard_map/ppermute | solution.py:228
  6.8 9.3 %collective-permute-start.3 = (bf16[256,384]{1,0:T(8,128)(2,1)S(1)}, bf16[256,384]{1,0:T(8,128)(2,1)S(1)}, u32[]{:S(2)}, u32[]{:S(2)}) collective-permute-start(bf16[256,384]{1,0:T(8,128)(2,1)S(1)} %get-tuple-element.32.refs_1_), channel_id=1, source_target_pairs={{0,2},{1,3},{2,0},{3,1},{4,6},{5,7},{6,4},{7,5},{8,10},{9,11},{10,... | collective-permute-start | bytes 589832 | tf_op jit(solution)/shard_map/ppermute | solution.py:228
  7.0 1.9 %copy-start = (bf16[1,1536,1024]{2,1,0:T(8,128)(2,1)S(1)}, bf16[1,1536,1024]{2,1,0:T(8,128)(2,1)}, u32[]{:S(2)}) copy-start(bf16[1,1536,1024]{2,1,0:T(8,128)(2,1)} %param.4) | copy-start | bytes 9437188
  8.9 0.7 copy-start.3
  9.5 0.7 copy-start.5
  12.6 5.8 %collective-permute-start.4 = (bf16[256,384]{1,0:T(8,128)(2,1)S(1)}, bf16[256,384]{1,0:T(8,128)(2,1)S(1)}, u32[]{:S(2)}, u32[]{:S(2)}) collective-permute-start(bf16[256,384]{1,0:T(8,128)(2,1)S(1)} %collective-permute-done.2.refs_4_), channel_id=1, source_target_pairs={{0,1},{1,0},{2,3},{3,2},{4,5},{5,4},{6,7},{7,6},{8,9},{9,8},{10,11... | collective-permute-start | bytes 589832 | tf_op jit(solution)/shard_map/ppermute | solution.py:228
  14.6 5.7 %collective-permute-start.5 = (bf16[256,384]{1,0:T(8,128)(2,1)S(1)}, bf16[256,384]{1,0:T(8,128)(2,1)S(1)}, u32[]{:S(2)}, u32[]{:S(2)}) collective-permute-start(bf16[256,384]{1,0:T(8,128)(2,1)S(1)} %collective-permute-done.1.refs_3_), channel_id=1, source_target_pairs={{0,2},{1,3},{2,0},{3,1},{4,6},{5,7},{6,4},{7,5},{8,10},{9,11},{10,... | collective-permute-start | bytes 589832 | tf_op jit(solution)/shard_map/ppermute | solution.py:228
  20.3 3.9 %copy-start.1 = (bf16[1,1536,1024]{2,1,0:T(8,128)(2,1)S(1)}, bf16[1,1536,1024]{2,1,0:T(8,128)(2,1)}, u32[]{:S(2)}) copy-start(bf16[1,1536,1024]{2,1,0:T(8,128)(2,1)} %param.4) | copy-start | bytes 9437188
  22.0 2.0 %collective-permute-start.6 = (f32[264,512]{1,0:T(8,128)S(1)}, f32[264,512]{1,0:T(8,128)S(1)}, u32[]{:S(2)}, u32[]{:S(2)}) collective-permute-start(f32[264,512]{1,0:T(8,128)S(1)} %get-tuple-element.36), channel_id=1, source_target_pairs={{0,4},{4,0},{8,12},{12,8},{16,20},{20,16},{24,28},{28,24},{1,5},{5... | collective-permute-start | bytes 1622024 | tf_op jit(solution)/shard_map/ppermute | solution.py:228
  26.5 9.4 %collective-permute-start.10 = (f32[2048,128]{1,0:T(8,128)S(1)}, f32[2048,128]{1,0:T(8,128)S(1)}, u32[]{:S(2)}, u32[]{:S(2)}) collective-permute-start(f32[2048,128]{1,0:T(8,128)S(1)} %get-tuple-element.46), channel_id=1, source_target_pairs={{0,4},{4,0},{8,12},{12,8},{16,20},{20,16},{24,28},{28,24},{1,5},{5... | collective-permute-start | bytes 3145736 | tf_op jit(solution)/shard_map/ppermute | solution.py:228
  26.7 5.3 %collective-permute-start.7 = (s16[80,512]{1,0:T(8,128)(2,1)S(1)}, s16[80,512]{1,0:T(8,128)(2,1)S(1)}, u32[]{:S(2)}, u32[]{:S(2)}) collective-permute-start(s16[80,512]{1,0:T(8,128)(2,1)S(1)} %get-tuple-element.42), channel_id=1, source_target_pairs={{0,1},{1,0},{2,3},{3,2},{4,5},{5,4},{6,7},{7,6},{8,9},{9,8},{10,11... | collective-permute-start | bytes 245768 | tf_op jit(solution)/shard_map/ppermute | solution.py:228
  26.8 5.7 %collective-permute-start.8 = (s16[80,512]{1,0:T(8,128)(2,1)S(1)}, s16[80,512]{1,0:T(8,128)(2,1)S(1)}, u32[]{:S(2)}, u32[]{:S(2)}) collective-permute-start(s16[80,512]{1,0:T(8,128)(2,1)S(1)} %get-tuple-element.43), channel_id=1, source_target_pairs={{0,2},{1,3},{2,0},{3,1},{4,6},{5,7},{6,4},{7,5},{8,10},{9,11},{10,... | collective-permute-start | bytes 245768 | tf_op jit(solution)/shard_map/ppermute | solution.py:228
  28.8 5.4 %collective-permute-start.9 = (s16[80,512]{1,0:T(8,128)(2,1)S(1)}, s16[80,512]{1,0:T(8,128)(2,1)S(1)}, u32[]{:S(2)}, u32[]{:S(2)}) collective-permute-start(s16[80,512]{1,0:T(8,128)(2,1)S(1)} %get-tuple-element.44), channel_id=1, source_target_pairs={{0,3},{1,2},{2,1},{3,0},{4,7},{5,6},{6,5},{7,4},{8,11},{9,10},{10,... | collective-permute-start | bytes 245768 | tf_op jit(solution)/shard_map/ppermute | solution.py:228
  34.3 4.5 %collective-permute-start.11 = (s16[80,512]{1,0:T(8,128)(2,1)S(1)}, s16[80,512]{1,0:T(8,128)(2,1)S(1)}, u32[]{:S(2)}, u32[]{:S(2)}) collective-permute-start(s16[80,512]{1,0:T(8,128)(2,1)S(1)} %shard_map.64.refs_0_), channel_id=1, source_target_pairs={{0,8},{4,12},{8,0},{12,4},{16,24},{20,28},{24,16},{28,20},{1,9},{5... | collective-permute-start | bytes 245768 | tf_op jit(solution)/shard_map/ppermute | solution.py:228
  38.9 5.4 %collective-permute-start.12 = (s16[80,512]{1,0:T(8,128)(2,1)S(1)}, s16[80,512]{1,0:T(8,128)(2,1)S(1)}, u32[]{:S(2)}, u32[]{:S(2)}) collective-permute-start(s16[80,512]{1,0:T(8,128)(2,1)S(1)} %shard_map.66.refs_0_), channel_id=1, source_target_pairs={{0,16},{4,20},{8,24},{12,28},{16,0},{20,4},{24,8},{28,12},{1,17},{... | collective-permute-start | bytes 245768 | tf_op jit(solution)/shard_map/ppermute | solution.py:228
  44.4 5.4 %collective-permute-start.15 = (s16[80,512]{1,0:T(8,128)(2,1)S(1)}, s16[80,512]{1,0:T(8,128)(2,1)S(1)}, u32[]{:S(2)}, u32[]{:S(2)}) collective-permute-start(s16[80,512]{1,0:T(8,128)(2,1)S(1)} %shard_map.67.refs_0_), channel_id=1, source_target_pairs={{0,3},{1,2},{2,1},{3,0},{4,7},{5,6},{6,5},{7,4},{8,11},{9,10},{10,... | collective-permute-start | bytes 245768 | tf_op jit(solution)/shard_map/ppermute | solution.py:228
  46.2 4.5 %collective-permute-start.14 = (s16[80,512]{1,0:T(8,128)(2,1)S(1)}, s16[80,512]{1,0:T(8,128)(2,1)S(1)}, u32[]{:S(2)}, u32[]{:S(2)}) collective-permute-start(s16[80,512]{1,0:T(8,128)(2,1)S(1)} %shard_map.67.refs_0_), channel_id=1, source_target_pairs={{0,2},{1,3},{2,0},{3,1},{4,6},{5,7},{6,4},{7,5},{8,10},{9,11},{10,... | collective-permute-start | bytes 245768 | tf_op jit(solution)/shard_map/ppermute | solution.py:228
  47.4 4.4 %collective-permute-start.13 = (s16[80,512]{1,0:T(8,128)(2,1)S(1)}, s16[80,512]{1,0:T(8,128)(2,1)S(1)}, u32[]{:S(2)}, u32[]{:S(2)}) collective-permute-start(s16[80,512]{1,0:T(8,128)(2,1)S(1)} %shard_map.67.refs_0_), channel_id=1, source_target_pairs={{0,1},{1,0},{2,3},{3,2},{4,5},{5,4},{6,7},{7,6},{8,9},{9,8},{10,11... | collective-permute-start | bytes 245768 | tf_op jit(solution)/shard_map/ppermute | solution.py:228
  48.0 6.5 %collective-permute-start.17 = (s16[1056,128]{1,0:T(8,128)(2,1)S(1)}, s16[1056,128]{1,0:T(8,128)(2,1)S(1)}, u32[]{:S(2)}, u32[]{:S(2)}) collective-permute-start(s16[1056,128]{1,0:T(8,128)(2,1)S(1)} %get-tuple-element.53), channel_id=1, source_target_pairs={{0,8},{4,12},{8,0},{12,4},{16,24},{20,28},{24,16},{28,20},{1,9},{5... | collective-permute-start | bytes 811016 | tf_op jit(solution)/shard_map/ppermute | solution.py:228
  51.9 15.9 %copy-start.4 = (s32[512]{0:T(512)S(1)}, s32[512]{0:T(512)}, u32[]{:S(2)}) copy-start(s32[512]{0:T(512)} %param.7) | copy-start | bytes 6148
  51.9 15.9 %copy-start.6 = (f32[128,1]{0,1:T(1,128)S(1)}, f32[128,1]{0,1:T(1,128)}, u32[]{:S(2)}) copy-start(f32[128,1]{0,1:T(1,128)} %param.6) | copy-start | bytes 1540
  51.9 5.7 %collective-permute-start.16 = (s16[320,512]{1,0:T(8,128)(2,1)S(1)}, s16[320,512]{1,0:T(8,128)(2,1)S(1)}, u32[]{:S(2)}, u32[]{:S(2)}) collective-permute-start(s16[320,512]{1,0:T(8,128)(2,1)S(1)} %shard_map.68.own_ref), channel_id=1, source_target_pairs={{0,4},{4,0},{8,12},{12,8},{16,20},{20,16},{24,28},{28,24},{1,5},{5... | collective-permute-start | bytes 983048 | tf_op jit(solution)/shard_map/ppermute | solution.py:228
  54.6 13.1 %collective-permute-start.18 = (s16[528,128]{1,0:T(8,128)(2,1)S(1)}, s16[528,128]{1,0:T(8,128)(2,1)S(1)}, u32[]{:S(2)}, u32[]{:S(2)}) collective-permute-start(s16[528,128]{1,0:T(8,128)(2,1)S(1)} %get-tuple-element.55), channel_id=1, source_target_pairs={{0,16},{4,20},{8,24},{12,28},{16,0},{20,4},{24,8},{28,12},{1,17},{... | collective-permute-start | bytes 405512 | tf_op jit(solution)/shard_map/ppermute | solution.py:228

commit v4 on v3

--- a/solution.py
+++ b/solution.py
@@ -10,6 +10,7 @@
 HALF = 256
 NEWTON = 8
 TAIL = 16
+CHUNKS = 4
 LEVELS = 32000.0
 F32 = jnp.float32
 BF16 = jnp.bfloat16
@@ -45,11 +46,18 @@
     norm_one = jnp.max(jnp.sum(size, axis=0, keepdims=True))
     norm_inf = jnp.max(jnp.sum(size, axis=1, keepdims=True))
     approx = pivot.T / (norm_one * norm_inf)
+    count = pivot.shape[0]
+    one = lax.broadcasted_iota(jnp.int32, pivot.shape, 0) == lax.broadcasted_iota(jnp.int32, pivot.shape, 1)
     pivot_right = right_of(pivot)
-    for step in range(NEWTON):
-        left = dot(left_of(approx), pivot_right)
-        approx = 2.0 * approx - product(left, approx)
-    return approx
+    rest = jnp.where(one, F32(1.0), F32(0.0)) - dot(left_of(approx), pivot_right)
+    for step in range(NEWTON - 1):
+        if step < NEWTON - 2:
+            both = product(rest, jnp.concatenate([rest, approx], axis=1))
+            rest, approx = both[:, :count], approx + both[:, count:]
+        else:
+            approx = approx + product(rest, approx)
+    left = dot(left_of(approx), pivot_right)
+    return 2.0 * approx - product(left, approx)
 
 
 def aligned(index, size):
@@ -81,24 +89,44 @@
     return ref[base:base + rows, :].astype(jnp.int32).astype(F32) * scale, diagonal
 
 
-def turn_kernel(solves_ref, upper_ref, lower_ref):
-    turned = solves_ref[...].T
+def turn_kernel(solves_ref, upper_ref, lower_ref, solves_copy, done):
+    copy = pltpu.make_async_copy(solves_ref, solves_copy, done)
+    copy.start()
+    copy.wait()
+    turned = solves_copy[...].T
     half = upper_ref.shape[0]
     upper_ref[...] = turned[:half]
     lower_ref[...] = turned[half:]
 
 
-def pick_kernel(place_ref, panel_ref, own_diagonal_ref, coupling_ref, chosen_ref, entry_ref):
+def pick_kernel(
+    place_ref, panel_ref, own_diagonal_ref, coupling_ref, chosen_ref, entry_ref,
+    panel_copy, diagonal_copy, coupling_copy, one_ref, small_done, done,
+):
+    chunks, rows, columns = coupling_copy.shape
+    small = [
+        pltpu.make_async_copy(panel_ref, panel_copy, small_done.at[0]),
+        pltpu.make_async_copy(own_diagonal_ref, diagonal_copy, small_done.at[1]),
+    ]
+    large = [
+        pltpu.make_async_copy(coupling_ref.at[pl.ds(i * rows, rows), :], coupling_copy.at[i], done.at[i])
+        for i in range(chunks)
+    ]
+    for copy in small + large:
+        copy.start()
+    for copy in small:
+        copy.wait()
     first_column, first_row = place_ref[0], place_ref[1]
-    panel = panel_ref.shape[1]
-    columns, share = coupling_ref.shape[1], own_diagonal_ref.shape[1]
-    here = panel_ref[...] - first_column == lax.broadcasted_iota(jnp.int32, (columns, panel), 0)
-    chosen = jnp.where(here, F32(1.0), F32(0.0)).astype(BF16)
-    chosen_ref[...] = dot(coupling_ref[...], chosen).astype(BF16)
-    owned = panel_ref[...] - first_row == lax.broadcasted_iota(jnp.int32, (share, panel), 0)
-    own = jnp.broadcast_to(own_diagonal_ref[...], (8, share)).T[:, :1]
+    panel, share = panel_copy.shape[1], diagonal_copy.shape[1]
+    here = panel_copy[...] - first_column == lax.broadcasted_iota(jnp.int32, (columns, panel), 0)
+    one_ref[...] = jnp.where(here, F32(1.0), F32(0.0)).astype(BF16)
+    owned = panel_copy[...] - first_row == lax.broadcasted_iota(jnp.int32, (share, panel), 0)
+    own = jnp.broadcast_to(diagonal_copy[...], (8, share)).T[:, :1]
     entry = jnp.sum(jnp.where(owned, own, F32(0.0)), axis=0, keepdims=True)
     entry_ref[...] = jnp.broadcast_to(entry, entry_ref.shape)
+    for i, copy in enumerate(large):
+        copy.wait()
+        chosen_ref[i * rows:(i + 1) * rows, :] = dot(coupling_copy[i], one_ref[...]).astype(BF16)
 
 
 def terms_kernel(rows, place_ref, chosen_ref, entry_ref, *refs):
@@ -209,13 +237,16 @@
     second_out[...] = product(inverse_second_ref[...], updated).T[:, None, :]
 
 
-def call(kernel, out_shape, *args, scratch=(), scalars=0, micros=0.0):
+def call(kernel, out_shape, *args, scratch=(), scalars=0, remain=0, micros=0.0):
+    hbm = pl.BlockSpec(memory_space=pltpu.HBM)
     vmem = pl.BlockSpec(memory_space=pltpu.VMEM)
     smem = pl.BlockSpec(memory_space=pltpu.SMEM)
+    stay = len(args) - remain
+    args = args[:stay] + tuple(pltpu.with_memory_space_constraint(x, pltpu.HBM) for x in args[stay:])
     return pl.pallas_call(
         kernel,
         out_shape=out_shape,
-        in_specs=[smem] * scalars + [vmem] * (len(args) - scalars),
+        in_specs=[smem] * scalars + [vmem] * (len(args) - scalars - remain) + [hbm] * remain,
         out_specs=jax.tree.map(lambda _: vmem, out_shape),
         scratch_shapes=scratch,
         compiler_params=pltpu.CompilerParams(vmem_limit_bytes=28 << 20),
@@ -246,7 +277,10 @@
     if rows != 4:
         return [lax.all_gather(solves.T, "row", axis=1, tiled=True)]
     half = jax.ShapeDtypeStruct((panel // 2, block), BF16)
-    upper, lower = call(turn_kernel, (half, half), solves)
+    upper, lower = call(
+        turn_kernel, (half, half), solves, remain=1,
+        scratch=[pltpu.VMEM((block, panel), BF16), pltpu.SemaphoreType.DMA],
+    )
     lower_x, upper_y = swap(lower, "row", 1), swap(upper, "row", 2)
     upper_x, lower_y = swap(upper, "row", 1), swap(lower, "row", 2)
     upper_far, lower_far = swap(after(upper_y, *ready), "row", 1), swap(after(lower_x, *ready), "row", 2)
@@ -269,8 +303,16 @@
     at = jnp.stack([row, place % 2, place // 2]).astype(jnp.int32)
 
     chosen, entry = call(
-        pick_kernel, (shape((local, panel), BF16), shape((8, panel), F32)),
-        starts, panel_row, diagonal_row, coupling, scalars=1, micros=3.0,
+        pick_kernel, (pltpu.VMEM((local, panel), BF16), pltpu.VMEM((8, panel), F32)),
+        starts, panel_row, diagonal_row, coupling, scalars=1, remain=3, micros=3.0,
+        scratch=[
+            pltpu.VMEM((1, panel), jnp.int32),
+            pltpu.VMEM((1, share), F32),
+            pltpu.VMEM((CHUNKS, local // CHUNKS, row_count), BF16),
+            pltpu.VMEM((row_count, panel), BF16),
+            pltpu.SemaphoreType.DMA((2,)),
+            pltpu.SemaphoreType.DMA((CHUNKS,)),
+        ],
     )
     pieces = gather_pieces(solves, rows, (entry,))
     turned, keep, send = call(
@@ -292,7 +334,7 @@
             part = call(sum_kernel, coded, part, swap(part, "scen", 2 * bit))
     else:
         bulk = shape((layers * panel, share), F32)
-        keep, send = call(schur_kernel, (bulk, bulk), at, coupling, after(turned, codes[0]), scalars=1)
+        keep, send = call(schur_kernel, (bulk, bulk), at, coupling, after(turned, arrived[0]), scalars=1)
         got = swap(send, "scen", 1)
         part = call(sum_kernel, coded, after(codes[0], keep), *arrived)
         steps = bits_of(layers)
@@ -303,14 +345,14 @@
             after(keep, part), got,
         )
         for bit in steps:
-            other = swap(part, "scen", 2 * bit)
+            before, other = part, swap(part, "scen", 2 * bit)
             part = call(sum_kernel, coded, after(part, bulk_codes), other)
         for bit in steps[:-1]:
             count //= 2
             own, bulk_codes = call(
                 functools.partial(bulk_sum_kernel, panel),
                 (shape((count * panel, share), F32), shape((count * (panel + TAIL), share), I16)),
-                own, swap(after(bulk_codes, part), "scen", 2 * bit),
+                own, swap(after(bulk_codes, before), "scen", 2 * bit),
             )
         got = [swap(bulk_codes, "scen", layers)]
 

time: 70.1 us -> 71.2 us (1.016)
  waiting for transfers between devices: 20.2 us -> 25.9 us
  local copies, waits for them, and re-layouts: 4.23 us -> 0.02 us
  starting transfers between devices: 24.8 us -> 23.3 us
  Pallas kernels: 19.7 us -> 20.8 us
    ppermute x19, waiting for transfers between devices: 20.2 us -> 25.9 us  [swap(): return lax.ppermute(x, axis, [(i, i ^ bit) for i in range(count)])]
    unnamed x14 -> x6, local copies, waits for them, and re-layouts: 4.23 us -> 0.02 us
    ppermute x19, starting transfers between devices: 24.8 us -> 23.3 us  [swap(): return lax.ppermute(x, axis, [(i, i ^ bit) for i in range(count)])]
    pallas_call x14, Pallas kernels: 19.7 us -> 20.8 us  [call(): pl.pallas_call(kernel, out_shape=out_shape, in_specs=[smem] * scalars + [...]
  transfers between devices with their start and end apart: 19 -> 19, of which waited for: 13 -> 14; matrix products, arithmetic and copies ran while one was open for 0% -> 0% of each run, Pallas kernels for 19% -> 18%
where the time goes in v4:
time: 71.2 us; the launch traced here: 71 us
  waiting for transfers between devices  25.9 us (36%)
  starting transfers between devices  23.3 us (33%)
  Pallas kernels  20.8 us (29%)
  between operations  0.81 us (1%)
    ppermute x19, waiting for transfers between devices, swap(): return lax.ppermute(x, axis, [(i, i ^ bit) for i in range(count)])  25.9 us
    ppermute x19, starting transfers between devices, swap(): return lax.ppermute(x, axis, [(i, i ^ bit) for i in range(count)])  23.3 us
    pallas_call x14, Pallas kernels, call(): pl.pallas_call(kernel, out_shape=out_shape, in_specs=[smem] * scalars + [...  20.8 us
  transfers between devices with their start and end apart: 19, of which 14 were waited for; matrix products, arithmetic and copies ran while one was open for 0% of the time, Pallas kernels for 18%

profile of v4, /device:TPU:0, one launch (start us, length us, event | category | flops | bytes accessed | tf_op | source)
XLA Modules:
  0.0 71.0 jit_solution(25952273592853030)
XLA Ops:
  0.6 1.2 %shard_map.60 = (bf16[256,384]{1,0:T(8,128)(2,1)S(1)}, bf16[256,384]{1,0:T(8,128)(2,1)S(1)}) custom-call(bf16[384,512]{1,0:T(8,128)(2,1)} %bitcast.15), custom_call_target="tpu_custom_call" | custom-call | bytes 1024 | tf_op jit(solution)/shard_map/pallas_call | solution.py:246
  1.8 3.0 %collective-permute-start.1 = (bf16[256,384]{1,0:T(8,128)(2,1)S(1)}, bf16[256,384]{1,0:T(8,128)(2,1)S(1)}, u32[]{:S(2)}, u32[]{:S(2)}) collective-permute-start(bf16[256,384]{1,0:T(8,128)(2,1)S(1)} %get-tuple-element.32.refs_1_), channel_id=1, source_target_pairs={{0,1},{1,0},{2,3},{3,2},{4,5},{5,4},{6,7},{7,6},{8,9},{9,8},{10,11... | collective-permute-start | bytes 589832 | tf_op jit(solution)/shard_map/ppermute | solution.py:259
  4.8 1.5 %collective-permute-start.2 = (bf16[256,384]{1,0:T(8,128)(2,1)S(1)}, bf16[256,384]{1,0:T(8,128)(2,1)S(1)}, u32[]{:S(2)}, u32[]{:S(2)}) collective-permute-start(bf16[256,384]{1,0:T(8,128)(2,1)S(1)} %get-tuple-element.31.refs_0_), channel_id=1, source_target_pairs={{0,2},{1,3},{2,0},{3,1},{4,6},{5,7},{6,4},{7,5},{8,10},{9,11},{10,... | collective-permute-start | bytes 589832 | tf_op jit(solution)/shard_map/ppermute | solution.py:259
  6.3 0.5 collective-permute-start
  6.9 0.1 collective-permute-start.3
  6.9 0.1 pad_add_fusion.place_ref
  7.0 4.6 %shard_map.59 = (bf16[1536,512]{1,0:T(8,128)(2,1)S(1)}, f32[8,512]{1,0:T(8,128)S(1)}) custom-call(s32[2]{0:T(128)S(1)} %pad_add_fusion.place_ref, s32[1,512]{1,0:T(1,128)} %bitcast.11, f32[1,128]{1,0:T(1,128)} %bitcast.13, bf16[1536,1024]{1,0:T(8,128)(2,1)} %bitcast.9), custom_call_target="tpu_custom_call" | custom-call | bytes 11071024 | tf_op jit(solution)/shard_map/pallas_call | solution.py:246
  11.6 0.0 collective-permute-done.1.refs_3_
  11.6 1.0 %collective-permute-done.2.refs_4_ = bf16[256,384]{1,0:T(8,128)(2,1)S(1)} collective-permute-done((bf16[256,384]{1,0:T(8,128)(2,1)S(1)}, bf16[256,384]{1,0:T(8,128)(2,1)S(1)}, u32[]{:S(2)}, u32[]{:S(2)}) %collective-permute-start.2) | collective-permute-done | bytes 196640 | tf_op jit(solution)/shard_map/ppermute | solution.py:259
  12.6 1.0 %collective-permute-start.4 = (bf16[256,384]{1,0:T(8,128)(2,1)S(1)}, bf16[256,384]{1,0:T(8,128)(2,1)S(1)}, u32[]{:S(2)}, u32[]{:S(2)}) collective-permute-start(bf16[256,384]{1,0:T(8,128)(2,1)S(1)} %collective-permute-done.2.refs_4_), channel_id=1, source_target_pairs={{0,1},{1,0},{2,3},{3,2},{4,5},{5,4},{6,7},{7,6},{8,9},{9,8},{10,11... | collective-permute-start | bytes 589832 | tf_op jit(solution)/shard_map/ppermute | solution.py:259
  13.7 1.5 %collective-permute-start.5 = (bf16[256,384]{1,0:T(8,128)(2,1)S(1)}, bf16[256,384]{1,0:T(8,128)(2,1)S(1)}, u32[]{:S(2)}, u32[]{:S(2)}) collective-permute-start(bf16[256,384]{1,0:T(8,128)(2,1)S(1)} %collective-permute-done.1.refs_3_), channel_id=1, source_target_pairs={{0,2},{1,3},{2,0},{3,1},{4,6},{5,7},{6,4},{7,5},{8,10},{9,11},{10,... | collective-permute-start | bytes 589832 | tf_op jit(solution)/shard_map/ppermute | solution.py:259
  15.2 0.1 pad_add_fusion.1.place_ref
  15.3 0.0 collective-permute-done.refs_2_
  15.3 0.7 %collective-permute-done.3.refs_5_ = bf16[256,384]{1,0:T(8,128)(2,1)S(1)} collective-permute-done((bf16[256,384]{1,0:T(8,128)(2,1)S(1)}, bf16[256,384]{1,0:T(8,128)(2,1)S(1)}, u32[]{:S(2)}, u32[]{:S(2)}) %collective-permute-start.3) | collective-permute-done | bytes 196640 | tf_op jit(solution)/shard_map/ppermute | solution.py:259
  16.0 2.3 %collective-permute-done.4.refs_6_ = bf16[256,384]{1,0:T(8,128)(2,1)S(1)} collective-permute-done((bf16[256,384]{1,0:T(8,128)(2,1)S(1)}, bf16[256,384]{1,0:T(8,128)(2,1)S(1)}, u32[]{:S(2)}, u32[]{:S(2)}) %collective-permute-start.4) | collective-permute-done | bytes 196640 | tf_op jit(solution)/shard_map/ppermute | solution.py:259
  18.3 1.3 %collective-permute-done.5.refs_7_ = bf16[256,384]{1,0:T(8,128)(2,1)S(1)} collective-permute-done((bf16[256,384]{1,0:T(8,128)(2,1)S(1)}, bf16[256,384]{1,0:T(8,128)(2,1)S(1)}, u32[]{:S(2)}, u32[]{:S(2)}) %collective-permute-start.5) | collective-permute-done | bytes 196640 | tf_op jit(solution)/shard_map/ppermute | solution.py:259
  19.6 0.0 copy-start
  19.6 1.7 %shard_map.61 = (bf16[512,1536]{1,0:T(8,128)(2,1)S(1)}, f32[256,512]{1,0:T(8,128)S(1)}, f32[264,512]{1,0:T(8,128)S(1)}) custom-call(s32[3]{0:T(128)S(1)} %pad_add_fusion.1.place_ref, bf16[1536,512]{1,0:T(8,128)(2,1)S(1)} %get-tuple-element.29.chosen_ref, f32[8,512]{1,0:T(8,128)S(1)} %get-tuple-element.30.entry_ref, ...), custom_call_target="tpu_custom_call" | custom-call | bytes 1024 | tf_op jit(solution)/shard_map/pallas_call | solution.py:246
  21.3 0.1 collective-permute-start.6
  21.4 1.9 %collective-permute-done.6.got_ref = f32[264,512]{1,0:T(8,128)S(1)} collective-permute-done((f32[264,512]{1,0:T(8,128)S(1)}, f32[264,512]{1,0:T(8,128)S(1)}, u32[]{:S(2)}, u32[]{:S(2)}) %collective-permute-start.6) | collective-permute-done | bytes 540704 | tf_op jit(solution)/shard_map/ppermute | solution.py:259
  23.3 0.2 shard_map.62
  23.5 0.8 %collective-permute-start.7 = (s16[80,512]{1,0:T(8,128)(2,1)S(1)}, s16[80,512]{1,0:T(8,128)(2,1)S(1)}, u32[]{:S(2)}, u32[]{:S(2)}) collective-permute-start(s16[80,512]{1,0:T(8,128)(2,1)S(1)} %get-tuple-element.39), channel_id=1, source_target_pairs={{0,1},{1,0},{2,3},{3,2},{4,5},{5,4},{6,7},{7,6},{8,9},{9,8},{10,11... | collective-permute-start | bytes 245768 | tf_op jit(solution)/shard_map/ppermute | solution.py:259
  24.3 3.8 %collective-permute-done.7.refs_1_ = s16[80,512]{1,0:T(8,128)(2,1)S(1)} collective-permute-done((s16[80,512]{1,0:T(8,128)(2,1)S(1)}, s16[80,512]{1,0:T(8,128)(2,1)S(1)}, u32[]{:S(2)}, u32[]{:S(2)}) %collective-permute-start.7) | collective-permute-done | bytes 81952 | tf_op jit(solution)/shard_map/ppermute | solution.py:259
  28.0 0.0 copy-done
  28.0 2.4 %shard_map.63 = (f32[2048,128]{1,0:T(8,128)S(1)}, f32[2048,128]{1,0:T(8,128)S(1)}) custom-call(s32[3]{0:T(128)S(1)} %pad_add_fusion.1.place_ref, bf16[1536,1024]{1,0:T(8,128)(2,1)S(1)} %bitcast.10, bf16[512,1536]{1,0:T(8,128)(2,1)S(1)} %get-tuple-element.40.turned_ref), custom_call_target="tpu_custom_call" | custom-call | bytes 1024 | tf_op jit(solution)/shard_map/pallas_call | solution.py:246
  30.4 0.1 collective-permute-start.10
  30.5 1.6 %collective-permute-start.8 = (s16[80,512]{1,0:T(8,128)(2,1)S(1)}, s16[80,512]{1,0:T(8,128)(2,1)S(1)}, u32[]{:S(2)}, u32[]{:S(2)}) collective-permute-start(s16[80,512]{1,0:T(8,128)(2,1)S(1)} %get-tuple-element.43), channel_id=1, source_target_pairs={{0,2},{1,3},{2,0},{3,1},{4,6},{5,7},{6,4},{7,5},{8,10},{9,11},{10,... | collective-permute-start | bytes 245768 | tf_op jit(solution)/shard_map/ppermute | solution.py:259
  32.1 0.7 collective-permute-start.9
  32.7 3.4 %collective-permute-done.8.refs_2_ = s16[80,512]{1,0:T(8,128)(2,1)S(1)} collective-permute-done((s16[80,512]{1,0:T(8,128)(2,1)S(1)}, s16[80,512]{1,0:T(8,128)(2,1)S(1)}, u32[]{:S(2)}, u32[]{:S(2)}) %collective-permute-start.8) | collective-permute-done | bytes 81952 | tf_op jit(solution)/shard_map/ppermute | solution.py:259
  36.2 1.3 %collective-permute-done.9.refs_3_ = s16[80,512]{1,0:T(8,128)(2,1)S(1)} collective-permute-done((s16[80,512]{1,0:T(8,128)(2,1)S(1)}, s16[80,512]{1,0:T(8,128)(2,1)S(1)}, u32[]{:S(2)}, u32[]{:S(2)}) %collective-permute-start.9) | collective-permute-done | bytes 81952 | tf_op jit(solution)/shard_map/ppermute | solution.py:259
  37.5 0.1 shard_map.64.refs_0_
  37.6 1.6 %collective-permute-start.11 = (s16[80,512]{1,0:T(8,128)(2,1)S(1)}, s16[80,512]{1,0:T(8,128)(2,1)S(1)}, u32[]{:S(2)}, u32[]{:S(2)}) collective-permute-start(s16[80,512]{1,0:T(8,128)(2,1)S(1)} %shard_map.64.refs_0_), channel_id=1, source_target_pairs={{0,8},{4,12},{8,0},{12,4},{16,24},{20,28},{24,16},{28,20},{1,9},{5... | collective-permute-start | bytes 245768 | tf_op jit(solution)/shard_map/ppermute | solution.py:259
  39.2 0.0 collective-permute-done.10.got_ref
  39.2 0.2 shard_map.65
  39.5 2.7 %collective-permute-done.11.refs_1_ = s16[80,512]{1,0:T(8,128)(2,1)S(1)} collective-permute-done((s16[80,512]{1,0:T(8,128)(2,1)S(1)}, s16[80,512]{1,0:T(8,128)(2,1)S(1)}, u32[]{:S(2)}, u32[]{:S(2)}) %collective-permute-start.11) | collective-permute-done | bytes 81952 | tf_op jit(solution)/shard_map/ppermute | solution.py:259
  42.1 0.1 shard_map.66.refs_0_
  42.2 2.7 %collective-permute-start.12 = (s16[80,512]{1,0:T(8,128)(2,1)S(1)}, s16[80,512]{1,0:T(8,128)(2,1)S(1)}, u32[]{:S(2)}, u32[]{:S(2)}) collective-permute-start(s16[80,512]{1,0:T(8,128)(2,1)S(1)} %shard_map.66.refs_0_), channel_id=1, source_target_pairs={{0,16},{4,20},{8,24},{12,28},{16,0},{20,4},{24,8},{28,12},{1,17},{... | collective-permute-start | bytes 245768 | tf_op jit(solution)/shard_map/ppermute | solution.py:259
  44.9 2.8 %collective-permute-done.12.refs_1_ = s16[80,512]{1,0:T(8,128)(2,1)S(1)} collective-permute-done((s16[80,512]{1,0:T(8,128)(2,1)S(1)}, s16[80,512]{1,0:T(8,128)(2,1)S(1)}, u32[]{:S(2)}, u32[]{:S(2)}) %collective-permute-start.12) | collective-permute-done | bytes 81952 | tf_op jit(solution)/shard_map/ppermute | solution.py:259
  47.6 0.1 shard_map.67.refs_0_
  47.7 1.4 %collective-permute-start.15 = (s16[80,512]{1,0:T(8,128)(2,1)S(1)}, s16[80,512]{1,0:T(8,128)(2,1)S(1)}, u32[]{:S(2)}, u32[]{:S(2)}) collective-permute-start(s16[80,512]{1,0:T(8,128)(2,1)S(1)} %shard_map.67.refs_0_), channel_id=1, source_target_pairs={{0,3},{1,2},{2,1},{3,0},{4,7},{5,6},{6,5},{7,4},{8,11},{9,10},{10,... | collective-permute-start | bytes 245768 | tf_op jit(solution)/shard_map/ppermute | solution.py:259
  49.1 0.9 %collective-permute-start.14 = (s16[80,512]{1,0:T(8,128)(2,1)S(1)}, s16[80,512]{1,0:T(8,128)(2,1)S(1)}, u32[]{:S(2)}, u32[]{:S(2)}) collective-permute-start(s16[80,512]{1,0:T(8,128)(2,1)S(1)} %shard_map.67.refs_0_), channel_id=1, source_target_pairs={{0,2},{1,3},{2,0},{3,1},{4,6},{5,7},{6,4},{7,5},{8,10},{9,11},{10,... | collective-permute-start | bytes 245768 | tf_op jit(solution)/shard_map/ppermute | solution.py:259
  50.0 1.3 %collective-permute-start.13 = (s16[80,512]{1,0:T(8,128)(2,1)S(1)}, s16[80,512]{1,0:T(8,128)(2,1)S(1)}, u32[]{:S(2)}, u32[]{:S(2)}) collective-permute-start(s16[80,512]{1,0:T(8,128)(2,1)S(1)} %shard_map.67.refs_0_), channel_id=1, source_target_pairs={{0,1},{1,0},{2,3},{3,2},{4,5},{5,4},{6,7},{7,6},{8,9},{9,8},{10,11... | collective-permute-start | bytes 245768 | tf_op jit(solution)/shard_map/ppermute | solution.py:259
  51.3 1.6 %collective-permute-start.17 = (s16[1056,128]{1,0:T(8,128)(2,1)S(1)}, s16[1056,128]{1,0:T(8,128)(2,1)S(1)}, u32[]{:S(2)}, u32[]{:S(2)}) collective-permute-start(s16[1056,128]{1,0:T(8,128)(2,1)S(1)} %get-tuple-element.53), channel_id=1, source_target_pairs={{0,8},{4,12},{8,0},{12,4},{16,24},{20,28},{24,16},{28,20},{1,9},{5... | collective-permute-start | bytes 811016 | tf_op jit(solution)/shard_map/ppermute | solution.py:259
  52.9 0.3 collective-permute-done.15.refs_3_
  53.2 0.8 %collective-permute-done.14.refs_2_ = s16[80,512]{1,0:T(8,128)(2,1)S(1)} collective-permute-done((s16[80,512]{1,0:T(8,128)(2,1)S(1)}, s16[80,512]{1,0:T(8,128)(2,1)S(1)}, u32[]{:S(2)}, u32[]{:S(2)}) %collective-permute-start.14) | collective-permute-done | bytes 81952 | tf_op jit(solution)/shard_map/ppermute | solution.py:259
  54.0 0.4 collective-permute-done.13.refs_1_
  54.5 0.0 copy-start.1
  54.5 0.0 copy-start.2
  54.5 0.1 collective-permute-start.16
  54.6 3.2 %collective-permute-done.17.got_ref = s16[1056,128]{1,0:T(8,128)(2,1)S(1)} collective-permute-done((s16[1056,128]{1,0:T(8,128)(2,1)S(1)}, s16[1056,128]{1,0:T(8,128)(2,1)S(1)}, u32[]{:S(2)}, u32[]{:S(2)}) %collective-permute-start.17) | collective-permute-done | bytes 270368 | tf_op jit(solution)/shard_map/ppermute | solution.py:259
  57.7 0.2 shard_map.71
  57.9 3.0 %collective-permute-start.18 = (s16[528,128]{1,0:T(8,128)(2,1)S(1)}, s16[528,128]{1,0:T(8,128)(2,1)S(1)}, u32[]{:S(2)}, u32[]{:S(2)}) collective-permute-start(s16[528,128]{1,0:T(8,128)(2,1)S(1)} %get-tuple-element.55), channel_id=1, source_target_pairs={{0,16},{4,20},{8,24},{12,28},{16,0},{20,4},{24,8},{28,12},{1,17},{... | collective-permute-start | bytes 405512 | tf_op jit(solution)/shard_map/ppermute | solution.py:259
  60.9 0.0 collective-permute-done.16.other_ref
  60.9 4.1 %shard_map.69 = (f32[256,256]{1,0:T(8,128)S(1)}, f32[512,512]{1,0:T(8,128)S(1)}) custom-call(s32[3]{0:T(128)S(1)} %pad_add_fusion.1.place_ref, s16[320,512]{1,0:T(8,128)(2,1)S(1)} %shard_map.68.own_ref, s16[320,512]{1,0:T(8,128)(2,1)S(1)} %collective-permute-done.16.other_ref), custom_call_target="tpu_custom_call" | custom-call | bytes 16606024 | tf_op jit(solution)/shard_map/pallas_call | solution.py:246
  65.0 3.8 %shard_map.70.inverse_second_ref = f32[256,256]{1,0:T(8,128)S(1)} custom-call(f32[512,512]{1,0:T(8,128)S(1)} %get-tuple-element.51.pivots_ref, f32[256,256]{1,0:T(8,128)S(1)} %get-tuple-element.50.inverse_first_ref), custom_call_target="tpu_custom_call" | custom-call | bytes 16606024 | tf_op jit(solution)/shard_map/pallas_call | solution.py:246
  68.8 0.0 collective-permute-done.18.refs_0_
  68.8 0.0 copy-done.1
  68.8 0.0 copy-done.2
  68.8 2.2 %shard_map.72 = (f32[128,1,256]{2,1,0:T(1,128)}, f32[128,1,256]{2,1,0:T(1,128)}) custom-call(s32[2]{0:T(128)S(1)} %pad_add_fusion.place_ref, s32[1,512]{1,0:T(1,128)S(1)} %bitcast.12, f32[1,128]{1,0:T(1,128)S(1)} %bitcast.14, f32[256,256]{1,0:T(8,128)S(1)} %get-tuple-element.50.inverse_first_ref, f32[256,256]{1,0:T(8,128)S(1)} %shard_map.70.inverse_second_ref, ...), custom_call_target="tpu_custom_call" | custom-call | bytes 1024 | tf_op jit(solution)/shard_map/pallas_call | solution.py:246
  (1 shorter events, 0.0 us)
Async XLA Ops:
  1.8 9.8 %collective-permute-start.1 = (bf16[256,384]{1,0:T(8,128)(2,1)S(1)}, bf16[256,384]{1,0:T(8,128)(2,1)S(1)}, u32[]{:S(2)}, u32[]{:S(2)}) collective-permute-start(bf16[256,384]{1,0:T(8,128)(2,1)S(1)} %get-tuple-element.32.refs_1_), channel_id=1, source_target_pairs={{0,1},{1,0},{2,3},{3,2},{4,5},{5,4},{6,7},{7,6},{8,9},{9,8},{10,11... | collective-permute-start | bytes 589832 | tf_op jit(solution)/shard_map/ppermute | solution.py:259
  4.8 7.8 %collective-permute-start.2 = (bf16[256,384]{1,0:T(8,128)(2,1)S(1)}, bf16[256,384]{1,0:T(8,128)(2,1)S(1)}, u32[]{:S(2)}, u32[]{:S(2)}) collective-permute-start(bf16[256,384]{1,0:T(8,128)(2,1)S(1)} %get-tuple-element.31.refs_0_), channel_id=1, source_target_pairs={{0,2},{1,3},{2,0},{3,1},{4,6},{5,7},{6,4},{7,5},{8,10},{9,11},{10,... | collective-permute-start | bytes 589832 | tf_op jit(solution)/shard_map/ppermute | solution.py:259
  6.3 8.9 %collective-permute-start = (bf16[256,384]{1,0:T(8,128)(2,1)S(1)}, bf16[256,384]{1,0:T(8,128)(2,1)S(1)}, u32[]{:S(2)}, u32[]{:S(2)}) collective-permute-start(bf16[256,384]{1,0:T(8,128)(2,1)S(1)} %get-tuple-element.31.refs_0_), channel_id=1, source_target_pairs={{0,1},{1,0},{2,3},{3,2},{4,5},{5,4},{6,7},{7,6},{8,9},{9,8},{10,11... | collective-permute-start | bytes 589832 | tf_op jit(solution)/shard_map/ppermute | solution.py:259
  6.9 9.1 %collective-permute-start.3 = (bf16[256,384]{1,0:T(8,128)(2,1)S(1)}, bf16[256,384]{1,0:T(8,128)(2,1)S(1)}, u32[]{:S(2)}, u32[]{:S(2)}) collective-permute-start(bf16[256,384]{1,0:T(8,128)(2,1)S(1)} %get-tuple-element.32.refs_1_), channel_id=1, source_target_pairs={{0,2},{1,3},{2,0},{3,1},{4,6},{5,7},{6,4},{7,5},{8,10},{9,11},{10,... | collective-permute-start | bytes 589832 | tf_op jit(solution)/shard_map/ppermute | solution.py:259
  12.6 5.7 %collective-permute-start.4 = (bf16[256,384]{1,0:T(8,128)(2,1)S(1)}, bf16[256,384]{1,0:T(8,128)(2,1)S(1)}, u32[]{:S(2)}, u32[]{:S(2)}) collective-permute-start(bf16[256,384]{1,0:T(8,128)(2,1)S(1)} %collective-permute-done.2.refs_4_), channel_id=1, source_target_pairs={{0,1},{1,0},{2,3},{3,2},{4,5},{5,4},{6,7},{7,6},{8,9},{9,8},{10,11... | collective-permute-start | bytes 589832 | tf_op jit(solution)/shard_map/ppermute | solution.py:259
  13.7 5.9 %collective-permute-start.5 = (bf16[256,384]{1,0:T(8,128)(2,1)S(1)}, bf16[256,384]{1,0:T(8,128)(2,1)S(1)}, u32[]{:S(2)}, u32[]{:S(2)}) collective-permute-start(bf16[256,384]{1,0:T(8,128)(2,1)S(1)} %collective-permute-done.1.refs_3_), channel_id=1, source_target_pairs={{0,2},{1,3},{2,0},{3,1},{4,6},{5,7},{6,4},{7,5},{8,10},{9,11},{10,... | collective-permute-start | bytes 589832 | tf_op jit(solution)/shard_map/ppermute | solution.py:259
  19.6 8.4 %copy-start = (bf16[1,1536,1024]{2,1,0:T(8,128)(2,1)S(1)}, bf16[1,1536,1024]{2,1,0:T(8,128)(2,1)}, u32[]{:S(2)}) copy-start(bf16[1,1536,1024]{2,1,0:T(8,128)(2,1)} %param.4) | copy-start | bytes 9437188
  21.3 2.0 %collective-permute-start.6 = (f32[264,512]{1,0:T(8,128)S(1)}, f32[264,512]{1,0:T(8,128)S(1)}, u32[]{:S(2)}, u32[]{:S(2)}) collective-permute-start(f32[264,512]{1,0:T(8,128)S(1)} %get-tuple-element.36), channel_id=1, source_target_pairs={{0,4},{4,0},{8,12},{12,8},{16,20},{20,16},{24,28},{28,24},{1,5},{5... | collective-permute-start | bytes 1622024 | tf_op jit(solution)/shard_map/ppermute | solution.py:259
  23.5 4.6 %collective-permute-start.7 = (s16[80,512]{1,0:T(8,128)(2,1)S(1)}, s16[80,512]{1,0:T(8,128)(2,1)S(1)}, u32[]{:S(2)}, u32[]{:S(2)}) collective-permute-start(s16[80,512]{1,0:T(8,128)(2,1)S(1)} %get-tuple-element.39), channel_id=1, source_target_pairs={{0,1},{1,0},{2,3},{3,2},{4,5},{5,4},{6,7},{7,6},{8,9},{9,8},{10,11... | collective-permute-start | bytes 245768 | tf_op jit(solution)/shard_map/ppermute | solution.py:259
  30.4 8.9 %collective-permute-start.10 = (f32[2048,128]{1,0:T(8,128)S(1)}, f32[2048,128]{1,0:T(8,128)S(1)}, u32[]{:S(2)}, u32[]{:S(2)}) collective-permute-start(f32[2048,128]{1,0:T(8,128)S(1)} %get-tuple-element.46), channel_id=1, source_target_pairs={{0,4},{4,0},{8,12},{12,8},{16,20},{20,16},{24,28},{28,24},{1,5},{5... | collective-permute-start | bytes 3145736 | tf_op jit(solution)/shard_map/ppermute | solution.py:259
  30.5 5.7 %collective-permute-start.8 = (s16[80,512]{1,0:T(8,128)(2,1)S(1)}, s16[80,512]{1,0:T(8,128)(2,1)S(1)}, u32[]{:S(2)}, u32[]{:S(2)}) collective-permute-start(s16[80,512]{1,0:T(8,128)(2,1)S(1)} %get-tuple-element.43), channel_id=1, source_target_pairs={{0,2},{1,3},{2,0},{3,1},{4,6},{5,7},{6,4},{7,5},{8,10},{9,11},{10,... | collective-permute-start | bytes 245768 | tf_op jit(solution)/shard_map/ppermute | solution.py:259
  32.1 5.4 %collective-permute-start.9 = (s16[80,512]{1,0:T(8,128)(2,1)S(1)}, s16[80,512]{1,0:T(8,128)(2,1)S(1)}, u32[]{:S(2)}, u32[]{:S(2)}) collective-permute-start(s16[80,512]{1,0:T(8,128)(2,1)S(1)} %get-tuple-element.44), channel_id=1, source_target_pairs={{0,3},{1,2},{2,1},{3,0},{4,7},{5,6},{6,5},{7,4},{8,11},{9,10},{10,... | collective-permute-start | bytes 245768 | tf_op jit(solution)/shard_map/ppermute | solution.py:259
  37.6 4.5 %collective-permute-start.11 = (s16[80,512]{1,0:T(8,128)(2,1)S(1)}, s16[80,512]{1,0:T(8,128)(2,1)S(1)}, u32[]{:S(2)}, u32[]{:S(2)}) collective-permute-start(s16[80,512]{1,0:T(8,128)(2,1)S(1)} %shard_map.64.refs_0_), channel_id=1, source_target_pairs={{0,8},{4,12},{8,0},{12,4},{16,24},{20,28},{24,16},{28,20},{1,9},{5... | collective-permute-start | bytes 245768 | tf_op jit(solution)/shard_map/ppermute | solution.py:259
  42.2 5.4 %collective-permute-start.12 = (s16[80,512]{1,0:T(8,128)(2,1)S(1)}, s16[80,512]{1,0:T(8,128)(2,1)S(1)}, u32[]{:S(2)}, u32[]{:S(2)}) collective-permute-start(s16[80,512]{1,0:T(8,128)(2,1)S(1)} %shard_map.66.refs_0_), channel_id=1, source_target_pairs={{0,16},{4,20},{8,24},{12,28},{16,0},{20,4},{24,8},{28,12},{1,17},{... | collective-permute-start | bytes 245768 | tf_op jit(solution)/shard_map/ppermute | solution.py:259
  47.7 5.5 %collective-permute-start.15 = (s16[80,512]{1,0:T(8,128)(2,1)S(1)}, s16[80,512]{1,0:T(8,128)(2,1)S(1)}, u32[]{:S(2)}, u32[]{:S(2)}) collective-permute-start(s16[80,512]{1,0:T(8,128)(2,1)S(1)} %shard_map.67.refs_0_), channel_id=1, source_target_pairs={{0,3},{1,2},{2,1},{3,0},{4,7},{5,6},{6,5},{7,4},{8,11},{9,10},{10,... | collective-permute-start | bytes 245768 | tf_op jit(solution)/shard_map/ppermute | solution.py:259
  49.1 4.9 %collective-permute-start.14 = (s16[80,512]{1,0:T(8,128)(2,1)S(1)}, s16[80,512]{1,0:T(8,128)(2,1)S(1)}, u32[]{:S(2)}, u32[]{:S(2)}) collective-permute-start(s16[80,512]{1,0:T(8,128)(2,1)S(1)} %shard_map.67.refs_0_), channel_id=1, source_target_pairs={{0,2},{1,3},{2,0},{3,1},{4,6},{5,7},{6,4},{7,5},{8,10},{9,11},{10,... | collective-permute-start | bytes 245768 | tf_op jit(solution)/shard_map/ppermute | solution.py:259
  50.0 4.4 %collective-permute-start.13 = (s16[80,512]{1,0:T(8,128)(2,1)S(1)}, s16[80,512]{1,0:T(8,128)(2,1)S(1)}, u32[]{:S(2)}, u32[]{:S(2)}) collective-permute-start(s16[80,512]{1,0:T(8,128)(2,1)S(1)} %shard_map.67.refs_0_), channel_id=1, source_target_pairs={{0,1},{1,0},{2,3},{3,2},{4,5},{5,4},{6,7},{7,6},{8,9},{9,8},{10,11... | collective-permute-start | bytes 245768 | tf_op jit(solution)/shard_map/ppermute | solution.py:259
  51.3 6.5 %collective-permute-start.17 = (s16[1056,128]{1,0:T(8,128)(2,1)S(1)}, s16[1056,128]{1,0:T(8,128)(2,1)S(1)}, u32[]{:S(2)}, u32[]{:S(2)}) collective-permute-start(s16[1056,128]{1,0:T(8,128)(2,1)S(1)} %get-tuple-element.53), channel_id=1, source_target_pairs={{0,8},{4,12},{8,0},{12,4},{16,24},{20,28},{24,16},{28,20},{1,9},{5... | collective-permute-start | bytes 811016 | tf_op jit(solution)/shard_map/ppermute | solution.py:259
  54.5 14.4 %copy-start.1 = (s32[512]{0:T(512)S(1)}, s32[512]{0:T(512)}, u32[]{:S(2)}) copy-start(s32[512]{0:T(512)} %param.7) | copy-start | bytes 6148
  54.5 14.4 %copy-start.2 = (f32[128,1]{0,1:T(1,128)S(1)}, f32[128,1]{0,1:T(1,128)}, u32[]{:S(2)}) copy-start(f32[128,1]{0,1:T(1,128)} %param.6) | copy-start | bytes 1540
  54.5 6.4 %collective-permute-start.16 = (s16[320,512]{1,0:T(8,128)(2,1)S(1)}, s16[320,512]{1,0:T(8,128)(2,1)S(1)}, u32[]{:S(2)}, u32[]{:S(2)}) collective-permute-start(s16[320,512]{1,0:T(8,128)(2,1)S(1)} %shard_map.68.own_ref), channel_id=1, source_target_pairs={{0,4},{4,0},{8,12},{12,8},{16,20},{20,16},{24,28},{28,24},{1,5},{5... | collective-permute-start | bytes 983048 | tf_op jit(solution)/shard_map/ppermute | solution.py:259
  57.9 10.9 %collective-permute-start.18 = (s16[528,128]{1,0:T(8,128)(2,1)S(1)}, s16[528,128]{1,0:T(8,128)(2,1)S(1)}, u32[]{:S(2)}, u32[]{:S(2)}) collective-permute-start(s16[528,128]{1,0:T(8,128)(2,1)S(1)} %get-tuple-element.55), channel_id=1, source_target_pairs={{0,16},{4,20},{8,24},{12,28},{16,0},{20,4},{24,8},{28,12},{1,17},{... | collective-permute-start | bytes 405512 | tf_op jit(solution)/shard_map/ppermute | solution.py:259

commit v5 on v4

--- a/solution.py
+++ b/solution.py
@@ -99,51 +99,79 @@
     lower_ref[...] = turned[half:]
 
 
+def fetch(source_ref, target_ref, done, first):
+    rows = target_ref.shape[1]
+    copies = [
+        pltpu.make_async_copy(source_ref.at[pl.ds((first + i) * rows, rows), :], target_ref.at[i], done.at[i])
+        for i in range(target_ref.shape[0])
+    ]
+    for copy in copies:
+        copy.start()
+    return copies
+
+
+def choose(copies, coupling_copy, one_ref, chosen_ref):
+    rows = coupling_copy.shape[1]
+    for i, copy in enumerate(copies):
+        copy.wait()
+        chosen_ref[i * rows:(i + 1) * rows, :] = dot(coupling_copy[i], one_ref[...]).astype(BF16)
+
+
 def pick_kernel(
-    place_ref, panel_ref, own_diagonal_ref, coupling_ref, chosen_ref, entry_ref,
-    panel_copy, diagonal_copy, coupling_copy, one_ref, small_done, done,
+    place_ref, panel_ref, own_diagonal_ref, coupling_ref,
+    chosen_ref, entry_ref, one_ref, panel_out, diagonal_out, coupling_copy, small_done, done,
 ):
-    chunks, rows, columns = coupling_copy.shape
     small = [
-        pltpu.make_async_copy(panel_ref, panel_copy, small_done.at[0]),
-        pltpu.make_async_copy(own_diagonal_ref, diagonal_copy, small_done.at[1]),
+        pltpu.make_async_copy(panel_ref, panel_out, small_done.at[0]),
+        pltpu.make_async_copy(own_diagonal_ref, diagonal_out, small_done.at[1]),
     ]
-    large = [
-        pltpu.make_async_copy(coupling_ref.at[pl.ds(i * rows, rows), :], coupling_copy.at[i], done.at[i])
-        for i in range(chunks)
-    ]
-    for copy in small + large:
+    for copy in small:
         copy.start()
+    copies = fetch(coupling_ref, coupling_copy, done, 0)
     for copy in small:
         copy.wait()
     first_column, first_row = place_ref[0], place_ref[1]
-    panel, share = panel_copy.shape[1], diagonal_copy.shape[1]
-    here = panel_copy[...] - first_column == lax.broadcasted_iota(jnp.int32, (columns, panel), 0)
+    columns, panel = one_ref.shape
+    share = diagonal_out.shape[1]
+    here = panel_out[...] - first_column == lax.broadcasted_iota(jnp.int32, (columns, panel), 0)
     one_ref[...] = jnp.where(here, F32(1.0), F32(0.0)).astype(BF16)
-    owned = panel_copy[...] - first_row == lax.broadcasted_iota(jnp.int32, (share, panel), 0)
-    own = jnp.broadcast_to(diagonal_copy[...], (8, share)).T[:, :1]
+    owned = panel_out[...] - first_row == lax.broadcasted_iota(jnp.int32, (share, panel), 0)
+    own = jnp.broadcast_to(diagonal_out[...], (8, share)).T[:, :1]
     entry = jnp.sum(jnp.where(owned, own, F32(0.0)), axis=0, keepdims=True)
     entry_ref[...] = jnp.broadcast_to(entry, entry_ref.shape)
-    for i, copy in enumerate(large):
-        copy.wait()
-        chosen_ref[i * rows:(i + 1) * rows, :] = dot(coupling_copy[i], one_ref[...]).astype(BF16)
-
-
-def terms_kernel(rows, place_ref, chosen_ref, entry_ref, *refs):
-    *pieces, turned_ref, keep_ref, send_ref, all_ref = refs
-    row, core = place_ref[0], place_ref[1]
+    choose(copies, coupling_copy, one_ref, chosen_ref)
+
+
+def rest_kernel(one_ref, coupling_ref, chosen_ref, coupling_copy, done):
+    copies = fetch(coupling_ref, coupling_copy, done, coupling_copy.shape[0])
+    choose(copies, coupling_copy, one_ref, chosen_ref)
+
+
+def pivot_terms(place_ref, turned_ref, chosen_ref, more_ref, out_ref, all_ref, rows, whose):
+    half = all_ref.shape[0]
+    size = half // rows
+    middle = chosen_ref.shape[0]
+    block = turned_ref[pl.ds(aligned(whose, half), half), :]
+    all_ref[...] = dot(block[:, :middle], chosen_ref[...]) + dot(block[:, middle:], more_ref[...])
+    for k in range(rows):
+        out_ref[k * size:(k + 1) * size, :] = all_ref[pl.ds(aligned(place_ref[0] ^ k, size), size), :]
+
+
+def send_kernel(rows, place_ref, chosen_ref, more_ref, entry_ref, *refs):
+    *pieces, turned_ref, send_ref, all_ref = refs
     if len(pieces) == 1:
         turned_ref[...] = pieces[0][...]
     else:
         half, width = pieces[0].shape
         for i, piece in enumerate(pieces):
-            turned_ref[i % 2 * half:(i % 2 + 1) * half, pl.ds(aligned(row ^ (i // 2), width), width)] = piece[...]
-    all_ref[...] = dot(turned_ref[...], chosen_ref[...])
-    size = keep_ref.shape[0] // rows
-    for out_ref, whose in ((keep_ref, core), (send_ref, 1 - core)):
-        for k in range(rows):
-            out_ref[k * size:(k + 1) * size, :] = all_ref[pl.ds(aligned(whose * rows + (row ^ k), size), size), :]
-    send_ref[rows * size:, :] = entry_ref[...]
+            start = aligned(place_ref[0] ^ (i // 2), width)
+            turned_ref[i % 2 * half:(i % 2 + 1) * half, pl.ds(start, width)] = piece[...]
+    pivot_terms(place_ref, turned_ref, chosen_ref, more_ref, send_ref, all_ref, rows, 1 - place_ref[1])
+    send_ref[all_ref.shape[0]:, :] = entry_ref[...]
+
+
+def keep_kernel(rows, place_ref, chosen_ref, more_ref, turned_ref, keep_ref, all_ref):
+    pivot_terms(place_ref, turned_ref, chosen_ref, more_ref, keep_ref, all_ref, rows, place_ref[1])
 
 
 def pair_kernel(rows, keep_ref, got_ref, entry_ref, *out_refs):
@@ -189,7 +217,7 @@
     inverse_ref[...] = newton(pivots_ref[half:, half:] - product(pivots_ref[half:, :half], lower_factor))
 
 
-def schur_kernel(place_ref, coupling_ref, turned_ref, keep_ref, send_ref):
+def schur_kernel(place_ref, panel_ref, own_diagonal_ref, coupling_ref, turned_ref, keep_ref, send_ref):
     core, layer = place_ref[1], place_ref[2]
     panel, share = turned_ref.shape[0], keep_ref.shape[1]
     layers = keep_ref.shape[0] // panel
@@ -198,7 +226,12 @@
         both = dot(turned_ref[...], coupling_ref[:, pl.ds(start, 2 * share)])
         rows = slice(position * panel, (position + 1) * panel)
         one, two = both[:, :share], both[:, share:]
-        keep_ref[rows, :] = jnp.where(core == 0, one, two)
+        kept = jnp.where(core == 0, one, two)
+        if position == 0:
+            wanted = jnp.broadcast_to(panel_ref[...].astype(F32), (share, panel)).T.astype(jnp.int32)
+            here = wanted - place_ref[3] == lax.broadcasted_iota(jnp.int32, (panel, share), 1)
+            kept = kept + jnp.where(here, own_diagonal_ref[...], F32(0.0))
+        keep_ref[rows, :] = kept
         send_ref[rows, :] = jnp.where(core == 0, two, one)
 
 
@@ -220,15 +253,11 @@
             encode(value, coded_ref, (i - half // panel) * (panel + TAIL))
 
 
-def factor_kernel(
-    place_ref, panel_ref, own_diagonal_ref, inverse_first_ref, inverse_second_ref, pivots_ref, rows_ref, *refs
-):
+def factor_kernel(inverse_first_ref, inverse_second_ref, pivots_ref, rows_ref, *refs):
     *got, first_out, second_out = refs
-    panel, share = rows_ref.shape
+    panel = rows_ref.shape[0]
     half = panel // 2
-    turned = jnp.broadcast_to(panel_ref[...].astype(F32), (share, panel)).T.astype(jnp.int32)
-    here = turned - place_ref[1] == lax.broadcasted_iota(jnp.int32, (panel, share), 1)
-    rows = rows_ref[...] + jnp.where(here, own_diagonal_ref[...], F32(0.0))
+    rows = rows_ref[...]
     for ref in got:
         rows = rows + decode(ref, 0, panel)[0]
     first_factor = product(inverse_first_ref[...], rows[:half])
@@ -245,6 +274,7 @@
     args = args[:stay] + tuple(pltpu.with_memory_space_constraint(x, pltpu.HBM) for x in args[stay:])
     return pl.pallas_call(
         kernel,
+        name=getattr(kernel, "func", kernel).__name__,
         out_shape=out_shape,
         in_specs=[smem] * scalars + [vmem] * (len(args) - scalars - remain) + [hbm] * remain,
         out_specs=jax.tree.map(lambda _: vmem, out_shape),
@@ -299,66 +329,71 @@
     size = panel // (2 * rows)
     shape = jax.ShapeDtypeStruct
     panel_row, diagonal_row = panel_rows[None, :], border_diagonal.T
-    starts = jnp.stack([row * row_count, row * row_count + place * share]).astype(jnp.int32)
-    at = jnp.stack([row, place % 2, place // 2]).astype(jnp.int32)
-
-    chosen, entry = call(
-        pick_kernel, (pltpu.VMEM((local, panel), BF16), pltpu.VMEM((8, panel), F32)),
-        starts, panel_row, diagonal_row, coupling, scalars=1, remain=3, micros=3.0,
-        scratch=[
-            pltpu.VMEM((1, panel), jnp.int32),
-            pltpu.VMEM((1, share), F32),
-            pltpu.VMEM((CHUNKS, local // CHUNKS, row_count), BF16),
-            pltpu.VMEM((row_count, panel), BF16),
-            pltpu.SemaphoreType.DMA((2,)),
-            pltpu.SemaphoreType.DMA((CHUNKS,)),
-        ],
+    first_row = row * row_count + place * share
+    starts = jnp.stack([row * row_count, first_row]).astype(jnp.int32)
+    at = jnp.stack([row, place % 2, place // 2, first_row]).astype(jnp.int32)
+
+    picked = shape((local // 2, panel), BF16)
+    chunk_room = [
+        pltpu.VMEM((CHUNKS // 2, local // CHUNKS, row_count), BF16), pltpu.SemaphoreType.DMA((CHUNKS // 2,))
+    ]
+    chosen, entry, one, panel_row, diagonal_row = call(
+        pick_kernel,
+        (
+            picked, shape((8, panel), F32), shape((row_count, panel), BF16),
+            shape((1, panel), jnp.int32), shape((1, share), F32),
+        ),
+        starts, panel_row, diagonal_row, coupling, scalars=1, remain=3,
+        scratch=[chunk_room[0], pltpu.SemaphoreType.DMA((2,)), chunk_room[1]],
     )
     pieces = gather_pieces(solves, rows, (entry,))
-    turned, keep, send = call(
-        functools.partial(terms_kernel, rows),
-        (shape((panel, local), BF16), shape((panel // 2, panel), F32), shape((panel // 2 + 8, panel), F32)),
-        at, chosen, entry, *pieces, scalars=1, scratch=[pltpu.VMEM((panel, panel), F32)],
+    more = call(rest_kernel, picked, one, coupling, remain=1, scratch=chunk_room)
+    room = [pltpu.VMEM((panel // 2, panel), F32)]
+    turned, send = call(
+        functools.partial(send_kernel, rows),
+        (shape((panel, local), BF16), shape((panel // 2 + 8, panel), F32)),
+        at, chosen, more, entry, *pieces, scalars=1, scratch=room,
+    )
+    keep = call(
+        functools.partial(keep_kernel, rows), shape((panel // 2, panel), F32),
+        at, chosen, more, turned, scalars=1, scratch=room,
     )
     coded = shape((size + TAIL, panel), I16)
     codes = call(
         functools.partial(pair_kernel, rows), (coded,) * rows, keep, swap(send, "scen", 1), entry
     )
-    arrived = [swap(codes[k], "row", k) for k in range(1, rows)]
-
-    if share % 128:
-        terms = dot(turned, coupling)
-        own, got = lax.psum_scatter(terms, "scen", scatter_dimension=1, tiled=True), []
-        part = call(sum_kernel, coded, codes[0], *arrived)
-        for bit in bits_of(layers):
-            part = call(sum_kernel, coded, part, swap(part, "scen", 2 * bit))
+    arrived = [swap(codes[k], "row", k) for k in range(rows - 1, 0, -1)]
+    part = codes[0]
+    steps = bits_of(layers)
+    split = share % 128 == 0
+    if split:
+        count = layers // 2
+        bulk = shape((layers * panel, share), F32)
+        halved = lambda count: (shape((count * panel, share), F32), shape((count * (panel + TAIL), share), I16))
+        own, send_rows = call(
+            schur_kernel, (bulk, bulk), at, panel_row, diagonal_row, coupling, after(turned, part), scalars=1
+        )
+        part = call(sum_kernel, coded, after(part, own), *arrived)
+        got = swap(after(send_rows, part), "scen", 1)
     else:
-        bulk = shape((layers * panel, share), F32)
-        keep, send = call(schur_kernel, (bulk, bulk), at, coupling, after(turned, arrived[0]), scalars=1)
-        got = swap(send, "scen", 1)
-        part = call(sum_kernel, coded, after(codes[0], keep), *arrived)
-        steps = bits_of(layers)
-        count = layers // 2
-        own, bulk_codes = call(
-            functools.partial(bulk_pair_kernel, panel),
-            (shape((count * panel, share), F32), shape((count * (panel + TAIL), share), I16)),
-            after(keep, part), got,
-        )
-        for bit in steps:
-            before, other = part, swap(part, "scen", 2 * bit)
-            part = call(sum_kernel, coded, after(part, bulk_codes), other)
+        own, got = lax.psum_scatter(dot(turned, coupling), "scen", scatter_dimension=1, tiled=True), []
+        mine = first_row + jnp.arange(share, dtype=jnp.int32)
+        own = own + jnp.where(panel_rows[:, None] == mine[None, :], border_diagonal[:, 0][None, :], F32(0.0))
+        part = call(sum_kernel, coded, part, *arrived)
+    for bit in steps:
+        other = swap(part, "scen", 2 * bit)
+        if split and bit == steps[-1]:
+            own, bulk_codes = call(functools.partial(bulk_pair_kernel, panel), halved(count), after(own, part), got)
+            part = after(part, bulk_codes)
+        part = call(sum_kernel, coded, part, other)
+    shared = [swap(part, "row", k) for k in range(1, rows)]
+    if split:
         for bit in steps[:-1]:
             count //= 2
-            own, bulk_codes = call(
-                functools.partial(bulk_sum_kernel, panel),
-                (shape((count * panel, share), F32), shape((count * (panel + TAIL), share), I16)),
-                own, swap(after(bulk_codes, before), "scen", 2 * bit),
-            )
+            got = swap(bulk_codes, "scen", 2 * bit)
+            own, bulk_codes = call(functools.partial(bulk_sum_kernel, panel), halved(count), own, got)
         got = [swap(bulk_codes, "scen", layers)]
-
-    joined = call(
-        join_kernel, shape((rows * (size + TAIL), panel), I16), part, *[swap(part, "row", k) for k in range(1, rows)]
-    )
+    joined = call(join_kernel, shape((rows * (size + TAIL), panel), I16), part, *shared)
     square = shape((half, half), F32)
     inverse_first, pivots = call(
         functools.partial(first_kernel, rows), (square, shape((panel, panel), F32)),
@@ -368,7 +403,7 @@
     out = shape((share, 1, half), F32)
     return call(
         factor_kernel, (out, out),
-        starts, panel_row, diagonal_row, inverse_first, inverse_second, pivots, own, *got, scalars=1,
+        inverse_first, inverse_second, pivots, own, *got,
     )
 
 

time: 71.2 us -> 66.2 us (0.930)
  waiting for transfers between devices: 25.9 us -> 20.2 us
  Pallas kernels: 20.8 us -> 22.4 us
  starting transfers between devices: 23.3 us -> 22.3 us
    ppermute x19, waiting for transfers between devices: 25.9 us -> 20.2 us  [swap(): return lax.ppermute(x, axis, [(i, i ^ bit) for i in range(count)])]
    pallas_call x14 -> x16, Pallas kernels: 20.8 us -> 22.4 us  [call(): pl.pallas_call(kernel, name=getattr(kernel, 'func', kernel).__name__, out...]
    ppermute x19, starting transfers between devices: 23.3 us -> 22.3 us  [swap(): return lax.ppermute(x, axis, [(i, i ^ bit) for i in range(count)])]
  transfers between devices with their start and end apart: 19 -> 19, of which waited for: 14 -> 13; matrix products, arithmetic and copies ran while one was open for 0% -> 0% of each run, Pallas kernels for 18% -> 26%
where the time goes in v5:
time: 66.2 us; the launch traced here: 65.9 us
  Pallas kernels  22.4 us (34%)
  starting transfers between devices  22.3 us (34%)
  waiting for transfers between devices  20.2 us (31%)
  between operations  0.81 us (1%)
    pallas_call x16, Pallas kernels, call(): pl.pallas_call(kernel, name=getattr(kernel, 'func', kernel).__name__, out...  22.4 us
    ppermute x19, starting transfers between devices, swap(): return lax.ppermute(x, axis, [(i, i ^ bit) for i in range(count)])  22.3 us
    ppermute x19, waiting for transfers between devices, swap(): return lax.ppermute(x, axis, [(i, i ^ bit) for i in range(count)])  20.2 us
  transfers between devices with their start and end apart: 19, of which 13 were waited for; matrix products, arithmetic and copies ran while one was open for 0% of the time, Pallas kernels for 26%

profile of v5, /device:TPU:0, one launch (start us, length us, event | category | flops | bytes accessed | tf_op | source)
XLA Modules:
  0.0 65.9 jit_solution(4893398389036859355)
XLA Ops:
  0.6 1.2 %turn_kernel.1 = (bf16[256,384]{1,0:T(8,128)(2,1)S(1)}, bf16[256,384]{1,0:T(8,128)(2,1)S(1)}) custom-call(bf16[384,512]{1,0:T(8,128)(2,1)} %bitcast.12), custom_call_target="tpu_custom_call" | custom-call | bytes 1024 | tf_op jit(solution)/shard_map/turn_kernel/pallas_call | solution.py:275
  1.8 3.0 %collective-permute-start.1 = (bf16[256,384]{1,0:T(8,128)(2,1)S(1)}, bf16[256,384]{1,0:T(8,128)(2,1)S(1)}, u32[]{:S(2)}, u32[]{:S(2)}) collective-permute-start(bf16[256,384]{1,0:T(8,128)(2,1)S(1)} %get-tuple-element.34.refs_1_), channel_id=1, source_target_pairs={{0,1},{1,0},{2,3},{3,2},{4,5},{5,4},{6,7},{7,6},{8,9},{9,8},{10,11... | collective-permute-start | bytes 589832 | tf_op jit(solution)/shard_map/ppermute | solution.py:289
  4.8 1.5 %collective-permute-start.2 = (bf16[256,384]{1,0:T(8,128)(2,1)S(1)}, bf16[256,384]{1,0:T(8,128)(2,1)S(1)}, u32[]{:S(2)}, u32[]{:S(2)}) collective-permute-start(bf16[256,384]{1,0:T(8,128)(2,1)S(1)} %get-tuple-element.33.refs_0_), channel_id=1, source_target_pairs={{0,2},{1,3},{2,0},{3,1},{4,6},{5,7},{6,4},{7,5},{8,10},{9,11},{10,... | collective-permute-start | bytes 589832 | tf_op jit(solution)/shard_map/ppermute | solution.py:289
  6.3 0.5 collective-permute-start
  6.9 0.1 collective-permute-start.3
  6.9 0.1 pad_add_fusion.1.place_ref
  7.0 3.2 %pick_kernel.1 = (bf16[768,512]{1,0:T(8,128)(2,1)S(1)}, f32[8,512]{1,0:T(8,128)S(1)}, bf16[1024,512]{1,0:T(8,128)(2,1)S(1)}, s32[1,512]{1,0:T(1,128)S(1)}, f32[1,128]{1,0:T(1,128)S(1)}) custom-call(s32[2]{0:T(128)S(1)} %pad_add_fusion.1.place_ref, s32[1,512]{1,0:T(1,128)} %bitcast.13, f32[1,128]{1,0:T(1,128)} %bitcast.14, bf16[1536,1024]{1,0:T(8,128)(2,1)} %bitcast.9), custom_call_target="tpu_custom_call" | custom-call | bytes 1024 | tf_op jit(solution)/shard_map/pick_kernel/pallas_call | solution.py:275
  10.2 0.4 collective-permute-done.1.refs_3_
  10.5 2.1 %collective-permute-done.2.refs_4_ = bf16[256,384]{1,0:T(8,128)(2,1)S(1)} collective-permute-done((bf16[256,384]{1,0:T(8,128)(2,1)S(1)}, bf16[256,384]{1,0:T(8,128)(2,1)S(1)}, u32[]{:S(2)}, u32[]{:S(2)}) %collective-permute-start.2) | collective-permute-done | bytes 196640 | tf_op jit(solution)/shard_map/ppermute | solution.py:289
  12.6 0.0 collective-permute-start.4
  12.7 2.0 %collective-permute-start.5 = (bf16[256,384]{1,0:T(8,128)(2,1)S(1)}, bf16[256,384]{1,0:T(8,128)(2,1)}, u32[]{:S(2)}, u32[]{:S(2)}) collective-permute-start(bf16[256,384]{1,0:T(8,128)(2,1)S(1)} %collective-permute-done.1.refs_3_), channel_id=1, source_target_pairs={{0,2},{1,3},{2,0},{3,1},{4,6},{5,7},{6,4},{7,5},{8,10},{9,11},{10,... | collective-permute-start | bytes 589832 | tf_op jit(solution)/shard_map/ppermute | solution.py:289
  14.7 2.3 %rest_kernel.1.more_ref = bf16[768,512]{1,0:T(8,128)(2,1)S(1)} custom-call(bf16[1024,512]{1,0:T(8,128)(2,1)S(1)} %get-tuple-element.31.one_ref, bf16[1536,1024]{1,0:T(8,128)(2,1)} %bitcast.10), custom_call_target="tpu_custom_call" | custom-call | bytes 1024 | tf_op jit(solution)/shard_map/rest_kernel/pallas_call | solution.py:275
  17.0 0.1 pad_add_fusion.place_ref
  17.1 0.0 collective-permute-done.refs_2_
  17.1 0.0 collective-permute-done.3.refs_5_
  17.1 1.3 %collective-permute-done.4.refs_6_ = bf16[256,384]{1,0:T(8,128)(2,1)} collective-permute-done((bf16[256,384]{1,0:T(8,128)(2,1)S(1)}, bf16[256,384]{1,0:T(8,128)(2,1)}, u32[]{:S(2)}, u32[]{:S(2)}) %collective-permute-start.4) | collective-permute-done | bytes 196640 | tf_op jit(solution)/shard_map/ppermute | solution.py:289
  18.4 1.3 %collective-permute-done.5.refs_7_ = bf16[256,384]{1,0:T(8,128)(2,1)} collective-permute-done((bf16[256,384]{1,0:T(8,128)(2,1)S(1)}, bf16[256,384]{1,0:T(8,128)(2,1)}, u32[]{:S(2)}, u32[]{:S(2)}) %collective-permute-start.5) | collective-permute-done | bytes 196640 | tf_op jit(solution)/shard_map/ppermute | solution.py:289
  19.7 1.9 %send_kernel.1 = (bf16[512,1536]{1,0:T(8,128)(2,1)S(1)}, f32[264,512]{1,0:T(8,128)S(1)}) custom-call(s32[4]{0:T(128)S(1)} %pad_add_fusion.place_ref, bf16[768,512]{1,0:T(8,128)(2,1)S(1)} %get-tuple-element.30.chosen_ref, bf16[768,512]{1,0:T(8,128)(2,1)S(1)} %rest_kernel.1.more_ref, f32[8,512]{1,0:T(8,128)S(1)} %get-tuple-element.32.entry_ref, ...), custom_call_target="tpu_custom_call" | custom-call | bytes 1024 | tf_op jit(solution)/shard_map/send_kernel/pallas_call | solution.py:275
  21.7 0.0 copy-start
  21.7 0.1 collective-permute-start.6
  21.7 1.1 %keep_kernel.1.keep_ref = f32[256,512]{1,0:T(8,128)S(1)} custom-call(s32[4]{0:T(128)S(1)} %pad_add_fusion.place_ref, bf16[768,512]{1,0:T(8,128)(2,1)S(1)} %get-tuple-element.30.chosen_ref, bf16[768,512]{1,0:T(8,128)(2,1)S(1)} %rest_kernel.1.more_ref, bf16[512,1536]{1,0:T(8,128)(2,1)S(1)} %get-tuple-element.42.turned_ref), custom_call_target="tpu_custom_call" | custom-call | bytes 1024 | tf_op jit(solution)/shard_map/keep_kernel/pallas_call | solution.py:275
  22.9 0.8 %collective-permute-done.6.got_ref = f32[264,512]{1,0:T(8,128)S(1)} collective-permute-done((f32[264,512]{1,0:T(8,128)S(1)}, f32[264,512]{1,0:T(8,128)S(1)}, u32[]{:S(2)}, u32[]{:S(2)}) %collective-permute-start.6) | collective-permute-done | bytes 540704 | tf_op jit(solution)/shard_map/ppermute | solution.py:289
  23.7 0.2 pair_kernel.1
  23.9 1.8 %collective-permute-start.7 = (s16[80,512]{1,0:T(8,128)(2,1)S(1)}, s16[80,512]{1,0:T(8,128)(2,1)S(1)}, u32[]{:S(2)}, u32[]{:S(2)}) collective-permute-start(s16[80,512]{1,0:T(8,128)(2,1)S(1)} %get-tuple-element.45), channel_id=1, source_target_pairs={{0,3},{1,2},{2,1},{3,0},{4,7},{5,6},{6,5},{7,4},{8,11},{9,10},{10,... | collective-permute-start | bytes 245768 | tf_op jit(solution)/shard_map/ppermute | solution.py:289
  25.6 0.5 collective-permute-start.8
  26.1 1.3 %collective-permute-start.9 = (s16[80,512]{1,0:T(8,128)(2,1)S(1)}, s16[80,512]{1,0:T(8,128)(2,1)S(1)}, u32[]{:S(2)}, u32[]{:S(2)}) collective-permute-start(s16[80,512]{1,0:T(8,128)(2,1)S(1)} %get-tuple-element.47), channel_id=1, source_target_pairs={{0,1},{1,0},{2,3},{3,2},{4,5},{5,4},{6,7},{7,6},{8,9},{9,8},{10,11... | collective-permute-start | bytes 245768 | tf_op jit(solution)/shard_map/ppermute | solution.py:289
  27.4 0.0 copy-done
  27.4 2.4 %schur_kernel.1 = (f32[2048,128]{1,0:T(8,128)S(1)}, f32[2048,128]{1,0:T(8,128)S(1)}) custom-call(s32[4]{0:T(128)S(1)} %pad_add_fusion.place_ref, s32[1,512]{1,0:T(1,128)S(1)} %get-tuple-element.40.panel_ref, f32[1,128]{1,0:T(1,128)S(1)} %get-tuple-element.41.own_diagonal_ref, bf16[1536,1024]{1,0:T(8,128)(2,1)S(1)} %bitcast.11, ...), custom_call_target="tpu_custom_call" | custom-call | bytes 1024 | tf_op jit(solution)/shard_map/schur_kernel/pallas_call | solution.py:275
  29.8 0.0 collective-permute-done.7.refs_1_
  29.8 1.3 %collective-permute-done.8.refs_2_ = s16[80,512]{1,0:T(8,128)(2,1)S(1)} collective-permute-done((s16[80,512]{1,0:T(8,128)(2,1)S(1)}, s16[80,512]{1,0:T(8,128)(2,1)S(1)}, u32[]{:S(2)}, u32[]{:S(2)}) %collective-permute-start.8) | collective-permute-done | bytes 81952 | tf_op jit(solution)/shard_map/ppermute | solution.py:289
  31.1 0.1 collective-permute-done.9.refs_3_
  31.2 0.1 sum_kernel.3.refs_0_
  31.3 0.1 collective-permute-start.11
  31.4 1.6 %collective-permute-start.10 = (s16[80,512]{1,0:T(8,128)(2,1)S(1)}, s16[80,512]{1,0:T(8,128)(2,1)S(1)}, u32[]{:S(2)}, u32[]{:S(2)}) collective-permute-start(s16[80,512]{1,0:T(8,128)(2,1)S(1)} %sum_kernel.3.refs_0_), channel_id=1, source_target_pairs={{0,8},{4,12},{8,0},{12,4},{16,24},{20,28},{24,16},{28,20},{1,9},{5... | collective-permute-start | bytes 245768 | tf_op jit(solution)/shard_map/ppermute | solution.py:289
  33.0 3.2 %collective-permute-done.10.refs_1_ = s16[80,512]{1,0:T(8,128)(2,1)S(1)} collective-permute-done((s16[80,512]{1,0:T(8,128)(2,1)S(1)}, s16[80,512]{1,0:T(8,128)(2,1)S(1)}, u32[]{:S(2)}, u32[]{:S(2)}) %collective-permute-start.10) | collective-permute-done | bytes 81952 | tf_op jit(solution)/shard_map/ppermute | solution.py:289
  36.2 0.1 sum_kernel.4.refs_0_
  36.3 2.7 %collective-permute-start.12 = (s16[80,512]{1,0:T(8,128)(2,1)S(1)}, s16[80,512]{1,0:T(8,128)(2,1)S(1)}, u32[]{:S(2)}, u32[]{:S(2)}) collective-permute-start(s16[80,512]{1,0:T(8,128)(2,1)S(1)} %sum_kernel.4.refs_0_), channel_id=1, source_target_pairs={{0,16},{4,20},{8,24},{12,28},{16,0},{20,4},{24,8},{28,12},{1,17},{... | collective-permute-start | bytes 245768 | tf_op jit(solution)/shard_map/ppermute | solution.py:289
  39.0 0.0 collective-permute-done.11.got_ref
  39.0 0.2 bulk_pair_kernel.1
  39.2 4.0 %collective-permute-done.12.refs_1_ = s16[80,512]{1,0:T(8,128)(2,1)S(1)} collective-permute-done((s16[80,512]{1,0:T(8,128)(2,1)S(1)}, s16[80,512]{1,0:T(8,128)(2,1)S(1)}, u32[]{:S(2)}, u32[]{:S(2)}) %collective-permute-start.12) | collective-permute-done | bytes 81952 | tf_op jit(solution)/shard_map/ppermute | solution.py:289
  43.2 0.1 sum_kernel.5.refs_0_
  43.3 1.7 %collective-permute-start.15 = (s16[80,512]{1,0:T(8,128)(2,1)S(1)}, s16[80,512]{1,0:T(8,128)(2,1)S(1)}, u32[]{:S(2)}, u32[]{:S(2)}) collective-permute-start(s16[80,512]{1,0:T(8,128)(2,1)S(1)} %sum_kernel.5.refs_0_), channel_id=1, source_target_pairs={{0,3},{1,2},{2,1},{3,0},{4,7},{5,6},{6,5},{7,4},{8,11},{9,10},{10,... | collective-permute-start | bytes 245768 | tf_op jit(solution)/shard_map/ppermute | solution.py:289
  45.0 0.5 collective-permute-start.14
  45.5 1.3 %collective-permute-start.13 = (s16[80,512]{1,0:T(8,128)(2,1)S(1)}, s16[80,512]{1,0:T(8,128)(2,1)S(1)}, u32[]{:S(2)}, u32[]{:S(2)}) collective-permute-start(s16[80,512]{1,0:T(8,128)(2,1)S(1)} %sum_kernel.5.refs_0_), channel_id=1, source_target_pairs={{0,1},{1,0},{2,3},{3,2},{4,5},{5,4},{6,7},{7,6},{8,9},{9,8},{10,11... | collective-permute-start | bytes 245768 | tf_op jit(solution)/shard_map/ppermute | solution.py:289
  46.9 0.5 collective-permute-start.17
  47.4 1.3 %collective-permute-done.15.refs_3_ = s16[80,512]{1,0:T(8,128)(2,1)S(1)} collective-permute-done((s16[80,512]{1,0:T(8,128)(2,1)S(1)}, s16[80,512]{1,0:T(8,128)(2,1)S(1)}, u32[]{:S(2)}, u32[]{:S(2)}) %collective-permute-start.15) | collective-permute-done | bytes 81952 | tf_op jit(solution)/shard_map/ppermute | solution.py:289
  48.7 0.9 %collective-permute-done.14.refs_2_ = s16[80,512]{1,0:T(8,128)(2,1)S(1)} collective-permute-done((s16[80,512]{1,0:T(8,128)(2,1)S(1)}, s16[80,512]{1,0:T(8,128)(2,1)S(1)}, u32[]{:S(2)}, u32[]{:S(2)}) %collective-permute-start.14) | collective-permute-done | bytes 81952 | tf_op jit(solution)/shard_map/ppermute | solution.py:289
  49.6 0.4 collective-permute-done.13.refs_1_
  50.0 0.1 collective-permute-start.16
  50.1 3.2 %collective-permute-done.17.got_ref = s16[1056,128]{1,0:T(8,128)(2,1)S(1)} collective-permute-done((s16[1056,128]{1,0:T(8,128)(2,1)S(1)}, s16[1056,128]{1,0:T(8,128)(2,1)S(1)}, u32[]{:S(2)}, u32[]{:S(2)}) %collective-permute-start.17) | collective-permute-done | bytes 270368 | tf_op jit(solution)/shard_map/ppermute | solution.py:289
  53.3 0.2 bulk_sum_kernel.1
  53.5 3.0 %collective-permute-start.18 = (s16[528,128]{1,0:T(8,128)(2,1)S(1)}, s16[528,128]{1,0:T(8,128)(2,1)S(1)}, u32[]{:S(2)}, u32[]{:S(2)}) collective-permute-start(s16[528,128]{1,0:T(8,128)(2,1)S(1)} %get-tuple-element.57), channel_id=1, source_target_pairs={{0,16},{4,20},{8,24},{12,28},{16,0},{20,4},{24,8},{28,12},{1,17},{... | collective-permute-start | bytes 405512 | tf_op jit(solution)/shard_map/ppermute | solution.py:289
  56.5 0.0 collective-permute-done.16.other_ref
  56.5 4.1 %first_kernel.1 = (f32[256,256]{1,0:T(8,128)S(1)}, f32[512,512]{1,0:T(8,128)S(1)}) custom-call(s32[4]{0:T(128)S(1)} %pad_add_fusion.place_ref, s16[320,512]{1,0:T(8,128)(2,1)S(1)} %join_kernel.1.own_ref, s16[320,512]{1,0:T(8,128)(2,1)S(1)} %collective-permute-done.16.other_ref), custom_call_target="tpu_custom_call" | custom-call | bytes 16606024 | tf_op jit(solution)/shard_map/first_kernel/pallas_call | solution.py:275
  60.5 3.8 %second_kernel.1.inverse_second_ref = f32[256,256]{1,0:T(8,128)S(1)} custom-call(f32[512,512]{1,0:T(8,128)S(1)} %get-tuple-element.54.pivots_ref, f32[256,256]{1,0:T(8,128)S(1)} %get-tuple-element.53.inverse_first_ref), custom_call_target="tpu_custom_call" | custom-call | bytes 16606024 | tf_op jit(solution)/shard_map/second_kernel/pallas_call | solution.py:275
  64.4 0.0 collective-permute-done.18.refs_0_
  64.4 1.5 %factor_kernel.1 = (f32[128,1,256]{2,1,0:T(1,128)}, f32[128,1,256]{2,1,0:T(1,128)}) custom-call(f32[256,256]{1,0:T(8,128)S(1)} %get-tuple-element.53.inverse_first_ref, f32[256,256]{1,0:T(8,128)S(1)} %second_kernel.1.inverse_second_ref, f32[512,512]{1,0:T(8,128)S(1)} %get-tuple-element.54.pivots_ref, f32[512,128]{1,0:T(8,128)S(1)} %get-tuple-element.56.rows_ref, ...), custom_call_target="tpu_custom_call" | custom-call | bytes 1024 | tf_op jit(solution)/shard_map/factor_kernel/pallas_call | solution.py:275
  (1 shorter events, 0.0 us)
Async XLA Ops:
  1.8 8.7 %collective-permute-start.1 = (bf16[256,384]{1,0:T(8,128)(2,1)S(1)}, bf16[256,384]{1,0:T(8,128)(2,1)S(1)}, u32[]{:S(2)}, u32[]{:S(2)}) collective-permute-start(bf16[256,384]{1,0:T(8,128)(2,1)S(1)} %get-tuple-element.34.refs_1_), channel_id=1, source_target_pairs={{0,1},{1,0},{2,3},{3,2},{4,5},{5,4},{6,7},{7,6},{8,9},{9,8},{10,11... | collective-permute-start | bytes 589832 | tf_op jit(solution)/shard_map/ppermute | solution.py:289
  4.8 7.8 %collective-permute-start.2 = (bf16[256,384]{1,0:T(8,128)(2,1)S(1)}, bf16[256,384]{1,0:T(8,128)(2,1)S(1)}, u32[]{:S(2)}, u32[]{:S(2)}) collective-permute-start(bf16[256,384]{1,0:T(8,128)(2,1)S(1)} %get-tuple-element.33.refs_0_), channel_id=1, source_target_pairs={{0,2},{1,3},{2,0},{3,1},{4,6},{5,7},{6,4},{7,5},{8,10},{9,11},{10,... | collective-permute-start | bytes 589832 | tf_op jit(solution)/shard_map/ppermute | solution.py:289
  6.3 10.8 %collective-permute-start = (bf16[256,384]{1,0:T(8,128)(2,1)S(1)}, bf16[256,384]{1,0:T(8,128)(2,1)}, u32[]{:S(2)}, u32[]{:S(2)}) collective-permute-start(bf16[256,384]{1,0:T(8,128)(2,1)S(1)} %get-tuple-element.33.refs_0_), channel_id=1, source_target_pairs={{0,1},{1,0},{2,3},{3,2},{4,5},{5,4},{6,7},{7,6},{8,9},{9,8},{10,11... | collective-permute-start | bytes 589832 | tf_op jit(solution)/shard_map/ppermute | solution.py:289
  6.9 10.2 %collective-permute-start.3 = (bf16[256,384]{1,0:T(8,128)(2,1)S(1)}, bf16[256,384]{1,0:T(8,128)(2,1)}, u32[]{:S(2)}, u32[]{:S(2)}) collective-permute-start(bf16[256,384]{1,0:T(8,128)(2,1)S(1)} %get-tuple-element.34.refs_1_), channel_id=1, source_target_pairs={{0,2},{1,3},{2,0},{3,1},{4,6},{5,7},{6,4},{7,5},{8,10},{9,11},{10,... | collective-permute-start | bytes 589832 | tf_op jit(solution)/shard_map/ppermute | solution.py:289
  12.6 5.8 %collective-permute-start.4 = (bf16[256,384]{1,0:T(8,128)(2,1)S(1)}, bf16[256,384]{1,0:T(8,128)(2,1)}, u32[]{:S(2)}, u32[]{:S(2)}) collective-permute-start(bf16[256,384]{1,0:T(8,128)(2,1)S(1)} %collective-permute-done.2.refs_4_), channel_id=1, source_target_pairs={{0,1},{1,0},{2,3},{3,2},{4,5},{5,4},{6,7},{7,6},{8,9},{9,8},{10,11... | collective-permute-start | bytes 589832 | tf_op jit(solution)/shard_map/ppermute | solution.py:289
  12.7 7.0 %collective-permute-start.5 = (bf16[256,384]{1,0:T(8,128)(2,1)S(1)}, bf16[256,384]{1,0:T(8,128)(2,1)}, u32[]{:S(2)}, u32[]{:S(2)}) collective-permute-start(bf16[256,384]{1,0:T(8,128)(2,1)S(1)} %collective-permute-done.1.refs_3_), channel_id=1, source_target_pairs={{0,2},{1,3},{2,0},{3,1},{4,6},{5,7},{6,4},{7,5},{8,10},{9,11},{10,... | collective-permute-start | bytes 589832 | tf_op jit(solution)/shard_map/ppermute | solution.py:289
  21.7 5.8 %copy-start = (bf16[1,1536,1024]{2,1,0:T(8,128)(2,1)S(1)}, bf16[1,1536,1024]{2,1,0:T(8,128)(2,1)}, u32[]{:S(2)}) copy-start(bf16[1,1536,1024]{2,1,0:T(8,128)(2,1)} %param.4) | copy-start | bytes 9437188
  21.7 2.0 %collective-permute-start.6 = (f32[264,512]{1,0:T(8,128)S(1)}, f32[264,512]{1,0:T(8,128)S(1)}, u32[]{:S(2)}, u32[]{:S(2)}) collective-permute-start(f32[264,512]{1,0:T(8,128)S(1)} %get-tuple-element.38), channel_id=1, source_target_pairs={{0,4},{4,0},{8,12},{12,8},{16,20},{20,16},{24,28},{28,24},{1,5},{5... | collective-permute-start | bytes 1622024 | tf_op jit(solution)/shard_map/ppermute | solution.py:289
  23.9 5.9 %collective-permute-start.7 = (s16[80,512]{1,0:T(8,128)(2,1)S(1)}, s16[80,512]{1,0:T(8,128)(2,1)S(1)}, u32[]{:S(2)}, u32[]{:S(2)}) collective-permute-start(s16[80,512]{1,0:T(8,128)(2,1)S(1)} %get-tuple-element.45), channel_id=1, source_target_pairs={{0,3},{1,2},{2,1},{3,0},{4,7},{5,6},{6,5},{7,4},{8,11},{9,10},{10,... | collective-permute-start | bytes 245768 | tf_op jit(solution)/shard_map/ppermute | solution.py:289
  25.6 5.4 %collective-permute-start.8 = (s16[80,512]{1,0:T(8,128)(2,1)S(1)}, s16[80,512]{1,0:T(8,128)(2,1)S(1)}, u32[]{:S(2)}, u32[]{:S(2)}) collective-permute-start(s16[80,512]{1,0:T(8,128)(2,1)S(1)} %get-tuple-element.46), channel_id=1, source_target_pairs={{0,2},{1,3},{2,0},{3,1},{4,6},{5,7},{6,4},{7,5},{8,10},{9,11},{10,... | collective-permute-start | bytes 245768 | tf_op jit(solution)/shard_map/ppermute | solution.py:289
  26.1 5.0 %collective-permute-start.9 = (s16[80,512]{1,0:T(8,128)(2,1)S(1)}, s16[80,512]{1,0:T(8,128)(2,1)S(1)}, u32[]{:S(2)}, u32[]{:S(2)}) collective-permute-start(s16[80,512]{1,0:T(8,128)(2,1)S(1)} %get-tuple-element.47), channel_id=1, source_target_pairs={{0,1},{1,0},{2,3},{3,2},{4,5},{5,4},{6,7},{7,6},{8,9},{9,8},{10,11... | collective-permute-start | bytes 245768 | tf_op jit(solution)/shard_map/ppermute | solution.py:289
  31.3 7.7 %collective-permute-start.11 = (f32[2048,128]{1,0:T(8,128)S(1)}, f32[2048,128]{1,0:T(8,128)S(1)}, u32[]{:S(2)}, u32[]{:S(2)}) collective-permute-start(f32[2048,128]{1,0:T(8,128)S(1)} %get-tuple-element.50), channel_id=1, source_target_pairs={{0,4},{4,0},{8,12},{12,8},{16,20},{20,16},{24,28},{28,24},{1,5},{5... | collective-permute-start | bytes 3145736 | tf_op jit(solution)/shard_map/ppermute | solution.py:289
  31.4 4.9 %collective-permute-start.10 = (s16[80,512]{1,0:T(8,128)(2,1)S(1)}, s16[80,512]{1,0:T(8,128)(2,1)S(1)}, u32[]{:S(2)}, u32[]{:S(2)}) collective-permute-start(s16[80,512]{1,0:T(8,128)(2,1)S(1)} %sum_kernel.3.refs_0_), channel_id=1, source_target_pairs={{0,8},{4,12},{8,0},{12,4},{16,24},{20,28},{24,16},{28,20},{1,9},{5... | collective-permute-start | bytes 245768 | tf_op jit(solution)/shard_map/ppermute | solution.py:289
  36.3 6.9 %collective-permute-start.12 = (s16[80,512]{1,0:T(8,128)(2,1)S(1)}, s16[80,512]{1,0:T(8,128)(2,1)S(1)}, u32[]{:S(2)}, u32[]{:S(2)}) collective-permute-start(s16[80,512]{1,0:T(8,128)(2,1)S(1)} %sum_kernel.4.refs_0_), channel_id=1, source_target_pairs={{0,16},{4,20},{8,24},{12,28},{16,0},{20,4},{24,8},{28,12},{1,17},{... | collective-permute-start | bytes 245768 | tf_op jit(solution)/shard_map/ppermute | solution.py:289
  43.3 5.4 %collective-permute-start.15 = (s16[80,512]{1,0:T(8,128)(2,1)S(1)}, s16[80,512]{1,0:T(8,128)(2,1)S(1)}, u32[]{:S(2)}, u32[]{:S(2)}) collective-permute-start(s16[80,512]{1,0:T(8,128)(2,1)S(1)} %sum_kernel.5.refs_0_), channel_id=1, source_target_pairs={{0,3},{1,2},{2,1},{3,0},{4,7},{5,6},{6,5},{7,4},{8,11},{9,10},{10,... | collective-permute-start | bytes 245768 | tf_op jit(solution)/shard_map/ppermute | solution.py:289
  45.0 4.6 %collective-permute-start.14 = (s16[80,512]{1,0:T(8,128)(2,1)S(1)}, s16[80,512]{1,0:T(8,128)(2,1)S(1)}, u32[]{:S(2)}, u32[]{:S(2)}) collective-permute-start(s16[80,512]{1,0:T(8,128)(2,1)S(1)} %sum_kernel.5.refs_0_), channel_id=1, source_target_pairs={{0,2},{1,3},{2,0},{3,1},{4,6},{5,7},{6,4},{7,5},{8,10},{9,11},{10,... | collective-permute-start | bytes 245768 | tf_op jit(solution)/shard_map/ppermute | solution.py:289
  45.5 4.4 %collective-permute-start.13 = (s16[80,512]{1,0:T(8,128)(2,1)S(1)}, s16[80,512]{1,0:T(8,128)(2,1)S(1)}, u32[]{:S(2)}, u32[]{:S(2)}) collective-permute-start(s16[80,512]{1,0:T(8,128)(2,1)S(1)} %sum_kernel.5.refs_0_), channel_id=1, source_target_pairs={{0,1},{1,0},{2,3},{3,2},{4,5},{5,4},{6,7},{7,6},{8,9},{9,8},{10,11... | collective-permute-start | bytes 245768 | tf_op jit(solution)/shard_map/ppermute | solution.py:289
  46.9 6.5 %collective-permute-start.17 = (s16[1056,128]{1,0:T(8,128)(2,1)S(1)}, s16[1056,128]{1,0:T(8,128)(2,1)S(1)}, u32[]{:S(2)}, u32[]{:S(2)}) collective-permute-start(s16[1056,128]{1,0:T(8,128)(2,1)S(1)} %get-tuple-element.51), channel_id=1, source_target_pairs={{0,8},{4,12},{8,0},{12,4},{16,24},{20,28},{24,16},{28,20},{1,9},{5... | collective-permute-start | bytes 811016 | tf_op jit(solution)/shard_map/ppermute | solution.py:289
  50.0 6.5 %collective-permute-start.16 = (s16[320,512]{1,0:T(8,128)(2,1)S(1)}, s16[320,512]{1,0:T(8,128)(2,1)S(1)}, u32[]{:S(2)}, u32[]{:S(2)}) collective-permute-start(s16[320,512]{1,0:T(8,128)(2,1)S(1)} %join_kernel.1.own_ref), channel_id=1, source_target_pairs={{0,4},{4,0},{8,12},{12,8},{16,20},{20,16},{24,28},{28,24},{1,5},{5... | collective-permute-start | bytes 983048 | tf_op jit(solution)/shard_map/ppermute | solution.py:289
  53.5 10.9 %collective-permute-start.18 = (s16[528,128]{1,0:T(8,128)(2,1)S(1)}, s16[528,128]{1,0:T(8,128)(2,1)S(1)}, u32[]{:S(2)}, u32[]{:S(2)}) collective-permute-start(s16[528,128]{1,0:T(8,128)(2,1)S(1)} %get-tuple-element.57), channel_id=1, source_target_pairs={{0,16},{4,20},{8,24},{12,28},{16,0},{20,4},{24,8},{28,12},{1,17},{... | collective-permute-start | bytes 405512 | tf_op jit(solution)/shard_map/ppermute | solution.py:289

commit v6 on v5

--- a/solution.py
+++ b/solution.py
@@ -10,6 +10,7 @@
 HALF = 256
 NEWTON = 8
 TAIL = 16
+SHORT = 8
 CHUNKS = 4
 LEVELS = 32000.0
 F32 = jnp.float32
@@ -64,7 +65,7 @@
     return pl.multiple_of(index * size, size)
 
 
-def encode(values, out_ref, base, diagonal=None):
+def encode(values, out_ref, base, tail_rows, diagonal=None):
     rows, lanes = values.shape
     top = jnp.maximum(jnp.max(jnp.abs(values), axis=0, keepdims=True), F32(1e-30))
     power = jnp.ceil(jnp.log2(top))
@@ -73,17 +74,17 @@
     scale = mantissa * unit * F32(1.0 / (16384.0 * LEVELS))
     codes = jnp.round(values * (F32(1.0) / scale)).astype(jnp.int32)
     out_ref[base:base + rows, :] = codes.astype(I16)
-    row = lax.broadcasted_iota(jnp.int32, (TAIL, lanes), 0)
+    row = lax.broadcasted_iota(jnp.int32, (tail_rows, lanes), 0)
     tail = jnp.where(row == 0, power, jnp.where(row == 1, mantissa, F32(0.0)))
     if diagonal is not None:
         coarse = jnp.floor(diagonal * F32(64.0))
         fine = (diagonal * F32(64.0) - coarse) * F32(4096.0)
         tail = jnp.where(row == 2, coarse, jnp.where(row == 3, fine, tail))
-    out_ref[base + rows:base + rows + TAIL, :] = tail.astype(jnp.int32).astype(I16)
-
-
-def decode(ref, base, rows):
-    tail = ref[base + rows:base + rows + TAIL, :].astype(jnp.int32).astype(F32)
+    out_ref[base + rows:base + rows + tail_rows, :] = tail.astype(jnp.int32).astype(I16)
+
+
+def decode(ref, base, rows, tail_rows):
+    tail = ref[base + rows:base + rows + tail_rows, :].astype(jnp.int32).astype(F32)
     scale = tail[1:2] * jnp.exp2(tail[0:1]) * F32(1.0 / (16384.0 * LEVELS))
     diagonal = tail[2:3] * F32(1.0 / 64.0) + tail[3:4] * F32(1.0 / (64.0 * 4096.0))
     return ref[base:base + rows, :].astype(jnp.int32).astype(F32) * scale, diagonal
@@ -110,11 +111,11 @@
     return copies
 
 
-def choose(copies, coupling_copy, one_ref, chosen_ref):
+def choose(copies, coupling_copy, one_ref, chosen_ref, first):
     rows = coupling_copy.shape[1]
     for i, copy in enumerate(copies):
         copy.wait()
-        chosen_ref[i * rows:(i + 1) * rows, :] = dot(coupling_copy[i], one_ref[...]).astype(BF16)
+        chosen_ref[(first + i) * rows:(first + i + 1) * rows, :] = dot(coupling_copy[i], one_ref[...]).astype(BF16)
 
 
 def pick_kernel(
@@ -139,26 +140,17 @@
     own = jnp.broadcast_to(diagonal_out[...], (8, share)).T[:, :1]
     entry = jnp.sum(jnp.where(owned, own, F32(0.0)), axis=0, keepdims=True)
     entry_ref[...] = jnp.broadcast_to(entry, entry_ref.shape)
-    choose(copies, coupling_copy, one_ref, chosen_ref)
-
-
-def rest_kernel(one_ref, coupling_ref, chosen_ref, coupling_copy, done):
-    copies = fetch(coupling_ref, coupling_copy, done, coupling_copy.shape[0])
-    choose(copies, coupling_copy, one_ref, chosen_ref)
-
-
-def pivot_terms(place_ref, turned_ref, chosen_ref, more_ref, out_ref, all_ref, rows, whose):
-    half = all_ref.shape[0]
-    size = half // rows
-    middle = chosen_ref.shape[0]
-    block = turned_ref[pl.ds(aligned(whose, half), half), :]
-    all_ref[...] = dot(block[:, :middle], chosen_ref[...]) + dot(block[:, middle:], more_ref[...])
-    for k in range(rows):
-        out_ref[k * size:(k + 1) * size, :] = all_ref[pl.ds(aligned(place_ref[0] ^ k, size), size), :]
-
-
-def send_kernel(rows, place_ref, chosen_ref, more_ref, entry_ref, *refs):
-    *pieces, turned_ref, send_ref, all_ref = refs
+    choose(copies, coupling_copy, one_ref, chosen_ref, 0)
+
+
+def rest_kernel(chosen_in, one_ref, coupling_ref, chosen_ref, coupling_copy, done):
+    first = coupling_copy.shape[0]
+    copies = fetch(coupling_ref, coupling_copy, done, first)
+    choose(copies, coupling_copy, one_ref, chosen_ref, first)
+
+
+def early_kernel(place_ref, chosen_ref, *refs):
+    *pieces, turned_ref, terms_ref = refs
     if len(pieces) == 1:
         turned_ref[...] = pieces[0][...]
     else:
@@ -166,12 +158,37 @@
         for i, piece in enumerate(pieces):
             start = aligned(place_ref[0] ^ (i // 2), width)
             turned_ref[i % 2 * half:(i % 2 + 1) * half, pl.ds(start, width)] = piece[...]
-    pivot_terms(place_ref, turned_ref, chosen_ref, more_ref, send_ref, all_ref, rows, 1 - place_ref[1])
+        start = aligned(place_ref[0] ^ (len(pieces) // 2), width)
+        turned_ref[:, pl.ds(start, width)] = jnp.zeros((2 * half, width), BF16)
+    terms_ref[...] = dot(turned_ref[...], chosen_ref[...])
+
+
+def half_terms(rows, place_ref, chosen_ref, terms_ref, far, whose, out_ref, all_ref):
+    half = all_ref.shape[0]
+    size = half // rows
+    total = terms_ref[pl.ds(aligned(whose, half), half), :]
+    if far:
+        width = far[0].shape[1]
+        block = jnp.where(whose == 0, far[0][...], far[1][...])
+        total = total + dot(block, chosen_ref[pl.ds(aligned(place_ref[0] ^ (rows - 1), width), width), :])
+    all_ref[...] = total
+    for k in range(rows):
+        out_ref[k * size:(k + 1) * size, :] = all_ref[pl.ds(aligned(place_ref[0] ^ k, size), size), :]
+
+
+def send_kernel(rows, place_ref, chosen_ref, entry_ref, terms_ref, *refs):
+    *far, send_ref, all_ref = refs
+    half_terms(rows, place_ref, chosen_ref, terms_ref, far, 1 - place_ref[1], send_ref, all_ref)
     send_ref[all_ref.shape[0]:, :] = entry_ref[...]
 
 
-def keep_kernel(rows, place_ref, chosen_ref, more_ref, turned_ref, keep_ref, all_ref):
-    pivot_terms(place_ref, turned_ref, chosen_ref, more_ref, keep_ref, all_ref, rows, place_ref[1])
+def keep_kernel(rows, place_ref, turned_in, chosen_ref, terms_ref, *refs):
+    *far, turned_ref, keep_ref, all_ref = refs
+    half_terms(rows, place_ref, chosen_ref, terms_ref, far, place_ref[1], keep_ref, all_ref)
+    for i, piece in enumerate(far):
+        half, width = piece.shape
+        start = aligned(place_ref[0] ^ (rows - 1), width)
+        turned_ref[i * half:(i + 1) * half, pl.ds(start, width)] = piece[...]
 
 
 def pair_kernel(rows, keep_ref, got_ref, entry_ref, *out_refs):
@@ -179,35 +196,46 @@
     entry = entry_ref[:1, :] + got_ref[rows * size:rows * size + 1, :]
     for k, out_ref in enumerate(out_refs):
         part = slice(k * size, (k + 1) * size)
-        encode(keep_ref[part, :] + got_ref[part, :], out_ref, 0, entry)
+        encode(keep_ref[part, :] + got_ref[part, :], out_ref, 0, SHORT, entry)
 
 
 def sum_kernel(*refs):
     *in_refs, out_ref = refs
-    size = out_ref.shape[0] - TAIL
-    parts = [decode(ref, 0, size) for ref in in_refs]
-    encode(sum(p[0] for p in parts), out_ref, 0, sum(p[1] for p in parts))
+    size = out_ref.shape[0] - SHORT
+    parts = [decode(ref, 0, size, SHORT) for ref in in_refs]
+    encode(sum(p[0] for p in parts), out_ref, 0, SHORT, sum(p[1] for p in parts))
 
 
 def join_kernel(*refs):
     *in_refs, out_ref = refs
-    size = in_refs[0].shape[0]
+    size = in_refs[0].shape[0] - SHORT
     for k, ref in enumerate(in_refs):
-        out_ref[k * size:(k + 1) * size, :] = ref[...]
-
-
-def first_kernel(rows, place_ref, own_ref, other_ref, inverse_ref, pivots_ref):
-    row, core = place_ref[0], place_ref[1]
-    panel = pivots_ref.shape[0]
+        start = k * (size + TAIL)
+        out_ref[start:start + size, :] = ref[:size, :]
+        tail = ref[size:, :].astype(jnp.int32)
+        out_ref[start + size:start + size + TAIL, :] = jnp.concatenate([tail, jnp.zeros_like(tail)], axis=0).astype(I16)
+
+
+def place_pieces(row, whose, ref, pivots_ref, rows, base):
+    panel = pivots_ref.shape[1]
     size = panel // (2 * rows)
     index = lax.broadcasted_iota(jnp.int32, (size, panel), 1)
-    for ref, whose in ((own_ref, core), (other_ref, 1 - core)):
-        for k in range(rows):
-            start = aligned(whose * rows + (row ^ k), size)
-            values, diagonal = decode(ref, k * (size + TAIL), size)
-            at = lax.broadcasted_iota(jnp.int32, (size, panel), 0) + start == index
-            pivots_ref[pl.ds(start, size), :] = values + jnp.where(at, diagonal, F32(0.0))
+    for k in range(rows):
+        start = aligned(whose * rows + (row ^ k), size)
+        values, diagonal = decode(ref, k * (size + TAIL), size, TAIL)
+        at = lax.broadcasted_iota(jnp.int32, (size, panel), 0) + start == index
+        pivots_ref[pl.ds(start - base, size), :] = values + jnp.where(at, diagonal, F32(0.0))
+
+
+def own_kernel(rows, place_ref, own_ref, half_ref):
+    place_pieces(place_ref[0], place_ref[1], own_ref, half_ref, rows, place_ref[1] * half_ref.shape[0])
+
+
+def first_kernel(rows, place_ref, half_ref, other_ref, inverse_ref, pivots_ref):
+    row, core = place_ref[0], place_ref[1]
     half = inverse_ref.shape[0]
+    pivots_ref[pl.ds(aligned(core, half), half), :] = half_ref[...]
+    place_pieces(row, 1 - core, other_ref, pivots_ref, rows, 0)
     inverse_ref[...] = newton(pivots_ref[:half, :half])
 
 
@@ -240,17 +268,17 @@
     own_ref[...] = keep_ref[:half, :] + got_ref[:half, :]
     for i in range(half // panel):
         part = slice(half + i * panel, half + (i + 1) * panel)
-        encode(keep_ref[part, :] + got_ref[part, :], coded_ref, i * (panel + TAIL))
+        encode(keep_ref[part, :] + got_ref[part, :], coded_ref, i * (panel + TAIL), TAIL)
 
 
 def bulk_sum_kernel(panel, keep_ref, got_ref, own_ref, coded_ref):
     half = own_ref.shape[0]
     for i in range(keep_ref.shape[0] // panel):
-        value = keep_ref[i * panel:(i + 1) * panel, :] + decode(got_ref, i * (panel + TAIL), panel)[0]
+        value = keep_ref[i * panel:(i + 1) * panel, :] + decode(got_ref, i * (panel + TAIL), panel, TAIL)[0]
         if i * panel < half:
             own_ref[i * panel:(i + 1) * panel, :] = value
         else:
-            encode(value, coded_ref, (i - half // panel) * (panel + TAIL))
+            encode(value, coded_ref, (i - half // panel) * (panel + TAIL), TAIL)
 
 
 def factor_kernel(inverse_first_ref, inverse_second_ref, pivots_ref, rows_ref, *refs):
@@ -259,14 +287,14 @@
     half = panel // 2
     rows = rows_ref[...]
     for ref in got:
-        rows = rows + decode(ref, 0, panel)[0]
+        rows = rows + decode(ref, 0, panel, TAIL)[0]
     first_factor = product(inverse_first_ref[...], rows[:half])
     updated = rows[half:] - product(pivots_ref[half:, :half], first_factor)
     first_out[...] = first_factor.T[:, None, :]
     second_out[...] = product(inverse_second_ref[...], updated).T[:, None, :]
 
 
-def call(kernel, out_shape, *args, scratch=(), scalars=0, remain=0, micros=0.0):
+def call(kernel, out_shape, *args, scratch=(), scalars=0, remain=0, micros=0.0, aliases=None):
     hbm = pl.BlockSpec(memory_space=pltpu.HBM)
     vmem = pl.BlockSpec(memory_space=pltpu.VMEM)
     smem = pl.BlockSpec(memory_space=pltpu.SMEM)
@@ -279,6 +307,7 @@
         in_specs=[smem] * scalars + [vmem] * (len(args) - scalars - remain) + [hbm] * remain,
         out_specs=jax.tree.map(lambda _: vmem, out_shape),
         scratch_shapes=scratch,
+        input_output_aliases=aliases or {},
         compiler_params=pltpu.CompilerParams(vmem_limit_bytes=28 << 20),
         cost_estimate=pl.CostEstimate(flops=0, bytes_accessed=int(micros * 3.69e6) + 1024, transcendentals=0),
     )(*args)
@@ -333,7 +362,7 @@
     starts = jnp.stack([row * row_count, first_row]).astype(jnp.int32)
     at = jnp.stack([row, place % 2, place // 2, first_row]).astype(jnp.int32)
 
-    picked = shape((local // 2, panel), BF16)
+    picked = shape((local, panel), BF16)
     chunk_room = [
         pltpu.VMEM((CHUNKS // 2, local // CHUNKS, row_count), BF16), pltpu.SemaphoreType.DMA((CHUNKS // 2,))
     ]
@@ -347,18 +376,21 @@
         scratch=[chunk_room[0], pltpu.SemaphoreType.DMA((2,)), chunk_room[1]],
     )
     pieces = gather_pieces(solves, rows, (entry,))
-    more = call(rest_kernel, picked, one, coupling, remain=1, scratch=chunk_room)
+    near, far = pieces[:6], pieces[6:]
+    chosen = call(rest_kernel, picked, chosen, one, coupling, remain=1, scratch=chunk_room, aliases={0: 0})
     room = [pltpu.VMEM((panel // 2, panel), F32)]
-    turned, send = call(
-        functools.partial(send_kernel, rows),
-        (shape((panel, local), BF16), shape((panel // 2 + 8, panel), F32)),
-        at, chosen, more, entry, *pieces, scalars=1, scratch=room,
-    )
-    keep = call(
-        functools.partial(keep_kernel, rows), shape((panel // 2, panel), F32),
-        at, chosen, more, turned, scalars=1, scratch=room,
-    )
-    coded = shape((size + TAIL, panel), I16)
+    turned, terms = call(
+        early_kernel, (shape((panel, local), BF16), shape((panel, panel), F32)), at, chosen, *near, scalars=1
+    )
+    send = call(
+        functools.partial(send_kernel, rows), shape((panel // 2 + 8, panel), F32),
+        at, chosen, entry, terms, *far, scalars=1, scratch=room,
+    )
+    turned, keep = call(
+        functools.partial(keep_kernel, rows), (shape((panel, local), BF16), shape((panel // 2, panel), F32)),
+        at, turned, chosen, terms, *far, scalars=1, scratch=room, aliases={1: 0},
+    )
+    coded = shape((size + SHORT, panel), I16)
     codes = call(
         functools.partial(pair_kernel, rows), (coded,) * rows, keep, swap(send, "scen", 1), entry
     )
@@ -390,14 +422,20 @@
     if split:
         for bit in steps[:-1]:
             count //= 2
-            got = swap(bulk_codes, "scen", 2 * bit)
+            got = swap(after(bulk_codes, part), "scen", 2 * bit)
             own, bulk_codes = call(functools.partial(bulk_sum_kernel, panel), halved(count), own, got)
         got = [swap(bulk_codes, "scen", layers)]
     joined = call(join_kernel, shape((rows * (size + TAIL), panel), I16), part, *shared)
+    if split:
+        joined = after(joined, bulk_codes)
+    other = swap(joined, "scen", 1)
+    own_half = call(
+        functools.partial(own_kernel, rows), shape((panel // 2, panel), F32), at, joined, scalars=1
+    )
     square = shape((half, half), F32)
     inverse_first, pivots = call(
         functools.partial(first_kernel, rows), (square, shape((panel, panel), F32)),
-        at, joined, swap(joined, "scen", 1), scalars=1, micros=4.5,
+        at, own_half, other, scalars=1, micros=4.5,
     )
     inverse_second = call(second_kernel, square, pivots, inverse_first, micros=4.5)
     out = shape((share, 1, half), F32)

time: 66.2 us -> 63.7 us (0.962)
  waiting for transfers between devices: 20.2 us -> 15.1 us
  Pallas kernels: 22.4 us -> 24.7 us
    ppermute x19, waiting for transfers between devices: 20.2 us -> 15.1 us  [swap(): return lax.ppermute(x, axis, [(i, i ^ bit) for i in range(count)])]
    pallas_call x16 -> x18, Pallas kernels: 22.4 us -> 24.7 us  [call(): pl.pallas_call(kernel, name=getattr(kernel, 'func', kernel).__name__, out...]
  transfers between devices with their start and end apart: 19 -> 19, of which waited for: 13 -> 11; matrix products, arithmetic and copies ran while one was open for 0% -> 0% of each run, Pallas kernels for 26% -> 31%
where the time goes in v6:
time: 63.7 us; the launch traced here: 63.5 us
  Pallas kernels  24.7 us (39%)
  starting transfers between devices  22.7 us (36%)
  waiting for transfers between devices  15.1 us (24%)
  between operations  0.83 us (1%)
    pallas_call x18, Pallas kernels, call(): pl.pallas_call(kernel, name=getattr(kernel, 'func', kernel).__name__, out...  24.7 us
    ppermute x19, starting transfers between devices, swap(): return lax.ppermute(x, axis, [(i, i ^ bit) for i in range(count)])  22.7 us
    ppermute x19, waiting for transfers between devices, swap(): return lax.ppermute(x, axis, [(i, i ^ bit) for i in range(count)])  15.1 us
  transfers between devices with their start and end apart: 19, of which 11 were waited for; matrix products, arithmetic and copies ran while one was open for 0% of the time, Pallas kernels for 31%

profile of v6, /device:TPU:0, one launch (start us, length us, event | category | flops | bytes accessed | tf_op | source)
XLA Modules:
  0.0 63.5 jit_solution(17389102364942955930)
XLA Ops:
  0.6 1.8 %turn_kernel.1 = (bf16[256,384]{1,0:T(8,128)(2,1)S(1)}, bf16[256,384]{1,0:T(8,128)(2,1)}) custom-call(bf16[384,512]{1,0:T(8,128)(2,1)} %bitcast.12), custom_call_target="tpu_custom_call" | custom-call | bytes 1024 | tf_op jit(solution)/shard_map/turn_kernel/pallas_call | solution.py:303
  2.5 3.0 %collective-permute-start.1 = (bf16[256,384]{1,0:T(8,128)(2,1)}, bf16[256,384]{1,0:T(8,128)(2,1)S(1)}, u32[]{:S(2)}, u32[]{:S(2)}) collective-permute-start(bf16[256,384]{1,0:T(8,128)(2,1)} %get-tuple-element.37.refs_1_), channel_id=1, source_target_pairs={{0,1},{1,0},{2,3},{3,2},{4,5},{5,4},{6,7},{7,6},{8,9},{9,8},{10,11... | collective-permute-start | bytes 589832 | tf_op jit(solution)/shard_map/ppermute | solution.py:318
  5.5 1.5 %collective-permute-start.2 = (bf16[256,384]{1,0:T(8,128)(2,1)S(1)}, bf16[256,384]{1,0:T(8,128)(2,1)}, u32[]{:S(2)}, u32[]{:S(2)}) collective-permute-start(bf16[256,384]{1,0:T(8,128)(2,1)S(1)} %get-tuple-element.36.refs_0_), channel_id=1, source_target_pairs={{0,2},{1,3},{2,0},{3,1},{4,6},{5,7},{6,4},{7,5},{8,10},{9,11},{10,... | collective-permute-start | bytes 589832 | tf_op jit(solution)/shard_map/ppermute | solution.py:318
  7.0 0.5 collective-permute-start
  7.5 0.0 collective-permute-start.3
  7.6 0.1 pad_add_fusion.1.place_ref
  7.7 3.2 %pick_kernel.1 = (bf16[1536,512]{1,0:T(8,128)(2,1)S(1)}, f32[8,512]{1,0:T(8,128)S(1)}, bf16[1024,512]{1,0:T(8,128)(2,1)S(1)}, s32[1,512]{1,0:T(1,128)S(1)}, f32[1,128]{1,0:T(1,128)S(1)}) custom-call(s32[2]{0:T(128)S(1)} %pad_add_fusion.1.place_ref, s32[1,512]{1,0:T(1,128)} %bitcast.13, f32[1,128]{1,0:T(1,128)} %bitcast.14, bf16[1536,1024]{1,0:T(8,128)(2,1)} %bitcast.9), custom_call_target="tpu_custom_call" | custom-call | bytes 1024 | tf_op jit(solution)/shard_map/pick_kernel/pallas_call | solution.py:303
  10.9 0.6 collective-permute-done.1.refs_3_
  11.4 2.0 %collective-permute-done.2.refs_4_ = bf16[256,384]{1,0:T(8,128)(2,1)} collective-permute-done((bf16[256,384]{1,0:T(8,128)(2,1)S(1)}, bf16[256,384]{1,0:T(8,128)(2,1)}, u32[]{:S(2)}, u32[]{:S(2)}) %collective-permute-start.2) | collective-permute-done | bytes 196640 | tf_op jit(solution)/shard_map/ppermute | solution.py:318
  13.4 0.1 collective-permute-start.4
  13.5 2.0 %collective-permute-start.5 = (bf16[256,384]{1,0:T(8,128)(2,1)S(1)}, bf16[256,384]{1,0:T(8,128)(2,1)S(1)}, u32[]{:S(2)}, u32[]{:S(2)}) collective-permute-start(bf16[256,384]{1,0:T(8,128)(2,1)S(1)} %collective-permute-done.1.refs_3_), channel_id=1, source_target_pairs={{0,2},{1,3},{2,0},{3,1},{4,6},{5,7},{6,4},{7,5},{8,10},{9,11},{10,... | collective-permute-start | bytes 589832 | tf_op jit(solution)/shard_map/ppermute | solution.py:318
  15.5 2.3 %rest_kernel.1.chosen_ref = bf16[1536,512]{1,0:T(8,128)(2,1)S(1)} custom-call(bf16[1536,512]{1,0:T(8,128)(2,1)S(1)} %get-tuple-element.34.chosen_in, bf16[1024,512]{1,0:T(8,128)(2,1)S(1)} %get-tuple-element.35.one_ref, bf16[1536,1024]{1,0:T(8,128)(2,1)} %bitcast.10), custom_call_target="tpu_custom_call", output_to_operand_aliasing={{}: (0, {})} | custom-call | bytes 1024 | tf_op jit(solution)/shard_map/rest_kernel/pallas_call | solution.py:303
  17.8 0.1 pad_add_fusion.place_ref
  17.8 0.0 collective-permute-done.refs_2_
  17.8 0.0 collective-permute-done.3.refs_5_
  17.9 2.3 %early_kernel.1 = (bf16[512,1536]{1,0:T(8,128)(2,1)S(1)}, f32[512,512]{1,0:T(8,128)S(1)}) custom-call(s32[4]{0:T(128)S(1)} %pad_add_fusion.place_ref, bf16[1536,512]{1,0:T(8,128)(2,1)S(1)} %rest_kernel.1.chosen_ref, bf16[256,384]{1,0:T(8,128)(2,1)S(1)} %get-tuple-element.36.refs_0_, bf16[256,384]{1,0:T(8,128)(2,1)} %get-tuple-element.37.refs_1_, ...), custom_call_target="tpu_custom_call" | custom-call | bytes 1024 | tf_op jit(solution)/shard_map/early_kernel/pallas_call | solution.py:303
  20.2 0.0 collective-permute-done.4.refs_0_
  20.2 0.1 collective-permute-done.5.refs_1_
  20.3 0.9 %send_kernel.1 = f32[264,512]{1,0:T(8,128)S(1)} custom-call(s32[4]{0:T(128)S(1)} %pad_add_fusion.place_ref, bf16[1536,512]{1,0:T(8,128)(2,1)S(1)} %rest_kernel.1.chosen_ref, f32[8,512]{1,0:T(8,128)S(1)} %get-tuple-element.40.entry_ref, f32[512,512]{1,0:T(8,128)S(1)} %get-tuple-element.39.terms_ref, bf16[256,384]{1,0:T(8,128)(2,1)S(1)} %collective-permute-done.4.refs_0_, ...), custom_call_target="tpu_custom_call" | custom-call | bytes 1024 | tf_op jit(solution)/shard_map/send_kernel/pallas_call | solution.py:303
  21.1 0.1 collective-permute-start.6
  21.2 0.0 copy-start
  21.2 0.9 %keep_kernel.1 = (bf16[512,1536]{1,0:T(8,128)(2,1)S(1)}, f32[256,512]{1,0:T(8,128)S(1)}) custom-call(s32[4]{0:T(128)S(1)} %pad_add_fusion.place_ref, bf16[512,1536]{1,0:T(8,128)(2,1)S(1)} %get-tuple-element.38.turned_in, bf16[1536,512]{1,0:T(8,128)(2,1)S(1)} %rest_kernel.1.chosen_ref, ...), custom_call_target="tpu_custom_call", output_to_operand_aliasing={{0}: (1, {})} | custom-call | bytes 1024 | tf_op jit(solution)/shard_map/keep_kernel/pallas_call | solution.py:303
  22.1 1.0 %collective-permute-done.6.got_ref = f32[264,512]{1,0:T(8,128)S(1)} collective-permute-done((f32[264,512]{1,0:T(8,128)S(1)}, f32[264,512]{1,0:T(8,128)S(1)}, u32[]{:S(2)}, u32[]{:S(2)}) %collective-permute-start.6) | collective-permute-done | bytes 540704 | tf_op jit(solution)/shard_map/ppermute | solution.py:318
  23.1 0.2 pair_kernel.1
  23.3 1.9 %collective-permute-start.7 = (s16[72,512]{1,0:T(8,128)(2,1)S(1)}, s16[72,512]{1,0:T(8,128)(2,1)S(1)}, u32[]{:S(2)}, u32[]{:S(2)}) collective-permute-start(s16[72,512]{1,0:T(8,128)(2,1)S(1)} %get-tuple-element.51), channel_id=1, source_target_pairs={{0,3},{1,2},{2,1},{3,0},{4,7},{5,6},{6,5},{7,4},{8,11},{9,10},{10,... | collective-permute-start | bytes 221192 | tf_op jit(solution)/shard_map/ppermute | solution.py:318
  25.2 1.1 %collective-permute-start.8 = (s16[72,512]{1,0:T(8,128)(2,1)S(1)}, s16[72,512]{1,0:T(8,128)(2,1)S(1)}, u32[]{:S(2)}, u32[]{:S(2)}) collective-permute-start(s16[72,512]{1,0:T(8,128)(2,1)S(1)} %get-tuple-element.52), channel_id=1, source_target_pairs={{0,2},{1,3},{2,0},{3,1},{4,6},{5,7},{6,4},{7,5},{8,10},{9,11},{10,... | collective-permute-start | bytes 221192 | tf_op jit(solution)/shard_map/ppermute | solution.py:318
  26.3 0.6 collective-permute-start.9
  26.9 0.0 copy-done
  26.9 2.4 %schur_kernel.1 = (f32[2048,128]{1,0:T(8,128)S(1)}, f32[2048,128]{1,0:T(8,128)S(1)}) custom-call(s32[4]{0:T(128)S(1)} %pad_add_fusion.place_ref, s32[1,512]{1,0:T(1,128)S(1)} %get-tuple-element.45.panel_ref, f32[1,128]{1,0:T(1,128)S(1)} %get-tuple-element.46.own_diagonal_ref, bf16[1536,1024]{1,0:T(8,128)(2,1)S(1)} %bitcast.11, ...), custom_call_target="tpu_custom_call" | custom-call | bytes 1024 | tf_op jit(solution)/shard_map/schur_kernel/pallas_call | solution.py:303
  29.2 0.0 collective-permute-done.7.refs_1_
  29.2 0.9 %collective-permute-done.8.refs_2_ = s16[72,512]{1,0:T(8,128)(2,1)S(1)} collective-permute-done((s16[72,512]{1,0:T(8,128)(2,1)S(1)}, s16[72,512]{1,0:T(8,128)(2,1)S(1)}, u32[]{:S(2)}, u32[]{:S(2)}) %collective-permute-start.8) | collective-permute-done | bytes 73760 | tf_op jit(solution)/shard_map/ppermute | solution.py:318
  30.2 0.5 collective-permute-done.9.refs_3_
  30.6 0.1 sum_kernel.3.refs_0_
  30.8 0.1 collective-permute-start.11
  30.8 1.6 %collective-permute-start.10 = (s16[72,512]{1,0:T(8,128)(2,1)S(1)}, s16[72,512]{1,0:T(8,128)(2,1)S(1)}, u32[]{:S(2)}, u32[]{:S(2)}) collective-permute-start(s16[72,512]{1,0:T(8,128)(2,1)S(1)} %sum_kernel.3.refs_0_), channel_id=1, source_target_pairs={{0,8},{4,12},{8,0},{12,4},{16,24},{20,28},{24,16},{28,20},{1,9},{5... | collective-permute-start | bytes 221192 | tf_op jit(solution)/shard_map/ppermute | solution.py:318
  32.5 3.0 %collective-permute-done.10.refs_1_ = s16[72,512]{1,0:T(8,128)(2,1)S(1)} collective-permute-done((s16[72,512]{1,0:T(8,128)(2,1)S(1)}, s16[72,512]{1,0:T(8,128)(2,1)S(1)}, u32[]{:S(2)}, u32[]{:S(2)}) %collective-permute-start.10) | collective-permute-done | bytes 73760 | tf_op jit(solution)/shard_map/ppermute | solution.py:318
  35.5 0.1 sum_kernel.4.refs_0_
  35.6 2.6 %collective-permute-start.12 = (s16[72,512]{1,0:T(8,128)(2,1)S(1)}, s16[72,512]{1,0:T(8,128)(2,1)S(1)}, u32[]{:S(2)}, u32[]{:S(2)}) collective-permute-start(s16[72,512]{1,0:T(8,128)(2,1)S(1)} %sum_kernel.4.refs_0_), channel_id=1, source_target_pairs={{0,16},{4,20},{8,24},{12,28},{16,0},{20,4},{24,8},{28,12},{1,17},{... | collective-permute-start | bytes 221192 | tf_op jit(solution)/shard_map/ppermute | solution.py:318
  38.3 0.0 collective-permute-done.11.got_ref
  38.3 0.2 bulk_pair_kernel.1
  38.5 3.7 %collective-permute-done.12.refs_1_ = s16[72,512]{1,0:T(8,128)(2,1)S(1)} collective-permute-done((s16[72,512]{1,0:T(8,128)(2,1)S(1)}, s16[72,512]{1,0:T(8,128)(2,1)S(1)}, u32[]{:S(2)}, u32[]{:S(2)}) %collective-permute-start.12) | collective-permute-done | bytes 73760 | tf_op jit(solution)/shard_map/ppermute | solution.py:318
  42.2 0.1 sum_kernel.5.refs_0_
  42.3 0.5 collective-permute-start.16
  42.8 1.6 %collective-permute-start.15 = (s16[72,512]{1,0:T(8,128)(2,1)S(1)}, s16[72,512]{1,0:T(8,128)(2,1)S(1)}, u32[]{:S(2)}, u32[]{:S(2)}) collective-permute-start(s16[72,512]{1,0:T(8,128)(2,1)S(1)} %sum_kernel.5.refs_0_), channel_id=1, source_target_pairs={{0,3},{1,2},{2,1},{3,0},{4,7},{5,6},{6,5},{7,4},{8,11},{9,10},{10,... | collective-permute-start | bytes 221192 | tf_op jit(solution)/shard_map/ppermute | solution.py:318
  44.4 0.9 %collective-permute-start.14 = (s16[72,512]{1,0:T(8,128)(2,1)S(1)}, s16[72,512]{1,0:T(8,128)(2,1)S(1)}, u32[]{:S(2)}, u32[]{:S(2)}) collective-permute-start(s16[72,512]{1,0:T(8,128)(2,1)S(1)} %sum_kernel.5.refs_0_), channel_id=1, source_target_pairs={{0,2},{1,3},{2,0},{3,1},{4,6},{5,7},{6,4},{7,5},{8,10},{9,11},{10,... | collective-permute-start | bytes 221192 | tf_op jit(solution)/shard_map/ppermute | solution.py:318
  45.3 1.1 %collective-permute-start.13 = (s16[72,512]{1,0:T(8,128)(2,1)S(1)}, s16[72,512]{1,0:T(8,128)(2,1)S(1)}, u32[]{:S(2)}, u32[]{:S(2)}) collective-permute-start(s16[72,512]{1,0:T(8,128)(2,1)S(1)} %sum_kernel.5.refs_0_), channel_id=1, source_target_pairs={{0,1},{1,0},{2,3},{3,2},{4,5},{5,4},{6,7},{7,6},{8,9},{9,8},{10,11... | collective-permute-start | bytes 221192 | tf_op jit(solution)/shard_map/ppermute | solution.py:318
  46.3 1.8 %collective-permute-done.15.refs_3_ = s16[72,512]{1,0:T(8,128)(2,1)S(1)} collective-permute-done((s16[72,512]{1,0:T(8,128)(2,1)S(1)}, s16[72,512]{1,0:T(8,128)(2,1)S(1)}, u32[]{:S(2)}, u32[]{:S(2)}) %collective-permute-start.15) | collective-permute-done | bytes 73760 | tf_op jit(solution)/shard_map/ppermute | solution.py:318
  48.1 0.8 %collective-permute-done.14.refs_2_ = s16[72,512]{1,0:T(8,128)(2,1)S(1)} collective-permute-done((s16[72,512]{1,0:T(8,128)(2,1)S(1)}, s16[72,512]{1,0:T(8,128)(2,1)S(1)}, u32[]{:S(2)}, u32[]{:S(2)}) %collective-permute-start.14) | collective-permute-done | bytes 73760 | tf_op jit(solution)/shard_map/ppermute | solution.py:318
  48.9 0.8 %collective-permute-done.13.refs_1_ = s16[72,512]{1,0:T(8,128)(2,1)S(1)} collective-permute-done((s16[72,512]{1,0:T(8,128)(2,1)S(1)}, s16[72,512]{1,0:T(8,128)(2,1)S(1)}, u32[]{:S(2)}, u32[]{:S(2)}) %collective-permute-start.13) | collective-permute-done | bytes 73760 | tf_op jit(solution)/shard_map/ppermute | solution.py:318
  49.7 0.0 collective-permute-done.16.got_ref
  49.7 0.2 bulk_sum_kernel.1
  49.8 0.1 collective-permute-start.17
  49.9 3.4 %collective-permute-start.18 = (s16[528,128]{1,0:T(8,128)(2,1)S(1)}, s16[528,128]{1,0:T(8,128)(2,1)S(1)}, u32[]{:S(2)}, u32[]{:S(2)}) collective-permute-start(s16[528,128]{1,0:T(8,128)(2,1)S(1)} %get-tuple-element.61), channel_id=1, source_target_pairs={{0,16},{4,20},{8,24},{12,28},{16,0},{20,4},{24,8},{28,12},{1,17},{... | collective-permute-start | bytes 405512 | tf_op jit(solution)/shard_map/ppermute | solution.py:318
  53.4 0.7 %own_kernel.1.half_ref = f32[256,512]{1,0:T(8,128)S(1)} custom-call(s32[4]{0:T(128)S(1)} %pad_add_fusion.place_ref, s16[320,512]{1,0:T(8,128)(2,1)S(1)} %join_kernel.1.own_ref), custom_call_target="tpu_custom_call" | custom-call | bytes 1024 | tf_op jit(solution)/shard_map/own_kernel/pallas_call | solution.py:303
  54.1 0.0 collective-permute-done.17.other_ref
  54.1 3.9 %first_kernel.1 = (f32[256,256]{1,0:T(8,128)S(1)}, f32[512,512]{1,0:T(8,128)S(1)}) custom-call(s32[4]{0:T(128)S(1)} %pad_add_fusion.place_ref, f32[256,512]{1,0:T(8,128)S(1)} %own_kernel.1.half_ref, s16[320,512]{1,0:T(8,128)(2,1)S(1)} %collective-permute-done.17.other_ref), custom_call_target="tpu_custom_call" | custom-call | bytes 16606024 | tf_op jit(solution)/shard_map/first_kernel/pallas_call | solution.py:303
  58.0 3.8 %second_kernel.1.inverse_second_ref = f32[256,256]{1,0:T(8,128)S(1)} custom-call(f32[512,512]{1,0:T(8,128)S(1)} %get-tuple-element.64.pivots_ref, f32[256,256]{1,0:T(8,128)S(1)} %get-tuple-element.63.inverse_first_ref), custom_call_target="tpu_custom_call" | custom-call | bytes 16606024 | tf_op jit(solution)/shard_map/second_kernel/pallas_call | solution.py:303
  61.9 0.0 collective-permute-done.18.refs_0_
  61.9 1.6 %factor_kernel.1 = (f32[128,1,256]{2,1,0:T(1,128)}, f32[128,1,256]{2,1,0:T(1,128)}) custom-call(f32[256,256]{1,0:T(8,128)S(1)} %get-tuple-element.63.inverse_first_ref, f32[256,256]{1,0:T(8,128)S(1)} %second_kernel.1.inverse_second_ref, f32[512,512]{1,0:T(8,128)S(1)} %get-tuple-element.64.pivots_ref, f32[512,128]{1,0:T(8,128)S(1)} %get-tuple-element.65.rows_ref, ...), custom_call_target="tpu_custom_call" | custom-call | bytes 1024 | tf_op jit(solution)/shard_map/factor_kernel/pallas_call | solution.py:303
  (1 shorter events, 0.0 us)
Async XLA Ops:
  2.5 8.9 %collective-permute-start.1 = (bf16[256,384]{1,0:T(8,128)(2,1)}, bf16[256,384]{1,0:T(8,128)(2,1)S(1)}, u32[]{:S(2)}, u32[]{:S(2)}) collective-permute-start(bf16[256,384]{1,0:T(8,128)(2,1)} %get-tuple-element.37.refs_1_), channel_id=1, source_target_pairs={{0,1},{1,0},{2,3},{3,2},{4,5},{5,4},{6,7},{7,6},{8,9},{9,8},{10,11... | collective-permute-start | bytes 589832 | tf_op jit(solution)/shard_map/ppermute | solution.py:318
  5.5 7.9 %collective-permute-start.2 = (bf16[256,384]{1,0:T(8,128)(2,1)S(1)}, bf16[256,384]{1,0:T(8,128)(2,1)}, u32[]{:S(2)}, u32[]{:S(2)}) collective-permute-start(bf16[256,384]{1,0:T(8,128)(2,1)S(1)} %get-tuple-element.36.refs_0_), channel_id=1, source_target_pairs={{0,2},{1,3},{2,0},{3,1},{4,6},{5,7},{6,4},{7,5},{8,10},{9,11},{10,... | collective-permute-start | bytes 589832 | tf_op jit(solution)/shard_map/ppermute | solution.py:318
  7.0 10.9 %collective-permute-start = (bf16[256,384]{1,0:T(8,128)(2,1)S(1)}, bf16[256,384]{1,0:T(8,128)(2,1)}, u32[]{:S(2)}, u32[]{:S(2)}) collective-permute-start(bf16[256,384]{1,0:T(8,128)(2,1)S(1)} %get-tuple-element.36.refs_0_), channel_id=1, source_target_pairs={{0,1},{1,0},{2,3},{3,2},{4,5},{5,4},{6,7},{7,6},{8,9},{9,8},{10,11... | collective-permute-start | bytes 589832 | tf_op jit(solution)/shard_map/ppermute | solution.py:318
  7.5 10.3 %collective-permute-start.3 = (bf16[256,384]{1,0:T(8,128)(2,1)}, bf16[256,384]{1,0:T(8,128)(2,1)}, u32[]{:S(2)}, u32[]{:S(2)}) collective-permute-start(bf16[256,384]{1,0:T(8,128)(2,1)} %get-tuple-element.37.refs_1_), channel_id=1, source_target_pairs={{0,2},{1,3},{2,0},{3,1},{4,6},{5,7},{6,4},{7,5},{8,10},{9,11},{10,... | collective-permute-start | bytes 589832 | tf_op jit(solution)/shard_map/ppermute | solution.py:318
  13.4 6.8 %collective-permute-start.4 = (bf16[256,384]{1,0:T(8,128)(2,1)}, bf16[256,384]{1,0:T(8,128)(2,1)S(1)}, u32[]{:S(2)}, u32[]{:S(2)}) collective-permute-start(bf16[256,384]{1,0:T(8,128)(2,1)} %collective-permute-done.2.refs_4_), channel_id=1, source_target_pairs={{0,1},{1,0},{2,3},{3,2},{4,5},{5,4},{6,7},{7,6},{8,9},{9,8},{10,11... | collective-permute-start | bytes 589832 | tf_op jit(solution)/shard_map/ppermute | solution.py:318
  13.5 6.8 %collective-permute-start.5 = (bf16[256,384]{1,0:T(8,128)(2,1)S(1)}, bf16[256,384]{1,0:T(8,128)(2,1)S(1)}, u32[]{:S(2)}, u32[]{:S(2)}) collective-permute-start(bf16[256,384]{1,0:T(8,128)(2,1)S(1)} %collective-permute-done.1.refs_3_), channel_id=1, source_target_pairs={{0,2},{1,3},{2,0},{3,1},{4,6},{5,7},{6,4},{7,5},{8,10},{9,11},{10,... | collective-permute-start | bytes 589832 | tf_op jit(solution)/shard_map/ppermute | solution.py:318
  21.1 2.0 %collective-permute-start.6 = (f32[264,512]{1,0:T(8,128)S(1)}, f32[264,512]{1,0:T(8,128)S(1)}, u32[]{:S(2)}, u32[]{:S(2)}) collective-permute-start(f32[264,512]{1,0:T(8,128)S(1)} %send_kernel.1), channel_id=1, source_target_pairs={{0,4},{4,0},{8,12},{12,8},{16,20},{20,16},{24,28},{28,24},{1,5},{5... | collective-permute-start | bytes 1622024 | tf_op jit(solution)/shard_map/ppermute | solution.py:318
  21.2 5.6 %copy-start = (bf16[1,1536,1024]{2,1,0:T(8,128)(2,1)S(1)}, bf16[1,1536,1024]{2,1,0:T(8,128)(2,1)}, u32[]{:S(2)}) copy-start(bf16[1,1536,1024]{2,1,0:T(8,128)(2,1)} %param.4) | copy-start | bytes 9437188
  23.3 5.9 %collective-permute-start.7 = (s16[72,512]{1,0:T(8,128)(2,1)S(1)}, s16[72,512]{1,0:T(8,128)(2,1)S(1)}, u32[]{:S(2)}, u32[]{:S(2)}) collective-permute-start(s16[72,512]{1,0:T(8,128)(2,1)S(1)} %get-tuple-element.51), channel_id=1, source_target_pairs={{0,3},{1,2},{2,1},{3,0},{4,7},{5,6},{6,5},{7,4},{8,11},{9,10},{10,... | collective-permute-start | bytes 221192 | tf_op jit(solution)/shard_map/ppermute | solution.py:318
  25.2 5.0 %collective-permute-start.8 = (s16[72,512]{1,0:T(8,128)(2,1)S(1)}, s16[72,512]{1,0:T(8,128)(2,1)S(1)}, u32[]{:S(2)}, u32[]{:S(2)}) collective-permute-start(s16[72,512]{1,0:T(8,128)(2,1)S(1)} %get-tuple-element.52), channel_id=1, source_target_pairs={{0,2},{1,3},{2,0},{3,1},{4,6},{5,7},{6,4},{7,5},{8,10},{9,11},{10,... | collective-permute-start | bytes 221192 | tf_op jit(solution)/shard_map/ppermute | solution.py:318
  26.3 4.4 %collective-permute-start.9 = (s16[72,512]{1,0:T(8,128)(2,1)S(1)}, s16[72,512]{1,0:T(8,128)(2,1)S(1)}, u32[]{:S(2)}, u32[]{:S(2)}) collective-permute-start(s16[72,512]{1,0:T(8,128)(2,1)S(1)} %get-tuple-element.53), channel_id=1, source_target_pairs={{0,1},{1,0},{2,3},{3,2},{4,5},{5,4},{6,7},{7,6},{8,9},{9,8},{10,11... | collective-permute-start | bytes 221192 | tf_op jit(solution)/shard_map/ppermute | solution.py:318
  30.8 7.5 %collective-permute-start.11 = (f32[2048,128]{1,0:T(8,128)S(1)}, f32[2048,128]{1,0:T(8,128)S(1)}, u32[]{:S(2)}, u32[]{:S(2)}) collective-permute-start(f32[2048,128]{1,0:T(8,128)S(1)} %get-tuple-element.56), channel_id=1, source_target_pairs={{0,4},{4,0},{8,12},{12,8},{16,20},{20,16},{24,28},{28,24},{1,5},{5... | collective-permute-start | bytes 3145736 | tf_op jit(solution)/shard_map/ppermute | solution.py:318
  30.8 4.7 %collective-permute-start.10 = (s16[72,512]{1,0:T(8,128)(2,1)S(1)}, s16[72,512]{1,0:T(8,128)(2,1)S(1)}, u32[]{:S(2)}, u32[]{:S(2)}) collective-permute-start(s16[72,512]{1,0:T(8,128)(2,1)S(1)} %sum_kernel.3.refs_0_), channel_id=1, source_target_pairs={{0,8},{4,12},{8,0},{12,4},{16,24},{20,28},{24,16},{28,20},{1,9},{5... | collective-permute-start | bytes 221192 | tf_op jit(solution)/shard_map/ppermute | solution.py:318
  35.6 6.6 %collective-permute-start.12 = (s16[72,512]{1,0:T(8,128)(2,1)S(1)}, s16[72,512]{1,0:T(8,128)(2,1)S(1)}, u32[]{:S(2)}, u32[]{:S(2)}) collective-permute-start(s16[72,512]{1,0:T(8,128)(2,1)S(1)} %sum_kernel.4.refs_0_), channel_id=1, source_target_pairs={{0,16},{4,20},{8,24},{12,28},{16,0},{20,4},{24,8},{28,12},{1,17},{... | collective-permute-start | bytes 221192 | tf_op jit(solution)/shard_map/ppermute | solution.py:318
  42.3 7.3 %collective-permute-start.16 = (s16[1056,128]{1,0:T(8,128)(2,1)S(1)}, s16[1056,128]{1,0:T(8,128)(2,1)S(1)}, u32[]{:S(2)}, u32[]{:S(2)}) collective-permute-start(s16[1056,128]{1,0:T(8,128)(2,1)S(1)} %get-tuple-element.60), channel_id=1, source_target_pairs={{0,8},{4,12},{8,0},{12,4},{16,24},{20,28},{24,16},{28,20},{1,9},{5... | collective-permute-start | bytes 811016 | tf_op jit(solution)/shard_map/ppermute | solution.py:318
  42.8 5.3 %collective-permute-start.15 = (s16[72,512]{1,0:T(8,128)(2,1)S(1)}, s16[72,512]{1,0:T(8,128)(2,1)S(1)}, u32[]{:S(2)}, u32[]{:S(2)}) collective-permute-start(s16[72,512]{1,0:T(8,128)(2,1)S(1)} %sum_kernel.5.refs_0_), channel_id=1, source_target_pairs={{0,3},{1,2},{2,1},{3,0},{4,7},{5,6},{6,5},{7,4},{8,11},{9,10},{10,... | collective-permute-start | bytes 221192 | tf_op jit(solution)/shard_map/ppermute | solution.py:318
  44.4 4.5 %collective-permute-start.14 = (s16[72,512]{1,0:T(8,128)(2,1)S(1)}, s16[72,512]{1,0:T(8,128)(2,1)S(1)}, u32[]{:S(2)}, u32[]{:S(2)}) collective-permute-start(s16[72,512]{1,0:T(8,128)(2,1)S(1)} %sum_kernel.5.refs_0_), channel_id=1, source_target_pairs={{0,2},{1,3},{2,0},{3,1},{4,6},{5,7},{6,4},{7,5},{8,10},{9,11},{10,... | collective-permute-start | bytes 221192 | tf_op jit(solution)/shard_map/ppermute | solution.py:318
  45.3 4.4 %collective-permute-start.13 = (s16[72,512]{1,0:T(8,128)(2,1)S(1)}, s16[72,512]{1,0:T(8,128)(2,1)S(1)}, u32[]{:S(2)}, u32[]{:S(2)}) collective-permute-start(s16[72,512]{1,0:T(8,128)(2,1)S(1)} %sum_kernel.5.refs_0_), channel_id=1, source_target_pairs={{0,1},{1,0},{2,3},{3,2},{4,5},{5,4},{6,7},{7,6},{8,9},{9,8},{10,11... | collective-permute-start | bytes 221192 | tf_op jit(solution)/shard_map/ppermute | solution.py:318
  49.8 4.2 %collective-permute-start.17 = (s16[320,512]{1,0:T(8,128)(2,1)S(1)}, s16[320,512]{1,0:T(8,128)(2,1)S(1)}, u32[]{:S(2)}, u32[]{:S(2)}) collective-permute-start(s16[320,512]{1,0:T(8,128)(2,1)S(1)} %join_kernel.1.own_ref), channel_id=1, source_target_pairs={{0,4},{4,0},{8,12},{12,8},{16,20},{20,16},{24,28},{28,24},{1,5},{5... | collective-permute-start | bytes 983048 | tf_op jit(solution)/shard_map/ppermute | solution.py:318
  49.9 12.0 %collective-permute-start.18 = (s16[528,128]{1,0:T(8,128)(2,1)S(1)}, s16[528,128]{1,0:T(8,128)(2,1)S(1)}, u32[]{:S(2)}, u32[]{:S(2)}) collective-permute-start(s16[528,128]{1,0:T(8,128)(2,1)S(1)} %get-tuple-element.61), channel_id=1, source_target_pairs={{0,16},{4,20},{8,24},{12,28},{16,0},{20,4},{24,8},{28,12},{1,17},{... | collective-permute-start | bytes 405512 | tf_op jit(solution)/shard_map/ppermute | solution.py:318

commit v7 on v6

--- a/solution.py
+++ b/solution.py
@@ -42,23 +42,34 @@
     return dot(left_of(a), right_of(b))
 
 
-def newton(pivot):
+def nearly(pivot):
     size = jnp.abs(pivot)
     norm_one = jnp.max(jnp.sum(size, axis=0, keepdims=True))
     norm_inf = jnp.max(jnp.sum(size, axis=1, keepdims=True))
     approx = pivot.T / (norm_one * norm_inf)
     count = pivot.shape[0]
     one = lax.broadcasted_iota(jnp.int32, pivot.shape, 0) == lax.broadcasted_iota(jnp.int32, pivot.shape, 1)
-    pivot_right = right_of(pivot)
-    rest = jnp.where(one, F32(1.0), F32(0.0)) - dot(left_of(approx), pivot_right)
-    for step in range(NEWTON - 1):
-        if step < NEWTON - 2:
-            both = product(rest, jnp.concatenate([rest, approx], axis=1))
-            rest, approx = both[:, :count], approx + both[:, count:]
-        else:
-            approx = approx + product(rest, approx)
-    left = dot(left_of(approx), pivot_right)
-    return 2.0 * approx - product(left, approx)
+    rest = jnp.where(one, F32(1.0), F32(0.0)) - product(approx, pivot)
+    for step in range(NEWTON - 2):
+        both = product(rest, jnp.concatenate([rest, approx], axis=1))
+        rest, approx = both[:, :count], approx + both[:, count:]
+    return approx + product(rest, approx)
+
+
+def newton_below(pivot, below):
+    approx = nearly(pivot)
+    count = pivot.shape[0]
+    both = product(jnp.concatenate([pivot, below], axis=0), approx)
+    stacked = jnp.concatenate([approx, both[count:]], axis=0)
+    return 2.0 * stacked - product(stacked, both[:count])
+
+
+def newton_beside(pivot, beside):
+    approx = nearly(pivot)
+    count = pivot.shape[0]
+    both = product(approx, jnp.concatenate([pivot, beside], axis=1))
+    stacked = jnp.concatenate([approx, both[:, count:]], axis=1)
+    return 2.0 * stacked - product(both[:, :count], stacked)
 
 
 def aligned(index, size):
@@ -233,16 +244,17 @@
 
 def first_kernel(rows, place_ref, half_ref, other_ref, inverse_ref, pivots_ref):
     row, core = place_ref[0], place_ref[1]
-    half = inverse_ref.shape[0]
+    half = half_ref.shape[0]
     pivots_ref[pl.ds(aligned(core, half), half), :] = half_ref[...]
     place_pieces(row, 1 - core, other_ref, pivots_ref, rows, 0)
-    inverse_ref[...] = newton(pivots_ref[:half, :half])
+    inverse_ref[...] = newton_below(pivots_ref[:half, :half], pivots_ref[half:, :half])
 
 
 def second_kernel(pivots_ref, inverse_first_ref, inverse_ref):
     half = inverse_ref.shape[0]
-    lower_factor = product(inverse_first_ref[...], pivots_ref[:half, half:])
-    inverse_ref[...] = newton(pivots_ref[half:, half:] - product(pivots_ref[half:, :half], lower_factor))
+    below = inverse_first_ref[half:, :]
+    pivot = pivots_ref[half:, half:] - product(below, pivots_ref[:half, half:])
+    inverse_ref[...] = newton_beside(pivot, -below)
 
 
 def schur_kernel(place_ref, panel_ref, own_diagonal_ref, coupling_ref, turned_ref, keep_ref, send_ref):
@@ -281,17 +293,16 @@
             encode(value, coded_ref, (i - half // panel) * (panel + TAIL), TAIL)
 
 
-def factor_kernel(inverse_first_ref, inverse_second_ref, pivots_ref, rows_ref, *refs):
+def factor_kernel(inverse_first_ref, inverse_second_ref, rows_ref, *refs):
     *got, first_out, second_out = refs
     panel = rows_ref.shape[0]
     half = panel // 2
     rows = rows_ref[...]
     for ref in got:
         rows = rows + decode(ref, 0, panel, TAIL)[0]
-    first_factor = product(inverse_first_ref[...], rows[:half])
-    updated = rows[half:] - product(pivots_ref[half:, :half], first_factor)
-    first_out[...] = first_factor.T[:, None, :]
-    second_out[...] = product(inverse_second_ref[...], updated).T[:, None, :]
+    first, second = rows[:half], rows[half:]
+    first_out[...] = product(inverse_first_ref[:half, :], first).T[:, None, :]
+    second_out[...] = product(inverse_second_ref[...], jnp.concatenate([second, first], axis=0)).T[:, None, :]
 
 
 def call(kernel, out_shape, *args, scratch=(), scalars=0, remain=0, micros=0.0, aliases=None):
@@ -335,7 +346,7 @@
     block, panel = solves.shape
     if rows != 4:
         return [lax.all_gather(solves.T, "row", axis=1, tiled=True)]
-    half = jax.ShapeDtypeStruct((panel // 2, block), BF16)
+    half = pltpu.VMEM((panel // 2, block), BF16)
     upper, lower = call(
         turn_kernel, (half, half), solves, remain=1,
         scratch=[pltpu.VMEM((block, panel), BF16), pltpu.SemaphoreType.DMA],
@@ -356,7 +367,7 @@
     row, place = lax.axis_index("row"), lax.axis_index("scen")
     share = row_count // scen
     size = panel // (2 * rows)
-    shape = jax.ShapeDtypeStruct
+    shape = pltpu.VMEM
     panel_row, diagonal_row = panel_rows[None, :], border_diagonal.T
     first_row = row * row_count + place * share
     starts = jnp.stack([row * row_count, first_row]).astype(jnp.int32)
@@ -432,16 +443,15 @@
     own_half = call(
         functools.partial(own_kernel, rows), shape((panel // 2, panel), F32), at, joined, scalars=1
     )
-    square = shape((half, half), F32)
     inverse_first, pivots = call(
-        functools.partial(first_kernel, rows), (square, shape((panel, panel), F32)),
+        functools.partial(first_kernel, rows), (shape((panel, half), F32), shape((panel, panel), F32)),
         at, own_half, other, scalars=1, micros=4.5,
     )
-    inverse_second = call(second_kernel, square, pivots, inverse_first, micros=4.5)
-    out = shape((share, 1, half), F32)
+    inverse_second = call(second_kernel, shape((half, panel), F32), pivots, inverse_first, micros=4.5)
+    out = jax.ShapeDtypeStruct((share, 1, half), F32)
     return call(
         factor_kernel, (out, out),
-        inverse_first, inverse_second, pivots, own, *got,
+        inverse_first, inverse_second, own, *got,
     )
 
 

time: 63.7 us -> 63.5 us (level)
  transfers between devices with their start and end apart: 19 -> 19, of which waited for: 11 -> 11; matrix products, arithmetic and copies ran while one was open for 0% -> 0% of each run, Pallas kernels for 31% -> 32%
where the time goes in v7:
time: 63.5 us; the launch traced here: 63.3 us
  Pallas kernels  24.5 us (39%)
  starting transfers between devices  22.7 us (36%)
  waiting for transfers between devices  15.1 us (24%)
  between operations  0.83 us (1%)
    pallas_call x18, Pallas kernels, call(): pl.pallas_call(kernel, name=getattr(kernel, 'func', kernel).__name__, out...  24.5 us
    ppermute x19, starting transfers between devices, swap(): return lax.ppermute(x, axis, [(i, i ^ bit) for i in range(count)])  22.7 us
    ppermute x19, waiting for transfers between devices, swap(): return lax.ppermute(x, axis, [(i, i ^ bit) for i in range(count)])  15.1 us
  transfers between devices with their start and end apart: 19, of which 11 were waited for; matrix products, arithmetic and copies ran while one was open for 0% of the time, Pallas kernels for 32%

profile of v7, /device:TPU:0, one launch (start us, length us, event | category | flops | bytes accessed | tf_op | source)
XLA Modules:
  0.0 63.3 jit_solution(4777012552143879308)
XLA Ops:
  0.6 1.8 %turn_kernel.1 = (bf16[256,384]{1,0:T(8,128)(2,1)S(1)}, bf16[256,384]{1,0:T(8,128)(2,1)}) custom-call(bf16[384,512]{1,0:T(8,128)(2,1)} %bitcast.12), custom_call_target="tpu_custom_call" | custom-call | bytes 1024 | tf_op jit(solution)/shard_map/turn_kernel/pallas_call | solution.py:314
  2.5 3.0 %collective-permute-start.1 = (bf16[256,384]{1,0:T(8,128)(2,1)}, bf16[256,384]{1,0:T(8,128)(2,1)S(1)}, u32[]{:S(2)}, u32[]{:S(2)}) collective-permute-start(bf16[256,384]{1,0:T(8,128)(2,1)} %get-tuple-element.37.refs_1_), channel_id=1, source_target_pairs={{0,1},{1,0},{2,3},{3,2},{4,5},{5,4},{6,7},{7,6},{8,9},{9,8},{10,11... | collective-permute-start | bytes 589832 | tf_op jit(solution)/shard_map/ppermute | solution.py:329
  5.5 1.5 %collective-permute-start.2 = (bf16[256,384]{1,0:T(8,128)(2,1)S(1)}, bf16[256,384]{1,0:T(8,128)(2,1)}, u32[]{:S(2)}, u32[]{:S(2)}) collective-permute-start(bf16[256,384]{1,0:T(8,128)(2,1)S(1)} %get-tuple-element.36.refs_0_), channel_id=1, source_target_pairs={{0,2},{1,3},{2,0},{3,1},{4,6},{5,7},{6,4},{7,5},{8,10},{9,11},{10,... | collective-permute-start | bytes 589832 | tf_op jit(solution)/shard_map/ppermute | solution.py:329
  7.0 0.5 collective-permute-start
  7.5 0.0 collective-permute-start.3
  7.6 0.1 pad_add_fusion.1.place_ref
  7.7 3.2 %pick_kernel.1 = (bf16[1536,512]{1,0:T(8,128)(2,1)S(1)}, f32[8,512]{1,0:T(8,128)S(1)}, bf16[1024,512]{1,0:T(8,128)(2,1)S(1)}, s32[1,512]{1,0:T(1,128)S(1)}, f32[1,128]{1,0:T(1,128)S(1)}) custom-call(s32[2]{0:T(128)S(1)} %pad_add_fusion.1.place_ref, s32[1,512]{1,0:T(1,128)} %bitcast.13, f32[1,128]{1,0:T(1,128)} %bitcast.14, bf16[1536,1024]{1,0:T(8,128)(2,1)} %bitcast.9), custom_call_target="tpu_custom_call" | custom-call | bytes 1024 | tf_op jit(solution)/shard_map/pick_kernel/pallas_call | solution.py:314
  10.9 0.6 collective-permute-done.1.refs_3_
  11.4 2.0 %collective-permute-done.2.refs_4_ = bf16[256,384]{1,0:T(8,128)(2,1)} collective-permute-done((bf16[256,384]{1,0:T(8,128)(2,1)S(1)}, bf16[256,384]{1,0:T(8,128)(2,1)}, u32[]{:S(2)}, u32[]{:S(2)}) %collective-permute-start.2) | collective-permute-done | bytes 196640 | tf_op jit(solution)/shard_map/ppermute | solution.py:329
  13.4 0.1 collective-permute-start.4
  13.5 2.0 %collective-permute-start.5 = (bf16[256,384]{1,0:T(8,128)(2,1)S(1)}, bf16[256,384]{1,0:T(8,128)(2,1)S(1)}, u32[]{:S(2)}, u32[]{:S(2)}) collective-permute-start(bf16[256,384]{1,0:T(8,128)(2,1)S(1)} %collective-permute-done.1.refs_3_), channel_id=1, source_target_pairs={{0,2},{1,3},{2,0},{3,1},{4,6},{5,7},{6,4},{7,5},{8,10},{9,11},{10,... | collective-permute-start | bytes 589832 | tf_op jit(solution)/shard_map/ppermute | solution.py:329
  15.5 2.3 %rest_kernel.1.chosen_ref = bf16[1536,512]{1,0:T(8,128)(2,1)S(1)} custom-call(bf16[1536,512]{1,0:T(8,128)(2,1)S(1)} %get-tuple-element.34.chosen_in, bf16[1024,512]{1,0:T(8,128)(2,1)S(1)} %get-tuple-element.35.one_ref, bf16[1536,1024]{1,0:T(8,128)(2,1)} %bitcast.10), custom_call_target="tpu_custom_call", output_to_operand_aliasing={{}: (0, {})} | custom-call | bytes 1024 | tf_op jit(solution)/shard_map/rest_kernel/pallas_call | solution.py:314
  17.8 0.1 pad_add_fusion.place_ref
  17.8 0.0 collective-permute-done.refs_2_
  17.8 0.0 collective-permute-done.3.refs_5_
  17.9 2.3 %early_kernel.1 = (bf16[512,1536]{1,0:T(8,128)(2,1)S(1)}, f32[512,512]{1,0:T(8,128)S(1)}) custom-call(s32[4]{0:T(128)S(1)} %pad_add_fusion.place_ref, bf16[1536,512]{1,0:T(8,128)(2,1)S(1)} %rest_kernel.1.chosen_ref, bf16[256,384]{1,0:T(8,128)(2,1)S(1)} %get-tuple-element.36.refs_0_, bf16[256,384]{1,0:T(8,128)(2,1)} %get-tuple-element.37.refs_1_, ...), custom_call_target="tpu_custom_call" | custom-call | bytes 1024 | tf_op jit(solution)/shard_map/early_kernel/pallas_call | solution.py:314
  20.2 0.0 collective-permute-done.4.refs_0_
  20.2 0.1 collective-permute-done.5.refs_1_
  20.3 0.9 %send_kernel.1 = f32[264,512]{1,0:T(8,128)S(1)} custom-call(s32[4]{0:T(128)S(1)} %pad_add_fusion.place_ref, bf16[1536,512]{1,0:T(8,128)(2,1)S(1)} %rest_kernel.1.chosen_ref, f32[8,512]{1,0:T(8,128)S(1)} %get-tuple-element.40.entry_ref, f32[512,512]{1,0:T(8,128)S(1)} %get-tuple-element.39.terms_ref, bf16[256,384]{1,0:T(8,128)(2,1)S(1)} %collective-permute-done.4.refs_0_, ...), custom_call_target="tpu_custom_call" | custom-call | bytes 1024 | tf_op jit(solution)/shard_map/send_kernel/pallas_call | solution.py:314
  21.1 0.1 collective-permute-start.6
  21.2 0.0 copy-start
  21.2 0.9 %keep_kernel.1 = (bf16[512,1536]{1,0:T(8,128)(2,1)S(1)}, f32[256,512]{1,0:T(8,128)S(1)}) custom-call(s32[4]{0:T(128)S(1)} %pad_add_fusion.place_ref, bf16[512,1536]{1,0:T(8,128)(2,1)S(1)} %get-tuple-element.38.turned_in, bf16[1536,512]{1,0:T(8,128)(2,1)S(1)} %rest_kernel.1.chosen_ref, ...), custom_call_target="tpu_custom_call", output_to_operand_aliasing={{0}: (1, {})} | custom-call | bytes 1024 | tf_op jit(solution)/shard_map/keep_kernel/pallas_call | solution.py:314
  22.1 1.0 %collective-permute-done.6.got_ref = f32[264,512]{1,0:T(8,128)S(1)} collective-permute-done((f32[264,512]{1,0:T(8,128)S(1)}, f32[264,512]{1,0:T(8,128)S(1)}, u32[]{:S(2)}, u32[]{:S(2)}) %collective-permute-start.6) | collective-permute-done | bytes 540704 | tf_op jit(solution)/shard_map/ppermute | solution.py:329
  23.1 0.2 pair_kernel.1
  23.3 1.9 %collective-permute-start.7 = (s16[72,512]{1,0:T(8,128)(2,1)S(1)}, s16[72,512]{1,0:T(8,128)(2,1)S(1)}, u32[]{:S(2)}, u32[]{:S(2)}) collective-permute-start(s16[72,512]{1,0:T(8,128)(2,1)S(1)} %get-tuple-element.51), channel_id=1, source_target_pairs={{0,3},{1,2},{2,1},{3,0},{4,7},{5,6},{6,5},{7,4},{8,11},{9,10},{10,... | collective-permute-start | bytes 221192 | tf_op jit(solution)/shard_map/ppermute | solution.py:329
  25.2 1.1 %collective-permute-start.8 = (s16[72,512]{1,0:T(8,128)(2,1)S(1)}, s16[72,512]{1,0:T(8,128)(2,1)S(1)}, u32[]{:S(2)}, u32[]{:S(2)}) collective-permute-start(s16[72,512]{1,0:T(8,128)(2,1)S(1)} %get-tuple-element.52), channel_id=1, source_target_pairs={{0,2},{1,3},{2,0},{3,1},{4,6},{5,7},{6,4},{7,5},{8,10},{9,11},{10,... | collective-permute-start | bytes 221192 | tf_op jit(solution)/shard_map/ppermute | solution.py:329
  26.3 0.6 collective-permute-start.9
  26.9 0.0 copy-done
  26.9 2.4 %schur_kernel.1 = (f32[2048,128]{1,0:T(8,128)S(1)}, f32[2048,128]{1,0:T(8,128)S(1)}) custom-call(s32[4]{0:T(128)S(1)} %pad_add_fusion.place_ref, s32[1,512]{1,0:T(1,128)S(1)} %get-tuple-element.45.panel_ref, f32[1,128]{1,0:T(1,128)S(1)} %get-tuple-element.46.own_diagonal_ref, bf16[1536,1024]{1,0:T(8,128)(2,1)S(1)} %bitcast.11, ...), custom_call_target="tpu_custom_call" | custom-call | bytes 1024 | tf_op jit(solution)/shard_map/schur_kernel/pallas_call | solution.py:314
  29.2 0.0 collective-permute-done.7.refs_1_
  29.2 0.9 %collective-permute-done.8.refs_2_ = s16[72,512]{1,0:T(8,128)(2,1)S(1)} collective-permute-done((s16[72,512]{1,0:T(8,128)(2,1)S(1)}, s16[72,512]{1,0:T(8,128)(2,1)S(1)}, u32[]{:S(2)}, u32[]{:S(2)}) %collective-permute-start.8) | collective-permute-done | bytes 73760 | tf_op jit(solution)/shard_map/ppermute | solution.py:329
  30.2 0.5 collective-permute-done.9.refs_3_
  30.6 0.1 sum_kernel.3.refs_0_
  30.8 0.1 collective-permute-start.11
  30.8 1.6 %collective-permute-start.10 = (s16[72,512]{1,0:T(8,128)(2,1)S(1)}, s16[72,512]{1,0:T(8,128)(2,1)S(1)}, u32[]{:S(2)}, u32[]{:S(2)}) collective-permute-start(s16[72,512]{1,0:T(8,128)(2,1)S(1)} %sum_kernel.3.refs_0_), channel_id=1, source_target_pairs={{0,8},{4,12},{8,0},{12,4},{16,24},{20,28},{24,16},{28,20},{1,9},{5... | collective-permute-start | bytes 221192 | tf_op jit(solution)/shard_map/ppermute | solution.py:329
  32.5 3.0 %collective-permute-done.10.refs_1_ = s16[72,512]{1,0:T(8,128)(2,1)S(1)} collective-permute-done((s16[72,512]{1,0:T(8,128)(2,1)S(1)}, s16[72,512]{1,0:T(8,128)(2,1)S(1)}, u32[]{:S(2)}, u32[]{:S(2)}) %collective-permute-start.10) | collective-permute-done | bytes 73760 | tf_op jit(solution)/shard_map/ppermute | solution.py:329
  35.5 0.1 sum_kernel.4.refs_0_
  35.6 2.6 %collective-permute-start.12 = (s16[72,512]{1,0:T(8,128)(2,1)S(1)}, s16[72,512]{1,0:T(8,128)(2,1)S(1)}, u32[]{:S(2)}, u32[]{:S(2)}) collective-permute-start(s16[72,512]{1,0:T(8,128)(2,1)S(1)} %sum_kernel.4.refs_0_), channel_id=1, source_target_pairs={{0,16},{4,20},{8,24},{12,28},{16,0},{20,4},{24,8},{28,12},{1,17},{... | collective-permute-start | bytes 221192 | tf_op jit(solution)/shard_map/ppermute | solution.py:329
  38.3 0.0 collective-permute-done.11.got_ref
  38.3 0.2 bulk_pair_kernel.1
  38.5 3.7 %collective-permute-done.12.refs_1_ = s16[72,512]{1,0:T(8,128)(2,1)S(1)} collective-permute-done((s16[72,512]{1,0:T(8,128)(2,1)S(1)}, s16[72,512]{1,0:T(8,128)(2,1)S(1)}, u32[]{:S(2)}, u32[]{:S(2)}) %collective-permute-start.12) | collective-permute-done | bytes 73760 | tf_op jit(solution)/shard_map/ppermute | solution.py:329
  42.2 0.1 sum_kernel.5.refs_0_
  42.3 0.5 collective-permute-start.16
  42.8 1.6 %collective-permute-start.15 = (s16[72,512]{1,0:T(8,128)(2,1)S(1)}, s16[72,512]{1,0:T(8,128)(2,1)S(1)}, u32[]{:S(2)}, u32[]{:S(2)}) collective-permute-start(s16[72,512]{1,0:T(8,128)(2,1)S(1)} %sum_kernel.5.refs_0_), channel_id=1, source_target_pairs={{0,3},{1,2},{2,1},{3,0},{4,7},{5,6},{6,5},{7,4},{8,11},{9,10},{10,... | collective-permute-start | bytes 221192 | tf_op jit(solution)/shard_map/ppermute | solution.py:329
  44.4 0.9 %collective-permute-start.14 = (s16[72,512]{1,0:T(8,128)(2,1)S(1)}, s16[72,512]{1,0:T(8,128)(2,1)S(1)}, u32[]{:S(2)}, u32[]{:S(2)}) collective-permute-start(s16[72,512]{1,0:T(8,128)(2,1)S(1)} %sum_kernel.5.refs_0_), channel_id=1, source_target_pairs={{0,2},{1,3},{2,0},{3,1},{4,6},{5,7},{6,4},{7,5},{8,10},{9,11},{10,... | collective-permute-start | bytes 221192 | tf_op jit(solution)/shard_map/ppermute | solution.py:329
  45.3 1.1 %collective-permute-start.13 = (s16[72,512]{1,0:T(8,128)(2,1)S(1)}, s16[72,512]{1,0:T(8,128)(2,1)S(1)}, u32[]{:S(2)}, u32[]{:S(2)}) collective-permute-start(s16[72,512]{1,0:T(8,128)(2,1)S(1)} %sum_kernel.5.refs_0_), channel_id=1, source_target_pairs={{0,1},{1,0},{2,3},{3,2},{4,5},{5,4},{6,7},{7,6},{8,9},{9,8},{10,11... | collective-permute-start | bytes 221192 | tf_op jit(solution)/shard_map/ppermute | solution.py:329
  46.3 1.8 %collective-permute-done.15.refs_3_ = s16[72,512]{1,0:T(8,128)(2,1)S(1)} collective-permute-done((s16[72,512]{1,0:T(8,128)(2,1)S(1)}, s16[72,512]{1,0:T(8,128)(2,1)S(1)}, u32[]{:S(2)}, u32[]{:S(2)}) %collective-permute-start.15) | collective-permute-done | bytes 73760 | tf_op jit(solution)/shard_map/ppermute | solution.py:329
  48.1 0.8 %collective-permute-done.14.refs_2_ = s16[72,512]{1,0:T(8,128)(2,1)S(1)} collective-permute-done((s16[72,512]{1,0:T(8,128)(2,1)S(1)}, s16[72,512]{1,0:T(8,128)(2,1)S(1)}, u32[]{:S(2)}, u32[]{:S(2)}) %collective-permute-start.14) | collective-permute-done | bytes 73760 | tf_op jit(solution)/shard_map/ppermute | solution.py:329
  48.9 0.8 %collective-permute-done.13.refs_1_ = s16[72,512]{1,0:T(8,128)(2,1)S(1)} collective-permute-done((s16[72,512]{1,0:T(8,128)(2,1)S(1)}, s16[72,512]{1,0:T(8,128)(2,1)S(1)}, u32[]{:S(2)}, u32[]{:S(2)}) %collective-permute-start.13) | collective-permute-done | bytes 73760 | tf_op jit(solution)/shard_map/ppermute | solution.py:329
  49.7 0.0 collective-permute-done.16.got_ref
  49.7 0.2 bulk_sum_kernel.1
  49.8 0.1 collective-permute-start.17
  49.9 3.4 %collective-permute-start.18 = (s16[528,128]{1,0:T(8,128)(2,1)S(1)}, s16[528,128]{1,0:T(8,128)(2,1)S(1)}, u32[]{:S(2)}, u32[]{:S(2)}) collective-permute-start(s16[528,128]{1,0:T(8,128)(2,1)S(1)} %get-tuple-element.61), channel_id=1, source_target_pairs={{0,16},{4,20},{8,24},{12,28},{16,0},{20,4},{24,8},{28,12},{1,17},{... | collective-permute-start | bytes 405512 | tf_op jit(solution)/shard_map/ppermute | solution.py:329
  53.4 0.7 %own_kernel.1.half_ref = f32[256,512]{1,0:T(8,128)S(1)} custom-call(s32[4]{0:T(128)S(1)} %pad_add_fusion.place_ref, s16[320,512]{1,0:T(8,128)(2,1)S(1)} %join_kernel.1.own_ref), custom_call_target="tpu_custom_call" | custom-call | bytes 1024 | tf_op jit(solution)/shard_map/own_kernel/pallas_call | solution.py:314
  54.1 0.0 collective-permute-done.17.other_ref
  54.1 4.4 %first_kernel.1 = (f32[512,256]{1,0:T(8,128)S(1)}, f32[512,512]{1,0:T(8,128)S(1)}) custom-call(s32[4]{0:T(128)S(1)} %pad_add_fusion.place_ref, f32[256,512]{1,0:T(8,128)S(1)} %own_kernel.1.half_ref, s16[320,512]{1,0:T(8,128)(2,1)S(1)} %collective-permute-done.17.other_ref), custom_call_target="tpu_custom_call" | custom-call | bytes 16606024 | tf_op jit(solution)/shard_map/first_kernel/pallas_call | solution.py:314
  58.5 3.5 %second_kernel.1.inverse_second_ref = f32[256,512]{1,0:T(8,128)S(1)} custom-call(f32[512,512]{1,0:T(8,128)S(1)} %get-tuple-element.64.pivots_ref, f32[512,256]{1,0:T(8,128)S(1)} %get-tuple-element.63.inverse_first_ref), custom_call_target="tpu_custom_call" | custom-call | bytes 16606024 | tf_op jit(solution)/shard_map/second_kernel/pallas_call | solution.py:314
  62.1 0.0 collective-permute-done.18.refs_0_
  62.1 1.2 %factor_kernel.1 = (f32[128,1,256]{2,1,0:T(1,128)}, f32[128,1,256]{2,1,0:T(1,128)}) custom-call(f32[512,256]{1,0:T(8,128)S(1)} %get-tuple-element.63.inverse_first_ref, f32[256,512]{1,0:T(8,128)S(1)} %second_kernel.1.inverse_second_ref, f32[512,128]{1,0:T(8,128)S(1)} %get-tuple-element.65.rows_ref, s16[528,128]{1,0:T(8,128)(2,1)S(1)} %collective-permute-done.18.refs_0_), custom_call_target="tpu_custom_call" | custom-call | bytes 1024 | tf_op jit(solution)/shard_map/factor_kernel/pallas_call | solution.py:314
  (1 shorter events, 0.0 us)
Async XLA Ops:
  2.5 8.9 %collective-permute-start.1 = (bf16[256,384]{1,0:T(8,128)(2,1)}, bf16[256,384]{1,0:T(8,128)(2,1)S(1)}, u32[]{:S(2)}, u32[]{:S(2)}) collective-permute-start(bf16[256,384]{1,0:T(8,128)(2,1)} %get-tuple-element.37.refs_1_), channel_id=1, source_target_pairs={{0,1},{1,0},{2,3},{3,2},{4,5},{5,4},{6,7},{7,6},{8,9},{9,8},{10,11... | collective-permute-start | bytes 589832 | tf_op jit(solution)/shard_map/ppermute | solution.py:329
  5.5 7.9 %collective-permute-start.2 = (bf16[256,384]{1,0:T(8,128)(2,1)S(1)}, bf16[256,384]{1,0:T(8,128)(2,1)}, u32[]{:S(2)}, u32[]{:S(2)}) collective-permute-start(bf16[256,384]{1,0:T(8,128)(2,1)S(1)} %get-tuple-element.36.refs_0_), channel_id=1, source_target_pairs={{0,2},{1,3},{2,0},{3,1},{4,6},{5,7},{6,4},{7,5},{8,10},{9,11},{10,... | collective-permute-start | bytes 589832 | tf_op jit(solution)/shard_map/ppermute | solution.py:329
  7.0 10.9 %collective-permute-start = (bf16[256,384]{1,0:T(8,128)(2,1)S(1)}, bf16[256,384]{1,0:T(8,128)(2,1)}, u32[]{:S(2)}, u32[]{:S(2)}) collective-permute-start(bf16[256,384]{1,0:T(8,128)(2,1)S(1)} %get-tuple-element.36.refs_0_), channel_id=1, source_target_pairs={{0,1},{1,0},{2,3},{3,2},{4,5},{5,4},{6,7},{7,6},{8,9},{9,8},{10,11... | collective-permute-start | bytes 589832 | tf_op jit(solution)/shard_map/ppermute | solution.py:329
  7.5 10.3 %collective-permute-start.3 = (bf16[256,384]{1,0:T(8,128)(2,1)}, bf16[256,384]{1,0:T(8,128)(2,1)}, u32[]{:S(2)}, u32[]{:S(2)}) collective-permute-start(bf16[256,384]{1,0:T(8,128)(2,1)} %get-tuple-element.37.refs_1_), channel_id=1, source_target_pairs={{0,2},{1,3},{2,0},{3,1},{4,6},{5,7},{6,4},{7,5},{8,10},{9,11},{10,... | collective-permute-start | bytes 589832 | tf_op jit(solution)/shard_map/ppermute | solution.py:329
  13.4 6.8 %collective-permute-start.4 = (bf16[256,384]{1,0:T(8,128)(2,1)}, bf16[256,384]{1,0:T(8,128)(2,1)S(1)}, u32[]{:S(2)}, u32[]{:S(2)}) collective-permute-start(bf16[256,384]{1,0:T(8,128)(2,1)} %collective-permute-done.2.refs_4_), channel_id=1, source_target_pairs={{0,1},{1,0},{2,3},{3,2},{4,5},{5,4},{6,7},{7,6},{8,9},{9,8},{10,11... | collective-permute-start | bytes 589832 | tf_op jit(solution)/shard_map/ppermute | solution.py:329
  13.5 6.8 %collective-permute-start.5 = (bf16[256,384]{1,0:T(8,128)(2,1)S(1)}, bf16[256,384]{1,0:T(8,128)(2,1)S(1)}, u32[]{:S(2)}, u32[]{:S(2)}) collective-permute-start(bf16[256,384]{1,0:T(8,128)(2,1)S(1)} %collective-permute-done.1.refs_3_), channel_id=1, source_target_pairs={{0,2},{1,3},{2,0},{3,1},{4,6},{5,7},{6,4},{7,5},{8,10},{9,11},{10,... | collective-permute-start | bytes 589832 | tf_op jit(solution)/shard_map/ppermute | solution.py:329
  21.1 2.0 %collective-permute-start.6 = (f32[264,512]{1,0:T(8,128)S(1)}, f32[264,512]{1,0:T(8,128)S(1)}, u32[]{:S(2)}, u32[]{:S(2)}) collective-permute-start(f32[264,512]{1,0:T(8,128)S(1)} %send_kernel.1), channel_id=1, source_target_pairs={{0,4},{4,0},{8,12},{12,8},{16,20},{20,16},{24,28},{28,24},{1,5},{5... | collective-permute-start | bytes 1622024 | tf_op jit(solution)/shard_map/ppermute | solution.py:329
  21.2 5.6 %copy-start = (bf16[1,1536,1024]{2,1,0:T(8,128)(2,1)S(1)}, bf16[1,1536,1024]{2,1,0:T(8,128)(2,1)}, u32[]{:S(2)}) copy-start(bf16[1,1536,1024]{2,1,0:T(8,128)(2,1)} %param.4) | copy-start | bytes 9437188
  23.3 5.9 %collective-permute-start.7 = (s16[72,512]{1,0:T(8,128)(2,1)S(1)}, s16[72,512]{1,0:T(8,128)(2,1)S(1)}, u32[]{:S(2)}, u32[]{:S(2)}) collective-permute-start(s16[72,512]{1,0:T(8,128)(2,1)S(1)} %get-tuple-element.51), channel_id=1, source_target_pairs={{0,3},{1,2},{2,1},{3,0},{4,7},{5,6},{6,5},{7,4},{8,11},{9,10},{10,... | collective-permute-start | bytes 221192 | tf_op jit(solution)/shard_map/ppermute | solution.py:329
  25.2 5.0 %collective-permute-start.8 = (s16[72,512]{1,0:T(8,128)(2,1)S(1)}, s16[72,512]{1,0:T(8,128)(2,1)S(1)}, u32[]{:S(2)}, u32[]{:S(2)}) collective-permute-start(s16[72,512]{1,0:T(8,128)(2,1)S(1)} %get-tuple-element.52), channel_id=1, source_target_pairs={{0,2},{1,3},{2,0},{3,1},{4,6},{5,7},{6,4},{7,5},{8,10},{9,11},{10,... | collective-permute-start | bytes 221192 | tf_op jit(solution)/shard_map/ppermute | solution.py:329
  26.3 4.4 %collective-permute-start.9 = (s16[72,512]{1,0:T(8,128)(2,1)S(1)}, s16[72,512]{1,0:T(8,128)(2,1)S(1)}, u32[]{:S(2)}, u32[]{:S(2)}) collective-permute-start(s16[72,512]{1,0:T(8,128)(2,1)S(1)} %get-tuple-element.53), channel_id=1, source_target_pairs={{0,1},{1,0},{2,3},{3,2},{4,5},{5,4},{6,7},{7,6},{8,9},{9,8},{10,11... | collective-permute-start | bytes 221192 | tf_op jit(solution)/shard_map/ppermute | solution.py:329
  30.8 7.5 %collective-permute-start.11 = (f32[2048,128]{1,0:T(8,128)S(1)}, f32[2048,128]{1,0:T(8,128)S(1)}, u32[]{:S(2)}, u32[]{:S(2)}) collective-permute-start(f32[2048,128]{1,0:T(8,128)S(1)} %get-tuple-element.56), channel_id=1, source_target_pairs={{0,4},{4,0},{8,12},{12,8},{16,20},{20,16},{24,28},{28,24},{1,5},{5... | collective-permute-start | bytes 3145736 | tf_op jit(solution)/shard_map/ppermute | solution.py:329
  30.8 4.7 %collective-permute-start.10 = (s16[72,512]{1,0:T(8,128)(2,1)S(1)}, s16[72,512]{1,0:T(8,128)(2,1)S(1)}, u32[]{:S(2)}, u32[]{:S(2)}) collective-permute-start(s16[72,512]{1,0:T(8,128)(2,1)S(1)} %sum_kernel.3.refs_0_), channel_id=1, source_target_pairs={{0,8},{4,12},{8,0},{12,4},{16,24},{20,28},{24,16},{28,20},{1,9},{5... | collective-permute-start | bytes 221192 | tf_op jit(solution)/shard_map/ppermute | solution.py:329
  35.6 6.6 %collective-permute-start.12 = (s16[72,512]{1,0:T(8,128)(2,1)S(1)}, s16[72,512]{1,0:T(8,128)(2,1)S(1)}, u32[]{:S(2)}, u32[]{:S(2)}) collective-permute-start(s16[72,512]{1,0:T(8,128)(2,1)S(1)} %sum_kernel.4.refs_0_), channel_id=1, source_target_pairs={{0,16},{4,20},{8,24},{12,28},{16,0},{20,4},{24,8},{28,12},{1,17},{... | collective-permute-start | bytes 221192 | tf_op jit(solution)/shard_map/ppermute | solution.py:329
  42.3 7.3 %collective-permute-start.16 = (s16[1056,128]{1,0:T(8,128)(2,1)S(1)}, s16[1056,128]{1,0:T(8,128)(2,1)S(1)}, u32[]{:S(2)}, u32[]{:S(2)}) collective-permute-start(s16[1056,128]{1,0:T(8,128)(2,1)S(1)} %get-tuple-element.60), channel_id=1, source_target_pairs={{0,8},{4,12},{8,0},{12,4},{16,24},{20,28},{24,16},{28,20},{1,9},{5... | collective-permute-start | bytes 811016 | tf_op jit(solution)/shard_map/ppermute | solution.py:329
  42.8 5.3 %collective-permute-start.15 = (s16[72,512]{1,0:T(8,128)(2,1)S(1)}, s16[72,512]{1,0:T(8,128)(2,1)S(1)}, u32[]{:S(2)}, u32[]{:S(2)}) collective-permute-start(s16[72,512]{1,0:T(8,128)(2,1)S(1)} %sum_kernel.5.refs_0_), channel_id=1, source_target_pairs={{0,3},{1,2},{2,1},{3,0},{4,7},{5,6},{6,5},{7,4},{8,11},{9,10},{10,... | collective-permute-start | bytes 221192 | tf_op jit(solution)/shard_map/ppermute | solution.py:329
  44.4 4.5 %collective-permute-start.14 = (s16[72,512]{1,0:T(8,128)(2,1)S(1)}, s16[72,512]{1,0:T(8,128)(2,1)S(1)}, u32[]{:S(2)}, u32[]{:S(2)}) collective-permute-start(s16[72,512]{1,0:T(8,128)(2,1)S(1)} %sum_kernel.5.refs_0_), channel_id=1, source_target_pairs={{0,2},{1,3},{2,0},{3,1},{4,6},{5,7},{6,4},{7,5},{8,10},{9,11},{10,... | collective-permute-start | bytes 221192 | tf_op jit(solution)/shard_map/ppermute | solution.py:329
  45.3 4.4 %collective-permute-start.13 = (s16[72,512]{1,0:T(8,128)(2,1)S(1)}, s16[72,512]{1,0:T(8,128)(2,1)S(1)}, u32[]{:S(2)}, u32[]{:S(2)}) collective-permute-start(s16[72,512]{1,0:T(8,128)(2,1)S(1)} %sum_kernel.5.refs_0_), channel_id=1, source_target_pairs={{0,1},{1,0},{2,3},{3,2},{4,5},{5,4},{6,7},{7,6},{8,9},{9,8},{10,11... | collective-permute-start | bytes 221192 | tf_op jit(solution)/shard_map/ppermute | solution.py:329
  49.8 4.2 %collective-permute-start.17 = (s16[320,512]{1,0:T(8,128)(2,1)S(1)}, s16[320,512]{1,0:T(8,128)(2,1)S(1)}, u32[]{:S(2)}, u32[]{:S(2)}) collective-permute-start(s16[320,512]{1,0:T(8,128)(2,1)S(1)} %join_kernel.1.own_ref), channel_id=1, source_target_pairs={{0,4},{4,0},{8,12},{12,8},{16,20},{20,16},{24,28},{28,24},{1,5},{5... | collective-permute-start | bytes 983048 | tf_op jit(solution)/shard_map/ppermute | solution.py:329
  49.9 12.1 %collective-permute-start.18 = (s16[528,128]{1,0:T(8,128)(2,1)S(1)}, s16[528,128]{1,0:T(8,128)(2,1)S(1)}, u32[]{:S(2)}, u32[]{:S(2)}) collective-permute-start(s16[528,128]{1,0:T(8,128)(2,1)S(1)} %get-tuple-element.61), channel_id=1, source_target_pairs={{0,16},{4,20},{8,24},{12,28},{16,0},{20,4},{24,8},{28,12},{1,17},{... | collective-permute-start | bytes 405512 | tf_op jit(solution)/shard_map/ppermute | solution.py:329

commit v8 on v7

--- a/solution.py
+++ b/solution.py
@@ -319,7 +319,7 @@
         out_specs=jax.tree.map(lambda _: vmem, out_shape),
         scratch_shapes=scratch,
         input_output_aliases=aliases or {},
-        compiler_params=pltpu.CompilerParams(vmem_limit_bytes=28 << 20),
+        compiler_params=pltpu.CompilerParams(vmem_limit_bytes=12 << 20),
         cost_estimate=pl.CostEstimate(flops=0, bytes_accessed=int(micros * 3.69e6) + 1024, transcendentals=0),
     )(*args)
 

time: 63.5 us -> 63.5 us (level)
  no operation moved by 1% of the time
where the time goes in v8:
time: 63.5 us; the launch traced here: 63.3 us
  Pallas kernels  24.5 us (39%)
  starting transfers between devices  22.7 us (36%)
  waiting for transfers between devices  15.1 us (24%)
  between operations  0.83 us (1%)
    pallas_call x18, Pallas kernels, call(): pl.pallas_call(kernel, name=getattr(kernel, 'func', kernel).__name__, out...  24.5 us
    ppermute x19, starting transfers between devices, swap(): return lax.ppermute(x, axis, [(i, i ^ bit) for i in range(count)])  22.7 us
    ppermute x19, waiting for transfers between devices, swap(): return lax.ppermute(x, axis, [(i, i ^ bit) for i in range(count)])  15.1 us
  transfers between devices with their start and end apart: 19, of which 11 were waited for; matrix products, arithmetic and copies ran while one was open for 0% of the time, Pallas kernels for 32%

profile of v8, /device:TPU:0, one launch (start us, length us, event | category | flops | bytes accessed | tf_op | source)
XLA Modules:
  0.0 63.3 jit_solution(2683031714510764817)
XLA Ops:
  0.6 1.8 %turn_kernel.1 = (bf16[256,384]{1,0:T(8,128)(2,1)S(1)}, bf16[256,384]{1,0:T(8,128)(2,1)}) custom-call(bf16[384,512]{1,0:T(8,128)(2,1)} %bitcast.12), custom_call_target="tpu_custom_call" | custom-call | bytes 1024 | tf_op jit(solution)/shard_map/turn_kernel/pallas_call | solution.py:314
  2.5 3.0 %collective-permute-start.1 = (bf16[256,384]{1,0:T(8,128)(2,1)}, bf16[256,384]{1,0:T(8,128)(2,1)S(1)}, u32[]{:S(2)}, u32[]{:S(2)}) collective-permute-start(bf16[256,384]{1,0:T(8,128)(2,1)} %get-tuple-element.37.refs_1_), channel_id=1, source_target_pairs={{0,1},{1,0},{2,3},{3,2},{4,5},{5,4},{6,7},{7,6},{8,9},{9,8},{10,11... | collective-permute-start | bytes 589832 | tf_op jit(solution)/shard_map/ppermute | solution.py:329
  5.5 1.5 %collective-permute-start.2 = (bf16[256,384]{1,0:T(8,128)(2,1)S(1)}, bf16[256,384]{1,0:T(8,128)(2,1)}, u32[]{:S(2)}, u32[]{:S(2)}) collective-permute-start(bf16[256,384]{1,0:T(8,128)(2,1)S(1)} %get-tuple-element.36.refs_0_), channel_id=1, source_target_pairs={{0,2},{1,3},{2,0},{3,1},{4,6},{5,7},{6,4},{7,5},{8,10},{9,11},{10,... | collective-permute-start | bytes 589832 | tf_op jit(solution)/shard_map/ppermute | solution.py:329
  7.0 0.5 collective-permute-start
  7.5 0.0 collective-permute-start.3
  7.6 0.1 pad_add_fusion.1.place_ref
  7.7 3.2 %pick_kernel.1 = (bf16[1536,512]{1,0:T(8,128)(2,1)S(1)}, f32[8,512]{1,0:T(8,128)S(1)}, bf16[1024,512]{1,0:T(8,128)(2,1)S(1)}, s32[1,512]{1,0:T(1,128)S(1)}, f32[1,128]{1,0:T(1,128)S(1)}) custom-call(s32[2]{0:T(128)S(1)} %pad_add_fusion.1.place_ref, s32[1,512]{1,0:T(1,128)} %bitcast.13, f32[1,128]{1,0:T(1,128)} %bitcast.14, bf16[1536,1024]{1,0:T(8,128)(2,1)} %bitcast.9), custom_call_target="tpu_custom_call" | custom-call | bytes 1024 | tf_op jit(solution)/shard_map/pick_kernel/pallas_call | solution.py:314
  10.9 0.6 collective-permute-done.1.refs_3_
  11.4 2.0 %collective-permute-done.2.refs_4_ = bf16[256,384]{1,0:T(8,128)(2,1)} collective-permute-done((bf16[256,384]{1,0:T(8,128)(2,1)S(1)}, bf16[256,384]{1,0:T(8,128)(2,1)}, u32[]{:S(2)}, u32[]{:S(2)}) %collective-permute-start.2) | collective-permute-done | bytes 196640 | tf_op jit(solution)/shard_map/ppermute | solution.py:329
  13.4 0.1 collective-permute-start.4
  13.5 2.0 %collective-permute-start.5 = (bf16[256,384]{1,0:T(8,128)(2,1)S(1)}, bf16[256,384]{1,0:T(8,128)(2,1)S(1)}, u32[]{:S(2)}, u32[]{:S(2)}) collective-permute-start(bf16[256,384]{1,0:T(8,128)(2,1)S(1)} %collective-permute-done.1.refs_3_), channel_id=1, source_target_pairs={{0,2},{1,3},{2,0},{3,1},{4,6},{5,7},{6,4},{7,5},{8,10},{9,11},{10,... | collective-permute-start | bytes 589832 | tf_op jit(solution)/shard_map/ppermute | solution.py:329
  15.5 2.3 %rest_kernel.1.chosen_ref = bf16[1536,512]{1,0:T(8,128)(2,1)S(1)} custom-call(bf16[1536,512]{1,0:T(8,128)(2,1)S(1)} %get-tuple-element.34.chosen_in, bf16[1024,512]{1,0:T(8,128)(2,1)S(1)} %get-tuple-element.35.one_ref, bf16[1536,1024]{1,0:T(8,128)(2,1)} %bitcast.10), custom_call_target="tpu_custom_call", output_to_operand_aliasing={{}: (0, {})} | custom-call | bytes 1024 | tf_op jit(solution)/shard_map/rest_kernel/pallas_call | solution.py:314
  17.8 0.1 pad_add_fusion.place_ref
  17.8 0.0 collective-permute-done.refs_2_
  17.8 0.0 collective-permute-done.3.refs_5_
  17.9 2.3 %early_kernel.1 = (bf16[512,1536]{1,0:T(8,128)(2,1)S(1)}, f32[512,512]{1,0:T(8,128)S(1)}) custom-call(s32[4]{0:T(128)S(1)} %pad_add_fusion.place_ref, bf16[1536,512]{1,0:T(8,128)(2,1)S(1)} %rest_kernel.1.chosen_ref, bf16[256,384]{1,0:T(8,128)(2,1)S(1)} %get-tuple-element.36.refs_0_, bf16[256,384]{1,0:T(8,128)(2,1)} %get-tuple-element.37.refs_1_, ...), custom_call_target="tpu_custom_call" | custom-call | bytes 1024 | tf_op jit(solution)/shard_map/early_kernel/pallas_call | solution.py:314
  20.2 0.0 collective-permute-done.4.refs_0_
  20.2 0.1 collective-permute-done.5.refs_1_
  20.3 0.9 %send_kernel.1 = f32[264,512]{1,0:T(8,128)S(1)} custom-call(s32[4]{0:T(128)S(1)} %pad_add_fusion.place_ref, bf16[1536,512]{1,0:T(8,128)(2,1)S(1)} %rest_kernel.1.chosen_ref, f32[8,512]{1,0:T(8,128)S(1)} %get-tuple-element.40.entry_ref, f32[512,512]{1,0:T(8,128)S(1)} %get-tuple-element.39.terms_ref, bf16[256,384]{1,0:T(8,128)(2,1)S(1)} %collective-permute-done.4.refs_0_, ...), custom_call_target="tpu_custom_call" | custom-call | bytes 1024 | tf_op jit(solution)/shard_map/send_kernel/pallas_call | solution.py:314
  21.1 0.1 collective-permute-start.6
  21.2 0.0 copy-start
  21.2 0.9 %keep_kernel.1 = (bf16[512,1536]{1,0:T(8,128)(2,1)S(1)}, f32[256,512]{1,0:T(8,128)S(1)}) custom-call(s32[4]{0:T(128)S(1)} %pad_add_fusion.place_ref, bf16[512,1536]{1,0:T(8,128)(2,1)S(1)} %get-tuple-element.38.turned_in, bf16[1536,512]{1,0:T(8,128)(2,1)S(1)} %rest_kernel.1.chosen_ref, ...), custom_call_target="tpu_custom_call", output_to_operand_aliasing={{0}: (1, {})} | custom-call | bytes 1024 | tf_op jit(solution)/shard_map/keep_kernel/pallas_call | solution.py:314
  22.1 1.0 %collective-permute-done.6.got_ref = f32[264,512]{1,0:T(8,128)S(1)} collective-permute-done((f32[264,512]{1,0:T(8,128)S(1)}, f32[264,512]{1,0:T(8,128)S(1)}, u32[]{:S(2)}, u32[]{:S(2)}) %collective-permute-start.6) | collective-permute-done | bytes 540704 | tf_op jit(solution)/shard_map/ppermute | solution.py:329
  23.1 0.2 pair_kernel.1
  23.3 1.9 %collective-permute-start.7 = (s16[72,512]{1,0:T(8,128)(2,1)S(1)}, s16[72,512]{1,0:T(8,128)(2,1)S(1)}, u32[]{:S(2)}, u32[]{:S(2)}) collective-permute-start(s16[72,512]{1,0:T(8,128)(2,1)S(1)} %get-tuple-element.51), channel_id=1, source_target_pairs={{0,3},{1,2},{2,1},{3,0},{4,7},{5,6},{6,5},{7,4},{8,11},{9,10},{10,... | collective-permute-start | bytes 221192 | tf_op jit(solution)/shard_map/ppermute | solution.py:329
  25.2 1.1 %collective-permute-start.8 = (s16[72,512]{1,0:T(8,128)(2,1)S(1)}, s16[72,512]{1,0:T(8,128)(2,1)S(1)}, u32[]{:S(2)}, u32[]{:S(2)}) collective-permute-start(s16[72,512]{1,0:T(8,128)(2,1)S(1)} %get-tuple-element.52), channel_id=1, source_target_pairs={{0,2},{1,3},{2,0},{3,1},{4,6},{5,7},{6,4},{7,5},{8,10},{9,11},{10,... | collective-permute-start | bytes 221192 | tf_op jit(solution)/shard_map/ppermute | solution.py:329
  26.3 0.6 collective-permute-start.9
  26.9 0.0 copy-done
  26.9 2.4 %schur_kernel.1 = (f32[2048,128]{1,0:T(8,128)S(1)}, f32[2048,128]{1,0:T(8,128)S(1)}) custom-call(s32[4]{0:T(128)S(1)} %pad_add_fusion.place_ref, s32[1,512]{1,0:T(1,128)S(1)} %get-tuple-element.45.panel_ref, f32[1,128]{1,0:T(1,128)S(1)} %get-tuple-element.46.own_diagonal_ref, bf16[1536,1024]{1,0:T(8,128)(2,1)S(1)} %bitcast.11, ...), custom_call_target="tpu_custom_call" | custom-call | bytes 1024 | tf_op jit(solution)/shard_map/schur_kernel/pallas_call | solution.py:314
  29.2 0.0 collective-permute-done.7.refs_1_
  29.2 0.9 %collective-permute-done.8.refs_2_ = s16[72,512]{1,0:T(8,128)(2,1)S(1)} collective-permute-done((s16[72,512]{1,0:T(8,128)(2,1)S(1)}, s16[72,512]{1,0:T(8,128)(2,1)S(1)}, u32[]{:S(2)}, u32[]{:S(2)}) %collective-permute-start.8) | collective-permute-done | bytes 73760 | tf_op jit(solution)/shard_map/ppermute | solution.py:329
  30.2 0.5 collective-permute-done.9.refs_3_
  30.6 0.1 sum_kernel.3.refs_0_
  30.8 0.1 collective-permute-start.11
  30.8 1.6 %collective-permute-start.10 = (s16[72,512]{1,0:T(8,128)(2,1)S(1)}, s16[72,512]{1,0:T(8,128)(2,1)S(1)}, u32[]{:S(2)}, u32[]{:S(2)}) collective-permute-start(s16[72,512]{1,0:T(8,128)(2,1)S(1)} %sum_kernel.3.refs_0_), channel_id=1, source_target_pairs={{0,8},{4,12},{8,0},{12,4},{16,24},{20,28},{24,16},{28,20},{1,9},{5... | collective-permute-start | bytes 221192 | tf_op jit(solution)/shard_map/ppermute | solution.py:329
  32.5 3.0 %collective-permute-done.10.refs_1_ = s16[72,512]{1,0:T(8,128)(2,1)S(1)} collective-permute-done((s16[72,512]{1,0:T(8,128)(2,1)S(1)}, s16[72,512]{1,0:T(8,128)(2,1)S(1)}, u32[]{:S(2)}, u32[]{:S(2)}) %collective-permute-start.10) | collective-permute-done | bytes 73760 | tf_op jit(solution)/shard_map/ppermute | solution.py:329
  35.5 0.1 sum_kernel.4.refs_0_
  35.6 2.6 %collective-permute-start.12 = (s16[72,512]{1,0:T(8,128)(2,1)S(1)}, s16[72,512]{1,0:T(8,128)(2,1)S(1)}, u32[]{:S(2)}, u32[]{:S(2)}) collective-permute-start(s16[72,512]{1,0:T(8,128)(2,1)S(1)} %sum_kernel.4.refs_0_), channel_id=1, source_target_pairs={{0,16},{4,20},{8,24},{12,28},{16,0},{20,4},{24,8},{28,12},{1,17},{... | collective-permute-start | bytes 221192 | tf_op jit(solution)/shard_map/ppermute | solution.py:329
  38.3 0.0 collective-permute-done.11.got_ref
  38.3 0.2 bulk_pair_kernel.1
  38.5 3.7 %collective-permute-done.12.refs_1_ = s16[72,512]{1,0:T(8,128)(2,1)S(1)} collective-permute-done((s16[72,512]{1,0:T(8,128)(2,1)S(1)}, s16[72,512]{1,0:T(8,128)(2,1)S(1)}, u32[]{:S(2)}, u32[]{:S(2)}) %collective-permute-start.12) | collective-permute-done | bytes 73760 | tf_op jit(solution)/shard_map/ppermute | solution.py:329
  42.2 0.1 sum_kernel.5.refs_0_
  42.3 0.5 collective-permute-start.16
  42.8 1.6 %collective-permute-start.15 = (s16[72,512]{1,0:T(8,128)(2,1)S(1)}, s16[72,512]{1,0:T(8,128)(2,1)S(1)}, u32[]{:S(2)}, u32[]{:S(2)}) collective-permute-start(s16[72,512]{1,0:T(8,128)(2,1)S(1)} %sum_kernel.5.refs_0_), channel_id=1, source_target_pairs={{0,3},{1,2},{2,1},{3,0},{4,7},{5,6},{6,5},{7,4},{8,11},{9,10},{10,... | collective-permute-start | bytes 221192 | tf_op jit(solution)/shard_map/ppermute | solution.py:329
  44.4 0.9 %collective-permute-start.14 = (s16[72,512]{1,0:T(8,128)(2,1)S(1)}, s16[72,512]{1,0:T(8,128)(2,1)S(1)}, u32[]{:S(2)}, u32[]{:S(2)}) collective-permute-start(s16[72,512]{1,0:T(8,128)(2,1)S(1)} %sum_kernel.5.refs_0_), channel_id=1, source_target_pairs={{0,2},{1,3},{2,0},{3,1},{4,6},{5,7},{6,4},{7,5},{8,10},{9,11},{10,... | collective-permute-start | bytes 221192 | tf_op jit(solution)/shard_map/ppermute | solution.py:329
  45.3 1.1 %collective-permute-start.13 = (s16[72,512]{1,0:T(8,128)(2,1)S(1)}, s16[72,512]{1,0:T(8,128)(2,1)S(1)}, u32[]{:S(2)}, u32[]{:S(2)}) collective-permute-start(s16[72,512]{1,0:T(8,128)(2,1)S(1)} %sum_kernel.5.refs_0_), channel_id=1, source_target_pairs={{0,1},{1,0},{2,3},{3,2},{4,5},{5,4},{6,7},{7,6},{8,9},{9,8},{10,11... | collective-permute-start | bytes 221192 | tf_op jit(solution)/shard_map/ppermute | solution.py:329
  46.3 1.8 %collective-permute-done.15.refs_3_ = s16[72,512]{1,0:T(8,128)(2,1)S(1)} collective-permute-done((s16[72,512]{1,0:T(8,128)(2,1)S(1)}, s16[72,512]{1,0:T(8,128)(2,1)S(1)}, u32[]{:S(2)}, u32[]{:S(2)}) %collective-permute-start.15) | collective-permute-done | bytes 73760 | tf_op jit(solution)/shard_map/ppermute | solution.py:329
  48.1 0.8 %collective-permute-done.14.refs_2_ = s16[72,512]{1,0:T(8,128)(2,1)S(1)} collective-permute-done((s16[72,512]{1,0:T(8,128)(2,1)S(1)}, s16[72,512]{1,0:T(8,128)(2,1)S(1)}, u32[]{:S(2)}, u32[]{:S(2)}) %collective-permute-start.14) | collective-permute-done | bytes 73760 | tf_op jit(solution)/shard_map/ppermute | solution.py:329
  48.9 0.8 %collective-permute-done.13.refs_1_ = s16[72,512]{1,0:T(8,128)(2,1)S(1)} collective-permute-done((s16[72,512]{1,0:T(8,128)(2,1)S(1)}, s16[72,512]{1,0:T(8,128)(2,1)S(1)}, u32[]{:S(2)}, u32[]{:S(2)}) %collective-permute-start.13) | collective-permute-done | bytes 73760 | tf_op jit(solution)/shard_map/ppermute | solution.py:329
  49.7 0.0 collective-permute-done.16.got_ref
  49.7 0.2 bulk_sum_kernel.1
  49.8 0.1 collective-permute-start.17
  49.9 3.4 %collective-permute-start.18 = (s16[528,128]{1,0:T(8,128)(2,1)S(1)}, s16[528,128]{1,0:T(8,128)(2,1)S(1)}, u32[]{:S(2)}, u32[]{:S(2)}) collective-permute-start(s16[528,128]{1,0:T(8,128)(2,1)S(1)} %get-tuple-element.61), channel_id=1, source_target_pairs={{0,16},{4,20},{8,24},{12,28},{16,0},{20,4},{24,8},{28,12},{1,17},{... | collective-permute-start | bytes 405512 | tf_op jit(solution)/shard_map/ppermute | solution.py:329
  53.4 0.7 %own_kernel.1.half_ref = f32[256,512]{1,0:T(8,128)S(1)} custom-call(s32[4]{0:T(128)S(1)} %pad_add_fusion.place_ref, s16[320,512]{1,0:T(8,128)(2,1)S(1)} %join_kernel.1.own_ref), custom_call_target="tpu_custom_call" | custom-call | bytes 1024 | tf_op jit(solution)/shard_map/own_kernel/pallas_call | solution.py:314
  54.1 0.0 collective-permute-done.17.other_ref
  54.1 4.4 %first_kernel.1 = (f32[512,256]{1,0:T(8,128)S(1)}, f32[512,512]{1,0:T(8,128)S(1)}) custom-call(s32[4]{0:T(128)S(1)} %pad_add_fusion.place_ref, f32[256,512]{1,0:T(8,128)S(1)} %own_kernel.1.half_ref, s16[320,512]{1,0:T(8,128)(2,1)S(1)} %collective-permute-done.17.other_ref), custom_call_target="tpu_custom_call" | custom-call | bytes 16606024 | tf_op jit(solution)/shard_map/first_kernel/pallas_call | solution.py:314
  58.5 3.5 %second_kernel.1.inverse_second_ref = f32[256,512]{1,0:T(8,128)S(1)} custom-call(f32[512,512]{1,0:T(8,128)S(1)} %get-tuple-element.64.pivots_ref, f32[512,256]{1,0:T(8,128)S(1)} %get-tuple-element.63.inverse_first_ref), custom_call_target="tpu_custom_call" | custom-call | bytes 16606024 | tf_op jit(solution)/shard_map/second_kernel/pallas_call | solution.py:314
  62.1 0.0 collective-permute-done.18.refs_0_
  62.1 1.2 %factor_kernel.1 = (f32[128,1,256]{2,1,0:T(1,128)}, f32[128,1,256]{2,1,0:T(1,128)}) custom-call(f32[512,256]{1,0:T(8,128)S(1)} %get-tuple-element.63.inverse_first_ref, f32[256,512]{1,0:T(8,128)S(1)} %second_kernel.1.inverse_second_ref, f32[512,128]{1,0:T(8,128)S(1)} %get-tuple-element.65.rows_ref, s16[528,128]{1,0:T(8,128)(2,1)S(1)} %collective-permute-done.18.refs_0_), custom_call_target="tpu_custom_call" | custom-call | bytes 1024 | tf_op jit(solution)/shard_map/factor_kernel/pallas_call | solution.py:314
  (1 shorter events, 0.0 us)
Async XLA Ops:
  2.5 8.9 %collective-permute-start.1 = (bf16[256,384]{1,0:T(8,128)(2,1)}, bf16[256,384]{1,0:T(8,128)(2,1)S(1)}, u32[]{:S(2)}, u32[]{:S(2)}) collective-permute-start(bf16[256,384]{1,0:T(8,128)(2,1)} %get-tuple-element.37.refs_1_), channel_id=1, source_target_pairs={{0,1},{1,0},{2,3},{3,2},{4,5},{5,4},{6,7},{7,6},{8,9},{9,8},{10,11... | collective-permute-start | bytes 589832 | tf_op jit(solution)/shard_map/ppermute | solution.py:329
  5.5 7.9 %collective-permute-start.2 = (bf16[256,384]{1,0:T(8,128)(2,1)S(1)}, bf16[256,384]{1,0:T(8,128)(2,1)}, u32[]{:S(2)}, u32[]{:S(2)}) collective-permute-start(bf16[256,384]{1,0:T(8,128)(2,1)S(1)} %get-tuple-element.36.refs_0_), channel_id=1, source_target_pairs={{0,2},{1,3},{2,0},{3,1},{4,6},{5,7},{6,4},{7,5},{8,10},{9,11},{10,... | collective-permute-start | bytes 589832 | tf_op jit(solution)/shard_map/ppermute | solution.py:329
  7.0 10.9 %collective-permute-start = (bf16[256,384]{1,0:T(8,128)(2,1)S(1)}, bf16[256,384]{1,0:T(8,128)(2,1)}, u32[]{:S(2)}, u32[]{:S(2)}) collective-permute-start(bf16[256,384]{1,0:T(8,128)(2,1)S(1)} %get-tuple-element.36.refs_0_), channel_id=1, source_target_pairs={{0,1},{1,0},{2,3},{3,2},{4,5},{5,4},{6,7},{7,6},{8,9},{9,8},{10,11... | collective-permute-start | bytes 589832 | tf_op jit(solution)/shard_map/ppermute | solution.py:329
  7.5 10.3 %collective-permute-start.3 = (bf16[256,384]{1,0:T(8,128)(2,1)}, bf16[256,384]{1,0:T(8,128)(2,1)}, u32[]{:S(2)}, u32[]{:S(2)}) collective-permute-start(bf16[256,384]{1,0:T(8,128)(2,1)} %get-tuple-element.37.refs_1_), channel_id=1, source_target_pairs={{0,2},{1,3},{2,0},{3,1},{4,6},{5,7},{6,4},{7,5},{8,10},{9,11},{10,... | collective-permute-start | bytes 589832 | tf_op jit(solution)/shard_map/ppermute | solution.py:329
  13.4 6.8 %collective-permute-start.4 = (bf16[256,384]{1,0:T(8,128)(2,1)}, bf16[256,384]{1,0:T(8,128)(2,1)S(1)}, u32[]{:S(2)}, u32[]{:S(2)}) collective-permute-start(bf16[256,384]{1,0:T(8,128)(2,1)} %collective-permute-done.2.refs_4_), channel_id=1, source_target_pairs={{0,1},{1,0},{2,3},{3,2},{4,5},{5,4},{6,7},{7,6},{8,9},{9,8},{10,11... | collective-permute-start | bytes 589832 | tf_op jit(solution)/shard_map/ppermute | solution.py:329
  13.5 6.8 %collective-permute-start.5 = (bf16[256,384]{1,0:T(8,128)(2,1)S(1)}, bf16[256,384]{1,0:T(8,128)(2,1)S(1)}, u32[]{:S(2)}, u32[]{:S(2)}) collective-permute-start(bf16[256,384]{1,0:T(8,128)(2,1)S(1)} %collective-permute-done.1.refs_3_), channel_id=1, source_target_pairs={{0,2},{1,3},{2,0},{3,1},{4,6},{5,7},{6,4},{7,5},{8,10},{9,11},{10,... | collective-permute-start | bytes 589832 | tf_op jit(solution)/shard_map/ppermute | solution.py:329
  21.1 2.0 %collective-permute-start.6 = (f32[264,512]{1,0:T(8,128)S(1)}, f32[264,512]{1,0:T(8,128)S(1)}, u32[]{:S(2)}, u32[]{:S(2)}) collective-permute-start(f32[264,512]{1,0:T(8,128)S(1)} %send_kernel.1), channel_id=1, source_target_pairs={{0,4},{4,0},{8,12},{12,8},{16,20},{20,16},{24,28},{28,24},{1,5},{5... | collective-permute-start | bytes 1622024 | tf_op jit(solution)/shard_map/ppermute | solution.py:329
  21.2 5.6 %copy-start = (bf16[1,1536,1024]{2,1,0:T(8,128)(2,1)S(1)}, bf16[1,1536,1024]{2,1,0:T(8,128)(2,1)}, u32[]{:S(2)}) copy-start(bf16[1,1536,1024]{2,1,0:T(8,128)(2,1)} %param.4) | copy-start | bytes 9437188
  23.3 5.9 %collective-permute-start.7 = (s16[72,512]{1,0:T(8,128)(2,1)S(1)}, s16[72,512]{1,0:T(8,128)(2,1)S(1)}, u32[]{:S(2)}, u32[]{:S(2)}) collective-permute-start(s16[72,512]{1,0:T(8,128)(2,1)S(1)} %get-tuple-element.51), channel_id=1, source_target_pairs={{0,3},{1,2},{2,1},{3,0},{4,7},{5,6},{6,5},{7,4},{8,11},{9,10},{10,... | collective-permute-start | bytes 221192 | tf_op jit(solution)/shard_map/ppermute | solution.py:329
  25.2 5.0 %collective-permute-start.8 = (s16[72,512]{1,0:T(8,128)(2,1)S(1)}, s16[72,512]{1,0:T(8,128)(2,1)S(1)}, u32[]{:S(2)}, u32[]{:S(2)}) collective-permute-start(s16[72,512]{1,0:T(8,128)(2,1)S(1)} %get-tuple-element.52), channel_id=1, source_target_pairs={{0,2},{1,3},{2,0},{3,1},{4,6},{5,7},{6,4},{7,5},{8,10},{9,11},{10,... | collective-permute-start | bytes 221192 | tf_op jit(solution)/shard_map/ppermute | solution.py:329
  26.3 4.4 %collective-permute-start.9 = (s16[72,512]{1,0:T(8,128)(2,1)S(1)}, s16[72,512]{1,0:T(8,128)(2,1)S(1)}, u32[]{:S(2)}, u32[]{:S(2)}) collective-permute-start(s16[72,512]{1,0:T(8,128)(2,1)S(1)} %get-tuple-element.53), channel_id=1, source_target_pairs={{0,1},{1,0},{2,3},{3,2},{4,5},{5,4},{6,7},{7,6},{8,9},{9,8},{10,11... | collective-permute-start | bytes 221192 | tf_op jit(solution)/shard_map/ppermute | solution.py:329
  30.8 7.5 %collective-permute-start.11 = (f32[2048,128]{1,0:T(8,128)S(1)}, f32[2048,128]{1,0:T(8,128)S(1)}, u32[]{:S(2)}, u32[]{:S(2)}) collective-permute-start(f32[2048,128]{1,0:T(8,128)S(1)} %get-tuple-element.56), channel_id=1, source_target_pairs={{0,4},{4,0},{8,12},{12,8},{16,20},{20,16},{24,28},{28,24},{1,5},{5... | collective-permute-start | bytes 3145736 | tf_op jit(solution)/shard_map/ppermute | solution.py:329
  30.8 4.7 %collective-permute-start.10 = (s16[72,512]{1,0:T(8,128)(2,1)S(1)}, s16[72,512]{1,0:T(8,128)(2,1)S(1)}, u32[]{:S(2)}, u32[]{:S(2)}) collective-permute-start(s16[72,512]{1,0:T(8,128)(2,1)S(1)} %sum_kernel.3.refs_0_), channel_id=1, source_target_pairs={{0,8},{4,12},{8,0},{12,4},{16,24},{20,28},{24,16},{28,20},{1,9},{5... | collective-permute-start | bytes 221192 | tf_op jit(solution)/shard_map/ppermute | solution.py:329
  35.6 6.6 %collective-permute-start.12 = (s16[72,512]{1,0:T(8,128)(2,1)S(1)}, s16[72,512]{1,0:T(8,128)(2,1)S(1)}, u32[]{:S(2)}, u32[]{:S(2)}) collective-permute-start(s16[72,512]{1,0:T(8,128)(2,1)S(1)} %sum_kernel.4.refs_0_), channel_id=1, source_target_pairs={{0,16},{4,20},{8,24},{12,28},{16,0},{20,4},{24,8},{28,12},{1,17},{... | collective-permute-start | bytes 221192 | tf_op jit(solution)/shard_map/ppermute | solution.py:329
  42.3 7.3 %collective-permute-start.16 = (s16[1056,128]{1,0:T(8,128)(2,1)S(1)}, s16[1056,128]{1,0:T(8,128)(2,1)S(1)}, u32[]{:S(2)}, u32[]{:S(2)}) collective-permute-start(s16[1056,128]{1,0:T(8,128)(2,1)S(1)} %get-tuple-element.60), channel_id=1, source_target_pairs={{0,8},{4,12},{8,0},{12,4},{16,24},{20,28},{24,16},{28,20},{1,9},{5... | collective-permute-start | bytes 811016 | tf_op jit(solution)/shard_map/ppermute | solution.py:329
  42.8 5.3 %collective-permute-start.15 = (s16[72,512]{1,0:T(8,128)(2,1)S(1)}, s16[72,512]{1,0:T(8,128)(2,1)S(1)}, u32[]{:S(2)}, u32[]{:S(2)}) collective-permute-start(s16[72,512]{1,0:T(8,128)(2,1)S(1)} %sum_kernel.5.refs_0_), channel_id=1, source_target_pairs={{0,3},{1,2},{2,1},{3,0},{4,7},{5,6},{6,5},{7,4},{8,11},{9,10},{10,... | collective-permute-start | bytes 221192 | tf_op jit(solution)/shard_map/ppermute | solution.py:329
  44.4 4.5 %collective-permute-start.14 = (s16[72,512]{1,0:T(8,128)(2,1)S(1)}, s16[72,512]{1,0:T(8,128)(2,1)S(1)}, u32[]{:S(2)}, u32[]{:S(2)}) collective-permute-start(s16[72,512]{1,0:T(8,128)(2,1)S(1)} %sum_kernel.5.refs_0_), channel_id=1, source_target_pairs={{0,2},{1,3},{2,0},{3,1},{4,6},{5,7},{6,4},{7,5},{8,10},{9,11},{10,... | collective-permute-start | bytes 221192 | tf_op jit(solution)/shard_map/ppermute | solution.py:329
  45.3 4.4 %collective-permute-start.13 = (s16[72,512]{1,0:T(8,128)(2,1)S(1)}, s16[72,512]{1,0:T(8,128)(2,1)S(1)}, u32[]{:S(2)}, u32[]{:S(2)}) collective-permute-start(s16[72,512]{1,0:T(8,128)(2,1)S(1)} %sum_kernel.5.refs_0_), channel_id=1, source_target_pairs={{0,1},{1,0},{2,3},{3,2},{4,5},{5,4},{6,7},{7,6},{8,9},{9,8},{10,11... | collective-permute-start | bytes 221192 | tf_op jit(solution)/shard_map/ppermute | solution.py:329
  49.8 4.2 %collective-permute-start.17 = (s16[320,512]{1,0:T(8,128)(2,1)S(1)}, s16[320,512]{1,0:T(8,128)(2,1)S(1)}, u32[]{:S(2)}, u32[]{:S(2)}) collective-permute-start(s16[320,512]{1,0:T(8,128)(2,1)S(1)} %join_kernel.1.own_ref), channel_id=1, source_target_pairs={{0,4},{4,0},{8,12},{12,8},{16,20},{20,16},{24,28},{28,24},{1,5},{5... | collective-permute-start | bytes 983048 | tf_op jit(solution)/shard_map/ppermute | solution.py:329
  49.9 12.1 %collective-permute-start.18 = (s16[528,128]{1,0:T(8,128)(2,1)S(1)}, s16[528,128]{1,0:T(8,128)(2,1)S(1)}, u32[]{:S(2)}, u32[]{:S(2)}) collective-permute-start(s16[528,128]{1,0:T(8,128)(2,1)S(1)} %get-tuple-element.61), channel_id=1, source_target_pairs={{0,16},{4,20},{8,24},{12,28},{16,0},{20,4},{24,8},{28,12},{1,17},{... | collective-permute-start | bytes 405512 | tf_op jit(solution)/shard_map/ppermute | solution.py:329

commit v9 on v8

--- a/solution.py
+++ b/solution.py
@@ -70,6 +70,11 @@
     both = product(approx, jnp.concatenate([pivot, beside], axis=1))
     stacked = jnp.concatenate([approx, both[:, count:]], axis=1)
     return 2.0 * stacked - product(both[:, :count], stacked)
+
+
+def whereabouts():
+    place = lax.axis_index("scen")
+    return lax.axis_index("row"), lax.rem(place, 2), lax.div(place, 2)
 
 
 def aligned(index, size):
@@ -130,7 +135,7 @@
 
 
 def pick_kernel(
-    place_ref, panel_ref, own_diagonal_ref, coupling_ref,
+    panel_ref, own_diagonal_ref, coupling_ref,
     chosen_ref, entry_ref, one_ref, panel_out, diagonal_out, coupling_copy, small_done, done,
 ):
     small = [
@@ -142,9 +147,10 @@
     copies = fetch(coupling_ref, coupling_copy, done, 0)
     for copy in small:
         copy.wait()
-    first_column, first_row = place_ref[0], place_ref[1]
     columns, panel = one_ref.shape
     share = diagonal_out.shape[1]
+    first_column = lax.axis_index("row") * columns
+    first_row = first_column + lax.axis_index("scen") * share
     here = panel_out[...] - first_column == lax.broadcasted_iota(jnp.int32, (columns, panel), 0)
     one_ref[...] = jnp.where(here, F32(1.0), F32(0.0)).astype(BF16)
     owned = panel_out[...] - first_row == lax.broadcasted_iota(jnp.int32, (share, panel), 0)
@@ -160,45 +166,48 @@
     choose(copies, coupling_copy, one_ref, chosen_ref, first)
 
 
-def early_kernel(place_ref, chosen_ref, *refs):
+def early_kernel(chosen_ref, *refs):
     *pieces, turned_ref, terms_ref = refs
+    row, _, _ = whereabouts()
     if len(pieces) == 1:
         turned_ref[...] = pieces[0][...]
     else:
         half, width = pieces[0].shape
         for i, piece in enumerate(pieces):
-            start = aligned(place_ref[0] ^ (i // 2), width)
+            start = aligned(row ^ (i // 2), width)
             turned_ref[i % 2 * half:(i % 2 + 1) * half, pl.ds(start, width)] = piece[...]
-        start = aligned(place_ref[0] ^ (len(pieces) // 2), width)
+        start = aligned(row ^ (len(pieces) // 2), width)
         turned_ref[:, pl.ds(start, width)] = jnp.zeros((2 * half, width), BF16)
     terms_ref[...] = dot(turned_ref[...], chosen_ref[...])
 
 
-def half_terms(rows, place_ref, chosen_ref, terms_ref, far, whose, out_ref, all_ref):
+def half_terms(rows, row, chosen_ref, terms_ref, far, whose, out_ref, all_ref):
     half = all_ref.shape[0]
     size = half // rows
     total = terms_ref[pl.ds(aligned(whose, half), half), :]
     if far:
         width = far[0].shape[1]
         block = jnp.where(whose == 0, far[0][...], far[1][...])
-        total = total + dot(block, chosen_ref[pl.ds(aligned(place_ref[0] ^ (rows - 1), width), width), :])
+        total = total + dot(block, chosen_ref[pl.ds(aligned(row ^ (rows - 1), width), width), :])
     all_ref[...] = total
     for k in range(rows):
-        out_ref[k * size:(k + 1) * size, :] = all_ref[pl.ds(aligned(place_ref[0] ^ k, size), size), :]
-
-
-def send_kernel(rows, place_ref, chosen_ref, entry_ref, terms_ref, *refs):
+        out_ref[k * size:(k + 1) * size, :] = all_ref[pl.ds(aligned(row ^ k, size), size), :]
+
+
+def send_kernel(rows, chosen_ref, entry_ref, terms_ref, *refs):
     *far, send_ref, all_ref = refs
-    half_terms(rows, place_ref, chosen_ref, terms_ref, far, 1 - place_ref[1], send_ref, all_ref)
+    row, core, _ = whereabouts()
+    half_terms(rows, row, chosen_ref, terms_ref, far, 1 - core, send_ref, all_ref)
     send_ref[all_ref.shape[0]:, :] = entry_ref[...]
 
 
-def keep_kernel(rows, place_ref, turned_in, chosen_ref, terms_ref, *refs):
+def keep_kernel(rows, turned_in, chosen_ref, terms_ref, *refs):
     *far, turned_ref, keep_ref, all_ref = refs
-    half_terms(rows, place_ref, chosen_ref, terms_ref, far, place_ref[1], keep_ref, all_ref)
+    row, core, _ = whereabouts()
+    half_terms(rows, row, chosen_ref, terms_ref, far, core, keep_ref, all_ref)
     for i, piece in enumerate(far):
         half, width = piece.shape
-        start = aligned(place_ref[0] ^ (rows - 1), width)
+        start = aligned(row ^ (rows - 1), width)
         turned_ref[i * half:(i + 1) * half, pl.ds(start, width)] = piece[...]
 
 
@@ -238,12 +247,13 @@
         pivots_ref[pl.ds(start - base, size), :] = values + jnp.where(at, diagonal, F32(0.0))
 
 
-def own_kernel(rows, place_ref, own_ref, half_ref):
-    place_pieces(place_ref[0], place_ref[1], own_ref, half_ref, rows, place_ref[1] * half_ref.shape[0])
-
-
-def first_kernel(rows, place_ref, half_ref, other_ref, inverse_ref, pivots_ref):
-    row, core = place_ref[0], place_ref[1]
+def own_kernel(rows, own_ref, half_ref):
+    row, core, _ = whereabouts()
+    place_pieces(row, core, own_ref, half_ref, rows, core * half_ref.shape[0])
+
+
+def first_kernel(rows, half_ref, other_ref, inverse_ref, pivots_ref):
+    row, core, _ = whereabouts()
     half = half_ref.shape[0]
     pivots_ref[pl.ds(aligned(core, half), half), :] = half_ref[...]
     place_pieces(row, 1 - core, other_ref, pivots_ref, rows, 0)
@@ -257,9 +267,10 @@
     inverse_ref[...] = newton_beside(pivot, -below)
 
 
-def schur_kernel(place_ref, panel_ref, own_diagonal_ref, coupling_ref, turned_ref, keep_ref, send_ref):
-    core, layer = place_ref[1], place_ref[2]
+def schur_kernel(panel_ref, own_diagonal_ref, coupling_ref, turned_ref, keep_ref, send_ref):
+    row, core, layer = whereabouts()
     panel, share = turned_ref.shape[0], keep_ref.shape[1]
+    first_row = row * coupling_ref.shape[1] + (2 * layer + core) * share
     layers = keep_ref.shape[0] // panel
     for position, k in enumerate(reversed_order(layers)):
         start = aligned(layer ^ k, 2 * share)
@@ -269,7 +280,7 @@
         kept = jnp.where(core == 0, one, two)
         if position == 0:
             wanted = jnp.broadcast_to(panel_ref[...].astype(F32), (share, panel)).T.astype(jnp.int32)
-            here = wanted - place_ref[3] == lax.broadcasted_iota(jnp.int32, (panel, share), 1)
+            here = wanted - first_row == lax.broadcasted_iota(jnp.int32, (panel, share), 1)
             kept = kept + jnp.where(here, own_diagonal_ref[...], F32(0.0))
         keep_ref[rows, :] = kept
         send_ref[rows, :] = jnp.where(core == 0, two, one)
@@ -305,17 +316,16 @@
     second_out[...] = product(inverse_second_ref[...], jnp.concatenate([second, first], axis=0)).T[:, None, :]
 
 
-def call(kernel, out_shape, *args, scratch=(), scalars=0, remain=0, micros=0.0, aliases=None):
+def call(kernel, out_shape, *args, scratch=(), remain=0, micros=0.0, aliases=None):
     hbm = pl.BlockSpec(memory_space=pltpu.HBM)
     vmem = pl.BlockSpec(memory_space=pltpu.VMEM)
-    smem = pl.BlockSpec(memory_space=pltpu.SMEM)
     stay = len(args) - remain
     args = args[:stay] + tuple(pltpu.with_memory_space_constraint(x, pltpu.HBM) for x in args[stay:])
     return pl.pallas_call(
         kernel,
         name=getattr(kernel, "func", kernel).__name__,
         out_shape=out_shape,
-        in_specs=[smem] * scalars + [vmem] * (len(args) - scalars - remain) + [hbm] * remain,
+        in_specs=[vmem] * (len(args) - remain) + [hbm] * remain,
         out_specs=jax.tree.map(lambda _: vmem, out_shape),
         scratch_shapes=scratch,
         input_output_aliases=aliases or {},
@@ -370,9 +380,6 @@
     shape = pltpu.VMEM
     panel_row, diagonal_row = panel_rows[None, :], border_diagonal.T
     first_row = row * row_count + place * share
-    starts = jnp.stack([row * row_count, first_row]).astype(jnp.int32)
-    at = jnp.stack([row, place % 2, place // 2, first_row]).astype(jnp.int32)
-
     picked = shape((local, panel), BF16)
     chunk_room = [
         pltpu.VMEM((CHUNKS // 2, local // CHUNKS, row_count), BF16), pltpu.SemaphoreType.DMA((CHUNKS // 2,))
@@ -383,7 +390,7 @@
             picked, shape((8, panel), F32), shape((row_count, panel), BF16),
             shape((1, panel), jnp.int32), shape((1, share), F32),
         ),
-        starts, panel_row, diagonal_row, coupling, scalars=1, remain=3,
+        panel_row, diagonal_row, coupling, remain=3,
         scratch=[chunk_room[0], pltpu.SemaphoreType.DMA((2,)), chunk_room[1]],
     )
     pieces = gather_pieces(solves, rows, (entry,))
@@ -391,15 +398,15 @@
     chosen = call(rest_kernel, picked, chosen, one, coupling, remain=1, scratch=chunk_room, aliases={0: 0})
     room = [pltpu.VMEM((panel // 2, panel), F32)]
     turned, terms = call(
-        early_kernel, (shape((panel, local), BF16), shape((panel, panel), F32)), at, chosen, *near, scalars=1
+        early_kernel, (shape((panel, local), BF16), shape((panel, panel), F32)), chosen, *near
     )
     send = call(
         functools.partial(send_kernel, rows), shape((panel // 2 + 8, panel), F32),
-        at, chosen, entry, terms, *far, scalars=1, scratch=room,
+        chosen, entry, terms, *far, scratch=room,
     )
     turned, keep = call(
         functools.partial(keep_kernel, rows), (shape((panel, local), BF16), shape((panel // 2, panel), F32)),
-        at, turned, chosen, terms, *far, scalars=1, scratch=room, aliases={1: 0},
+        turned, chosen, terms, *far, scratch=room, aliases={0: 0},
     )
     coded = shape((size + SHORT, panel), I16)
     codes = call(
@@ -414,7 +421,7 @@
         bulk = shape((layers * panel, share), F32)
         halved = lambda count: (shape((count * panel, share), F32), shape((count * (panel + TAIL), share), I16))
         own, send_rows = call(
-            schur_kernel, (bulk, bulk), at, panel_row, diagonal_row, coupling, after(turned, part), scalars=1
+            schur_kernel, (bulk, bulk), panel_row, diagonal_row, coupling, after(turned, part)
         )
         part = call(sum_kernel, coded, after(part, own), *arrived)
         got = swap(after(send_rows, part), "scen", 1)
@@ -441,11 +448,11 @@
         joined = after(joined, bulk_codes)
     other = swap(joined, "scen", 1)
     own_half = call(
-        functools.partial(own_kernel, rows), shape((panel // 2, panel), F32), at, joined, scalars=1
+        functools.partial(own_kernel, rows), shape((panel // 2, panel), F32), joined
     )
     inverse_first, pivots = call(
         functools.partial(first_kernel, rows), (shape((panel, half), F32), shape((panel, panel), F32)),
-        at, own_half, other, scalars=1, micros=4.5,
+        own_half, other, micros=4.5,
     )
     inverse_second = call(second_kernel, shape((half, panel), F32), pivots, inverse_first, micros=4.5)
     out = jax.ShapeDtypeStruct((share, 1, half), F32)

time: 63.5 us -> 60.8 us (0.957)
  Pallas kernels: 24.5 us -> 19.4 us
  waiting for transfers between devices: 15.1 us -> 17.7 us
    pallas_call x18, Pallas kernels: 24.5 us -> 19.4 us  [call(): pl.pallas_call(kernel, name=getattr(kernel, 'func', kernel).__name__, out...]
    ppermute x19, waiting for transfers between devices: 15.1 us -> 17.7 us  [swap(): return lax.ppermute(x, axis, [(i, i ^ bit) for i in range(count)])]
  transfers between devices with their start and end apart: 19 -> 19, of which waited for: 11 -> 12; matrix products, arithmetic and copies ran while one was open for 0% -> 0% of each run, Pallas kernels for 32% -> 27%
where the time goes in v9:
time: 60.8 us; the launch traced here: 60.6 us
  starting transfers between devices  22.7 us (37%)
  Pallas kernels  19.4 us (32%)
  waiting for transfers between devices  17.7 us (29%)
  between operations  0.83 us (1%)
    ppermute x19, starting transfers between devices, swap(): return lax.ppermute(x, axis, [(i, i ^ bit) for i in range(count)])  22.7 us
    pallas_call x18, Pallas kernels, call(): pl.pallas_call(kernel, name=getattr(kernel, 'func', kernel).__name__, out...  19.4 us
    ppermute x19, waiting for transfers between devices, swap(): return lax.ppermute(x, axis, [(i, i ^ bit) for i in range(count)])  17.7 us
  transfers between devices with their start and end apart: 19, of which 12 were waited for; matrix products, arithmetic and copies ran while one was open for 0% of the time, Pallas kernels for 27%

profile of v9, /device:TPU:0, one launch (start us, length us, event | category | flops | bytes accessed | tf_op | source)
XLA Modules:
  0.0 60.6 jit_solution(2619970672104493168)
XLA Ops:
  0.6 1.2 %turn_kernel.1 = (bf16[256,384]{1,0:T(8,128)(2,1)S(1)}, bf16[256,384]{1,0:T(8,128)(2,1)S(1)}) custom-call(bf16[384,512]{1,0:T(8,128)(2,1)} %bitcast.7), custom_call_target="tpu_custom_call" | custom-call | bytes 1024 | tf_op jit(solution)/shard_map/turn_kernel/pallas_call | solution.py:324
  1.8 3.0 %collective-permute-start.1 = (bf16[256,384]{1,0:T(8,128)(2,1)S(1)}, bf16[256,384]{1,0:T(8,128)(2,1)S(1)}, u32[]{:S(2)}, u32[]{:S(2)}) collective-permute-start(bf16[256,384]{1,0:T(8,128)(2,1)S(1)} %get-tuple-element.37.refs_1_), channel_id=1, source_target_pairs={{0,1},{1,0},{2,3},{3,2},{4,5},{5,4},{6,7},{7,6},{8,9},{9,8},{10,11... | collective-permute-start | bytes 589832 | tf_op jit(solution)/shard_map/ppermute | solution.py:339
  4.8 1.5 %collective-permute-start.2 = (bf16[256,384]{1,0:T(8,128)(2,1)S(1)}, bf16[256,384]{1,0:T(8,128)(2,1)S(1)}, u32[]{:S(2)}, u32[]{:S(2)}) collective-permute-start(bf16[256,384]{1,0:T(8,128)(2,1)S(1)} %get-tuple-element.36.refs_0_), channel_id=1, source_target_pairs={{0,2},{1,3},{2,0},{3,1},{4,6},{5,7},{6,4},{7,5},{8,10},{9,11},{10,... | collective-permute-start | bytes 589832 | tf_op jit(solution)/shard_map/ppermute | solution.py:339
  6.3 0.5 collective-permute-start
  6.9 0.1 collective-permute-start.3
  6.9 2.6 %pick_kernel.1 = (bf16[1536,512]{1,0:T(8,128)(2,1)S(1)}, f32[8,512]{1,0:T(8,128)S(1)}, bf16[1024,512]{1,0:T(8,128)(2,1)S(1)}, s32[1,512]{1,0:T(1,128)S(1)}, f32[1,128]{1,0:T(1,128)S(1)}) custom-call(s32[1,512]{1,0:T(1,128)} %bitcast.8, f32[1,128]{1,0:T(1,128)} %bitcast.9, bf16[1536,1024]{1,0:T(8,128)(2,1)} %bitcast.4), custom_call_target="tpu_custom_call" | custom-call | bytes 1024 | tf_op jit(solution)/shard_map/pick_kernel/pallas_call | solution.py:324
  9.6 1.0 %collective-permute-done.1.refs_3_ = bf16[256,384]{1,0:T(8,128)(2,1)S(1)} collective-permute-done((bf16[256,384]{1,0:T(8,128)(2,1)S(1)}, bf16[256,384]{1,0:T(8,128)(2,1)S(1)}, u32[]{:S(2)}, u32[]{:S(2)}) %collective-permute-start.1) | collective-permute-done | bytes 196640 | tf_op jit(solution)/shard_map/ppermute | solution.py:339
  10.5 2.1 %collective-permute-done.2.refs_4_ = bf16[256,384]{1,0:T(8,128)(2,1)S(1)} collective-permute-done((bf16[256,384]{1,0:T(8,128)(2,1)S(1)}, bf16[256,384]{1,0:T(8,128)(2,1)S(1)}, u32[]{:S(2)}, u32[]{:S(2)}) %collective-permute-start.2) | collective-permute-done | bytes 196640 | tf_op jit(solution)/shard_map/ppermute | solution.py:339
  12.6 0.0 collective-permute-start.4
  12.7 2.0 %collective-permute-start.5 = (bf16[256,384]{1,0:T(8,128)(2,1)S(1)}, bf16[256,384]{1,0:T(8,128)(2,1)S(1)}, u32[]{:S(2)}, u32[]{:S(2)}) collective-permute-start(bf16[256,384]{1,0:T(8,128)(2,1)S(1)} %collective-permute-done.1.refs_3_), channel_id=1, source_target_pairs={{0,2},{1,3},{2,0},{3,1},{4,6},{5,7},{6,4},{7,5},{8,10},{9,11},{10,... | collective-permute-start | bytes 589832 | tf_op jit(solution)/shard_map/ppermute | solution.py:339
  14.7 2.3 %rest_kernel.1.chosen_ref = bf16[1536,512]{1,0:T(8,128)(2,1)S(1)} custom-call(bf16[1536,512]{1,0:T(8,128)(2,1)S(1)} %get-tuple-element.34.chosen_in, bf16[1024,512]{1,0:T(8,128)(2,1)S(1)} %get-tuple-element.35.one_ref, bf16[1536,1024]{1,0:T(8,128)(2,1)} %bitcast.5), custom_call_target="tpu_custom_call", output_to_operand_aliasing={{}: (0, {})} | custom-call | bytes 1024 | tf_op jit(solution)/shard_map/rest_kernel/pallas_call | solution.py:324
  17.0 0.0 collective-permute-done.refs_2_
  17.0 0.0 collective-permute-done.3.refs_5_
  17.0 1.1 %early_kernel.1 = (bf16[512,1536]{1,0:T(8,128)(2,1)S(1)}, f32[512,512]{1,0:T(8,128)S(1)}) custom-call(bf16[1536,512]{1,0:T(8,128)(2,1)S(1)} %rest_kernel.1.chosen_ref, bf16[256,384]{1,0:T(8,128)(2,1)S(1)} %get-tuple-element.36.refs_0_, bf16[256,384]{1,0:T(8,128)(2,1)S(1)} %get-tuple-element.37.refs_1_, bf16[256,384]{1,0:T(8,128)(2,1)S(1)} %collective-permute-done.refs_2_, ...), custom_call_target="tpu_custom_call" | custom-call | bytes 1024 | tf_op jit(solution)/shard_map/early_kernel/pallas_call | solution.py:324
  18.1 0.2 collective-permute-done.4.refs_0_
  18.3 1.3 %collective-permute-done.5.refs_1_ = bf16[256,384]{1,0:T(8,128)(2,1)S(1)} collective-permute-done((bf16[256,384]{1,0:T(8,128)(2,1)S(1)}, bf16[256,384]{1,0:T(8,128)(2,1)S(1)}, u32[]{:S(2)}, u32[]{:S(2)}) %collective-permute-start.5) | collective-permute-done | bytes 196640 | tf_op jit(solution)/shard_map/ppermute | solution.py:339
  19.6 0.3 send_kernel.1
  19.9 0.1 collective-permute-start.6
  20.0 0.0 copy-start
  20.0 0.4 keep_kernel.1
  20.4 1.5 %collective-permute-done.6.got_ref = f32[264,512]{1,0:T(8,128)S(1)} collective-permute-done((f32[264,512]{1,0:T(8,128)S(1)}, f32[264,512]{1,0:T(8,128)S(1)}, u32[]{:S(2)}, u32[]{:S(2)}) %collective-permute-start.6) | collective-permute-done | bytes 540704 | tf_op jit(solution)/shard_map/ppermute | solution.py:339
  21.9 0.2 pair_kernel.1
  22.1 1.8 %collective-permute-start.7 = (s16[72,512]{1,0:T(8,128)(2,1)S(1)}, s16[72,512]{1,0:T(8,128)(2,1)S(1)}, u32[]{:S(2)}, u32[]{:S(2)}) collective-permute-start(s16[72,512]{1,0:T(8,128)(2,1)S(1)} %get-tuple-element.51), channel_id=1, source_target_pairs={{0,3},{1,2},{2,1},{3,0},{4,7},{5,6},{6,5},{7,4},{8,11},{9,10},{10,... | collective-permute-start | bytes 221192 | tf_op jit(solution)/shard_map/ppermute | solution.py:339
  23.9 0.5 collective-permute-start.8
  24.4 1.3 %collective-permute-start.9 = (s16[72,512]{1,0:T(8,128)(2,1)S(1)}, s16[72,512]{1,0:T(8,128)(2,1)S(1)}, u32[]{:S(2)}, u32[]{:S(2)}) collective-permute-start(s16[72,512]{1,0:T(8,128)(2,1)S(1)} %get-tuple-element.53), channel_id=1, source_target_pairs={{0,1},{1,0},{2,3},{3,2},{4,5},{5,4},{6,7},{7,6},{8,9},{9,8},{10,11... | collective-permute-start | bytes 221192 | tf_op jit(solution)/shard_map/ppermute | solution.py:339
  25.6 0.0 copy-done
  25.7 1.8 %schur_kernel.1 = (f32[2048,128]{1,0:T(8,128)S(1)}, f32[2048,128]{1,0:T(8,128)S(1)}) custom-call(s32[1,512]{1,0:T(1,128)S(1)} %get-tuple-element.45.panel_ref, f32[1,128]{1,0:T(1,128)S(1)} %get-tuple-element.46.own_diagonal_ref, bf16[1536,1024]{1,0:T(8,128)(2,1)S(1)} %bitcast.6, bf16[512,1536]{1,0:T(8,128)(2,1)S(1)} %get-tuple-element.48.turned_ref), custom_call_target="tpu_custom_call" | custom-call | bytes 1024 | tf_op jit(solution)/shard_map/schur_kernel/pallas_call | solution.py:324
  27.5 0.0 collective-permute-done.7.refs_1_
  27.5 1.5 %collective-permute-done.8.refs_2_ = s16[72,512]{1,0:T(8,128)(2,1)S(1)} collective-permute-done((s16[72,512]{1,0:T(8,128)(2,1)S(1)}, s16[72,512]{1,0:T(8,128)(2,1)S(1)}, u32[]{:S(2)}, u32[]{:S(2)}) %collective-permute-start.8) | collective-permute-done | bytes 73760 | tf_op jit(solution)/shard_map/ppermute | solution.py:339
  28.9 0.1 collective-permute-done.9.refs_3_
  29.0 0.1 sum_kernel.3.refs_0_
  29.1 0.1 collective-permute-start.11
  29.2 1.6 %collective-permute-start.10 = (s16[72,512]{1,0:T(8,128)(2,1)S(1)}, s16[72,512]{1,0:T(8,128)(2,1)S(1)}, u32[]{:S(2)}, u32[]{:S(2)}) collective-permute-start(s16[72,512]{1,0:T(8,128)(2,1)S(1)} %sum_kernel.3.refs_0_), channel_id=1, source_target_pairs={{0,8},{4,12},{8,0},{12,4},{16,24},{20,28},{24,16},{28,20},{1,9},{5... | collective-permute-start | bytes 221192 | tf_op jit(solution)/shard_map/ppermute | solution.py:339
  30.9 3.0 %collective-permute-done.10.refs_1_ = s16[72,512]{1,0:T(8,128)(2,1)S(1)} collective-permute-done((s16[72,512]{1,0:T(8,128)(2,1)S(1)}, s16[72,512]{1,0:T(8,128)(2,1)S(1)}, u32[]{:S(2)}, u32[]{:S(2)}) %collective-permute-start.10) | collective-permute-done | bytes 73760 | tf_op jit(solution)/shard_map/ppermute | solution.py:339
  33.9 0.1 sum_kernel.4.refs_0_
  34.0 2.7 %collective-permute-start.12 = (s16[72,512]{1,0:T(8,128)(2,1)S(1)}, s16[72,512]{1,0:T(8,128)(2,1)S(1)}, u32[]{:S(2)}, u32[]{:S(2)}) collective-permute-start(s16[72,512]{1,0:T(8,128)(2,1)S(1)} %sum_kernel.4.refs_0_), channel_id=1, source_target_pairs={{0,16},{4,20},{8,24},{12,28},{16,0},{20,4},{24,8},{28,12},{1,17},{... | collective-permute-start | bytes 221192 | tf_op jit(solution)/shard_map/ppermute | solution.py:339
  36.7 0.0 collective-permute-done.11.got_ref
  36.7 0.2 bulk_pair_kernel.1
  36.9 3.7 %collective-permute-done.12.refs_1_ = s16[72,512]{1,0:T(8,128)(2,1)S(1)} collective-permute-done((s16[72,512]{1,0:T(8,128)(2,1)S(1)}, s16[72,512]{1,0:T(8,128)(2,1)S(1)}, u32[]{:S(2)}, u32[]{:S(2)}) %collective-permute-start.12) | collective-permute-done | bytes 73760 | tf_op jit(solution)/shard_map/ppermute | solution.py:339
  40.6 0.1 sum_kernel.5.refs_0_
  40.7 0.5 collective-permute-start.16
  41.2 2.0 %collective-permute-start.15 = (s16[72,512]{1,0:T(8,128)(2,1)S(1)}, s16[72,512]{1,0:T(8,128)(2,1)S(1)}, u32[]{:S(2)}, u32[]{:S(2)}) collective-permute-start(s16[72,512]{1,0:T(8,128)(2,1)S(1)} %sum_kernel.5.refs_0_), channel_id=1, source_target_pairs={{0,3},{1,2},{2,1},{3,0},{4,7},{5,6},{6,5},{7,4},{8,11},{9,10},{10,... | collective-permute-start | bytes 221192 | tf_op jit(solution)/shard_map/ppermute | solution.py:339
  43.2 0.5 collective-permute-start.14
  43.7 1.0 %collective-permute-start.13 = (s16[72,512]{1,0:T(8,128)(2,1)S(1)}, s16[72,512]{1,0:T(8,128)(2,1)S(1)}, u32[]{:S(2)}, u32[]{:S(2)}) collective-permute-start(s16[72,512]{1,0:T(8,128)(2,1)S(1)} %sum_kernel.5.refs_0_), channel_id=1, source_target_pairs={{0,1},{1,0},{2,3},{3,2},{4,5},{5,4},{6,7},{7,6},{8,9},{9,8},{10,11... | collective-permute-start | bytes 221192 | tf_op jit(solution)/shard_map/ppermute | solution.py:339
  44.7 1.8 %collective-permute-done.15.refs_3_ = s16[72,512]{1,0:T(8,128)(2,1)S(1)} collective-permute-done((s16[72,512]{1,0:T(8,128)(2,1)S(1)}, s16[72,512]{1,0:T(8,128)(2,1)S(1)}, u32[]{:S(2)}, u32[]{:S(2)}) %collective-permute-start.15) | collective-permute-done | bytes 73760 | tf_op jit(solution)/shard_map/ppermute | solution.py:339
  46.5 1.0 %collective-permute-done.14.refs_2_ = s16[72,512]{1,0:T(8,128)(2,1)S(1)} collective-permute-done((s16[72,512]{1,0:T(8,128)(2,1)S(1)}, s16[72,512]{1,0:T(8,128)(2,1)S(1)}, u32[]{:S(2)}, u32[]{:S(2)}) %collective-permute-start.14) | collective-permute-done | bytes 73760 | tf_op jit(solution)/shard_map/ppermute | solution.py:339
  47.5 0.5 collective-permute-done.13.refs_1_
  48.1 0.0 collective-permute-done.16.got_ref
  48.1 0.2 bulk_sum_kernel.1
  48.3 0.1 collective-permute-start.17
  48.3 3.4 %collective-permute-start.18 = (s16[528,128]{1,0:T(8,128)(2,1)S(1)}, s16[528,128]{1,0:T(8,128)(2,1)S(1)}, u32[]{:S(2)}, u32[]{:S(2)}) collective-permute-start(s16[528,128]{1,0:T(8,128)(2,1)S(1)} %get-tuple-element.61), channel_id=1, source_target_pairs={{0,16},{4,20},{8,24},{12,28},{16,0},{20,4},{24,8},{28,12},{1,17},{... | collective-permute-start | bytes 405512 | tf_op jit(solution)/shard_map/ppermute | solution.py:339
  51.8 0.2 own_kernel.1.half_ref
  52.0 0.0 collective-permute-done.17.other_ref
  52.0 3.9 %first_kernel.1 = (f32[512,256]{1,0:T(8,128)S(1)}, f32[512,512]{1,0:T(8,128)S(1)}) custom-call(f32[256,512]{1,0:T(8,128)S(1)} %own_kernel.1.half_ref, s16[320,512]{1,0:T(8,128)(2,1)S(1)} %collective-permute-done.17.other_ref), custom_call_target="tpu_custom_call" | custom-call | bytes 16606024 | tf_op jit(solution)/shard_map/first_kernel/pallas_call | solution.py:324
  55.8 3.6 %second_kernel.1.inverse_second_ref = f32[256,512]{1,0:T(8,128)S(1)} custom-call(f32[512,512]{1,0:T(8,128)S(1)} %get-tuple-element.64.pivots_ref, f32[512,256]{1,0:T(8,128)S(1)} %get-tuple-element.63.inverse_first_ref), custom_call_target="tpu_custom_call" | custom-call | bytes 16606024 | tf_op jit(solution)/shard_map/second_kernel/pallas_call | solution.py:324
  59.4 0.0 collective-permute-done.18.refs_0_
  59.4 1.2 %factor_kernel.1 = (f32[128,1,256]{2,1,0:T(1,128)}, f32[128,1,256]{2,1,0:T(1,128)}) custom-call(f32[512,256]{1,0:T(8,128)S(1)} %get-tuple-element.63.inverse_first_ref, f32[256,512]{1,0:T(8,128)S(1)} %second_kernel.1.inverse_second_ref, f32[512,128]{1,0:T(8,128)S(1)} %get-tuple-element.65.rows_ref, s16[528,128]{1,0:T(8,128)(2,1)S(1)} %collective-permute-done.18.refs_0_), custom_call_target="tpu_custom_call" | custom-call | bytes 1024 | tf_op jit(solution)/shard_map/factor_kernel/pallas_call | solution.py:324
  (1 shorter events, 0.0 us)
Async XLA Ops:
  1.8 8.7 %collective-permute-start.1 = (bf16[256,384]{1,0:T(8,128)(2,1)S(1)}, bf16[256,384]{1,0:T(8,128)(2,1)S(1)}, u32[]{:S(2)}, u32[]{:S(2)}) collective-permute-start(bf16[256,384]{1,0:T(8,128)(2,1)S(1)} %get-tuple-element.37.refs_1_), channel_id=1, source_target_pairs={{0,1},{1,0},{2,3},{3,2},{4,5},{5,4},{6,7},{7,6},{8,9},{9,8},{10,11... | collective-permute-start | bytes 589832 | tf_op jit(solution)/shard_map/ppermute | solution.py:339
  4.8 7.8 %collective-permute-start.2 = (bf16[256,384]{1,0:T(8,128)(2,1)S(1)}, bf16[256,384]{1,0:T(8,128)(2,1)S(1)}, u32[]{:S(2)}, u32[]{:S(2)}) collective-permute-start(bf16[256,384]{1,0:T(8,128)(2,1)S(1)} %get-tuple-element.36.refs_0_), channel_id=1, source_target_pairs={{0,2},{1,3},{2,0},{3,1},{4,6},{5,7},{6,4},{7,5},{8,10},{9,11},{10,... | collective-permute-start | bytes 589832 | tf_op jit(solution)/shard_map/ppermute | solution.py:339
  6.3 10.7 %collective-permute-start = (bf16[256,384]{1,0:T(8,128)(2,1)S(1)}, bf16[256,384]{1,0:T(8,128)(2,1)S(1)}, u32[]{:S(2)}, u32[]{:S(2)}) collective-permute-start(bf16[256,384]{1,0:T(8,128)(2,1)S(1)} %get-tuple-element.36.refs_0_), channel_id=1, source_target_pairs={{0,1},{1,0},{2,3},{3,2},{4,5},{5,4},{6,7},{7,6},{8,9},{9,8},{10,11... | collective-permute-start | bytes 589832 | tf_op jit(solution)/shard_map/ppermute | solution.py:339
  6.9 10.1 %collective-permute-start.3 = (bf16[256,384]{1,0:T(8,128)(2,1)S(1)}, bf16[256,384]{1,0:T(8,128)(2,1)S(1)}, u32[]{:S(2)}, u32[]{:S(2)}) collective-permute-start(bf16[256,384]{1,0:T(8,128)(2,1)S(1)} %get-tuple-element.37.refs_1_), channel_id=1, source_target_pairs={{0,2},{1,3},{2,0},{3,1},{4,6},{5,7},{6,4},{7,5},{8,10},{9,11},{10,... | collective-permute-start | bytes 589832 | tf_op jit(solution)/shard_map/ppermute | solution.py:339
  12.6 5.7 %collective-permute-start.4 = (bf16[256,384]{1,0:T(8,128)(2,1)S(1)}, bf16[256,384]{1,0:T(8,128)(2,1)S(1)}, u32[]{:S(2)}, u32[]{:S(2)}) collective-permute-start(bf16[256,384]{1,0:T(8,128)(2,1)S(1)} %collective-permute-done.2.refs_4_), channel_id=1, source_target_pairs={{0,1},{1,0},{2,3},{3,2},{4,5},{5,4},{6,7},{7,6},{8,9},{9,8},{10,11... | collective-permute-start | bytes 589832 | tf_op jit(solution)/shard_map/ppermute | solution.py:339
  12.7 6.9 %collective-permute-start.5 = (bf16[256,384]{1,0:T(8,128)(2,1)S(1)}, bf16[256,384]{1,0:T(8,128)(2,1)S(1)}, u32[]{:S(2)}, u32[]{:S(2)}) collective-permute-start(bf16[256,384]{1,0:T(8,128)(2,1)S(1)} %collective-permute-done.1.refs_3_), channel_id=1, source_target_pairs={{0,2},{1,3},{2,0},{3,1},{4,6},{5,7},{6,4},{7,5},{8,10},{9,11},{10,... | collective-permute-start | bytes 589832 | tf_op jit(solution)/shard_map/ppermute | solution.py:339
  19.9 2.0 %collective-permute-start.6 = (f32[264,512]{1,0:T(8,128)S(1)}, f32[264,512]{1,0:T(8,128)S(1)}, u32[]{:S(2)}, u32[]{:S(2)}) collective-permute-start(f32[264,512]{1,0:T(8,128)S(1)} %send_kernel.1), channel_id=1, source_target_pairs={{0,4},{4,0},{8,12},{12,8},{16,20},{20,16},{24,28},{28,24},{1,5},{5... | collective-permute-start | bytes 1622024 | tf_op jit(solution)/shard_map/ppermute | solution.py:339
  20.0 5.6 %copy-start = (bf16[1,1536,1024]{2,1,0:T(8,128)(2,1)S(1)}, bf16[1,1536,1024]{2,1,0:T(8,128)(2,1)}, u32[]{:S(2)}) copy-start(bf16[1,1536,1024]{2,1,0:T(8,128)(2,1)} %param.4) | copy-start | bytes 9437188
  22.1 5.4 %collective-permute-start.7 = (s16[72,512]{1,0:T(8,128)(2,1)S(1)}, s16[72,512]{1,0:T(8,128)(2,1)S(1)}, u32[]{:S(2)}, u32[]{:S(2)}) collective-permute-start(s16[72,512]{1,0:T(8,128)(2,1)S(1)} %get-tuple-element.51), channel_id=1, source_target_pairs={{0,3},{1,2},{2,1},{3,0},{4,7},{5,6},{6,5},{7,4},{8,11},{9,10},{10,... | collective-permute-start | bytes 221192 | tf_op jit(solution)/shard_map/ppermute | solution.py:339
  23.9 5.1 %collective-permute-start.8 = (s16[72,512]{1,0:T(8,128)(2,1)S(1)}, s16[72,512]{1,0:T(8,128)(2,1)S(1)}, u32[]{:S(2)}, u32[]{:S(2)}) collective-permute-start(s16[72,512]{1,0:T(8,128)(2,1)S(1)} %get-tuple-element.52), channel_id=1, source_target_pairs={{0,2},{1,3},{2,0},{3,1},{4,6},{5,7},{6,4},{7,5},{8,10},{9,11},{10,... | collective-permute-start | bytes 221192 | tf_op jit(solution)/shard_map/ppermute | solution.py:339
  24.4 4.6 %collective-permute-start.9 = (s16[72,512]{1,0:T(8,128)(2,1)S(1)}, s16[72,512]{1,0:T(8,128)(2,1)S(1)}, u32[]{:S(2)}, u32[]{:S(2)}) collective-permute-start(s16[72,512]{1,0:T(8,128)(2,1)S(1)} %get-tuple-element.53), channel_id=1, source_target_pairs={{0,1},{1,0},{2,3},{3,2},{4,5},{5,4},{6,7},{7,6},{8,9},{9,8},{10,11... | collective-permute-start | bytes 221192 | tf_op jit(solution)/shard_map/ppermute | solution.py:339
  29.1 7.5 %collective-permute-start.11 = (f32[2048,128]{1,0:T(8,128)S(1)}, f32[2048,128]{1,0:T(8,128)S(1)}, u32[]{:S(2)}, u32[]{:S(2)}) collective-permute-start(f32[2048,128]{1,0:T(8,128)S(1)} %get-tuple-element.56), channel_id=1, source_target_pairs={{0,4},{4,0},{8,12},{12,8},{16,20},{20,16},{24,28},{28,24},{1,5},{5... | collective-permute-start | bytes 3145736 | tf_op jit(solution)/shard_map/ppermute | solution.py:339
  29.2 4.7 %collective-permute-start.10 = (s16[72,512]{1,0:T(8,128)(2,1)S(1)}, s16[72,512]{1,0:T(8,128)(2,1)S(1)}, u32[]{:S(2)}, u32[]{:S(2)}) collective-permute-start(s16[72,512]{1,0:T(8,128)(2,1)S(1)} %sum_kernel.3.refs_0_), channel_id=1, source_target_pairs={{0,8},{4,12},{8,0},{12,4},{16,24},{20,28},{24,16},{28,20},{1,9},{5... | collective-permute-start | bytes 221192 | tf_op jit(solution)/shard_map/ppermute | solution.py:339
  34.0 6.6 %collective-permute-start.12 = (s16[72,512]{1,0:T(8,128)(2,1)S(1)}, s16[72,512]{1,0:T(8,128)(2,1)S(1)}, u32[]{:S(2)}, u32[]{:S(2)}) collective-permute-start(s16[72,512]{1,0:T(8,128)(2,1)S(1)} %sum_kernel.4.refs_0_), channel_id=1, source_target_pairs={{0,16},{4,20},{8,24},{12,28},{16,0},{20,4},{24,8},{28,12},{1,17},{... | collective-permute-start | bytes 221192 | tf_op jit(solution)/shard_map/ppermute | solution.py:339
  40.7 7.4 %collective-permute-start.16 = (s16[1056,128]{1,0:T(8,128)(2,1)S(1)}, s16[1056,128]{1,0:T(8,128)(2,1)S(1)}, u32[]{:S(2)}, u32[]{:S(2)}) collective-permute-start(s16[1056,128]{1,0:T(8,128)(2,1)S(1)} %get-tuple-element.60), channel_id=1, source_target_pairs={{0,8},{4,12},{8,0},{12,4},{16,24},{20,28},{24,16},{28,20},{1,9},{5... | collective-permute-start | bytes 811016 | tf_op jit(solution)/shard_map/ppermute | solution.py:339
  41.2 5.3 %collective-permute-start.15 = (s16[72,512]{1,0:T(8,128)(2,1)S(1)}, s16[72,512]{1,0:T(8,128)(2,1)S(1)}, u32[]{:S(2)}, u32[]{:S(2)}) collective-permute-start(s16[72,512]{1,0:T(8,128)(2,1)S(1)} %sum_kernel.5.refs_0_), channel_id=1, source_target_pairs={{0,3},{1,2},{2,1},{3,0},{4,7},{5,6},{6,5},{7,4},{8,11},{9,10},{10,... | collective-permute-start | bytes 221192 | tf_op jit(solution)/shard_map/ppermute | solution.py:339
  43.2 4.4 %collective-permute-start.14 = (s16[72,512]{1,0:T(8,128)(2,1)S(1)}, s16[72,512]{1,0:T(8,128)(2,1)S(1)}, u32[]{:S(2)}, u32[]{:S(2)}) collective-permute-start(s16[72,512]{1,0:T(8,128)(2,1)S(1)} %sum_kernel.5.refs_0_), channel_id=1, source_target_pairs={{0,2},{1,3},{2,0},{3,1},{4,6},{5,7},{6,4},{7,5},{8,10},{9,11},{10,... | collective-permute-start | bytes 221192 | tf_op jit(solution)/shard_map/ppermute | solution.py:339
  43.7 4.4 %collective-permute-start.13 = (s16[72,512]{1,0:T(8,128)(2,1)S(1)}, s16[72,512]{1,0:T(8,128)(2,1)S(1)}, u32[]{:S(2)}, u32[]{:S(2)}) collective-permute-start(s16[72,512]{1,0:T(8,128)(2,1)S(1)} %sum_kernel.5.refs_0_), channel_id=1, source_target_pairs={{0,1},{1,0},{2,3},{3,2},{4,5},{5,4},{6,7},{7,6},{8,9},{9,8},{10,11... | collective-permute-start | bytes 221192 | tf_op jit(solution)/shard_map/ppermute | solution.py:339
  48.3 3.7 %collective-permute-start.17 = (s16[320,512]{1,0:T(8,128)(2,1)S(1)}, s16[320,512]{1,0:T(8,128)(2,1)S(1)}, u32[]{:S(2)}, u32[]{:S(2)}) collective-permute-start(s16[320,512]{1,0:T(8,128)(2,1)S(1)} %join_kernel.1.own_ref), channel_id=1, source_target_pairs={{0,4},{4,0},{8,12},{12,8},{16,20},{20,16},{24,28},{28,24},{1,5},{5... | collective-permute-start | bytes 983048 | tf_op jit(solution)/shard_map/ppermute | solution.py:339
  48.3 11.1 %collective-permute-start.18 = (s16[528,128]{1,0:T(8,128)(2,1)S(1)}, s16[528,128]{1,0:T(8,128)(2,1)S(1)}, u32[]{:S(2)}, u32[]{:S(2)}) collective-permute-start(s16[528,128]{1,0:T(8,128)(2,1)S(1)} %get-tuple-element.61), channel_id=1, source_target_pairs={{0,16},{4,20},{8,24},{12,28},{16,0},{20,4},{24,8},{28,12},{1,17},{... | collective-permute-start | bytes 405512 | tf_op jit(solution)/shard_map/ppermute | solution.py:339

commit v10 on v9

--- a/solution.py
+++ b/solution.py
@@ -44,16 +44,19 @@
 
 def nearly(pivot):
     size = jnp.abs(pivot)
+    turned = pivot.T
+    square = product(pivot, turned)
     norm_one = jnp.max(jnp.sum(size, axis=0, keepdims=True))
     norm_inf = jnp.max(jnp.sum(size, axis=1, keepdims=True))
-    approx = pivot.T / (norm_one * norm_inf)
+    scale = F32(1.0) / (norm_one * norm_inf)
     count = pivot.shape[0]
     one = lax.broadcasted_iota(jnp.int32, pivot.shape, 0) == lax.broadcasted_iota(jnp.int32, pivot.shape, 1)
-    rest = jnp.where(one, F32(1.0), F32(0.0)) - product(approx, pivot)
+    rest = jnp.where(one, F32(1.0), F32(0.0)) - square * scale
+    approx = turned * scale
     for step in range(NEWTON - 2):
-        both = product(rest, jnp.concatenate([rest, approx], axis=1))
-        rest, approx = both[:, :count], approx + both[:, count:]
-    return approx + product(rest, approx)
+        both = product(jnp.concatenate([rest, approx], axis=0), rest)
+        rest, approx = both[:count], approx + both[count:]
+    return approx + product(approx, rest)
 
 
 def newton_below(pivot, below):

time: 60.8 us -> 62.5 us (1.028)
  Pallas kernels: 19.4 us -> 21.1 us
    pallas_call x18, Pallas kernels: 19.4 us -> 21.1 us  [call(): pl.pallas_call(kernel, name=getattr(kernel, 'func', kernel).__name__, out...]
  transfers between devices with their start and end apart: 19 -> 19, of which waited for: 12 -> 12; matrix products, arithmetic and copies ran while one was open for 0% -> 0% of each run, Pallas kernels for 27% -> 29%
where the time goes in v10:
time: 62.5 us; the launch traced here: 62.3 us
  starting transfers between devices  22.7 us (36%)
  Pallas kernels  21.1 us (34%)
  waiting for transfers between devices  17.7 us (28%)
  between operations  0.83 us (1%)
    ppermute x19, starting transfers between devices, swap(): return lax.ppermute(x, axis, [(i, i ^ bit) for i in range(count)])  22.7 us
    pallas_call x18, Pallas kernels, call(): pl.pallas_call(kernel, name=getattr(kernel, 'func', kernel).__name__, out...  21.1 us
    ppermute x19, waiting for transfers between devices, swap(): return lax.ppermute(x, axis, [(i, i ^ bit) for i in range(count)])  17.7 us
  transfers between devices with their start and end apart: 19, of which 12 were waited for; matrix products, arithmetic and copies ran while one was open for 0% of the time, Pallas kernels for 29%

profile of v10, /device:TPU:0, one launch (start us, length us, event | category | flops | bytes accessed | tf_op | source)
XLA Modules:
  0.0 62.3 jit_solution(10045800437709015629)
XLA Ops:
  0.6 1.2 %turn_kernel.1 = (bf16[256,384]{1,0:T(8,128)(2,1)S(1)}, bf16[256,384]{1,0:T(8,128)(2,1)S(1)}) custom-call(bf16[384,512]{1,0:T(8,128)(2,1)} %bitcast.7), custom_call_target="tpu_custom_call" | custom-call | bytes 1024 | tf_op jit(solution)/shard_map/turn_kernel/pallas_call | solution.py:327
  1.8 3.0 %collective-permute-start.1 = (bf16[256,384]{1,0:T(8,128)(2,1)S(1)}, bf16[256,384]{1,0:T(8,128)(2,1)S(1)}, u32[]{:S(2)}, u32[]{:S(2)}) collective-permute-start(bf16[256,384]{1,0:T(8,128)(2,1)S(1)} %get-tuple-element.37.refs_1_), channel_id=1, source_target_pairs={{0,1},{1,0},{2,3},{3,2},{4,5},{5,4},{6,7},{7,6},{8,9},{9,8},{10,11... | collective-permute-start | bytes 589832 | tf_op jit(solution)/shard_map/ppermute | solution.py:342
  4.8 1.5 %collective-permute-start.2 = (bf16[256,384]{1,0:T(8,128)(2,1)S(1)}, bf16[256,384]{1,0:T(8,128)(2,1)S(1)}, u32[]{:S(2)}, u32[]{:S(2)}) collective-permute-start(bf16[256,384]{1,0:T(8,128)(2,1)S(1)} %get-tuple-element.36.refs_0_), channel_id=1, source_target_pairs={{0,2},{1,3},{2,0},{3,1},{4,6},{5,7},{6,4},{7,5},{8,10},{9,11},{10,... | collective-permute-start | bytes 589832 | tf_op jit(solution)/shard_map/ppermute | solution.py:342
  6.3 0.5 collective-permute-start
  6.9 0.1 collective-permute-start.3
  6.9 2.6 %pick_kernel.1 = (bf16[1536,512]{1,0:T(8,128)(2,1)S(1)}, f32[8,512]{1,0:T(8,128)S(1)}, bf16[1024,512]{1,0:T(8,128)(2,1)S(1)}, s32[1,512]{1,0:T(1,128)S(1)}, f32[1,128]{1,0:T(1,128)S(1)}) custom-call(s32[1,512]{1,0:T(1,128)} %bitcast.8, f32[1,128]{1,0:T(1,128)} %bitcast.9, bf16[1536,1024]{1,0:T(8,128)(2,1)} %bitcast.4), custom_call_target="tpu_custom_call" | custom-call | bytes 1024 | tf_op jit(solution)/shard_map/pick_kernel/pallas_call | solution.py:327
  9.6 1.0 %collective-permute-done.1.refs_3_ = bf16[256,384]{1,0:T(8,128)(2,1)S(1)} collective-permute-done((bf16[256,384]{1,0:T(8,128)(2,1)S(1)}, bf16[256,384]{1,0:T(8,128)(2,1)S(1)}, u32[]{:S(2)}, u32[]{:S(2)}) %collective-permute-start.1) | collective-permute-done | bytes 196640 | tf_op jit(solution)/shard_map/ppermute | solution.py:342
  10.5 2.1 %collective-permute-done.2.refs_4_ = bf16[256,384]{1,0:T(8,128)(2,1)S(1)} collective-permute-done((bf16[256,384]{1,0:T(8,128)(2,1)S(1)}, bf16[256,384]{1,0:T(8,128)(2,1)S(1)}, u32[]{:S(2)}, u32[]{:S(2)}) %collective-permute-start.2) | collective-permute-done | bytes 196640 | tf_op jit(solution)/shard_map/ppermute | solution.py:342
  12.6 0.0 collective-permute-start.4
  12.7 2.0 %collective-permute-start.5 = (bf16[256,384]{1,0:T(8,128)(2,1)S(1)}, bf16[256,384]{1,0:T(8,128)(2,1)S(1)}, u32[]{:S(2)}, u32[]{:S(2)}) collective-permute-start(bf16[256,384]{1,0:T(8,128)(2,1)S(1)} %collective-permute-done.1.refs_3_), channel_id=1, source_target_pairs={{0,2},{1,3},{2,0},{3,1},{4,6},{5,7},{6,4},{7,5},{8,10},{9,11},{10,... | collective-permute-start | bytes 589832 | tf_op jit(solution)/shard_map/ppermute | solution.py:342
  14.7 2.3 %rest_kernel.1.chosen_ref = bf16[1536,512]{1,0:T(8,128)(2,1)S(1)} custom-call(bf16[1536,512]{1,0:T(8,128)(2,1)S(1)} %get-tuple-element.34.chosen_in, bf16[1024,512]{1,0:T(8,128)(2,1)S(1)} %get-tuple-element.35.one_ref, bf16[1536,1024]{1,0:T(8,128)(2,1)} %bitcast.5), custom_call_target="tpu_custom_call", output_to_operand_aliasing={{}: (0, {})} | custom-call | bytes 1024 | tf_op jit(solution)/shard_map/rest_kernel/pallas_call | solution.py:327
  17.0 0.0 collective-permute-done.refs_2_
  17.0 0.0 collective-permute-done.3.refs_5_
  17.0 1.1 %early_kernel.1 = (bf16[512,1536]{1,0:T(8,128)(2,1)S(1)}, f32[512,512]{1,0:T(8,128)S(1)}) custom-call(bf16[1536,512]{1,0:T(8,128)(2,1)S(1)} %rest_kernel.1.chosen_ref, bf16[256,384]{1,0:T(8,128)(2,1)S(1)} %get-tuple-element.36.refs_0_, bf16[256,384]{1,0:T(8,128)(2,1)S(1)} %get-tuple-element.37.refs_1_, bf16[256,384]{1,0:T(8,128)(2,1)S(1)} %collective-permute-done.refs_2_, ...), custom_call_target="tpu_custom_call" | custom-call | bytes 1024 | tf_op jit(solution)/shard_map/early_kernel/pallas_call | solution.py:327
  18.1 0.2 collective-permute-done.4.refs_0_
  18.3 1.3 %collective-permute-done.5.refs_1_ = bf16[256,384]{1,0:T(8,128)(2,1)S(1)} collective-permute-done((bf16[256,384]{1,0:T(8,128)(2,1)S(1)}, bf16[256,384]{1,0:T(8,128)(2,1)S(1)}, u32[]{:S(2)}, u32[]{:S(2)}) %collective-permute-start.5) | collective-permute-done | bytes 196640 | tf_op jit(solution)/shard_map/ppermute | solution.py:342
  19.6 0.3 send_kernel.1
  19.9 0.1 collective-permute-start.6
  20.0 0.0 copy-start
  20.0 0.4 keep_kernel.1
  20.4 1.5 %collective-permute-done.6.got_ref = f32[264,512]{1,0:T(8,128)S(1)} collective-permute-done((f32[264,512]{1,0:T(8,128)S(1)}, f32[264,512]{1,0:T(8,128)S(1)}, u32[]{:S(2)}, u32[]{:S(2)}) %collective-permute-start.6) | collective-permute-done | bytes 540704 | tf_op jit(solution)/shard_map/ppermute | solution.py:342
  21.9 0.2 pair_kernel.1
  22.1 1.8 %collective-permute-start.7 = (s16[72,512]{1,0:T(8,128)(2,1)S(1)}, s16[72,512]{1,0:T(8,128)(2,1)S(1)}, u32[]{:S(2)}, u32[]{:S(2)}) collective-permute-start(s16[72,512]{1,0:T(8,128)(2,1)S(1)} %get-tuple-element.51), channel_id=1, source_target_pairs={{0,3},{1,2},{2,1},{3,0},{4,7},{5,6},{6,5},{7,4},{8,11},{9,10},{10,... | collective-permute-start | bytes 221192 | tf_op jit(solution)/shard_map/ppermute | solution.py:342
  23.9 0.5 collective-permute-start.8
  24.4 1.3 %collective-permute-start.9 = (s16[72,512]{1,0:T(8,128)(2,1)S(1)}, s16[72,512]{1,0:T(8,128)(2,1)S(1)}, u32[]{:S(2)}, u32[]{:S(2)}) collective-permute-start(s16[72,512]{1,0:T(8,128)(2,1)S(1)} %get-tuple-element.53), channel_id=1, source_target_pairs={{0,1},{1,0},{2,3},{3,2},{4,5},{5,4},{6,7},{7,6},{8,9},{9,8},{10,11... | collective-permute-start | bytes 221192 | tf_op jit(solution)/shard_map/ppermute | solution.py:342
  25.6 0.0 copy-done
  25.7 1.8 %schur_kernel.1 = (f32[2048,128]{1,0:T(8,128)S(1)}, f32[2048,128]{1,0:T(8,128)S(1)}) custom-call(s32[1,512]{1,0:T(1,128)S(1)} %get-tuple-element.45.panel_ref, f32[1,128]{1,0:T(1,128)S(1)} %get-tuple-element.46.own_diagonal_ref, bf16[1536,1024]{1,0:T(8,128)(2,1)S(1)} %bitcast.6, bf16[512,1536]{1,0:T(8,128)(2,1)S(1)} %get-tuple-element.48.turned_ref), custom_call_target="tpu_custom_call" | custom-call | bytes 1024 | tf_op jit(solution)/shard_map/schur_kernel/pallas_call | solution.py:327
  27.5 0.0 collective-permute-done.7.refs_1_
  27.5 1.5 %collective-permute-done.8.refs_2_ = s16[72,512]{1,0:T(8,128)(2,1)S(1)} collective-permute-done((s16[72,512]{1,0:T(8,128)(2,1)S(1)}, s16[72,512]{1,0:T(8,128)(2,1)S(1)}, u32[]{:S(2)}, u32[]{:S(2)}) %collective-permute-start.8) | collective-permute-done | bytes 73760 | tf_op jit(solution)/shard_map/ppermute | solution.py:342
  28.9 0.1 collective-permute-done.9.refs_3_
  29.0 0.1 sum_kernel.3.refs_0_
  29.1 0.1 collective-permute-start.11
  29.2 1.6 %collective-permute-start.10 = (s16[72,512]{1,0:T(8,128)(2,1)S(1)}, s16[72,512]{1,0:T(8,128)(2,1)S(1)}, u32[]{:S(2)}, u32[]{:S(2)}) collective-permute-start(s16[72,512]{1,0:T(8,128)(2,1)S(1)} %sum_kernel.3.refs_0_), channel_id=1, source_target_pairs={{0,8},{4,12},{8,0},{12,4},{16,24},{20,28},{24,16},{28,20},{1,9},{5... | collective-permute-start | bytes 221192 | tf_op jit(solution)/shard_map/ppermute | solution.py:342
  30.9 3.0 %collective-permute-done.10.refs_1_ = s16[72,512]{1,0:T(8,128)(2,1)S(1)} collective-permute-done((s16[72,512]{1,0:T(8,128)(2,1)S(1)}, s16[72,512]{1,0:T(8,128)(2,1)S(1)}, u32[]{:S(2)}, u32[]{:S(2)}) %collective-permute-start.10) | collective-permute-done | bytes 73760 | tf_op jit(solution)/shard_map/ppermute | solution.py:342
  33.9 0.1 sum_kernel.4.refs_0_
  34.0 2.7 %collective-permute-start.12 = (s16[72,512]{1,0:T(8,128)(2,1)S(1)}, s16[72,512]{1,0:T(8,128)(2,1)S(1)}, u32[]{:S(2)}, u32[]{:S(2)}) collective-permute-start(s16[72,512]{1,0:T(8,128)(2,1)S(1)} %sum_kernel.4.refs_0_), channel_id=1, source_target_pairs={{0,16},{4,20},{8,24},{12,28},{16,0},{20,4},{24,8},{28,12},{1,17},{... | collective-permute-start | bytes 221192 | tf_op jit(solution)/shard_map/ppermute | solution.py:342
  36.7 0.0 collective-permute-done.11.got_ref
  36.7 0.2 bulk_pair_kernel.1
  36.9 3.7 %collective-permute-done.12.refs_1_ = s16[72,512]{1,0:T(8,128)(2,1)S(1)} collective-permute-done((s16[72,512]{1,0:T(8,128)(2,1)S(1)}, s16[72,512]{1,0:T(8,128)(2,1)S(1)}, u32[]{:S(2)}, u32[]{:S(2)}) %collective-permute-start.12) | collective-permute-done | bytes 73760 | tf_op jit(solution)/shard_map/ppermute | solution.py:342
  40.6 0.1 sum_kernel.5.refs_0_
  40.7 0.5 collective-permute-start.16
  41.2 2.0 %collective-permute-start.15 = (s16[72,512]{1,0:T(8,128)(2,1)S(1)}, s16[72,512]{1,0:T(8,128)(2,1)S(1)}, u32[]{:S(2)}, u32[]{:S(2)}) collective-permute-start(s16[72,512]{1,0:T(8,128)(2,1)S(1)} %sum_kernel.5.refs_0_), channel_id=1, source_target_pairs={{0,3},{1,2},{2,1},{3,0},{4,7},{5,6},{6,5},{7,4},{8,11},{9,10},{10,... | collective-permute-start | bytes 221192 | tf_op jit(solution)/shard_map/ppermute | solution.py:342
  43.2 0.5 collective-permute-start.14
  43.7 1.0 %collective-permute-start.13 = (s16[72,512]{1,0:T(8,128)(2,1)S(1)}, s16[72,512]{1,0:T(8,128)(2,1)S(1)}, u32[]{:S(2)}, u32[]{:S(2)}) collective-permute-start(s16[72,512]{1,0:T(8,128)(2,1)S(1)} %sum_kernel.5.refs_0_), channel_id=1, source_target_pairs={{0,1},{1,0},{2,3},{3,2},{4,5},{5,4},{6,7},{7,6},{8,9},{9,8},{10,11... | collective-permute-start | bytes 221192 | tf_op jit(solution)/shard_map/ppermute | solution.py:342
  44.7 1.8 %collective-permute-done.15.refs_3_ = s16[72,512]{1,0:T(8,128)(2,1)S(1)} collective-permute-done((s16[72,512]{1,0:T(8,128)(2,1)S(1)}, s16[72,512]{1,0:T(8,128)(2,1)S(1)}, u32[]{:S(2)}, u32[]{:S(2)}) %collective-permute-start.15) | collective-permute-done | bytes 73760 | tf_op jit(solution)/shard_map/ppermute | solution.py:342
  46.5 1.0 %collective-permute-done.14.refs_2_ = s16[72,512]{1,0:T(8,128)(2,1)S(1)} collective-permute-done((s16[72,512]{1,0:T(8,128)(2,1)S(1)}, s16[72,512]{1,0:T(8,128)(2,1)S(1)}, u32[]{:S(2)}, u32[]{:S(2)}) %collective-permute-start.14) | collective-permute-done | bytes 73760 | tf_op jit(solution)/shard_map/ppermute | solution.py:342
  47.5 0.5 collective-permute-done.13.refs_1_
  48.1 0.0 collective-permute-done.16.got_ref
  48.1 0.2 bulk_sum_kernel.1
  48.3 0.1 collective-permute-start.17
  48.3 3.4 %collective-permute-start.18 = (s16[528,128]{1,0:T(8,128)(2,1)S(1)}, s16[528,128]{1,0:T(8,128)(2,1)S(1)}, u32[]{:S(2)}, u32[]{:S(2)}) collective-permute-start(s16[528,128]{1,0:T(8,128)(2,1)S(1)} %get-tuple-element.61), channel_id=1, source_target_pairs={{0,16},{4,20},{8,24},{12,28},{16,0},{20,4},{24,8},{28,12},{1,17},{... | collective-permute-start | bytes 405512 | tf_op jit(solution)/shard_map/ppermute | solution.py:342
  51.8 0.2 own_kernel.1.half_ref
  52.0 0.0 collective-permute-done.17.other_ref
  52.0 4.7 %first_kernel.1 = (f32[512,256]{1,0:T(8,128)S(1)}, f32[512,512]{1,0:T(8,128)S(1)}) custom-call(f32[256,512]{1,0:T(8,128)S(1)} %own_kernel.1.half_ref, s16[320,512]{1,0:T(8,128)(2,1)S(1)} %collective-permute-done.17.other_ref), custom_call_target="tpu_custom_call" | custom-call | bytes 16606024 | tf_op jit(solution)/shard_map/first_kernel/pallas_call | solution.py:327
  56.7 4.4 %second_kernel.1.inverse_second_ref = f32[256,512]{1,0:T(8,128)S(1)} custom-call(f32[512,512]{1,0:T(8,128)S(1)} %get-tuple-element.64.pivots_ref, f32[512,256]{1,0:T(8,128)S(1)} %get-tuple-element.63.inverse_first_ref), custom_call_target="tpu_custom_call" | custom-call | bytes 16606024 | tf_op jit(solution)/shard_map/second_kernel/pallas_call | solution.py:327
  61.1 0.0 collective-permute-done.18.refs_0_
  61.1 1.2 %factor_kernel.1 = (f32[128,1,256]{2,1,0:T(1,128)}, f32[128,1,256]{2,1,0:T(1,128)}) custom-call(f32[512,256]{1,0:T(8,128)S(1)} %get-tuple-element.63.inverse_first_ref, f32[256,512]{1,0:T(8,128)S(1)} %second_kernel.1.inverse_second_ref, f32[512,128]{1,0:T(8,128)S(1)} %get-tuple-element.65.rows_ref, s16[528,128]{1,0:T(8,128)(2,1)S(1)} %collective-permute-done.18.refs_0_), custom_call_target="tpu_custom_call" | custom-call | bytes 1024 | tf_op jit(solution)/shard_map/factor_kernel/pallas_call | solution.py:327
  (1 shorter events, 0.0 us)
Async XLA Ops:
  1.8 8.7 %collective-permute-start.1 = (bf16[256,384]{1,0:T(8,128)(2,1)S(1)}, bf16[256,384]{1,0:T(8,128)(2,1)S(1)}, u32[]{:S(2)}, u32[]{:S(2)}) collective-permute-start(bf16[256,384]{1,0:T(8,128)(2,1)S(1)} %get-tuple-element.37.refs_1_), channel_id=1, source_target_pairs={{0,1},{1,0},{2,3},{3,2},{4,5},{5,4},{6,7},{7,6},{8,9},{9,8},{10,11... | collective-permute-start | bytes 589832 | tf_op jit(solution)/shard_map/ppermute | solution.py:342
  4.8 7.8 %collective-permute-start.2 = (bf16[256,384]{1,0:T(8,128)(2,1)S(1)}, bf16[256,384]{1,0:T(8,128)(2,1)S(1)}, u32[]{:S(2)}, u32[]{:S(2)}) collective-permute-start(bf16[256,384]{1,0:T(8,128)(2,1)S(1)} %get-tuple-element.36.refs_0_), channel_id=1, source_target_pairs={{0,2},{1,3},{2,0},{3,1},{4,6},{5,7},{6,4},{7,5},{8,10},{9,11},{10,... | collective-permute-start | bytes 589832 | tf_op jit(solution)/shard_map/ppermute | solution.py:342
  6.3 10.7 %collective-permute-start = (bf16[256,384]{1,0:T(8,128)(2,1)S(1)}, bf16[256,384]{1,0:T(8,128)(2,1)S(1)}, u32[]{:S(2)}, u32[]{:S(2)}) collective-permute-start(bf16[256,384]{1,0:T(8,128)(2,1)S(1)} %get-tuple-element.36.refs_0_), channel_id=1, source_target_pairs={{0,1},{1,0},{2,3},{3,2},{4,5},{5,4},{6,7},{7,6},{8,9},{9,8},{10,11... | collective-permute-start | bytes 589832 | tf_op jit(solution)/shard_map/ppermute | solution.py:342
  6.9 10.1 %collective-permute-start.3 = (bf16[256,384]{1,0:T(8,128)(2,1)S(1)}, bf16[256,384]{1,0:T(8,128)(2,1)S(1)}, u32[]{:S(2)}, u32[]{:S(2)}) collective-permute-start(bf16[256,384]{1,0:T(8,128)(2,1)S(1)} %get-tuple-element.37.refs_1_), channel_id=1, source_target_pairs={{0,2},{1,3},{2,0},{3,1},{4,6},{5,7},{6,4},{7,5},{8,10},{9,11},{10,... | collective-permute-start | bytes 589832 | tf_op jit(solution)/shard_map/ppermute | solution.py:342
  12.6 5.7 %collective-permute-start.4 = (bf16[256,384]{1,0:T(8,128)(2,1)S(1)}, bf16[256,384]{1,0:T(8,128)(2,1)S(1)}, u32[]{:S(2)}, u32[]{:S(2)}) collective-permute-start(bf16[256,384]{1,0:T(8,128)(2,1)S(1)} %collective-permute-done.2.refs_4_), channel_id=1, source_target_pairs={{0,1},{1,0},{2,3},{3,2},{4,5},{5,4},{6,7},{7,6},{8,9},{9,8},{10,11... | collective-permute-start | bytes 589832 | tf_op jit(solution)/shard_map/ppermute | solution.py:342
  12.7 6.9 %collective-permute-start.5 = (bf16[256,384]{1,0:T(8,128)(2,1)S(1)}, bf16[256,384]{1,0:T(8,128)(2,1)S(1)}, u32[]{:S(2)}, u32[]{:S(2)}) collective-permute-start(bf16[256,384]{1,0:T(8,128)(2,1)S(1)} %collective-permute-done.1.refs_3_), channel_id=1, source_target_pairs={{0,2},{1,3},{2,0},{3,1},{4,6},{5,7},{6,4},{7,5},{8,10},{9,11},{10,... | collective-permute-start | bytes 589832 | tf_op jit(solution)/shard_map/ppermute | solution.py:342
  19.9 2.0 %collective-permute-start.6 = (f32[264,512]{1,0:T(8,128)S(1)}, f32[264,512]{1,0:T(8,128)S(1)}, u32[]{:S(2)}, u32[]{:S(2)}) collective-permute-start(f32[264,512]{1,0:T(8,128)S(1)} %send_kernel.1), channel_id=1, source_target_pairs={{0,4},{4,0},{8,12},{12,8},{16,20},{20,16},{24,28},{28,24},{1,5},{5... | collective-permute-start | bytes 1622024 | tf_op jit(solution)/shard_map/ppermute | solution.py:342
  20.0 5.6 %copy-start = (bf16[1,1536,1024]{2,1,0:T(8,128)(2,1)S(1)}, bf16[1,1536,1024]{2,1,0:T(8,128)(2,1)}, u32[]{:S(2)}) copy-start(bf16[1,1536,1024]{2,1,0:T(8,128)(2,1)} %param.4) | copy-start | bytes 9437188
  22.1 5.4 %collective-permute-start.7 = (s16[72,512]{1,0:T(8,128)(2,1)S(1)}, s16[72,512]{1,0:T(8,128)(2,1)S(1)}, u32[]{:S(2)}, u32[]{:S(2)}) collective-permute-start(s16[72,512]{1,0:T(8,128)(2,1)S(1)} %get-tuple-element.51), channel_id=1, source_target_pairs={{0,3},{1,2},{2,1},{3,0},{4,7},{5,6},{6,5},{7,4},{8,11},{9,10},{10,... | collective-permute-start | bytes 221192 | tf_op jit(solution)/shard_map/ppermute | solution.py:342
  23.9 5.1 %collective-permute-start.8 = (s16[72,512]{1,0:T(8,128)(2,1)S(1)}, s16[72,512]{1,0:T(8,128)(2,1)S(1)}, u32[]{:S(2)}, u32[]{:S(2)}) collective-permute-start(s16[72,512]{1,0:T(8,128)(2,1)S(1)} %get-tuple-element.52), channel_id=1, source_target_pairs={{0,2},{1,3},{2,0},{3,1},{4,6},{5,7},{6,4},{7,5},{8,10},{9,11},{10,... | collective-permute-start | bytes 221192 | tf_op jit(solution)/shard_map/ppermute | solution.py:342
  24.4 4.6 %collective-permute-start.9 = (s16[72,512]{1,0:T(8,128)(2,1)S(1)}, s16[72,512]{1,0:T(8,128)(2,1)S(1)}, u32[]{:S(2)}, u32[]{:S(2)}) collective-permute-start(s16[72,512]{1,0:T(8,128)(2,1)S(1)} %get-tuple-element.53), channel_id=1, source_target_pairs={{0,1},{1,0},{2,3},{3,2},{4,5},{5,4},{6,7},{7,6},{8,9},{9,8},{10,11... | collective-permute-start | bytes 221192 | tf_op jit(solution)/shard_map/ppermute | solution.py:342
  29.1 7.5 %collective-permute-start.11 = (f32[2048,128]{1,0:T(8,128)S(1)}, f32[2048,128]{1,0:T(8,128)S(1)}, u32[]{:S(2)}, u32[]{:S(2)}) collective-permute-start(f32[2048,128]{1,0:T(8,128)S(1)} %get-tuple-element.56), channel_id=1, source_target_pairs={{0,4},{4,0},{8,12},{12,8},{16,20},{20,16},{24,28},{28,24},{1,5},{5... | collective-permute-start | bytes 3145736 | tf_op jit(solution)/shard_map/ppermute | solution.py:342
  29.2 4.7 %collective-permute-start.10 = (s16[72,512]{1,0:T(8,128)(2,1)S(1)}, s16[72,512]{1,0:T(8,128)(2,1)S(1)}, u32[]{:S(2)}, u32[]{:S(2)}) collective-permute-start(s16[72,512]{1,0:T(8,128)(2,1)S(1)} %sum_kernel.3.refs_0_), channel_id=1, source_target_pairs={{0,8},{4,12},{8,0},{12,4},{16,24},{20,28},{24,16},{28,20},{1,9},{5... | collective-permute-start | bytes 221192 | tf_op jit(solution)/shard_map/ppermute | solution.py:342
  34.0 6.6 %collective-permute-start.12 = (s16[72,512]{1,0:T(8,128)(2,1)S(1)}, s16[72,512]{1,0:T(8,128)(2,1)S(1)}, u32[]{:S(2)}, u32[]{:S(2)}) collective-permute-start(s16[72,512]{1,0:T(8,128)(2,1)S(1)} %sum_kernel.4.refs_0_), channel_id=1, source_target_pairs={{0,16},{4,20},{8,24},{12,28},{16,0},{20,4},{24,8},{28,12},{1,17},{... | collective-permute-start | bytes 221192 | tf_op jit(solution)/shard_map/ppermute | solution.py:342
  40.7 7.4 %collective-permute-start.16 = (s16[1056,128]{1,0:T(8,128)(2,1)S(1)}, s16[1056,128]{1,0:T(8,128)(2,1)S(1)}, u32[]{:S(2)}, u32[]{:S(2)}) collective-permute-start(s16[1056,128]{1,0:T(8,128)(2,1)S(1)} %get-tuple-element.60), channel_id=1, source_target_pairs={{0,8},{4,12},{8,0},{12,4},{16,24},{20,28},{24,16},{28,20},{1,9},{5... | collective-permute-start | bytes 811016 | tf_op jit(solution)/shard_map/ppermute | solution.py:342
  41.2 5.3 %collective-permute-start.15 = (s16[72,512]{1,0:T(8,128)(2,1)S(1)}, s16[72,512]{1,0:T(8,128)(2,1)S(1)}, u32[]{:S(2)}, u32[]{:S(2)}) collective-permute-start(s16[72,512]{1,0:T(8,128)(2,1)S(1)} %sum_kernel.5.refs_0_), channel_id=1, source_target_pairs={{0,3},{1,2},{2,1},{3,0},{4,7},{5,6},{6,5},{7,4},{8,11},{9,10},{10,... | collective-permute-start | bytes 221192 | tf_op jit(solution)/shard_map/ppermute | solution.py:342
  43.2 4.4 %collective-permute-start.14 = (s16[72,512]{1,0:T(8,128)(2,1)S(1)}, s16[72,512]{1,0:T(8,128)(2,1)S(1)}, u32[]{:S(2)}, u32[]{:S(2)}) collective-permute-start(s16[72,512]{1,0:T(8,128)(2,1)S(1)} %sum_kernel.5.refs_0_), channel_id=1, source_target_pairs={{0,2},{1,3},{2,0},{3,1},{4,6},{5,7},{6,4},{7,5},{8,10},{9,11},{10,... | collective-permute-start | bytes 221192 | tf_op jit(solution)/shard_map/ppermute | solution.py:342
  43.7 4.4 %collective-permute-start.13 = (s16[72,512]{1,0:T(8,128)(2,1)S(1)}, s16[72,512]{1,0:T(8,128)(2,1)S(1)}, u32[]{:S(2)}, u32[]{:S(2)}) collective-permute-start(s16[72,512]{1,0:T(8,128)(2,1)S(1)} %sum_kernel.5.refs_0_), channel_id=1, source_target_pairs={{0,1},{1,0},{2,3},{3,2},{4,5},{5,4},{6,7},{7,6},{8,9},{9,8},{10,11... | collective-permute-start | bytes 221192 | tf_op jit(solution)/shard_map/ppermute | solution.py:342
  48.3 3.7 %collective-permute-start.17 = (s16[320,512]{1,0:T(8,128)(2,1)S(1)}, s16[320,512]{1,0:T(8,128)(2,1)S(1)}, u32[]{:S(2)}, u32[]{:S(2)}) collective-permute-start(s16[320,512]{1,0:T(8,128)(2,1)S(1)} %join_kernel.1.own_ref), channel_id=1, source_target_pairs={{0,4},{4,0},{8,12},{12,8},{16,20},{20,16},{24,28},{28,24},{1,5},{5... | collective-permute-start | bytes 983048 | tf_op jit(solution)/shard_map/ppermute | solution.py:342
  48.3 12.7 %collective-permute-start.18 = (s16[528,128]{1,0:T(8,128)(2,1)S(1)}, s16[528,128]{1,0:T(8,128)(2,1)S(1)}, u32[]{:S(2)}, u32[]{:S(2)}) collective-permute-start(s16[528,128]{1,0:T(8,128)(2,1)S(1)} %get-tuple-element.61), channel_id=1, source_target_pairs={{0,16},{4,20},{8,24},{12,28},{16,0},{20,4},{24,8},{28,12},{1,17},{... | collective-permute-start | bytes 405512 | tf_op jit(solution)/shard_map/ppermute | solution.py:342

commit v11 on v9

--- a/solution.py
+++ b/solution.py
@@ -44,24 +44,19 @@
 
 def nearly(pivot):
     size = jnp.abs(pivot)
+    turned = pivot.T
+    square = product(turned, pivot)
     norm_one = jnp.max(jnp.sum(size, axis=0, keepdims=True))
     norm_inf = jnp.max(jnp.sum(size, axis=1, keepdims=True))
-    approx = pivot.T / (norm_one * norm_inf)
+    scale = F32(1.0) / (norm_one * norm_inf)
     count = pivot.shape[0]
     one = lax.broadcasted_iota(jnp.int32, pivot.shape, 0) == lax.broadcasted_iota(jnp.int32, pivot.shape, 1)
-    rest = jnp.where(one, F32(1.0), F32(0.0)) - product(approx, pivot)
+    rest = jnp.where(one, F32(1.0), F32(0.0)) - square * scale
+    approx = turned * scale
     for step in range(NEWTON - 2):
         both = product(rest, jnp.concatenate([rest, approx], axis=1))
         rest, approx = both[:, :count], approx + both[:, count:]
     return approx + product(rest, approx)
-
-
-def newton_below(pivot, below):
-    approx = nearly(pivot)
-    count = pivot.shape[0]
-    both = product(jnp.concatenate([pivot, below], axis=0), approx)
-    stacked = jnp.concatenate([approx, both[count:]], axis=0)
-    return 2.0 * stacked - product(stacked, both[:count])
 
 
 def newton_beside(pivot, beside):
@@ -257,14 +252,14 @@
     half = half_ref.shape[0]
     pivots_ref[pl.ds(aligned(core, half), half), :] = half_ref[...]
     place_pieces(row, 1 - core, other_ref, pivots_ref, rows, 0)
-    inverse_ref[...] = newton_below(pivots_ref[:half, :half], pivots_ref[half:, :half])
+    inverse_ref[...] = newton_beside(pivots_ref[:half, :half], pivots_ref[:half, half:])
 
 
 def second_kernel(pivots_ref, inverse_first_ref, inverse_ref):
     half = inverse_ref.shape[0]
-    below = inverse_first_ref[half:, :]
-    pivot = pivots_ref[half:, half:] - product(below, pivots_ref[:half, half:])
-    inverse_ref[...] = newton_beside(pivot, -below)
+    corner = pivots_ref[half:, :half]
+    pivot = pivots_ref[half:, half:] - product(corner, inverse_first_ref[:, half:])
+    inverse_ref[...] = newton_beside(pivot, -product(corner, inverse_first_ref[:, :half]))
 
 
 def schur_kernel(panel_ref, own_diagonal_ref, coupling_ref, turned_ref, keep_ref, send_ref):
@@ -312,7 +307,7 @@
     for ref in got:
         rows = rows + decode(ref, 0, panel, TAIL)[0]
     first, second = rows[:half], rows[half:]
-    first_out[...] = product(inverse_first_ref[:half, :], first).T[:, None, :]
+    first_out[...] = product(inverse_first_ref[:, :half], first).T[:, None, :]
     second_out[...] = product(inverse_second_ref[...], jnp.concatenate([second, first], axis=0)).T[:, None, :]
 
 
@@ -451,7 +446,7 @@
         functools.partial(own_kernel, rows), shape((panel // 2, panel), F32), joined
     )
     inverse_first, pivots = call(
-        functools.partial(first_kernel, rows), (shape((panel, half), F32), shape((panel, panel), F32)),
+        functools.partial(first_kernel, rows), (shape((half, panel), F32), shape((panel, panel), F32)),
         own_half, other, micros=4.5,
     )
     inverse_second = call(second_kernel, shape((half, panel), F32), pivots, inverse_first, micros=4.5)

time: 60.8 us -> 60.4 us (level)
  transfers between devices with their start and end apart: 19 -> 19, of which waited for: 12 -> 12; matrix products, arithmetic and copies ran while one was open for 0% -> 0% of each run, Pallas kernels for 27% -> 26%
where the time goes in v11:
time: 60.4 us; the launch traced here: 60.2 us
  starting transfers between devices  22.7 us (38%)
  Pallas kernels  19 us (31%)
  waiting for transfers between devices  17.7 us (29%)
  between operations  0.83 us (1%)
    ppermute x19, starting transfers between devices, swap(): return lax.ppermute(x, axis, [(i, i ^ bit) for i in range(count)])  22.7 us
    pallas_call x18, Pallas kernels, call(): pl.pallas_call(kernel, name=getattr(kernel, 'func', kernel).__name__, out...  19 us
    ppermute x19, waiting for transfers between devices, swap(): return lax.ppermute(x, axis, [(i, i ^ bit) for i in range(count)])  17.7 us
  transfers between devices with their start and end apart: 19, of which 12 were waited for; matrix products, arithmetic and copies ran while one was open for 0% of the time, Pallas kernels for 26%

profile of v11, /device:TPU:0, one launch (start us, length us, event | category | flops | bytes accessed | tf_op | source)
XLA Modules:
  0.0 60.2 jit_solution(9748565390059074425)
XLA Ops:
  0.6 1.2 %turn_kernel.1 = (bf16[256,384]{1,0:T(8,128)(2,1)S(1)}, bf16[256,384]{1,0:T(8,128)(2,1)S(1)}) custom-call(bf16[384,512]{1,0:T(8,128)(2,1)} %bitcast.7), custom_call_target="tpu_custom_call" | custom-call | bytes 1024 | tf_op jit(solution)/shard_map/turn_kernel/pallas_call | solution.py:319
  1.8 3.0 %collective-permute-start.1 = (bf16[256,384]{1,0:T(8,128)(2,1)S(1)}, bf16[256,384]{1,0:T(8,128)(2,1)S(1)}, u32[]{:S(2)}, u32[]{:S(2)}) collective-permute-start(bf16[256,384]{1,0:T(8,128)(2,1)S(1)} %get-tuple-element.37.refs_1_), channel_id=1, source_target_pairs={{0,1},{1,0},{2,3},{3,2},{4,5},{5,4},{6,7},{7,6},{8,9},{9,8},{10,11... | collective-permute-start | bytes 589832 | tf_op jit(solution)/shard_map/ppermute | solution.py:334
  4.8 1.5 %collective-permute-start.2 = (bf16[256,384]{1,0:T(8,128)(2,1)S(1)}, bf16[256,384]{1,0:T(8,128)(2,1)S(1)}, u32[]{:S(2)}, u32[]{:S(2)}) collective-permute-start(bf16[256,384]{1,0:T(8,128)(2,1)S(1)} %get-tuple-element.36.refs_0_), channel_id=1, source_target_pairs={{0,2},{1,3},{2,0},{3,1},{4,6},{5,7},{6,4},{7,5},{8,10},{9,11},{10,... | collective-permute-start | bytes 589832 | tf_op jit(solution)/shard_map/ppermute | solution.py:334
  6.3 0.5 collective-permute-start
  6.9 0.1 collective-permute-start.3
  6.9 2.6 %pick_kernel.1 = (bf16[1536,512]{1,0:T(8,128)(2,1)S(1)}, f32[8,512]{1,0:T(8,128)S(1)}, bf16[1024,512]{1,0:T(8,128)(2,1)S(1)}, s32[1,512]{1,0:T(1,128)S(1)}, f32[1,128]{1,0:T(1,128)S(1)}) custom-call(s32[1,512]{1,0:T(1,128)} %bitcast.8, f32[1,128]{1,0:T(1,128)} %bitcast.9, bf16[1536,1024]{1,0:T(8,128)(2,1)} %bitcast.4), custom_call_target="tpu_custom_call" | custom-call | bytes 1024 | tf_op jit(solution)/shard_map/pick_kernel/pallas_call | solution.py:319
  9.6 1.0 %collective-permute-done.1.refs_3_ = bf16[256,384]{1,0:T(8,128)(2,1)S(1)} collective-permute-done((bf16[256,384]{1,0:T(8,128)(2,1)S(1)}, bf16[256,384]{1,0:T(8,128)(2,1)S(1)}, u32[]{:S(2)}, u32[]{:S(2)}) %collective-permute-start.1) | collective-permute-done | bytes 196640 | tf_op jit(solution)/shard_map/ppermute | solution.py:334
  10.5 2.1 %collective-permute-done.2.refs_4_ = bf16[256,384]{1,0:T(8,128)(2,1)S(1)} collective-permute-done((bf16[256,384]{1,0:T(8,128)(2,1)S(1)}, bf16[256,384]{1,0:T(8,128)(2,1)S(1)}, u32[]{:S(2)}, u32[]{:S(2)}) %collective-permute-start.2) | collective-permute-done | bytes 196640 | tf_op jit(solution)/shard_map/ppermute | solution.py:334
  12.6 0.0 collective-permute-start.4
  12.7 2.0 %collective-permute-start.5 = (bf16[256,384]{1,0:T(8,128)(2,1)S(1)}, bf16[256,384]{1,0:T(8,128)(2,1)S(1)}, u32[]{:S(2)}, u32[]{:S(2)}) collective-permute-start(bf16[256,384]{1,0:T(8,128)(2,1)S(1)} %collective-permute-done.1.refs_3_), channel_id=1, source_target_pairs={{0,2},{1,3},{2,0},{3,1},{4,6},{5,7},{6,4},{7,5},{8,10},{9,11},{10,... | collective-permute-start | bytes 589832 | tf_op jit(solution)/shard_map/ppermute | solution.py:334
  14.7 2.3 %rest_kernel.1.chosen_ref = bf16[1536,512]{1,0:T(8,128)(2,1)S(1)} custom-call(bf16[1536,512]{1,0:T(8,128)(2,1)S(1)} %get-tuple-element.34.chosen_in, bf16[1024,512]{1,0:T(8,128)(2,1)S(1)} %get-tuple-element.35.one_ref, bf16[1536,1024]{1,0:T(8,128)(2,1)} %bitcast.5), custom_call_target="tpu_custom_call", output_to_operand_aliasing={{}: (0, {})} | custom-call | bytes 1024 | tf_op jit(solution)/shard_map/rest_kernel/pallas_call | solution.py:319
  17.0 0.0 collective-permute-done.refs_2_
  17.0 0.0 collective-permute-done.3.refs_5_
  17.0 1.1 %early_kernel.1 = (bf16[512,1536]{1,0:T(8,128)(2,1)S(1)}, f32[512,512]{1,0:T(8,128)S(1)}) custom-call(bf16[1536,512]{1,0:T(8,128)(2,1)S(1)} %rest_kernel.1.chosen_ref, bf16[256,384]{1,0:T(8,128)(2,1)S(1)} %get-tuple-element.36.refs_0_, bf16[256,384]{1,0:T(8,128)(2,1)S(1)} %get-tuple-element.37.refs_1_, bf16[256,384]{1,0:T(8,128)(2,1)S(1)} %collective-permute-done.refs_2_, ...), custom_call_target="tpu_custom_call" | custom-call | bytes 1024 | tf_op jit(solution)/shard_map/early_kernel/pallas_call | solution.py:319
  18.1 0.2 collective-permute-done.4.refs_0_
  18.3 1.3 %collective-permute-done.5.refs_1_ = bf16[256,384]{1,0:T(8,128)(2,1)S(1)} collective-permute-done((bf16[256,384]{1,0:T(8,128)(2,1)S(1)}, bf16[256,384]{1,0:T(8,128)(2,1)S(1)}, u32[]{:S(2)}, u32[]{:S(2)}) %collective-permute-start.5) | collective-permute-done | bytes 196640 | tf_op jit(solution)/shard_map/ppermute | solution.py:334
  19.6 0.3 send_kernel.1
  19.9 0.1 collective-permute-start.6
  20.0 0.0 copy-start
  20.0 0.4 keep_kernel.1
  20.4 1.5 %collective-permute-done.6.got_ref = f32[264,512]{1,0:T(8,128)S(1)} collective-permute-done((f32[264,512]{1,0:T(8,128)S(1)}, f32[264,512]{1,0:T(8,128)S(1)}, u32[]{:S(2)}, u32[]{:S(2)}) %collective-permute-start.6) | collective-permute-done | bytes 540704 | tf_op jit(solution)/shard_map/ppermute | solution.py:334
  21.9 0.2 pair_kernel.1
  22.1 1.8 %collective-permute-start.7 = (s16[72,512]{1,0:T(8,128)(2,1)S(1)}, s16[72,512]{1,0:T(8,128)(2,1)S(1)}, u32[]{:S(2)}, u32[]{:S(2)}) collective-permute-start(s16[72,512]{1,0:T(8,128)(2,1)S(1)} %get-tuple-element.51), channel_id=1, source_target_pairs={{0,3},{1,2},{2,1},{3,0},{4,7},{5,6},{6,5},{7,4},{8,11},{9,10},{10,... | collective-permute-start | bytes 221192 | tf_op jit(solution)/shard_map/ppermute | solution.py:334
  23.9 0.5 collective-permute-start.8
  24.4 1.3 %collective-permute-start.9 = (s16[72,512]{1,0:T(8,128)(2,1)S(1)}, s16[72,512]{1,0:T(8,128)(2,1)S(1)}, u32[]{:S(2)}, u32[]{:S(2)}) collective-permute-start(s16[72,512]{1,0:T(8,128)(2,1)S(1)} %get-tuple-element.53), channel_id=1, source_target_pairs={{0,1},{1,0},{2,3},{3,2},{4,5},{5,4},{6,7},{7,6},{8,9},{9,8},{10,11... | collective-permute-start | bytes 221192 | tf_op jit(solution)/shard_map/ppermute | solution.py:334
  25.6 0.0 copy-done
  25.7 1.8 %schur_kernel.1 = (f32[2048,128]{1,0:T(8,128)S(1)}, f32[2048,128]{1,0:T(8,128)S(1)}) custom-call(s32[1,512]{1,0:T(1,128)S(1)} %get-tuple-element.45.panel_ref, f32[1,128]{1,0:T(1,128)S(1)} %get-tuple-element.46.own_diagonal_ref, bf16[1536,1024]{1,0:T(8,128)(2,1)S(1)} %bitcast.6, bf16[512,1536]{1,0:T(8,128)(2,1)S(1)} %get-tuple-element.48.turned_ref), custom_call_target="tpu_custom_call" | custom-call | bytes 1024 | tf_op jit(solution)/shard_map/schur_kernel/pallas_call | solution.py:319
  27.5 0.0 collective-permute-done.7.refs_1_
  27.5 1.5 %collective-permute-done.8.refs_2_ = s16[72,512]{1,0:T(8,128)(2,1)S(1)} collective-permute-done((s16[72,512]{1,0:T(8,128)(2,1)S(1)}, s16[72,512]{1,0:T(8,128)(2,1)S(1)}, u32[]{:S(2)}, u32[]{:S(2)}) %collective-permute-start.8) | collective-permute-done | bytes 73760 | tf_op jit(solution)/shard_map/ppermute | solution.py:334
  28.9 0.1 collective-permute-done.9.refs_3_
  29.0 0.1 sum_kernel.3.refs_0_
  29.1 0.1 collective-permute-start.11
  29.2 1.6 %collective-permute-start.10 = (s16[72,512]{1,0:T(8,128)(2,1)S(1)}, s16[72,512]{1,0:T(8,128)(2,1)S(1)}, u32[]{:S(2)}, u32[]{:S(2)}) collective-permute-start(s16[72,512]{1,0:T(8,128)(2,1)S(1)} %sum_kernel.3.refs_0_), channel_id=1, source_target_pairs={{0,8},{4,12},{8,0},{12,4},{16,24},{20,28},{24,16},{28,20},{1,9},{5... | collective-permute-start | bytes 221192 | tf_op jit(solution)/shard_map/ppermute | solution.py:334
  30.9 3.0 %collective-permute-done.10.refs_1_ = s16[72,512]{1,0:T(8,128)(2,1)S(1)} collective-permute-done((s16[72,512]{1,0:T(8,128)(2,1)S(1)}, s16[72,512]{1,0:T(8,128)(2,1)S(1)}, u32[]{:S(2)}, u32[]{:S(2)}) %collective-permute-start.10) | collective-permute-done | bytes 73760 | tf_op jit(solution)/shard_map/ppermute | solution.py:334
  33.9 0.1 sum_kernel.4.refs_0_
  34.0 2.7 %collective-permute-start.12 = (s16[72,512]{1,0:T(8,128)(2,1)S(1)}, s16[72,512]{1,0:T(8,128)(2,1)S(1)}, u32[]{:S(2)}, u32[]{:S(2)}) collective-permute-start(s16[72,512]{1,0:T(8,128)(2,1)S(1)} %sum_kernel.4.refs_0_), channel_id=1, source_target_pairs={{0,16},{4,20},{8,24},{12,28},{16,0},{20,4},{24,8},{28,12},{1,17},{... | collective-permute-start | bytes 221192 | tf_op jit(solution)/shard_map/ppermute | solution.py:334
  36.7 0.0 collective-permute-done.11.got_ref
  36.7 0.2 bulk_pair_kernel.1
  36.9 3.7 %collective-permute-done.12.refs_1_ = s16[72,512]{1,0:T(8,128)(2,1)S(1)} collective-permute-done((s16[72,512]{1,0:T(8,128)(2,1)S(1)}, s16[72,512]{1,0:T(8,128)(2,1)S(1)}, u32[]{:S(2)}, u32[]{:S(2)}) %collective-permute-start.12) | collective-permute-done | bytes 73760 | tf_op jit(solution)/shard_map/ppermute | solution.py:334
  40.6 0.1 sum_kernel.5.refs_0_
  40.7 0.5 collective-permute-start.16
  41.2 2.0 %collective-permute-start.15 = (s16[72,512]{1,0:T(8,128)(2,1)S(1)}, s16[72,512]{1,0:T(8,128)(2,1)S(1)}, u32[]{:S(2)}, u32[]{:S(2)}) collective-permute-start(s16[72,512]{1,0:T(8,128)(2,1)S(1)} %sum_kernel.5.refs_0_), channel_id=1, source_target_pairs={{0,3},{1,2},{2,1},{3,0},{4,7},{5,6},{6,5},{7,4},{8,11},{9,10},{10,... | collective-permute-start | bytes 221192 | tf_op jit(solution)/shard_map/ppermute | solution.py:334
  43.2 0.5 collective-permute-start.14
  43.7 1.0 %collective-permute-start.13 = (s16[72,512]{1,0:T(8,128)(2,1)S(1)}, s16[72,512]{1,0:T(8,128)(2,1)S(1)}, u32[]{:S(2)}, u32[]{:S(2)}) collective-permute-start(s16[72,512]{1,0:T(8,128)(2,1)S(1)} %sum_kernel.5.refs_0_), channel_id=1, source_target_pairs={{0,1},{1,0},{2,3},{3,2},{4,5},{5,4},{6,7},{7,6},{8,9},{9,8},{10,11... | collective-permute-start | bytes 221192 | tf_op jit(solution)/shard_map/ppermute | solution.py:334
  44.7 1.8 %collective-permute-done.15.refs_3_ = s16[72,512]{1,0:T(8,128)(2,1)S(1)} collective-permute-done((s16[72,512]{1,0:T(8,128)(2,1)S(1)}, s16[72,512]{1,0:T(8,128)(2,1)S(1)}, u32[]{:S(2)}, u32[]{:S(2)}) %collective-permute-start.15) | collective-permute-done | bytes 73760 | tf_op jit(solution)/shard_map/ppermute | solution.py:334
  46.5 1.0 %collective-permute-done.14.refs_2_ = s16[72,512]{1,0:T(8,128)(2,1)S(1)} collective-permute-done((s16[72,512]{1,0:T(8,128)(2,1)S(1)}, s16[72,512]{1,0:T(8,128)(2,1)S(1)}, u32[]{:S(2)}, u32[]{:S(2)}) %collective-permute-start.14) | collective-permute-done | bytes 73760 | tf_op jit(solution)/shard_map/ppermute | solution.py:334
  47.5 0.5 collective-permute-done.13.refs_1_
  48.1 0.0 collective-permute-done.16.got_ref
  48.1 0.2 bulk_sum_kernel.1
  48.3 0.1 collective-permute-start.17
  48.3 3.4 %collective-permute-start.18 = (s16[528,128]{1,0:T(8,128)(2,1)S(1)}, s16[528,128]{1,0:T(8,128)(2,1)S(1)}, u32[]{:S(2)}, u32[]{:S(2)}) collective-permute-start(s16[528,128]{1,0:T(8,128)(2,1)S(1)} %get-tuple-element.61), channel_id=1, source_target_pairs={{0,16},{4,20},{8,24},{12,28},{16,0},{20,4},{24,8},{28,12},{1,17},{... | collective-permute-start | bytes 405512 | tf_op jit(solution)/shard_map/ppermute | solution.py:334
  51.8 0.2 own_kernel.1.half_ref
  52.0 0.0 collective-permute-done.17.other_ref
  52.0 3.4 %first_kernel.1 = (f32[256,512]{1,0:T(8,128)S(1)}, f32[512,512]{1,0:T(8,128)S(1)}) custom-call(f32[256,512]{1,0:T(8,128)S(1)} %own_kernel.1.half_ref, s16[320,512]{1,0:T(8,128)(2,1)S(1)} %collective-permute-done.17.other_ref), custom_call_target="tpu_custom_call" | custom-call | bytes 16606024 | tf_op jit(solution)/shard_map/first_kernel/pallas_call | solution.py:319
  55.4 3.6 %second_kernel.1.inverse_second_ref = f32[256,512]{1,0:T(8,128)S(1)} custom-call(f32[512,512]{1,0:T(8,128)S(1)} %get-tuple-element.64.pivots_ref, f32[256,512]{1,0:T(8,128)S(1)} %get-tuple-element.63.inverse_first_ref), custom_call_target="tpu_custom_call" | custom-call | bytes 16606024 | tf_op jit(solution)/shard_map/second_kernel/pallas_call | solution.py:319
  59.0 0.0 collective-permute-done.18.refs_0_
  59.0 1.2 %factor_kernel.1 = (f32[128,1,256]{2,1,0:T(1,128)}, f32[128,1,256]{2,1,0:T(1,128)}) custom-call(f32[256,512]{1,0:T(8,128)S(1)} %get-tuple-element.63.inverse_first_ref, f32[256,512]{1,0:T(8,128)S(1)} %second_kernel.1.inverse_second_ref, f32[512,128]{1,0:T(8,128)S(1)} %get-tuple-element.65.rows_ref, s16[528,128]{1,0:T(8,128)(2,1)S(1)} %collective-permute-done.18.refs_0_), custom_call_target="tpu_custom_call" | custom-call | bytes 1024 | tf_op jit(solution)/shard_map/factor_kernel/pallas_call | solution.py:319
  (1 shorter events, 0.0 us)
Async XLA Ops:
  1.8 8.7 %collective-permute-start.1 = (bf16[256,384]{1,0:T(8,128)(2,1)S(1)}, bf16[256,384]{1,0:T(8,128)(2,1)S(1)}, u32[]{:S(2)}, u32[]{:S(2)}) collective-permute-start(bf16[256,384]{1,0:T(8,128)(2,1)S(1)} %get-tuple-element.37.refs_1_), channel_id=1, source_target_pairs={{0,1},{1,0},{2,3},{3,2},{4,5},{5,4},{6,7},{7,6},{8,9},{9,8},{10,11... | collective-permute-start | bytes 589832 | tf_op jit(solution)/shard_map/ppermute | solution.py:334
  4.8 7.8 %collective-permute-start.2 = (bf16[256,384]{1,0:T(8,128)(2,1)S(1)}, bf16[256,384]{1,0:T(8,128)(2,1)S(1)}, u32[]{:S(2)}, u32[]{:S(2)}) collective-permute-start(bf16[256,384]{1,0:T(8,128)(2,1)S(1)} %get-tuple-element.36.refs_0_), channel_id=1, source_target_pairs={{0,2},{1,3},{2,0},{3,1},{4,6},{5,7},{6,4},{7,5},{8,10},{9,11},{10,... | collective-permute-start | bytes 589832 | tf_op jit(solution)/shard_map/ppermute | solution.py:334
  6.3 10.7 %collective-permute-start = (bf16[256,384]{1,0:T(8,128)(2,1)S(1)}, bf16[256,384]{1,0:T(8,128)(2,1)S(1)}, u32[]{:S(2)}, u32[]{:S(2)}) collective-permute-start(bf16[256,384]{1,0:T(8,128)(2,1)S(1)} %get-tuple-element.36.refs_0_), channel_id=1, source_target_pairs={{0,1},{1,0},{2,3},{3,2},{4,5},{5,4},{6,7},{7,6},{8,9},{9,8},{10,11... | collective-permute-start | bytes 589832 | tf_op jit(solution)/shard_map/ppermute | solution.py:334
  6.9 10.1 %collective-permute-start.3 = (bf16[256,384]{1,0:T(8,128)(2,1)S(1)}, bf16[256,384]{1,0:T(8,128)(2,1)S(1)}, u32[]{:S(2)}, u32[]{:S(2)}) collective-permute-start(bf16[256,384]{1,0:T(8,128)(2,1)S(1)} %get-tuple-element.37.refs_1_), channel_id=1, source_target_pairs={{0,2},{1,3},{2,0},{3,1},{4,6},{5,7},{6,4},{7,5},{8,10},{9,11},{10,... | collective-permute-start | bytes 589832 | tf_op jit(solution)/shard_map/ppermute | solution.py:334
  12.6 5.7 %collective-permute-start.4 = (bf16[256,384]{1,0:T(8,128)(2,1)S(1)}, bf16[256,384]{1,0:T(8,128)(2,1)S(1)}, u32[]{:S(2)}, u32[]{:S(2)}) collective-permute-start(bf16[256,384]{1,0:T(8,128)(2,1)S(1)} %collective-permute-done.2.refs_4_), channel_id=1, source_target_pairs={{0,1},{1,0},{2,3},{3,2},{4,5},{5,4},{6,7},{7,6},{8,9},{9,8},{10,11... | collective-permute-start | bytes 589832 | tf_op jit(solution)/shard_map/ppermute | solution.py:334
  12.7 6.9 %collective-permute-start.5 = (bf16[256,384]{1,0:T(8,128)(2,1)S(1)}, bf16[256,384]{1,0:T(8,128)(2,1)S(1)}, u32[]{:S(2)}, u32[]{:S(2)}) collective-permute-start(bf16[256,384]{1,0:T(8,128)(2,1)S(1)} %collective-permute-done.1.refs_3_), channel_id=1, source_target_pairs={{0,2},{1,3},{2,0},{3,1},{4,6},{5,7},{6,4},{7,5},{8,10},{9,11},{10,... | collective-permute-start | bytes 589832 | tf_op jit(solution)/shard_map/ppermute | solution.py:334
  19.9 2.0 %collective-permute-start.6 = (f32[264,512]{1,0:T(8,128)S(1)}, f32[264,512]{1,0:T(8,128)S(1)}, u32[]{:S(2)}, u32[]{:S(2)}) collective-permute-start(f32[264,512]{1,0:T(8,128)S(1)} %send_kernel.1), channel_id=1, source_target_pairs={{0,4},{4,0},{8,12},{12,8},{16,20},{20,16},{24,28},{28,24},{1,5},{5... | collective-permute-start | bytes 1622024 | tf_op jit(solution)/shard_map/ppermute | solution.py:334
  20.0 5.6 %copy-start = (bf16[1,1536,1024]{2,1,0:T(8,128)(2,1)S(1)}, bf16[1,1536,1024]{2,1,0:T(8,128)(2,1)}, u32[]{:S(2)}) copy-start(bf16[1,1536,1024]{2,1,0:T(8,128)(2,1)} %param.4) | copy-start | bytes 9437188
  22.1 5.4 %collective-permute-start.7 = (s16[72,512]{1,0:T(8,128)(2,1)S(1)}, s16[72,512]{1,0:T(8,128)(2,1)S(1)}, u32[]{:S(2)}, u32[]{:S(2)}) collective-permute-start(s16[72,512]{1,0:T(8,128)(2,1)S(1)} %get-tuple-element.51), channel_id=1, source_target_pairs={{0,3},{1,2},{2,1},{3,0},{4,7},{5,6},{6,5},{7,4},{8,11},{9,10},{10,... | collective-permute-start | bytes 221192 | tf_op jit(solution)/shard_map/ppermute | solution.py:334
  23.9 5.1 %collective-permute-start.8 = (s16[72,512]{1,0:T(8,128)(2,1)S(1)}, s16[72,512]{1,0:T(8,128)(2,1)S(1)}, u32[]{:S(2)}, u32[]{:S(2)}) collective-permute-start(s16[72,512]{1,0:T(8,128)(2,1)S(1)} %get-tuple-element.52), channel_id=1, source_target_pairs={{0,2},{1,3},{2,0},{3,1},{4,6},{5,7},{6,4},{7,5},{8,10},{9,11},{10,... | collective-permute-start | bytes 221192 | tf_op jit(solution)/shard_map/ppermute | solution.py:334
  24.4 4.6 %collective-permute-start.9 = (s16[72,512]{1,0:T(8,128)(2,1)S(1)}, s16[72,512]{1,0:T(8,128)(2,1)S(1)}, u32[]{:S(2)}, u32[]{:S(2)}) collective-permute-start(s16[72,512]{1,0:T(8,128)(2,1)S(1)} %get-tuple-element.53), channel_id=1, source_target_pairs={{0,1},{1,0},{2,3},{3,2},{4,5},{5,4},{6,7},{7,6},{8,9},{9,8},{10,11... | collective-permute-start | bytes 221192 | tf_op jit(solution)/shard_map/ppermute | solution.py:334
  29.1 7.5 %collective-permute-start.11 = (f32[2048,128]{1,0:T(8,128)S(1)}, f32[2048,128]{1,0:T(8,128)S(1)}, u32[]{:S(2)}, u32[]{:S(2)}) collective-permute-start(f32[2048,128]{1,0:T(8,128)S(1)} %get-tuple-element.56), channel_id=1, source_target_pairs={{0,4},{4,0},{8,12},{12,8},{16,20},{20,16},{24,28},{28,24},{1,5},{5... | collective-permute-start | bytes 3145736 | tf_op jit(solution)/shard_map/ppermute | solution.py:334
  29.2 4.7 %collective-permute-start.10 = (s16[72,512]{1,0:T(8,128)(2,1)S(1)}, s16[72,512]{1,0:T(8,128)(2,1)S(1)}, u32[]{:S(2)}, u32[]{:S(2)}) collective-permute-start(s16[72,512]{1,0:T(8,128)(2,1)S(1)} %sum_kernel.3.refs_0_), channel_id=1, source_target_pairs={{0,8},{4,12},{8,0},{12,4},{16,24},{20,28},{24,16},{28,20},{1,9},{5... | collective-permute-start | bytes 221192 | tf_op jit(solution)/shard_map/ppermute | solution.py:334
  34.0 6.6 %collective-permute-start.12 = (s16[72,512]{1,0:T(8,128)(2,1)S(1)}, s16[72,512]{1,0:T(8,128)(2,1)S(1)}, u32[]{:S(2)}, u32[]{:S(2)}) collective-permute-start(s16[72,512]{1,0:T(8,128)(2,1)S(1)} %sum_kernel.4.refs_0_), channel_id=1, source_target_pairs={{0,16},{4,20},{8,24},{12,28},{16,0},{20,4},{24,8},{28,12},{1,17},{... | collective-permute-start | bytes 221192 | tf_op jit(solution)/shard_map/ppermute | solution.py:334
  40.7 7.4 %collective-permute-start.16 = (s16[1056,128]{1,0:T(8,128)(2,1)S(1)}, s16[1056,128]{1,0:T(8,128)(2,1)S(1)}, u32[]{:S(2)}, u32[]{:S(2)}) collective-permute-start(s16[1056,128]{1,0:T(8,128)(2,1)S(1)} %get-tuple-element.60), channel_id=1, source_target_pairs={{0,8},{4,12},{8,0},{12,4},{16,24},{20,28},{24,16},{28,20},{1,9},{5... | collective-permute-start | bytes 811016 | tf_op jit(solution)/shard_map/ppermute | solution.py:334
  41.2 5.3 %collective-permute-start.15 = (s16[72,512]{1,0:T(8,128)(2,1)S(1)}, s16[72,512]{1,0:T(8,128)(2,1)S(1)}, u32[]{:S(2)}, u32[]{:S(2)}) collective-permute-start(s16[72,512]{1,0:T(8,128)(2,1)S(1)} %sum_kernel.5.refs_0_), channel_id=1, source_target_pairs={{0,3},{1,2},{2,1},{3,0},{4,7},{5,6},{6,5},{7,4},{8,11},{9,10},{10,... | collective-permute-start | bytes 221192 | tf_op jit(solution)/shard_map/ppermute | solution.py:334
  43.2 4.4 %collective-permute-start.14 = (s16[72,512]{1,0:T(8,128)(2,1)S(1)}, s16[72,512]{1,0:T(8,128)(2,1)S(1)}, u32[]{:S(2)}, u32[]{:S(2)}) collective-permute-start(s16[72,512]{1,0:T(8,128)(2,1)S(1)} %sum_kernel.5.refs_0_), channel_id=1, source_target_pairs={{0,2},{1,3},{2,0},{3,1},{4,6},{5,7},{6,4},{7,5},{8,10},{9,11},{10,... | collective-permute-start | bytes 221192 | tf_op jit(solution)/shard_map/ppermute | solution.py:334
  43.7 4.4 %collective-permute-start.13 = (s16[72,512]{1,0:T(8,128)(2,1)S(1)}, s16[72,512]{1,0:T(8,128)(2,1)S(1)}, u32[]{:S(2)}, u32[]{:S(2)}) collective-permute-start(s16[72,512]{1,0:T(8,128)(2,1)S(1)} %sum_kernel.5.refs_0_), channel_id=1, source_target_pairs={{0,1},{1,0},{2,3},{3,2},{4,5},{5,4},{6,7},{7,6},{8,9},{9,8},{10,11... | collective-permute-start | bytes 221192 | tf_op jit(solution)/shard_map/ppermute | solution.py:334
  48.3 3.7 %collective-permute-start.17 = (s16[320,512]{1,0:T(8,128)(2,1)S(1)}, s16[320,512]{1,0:T(8,128)(2,1)S(1)}, u32[]{:S(2)}, u32[]{:S(2)}) collective-permute-start(s16[320,512]{1,0:T(8,128)(2,1)S(1)} %join_kernel.1.own_ref), channel_id=1, source_target_pairs={{0,4},{4,0},{8,12},{12,8},{16,20},{20,16},{24,28},{28,24},{1,5},{5... | collective-permute-start | bytes 983048 | tf_op jit(solution)/shard_map/ppermute | solution.py:334
  48.3 10.6 %collective-permute-start.18 = (s16[528,128]{1,0:T(8,128)(2,1)S(1)}, s16[528,128]{1,0:T(8,128)(2,1)S(1)}, u32[]{:S(2)}, u32[]{:S(2)}) collective-permute-start(s16[528,128]{1,0:T(8,128)(2,1)S(1)} %get-tuple-element.61), channel_id=1, source_target_pairs={{0,16},{4,20},{8,24},{12,28},{16,0},{20,4},{24,8},{28,12},{1,17},{... | collective-permute-start | bytes 405512 | tf_op jit(solution)/shard_map/ppermute | solution.py:334

commit v12 on v11

--- a/solution.py
+++ b/solution.py
@@ -247,19 +247,17 @@
     place_pieces(row, core, own_ref, half_ref, rows, core * half_ref.shape[0])
 
 
-def first_kernel(rows, half_ref, other_ref, inverse_ref, pivots_ref):
+def newton_kernel(rows, half_ref, other_ref, inverse_ref, second_ref, pivots_ref):
     row, core, _ = whereabouts()
     half = half_ref.shape[0]
     pivots_ref[pl.ds(aligned(core, half), half), :] = half_ref[...]
     place_pieces(row, 1 - core, other_ref, pivots_ref, rows, 0)
-    inverse_ref[...] = newton_beside(pivots_ref[:half, :half], pivots_ref[:half, half:])
-
-
-def second_kernel(pivots_ref, inverse_first_ref, inverse_ref):
-    half = inverse_ref.shape[0]
+    both = newton_beside(pivots_ref[:half, :half], pivots_ref[:half, half:])
+    inverse_first = both[:, :half]
+    inverse_ref[...] = inverse_first
     corner = pivots_ref[half:, :half]
-    pivot = pivots_ref[half:, half:] - product(corner, inverse_first_ref[:, half:])
-    inverse_ref[...] = newton_beside(pivot, -product(corner, inverse_first_ref[:, :half]))
+    pivot = pivots_ref[half:, half:] - product(corner, both[:, half:])
+    second_ref[...] = newton_beside(pivot, -product(corner, inverse_first))
 
 
 def schur_kernel(panel_ref, own_diagonal_ref, coupling_ref, turned_ref, keep_ref, send_ref):
@@ -307,7 +305,7 @@
     for ref in got:
         rows = rows + decode(ref, 0, panel, TAIL)[0]
     first, second = rows[:half], rows[half:]
-    first_out[...] = product(inverse_first_ref[:, :half], first).T[:, None, :]
+    first_out[...] = product(inverse_first_ref[...], first).T[:, None, :]
     second_out[...] = product(inverse_second_ref[...], jnp.concatenate([second, first], axis=0)).T[:, None, :]
 
 
@@ -425,12 +423,13 @@
         mine = first_row + jnp.arange(share, dtype=jnp.int32)
         own = own + jnp.where(panel_rows[:, None] == mine[None, :], border_diagonal[:, 0][None, :], F32(0.0))
         part = call(sum_kernel, coded, part, *arrived)
-    for bit in steps:
-        other = swap(part, "scen", 2 * bit)
-        if split and bit == steps[-1]:
-            own, bulk_codes = call(functools.partial(bulk_pair_kernel, panel), halved(count), after(own, part), got)
-            part = after(part, bulk_codes)
-        part = call(sum_kernel, coded, part, other)
+    if split:
+        others = [swap(part, "scen", 2 * k) for k in range(1, layers)]
+        own, bulk_codes = call(functools.partial(bulk_pair_kernel, panel), halved(count), after(own, part), got)
+        part = call(sum_kernel, coded, after(part, bulk_codes), *others)
+    else:
+        for bit in steps:
+            part = call(sum_kernel, coded, part, swap(part, "scen", 2 * bit))
     shared = [swap(part, "row", k) for k in range(1, rows)]
     if split:
         for bit in steps[:-1]:
@@ -445,11 +444,10 @@
     own_half = call(
         functools.partial(own_kernel, rows), shape((panel // 2, panel), F32), joined
     )
-    inverse_first, pivots = call(
-        functools.partial(first_kernel, rows), (shape((half, panel), F32), shape((panel, panel), F32)),
-        own_half, other, micros=4.5,
-    )
-    inverse_second = call(second_kernel, shape((half, panel), F32), pivots, inverse_first, micros=4.5)
+    inverse_first, inverse_second = call(
+        functools.partial(newton_kernel, rows), (shape((half, half), F32), shape((half, panel), F32)),
+        own_half, other, micros=9.0, scratch=[pltpu.VMEM((panel, panel), F32)],
+    )
     out = jax.ShapeDtypeStruct((share, 1, half), F32)
     return call(
         factor_kernel, (out, out),

time: 60.4 us -> 59.4 us (0.983)
  starting transfers between devices: 22.7 us -> 21.9 us
    ppermute x19 -> x20, starting transfers between devices: 22.7 us -> 21.9 us  [swap(): return lax.ppermute(x, axis, [(i, i ^ bit) for i in range(count)])]
    ppermute x19 -> x20, waiting for transfers between devices: 17.7 us -> 17.6 us  [swap(): return lax.ppermute(x, axis, [(i, i ^ bit) for i in range(count)])]
    pallas_call x18 -> x16, Pallas kernels: 19 us -> 18.9 us  [call(): pl.pallas_call(kernel, name=getattr(kernel, 'func', kernel).__name__, out...]
  transfers between devices with their start and end apart: 19 -> 20, of which waited for: 12 -> 14; matrix products, arithmetic and copies ran while one was open for 0% -> 0% of each run, Pallas kernels for 26% -> 26%
where the time goes in v12:
time: 59.4 us; the launch traced here: 59.2 us
  starting transfers between devices  21.9 us (37%)
  Pallas kernels  18.9 us (32%)
  waiting for transfers between devices  17.6 us (30%)
  between operations  0.81 us (1%)
    ppermute x20, starting transfers between devices, swap(): return lax.ppermute(x, axis, [(i, i ^ bit) for i in range(count)])  21.9 us
    pallas_call x16, Pallas kernels, call(): pl.pallas_call(kernel, name=getattr(kernel, 'func', kernel).__name__, out...  18.9 us
    ppermute x20, waiting for transfers between devices, swap(): return lax.ppermute(x, axis, [(i, i ^ bit) for i in range(count)])  17.6 us
  transfers between devices with their start and end apart: 20, of which 14 were waited for; matrix products, arithmetic and copies ran while one was open for 0% of the time, Pallas kernels for 26%

profile of v12, /device:TPU:0, one launch (start us, length us, event | category | flops | bytes accessed | tf_op | source)
XLA Modules:
  0.0 59.2 jit_solution(15019155610337052977)
XLA Ops:
  0.6 1.2 %turn_kernel.1 = (bf16[256,384]{1,0:T(8,128)(2,1)S(1)}, bf16[256,384]{1,0:T(8,128)(2,1)S(1)}) custom-call(bf16[384,512]{1,0:T(8,128)(2,1)} %bitcast.7), custom_call_target="tpu_custom_call" | custom-call | bytes 1024 | tf_op jit(solution)/shard_map/turn_kernel/pallas_call | solution.py:317
  1.8 3.0 %collective-permute-start.1 = (bf16[256,384]{1,0:T(8,128)(2,1)S(1)}, bf16[256,384]{1,0:T(8,128)(2,1)S(1)}, u32[]{:S(2)}, u32[]{:S(2)}) collective-permute-start(bf16[256,384]{1,0:T(8,128)(2,1)S(1)} %get-tuple-element.37.refs_1_), channel_id=1, source_target_pairs={{0,1},{1,0},{2,3},{3,2},{4,5},{5,4},{6,7},{7,6},{8,9},{9,8},{10,11... | collective-permute-start | bytes 589832 | tf_op jit(solution)/shard_map/ppermute | solution.py:332
  4.8 1.5 %collective-permute-start.2 = (bf16[256,384]{1,0:T(8,128)(2,1)S(1)}, bf16[256,384]{1,0:T(8,128)(2,1)S(1)}, u32[]{:S(2)}, u32[]{:S(2)}) collective-permute-start(bf16[256,384]{1,0:T(8,128)(2,1)S(1)} %get-tuple-element.36.refs_0_), channel_id=1, source_target_pairs={{0,2},{1,3},{2,0},{3,1},{4,6},{5,7},{6,4},{7,5},{8,10},{9,11},{10,... | collective-permute-start | bytes 589832 | tf_op jit(solution)/shard_map/ppermute | solution.py:332
  6.3 0.5 collective-permute-start
  6.9 0.1 collective-permute-start.3
  6.9 2.6 %pick_kernel.1 = (bf16[1536,512]{1,0:T(8,128)(2,1)S(1)}, f32[8,512]{1,0:T(8,128)S(1)}, bf16[1024,512]{1,0:T(8,128)(2,1)S(1)}, s32[1,512]{1,0:T(1,128)S(1)}, f32[1,128]{1,0:T(1,128)S(1)}) custom-call(s32[1,512]{1,0:T(1,128)} %bitcast.8, f32[1,128]{1,0:T(1,128)} %bitcast.9, bf16[1536,1024]{1,0:T(8,128)(2,1)} %bitcast.4), custom_call_target="tpu_custom_call" | custom-call | bytes 1024 | tf_op jit(solution)/shard_map/pick_kernel/pallas_call | solution.py:317
  9.6 1.0 %collective-permute-done.1.refs_3_ = bf16[256,384]{1,0:T(8,128)(2,1)S(1)} collective-permute-done((bf16[256,384]{1,0:T(8,128)(2,1)S(1)}, bf16[256,384]{1,0:T(8,128)(2,1)S(1)}, u32[]{:S(2)}, u32[]{:S(2)}) %collective-permute-start.1) | collective-permute-done | bytes 196640 | tf_op jit(solution)/shard_map/ppermute | solution.py:332
  10.5 2.1 %collective-permute-done.2.refs_4_ = bf16[256,384]{1,0:T(8,128)(2,1)S(1)} collective-permute-done((bf16[256,384]{1,0:T(8,128)(2,1)S(1)}, bf16[256,384]{1,0:T(8,128)(2,1)S(1)}, u32[]{:S(2)}, u32[]{:S(2)}) %collective-permute-start.2) | collective-permute-done | bytes 196640 | tf_op jit(solution)/shard_map/ppermute | solution.py:332
  12.6 0.0 collective-permute-start.4
  12.7 2.0 %collective-permute-start.5 = (bf16[256,384]{1,0:T(8,128)(2,1)S(1)}, bf16[256,384]{1,0:T(8,128)(2,1)S(1)}, u32[]{:S(2)}, u32[]{:S(2)}) collective-permute-start(bf16[256,384]{1,0:T(8,128)(2,1)S(1)} %collective-permute-done.1.refs_3_), channel_id=1, source_target_pairs={{0,2},{1,3},{2,0},{3,1},{4,6},{5,7},{6,4},{7,5},{8,10},{9,11},{10,... | collective-permute-start | bytes 589832 | tf_op jit(solution)/shard_map/ppermute | solution.py:332
  14.7 2.3 %rest_kernel.1.chosen_ref = bf16[1536,512]{1,0:T(8,128)(2,1)S(1)} custom-call(bf16[1536,512]{1,0:T(8,128)(2,1)S(1)} %get-tuple-element.34.chosen_in, bf16[1024,512]{1,0:T(8,128)(2,1)S(1)} %get-tuple-element.35.one_ref, bf16[1536,1024]{1,0:T(8,128)(2,1)} %bitcast.5), custom_call_target="tpu_custom_call", output_to_operand_aliasing={{}: (0, {})} | custom-call | bytes 1024 | tf_op jit(solution)/shard_map/rest_kernel/pallas_call | solution.py:317
  17.0 0.0 collective-permute-done.refs_2_
  17.0 0.0 collective-permute-done.3.refs_5_
  17.0 1.1 %early_kernel.1 = (bf16[512,1536]{1,0:T(8,128)(2,1)S(1)}, f32[512,512]{1,0:T(8,128)S(1)}) custom-call(bf16[1536,512]{1,0:T(8,128)(2,1)S(1)} %rest_kernel.1.chosen_ref, bf16[256,384]{1,0:T(8,128)(2,1)S(1)} %get-tuple-element.36.refs_0_, bf16[256,384]{1,0:T(8,128)(2,1)S(1)} %get-tuple-element.37.refs_1_, bf16[256,384]{1,0:T(8,128)(2,1)S(1)} %collective-permute-done.refs_2_, ...), custom_call_target="tpu_custom_call" | custom-call | bytes 1024 | tf_op jit(solution)/shard_map/early_kernel/pallas_call | solution.py:317
  18.1 0.2 collective-permute-done.4.refs_0_
  18.3 1.3 %collective-permute-done.5.refs_1_ = bf16[256,384]{1,0:T(8,128)(2,1)S(1)} collective-permute-done((bf16[256,384]{1,0:T(8,128)(2,1)S(1)}, bf16[256,384]{1,0:T(8,128)(2,1)S(1)}, u32[]{:S(2)}, u32[]{:S(2)}) %collective-permute-start.5) | collective-permute-done | bytes 196640 | tf_op jit(solution)/shard_map/ppermute | solution.py:332
  19.6 0.3 send_kernel.1
  19.9 0.1 collective-permute-start.6
  20.0 0.0 copy-start
  20.0 0.4 keep_kernel.1
  20.4 1.5 %collective-permute-done.6.got_ref = f32[264,512]{1,0:T(8,128)S(1)} collective-permute-done((f32[264,512]{1,0:T(8,128)S(1)}, f32[264,512]{1,0:T(8,128)S(1)}, u32[]{:S(2)}, u32[]{:S(2)}) %collective-permute-start.6) | collective-permute-done | bytes 540704 | tf_op jit(solution)/shard_map/ppermute | solution.py:332
  21.9 0.2 pair_kernel.1
  22.1 1.8 %collective-permute-start.7 = (s16[72,512]{1,0:T(8,128)(2,1)S(1)}, s16[72,512]{1,0:T(8,128)(2,1)S(1)}, u32[]{:S(2)}, u32[]{:S(2)}) collective-permute-start(s16[72,512]{1,0:T(8,128)(2,1)S(1)} %get-tuple-element.51), channel_id=1, source_target_pairs={{0,3},{1,2},{2,1},{3,0},{4,7},{5,6},{6,5},{7,4},{8,11},{9,10},{10,... | collective-permute-start | bytes 221192 | tf_op jit(solution)/shard_map/ppermute | solution.py:332
  23.9 0.5 collective-permute-start.8
  24.4 1.3 %collective-permute-start.9 = (s16[72,512]{1,0:T(8,128)(2,1)S(1)}, s16[72,512]{1,0:T(8,128)(2,1)S(1)}, u32[]{:S(2)}, u32[]{:S(2)}) collective-permute-start(s16[72,512]{1,0:T(8,128)(2,1)S(1)} %get-tuple-element.53), channel_id=1, source_target_pairs={{0,1},{1,0},{2,3},{3,2},{4,5},{5,4},{6,7},{7,6},{8,9},{9,8},{10,11... | collective-permute-start | bytes 221192 | tf_op jit(solution)/shard_map/ppermute | solution.py:332
  25.6 0.0 copy-done
  25.7 1.8 %schur_kernel.1 = (f32[2048,128]{1,0:T(8,128)S(1)}, f32[2048,128]{1,0:T(8,128)S(1)}) custom-call(s32[1,512]{1,0:T(1,128)S(1)} %get-tuple-element.45.panel_ref, f32[1,128]{1,0:T(1,128)S(1)} %get-tuple-element.46.own_diagonal_ref, bf16[1536,1024]{1,0:T(8,128)(2,1)S(1)} %bitcast.6, bf16[512,1536]{1,0:T(8,128)(2,1)S(1)} %get-tuple-element.48.turned_ref), custom_call_target="tpu_custom_call" | custom-call | bytes 1024 | tf_op jit(solution)/shard_map/schur_kernel/pallas_call | solution.py:317
  27.5 0.0 collective-permute-done.7.refs_1_
  27.5 1.5 %collective-permute-done.8.refs_2_ = s16[72,512]{1,0:T(8,128)(2,1)S(1)} collective-permute-done((s16[72,512]{1,0:T(8,128)(2,1)S(1)}, s16[72,512]{1,0:T(8,128)(2,1)S(1)}, u32[]{:S(2)}, u32[]{:S(2)}) %collective-permute-start.8) | collective-permute-done | bytes 73760 | tf_op jit(solution)/shard_map/ppermute | solution.py:332
  28.9 0.1 collective-permute-done.9.refs_3_
  29.0 0.1 sum_kernel.2.refs_0_
  29.1 0.1 collective-permute-start.10
  29.2 3.7 %collective-permute-start.13 = (s16[72,512]{1,0:T(8,128)(2,1)S(1)}, s16[72,512]{1,0:T(8,128)(2,1)S(1)}, u32[]{:S(2)}, u32[]{:S(2)}) collective-permute-start(s16[72,512]{1,0:T(8,128)(2,1)S(1)} %sum_kernel.2.refs_0_), channel_id=1, source_target_pairs={{0,24},{4,28},{8,16},{12,20},{16,8},{20,12},{24,0},{28,4},{1,25},{... | collective-permute-start | bytes 221192 | tf_op jit(solution)/shard_map/ppermute | solution.py:332
  32.9 0.0 collective-permute-start.12
  32.9 0.8 %collective-permute-start.11 = (s16[72,512]{1,0:T(8,128)(2,1)S(1)}, s16[72,512]{1,0:T(8,128)(2,1)S(1)}, u32[]{:S(2)}, u32[]{:S(2)}) collective-permute-start(s16[72,512]{1,0:T(8,128)(2,1)S(1)} %sum_kernel.2.refs_0_), channel_id=1, source_target_pairs={{0,8},{4,12},{8,0},{12,4},{16,24},{20,28},{24,16},{28,20},{1,9},{5... | collective-permute-start | bytes 221192 | tf_op jit(solution)/shard_map/ppermute | solution.py:332
  33.7 0.0 collective-permute-done.10.got_ref
  33.7 0.2 bulk_pair_kernel.1
  33.9 2.2 %collective-permute-done.13.refs_3_ = s16[72,512]{1,0:T(8,128)(2,1)S(1)} collective-permute-done((s16[72,512]{1,0:T(8,128)(2,1)S(1)}, s16[72,512]{1,0:T(8,128)(2,1)S(1)}, u32[]{:S(2)}, u32[]{:S(2)}) %collective-permute-start.13) | collective-permute-done | bytes 73760 | tf_op jit(solution)/shard_map/ppermute | solution.py:332
  36.1 3.5 %collective-permute-done.12.refs_2_ = s16[72,512]{1,0:T(8,128)(2,1)S(1)} collective-permute-done((s16[72,512]{1,0:T(8,128)(2,1)S(1)}, s16[72,512]{1,0:T(8,128)(2,1)S(1)}, u32[]{:S(2)}, u32[]{:S(2)}) %collective-permute-start.12) | collective-permute-done | bytes 73760 | tf_op jit(solution)/shard_map/ppermute | solution.py:332
  39.7 0.0 collective-permute-done.11.refs_1_
  39.7 0.1 sum_kernel.3.refs_0_
  39.8 1.1 %collective-permute-start.17 = (s16[1056,128]{1,0:T(8,128)(2,1)S(1)}, s16[1056,128]{1,0:T(8,128)(2,1)S(1)}, u32[]{:S(2)}, u32[]{:S(2)}) collective-permute-start(s16[1056,128]{1,0:T(8,128)(2,1)S(1)} %get-tuple-element.60), channel_id=1, source_target_pairs={{0,8},{4,12},{8,0},{12,4},{16,24},{20,28},{24,16},{28,20},{1,9},{5... | collective-permute-start | bytes 811016 | tf_op jit(solution)/shard_map/ppermute | solution.py:332
  40.9 2.0 %collective-permute-start.16 = (s16[72,512]{1,0:T(8,128)(2,1)S(1)}, s16[72,512]{1,0:T(8,128)(2,1)S(1)}, u32[]{:S(2)}, u32[]{:S(2)}) collective-permute-start(s16[72,512]{1,0:T(8,128)(2,1)S(1)} %sum_kernel.3.refs_0_), channel_id=1, source_target_pairs={{0,3},{1,2},{2,1},{3,0},{4,7},{5,6},{6,5},{7,4},{8,11},{9,10},{10,... | collective-permute-start | bytes 221192 | tf_op jit(solution)/shard_map/ppermute | solution.py:332
  42.9 0.5 collective-permute-start.15
  43.4 1.0 %collective-permute-start.14 = (s16[72,512]{1,0:T(8,128)(2,1)S(1)}, s16[72,512]{1,0:T(8,128)(2,1)S(1)}, u32[]{:S(2)}, u32[]{:S(2)}) collective-permute-start(s16[72,512]{1,0:T(8,128)(2,1)S(1)} %sum_kernel.3.refs_0_), channel_id=1, source_target_pairs={{0,1},{1,0},{2,3},{3,2},{4,5},{5,4},{6,7},{7,6},{8,9},{9,8},{10,11... | collective-permute-start | bytes 221192 | tf_op jit(solution)/shard_map/ppermute | solution.py:332
  44.4 2.3 %collective-permute-done.16.refs_3_ = s16[72,512]{1,0:T(8,128)(2,1)S(1)} collective-permute-done((s16[72,512]{1,0:T(8,128)(2,1)S(1)}, s16[72,512]{1,0:T(8,128)(2,1)S(1)}, u32[]{:S(2)}, u32[]{:S(2)}) %collective-permute-start.16) | collective-permute-done | bytes 73760 | tf_op jit(solution)/shard_map/ppermute | solution.py:332
  46.7 0.7 %collective-permute-done.15.refs_2_ = s16[72,512]{1,0:T(8,128)(2,1)S(1)} collective-permute-done((s16[72,512]{1,0:T(8,128)(2,1)S(1)}, s16[72,512]{1,0:T(8,128)(2,1)S(1)}, u32[]{:S(2)}, u32[]{:S(2)}) %collective-permute-start.15) | collective-permute-done | bytes 73760 | tf_op jit(solution)/shard_map/ppermute | solution.py:332
  47.4 0.4 collective-permute-done.14.refs_1_
  47.8 0.2 collective-permute-done.17.got_ref
  47.9 0.2 bulk_sum_kernel.1
  48.1 0.1 collective-permute-start.18
  48.2 1.9 %collective-permute-start.19 = (s16[528,128]{1,0:T(8,128)(2,1)S(1)}, s16[528,128]{1,0:T(8,128)(2,1)S(1)}, u32[]{:S(2)}, u32[]{:S(2)}) collective-permute-start(s16[528,128]{1,0:T(8,128)(2,1)S(1)} %get-tuple-element.61), channel_id=1, source_target_pairs={{0,16},{4,20},{8,24},{12,28},{16,0},{20,4},{24,8},{28,12},{1,17},{... | collective-permute-start | bytes 405512 | tf_op jit(solution)/shard_map/ppermute | solution.py:332
  50.1 0.2 own_kernel.1.half_ref
  50.3 0.0 collective-permute-done.18.other_ref
  50.3 7.0 %newton_kernel.1 = (f32[256,256]{1,0:T(8,128)S(1)}, f32[256,512]{1,0:T(8,128)S(1)}) custom-call(f32[256,512]{1,0:T(8,128)S(1)} %own_kernel.1.half_ref, s16[320,512]{1,0:T(8,128)(2,1)S(1)} %collective-permute-done.18.other_ref), custom_call_target="tpu_custom_call" | custom-call | bytes 33211024 | tf_op jit(solution)/shard_map/newton_kernel/pallas_call | solution.py:317
  57.2 0.7 %collective-permute-done.19.refs_0_ = s16[528,128]{1,0:T(8,128)(2,1)S(1)} collective-permute-done((s16[528,128]{1,0:T(8,128)(2,1)S(1)}, s16[528,128]{1,0:T(8,128)(2,1)S(1)}, u32[]{:S(2)}, u32[]{:S(2)}) %collective-permute-start.19) | collective-permute-done | bytes 135200 | tf_op jit(solution)/shard_map/ppermute | solution.py:332
  58.0 1.2 %factor_kernel.1 = (f32[128,1,256]{2,1,0:T(1,128)}, f32[128,1,256]{2,1,0:T(1,128)}) custom-call(f32[256,256]{1,0:T(8,128)S(1)} %get-tuple-element.63.inverse_first_ref, f32[256,512]{1,0:T(8,128)S(1)} %get-tuple-element.64.inverse_second_ref, f32[512,128]{1,0:T(8,128)S(1)} %get-tuple-element.65.rows_ref, s16[528,128]{1,0:T(8,128)(2,1)S(1)} %collective-permute-done.19.refs_0_), custom_call_target="tpu_custom_call" | custom-call | bytes 1024 | tf_op jit(solution)/shard_map/factor_kernel/pallas_call | solution.py:317
  (1 shorter events, 0.0 us)
Async XLA Ops:
  1.8 8.7 %collective-permute-start.1 = (bf16[256,384]{1,0:T(8,128)(2,1)S(1)}, bf16[256,384]{1,0:T(8,128)(2,1)S(1)}, u32[]{:S(2)}, u32[]{:S(2)}) collective-permute-start(bf16[256,384]{1,0:T(8,128)(2,1)S(1)} %get-tuple-element.37.refs_1_), channel_id=1, source_target_pairs={{0,1},{1,0},{2,3},{3,2},{4,5},{5,4},{6,7},{7,6},{8,9},{9,8},{10,11... | collective-permute-start | bytes 589832 | tf_op jit(solution)/shard_map/ppermute | solution.py:332
  4.8 7.8 %collective-permute-start.2 = (bf16[256,384]{1,0:T(8,128)(2,1)S(1)}, bf16[256,384]{1,0:T(8,128)(2,1)S(1)}, u32[]{:S(2)}, u32[]{:S(2)}) collective-permute-start(bf16[256,384]{1,0:T(8,128)(2,1)S(1)} %get-tuple-element.36.refs_0_), channel_id=1, source_target_pairs={{0,2},{1,3},{2,0},{3,1},{4,6},{5,7},{6,4},{7,5},{8,10},{9,11},{10,... | collective-permute-start | bytes 589832 | tf_op jit(solution)/shard_map/ppermute | solution.py:332
  6.3 10.7 %collective-permute-start = (bf16[256,384]{1,0:T(8,128)(2,1)S(1)}, bf16[256,384]{1,0:T(8,128)(2,1)S(1)}, u32[]{:S(2)}, u32[]{:S(2)}) collective-permute-start(bf16[256,384]{1,0:T(8,128)(2,1)S(1)} %get-tuple-element.36.refs_0_), channel_id=1, source_target_pairs={{0,1},{1,0},{2,3},{3,2},{4,5},{5,4},{6,7},{7,6},{8,9},{9,8},{10,11... | collective-permute-start | bytes 589832 | tf_op jit(solution)/shard_map/ppermute | solution.py:332
  6.9 10.1 %collective-permute-start.3 = (bf16[256,384]{1,0:T(8,128)(2,1)S(1)}, bf16[256,384]{1,0:T(8,128)(2,1)S(1)}, u32[]{:S(2)}, u32[]{:S(2)}) collective-permute-start(bf16[256,384]{1,0:T(8,128)(2,1)S(1)} %get-tuple-element.37.refs_1_), channel_id=1, source_target_pairs={{0,2},{1,3},{2,0},{3,1},{4,6},{5,7},{6,4},{7,5},{8,10},{9,11},{10,... | collective-permute-start | bytes 589832 | tf_op jit(solution)/shard_map/ppermute | solution.py:332
  12.6 5.7 %collective-permute-start.4 = (bf16[256,384]{1,0:T(8,128)(2,1)S(1)}, bf16[256,384]{1,0:T(8,128)(2,1)S(1)}, u32[]{:S(2)}, u32[]{:S(2)}) collective-permute-start(bf16[256,384]{1,0:T(8,128)(2,1)S(1)} %collective-permute-done.2.refs_4_), channel_id=1, source_target_pairs={{0,1},{1,0},{2,3},{3,2},{4,5},{5,4},{6,7},{7,6},{8,9},{9,8},{10,11... | collective-permute-start | bytes 589832 | tf_op jit(solution)/shard_map/ppermute | solution.py:332
  12.7 6.9 %collective-permute-start.5 = (bf16[256,384]{1,0:T(8,128)(2,1)S(1)}, bf16[256,384]{1,0:T(8,128)(2,1)S(1)}, u32[]{:S(2)}, u32[]{:S(2)}) collective-permute-start(bf16[256,384]{1,0:T(8,128)(2,1)S(1)} %collective-permute-done.1.refs_3_), channel_id=1, source_target_pairs={{0,2},{1,3},{2,0},{3,1},{4,6},{5,7},{6,4},{7,5},{8,10},{9,11},{10,... | collective-permute-start | bytes 589832 | tf_op jit(solution)/shard_map/ppermute | solution.py:332
  19.9 2.0 %collective-permute-start.6 = (f32[264,512]{1,0:T(8,128)S(1)}, f32[264,512]{1,0:T(8,128)S(1)}, u32[]{:S(2)}, u32[]{:S(2)}) collective-permute-start(f32[264,512]{1,0:T(8,128)S(1)} %send_kernel.1), channel_id=1, source_target_pairs={{0,4},{4,0},{8,12},{12,8},{16,20},{20,16},{24,28},{28,24},{1,5},{5... | collective-permute-start | bytes 1622024 | tf_op jit(solution)/shard_map/ppermute | solution.py:332
  20.0 5.6 %copy-start = (bf16[1,1536,1024]{2,1,0:T(8,128)(2,1)S(1)}, bf16[1,1536,1024]{2,1,0:T(8,128)(2,1)}, u32[]{:S(2)}) copy-start(bf16[1,1536,1024]{2,1,0:T(8,128)(2,1)} %param.4) | copy-start | bytes 9437188
  22.1 5.4 %collective-permute-start.7 = (s16[72,512]{1,0:T(8,128)(2,1)S(1)}, s16[72,512]{1,0:T(8,128)(2,1)S(1)}, u32[]{:S(2)}, u32[]{:S(2)}) collective-permute-start(s16[72,512]{1,0:T(8,128)(2,1)S(1)} %get-tuple-element.51), channel_id=1, source_target_pairs={{0,3},{1,2},{2,1},{3,0},{4,7},{5,6},{6,5},{7,4},{8,11},{9,10},{10,... | collective-permute-start | bytes 221192 | tf_op jit(solution)/shard_map/ppermute | solution.py:332
  23.9 5.1 %collective-permute-start.8 = (s16[72,512]{1,0:T(8,128)(2,1)S(1)}, s16[72,512]{1,0:T(8,128)(2,1)S(1)}, u32[]{:S(2)}, u32[]{:S(2)}) collective-permute-start(s16[72,512]{1,0:T(8,128)(2,1)S(1)} %get-tuple-element.52), channel_id=1, source_target_pairs={{0,2},{1,3},{2,0},{3,1},{4,6},{5,7},{6,4},{7,5},{8,10},{9,11},{10,... | collective-permute-start | bytes 221192 | tf_op jit(solution)/shard_map/ppermute | solution.py:332
  24.4 4.6 %collective-permute-start.9 = (s16[72,512]{1,0:T(8,128)(2,1)S(1)}, s16[72,512]{1,0:T(8,128)(2,1)S(1)}, u32[]{:S(2)}, u32[]{:S(2)}) collective-permute-start(s16[72,512]{1,0:T(8,128)(2,1)S(1)} %get-tuple-element.53), channel_id=1, source_target_pairs={{0,1},{1,0},{2,3},{3,2},{4,5},{5,4},{6,7},{7,6},{8,9},{9,8},{10,11... | collective-permute-start | bytes 221192 | tf_op jit(solution)/shard_map/ppermute | solution.py:332
  29.1 4.5 %collective-permute-start.10 = (f32[2048,128]{1,0:T(8,128)S(1)}, f32[2048,128]{1,0:T(8,128)S(1)}, u32[]{:S(2)}, u32[]{:S(2)}) collective-permute-start(f32[2048,128]{1,0:T(8,128)S(1)} %get-tuple-element.56), channel_id=1, source_target_pairs={{0,4},{4,0},{8,12},{12,8},{16,20},{20,16},{24,28},{28,24},{1,5},{5... | collective-permute-start | bytes 3145736 | tf_op jit(solution)/shard_map/ppermute | solution.py:332
  29.2 6.9 %collective-permute-start.13 = (s16[72,512]{1,0:T(8,128)(2,1)S(1)}, s16[72,512]{1,0:T(8,128)(2,1)S(1)}, u32[]{:S(2)}, u32[]{:S(2)}) collective-permute-start(s16[72,512]{1,0:T(8,128)(2,1)S(1)} %sum_kernel.2.refs_0_), channel_id=1, source_target_pairs={{0,24},{4,28},{8,16},{12,20},{16,8},{20,12},{24,0},{28,4},{1,25},{... | collective-permute-start | bytes 221192 | tf_op jit(solution)/shard_map/ppermute | solution.py:332
  32.9 6.8 %collective-permute-start.12 = (s16[72,512]{1,0:T(8,128)(2,1)S(1)}, s16[72,512]{1,0:T(8,128)(2,1)S(1)}, u32[]{:S(2)}, u32[]{:S(2)}) collective-permute-start(s16[72,512]{1,0:T(8,128)(2,1)S(1)} %sum_kernel.2.refs_0_), channel_id=1, source_target_pairs={{0,16},{4,20},{8,24},{12,28},{16,0},{20,4},{24,8},{28,12},{1,17},{... | collective-permute-start | bytes 221192 | tf_op jit(solution)/shard_map/ppermute | solution.py:332
  32.9 6.8 %collective-permute-start.11 = (s16[72,512]{1,0:T(8,128)(2,1)S(1)}, s16[72,512]{1,0:T(8,128)(2,1)S(1)}, u32[]{:S(2)}, u32[]{:S(2)}) collective-permute-start(s16[72,512]{1,0:T(8,128)(2,1)S(1)} %sum_kernel.2.refs_0_), channel_id=1, source_target_pairs={{0,8},{4,12},{8,0},{12,4},{16,24},{20,28},{24,16},{28,20},{1,9},{5... | collective-permute-start | bytes 221192 | tf_op jit(solution)/shard_map/ppermute | solution.py:332
  39.8 8.1 %collective-permute-start.17 = (s16[1056,128]{1,0:T(8,128)(2,1)S(1)}, s16[1056,128]{1,0:T(8,128)(2,1)S(1)}, u32[]{:S(2)}, u32[]{:S(2)}) collective-permute-start(s16[1056,128]{1,0:T(8,128)(2,1)S(1)} %get-tuple-element.60), channel_id=1, source_target_pairs={{0,8},{4,12},{8,0},{12,4},{16,24},{20,28},{24,16},{28,20},{1,9},{5... | collective-permute-start | bytes 811016 | tf_op jit(solution)/shard_map/ppermute | solution.py:332
  40.9 5.8 %collective-permute-start.16 = (s16[72,512]{1,0:T(8,128)(2,1)S(1)}, s16[72,512]{1,0:T(8,128)(2,1)S(1)}, u32[]{:S(2)}, u32[]{:S(2)}) collective-permute-start(s16[72,512]{1,0:T(8,128)(2,1)S(1)} %sum_kernel.3.refs_0_), channel_id=1, source_target_pairs={{0,3},{1,2},{2,1},{3,0},{4,7},{5,6},{6,5},{7,4},{8,11},{9,10},{10,... | collective-permute-start | bytes 221192 | tf_op jit(solution)/shard_map/ppermute | solution.py:332
  42.9 4.5 %collective-permute-start.15 = (s16[72,512]{1,0:T(8,128)(2,1)S(1)}, s16[72,512]{1,0:T(8,128)(2,1)S(1)}, u32[]{:S(2)}, u32[]{:S(2)}) collective-permute-start(s16[72,512]{1,0:T(8,128)(2,1)S(1)} %sum_kernel.3.refs_0_), channel_id=1, source_target_pairs={{0,2},{1,3},{2,0},{3,1},{4,6},{5,7},{6,4},{7,5},{8,10},{9,11},{10,... | collective-permute-start | bytes 221192 | tf_op jit(solution)/shard_map/ppermute | solution.py:332
  43.4 4.4 %collective-permute-start.14 = (s16[72,512]{1,0:T(8,128)(2,1)S(1)}, s16[72,512]{1,0:T(8,128)(2,1)S(1)}, u32[]{:S(2)}, u32[]{:S(2)}) collective-permute-start(s16[72,512]{1,0:T(8,128)(2,1)S(1)} %sum_kernel.3.refs_0_), channel_id=1, source_target_pairs={{0,1},{1,0},{2,3},{3,2},{4,5},{5,4},{6,7},{7,6},{8,9},{9,8},{10,11... | collective-permute-start | bytes 221192 | tf_op jit(solution)/shard_map/ppermute | solution.py:332
  48.1 2.2 %collective-permute-start.18 = (s16[320,512]{1,0:T(8,128)(2,1)S(1)}, s16[320,512]{1,0:T(8,128)(2,1)S(1)}, u32[]{:S(2)}, u32[]{:S(2)}) collective-permute-start(s16[320,512]{1,0:T(8,128)(2,1)S(1)} %join_kernel.1.own_ref), channel_id=1, source_target_pairs={{0,4},{4,0},{8,12},{12,8},{16,20},{20,16},{24,28},{28,24},{1,5},{5... | collective-permute-start | bytes 983048 | tf_op jit(solution)/shard_map/ppermute | solution.py:332
  48.2 9.8 %collective-permute-start.19 = (s16[528,128]{1,0:T(8,128)(2,1)S(1)}, s16[528,128]{1,0:T(8,128)(2,1)S(1)}, u32[]{:S(2)}, u32[]{:S(2)}) collective-permute-start(s16[528,128]{1,0:T(8,128)(2,1)S(1)} %get-tuple-element.61), channel_id=1, source_target_pairs={{0,16},{4,20},{8,24},{12,28},{16,0},{20,4},{24,8},{28,12},{1,17},{... | collective-permute-start | bytes 405512 | tf_op jit(solution)/shard_map/ppermute | solution.py:332

commit v13 on v12

--- a/solution.py
+++ b/solution.py
@@ -102,13 +102,15 @@
 
 
 def turn_kernel(solves_ref, upper_ref, lower_ref, solves_copy, done):
-    copy = pltpu.make_async_copy(solves_ref, solves_copy, done)
-    copy.start()
-    copy.wait()
-    turned = solves_copy[...].T
     half = upper_ref.shape[0]
-    upper_ref[...] = turned[:half]
-    lower_ref[...] = turned[half:]
+    copies = [
+        pltpu.make_async_copy(solves_ref.at[:, pl.ds(i * half, half)], solves_copy.at[i], done.at[i]) for i in (0, 1)
+    ]
+    for copy in copies:
+        copy.start()
+    for i, out_ref in enumerate((upper_ref, lower_ref)):
+        copies[i].wait()
+        out_ref[...] = solves_copy[i].T
 
 
 def fetch(source_ref, target_ref, done, first):
@@ -352,7 +354,7 @@
     half = pltpu.VMEM((panel // 2, block), BF16)
     upper, lower = call(
         turn_kernel, (half, half), solves, remain=1,
-        scratch=[pltpu.VMEM((block, panel), BF16), pltpu.SemaphoreType.DMA],
+        scratch=[pltpu.VMEM((2, block, panel // 2), BF16), pltpu.SemaphoreType.DMA((2,))],
     )
     lower_x, upper_y = swap(lower, "row", 1), swap(upper, "row", 2)
     upper_x, lower_y = swap(upper, "row", 1), swap(lower, "row", 2)
@@ -434,12 +436,10 @@
     if split:
         for bit in steps[:-1]:
             count //= 2
-            got = swap(after(bulk_codes, part), "scen", 2 * bit)
+            got = swap(bulk_codes, "scen", 2 * bit)
             own, bulk_codes = call(functools.partial(bulk_sum_kernel, panel), halved(count), own, got)
         got = [swap(bulk_codes, "scen", layers)]
     joined = call(join_kernel, shape((rows * (size + TAIL), panel), I16), part, *shared)
-    if split:
-        joined = after(joined, bulk_codes)
     other = swap(joined, "scen", 1)
     own_half = call(
         functools.partial(own_kernel, rows), shape((panel // 2, panel), F32), joined

time: 59.4 us -> 58.3 us (0.981)
  waiting for transfers between devices: 17.6 us -> 16.9 us
    ppermute x20, waiting for transfers between devices: 17.6 us -> 16.9 us  [swap(): return lax.ppermute(x, axis, [(i, i ^ bit) for i in range(count)])]
  transfers between devices with their start and end apart: 20 -> 20, of which waited for: 14 -> 13; matrix products, arithmetic and copies ran while one was open for 0% -> 0% of each run, Pallas kernels for 26% -> 27%
where the time goes in v13:
time: 58.3 us; the launch traced here: 58.1 us
  starting transfers between devices  21.5 us (37%)
  Pallas kernels  18.9 us (32%)
  waiting for transfers between devices  16.9 us (29%)
  between operations  0.81 us (1%)
    ppermute x20, starting transfers between devices, swap(): return lax.ppermute(x, axis, [(i, i ^ bit) for i in range(count)])  21.5 us
    pallas_call x16, Pallas kernels, call(): pl.pallas_call(kernel, name=getattr(kernel, 'func', kernel).__name__, out...  18.9 us
    ppermute x20, waiting for transfers between devices, swap(): return lax.ppermute(x, axis, [(i, i ^ bit) for i in range(count)])  16.9 us
  transfers between devices with their start and end apart: 20, of which 13 were waited for; matrix products, arithmetic and copies ran while one was open for 0% of the time, Pallas kernels for 27%

profile of v13, /device:TPU:0, one launch (start us, length us, event | category | flops | bytes accessed | tf_op | source)
XLA Modules:
  0.0 58.1 jit_solution(2275460289361771842)
XLA Ops:
  0.6 1.2 %turn_kernel.1 = (bf16[256,384]{1,0:T(8,128)(2,1)S(1)}, bf16[256,384]{1,0:T(8,128)(2,1)S(1)}) custom-call(bf16[384,512]{1,0:T(8,128)(2,1)} %bitcast.7), custom_call_target="tpu_custom_call" | custom-call | bytes 1024 | tf_op jit(solution)/shard_map/turn_kernel/pallas_call | solution.py:319
  1.8 3.0 %collective-permute-start.1 = (bf16[256,384]{1,0:T(8,128)(2,1)S(1)}, bf16[256,384]{1,0:T(8,128)(2,1)S(1)}, u32[]{:S(2)}, u32[]{:S(2)}) collective-permute-start(bf16[256,384]{1,0:T(8,128)(2,1)S(1)} %get-tuple-element.35.refs_1_), channel_id=1, source_target_pairs={{0,1},{1,0},{2,3},{3,2},{4,5},{5,4},{6,7},{7,6},{8,9},{9,8},{10,11... | collective-permute-start | bytes 589832 | tf_op jit(solution)/shard_map/ppermute | solution.py:334
  4.8 1.5 %collective-permute-start.2 = (bf16[256,384]{1,0:T(8,128)(2,1)S(1)}, bf16[256,384]{1,0:T(8,128)(2,1)S(1)}, u32[]{:S(2)}, u32[]{:S(2)}) collective-permute-start(bf16[256,384]{1,0:T(8,128)(2,1)S(1)} %get-tuple-element.34.refs_0_), channel_id=1, source_target_pairs={{0,2},{1,3},{2,0},{3,1},{4,6},{5,7},{6,4},{7,5},{8,10},{9,11},{10,... | collective-permute-start | bytes 589832 | tf_op jit(solution)/shard_map/ppermute | solution.py:334
  6.3 0.5 collective-permute-start
  6.9 0.1 collective-permute-start.3
  6.9 2.6 %pick_kernel.1 = (bf16[1536,512]{1,0:T(8,128)(2,1)S(1)}, f32[8,512]{1,0:T(8,128)S(1)}, bf16[1024,512]{1,0:T(8,128)(2,1)S(1)}, s32[1,512]{1,0:T(1,128)S(1)}, f32[1,128]{1,0:T(1,128)S(1)}) custom-call(s32[1,512]{1,0:T(1,128)} %bitcast.8, f32[1,128]{1,0:T(1,128)} %bitcast.9, bf16[1536,1024]{1,0:T(8,128)(2,1)} %bitcast.4), custom_call_target="tpu_custom_call" | custom-call | bytes 1024 | tf_op jit(solution)/shard_map/pick_kernel/pallas_call | solution.py:319
  9.6 1.0 %collective-permute-done.1.refs_3_ = bf16[256,384]{1,0:T(8,128)(2,1)S(1)} collective-permute-done((bf16[256,384]{1,0:T(8,128)(2,1)S(1)}, bf16[256,384]{1,0:T(8,128)(2,1)S(1)}, u32[]{:S(2)}, u32[]{:S(2)}) %collective-permute-start.1) | collective-permute-done | bytes 196640 | tf_op jit(solution)/shard_map/ppermute | solution.py:334
  10.5 2.1 %collective-permute-done.2.refs_4_ = bf16[256,384]{1,0:T(8,128)(2,1)S(1)} collective-permute-done((bf16[256,384]{1,0:T(8,128)(2,1)S(1)}, bf16[256,384]{1,0:T(8,128)(2,1)S(1)}, u32[]{:S(2)}, u32[]{:S(2)}) %collective-permute-start.2) | collective-permute-done | bytes 196640 | tf_op jit(solution)/shard_map/ppermute | solution.py:334
  12.6 0.0 collective-permute-start.4
  12.7 2.0 %collective-permute-start.5 = (bf16[256,384]{1,0:T(8,128)(2,1)S(1)}, bf16[256,384]{1,0:T(8,128)(2,1)S(1)}, u32[]{:S(2)}, u32[]{:S(2)}) collective-permute-start(bf16[256,384]{1,0:T(8,128)(2,1)S(1)} %collective-permute-done.1.refs_3_), channel_id=1, source_target_pairs={{0,2},{1,3},{2,0},{3,1},{4,6},{5,7},{6,4},{7,5},{8,10},{9,11},{10,... | collective-permute-start | bytes 589832 | tf_op jit(solution)/shard_map/ppermute | solution.py:334
  14.7 2.3 %rest_kernel.1.chosen_ref = bf16[1536,512]{1,0:T(8,128)(2,1)S(1)} custom-call(bf16[1536,512]{1,0:T(8,128)(2,1)S(1)} %get-tuple-element.32.chosen_in, bf16[1024,512]{1,0:T(8,128)(2,1)S(1)} %get-tuple-element.33.one_ref, bf16[1536,1024]{1,0:T(8,128)(2,1)} %bitcast.5), custom_call_target="tpu_custom_call", output_to_operand_aliasing={{}: (0, {})} | custom-call | bytes 1024 | tf_op jit(solution)/shard_map/rest_kernel/pallas_call | solution.py:319
  17.0 0.0 collective-permute-done.refs_2_
  17.0 0.0 collective-permute-done.3.refs_5_
  17.0 1.1 %early_kernel.1 = (bf16[512,1536]{1,0:T(8,128)(2,1)S(1)}, f32[512,512]{1,0:T(8,128)S(1)}) custom-call(bf16[1536,512]{1,0:T(8,128)(2,1)S(1)} %rest_kernel.1.chosen_ref, bf16[256,384]{1,0:T(8,128)(2,1)S(1)} %get-tuple-element.34.refs_0_, bf16[256,384]{1,0:T(8,128)(2,1)S(1)} %get-tuple-element.35.refs_1_, bf16[256,384]{1,0:T(8,128)(2,1)S(1)} %collective-permute-done.refs_2_, ...), custom_call_target="tpu_custom_call" | custom-call | bytes 1024 | tf_op jit(solution)/shard_map/early_kernel/pallas_call | solution.py:319
  18.1 0.2 collective-permute-done.4.refs_0_
  18.3 1.3 %collective-permute-done.5.refs_1_ = bf16[256,384]{1,0:T(8,128)(2,1)S(1)} collective-permute-done((bf16[256,384]{1,0:T(8,128)(2,1)S(1)}, bf16[256,384]{1,0:T(8,128)(2,1)S(1)}, u32[]{:S(2)}, u32[]{:S(2)}) %collective-permute-start.5) | collective-permute-done | bytes 196640 | tf_op jit(solution)/shard_map/ppermute | solution.py:334
  19.6 0.3 send_kernel.1
  19.9 0.1 collective-permute-start.6
  20.0 0.0 copy-start
  20.0 0.4 keep_kernel.1
  20.4 1.5 %collective-permute-done.6.got_ref = f32[264,512]{1,0:T(8,128)S(1)} collective-permute-done((f32[264,512]{1,0:T(8,128)S(1)}, f32[264,512]{1,0:T(8,128)S(1)}, u32[]{:S(2)}, u32[]{:S(2)}) %collective-permute-start.6) | collective-permute-done | bytes 540704 | tf_op jit(solution)/shard_map/ppermute | solution.py:334
  21.9 0.2 pair_kernel.1
  22.1 1.8 %collective-permute-start.7 = (s16[72,512]{1,0:T(8,128)(2,1)S(1)}, s16[72,512]{1,0:T(8,128)(2,1)S(1)}, u32[]{:S(2)}, u32[]{:S(2)}) collective-permute-start(s16[72,512]{1,0:T(8,128)(2,1)S(1)} %get-tuple-element.49), channel_id=1, source_target_pairs={{0,3},{1,2},{2,1},{3,0},{4,7},{5,6},{6,5},{7,4},{8,11},{9,10},{10,... | collective-permute-start | bytes 221192 | tf_op jit(solution)/shard_map/ppermute | solution.py:334
  23.9 0.5 collective-permute-start.8
  24.4 1.3 %collective-permute-start.9 = (s16[72,512]{1,0:T(8,128)(2,1)S(1)}, s16[72,512]{1,0:T(8,128)(2,1)S(1)}, u32[]{:S(2)}, u32[]{:S(2)}) collective-permute-start(s16[72,512]{1,0:T(8,128)(2,1)S(1)} %get-tuple-element.51), channel_id=1, source_target_pairs={{0,1},{1,0},{2,3},{3,2},{4,5},{5,4},{6,7},{7,6},{8,9},{9,8},{10,11... | collective-permute-start | bytes 221192 | tf_op jit(solution)/shard_map/ppermute | solution.py:334
  25.6 0.0 copy-done
  25.7 1.8 %schur_kernel.1 = (f32[2048,128]{1,0:T(8,128)S(1)}, f32[2048,128]{1,0:T(8,128)S(1)}) custom-call(s32[1,512]{1,0:T(1,128)S(1)} %get-tuple-element.43.panel_ref, f32[1,128]{1,0:T(1,128)S(1)} %get-tuple-element.44.own_diagonal_ref, bf16[1536,1024]{1,0:T(8,128)(2,1)S(1)} %bitcast.6, bf16[512,1536]{1,0:T(8,128)(2,1)S(1)} %get-tuple-element.46.turned_ref), custom_call_target="tpu_custom_call" | custom-call | bytes 1024 | tf_op jit(solution)/shard_map/schur_kernel/pallas_call | solution.py:319
  27.5 0.0 collective-permute-done.7.refs_1_
  27.5 1.5 %collective-permute-done.8.refs_2_ = s16[72,512]{1,0:T(8,128)(2,1)S(1)} collective-permute-done((s16[72,512]{1,0:T(8,128)(2,1)S(1)}, s16[72,512]{1,0:T(8,128)(2,1)S(1)}, u32[]{:S(2)}, u32[]{:S(2)}) %collective-permute-start.8) | collective-permute-done | bytes 73760 | tf_op jit(solution)/shard_map/ppermute | solution.py:334
  28.9 0.1 collective-permute-done.9.refs_3_
  29.0 0.1 sum_kernel.2.refs_0_
  29.1 0.1 collective-permute-start.10
  29.2 3.7 %collective-permute-start.13 = (s16[72,512]{1,0:T(8,128)(2,1)S(1)}, s16[72,512]{1,0:T(8,128)(2,1)S(1)}, u32[]{:S(2)}, u32[]{:S(2)}) collective-permute-start(s16[72,512]{1,0:T(8,128)(2,1)S(1)} %sum_kernel.2.refs_0_), channel_id=1, source_target_pairs={{0,24},{4,28},{8,16},{12,20},{16,8},{20,12},{24,0},{28,4},{1,25},{... | collective-permute-start | bytes 221192 | tf_op jit(solution)/shard_map/ppermute | solution.py:334
  32.9 0.0 collective-permute-start.12
  32.9 0.8 %collective-permute-start.11 = (s16[72,512]{1,0:T(8,128)(2,1)S(1)}, s16[72,512]{1,0:T(8,128)(2,1)S(1)}, u32[]{:S(2)}, u32[]{:S(2)}) collective-permute-start(s16[72,512]{1,0:T(8,128)(2,1)S(1)} %sum_kernel.2.refs_0_), channel_id=1, source_target_pairs={{0,8},{4,12},{8,0},{12,4},{16,24},{20,28},{24,16},{28,20},{1,9},{5... | collective-permute-start | bytes 221192 | tf_op jit(solution)/shard_map/ppermute | solution.py:334
  33.7 0.0 collective-permute-done.10.got_ref
  33.7 0.2 bulk_pair_kernel.1
  33.9 1.3 %collective-permute-start.18 = (s16[1056,128]{1,0:T(8,128)(2,1)S(1)}, s16[1056,128]{1,0:T(8,128)(2,1)S(1)}, u32[]{:S(2)}, u32[]{:S(2)}) collective-permute-start(s16[1056,128]{1,0:T(8,128)(2,1)S(1)} %get-tuple-element.55), channel_id=1, source_target_pairs={{0,8},{4,12},{8,0},{12,4},{16,24},{20,28},{24,16},{28,20},{1,9},{5... | collective-permute-start | bytes 811016 | tf_op jit(solution)/shard_map/ppermute | solution.py:334
  35.2 0.9 %collective-permute-done.13.refs_3_ = s16[72,512]{1,0:T(8,128)(2,1)S(1)} collective-permute-done((s16[72,512]{1,0:T(8,128)(2,1)S(1)}, s16[72,512]{1,0:T(8,128)(2,1)S(1)}, u32[]{:S(2)}, u32[]{:S(2)}) %collective-permute-start.13) | collective-permute-done | bytes 73760 | tf_op jit(solution)/shard_map/ppermute | solution.py:334
  36.1 3.6 %collective-permute-done.12.refs_2_ = s16[72,512]{1,0:T(8,128)(2,1)S(1)} collective-permute-done((s16[72,512]{1,0:T(8,128)(2,1)S(1)}, s16[72,512]{1,0:T(8,128)(2,1)S(1)}, u32[]{:S(2)}, u32[]{:S(2)}) %collective-permute-start.12) | collective-permute-done | bytes 73760 | tf_op jit(solution)/shard_map/ppermute | solution.py:334
  39.8 0.0 collective-permute-done.11.refs_1_
  39.8 0.1 sum_kernel.3.refs_0_
  39.9 2.0 %collective-permute-start.16 = (s16[72,512]{1,0:T(8,128)(2,1)S(1)}, s16[72,512]{1,0:T(8,128)(2,1)S(1)}, u32[]{:S(2)}, u32[]{:S(2)}) collective-permute-start(s16[72,512]{1,0:T(8,128)(2,1)S(1)} %sum_kernel.3.refs_0_), channel_id=1, source_target_pairs={{0,3},{1,2},{2,1},{3,0},{4,7},{5,6},{6,5},{7,4},{8,11},{9,10},{10,... | collective-permute-start | bytes 221192 | tf_op jit(solution)/shard_map/ppermute | solution.py:334
  41.9 0.5 collective-permute-start.15
  42.4 1.0 %collective-permute-start.14 = (s16[72,512]{1,0:T(8,128)(2,1)S(1)}, s16[72,512]{1,0:T(8,128)(2,1)S(1)}, u32[]{:S(2)}, u32[]{:S(2)}) collective-permute-start(s16[72,512]{1,0:T(8,128)(2,1)S(1)} %sum_kernel.3.refs_0_), channel_id=1, source_target_pairs={{0,1},{1,0},{2,3},{3,2},{4,5},{5,4},{6,7},{7,6},{8,9},{9,8},{10,11... | collective-permute-start | bytes 221192 | tf_op jit(solution)/shard_map/ppermute | solution.py:334
  43.5 2.1 %collective-permute-done.16.refs_3_ = s16[72,512]{1,0:T(8,128)(2,1)S(1)} collective-permute-done((s16[72,512]{1,0:T(8,128)(2,1)S(1)}, s16[72,512]{1,0:T(8,128)(2,1)S(1)}, u32[]{:S(2)}, u32[]{:S(2)}) %collective-permute-start.16) | collective-permute-done | bytes 73760 | tf_op jit(solution)/shard_map/ppermute | solution.py:334
  45.6 0.8 %collective-permute-done.15.refs_2_ = s16[72,512]{1,0:T(8,128)(2,1)S(1)} collective-permute-done((s16[72,512]{1,0:T(8,128)(2,1)S(1)}, s16[72,512]{1,0:T(8,128)(2,1)S(1)}, u32[]{:S(2)}, u32[]{:S(2)}) %collective-permute-start.15) | collective-permute-done | bytes 73760 | tf_op jit(solution)/shard_map/ppermute | solution.py:334
  46.3 0.5 collective-permute-done.14.refs_1_
  46.8 0.1 collective-permute-start.17
  46.9 0.0 collective-permute-done.18.got_ref
  46.9 0.2 bulk_sum_kernel.1
  47.1 1.3 %collective-permute-start.19 = (s16[528,128]{1,0:T(8,128)(2,1)S(1)}, s16[528,128]{1,0:T(8,128)(2,1)S(1)}, u32[]{:S(2)}, u32[]{:S(2)}) collective-permute-start(s16[528,128]{1,0:T(8,128)(2,1)S(1)} %get-tuple-element.61), channel_id=1, source_target_pairs={{0,16},{4,20},{8,24},{12,28},{16,0},{20,4},{24,8},{28,12},{1,17},{... | collective-permute-start | bytes 405512 | tf_op jit(solution)/shard_map/ppermute | solution.py:334
  48.3 0.2 own_kernel.1.half_ref
  48.5 0.0 collective-permute-done.17.other_ref
  48.5 7.0 %newton_kernel.1 = (f32[256,256]{1,0:T(8,128)S(1)}, f32[256,512]{1,0:T(8,128)S(1)}) custom-call(f32[256,512]{1,0:T(8,128)S(1)} %own_kernel.1.half_ref, s16[320,512]{1,0:T(8,128)(2,1)S(1)} %collective-permute-done.17.other_ref), custom_call_target="tpu_custom_call" | custom-call | bytes 33211024 | tf_op jit(solution)/shard_map/newton_kernel/pallas_call | solution.py:319
  55.5 1.4 %collective-permute-done.19.refs_0_ = s16[528,128]{1,0:T(8,128)(2,1)S(1)} collective-permute-done((s16[528,128]{1,0:T(8,128)(2,1)S(1)}, s16[528,128]{1,0:T(8,128)(2,1)S(1)}, u32[]{:S(2)}, u32[]{:S(2)}) %collective-permute-start.19) | collective-permute-done | bytes 135200 | tf_op jit(solution)/shard_map/ppermute | solution.py:334
  56.9 1.2 %factor_kernel.1 = (f32[128,1,256]{2,1,0:T(1,128)}, f32[128,1,256]{2,1,0:T(1,128)}) custom-call(f32[256,256]{1,0:T(8,128)S(1)} %get-tuple-element.57.inverse_first_ref, f32[256,512]{1,0:T(8,128)S(1)} %get-tuple-element.58.inverse_second_ref, f32[512,128]{1,0:T(8,128)S(1)} %get-tuple-element.60.rows_ref, s16[528,128]{1,0:T(8,128)(2,1)S(1)} %collective-permute-done.19.refs_0_), custom_call_target="tpu_custom_call" | custom-call | bytes 1024 | tf_op jit(solution)/shard_map/factor_kernel/pallas_call | solution.py:319
  (1 shorter events, 0.0 us)
Async XLA Ops:
  1.8 8.7 %collective-permute-start.1 = (bf16[256,384]{1,0:T(8,128)(2,1)S(1)}, bf16[256,384]{1,0:T(8,128)(2,1)S(1)}, u32[]{:S(2)}, u32[]{:S(2)}) collective-permute-start(bf16[256,384]{1,0:T(8,128)(2,1)S(1)} %get-tuple-element.35.refs_1_), channel_id=1, source_target_pairs={{0,1},{1,0},{2,3},{3,2},{4,5},{5,4},{6,7},{7,6},{8,9},{9,8},{10,11... | collective-permute-start | bytes 589832 | tf_op jit(solution)/shard_map/ppermute | solution.py:334
  4.8 7.8 %collective-permute-start.2 = (bf16[256,384]{1,0:T(8,128)(2,1)S(1)}, bf16[256,384]{1,0:T(8,128)(2,1)S(1)}, u32[]{:S(2)}, u32[]{:S(2)}) collective-permute-start(bf16[256,384]{1,0:T(8,128)(2,1)S(1)} %get-tuple-element.34.refs_0_), channel_id=1, source_target_pairs={{0,2},{1,3},{2,0},{3,1},{4,6},{5,7},{6,4},{7,5},{8,10},{9,11},{10,... | collective-permute-start | bytes 589832 | tf_op jit(solution)/shard_map/ppermute | solution.py:334
  6.3 10.7 %collective-permute-start = (bf16[256,384]{1,0:T(8,128)(2,1)S(1)}, bf16[256,384]{1,0:T(8,128)(2,1)S(1)}, u32[]{:S(2)}, u32[]{:S(2)}) collective-permute-start(bf16[256,384]{1,0:T(8,128)(2,1)S(1)} %get-tuple-element.34.refs_0_), channel_id=1, source_target_pairs={{0,1},{1,0},{2,3},{3,2},{4,5},{5,4},{6,7},{7,6},{8,9},{9,8},{10,11... | collective-permute-start | bytes 589832 | tf_op jit(solution)/shard_map/ppermute | solution.py:334
  6.9 10.1 %collective-permute-start.3 = (bf16[256,384]{1,0:T(8,128)(2,1)S(1)}, bf16[256,384]{1,0:T(8,128)(2,1)S(1)}, u32[]{:S(2)}, u32[]{:S(2)}) collective-permute-start(bf16[256,384]{1,0:T(8,128)(2,1)S(1)} %get-tuple-element.35.refs_1_), channel_id=1, source_target_pairs={{0,2},{1,3},{2,0},{3,1},{4,6},{5,7},{6,4},{7,5},{8,10},{9,11},{10,... | collective-permute-start | bytes 589832 | tf_op jit(solution)/shard_map/ppermute | solution.py:334
  12.6 5.7 %collective-permute-start.4 = (bf16[256,384]{1,0:T(8,128)(2,1)S(1)}, bf16[256,384]{1,0:T(8,128)(2,1)S(1)}, u32[]{:S(2)}, u32[]{:S(2)}) collective-permute-start(bf16[256,384]{1,0:T(8,128)(2,1)S(1)} %collective-permute-done.2.refs_4_), channel_id=1, source_target_pairs={{0,1},{1,0},{2,3},{3,2},{4,5},{5,4},{6,7},{7,6},{8,9},{9,8},{10,11... | collective-permute-start | bytes 589832 | tf_op jit(solution)/shard_map/ppermute | solution.py:334
  12.7 6.9 %collective-permute-start.5 = (bf16[256,384]{1,0:T(8,128)(2,1)S(1)}, bf16[256,384]{1,0:T(8,128)(2,1)S(1)}, u32[]{:S(2)}, u32[]{:S(2)}) collective-permute-start(bf16[256,384]{1,0:T(8,128)(2,1)S(1)} %collective-permute-done.1.refs_3_), channel_id=1, source_target_pairs={{0,2},{1,3},{2,0},{3,1},{4,6},{5,7},{6,4},{7,5},{8,10},{9,11},{10,... | collective-permute-start | bytes 589832 | tf_op jit(solution)/shard_map/ppermute | solution.py:334
  19.9 2.0 %collective-permute-start.6 = (f32[264,512]{1,0:T(8,128)S(1)}, f32[264,512]{1,0:T(8,128)S(1)}, u32[]{:S(2)}, u32[]{:S(2)}) collective-permute-start(f32[264,512]{1,0:T(8,128)S(1)} %send_kernel.1), channel_id=1, source_target_pairs={{0,4},{4,0},{8,12},{12,8},{16,20},{20,16},{24,28},{28,24},{1,5},{5... | collective-permute-start | bytes 1622024 | tf_op jit(solution)/shard_map/ppermute | solution.py:334
  20.0 5.6 %copy-start = (bf16[1,1536,1024]{2,1,0:T(8,128)(2,1)S(1)}, bf16[1,1536,1024]{2,1,0:T(8,128)(2,1)}, u32[]{:S(2)}) copy-start(bf16[1,1536,1024]{2,1,0:T(8,128)(2,1)} %param.4) | copy-start | bytes 9437188
  22.1 5.4 %collective-permute-start.7 = (s16[72,512]{1,0:T(8,128)(2,1)S(1)}, s16[72,512]{1,0:T(8,128)(2,1)S(1)}, u32[]{:S(2)}, u32[]{:S(2)}) collective-permute-start(s16[72,512]{1,0:T(8,128)(2,1)S(1)} %get-tuple-element.49), channel_id=1, source_target_pairs={{0,3},{1,2},{2,1},{3,0},{4,7},{5,6},{6,5},{7,4},{8,11},{9,10},{10,... | collective-permute-start | bytes 221192 | tf_op jit(solution)/shard_map/ppermute | solution.py:334
  23.9 5.1 %collective-permute-start.8 = (s16[72,512]{1,0:T(8,128)(2,1)S(1)}, s16[72,512]{1,0:T(8,128)(2,1)S(1)}, u32[]{:S(2)}, u32[]{:S(2)}) collective-permute-start(s16[72,512]{1,0:T(8,128)(2,1)S(1)} %get-tuple-element.50), channel_id=1, source_target_pairs={{0,2},{1,3},{2,0},{3,1},{4,6},{5,7},{6,4},{7,5},{8,10},{9,11},{10,... | collective-permute-start | bytes 221192 | tf_op jit(solution)/shard_map/ppermute | solution.py:334
  24.4 4.7 %collective-permute-start.9 = (s16[72,512]{1,0:T(8,128)(2,1)S(1)}, s16[72,512]{1,0:T(8,128)(2,1)S(1)}, u32[]{:S(2)}, u32[]{:S(2)}) collective-permute-start(s16[72,512]{1,0:T(8,128)(2,1)S(1)} %get-tuple-element.51), channel_id=1, source_target_pairs={{0,1},{1,0},{2,3},{3,2},{4,5},{5,4},{6,7},{7,6},{8,9},{9,8},{10,11... | collective-permute-start | bytes 221192 | tf_op jit(solution)/shard_map/ppermute | solution.py:334
  29.1 4.5 %collective-permute-start.10 = (f32[2048,128]{1,0:T(8,128)S(1)}, f32[2048,128]{1,0:T(8,128)S(1)}, u32[]{:S(2)}, u32[]{:S(2)}) collective-permute-start(f32[2048,128]{1,0:T(8,128)S(1)} %get-tuple-element.54), channel_id=1, source_target_pairs={{0,4},{4,0},{8,12},{12,8},{16,20},{20,16},{24,28},{28,24},{1,5},{5... | collective-permute-start | bytes 3145736 | tf_op jit(solution)/shard_map/ppermute | solution.py:334
  29.2 6.9 %collective-permute-start.13 = (s16[72,512]{1,0:T(8,128)(2,1)S(1)}, s16[72,512]{1,0:T(8,128)(2,1)S(1)}, u32[]{:S(2)}, u32[]{:S(2)}) collective-permute-start(s16[72,512]{1,0:T(8,128)(2,1)S(1)} %sum_kernel.2.refs_0_), channel_id=1, source_target_pairs={{0,24},{4,28},{8,16},{12,20},{16,8},{20,12},{24,0},{28,4},{1,25},{... | collective-permute-start | bytes 221192 | tf_op jit(solution)/shard_map/ppermute | solution.py:334
  32.9 6.9 %collective-permute-start.12 = (s16[72,512]{1,0:T(8,128)(2,1)S(1)}, s16[72,512]{1,0:T(8,128)(2,1)S(1)}, u32[]{:S(2)}, u32[]{:S(2)}) collective-permute-start(s16[72,512]{1,0:T(8,128)(2,1)S(1)} %sum_kernel.2.refs_0_), channel_id=1, source_target_pairs={{0,16},{4,20},{8,24},{12,28},{16,0},{20,4},{24,8},{28,12},{1,17},{... | collective-permute-start | bytes 221192 | tf_op jit(solution)/shard_map/ppermute | solution.py:334
  32.9 6.9 %collective-permute-start.11 = (s16[72,512]{1,0:T(8,128)(2,1)S(1)}, s16[72,512]{1,0:T(8,128)(2,1)S(1)}, u32[]{:S(2)}, u32[]{:S(2)}) collective-permute-start(s16[72,512]{1,0:T(8,128)(2,1)S(1)} %sum_kernel.2.refs_0_), channel_id=1, source_target_pairs={{0,8},{4,12},{8,0},{12,4},{16,24},{20,28},{24,16},{28,20},{1,9},{5... | collective-permute-start | bytes 221192 | tf_op jit(solution)/shard_map/ppermute | solution.py:334
  33.9 13.0 %collective-permute-start.18 = (s16[1056,128]{1,0:T(8,128)(2,1)S(1)}, s16[1056,128]{1,0:T(8,128)(2,1)S(1)}, u32[]{:S(2)}, u32[]{:S(2)}) collective-permute-start(s16[1056,128]{1,0:T(8,128)(2,1)S(1)} %get-tuple-element.55), channel_id=1, source_target_pairs={{0,8},{4,12},{8,0},{12,4},{16,24},{20,28},{24,16},{28,20},{1,9},{5... | collective-permute-start | bytes 811016 | tf_op jit(solution)/shard_map/ppermute | solution.py:334
  39.9 5.6 %collective-permute-start.16 = (s16[72,512]{1,0:T(8,128)(2,1)S(1)}, s16[72,512]{1,0:T(8,128)(2,1)S(1)}, u32[]{:S(2)}, u32[]{:S(2)}) collective-permute-start(s16[72,512]{1,0:T(8,128)(2,1)S(1)} %sum_kernel.3.refs_0_), channel_id=1, source_target_pairs={{0,3},{1,2},{2,1},{3,0},{4,7},{5,6},{6,5},{7,4},{8,11},{9,10},{10,... | collective-permute-start | bytes 221192 | tf_op jit(solution)/shard_map/ppermute | solution.py:334
  41.9 4.4 %collective-permute-start.15 = (s16[72,512]{1,0:T(8,128)(2,1)S(1)}, s16[72,512]{1,0:T(8,128)(2,1)S(1)}, u32[]{:S(2)}, u32[]{:S(2)}) collective-permute-start(s16[72,512]{1,0:T(8,128)(2,1)S(1)} %sum_kernel.3.refs_0_), channel_id=1, source_target_pairs={{0,2},{1,3},{2,0},{3,1},{4,6},{5,7},{6,4},{7,5},{8,10},{9,11},{10,... | collective-permute-start | bytes 221192 | tf_op jit(solution)/shard_map/ppermute | solution.py:334
  42.4 4.4 %collective-permute-start.14 = (s16[72,512]{1,0:T(8,128)(2,1)S(1)}, s16[72,512]{1,0:T(8,128)(2,1)S(1)}, u32[]{:S(2)}, u32[]{:S(2)}) collective-permute-start(s16[72,512]{1,0:T(8,128)(2,1)S(1)} %sum_kernel.3.refs_0_), channel_id=1, source_target_pairs={{0,1},{1,0},{2,3},{3,2},{4,5},{5,4},{6,7},{7,6},{8,9},{9,8},{10,11... | collective-permute-start | bytes 221192 | tf_op jit(solution)/shard_map/ppermute | solution.py:334
  46.8 1.7 %collective-permute-start.17 = (s16[320,512]{1,0:T(8,128)(2,1)S(1)}, s16[320,512]{1,0:T(8,128)(2,1)S(1)}, u32[]{:S(2)}, u32[]{:S(2)}) collective-permute-start(s16[320,512]{1,0:T(8,128)(2,1)S(1)} %join_kernel.1.own_ref), channel_id=1, source_target_pairs={{0,4},{4,0},{8,12},{12,8},{16,20},{20,16},{24,28},{28,24},{1,5},{5... | collective-permute-start | bytes 983048 | tf_op jit(solution)/shard_map/ppermute | solution.py:334
  47.1 9.8 %collective-permute-start.19 = (s16[528,128]{1,0:T(8,128)(2,1)S(1)}, s16[528,128]{1,0:T(8,128)(2,1)S(1)}, u32[]{:S(2)}, u32[]{:S(2)}) collective-permute-start(s16[528,128]{1,0:T(8,128)(2,1)S(1)} %get-tuple-element.61), channel_id=1, source_target_pairs={{0,16},{4,20},{8,24},{12,28},{16,0},{20,4},{24,8},{28,12},{1,17},{... | collective-permute-start | bytes 405512 | tf_op jit(solution)/shard_map/ppermute | solution.py:334

commit v14 on v12

--- a/solution.py
+++ b/solution.py
@@ -13,6 +13,7 @@
 SHORT = 8
 CHUNKS = 4
 LEVELS = 32000.0
+UPPER = 288
 F32 = jnp.float32
 BF16 = jnp.bfloat16
 I16 = jnp.int16
@@ -24,22 +25,16 @@
     return high, low
 
 
-def left_of(a):
-    high, low = halves(a)
-    return jnp.concatenate([high, high, low], axis=1)
-
-
-def right_of(b):
-    high, low = halves(b)
-    return jnp.concatenate([high, low, high], axis=0)
-
-
 def dot(a, b):
     return jnp.dot(a, b, preferred_element_type=F32)
 
 
 def product(a, b):
-    return dot(left_of(a), right_of(b))
+    high, low = halves(a)
+    other_high, other_low = halves(b)
+    both = dot(jnp.concatenate([high, low], axis=0), other_high)
+    count = a.shape[0]
+    return both[:count] + (both[count:] + dot(high, other_low))
 
 
 def nearly(pivot):
@@ -106,9 +101,8 @@
     copy.start()
     copy.wait()
     turned = solves_copy[...].T
-    half = upper_ref.shape[0]
-    upper_ref[...] = turned[:half]
-    lower_ref[...] = turned[half:]
+    upper_ref[...] = turned[:UPPER]
+    lower_ref[...] = turned[UPPER:]
 
 
 def fetch(source_ref, target_ref, done, first):
@@ -161,28 +155,35 @@
     choose(copies, coupling_copy, one_ref, chosen_ref, first)
 
 
+def put_pieces(turned_ref, start, upper_ref, lower_ref):
+    width = upper_ref.shape[1]
+    turned_ref[:UPPER, pl.ds(start, width)] = upper_ref[...]
+    turned_ref[UPPER:, pl.ds(start, width)] = lower_ref[...]
+
+
 def early_kernel(chosen_ref, *refs):
     *pieces, turned_ref, terms_ref = refs
     row, _, _ = whereabouts()
     if len(pieces) == 1:
         turned_ref[...] = pieces[0][...]
     else:
-        half, width = pieces[0].shape
-        for i, piece in enumerate(pieces):
-            start = aligned(row ^ (i // 2), width)
-            turned_ref[i % 2 * half:(i % 2 + 1) * half, pl.ds(start, width)] = piece[...]
+        width = pieces[0].shape[1]
+        for k in range(len(pieces) // 2):
+            put_pieces(turned_ref, aligned(row ^ k, width), *pieces[2 * k:2 * k + 2])
         start = aligned(row ^ (len(pieces) // 2), width)
-        turned_ref[:, pl.ds(start, width)] = jnp.zeros((2 * half, width), BF16)
+        turned_ref[:, pl.ds(start, width)] = jnp.zeros((turned_ref.shape[0], width), BF16)
     terms_ref[...] = dot(turned_ref[...], chosen_ref[...])
 
 
-def half_terms(rows, row, chosen_ref, terms_ref, far, whose, out_ref, all_ref):
+def half_terms(rows, chosen_ref, terms_ref, far, whose, out_ref, all_ref, far_ref):
+    row, _, _ = whereabouts()
     half = all_ref.shape[0]
     size = half // rows
     total = terms_ref[pl.ds(aligned(whose, half), half), :]
     if far:
-        width = far[0].shape[1]
-        block = jnp.where(whose == 0, far[0][...], far[1][...])
+        put_pieces(far_ref, 0, *far)
+        width = far_ref.shape[1]
+        block = far_ref[pl.ds(aligned(whose, half), half), :]
         total = total + dot(block, chosen_ref[pl.ds(aligned(row ^ (rows - 1), width), width), :])
     all_ref[...] = total
     for k in range(rows):
@@ -190,20 +191,17 @@
 
 
 def send_kernel(rows, chosen_ref, entry_ref, terms_ref, *refs):
-    *far, send_ref, all_ref = refs
+    *far, send_ref, all_ref, far_ref = refs
+    half_terms(rows, chosen_ref, terms_ref, far, 1 - whereabouts()[1], send_ref, all_ref, far_ref)
+    send_ref[all_ref.shape[0]:, :] = entry_ref[...]
+
+
+def keep_kernel(rows, turned_in, chosen_ref, terms_ref, *refs):
+    *far, turned_ref, keep_ref, all_ref, far_ref = refs
     row, core, _ = whereabouts()
-    half_terms(rows, row, chosen_ref, terms_ref, far, 1 - core, send_ref, all_ref)
-    send_ref[all_ref.shape[0]:, :] = entry_ref[...]
-
-
-def keep_kernel(rows, turned_in, chosen_ref, terms_ref, *refs):
-    *far, turned_ref, keep_ref, all_ref = refs
-    row, core, _ = whereabouts()
-    half_terms(rows, row, chosen_ref, terms_ref, far, core, keep_ref, all_ref)
-    for i, piece in enumerate(far):
-        half, width = piece.shape
-        start = aligned(row ^ (rows - 1), width)
-        turned_ref[i * half:(i + 1) * half, pl.ds(start, width)] = piece[...]
+    half_terms(rows, chosen_ref, terms_ref, far, core, keep_ref, all_ref, far_ref)
+    if far:
+        put_pieces(turned_ref, aligned(row ^ (rows - 1), far_ref.shape[1]), *far)
 
 
 def pair_kernel(rows, keep_ref, got_ref, entry_ref, *out_refs):
@@ -349,9 +347,8 @@
     block, panel = solves.shape
     if rows != 4:
         return [lax.all_gather(solves.T, "row", axis=1, tiled=True)]
-    half = pltpu.VMEM((panel // 2, block), BF16)
     upper, lower = call(
-        turn_kernel, (half, half), solves, remain=1,
+        turn_kernel, (pltpu.VMEM((UPPER, block), BF16), pltpu.VMEM((panel - UPPER, block), BF16)), solves, remain=1,
         scratch=[pltpu.VMEM((block, panel), BF16), pltpu.SemaphoreType.DMA],
     )
     lower_x, upper_y = swap(lower, "row", 1), swap(upper, "row", 2)
@@ -389,7 +386,7 @@
     pieces = gather_pieces(solves, rows, (entry,))
     near, far = pieces[:6], pieces[6:]
     chosen = call(rest_kernel, picked, chosen, one, coupling, remain=1, scratch=chunk_room, aliases={0: 0})
-    room = [pltpu.VMEM((panel // 2, panel), F32)]
+    room = [pltpu.VMEM((panel // 2, panel), F32), pltpu.VMEM((panel, local // rows if rows == 4 else 128), BF16)]
     turned, terms = call(
         early_kernel, (shape((panel, local), BF16), shape((panel, panel), F32)), chosen, *near
     )
@@ -434,12 +431,10 @@
     if split:
         for bit in steps[:-1]:
             count //= 2
-            got = swap(after(bulk_codes, part), "scen", 2 * bit)
+            got = swap(bulk_codes, "scen", 2 * bit)
             own, bulk_codes = call(functools.partial(bulk_sum_kernel, panel), halved(count), own, got)
         got = [swap(bulk_codes, "scen", layers)]
     joined = call(join_kernel, shape((rows * (size + TAIL), panel), I16), part, *shared)
-    if split:
-        joined = after(joined, bulk_codes)
     other = swap(joined, "scen", 1)
     own_half = call(
         functools.partial(own_kernel, rows), shape((panel // 2, panel), F32), joined

time: 59.4 us -> 59.8 us (level)
  waiting for transfers between devices: 17.6 us -> 14.9 us
  Pallas kernels: 18.9 us -> 20.7 us
  starting transfers between devices: 21.9 us -> 23.1 us
    ppermute x20, waiting for transfers between devices: 17.6 us -> 14.9 us  [swap(): return lax.ppermute(x, axis, [(i, i ^ bit) for i in range(count)])]
    pallas_call x16, Pallas kernels: 18.9 us -> 20.7 us  [call(): pl.pallas_call(kernel, name=getattr(kernel, 'func', kernel).__name__, out...]
    ppermute x20, starting transfers between devices: 21.9 us -> 23.1 us  [swap(): return lax.ppermute(x, axis, [(i, i ^ bit) for i in range(count)])]
  transfers between devices with their start and end apart: 20 -> 20, of which waited for: 14 -> 12; matrix products, arithmetic and copies ran while one was open for 0% -> 0% of each run, Pallas kernels for 26% -> 30%
where the time goes in v14:
time: 59.8 us; the launch traced here: 59.6 us
  starting transfers between devices  23.1 us (39%)
  Pallas kernels  20.7 us (35%)
  waiting for transfers between devices  14.9 us (25%)
  between operations  0.8 us (1%)
    ppermute x20, starting transfers between devices, swap(): return lax.ppermute(x, axis, [(i, i ^ bit) for i in range(count)])  23.1 us
    pallas_call x16, Pallas kernels, call(): pl.pallas_call(kernel, name=getattr(kernel, 'func', kernel).__name__, out...  20.7 us
    ppermute x20, waiting for transfers between devices, swap(): return lax.ppermute(x, axis, [(i, i ^ bit) for i in range(count)])  14.9 us
  transfers between devices with their start and end apart: 20, of which 12 were waited for; matrix products, arithmetic and copies ran while one was open for 0% of the time, Pallas kernels for 30%

profile of v14, /device:TPU:0, one launch (start us, length us, event | category | flops | bytes accessed | tf_op | source)
XLA Modules:
  0.0 59.6 jit_solution(15738204795143041335)
XLA Ops:
  0.6 1.2 %turn_kernel.1 = (bf16[288,384]{1,0:T(8,128)(2,1)S(1)}, bf16[224,384]{1,0:T(8,128)(2,1)S(1)}) custom-call(bf16[384,512]{1,0:T(8,128)(2,1)} %bitcast.7), custom_call_target="tpu_custom_call" | custom-call | bytes 1024 | tf_op jit(solution)/shard_map/turn_kernel/pallas_call | solution.py:315
  1.8 3.0 %collective-permute-start.2 = (bf16[288,384]{1,0:T(8,128)(2,1)S(1)}, bf16[288,384]{1,0:T(8,128)(2,1)S(1)}, u32[]{:S(2)}, u32[]{:S(2)}) collective-permute-start(bf16[288,384]{1,0:T(8,128)(2,1)S(1)} %get-tuple-element.34.refs_0_), channel_id=1, source_target_pairs={{0,2},{1,3},{2,0},{3,1},{4,6},{5,7},{6,4},{7,5},{8,10},{9,11},{10,... | collective-permute-start | bytes 663560 | tf_op jit(solution)/shard_map/ppermute | solution.py:330
  4.8 1.5 %collective-permute-start.1 = (bf16[224,384]{1,0:T(8,128)(2,1)S(1)}, bf16[224,384]{1,0:T(8,128)(2,1)S(1)}, u32[]{:S(2)}, u32[]{:S(2)}) collective-permute-start(bf16[224,384]{1,0:T(8,128)(2,1)S(1)} %get-tuple-element.35.refs_1_), channel_id=1, source_target_pairs={{0,1},{1,0},{2,3},{3,2},{4,5},{5,4},{6,7},{7,6},{8,9},{9,8},{10,11... | collective-permute-start | bytes 516104 | tf_op jit(solution)/shard_map/ppermute | solution.py:330
  6.3 0.5 collective-permute-start
  6.9 2.6 %pick_kernel.1 = (bf16[1536,512]{1,0:T(8,128)(2,1)S(1)}, f32[8,512]{1,0:T(8,128)S(1)}, bf16[1024,512]{1,0:T(8,128)(2,1)S(1)}, s32[1,512]{1,0:T(1,128)S(1)}, f32[1,128]{1,0:T(1,128)S(1)}) custom-call(s32[1,512]{1,0:T(1,128)} %bitcast.8, f32[1,128]{1,0:T(1,128)} %bitcast.9, bf16[1536,1024]{1,0:T(8,128)(2,1)} %bitcast.4), custom_call_target="tpu_custom_call" | custom-call | bytes 1024 | tf_op jit(solution)/shard_map/pick_kernel/pallas_call | solution.py:315
  9.5 0.7 %collective-permute-done.2.refs_4_ = bf16[288,384]{1,0:T(8,128)(2,1)S(1)} collective-permute-done((bf16[288,384]{1,0:T(8,128)(2,1)S(1)}, bf16[288,384]{1,0:T(8,128)(2,1)S(1)}, u32[]{:S(2)}, u32[]{:S(2)}) %collective-permute-start.2) | collective-permute-done | bytes 221216 | tf_op jit(solution)/shard_map/ppermute | solution.py:330
  10.3 1.7 %collective-permute-start.4 = (bf16[288,384]{1,0:T(8,128)(2,1)S(1)}, bf16[288,384]{1,0:T(8,128)(2,1)S(1)}, u32[]{:S(2)}, u32[]{:S(2)}) collective-permute-start(bf16[288,384]{1,0:T(8,128)(2,1)S(1)} %collective-permute-done.2.refs_4_), channel_id=1, source_target_pairs={{0,1},{1,0},{2,3},{3,2},{4,5},{5,4},{6,7},{7,6},{8,9},{9,8},{10,11... | collective-permute-start | bytes 663560 | tf_op jit(solution)/shard_map/ppermute | solution.py:330
  12.0 1.5 %collective-permute-start.3 = (bf16[224,384]{1,0:T(8,128)(2,1)S(1)}, bf16[224,384]{1,0:T(8,128)(2,1)S(1)}, u32[]{:S(2)}, u32[]{:S(2)}) collective-permute-start(bf16[224,384]{1,0:T(8,128)(2,1)S(1)} %get-tuple-element.35.refs_1_), channel_id=1, source_target_pairs={{0,2},{1,3},{2,0},{3,1},{4,6},{5,7},{6,4},{7,5},{8,10},{9,11},{10,... | collective-permute-start | bytes 516104 | tf_op jit(solution)/shard_map/ppermute | solution.py:330
  13.5 0.0 collective-permute-done.1.refs_3_
  13.5 0.5 collective-permute-start.5
  14.0 2.3 %rest_kernel.1.chosen_ref = bf16[1536,512]{1,0:T(8,128)(2,1)S(1)} custom-call(bf16[1536,512]{1,0:T(8,128)(2,1)S(1)} %get-tuple-element.32.chosen_in, bf16[1024,512]{1,0:T(8,128)(2,1)S(1)} %get-tuple-element.33.one_ref, bf16[1536,1024]{1,0:T(8,128)(2,1)} %bitcast.5), custom_call_target="tpu_custom_call", output_to_operand_aliasing={{}: (0, {})} | custom-call | bytes 1024 | tf_op jit(solution)/shard_map/rest_kernel/pallas_call | solution.py:315
  16.3 2.5 %collective-permute-done.3.refs_5_ = bf16[224,384]{1,0:T(8,128)(2,1)S(1)} collective-permute-done((bf16[224,384]{1,0:T(8,128)(2,1)S(1)}, bf16[224,384]{1,0:T(8,128)(2,1)S(1)}, u32[]{:S(2)}, u32[]{:S(2)}) %collective-permute-start.3) | collective-permute-done | bytes 172064 | tf_op jit(solution)/shard_map/ppermute | solution.py:330
  18.8 0.0 collective-permute-done.refs_2_
  18.8 1.1 %early_kernel.1 = (bf16[512,1536]{1,0:T(8,128)(2,1)S(1)}, f32[512,512]{1,0:T(8,128)S(1)}) custom-call(bf16[1536,512]{1,0:T(8,128)(2,1)S(1)} %rest_kernel.1.chosen_ref, bf16[288,384]{1,0:T(8,128)(2,1)S(1)} %get-tuple-element.34.refs_0_, bf16[224,384]{1,0:T(8,128)(2,1)S(1)} %get-tuple-element.35.refs_1_, bf16[288,384]{1,0:T(8,128)(2,1)S(1)} %collective-permute-done.refs_2_, ...), custom_call_target="tpu_custom_call" | custom-call | bytes 1024 | tf_op jit(solution)/shard_map/early_kernel/pallas_call | solution.py:315
  19.9 0.7 %collective-permute-done.5.refs_1_ = bf16[224,384]{1,0:T(8,128)(2,1)S(1)} collective-permute-done((bf16[224,384]{1,0:T(8,128)(2,1)S(1)}, bf16[224,384]{1,0:T(8,128)(2,1)S(1)}, u32[]{:S(2)}, u32[]{:S(2)}) %collective-permute-start.5) | collective-permute-done | bytes 172064 | tf_op jit(solution)/shard_map/ppermute | solution.py:330
  20.6 0.0 collective-permute-done.4.refs_0_
  20.6 0.4 send_kernel.1
  21.0 0.1 collective-permute-start.6
  21.1 0.0 copy-start
  21.1 0.4 keep_kernel.1
  21.5 1.5 %collective-permute-done.6.got_ref = f32[264,512]{1,0:T(8,128)S(1)} collective-permute-done((f32[264,512]{1,0:T(8,128)S(1)}, f32[264,512]{1,0:T(8,128)S(1)}, u32[]{:S(2)}, u32[]{:S(2)}) %collective-permute-start.6) | collective-permute-done | bytes 540704 | tf_op jit(solution)/shard_map/ppermute | solution.py:330
  23.0 0.2 pair_kernel.1
  23.1 1.6 %collective-permute-start.7 = (s16[72,512]{1,0:T(8,128)(2,1)S(1)}, s16[72,512]{1,0:T(8,128)(2,1)S(1)}, u32[]{:S(2)}, u32[]{:S(2)}) collective-permute-start(s16[72,512]{1,0:T(8,128)(2,1)S(1)} %get-tuple-element.49), channel_id=1, source_target_pairs={{0,3},{1,2},{2,1},{3,0},{4,7},{5,6},{6,5},{7,4},{8,11},{9,10},{10,... | collective-permute-start | bytes 221192 | tf_op jit(solution)/shard_map/ppermute | solution.py:330
  24.7 1.0 %collective-permute-start.8 = (s16[72,512]{1,0:T(8,128)(2,1)S(1)}, s16[72,512]{1,0:T(8,128)(2,1)S(1)}, u32[]{:S(2)}, u32[]{:S(2)}) collective-permute-start(s16[72,512]{1,0:T(8,128)(2,1)S(1)} %get-tuple-element.50), channel_id=1, source_target_pairs={{0,2},{1,3},{2,0},{3,1},{4,6},{5,7},{6,4},{7,5},{8,10},{9,11},{10,... | collective-permute-start | bytes 221192 | tf_op jit(solution)/shard_map/ppermute | solution.py:330
  25.7 1.0 %collective-permute-start.9 = (s16[72,512]{1,0:T(8,128)(2,1)S(1)}, s16[72,512]{1,0:T(8,128)(2,1)S(1)}, u32[]{:S(2)}, u32[]{:S(2)}) collective-permute-start(s16[72,512]{1,0:T(8,128)(2,1)S(1)} %get-tuple-element.51), channel_id=1, source_target_pairs={{0,1},{1,0},{2,3},{3,2},{4,5},{5,4},{6,7},{7,6},{8,9},{9,8},{10,11... | collective-permute-start | bytes 221192 | tf_op jit(solution)/shard_map/ppermute | solution.py:330
  26.7 0.0 copy-done
  26.7 1.8 %schur_kernel.1 = (f32[2048,128]{1,0:T(8,128)S(1)}, f32[2048,128]{1,0:T(8,128)S(1)}) custom-call(s32[1,512]{1,0:T(1,128)S(1)} %get-tuple-element.43.panel_ref, f32[1,128]{1,0:T(1,128)S(1)} %get-tuple-element.44.own_diagonal_ref, bf16[1536,1024]{1,0:T(8,128)(2,1)S(1)} %bitcast.6, bf16[512,1536]{1,0:T(8,128)(2,1)S(1)} %get-tuple-element.46.turned_ref), custom_call_target="tpu_custom_call" | custom-call | bytes 1024 | tf_op jit(solution)/shard_map/schur_kernel/pallas_call | solution.py:315
  28.5 0.1 collective-permute-done.7.refs_1_
  28.6 1.4 %collective-permute-done.8.refs_2_ = s16[72,512]{1,0:T(8,128)(2,1)S(1)} collective-permute-done((s16[72,512]{1,0:T(8,128)(2,1)S(1)}, s16[72,512]{1,0:T(8,128)(2,1)S(1)}, u32[]{:S(2)}, u32[]{:S(2)}) %collective-permute-start.8) | collective-permute-done | bytes 73760 | tf_op jit(solution)/shard_map/ppermute | solution.py:330
  30.0 0.1 collective-permute-done.9.refs_3_
  30.1 0.1 sum_kernel.2.refs_0_
  30.2 0.1 collective-permute-start.10
  30.3 3.7 %collective-permute-start.13 = (s16[72,512]{1,0:T(8,128)(2,1)S(1)}, s16[72,512]{1,0:T(8,128)(2,1)S(1)}, u32[]{:S(2)}, u32[]{:S(2)}) collective-permute-start(s16[72,512]{1,0:T(8,128)(2,1)S(1)} %sum_kernel.2.refs_0_), channel_id=1, source_target_pairs={{0,24},{4,28},{8,16},{12,20},{16,8},{20,12},{24,0},{28,4},{1,25},{... | collective-permute-start | bytes 221192 | tf_op jit(solution)/shard_map/ppermute | solution.py:330
  34.0 0.0 collective-permute-start.12
  34.0 0.8 %collective-permute-start.11 = (s16[72,512]{1,0:T(8,128)(2,1)S(1)}, s16[72,512]{1,0:T(8,128)(2,1)S(1)}, u32[]{:S(2)}, u32[]{:S(2)}) collective-permute-start(s16[72,512]{1,0:T(8,128)(2,1)S(1)} %sum_kernel.2.refs_0_), channel_id=1, source_target_pairs={{0,8},{4,12},{8,0},{12,4},{16,24},{20,28},{24,16},{28,20},{1,9},{5... | collective-permute-start | bytes 221192 | tf_op jit(solution)/shard_map/ppermute | solution.py:330
  34.8 0.0 collective-permute-done.10.got_ref
  34.8 0.2 bulk_pair_kernel.1
  35.0 1.3 %collective-permute-start.18 = (s16[1056,128]{1,0:T(8,128)(2,1)S(1)}, s16[1056,128]{1,0:T(8,128)(2,1)S(1)}, u32[]{:S(2)}, u32[]{:S(2)}) collective-permute-start(s16[1056,128]{1,0:T(8,128)(2,1)S(1)} %get-tuple-element.55), channel_id=1, source_target_pairs={{0,8},{4,12},{8,0},{12,4},{16,24},{20,28},{24,16},{28,20},{1,9},{5... | collective-permute-start | bytes 811016 | tf_op jit(solution)/shard_map/ppermute | solution.py:330
  36.3 0.9 %collective-permute-done.13.refs_3_ = s16[72,512]{1,0:T(8,128)(2,1)S(1)} collective-permute-done((s16[72,512]{1,0:T(8,128)(2,1)S(1)}, s16[72,512]{1,0:T(8,128)(2,1)S(1)}, u32[]{:S(2)}, u32[]{:S(2)}) %collective-permute-start.13) | collective-permute-done | bytes 73760 | tf_op jit(solution)/shard_map/ppermute | solution.py:330
  37.2 3.6 %collective-permute-done.12.refs_2_ = s16[72,512]{1,0:T(8,128)(2,1)S(1)} collective-permute-done((s16[72,512]{1,0:T(8,128)(2,1)S(1)}, s16[72,512]{1,0:T(8,128)(2,1)S(1)}, u32[]{:S(2)}, u32[]{:S(2)}) %collective-permute-start.12) | collective-permute-done | bytes 73760 | tf_op jit(solution)/shard_map/ppermute | solution.py:330
  40.9 0.0 collective-permute-done.11.refs_1_
  40.9 0.1 sum_kernel.3.refs_0_
  41.0 2.0 %collective-permute-start.16 = (s16[72,512]{1,0:T(8,128)(2,1)S(1)}, s16[72,512]{1,0:T(8,128)(2,1)S(1)}, u32[]{:S(2)}, u32[]{:S(2)}) collective-permute-start(s16[72,512]{1,0:T(8,128)(2,1)S(1)} %sum_kernel.3.refs_0_), channel_id=1, source_target_pairs={{0,3},{1,2},{2,1},{3,0},{4,7},{5,6},{6,5},{7,4},{8,11},{9,10},{10,... | collective-permute-start | bytes 221192 | tf_op jit(solution)/shard_map/ppermute | solution.py:330
  43.0 0.5 collective-permute-start.15
  43.5 1.1 %collective-permute-start.14 = (s16[72,512]{1,0:T(8,128)(2,1)S(1)}, s16[72,512]{1,0:T(8,128)(2,1)S(1)}, u32[]{:S(2)}, u32[]{:S(2)}) collective-permute-start(s16[72,512]{1,0:T(8,128)(2,1)S(1)} %sum_kernel.3.refs_0_), channel_id=1, source_target_pairs={{0,1},{1,0},{2,3},{3,2},{4,5},{5,4},{6,7},{7,6},{8,9},{9,8},{10,11... | collective-permute-start | bytes 221192 | tf_op jit(solution)/shard_map/ppermute | solution.py:330
  44.6 2.1 %collective-permute-done.16.refs_3_ = s16[72,512]{1,0:T(8,128)(2,1)S(1)} collective-permute-done((s16[72,512]{1,0:T(8,128)(2,1)S(1)}, s16[72,512]{1,0:T(8,128)(2,1)S(1)}, u32[]{:S(2)}, u32[]{:S(2)}) %collective-permute-start.16) | collective-permute-done | bytes 73760 | tf_op jit(solution)/shard_map/ppermute | solution.py:330
  46.7 0.7 %collective-permute-done.15.refs_2_ = s16[72,512]{1,0:T(8,128)(2,1)S(1)} collective-permute-done((s16[72,512]{1,0:T(8,128)(2,1)S(1)}, s16[72,512]{1,0:T(8,128)(2,1)S(1)}, u32[]{:S(2)}, u32[]{:S(2)}) %collective-permute-start.15) | collective-permute-done | bytes 73760 | tf_op jit(solution)/shard_map/ppermute | solution.py:330
  47.4 0.4 collective-permute-done.14.refs_1_
  47.9 0.1 collective-permute-start.17
  48.0 0.0 collective-permute-done.18.got_ref
  48.0 0.2 bulk_sum_kernel.1
  48.1 1.3 %collective-permute-start.19 = (s16[528,128]{1,0:T(8,128)(2,1)S(1)}, s16[528,128]{1,0:T(8,128)(2,1)S(1)}, u32[]{:S(2)}, u32[]{:S(2)}) collective-permute-start(s16[528,128]{1,0:T(8,128)(2,1)S(1)} %get-tuple-element.61), channel_id=1, source_target_pairs={{0,16},{4,20},{8,24},{12,28},{16,0},{20,4},{24,8},{28,12},{1,17},{... | collective-permute-start | bytes 405512 | tf_op jit(solution)/shard_map/ppermute | solution.py:330
  49.4 0.2 own_kernel.1.half_ref
  49.6 0.0 collective-permute-done.17.other_ref
  49.6 8.8 %newton_kernel.1 = (f32[256,256]{1,0:T(8,128)S(1)}, f32[256,512]{1,0:T(8,128)S(1)}) custom-call(f32[256,512]{1,0:T(8,128)S(1)} %own_kernel.1.half_ref, s16[320,512]{1,0:T(8,128)(2,1)S(1)} %collective-permute-done.17.other_ref), custom_call_target="tpu_custom_call" | custom-call | bytes 33211024 | tf_op jit(solution)/shard_map/newton_kernel/pallas_call | solution.py:315
  58.3 0.0 collective-permute-done.19.refs_0_
  58.4 1.2 %factor_kernel.1 = (f32[128,1,256]{2,1,0:T(1,128)}, f32[128,1,256]{2,1,0:T(1,128)}) custom-call(f32[256,256]{1,0:T(8,128)S(1)} %get-tuple-element.57.inverse_first_ref, f32[256,512]{1,0:T(8,128)S(1)} %get-tuple-element.58.inverse_second_ref, f32[512,128]{1,0:T(8,128)S(1)} %get-tuple-element.60.rows_ref, s16[528,128]{1,0:T(8,128)(2,1)S(1)} %collective-permute-done.19.refs_0_), custom_call_target="tpu_custom_call" | custom-call | bytes 1024 | tf_op jit(solution)/shard_map/factor_kernel/pallas_call | solution.py:315
  (1 shorter events, 0.0 us)
Async XLA Ops:
  1.8 8.5 %collective-permute-start.2 = (bf16[288,384]{1,0:T(8,128)(2,1)S(1)}, bf16[288,384]{1,0:T(8,128)(2,1)S(1)}, u32[]{:S(2)}, u32[]{:S(2)}) collective-permute-start(bf16[288,384]{1,0:T(8,128)(2,1)S(1)} %get-tuple-element.34.refs_0_), channel_id=1, source_target_pairs={{0,2},{1,3},{2,0},{3,1},{4,6},{5,7},{6,4},{7,5},{8,10},{9,11},{10,... | collective-permute-start | bytes 663560 | tf_op jit(solution)/shard_map/ppermute | solution.py:330
  4.8 8.7 %collective-permute-start.1 = (bf16[224,384]{1,0:T(8,128)(2,1)S(1)}, bf16[224,384]{1,0:T(8,128)(2,1)S(1)}, u32[]{:S(2)}, u32[]{:S(2)}) collective-permute-start(bf16[224,384]{1,0:T(8,128)(2,1)S(1)} %get-tuple-element.35.refs_1_), channel_id=1, source_target_pairs={{0,1},{1,0},{2,3},{3,2},{4,5},{5,4},{6,7},{7,6},{8,9},{9,8},{10,11... | collective-permute-start | bytes 516104 | tf_op jit(solution)/shard_map/ppermute | solution.py:330
  6.3 12.5 %collective-permute-start = (bf16[288,384]{1,0:T(8,128)(2,1)S(1)}, bf16[288,384]{1,0:T(8,128)(2,1)S(1)}, u32[]{:S(2)}, u32[]{:S(2)}) collective-permute-start(bf16[288,384]{1,0:T(8,128)(2,1)S(1)} %get-tuple-element.34.refs_0_), channel_id=1, source_target_pairs={{0,1},{1,0},{2,3},{3,2},{4,5},{5,4},{6,7},{7,6},{8,9},{9,8},{10,11... | collective-permute-start | bytes 663560 | tf_op jit(solution)/shard_map/ppermute | solution.py:330
  10.3 10.4 %collective-permute-start.4 = (bf16[288,384]{1,0:T(8,128)(2,1)S(1)}, bf16[288,384]{1,0:T(8,128)(2,1)S(1)}, u32[]{:S(2)}, u32[]{:S(2)}) collective-permute-start(bf16[288,384]{1,0:T(8,128)(2,1)S(1)} %collective-permute-done.2.refs_4_), channel_id=1, source_target_pairs={{0,1},{1,0},{2,3},{3,2},{4,5},{5,4},{6,7},{7,6},{8,9},{9,8},{10,11... | collective-permute-start | bytes 663560 | tf_op jit(solution)/shard_map/ppermute | solution.py:330
  12.0 6.8 %collective-permute-start.3 = (bf16[224,384]{1,0:T(8,128)(2,1)S(1)}, bf16[224,384]{1,0:T(8,128)(2,1)S(1)}, u32[]{:S(2)}, u32[]{:S(2)}) collective-permute-start(bf16[224,384]{1,0:T(8,128)(2,1)S(1)} %get-tuple-element.35.refs_1_), channel_id=1, source_target_pairs={{0,2},{1,3},{2,0},{3,1},{4,6},{5,7},{6,4},{7,5},{8,10},{9,11},{10,... | collective-permute-start | bytes 516104 | tf_op jit(solution)/shard_map/ppermute | solution.py:330
  13.5 7.1 %collective-permute-start.5 = (bf16[224,384]{1,0:T(8,128)(2,1)S(1)}, bf16[224,384]{1,0:T(8,128)(2,1)S(1)}, u32[]{:S(2)}, u32[]{:S(2)}) collective-permute-start(bf16[224,384]{1,0:T(8,128)(2,1)S(1)} %collective-permute-done.1.refs_3_), channel_id=1, source_target_pairs={{0,2},{1,3},{2,0},{3,1},{4,6},{5,7},{6,4},{7,5},{8,10},{9,11},{10,... | collective-permute-start | bytes 516104 | tf_op jit(solution)/shard_map/ppermute | solution.py:330
  21.0 2.0 %collective-permute-start.6 = (f32[264,512]{1,0:T(8,128)S(1)}, f32[264,512]{1,0:T(8,128)S(1)}, u32[]{:S(2)}, u32[]{:S(2)}) collective-permute-start(f32[264,512]{1,0:T(8,128)S(1)} %send_kernel.1), channel_id=1, source_target_pairs={{0,4},{4,0},{8,12},{12,8},{16,20},{20,16},{24,28},{28,24},{1,5},{5... | collective-permute-start | bytes 1622024 | tf_op jit(solution)/shard_map/ppermute | solution.py:330
  21.1 5.6 %copy-start = (bf16[1,1536,1024]{2,1,0:T(8,128)(2,1)S(1)}, bf16[1,1536,1024]{2,1,0:T(8,128)(2,1)}, u32[]{:S(2)}) copy-start(bf16[1,1536,1024]{2,1,0:T(8,128)(2,1)} %param.4) | copy-start | bytes 9437188
  23.1 5.5 %collective-permute-start.7 = (s16[72,512]{1,0:T(8,128)(2,1)S(1)}, s16[72,512]{1,0:T(8,128)(2,1)S(1)}, u32[]{:S(2)}, u32[]{:S(2)}) collective-permute-start(s16[72,512]{1,0:T(8,128)(2,1)S(1)} %get-tuple-element.49), channel_id=1, source_target_pairs={{0,3},{1,2},{2,1},{3,0},{4,7},{5,6},{6,5},{7,4},{8,11},{9,10},{10,... | collective-permute-start | bytes 221192 | tf_op jit(solution)/shard_map/ppermute | solution.py:330
  24.7 5.3 %collective-permute-start.8 = (s16[72,512]{1,0:T(8,128)(2,1)S(1)}, s16[72,512]{1,0:T(8,128)(2,1)S(1)}, u32[]{:S(2)}, u32[]{:S(2)}) collective-permute-start(s16[72,512]{1,0:T(8,128)(2,1)S(1)} %get-tuple-element.50), channel_id=1, source_target_pairs={{0,2},{1,3},{2,0},{3,1},{4,6},{5,7},{6,4},{7,5},{8,10},{9,11},{10,... | collective-permute-start | bytes 221192 | tf_op jit(solution)/shard_map/ppermute | solution.py:330
  25.7 4.4 %collective-permute-start.9 = (s16[72,512]{1,0:T(8,128)(2,1)S(1)}, s16[72,512]{1,0:T(8,128)(2,1)S(1)}, u32[]{:S(2)}, u32[]{:S(2)}) collective-permute-start(s16[72,512]{1,0:T(8,128)(2,1)S(1)} %get-tuple-element.51), channel_id=1, source_target_pairs={{0,1},{1,0},{2,3},{3,2},{4,5},{5,4},{6,7},{7,6},{8,9},{9,8},{10,11... | collective-permute-start | bytes 221192 | tf_op jit(solution)/shard_map/ppermute | solution.py:330
  30.2 4.5 %collective-permute-start.10 = (f32[2048,128]{1,0:T(8,128)S(1)}, f32[2048,128]{1,0:T(8,128)S(1)}, u32[]{:S(2)}, u32[]{:S(2)}) collective-permute-start(f32[2048,128]{1,0:T(8,128)S(1)} %get-tuple-element.54), channel_id=1, source_target_pairs={{0,4},{4,0},{8,12},{12,8},{16,20},{20,16},{24,28},{28,24},{1,5},{5... | collective-permute-start | bytes 3145736 | tf_op jit(solution)/shard_map/ppermute | solution.py:330
  30.3 6.9 %collective-permute-start.13 = (s16[72,512]{1,0:T(8,128)(2,1)S(1)}, s16[72,512]{1,0:T(8,128)(2,1)S(1)}, u32[]{:S(2)}, u32[]{:S(2)}) collective-permute-start(s16[72,512]{1,0:T(8,128)(2,1)S(1)} %sum_kernel.2.refs_0_), channel_id=1, source_target_pairs={{0,24},{4,28},{8,16},{12,20},{16,8},{20,12},{24,0},{28,4},{1,25},{... | collective-permute-start | bytes 221192 | tf_op jit(solution)/shard_map/ppermute | solution.py:330
  34.0 6.9 %collective-permute-start.12 = (s16[72,512]{1,0:T(8,128)(2,1)S(1)}, s16[72,512]{1,0:T(8,128)(2,1)S(1)}, u32[]{:S(2)}, u32[]{:S(2)}) collective-permute-start(s16[72,512]{1,0:T(8,128)(2,1)S(1)} %sum_kernel.2.refs_0_), channel_id=1, source_target_pairs={{0,16},{4,20},{8,24},{12,28},{16,0},{20,4},{24,8},{28,12},{1,17},{... | collective-permute-start | bytes 221192 | tf_op jit(solution)/shard_map/ppermute | solution.py:330
  34.0 6.9 %collective-permute-start.11 = (s16[72,512]{1,0:T(8,128)(2,1)S(1)}, s16[72,512]{1,0:T(8,128)(2,1)S(1)}, u32[]{:S(2)}, u32[]{:S(2)}) collective-permute-start(s16[72,512]{1,0:T(8,128)(2,1)S(1)} %sum_kernel.2.refs_0_), channel_id=1, source_target_pairs={{0,8},{4,12},{8,0},{12,4},{16,24},{20,28},{24,16},{28,20},{1,9},{5... | collective-permute-start | bytes 221192 | tf_op jit(solution)/shard_map/ppermute | solution.py:330
  35.0 12.9 %collective-permute-start.18 = (s16[1056,128]{1,0:T(8,128)(2,1)S(1)}, s16[1056,128]{1,0:T(8,128)(2,1)S(1)}, u32[]{:S(2)}, u32[]{:S(2)}) collective-permute-start(s16[1056,128]{1,0:T(8,128)(2,1)S(1)} %get-tuple-element.55), channel_id=1, source_target_pairs={{0,8},{4,12},{8,0},{12,4},{16,24},{20,28},{24,16},{28,20},{1,9},{5... | collective-permute-start | bytes 811016 | tf_op jit(solution)/shard_map/ppermute | solution.py:330
  41.0 5.7 %collective-permute-start.16 = (s16[72,512]{1,0:T(8,128)(2,1)S(1)}, s16[72,512]{1,0:T(8,128)(2,1)S(1)}, u32[]{:S(2)}, u32[]{:S(2)}) collective-permute-start(s16[72,512]{1,0:T(8,128)(2,1)S(1)} %sum_kernel.3.refs_0_), channel_id=1, source_target_pairs={{0,3},{1,2},{2,1},{3,0},{4,7},{5,6},{6,5},{7,4},{8,11},{9,10},{10,... | collective-permute-start | bytes 221192 | tf_op jit(solution)/shard_map/ppermute | solution.py:330
  43.0 4.4 %collective-permute-start.15 = (s16[72,512]{1,0:T(8,128)(2,1)S(1)}, s16[72,512]{1,0:T(8,128)(2,1)S(1)}, u32[]{:S(2)}, u32[]{:S(2)}) collective-permute-start(s16[72,512]{1,0:T(8,128)(2,1)S(1)} %sum_kernel.3.refs_0_), channel_id=1, source_target_pairs={{0,2},{1,3},{2,0},{3,1},{4,6},{5,7},{6,4},{7,5},{8,10},{9,11},{10,... | collective-permute-start | bytes 221192 | tf_op jit(solution)/shard_map/ppermute | solution.py:330
  43.5 4.4 %collective-permute-start.14 = (s16[72,512]{1,0:T(8,128)(2,1)S(1)}, s16[72,512]{1,0:T(8,128)(2,1)S(1)}, u32[]{:S(2)}, u32[]{:S(2)}) collective-permute-start(s16[72,512]{1,0:T(8,128)(2,1)S(1)} %sum_kernel.3.refs_0_), channel_id=1, source_target_pairs={{0,1},{1,0},{2,3},{3,2},{4,5},{5,4},{6,7},{7,6},{8,9},{9,8},{10,11... | collective-permute-start | bytes 221192 | tf_op jit(solution)/shard_map/ppermute | solution.py:330
  47.9 1.7 %collective-permute-start.17 = (s16[320,512]{1,0:T(8,128)(2,1)S(1)}, s16[320,512]{1,0:T(8,128)(2,1)S(1)}, u32[]{:S(2)}, u32[]{:S(2)}) collective-permute-start(s16[320,512]{1,0:T(8,128)(2,1)S(1)} %join_kernel.1.own_ref), channel_id=1, source_target_pairs={{0,4},{4,0},{8,12},{12,8},{16,20},{20,16},{24,28},{28,24},{1,5},{5... | collective-permute-start | bytes 983048 | tf_op jit(solution)/shard_map/ppermute | solution.py:330
  48.1 10.2 %collective-permute-start.19 = (s16[528,128]{1,0:T(8,128)(2,1)S(1)}, s16[528,128]{1,0:T(8,128)(2,1)S(1)}, u32[]{:S(2)}, u32[]{:S(2)}) collective-permute-start(s16[528,128]{1,0:T(8,128)(2,1)S(1)} %get-tuple-element.61), channel_id=1, source_target_pairs={{0,16},{4,20},{8,24},{12,28},{16,0},{20,4},{24,8},{28,12},{1,17},{... | collective-permute-start | bytes 405512 | tf_op jit(solution)/shard_map/ppermute | solution.py:330

commit v15 on v13

--- a/solution.py
+++ b/solution.py
@@ -325,7 +325,7 @@
         scratch_shapes=scratch,
         input_output_aliases=aliases or {},
         compiler_params=pltpu.CompilerParams(vmem_limit_bytes=12 << 20),
-        cost_estimate=pl.CostEstimate(flops=0, bytes_accessed=int(micros * 3.69e6) + 1024, transcendentals=0),
+        cost_estimate=pl.CostEstimate(flops=int(micros * 1.15e9), bytes_accessed=1024, transcendentals=0),
     )(*args)
 
 
@@ -416,10 +416,10 @@
         bulk = shape((layers * panel, share), F32)
         halved = lambda count: (shape((count * panel, share), F32), shape((count * (panel + TAIL), share), I16))
         own, send_rows = call(
-            schur_kernel, (bulk, bulk), panel_row, diagonal_row, coupling, after(turned, part)
+            schur_kernel, (bulk, bulk), panel_row, diagonal_row, coupling, after(turned, part), micros=2.0
         )
-        part = call(sum_kernel, coded, after(part, own), *arrived)
-        got = swap(after(send_rows, part), "scen", 1)
+        part = call(sum_kernel, coded, after(part, own), *arrived, micros=10.0)
+        got = swap(send_rows, "scen", 1)
     else:
         own, got = lax.psum_scatter(dot(turned, coupling), "scen", scatter_dimension=1, tiled=True), []
         mine = first_row + jnp.arange(share, dtype=jnp.int32)
@@ -428,7 +428,7 @@
     if split:
         others = [swap(part, "scen", 2 * k) for k in range(1, layers)]
         own, bulk_codes = call(functools.partial(bulk_pair_kernel, panel), halved(count), after(own, part), got)
-        part = call(sum_kernel, coded, after(part, bulk_codes), *others)
+        part = call(sum_kernel, coded, after(part, bulk_codes), *others, micros=5.0)
     else:
         for bit in steps:
             part = call(sum_kernel, coded, part, swap(part, "scen", 2 * bit))
@@ -439,6 +439,8 @@
             got = swap(bulk_codes, "scen", 2 * bit)
             own, bulk_codes = call(functools.partial(bulk_sum_kernel, panel), halved(count), own, got)
         got = [swap(bulk_codes, "scen", layers)]
+    if split:
+        part = after(part, bulk_codes)
     joined = call(join_kernel, shape((rows * (size + TAIL), panel), I16), part, *shared)
     other = swap(joined, "scen", 1)
     own_half = call(
@@ -446,7 +448,7 @@
     )
     inverse_first, inverse_second = call(
         functools.partial(newton_kernel, rows), (shape((half, half), F32), shape((half, panel), F32)),
-        own_half, other, micros=9.0, scratch=[pltpu.VMEM((panel, panel), F32)],
+        own_half, other, scratch=[pltpu.VMEM((panel, panel), F32)],
     )
     out = jax.ShapeDtypeStruct((share, 1, half), F32)
     return call(

time: 58.3 us -> 57.8 us (level)
  waiting for transfers between devices: 16.9 us -> 16.1 us
    ppermute x20, waiting for transfers between devices: 16.9 us -> 16.1 us  [swap(): return lax.ppermute(x, axis, [(i, i ^ bit) for i in range(count)])]
  transfers between devices with their start and end apart: 20 -> 20, of which waited for: 13 -> 15; matrix products, arithmetic and copies ran while one was open for 0% -> 0% of each run, Pallas kernels for 27% -> 28%
where the time goes in v15:
time: 57.8 us; the launch traced here: 57.6 us
  starting transfers between devices  21.8 us (38%)
  Pallas kernels  18.9 us (33%)
  waiting for transfers between devices  16.1 us (28%)
  between operations  0.81 us (1%)
    ppermute x20, starting transfers between devices, swap(): return lax.ppermute(x, axis, [(i, i ^ bit) for i in range(count)])  21.8 us
    pallas_call x16, Pallas kernels, call(): pl.pallas_call(kernel, name=getattr(kernel, 'func', kernel).__name__, out...  18.9 us
    ppermute x20, waiting for transfers between devices, swap(): return lax.ppermute(x, axis, [(i, i ^ bit) for i in range(count)])  16.1 us
  transfers between devices with their start and end apart: 20, of which 15 were waited for; matrix products, arithmetic and copies ran while one was open for 0% of the time, Pallas kernels for 28%

profile of v15, /device:TPU:0, one launch (start us, length us, event | category | flops | bytes accessed | tf_op | source)
XLA Modules:
  0.0 57.6 jit_solution(7175853472111600213)
XLA Ops:
  0.6 1.2 %turn_kernel.1 = (bf16[256,384]{1,0:T(8,128)(2,1)S(1)}, bf16[256,384]{1,0:T(8,128)(2,1)S(1)}) custom-call(bf16[384,512]{1,0:T(8,128)(2,1)} %bitcast.7), custom_call_target="tpu_custom_call" | custom-call | bytes 1024 | tf_op jit(solution)/shard_map/turn_kernel/pallas_call | solution.py:319
  1.8 3.0 %collective-permute-start.1 = (bf16[256,384]{1,0:T(8,128)(2,1)S(1)}, bf16[256,384]{1,0:T(8,128)(2,1)S(1)}, u32[]{:S(2)}, u32[]{:S(2)}) collective-permute-start(bf16[256,384]{1,0:T(8,128)(2,1)S(1)} %get-tuple-element.35.refs_1_), channel_id=1, source_target_pairs={{0,1},{1,0},{2,3},{3,2},{4,5},{5,4},{6,7},{7,6},{8,9},{9,8},{10,11... | collective-permute-start | bytes 589832 | tf_op jit(solution)/shard_map/ppermute | solution.py:334
  4.8 1.5 %collective-permute-start.2 = (bf16[256,384]{1,0:T(8,128)(2,1)S(1)}, bf16[256,384]{1,0:T(8,128)(2,1)S(1)}, u32[]{:S(2)}, u32[]{:S(2)}) collective-permute-start(bf16[256,384]{1,0:T(8,128)(2,1)S(1)} %get-tuple-element.34.refs_0_), channel_id=1, source_target_pairs={{0,2},{1,3},{2,0},{3,1},{4,6},{5,7},{6,4},{7,5},{8,10},{9,11},{10,... | collective-permute-start | bytes 589832 | tf_op jit(solution)/shard_map/ppermute | solution.py:334
  6.3 0.5 collective-permute-start
  6.9 0.1 collective-permute-start.3
  6.9 2.6 %pick_kernel.1 = (bf16[1536,512]{1,0:T(8,128)(2,1)S(1)}, f32[8,512]{1,0:T(8,128)S(1)}, bf16[1024,512]{1,0:T(8,128)(2,1)S(1)}, s32[1,512]{1,0:T(1,128)S(1)}, f32[1,128]{1,0:T(1,128)S(1)}) custom-call(s32[1,512]{1,0:T(1,128)} %bitcast.8, f32[1,128]{1,0:T(1,128)} %bitcast.9, bf16[1536,1024]{1,0:T(8,128)(2,1)} %bitcast.4), custom_call_target="tpu_custom_call" | custom-call | bytes 1024 | tf_op jit(solution)/shard_map/pick_kernel/pallas_call | solution.py:319
  9.6 1.0 %collective-permute-done.1.refs_3_ = bf16[256,384]{1,0:T(8,128)(2,1)S(1)} collective-permute-done((bf16[256,384]{1,0:T(8,128)(2,1)S(1)}, bf16[256,384]{1,0:T(8,128)(2,1)S(1)}, u32[]{:S(2)}, u32[]{:S(2)}) %collective-permute-start.1) | collective-permute-done | bytes 196640 | tf_op jit(solution)/shard_map/ppermute | solution.py:334
  10.5 2.1 %collective-permute-done.2.refs_4_ = bf16[256,384]{1,0:T(8,128)(2,1)S(1)} collective-permute-done((bf16[256,384]{1,0:T(8,128)(2,1)S(1)}, bf16[256,384]{1,0:T(8,128)(2,1)S(1)}, u32[]{:S(2)}, u32[]{:S(2)}) %collective-permute-start.2) | collective-permute-done | bytes 196640 | tf_op jit(solution)/shard_map/ppermute | solution.py:334
  12.6 0.0 collective-permute-start.4
  12.7 2.0 %collective-permute-start.5 = (bf16[256,384]{1,0:T(8,128)(2,1)S(1)}, bf16[256,384]{1,0:T(8,128)(2,1)S(1)}, u32[]{:S(2)}, u32[]{:S(2)}) collective-permute-start(bf16[256,384]{1,0:T(8,128)(2,1)S(1)} %collective-permute-done.1.refs_3_), channel_id=1, source_target_pairs={{0,2},{1,3},{2,0},{3,1},{4,6},{5,7},{6,4},{7,5},{8,10},{9,11},{10,... | collective-permute-start | bytes 589832 | tf_op jit(solution)/shard_map/ppermute | solution.py:334
  14.7 2.3 %rest_kernel.1.chosen_ref = bf16[1536,512]{1,0:T(8,128)(2,1)S(1)} custom-call(bf16[1536,512]{1,0:T(8,128)(2,1)S(1)} %get-tuple-element.32.chosen_in, bf16[1024,512]{1,0:T(8,128)(2,1)S(1)} %get-tuple-element.33.one_ref, bf16[1536,1024]{1,0:T(8,128)(2,1)} %bitcast.5), custom_call_target="tpu_custom_call", output_to_operand_aliasing={{}: (0, {})} | custom-call | bytes 1024 | tf_op jit(solution)/shard_map/rest_kernel/pallas_call | solution.py:319
  17.0 0.0 collective-permute-done.refs_2_
  17.0 0.0 collective-permute-done.3.refs_5_
  17.0 1.1 %early_kernel.1 = (bf16[512,1536]{1,0:T(8,128)(2,1)S(1)}, f32[512,512]{1,0:T(8,128)S(1)}) custom-call(bf16[1536,512]{1,0:T(8,128)(2,1)S(1)} %rest_kernel.1.chosen_ref, bf16[256,384]{1,0:T(8,128)(2,1)S(1)} %get-tuple-element.34.refs_0_, bf16[256,384]{1,0:T(8,128)(2,1)S(1)} %get-tuple-element.35.refs_1_, bf16[256,384]{1,0:T(8,128)(2,1)S(1)} %collective-permute-done.refs_2_, ...), custom_call_target="tpu_custom_call" | custom-call | bytes 1024 | tf_op jit(solution)/shard_map/early_kernel/pallas_call | solution.py:319
  18.1 0.2 collective-permute-done.4.refs_0_
  18.3 1.3 %collective-permute-done.5.refs_1_ = bf16[256,384]{1,0:T(8,128)(2,1)S(1)} collective-permute-done((bf16[256,384]{1,0:T(8,128)(2,1)S(1)}, bf16[256,384]{1,0:T(8,128)(2,1)S(1)}, u32[]{:S(2)}, u32[]{:S(2)}) %collective-permute-start.5) | collective-permute-done | bytes 196640 | tf_op jit(solution)/shard_map/ppermute | solution.py:334
  19.6 0.3 send_kernel.1
  19.9 0.1 collective-permute-start.6
  20.0 0.0 copy-start
  20.0 0.4 keep_kernel.1
  20.4 1.5 %collective-permute-done.6.got_ref = f32[264,512]{1,0:T(8,128)S(1)} collective-permute-done((f32[264,512]{1,0:T(8,128)S(1)}, f32[264,512]{1,0:T(8,128)S(1)}, u32[]{:S(2)}, u32[]{:S(2)}) %collective-permute-start.6) | collective-permute-done | bytes 540704 | tf_op jit(solution)/shard_map/ppermute | solution.py:334
  21.9 0.2 pair_kernel.1
  22.1 1.8 %collective-permute-start.7 = (s16[72,512]{1,0:T(8,128)(2,1)S(1)}, s16[72,512]{1,0:T(8,128)(2,1)S(1)}, u32[]{:S(2)}, u32[]{:S(2)}) collective-permute-start(s16[72,512]{1,0:T(8,128)(2,1)S(1)} %get-tuple-element.49), channel_id=1, source_target_pairs={{0,3},{1,2},{2,1},{3,0},{4,7},{5,6},{6,5},{7,4},{8,11},{9,10},{10,... | collective-permute-start | bytes 221192 | tf_op jit(solution)/shard_map/ppermute | solution.py:334
  23.9 0.5 collective-permute-start.8
  24.4 1.3 %collective-permute-start.9 = (s16[72,512]{1,0:T(8,128)(2,1)S(1)}, s16[72,512]{1,0:T(8,128)(2,1)S(1)}, u32[]{:S(2)}, u32[]{:S(2)}) collective-permute-start(s16[72,512]{1,0:T(8,128)(2,1)S(1)} %get-tuple-element.51), channel_id=1, source_target_pairs={{0,1},{1,0},{2,3},{3,2},{4,5},{5,4},{6,7},{7,6},{8,9},{9,8},{10,11... | collective-permute-start | bytes 221192 | tf_op jit(solution)/shard_map/ppermute | solution.py:334
  25.6 0.0 copy-done
  25.7 1.8 %schur_kernel.1 = (f32[2048,128]{1,0:T(8,128)S(1)}, f32[2048,128]{1,0:T(8,128)S(1)}) custom-call(s32[1,512]{1,0:T(1,128)S(1)} %get-tuple-element.43.panel_ref, f32[1,128]{1,0:T(1,128)S(1)} %get-tuple-element.44.own_diagonal_ref, bf16[1536,1024]{1,0:T(8,128)(2,1)S(1)} %bitcast.6, bf16[512,1536]{1,0:T(8,128)(2,1)S(1)} %get-tuple-element.46.turned_ref), custom_call_target="tpu_custom_call" | custom-call | flops 2300000000 | bytes 1024 | tf_op jit(solution)/shard_map/schur_kernel/pallas_call | solution.py:319
  27.5 0.1 collective-permute-start.10
  27.5 0.0 collective-permute-done.7.refs_1_
  27.6 1.4 %collective-permute-done.8.refs_2_ = s16[72,512]{1,0:T(8,128)(2,1)S(1)} collective-permute-done((s16[72,512]{1,0:T(8,128)(2,1)S(1)}, s16[72,512]{1,0:T(8,128)(2,1)S(1)}, u32[]{:S(2)}, u32[]{:S(2)}) %collective-permute-start.8) | collective-permute-done | bytes 73760 | tf_op jit(solution)/shard_map/ppermute | solution.py:334
  28.9 0.1 collective-permute-done.9.refs_3_
  29.0 0.1 sum_kernel.2.refs_0_
  29.1 3.7 %collective-permute-start.13 = (s16[72,512]{1,0:T(8,128)(2,1)S(1)}, s16[72,512]{1,0:T(8,128)(2,1)S(1)}, u32[]{:S(2)}, u32[]{:S(2)}) collective-permute-start(s16[72,512]{1,0:T(8,128)(2,1)S(1)} %sum_kernel.2.refs_0_), channel_id=1, source_target_pairs={{0,24},{4,28},{8,16},{12,20},{16,8},{20,12},{24,0},{28,4},{1,25},{... | collective-permute-start | bytes 221192 | tf_op jit(solution)/shard_map/ppermute | solution.py:334
  32.8 0.0 collective-permute-start.12
  32.8 0.8 %collective-permute-start.11 = (s16[72,512]{1,0:T(8,128)(2,1)S(1)}, s16[72,512]{1,0:T(8,128)(2,1)S(1)}, u32[]{:S(2)}, u32[]{:S(2)}) collective-permute-start(s16[72,512]{1,0:T(8,128)(2,1)S(1)} %sum_kernel.2.refs_0_), channel_id=1, source_target_pairs={{0,8},{4,12},{8,0},{12,4},{16,24},{20,28},{24,16},{28,20},{1,9},{5... | collective-permute-start | bytes 221192 | tf_op jit(solution)/shard_map/ppermute | solution.py:334
  33.6 0.0 collective-permute-done.10.got_ref
  33.6 0.2 bulk_pair_kernel.1
  33.8 1.3 %collective-permute-start.14 = (s16[1056,128]{1,0:T(8,128)(2,1)S(1)}, s16[1056,128]{1,0:T(8,128)(2,1)S(1)}, u32[]{:S(2)}, u32[]{:S(2)}) collective-permute-start(s16[1056,128]{1,0:T(8,128)(2,1)S(1)} %get-tuple-element.54), channel_id=1, source_target_pairs={{0,8},{4,12},{8,0},{12,4},{16,24},{20,28},{24,16},{28,20},{1,9},{5... | collective-permute-start | bytes 811016 | tf_op jit(solution)/shard_map/ppermute | solution.py:334
  35.1 0.8 %collective-permute-done.13.refs_3_ = s16[72,512]{1,0:T(8,128)(2,1)S(1)} collective-permute-done((s16[72,512]{1,0:T(8,128)(2,1)S(1)}, s16[72,512]{1,0:T(8,128)(2,1)S(1)}, u32[]{:S(2)}, u32[]{:S(2)}) %collective-permute-start.13) | collective-permute-done | bytes 73760 | tf_op jit(solution)/shard_map/ppermute | solution.py:334
  35.9 3.4 %collective-permute-done.12.refs_2_ = s16[72,512]{1,0:T(8,128)(2,1)S(1)} collective-permute-done((s16[72,512]{1,0:T(8,128)(2,1)S(1)}, s16[72,512]{1,0:T(8,128)(2,1)S(1)}, u32[]{:S(2)}, u32[]{:S(2)}) %collective-permute-start.12) | collective-permute-done | bytes 73760 | tf_op jit(solution)/shard_map/ppermute | solution.py:334
  39.3 0.3 collective-permute-done.11.refs_1_
  39.5 0.1 sum_kernel.3.refs_0_
  39.7 2.1 %collective-permute-start.17 = (s16[72,512]{1,0:T(8,128)(2,1)S(1)}, s16[72,512]{1,0:T(8,128)(2,1)S(1)}, u32[]{:S(2)}, u32[]{:S(2)}) collective-permute-start(s16[72,512]{1,0:T(8,128)(2,1)S(1)} %sum_kernel.3.refs_0_), channel_id=1, source_target_pairs={{0,3},{1,2},{2,1},{3,0},{4,7},{5,6},{6,5},{7,4},{8,11},{9,10},{10,... | collective-permute-start | bytes 221192 | tf_op jit(solution)/shard_map/ppermute | solution.py:334
  41.8 0.4 collective-permute-start.16
  42.2 1.1 %collective-permute-start.15 = (s16[72,512]{1,0:T(8,128)(2,1)S(1)}, s16[72,512]{1,0:T(8,128)(2,1)S(1)}, u32[]{:S(2)}, u32[]{:S(2)}) collective-permute-start(s16[72,512]{1,0:T(8,128)(2,1)S(1)} %sum_kernel.3.refs_0_), channel_id=1, source_target_pairs={{0,1},{1,0},{2,3},{3,2},{4,5},{5,4},{6,7},{7,6},{8,9},{9,8},{10,11... | collective-permute-start | bytes 221192 | tf_op jit(solution)/shard_map/ppermute | solution.py:334
  43.2 1.2 %collective-permute-done.14.got_ref = s16[1056,128]{1,0:T(8,128)(2,1)S(1)} collective-permute-done((s16[1056,128]{1,0:T(8,128)(2,1)S(1)}, s16[1056,128]{1,0:T(8,128)(2,1)S(1)}, u32[]{:S(2)}, u32[]{:S(2)}) %collective-permute-start.14) | collective-permute-done | bytes 270368 | tf_op jit(solution)/shard_map/ppermute | solution.py:334
  44.4 0.2 bulk_sum_kernel.1
  44.6 0.9 %collective-permute-done.17.refs_3_ = s16[72,512]{1,0:T(8,128)(2,1)S(1)} collective-permute-done((s16[72,512]{1,0:T(8,128)(2,1)S(1)}, s16[72,512]{1,0:T(8,128)(2,1)S(1)}, u32[]{:S(2)}, u32[]{:S(2)}) %collective-permute-start.17) | collective-permute-done | bytes 73760 | tf_op jit(solution)/shard_map/ppermute | solution.py:334
  45.5 0.7 %collective-permute-done.16.refs_2_ = s16[72,512]{1,0:T(8,128)(2,1)S(1)} collective-permute-done((s16[72,512]{1,0:T(8,128)(2,1)S(1)}, s16[72,512]{1,0:T(8,128)(2,1)S(1)}, u32[]{:S(2)}, u32[]{:S(2)}) %collective-permute-start.16) | collective-permute-done | bytes 73760 | tf_op jit(solution)/shard_map/ppermute | solution.py:334
  46.2 0.3 collective-permute-done.15.refs_1_
  46.5 0.1 collective-permute-start.18
  46.6 1.5 %collective-permute-start.19 = (s16[528,128]{1,0:T(8,128)(2,1)S(1)}, s16[528,128]{1,0:T(8,128)(2,1)S(1)}, u32[]{:S(2)}, u32[]{:S(2)}) collective-permute-start(s16[528,128]{1,0:T(8,128)(2,1)S(1)} %get-tuple-element.57), channel_id=1, source_target_pairs={{0,16},{4,20},{8,24},{12,28},{16,0},{20,4},{24,8},{28,12},{1,17},{... | collective-permute-start | bytes 405512 | tf_op jit(solution)/shard_map/ppermute | solution.py:334
  48.1 0.2 own_kernel.1.half_ref
  48.3 0.0 collective-permute-done.18.other_ref
  48.3 7.0 %newton_kernel.1 = (f32[256,256]{1,0:T(8,128)S(1)}, f32[256,512]{1,0:T(8,128)S(1)}) custom-call(f32[256,512]{1,0:T(8,128)S(1)} %own_kernel.1.half_ref, s16[320,512]{1,0:T(8,128)(2,1)S(1)} %collective-permute-done.18.other_ref), custom_call_target="tpu_custom_call" | custom-call | bytes 1024 | tf_op jit(solution)/shard_map/newton_kernel/pallas_call | solution.py:319
  55.3 1.1 %collective-permute-done.19.refs_0_ = s16[528,128]{1,0:T(8,128)(2,1)S(1)} collective-permute-done((s16[528,128]{1,0:T(8,128)(2,1)S(1)}, s16[528,128]{1,0:T(8,128)(2,1)S(1)}, u32[]{:S(2)}, u32[]{:S(2)}) %collective-permute-start.19) | collective-permute-done | bytes 135200 | tf_op jit(solution)/shard_map/ppermute | solution.py:334
  56.4 1.2 %factor_kernel.1 = (f32[128,1,256]{2,1,0:T(1,128)}, f32[128,1,256]{2,1,0:T(1,128)}) custom-call(f32[256,256]{1,0:T(8,128)S(1)} %get-tuple-element.59.inverse_first_ref, f32[256,512]{1,0:T(8,128)S(1)} %get-tuple-element.60.inverse_second_ref, f32[512,128]{1,0:T(8,128)S(1)} %get-tuple-element.61.rows_ref, s16[528,128]{1,0:T(8,128)(2,1)S(1)} %collective-permute-done.19.refs_0_), custom_call_target="tpu_custom_call" | custom-call | bytes 1024 | tf_op jit(solution)/shard_map/factor_kernel/pallas_call | solution.py:319
  (1 shorter events, 0.0 us)
Async XLA Ops:
  1.8 8.7 %collective-permute-start.1 = (bf16[256,384]{1,0:T(8,128)(2,1)S(1)}, bf16[256,384]{1,0:T(8,128)(2,1)S(1)}, u32[]{:S(2)}, u32[]{:S(2)}) collective-permute-start(bf16[256,384]{1,0:T(8,128)(2,1)S(1)} %get-tuple-element.35.refs_1_), channel_id=1, source_target_pairs={{0,1},{1,0},{2,3},{3,2},{4,5},{5,4},{6,7},{7,6},{8,9},{9,8},{10,11... | collective-permute-start | bytes 589832 | tf_op jit(solution)/shard_map/ppermute | solution.py:334
  4.8 7.8 %collective-permute-start.2 = (bf16[256,384]{1,0:T(8,128)(2,1)S(1)}, bf16[256,384]{1,0:T(8,128)(2,1)S(1)}, u32[]{:S(2)}, u32[]{:S(2)}) collective-permute-start(bf16[256,384]{1,0:T(8,128)(2,1)S(1)} %get-tuple-element.34.refs_0_), channel_id=1, source_target_pairs={{0,2},{1,3},{2,0},{3,1},{4,6},{5,7},{6,4},{7,5},{8,10},{9,11},{10,... | collective-permute-start | bytes 589832 | tf_op jit(solution)/shard_map/ppermute | solution.py:334
  6.3 10.7 %collective-permute-start = (bf16[256,384]{1,0:T(8,128)(2,1)S(1)}, bf16[256,384]{1,0:T(8,128)(2,1)S(1)}, u32[]{:S(2)}, u32[]{:S(2)}) collective-permute-start(bf16[256,384]{1,0:T(8,128)(2,1)S(1)} %get-tuple-element.34.refs_0_), channel_id=1, source_target_pairs={{0,1},{1,0},{2,3},{3,2},{4,5},{5,4},{6,7},{7,6},{8,9},{9,8},{10,11... | collective-permute-start | bytes 589832 | tf_op jit(solution)/shard_map/ppermute | solution.py:334
  6.9 10.1 %collective-permute-start.3 = (bf16[256,384]{1,0:T(8,128)(2,1)S(1)}, bf16[256,384]{1,0:T(8,128)(2,1)S(1)}, u32[]{:S(2)}, u32[]{:S(2)}) collective-permute-start(bf16[256,384]{1,0:T(8,128)(2,1)S(1)} %get-tuple-element.35.refs_1_), channel_id=1, source_target_pairs={{0,2},{1,3},{2,0},{3,1},{4,6},{5,7},{6,4},{7,5},{8,10},{9,11},{10,... | collective-permute-start | bytes 589832 | tf_op jit(solution)/shard_map/ppermute | solution.py:334
  12.6 5.7 %collective-permute-start.4 = (bf16[256,384]{1,0:T(8,128)(2,1)S(1)}, bf16[256,384]{1,0:T(8,128)(2,1)S(1)}, u32[]{:S(2)}, u32[]{:S(2)}) collective-permute-start(bf16[256,384]{1,0:T(8,128)(2,1)S(1)} %collective-permute-done.2.refs_4_), channel_id=1, source_target_pairs={{0,1},{1,0},{2,3},{3,2},{4,5},{5,4},{6,7},{7,6},{8,9},{9,8},{10,11... | collective-permute-start | bytes 589832 | tf_op jit(solution)/shard_map/ppermute | solution.py:334
  12.7 6.9 %collective-permute-start.5 = (bf16[256,384]{1,0:T(8,128)(2,1)S(1)}, bf16[256,384]{1,0:T(8,128)(2,1)S(1)}, u32[]{:S(2)}, u32[]{:S(2)}) collective-permute-start(bf16[256,384]{1,0:T(8,128)(2,1)S(1)} %collective-permute-done.1.refs_3_), channel_id=1, source_target_pairs={{0,2},{1,3},{2,0},{3,1},{4,6},{5,7},{6,4},{7,5},{8,10},{9,11},{10,... | collective-permute-start | bytes 589832 | tf_op jit(solution)/shard_map/ppermute | solution.py:334
  19.9 2.0 %collective-permute-start.6 = (f32[264,512]{1,0:T(8,128)S(1)}, f32[264,512]{1,0:T(8,128)S(1)}, u32[]{:S(2)}, u32[]{:S(2)}) collective-permute-start(f32[264,512]{1,0:T(8,128)S(1)} %send_kernel.1), channel_id=1, source_target_pairs={{0,4},{4,0},{8,12},{12,8},{16,20},{20,16},{24,28},{28,24},{1,5},{5... | collective-permute-start | bytes 1622024 | tf_op jit(solution)/shard_map/ppermute | solution.py:334
  20.0 5.6 %copy-start = (bf16[1,1536,1024]{2,1,0:T(8,128)(2,1)S(1)}, bf16[1,1536,1024]{2,1,0:T(8,128)(2,1)}, u32[]{:S(2)}) copy-start(bf16[1,1536,1024]{2,1,0:T(8,128)(2,1)} %param.4) | copy-start | bytes 9437188
  22.1 5.5 %collective-permute-start.7 = (s16[72,512]{1,0:T(8,128)(2,1)S(1)}, s16[72,512]{1,0:T(8,128)(2,1)S(1)}, u32[]{:S(2)}, u32[]{:S(2)}) collective-permute-start(s16[72,512]{1,0:T(8,128)(2,1)S(1)} %get-tuple-element.49), channel_id=1, source_target_pairs={{0,3},{1,2},{2,1},{3,0},{4,7},{5,6},{6,5},{7,4},{8,11},{9,10},{10,... | collective-permute-start | bytes 221192 | tf_op jit(solution)/shard_map/ppermute | solution.py:334
  23.9 5.1 %collective-permute-start.8 = (s16[72,512]{1,0:T(8,128)(2,1)S(1)}, s16[72,512]{1,0:T(8,128)(2,1)S(1)}, u32[]{:S(2)}, u32[]{:S(2)}) collective-permute-start(s16[72,512]{1,0:T(8,128)(2,1)S(1)} %get-tuple-element.50), channel_id=1, source_target_pairs={{0,2},{1,3},{2,0},{3,1},{4,6},{5,7},{6,4},{7,5},{8,10},{9,11},{10,... | collective-permute-start | bytes 221192 | tf_op jit(solution)/shard_map/ppermute | solution.py:334
  24.4 4.7 %collective-permute-start.9 = (s16[72,512]{1,0:T(8,128)(2,1)S(1)}, s16[72,512]{1,0:T(8,128)(2,1)S(1)}, u32[]{:S(2)}, u32[]{:S(2)}) collective-permute-start(s16[72,512]{1,0:T(8,128)(2,1)S(1)} %get-tuple-element.51), channel_id=1, source_target_pairs={{0,1},{1,0},{2,3},{3,2},{4,5},{5,4},{6,7},{7,6},{8,9},{9,8},{10,11... | collective-permute-start | bytes 221192 | tf_op jit(solution)/shard_map/ppermute | solution.py:334
  27.5 6.1 %collective-permute-start.10 = (f32[2048,128]{1,0:T(8,128)S(1)}, f32[2048,128]{1,0:T(8,128)S(1)}, u32[]{:S(2)}, u32[]{:S(2)}) collective-permute-start(f32[2048,128]{1,0:T(8,128)S(1)} %get-tuple-element.53), channel_id=1, source_target_pairs={{0,4},{4,0},{8,12},{12,8},{16,20},{20,16},{24,28},{28,24},{1,5},{5... | collective-permute-start | bytes 3145736 | tf_op jit(solution)/shard_map/ppermute | solution.py:334
  29.1 6.7 %collective-permute-start.13 = (s16[72,512]{1,0:T(8,128)(2,1)S(1)}, s16[72,512]{1,0:T(8,128)(2,1)S(1)}, u32[]{:S(2)}, u32[]{:S(2)}) collective-permute-start(s16[72,512]{1,0:T(8,128)(2,1)S(1)} %sum_kernel.2.refs_0_), channel_id=1, source_target_pairs={{0,24},{4,28},{8,16},{12,20},{16,8},{20,12},{24,0},{28,4},{1,25},{... | collective-permute-start | bytes 221192 | tf_op jit(solution)/shard_map/ppermute | solution.py:334
  32.8 6.5 %collective-permute-start.12 = (s16[72,512]{1,0:T(8,128)(2,1)S(1)}, s16[72,512]{1,0:T(8,128)(2,1)S(1)}, u32[]{:S(2)}, u32[]{:S(2)}) collective-permute-start(s16[72,512]{1,0:T(8,128)(2,1)S(1)} %sum_kernel.2.refs_0_), channel_id=1, source_target_pairs={{0,16},{4,20},{8,24},{12,28},{16,0},{20,4},{24,8},{28,12},{1,17},{... | collective-permute-start | bytes 221192 | tf_op jit(solution)/shard_map/ppermute | solution.py:334
  32.8 6.7 %collective-permute-start.11 = (s16[72,512]{1,0:T(8,128)(2,1)S(1)}, s16[72,512]{1,0:T(8,128)(2,1)S(1)}, u32[]{:S(2)}, u32[]{:S(2)}) collective-permute-start(s16[72,512]{1,0:T(8,128)(2,1)S(1)} %sum_kernel.2.refs_0_), channel_id=1, source_target_pairs={{0,8},{4,12},{8,0},{12,4},{16,24},{20,28},{24,16},{28,20},{1,9},{5... | collective-permute-start | bytes 221192 | tf_op jit(solution)/shard_map/ppermute | solution.py:334
  33.8 10.6 %collective-permute-start.14 = (s16[1056,128]{1,0:T(8,128)(2,1)S(1)}, s16[1056,128]{1,0:T(8,128)(2,1)S(1)}, u32[]{:S(2)}, u32[]{:S(2)}) collective-permute-start(s16[1056,128]{1,0:T(8,128)(2,1)S(1)} %get-tuple-element.54), channel_id=1, source_target_pairs={{0,8},{4,12},{8,0},{12,4},{16,24},{20,28},{24,16},{28,20},{1,9},{5... | collective-permute-start | bytes 811016 | tf_op jit(solution)/shard_map/ppermute | solution.py:334
  39.7 5.9 %collective-permute-start.17 = (s16[72,512]{1,0:T(8,128)(2,1)S(1)}, s16[72,512]{1,0:T(8,128)(2,1)S(1)}, u32[]{:S(2)}, u32[]{:S(2)}) collective-permute-start(s16[72,512]{1,0:T(8,128)(2,1)S(1)} %sum_kernel.3.refs_0_), channel_id=1, source_target_pairs={{0,3},{1,2},{2,1},{3,0},{4,7},{5,6},{6,5},{7,4},{8,11},{9,10},{10,... | collective-permute-start | bytes 221192 | tf_op jit(solution)/shard_map/ppermute | solution.py:334
  41.8 4.5 %collective-permute-start.16 = (s16[72,512]{1,0:T(8,128)(2,1)S(1)}, s16[72,512]{1,0:T(8,128)(2,1)S(1)}, u32[]{:S(2)}, u32[]{:S(2)}) collective-permute-start(s16[72,512]{1,0:T(8,128)(2,1)S(1)} %sum_kernel.3.refs_0_), channel_id=1, source_target_pairs={{0,2},{1,3},{2,0},{3,1},{4,6},{5,7},{6,4},{7,5},{8,10},{9,11},{10,... | collective-permute-start | bytes 221192 | tf_op jit(solution)/shard_map/ppermute | solution.py:334
  42.2 4.4 %collective-permute-start.15 = (s16[72,512]{1,0:T(8,128)(2,1)S(1)}, s16[72,512]{1,0:T(8,128)(2,1)S(1)}, u32[]{:S(2)}, u32[]{:S(2)}) collective-permute-start(s16[72,512]{1,0:T(8,128)(2,1)S(1)} %sum_kernel.3.refs_0_), channel_id=1, source_target_pairs={{0,1},{1,0},{2,3},{3,2},{4,5},{5,4},{6,7},{7,6},{8,9},{9,8},{10,11... | collective-permute-start | bytes 221192 | tf_op jit(solution)/shard_map/ppermute | solution.py:334
  46.5 1.8 %collective-permute-start.18 = (s16[320,512]{1,0:T(8,128)(2,1)S(1)}, s16[320,512]{1,0:T(8,128)(2,1)S(1)}, u32[]{:S(2)}, u32[]{:S(2)}) collective-permute-start(s16[320,512]{1,0:T(8,128)(2,1)S(1)} %join_kernel.1.own_ref), channel_id=1, source_target_pairs={{0,4},{4,0},{8,12},{12,8},{16,20},{20,16},{24,28},{28,24},{1,5},{5... | collective-permute-start | bytes 983048 | tf_op jit(solution)/shard_map/ppermute | solution.py:334
  46.6 9.8 %collective-permute-start.19 = (s16[528,128]{1,0:T(8,128)(2,1)S(1)}, s16[528,128]{1,0:T(8,128)(2,1)S(1)}, u32[]{:S(2)}, u32[]{:S(2)}) collective-permute-start(s16[528,128]{1,0:T(8,128)(2,1)S(1)} %get-tuple-element.57), channel_id=1, source_target_pairs={{0,16},{4,20},{8,24},{12,28},{16,0},{20,4},{24,8},{28,12},{1,17},{... | collective-permute-start | bytes 405512 | tf_op jit(solution)/shard_map/ppermute | solution.py:334

commit v16 on v15

--- a/solution.py
+++ b/solution.py
@@ -300,18 +300,26 @@
 
 
 def factor_kernel(inverse_first_ref, inverse_second_ref, rows_ref, *refs):
-    *got, first_out, second_out = refs
+    *got, first_out, second_out, first_copy, second_copy, done = refs
     panel = rows_ref.shape[0]
     half = panel // 2
     rows = rows_ref[...]
     for ref in got:
         rows = rows + decode(ref, 0, panel, TAIL)[0]
     first, second = rows[:half], rows[half:]
-    first_out[...] = product(inverse_first_ref[...], first).T[:, None, :]
-    second_out[...] = product(inverse_second_ref[...], jnp.concatenate([second, first], axis=0)).T[:, None, :]
-
-
-def call(kernel, out_shape, *args, scratch=(), remain=0, micros=0.0, aliases=None):
+    copies = [
+        pltpu.make_async_copy(first_copy, first_out, done.at[0]),
+        pltpu.make_async_copy(second_copy, second_out, done.at[1]),
+    ]
+    first_copy[...] = product(inverse_first_ref[...], first).T[:, None, :]
+    copies[0].start()
+    second_copy[...] = product(inverse_second_ref[...], jnp.concatenate([second, first], axis=0)).T[:, None, :]
+    copies[1].start()
+    for copy in copies:
+        copy.wait()
+
+
+def call(kernel, out_shape, *args, scratch=(), remain=0, micros=0.0, aliases=None, out_space=pltpu.VMEM):
     hbm = pl.BlockSpec(memory_space=pltpu.HBM)
     vmem = pl.BlockSpec(memory_space=pltpu.VMEM)
     stay = len(args) - remain
@@ -321,7 +329,7 @@
         name=getattr(kernel, "func", kernel).__name__,
         out_shape=out_shape,
         in_specs=[vmem] * (len(args) - remain) + [hbm] * remain,
-        out_specs=jax.tree.map(lambda _: vmem, out_shape),
+        out_specs=jax.tree.map(lambda _: pl.BlockSpec(memory_space=out_space), out_shape),
         scratch_shapes=scratch,
         input_output_aliases=aliases or {},
         compiler_params=pltpu.CompilerParams(vmem_limit_bytes=12 << 20),
@@ -451,9 +459,9 @@
         own_half, other, scratch=[pltpu.VMEM((panel, panel), F32)],
     )
     out = jax.ShapeDtypeStruct((share, 1, half), F32)
+    room = [pltpu.VMEM(out.shape, F32)] * 2 + [pltpu.SemaphoreType.DMA((2,))]
     return call(
-        factor_kernel, (out, out),
-        inverse_first, inverse_second, own, *got,
+        factor_kernel, (out, out), inverse_first, inverse_second, own, *got, scratch=room, out_space=pltpu.HBM
     )
 
 

time: 57.8 us -> 57.8 us (level)
  no operation moved by 1% of the time
where the time goes in v16:
time: 57.8 us; the launch traced here: 57.6 us
  starting transfers between devices  21.8 us (38%)
  Pallas kernels  18.9 us (33%)
  waiting for transfers between devices  16.1 us (28%)
  between operations  0.81 us (1%)
    ppermute x20, starting transfers between devices, swap(): return lax.ppermute(x, axis, [(i, i ^ bit) for i in range(count)])  21.8 us
    pallas_call x16, Pallas kernels, call(): pl.pallas_call(kernel, name=getattr(kernel, 'func', kernel).__name__, out...  18.9 us
    ppermute x20, waiting for transfers between devices, swap(): return lax.ppermute(x, axis, [(i, i ^ bit) for i in range(count)])  16.1 us
  transfers between devices with their start and end apart: 20, of which 15 were waited for; matrix products, arithmetic and copies ran while one was open for 0% of the time, Pallas kernels for 28%

profile of v16, /device:TPU:0, one launch (start us, length us, event | category | flops | bytes accessed | tf_op | source)
XLA Modules:
  0.0 57.6 jit_solution(15300845753015435233)
XLA Ops:
  0.6 1.2 %turn_kernel.1 = (bf16[256,384]{1,0:T(8,128)(2,1)S(1)}, bf16[256,384]{1,0:T(8,128)(2,1)S(1)}) custom-call(bf16[384,512]{1,0:T(8,128)(2,1)} %bitcast.7), custom_call_target="tpu_custom_call" | custom-call | bytes 1024 | tf_op jit(solution)/shard_map/turn_kernel/pallas_call | solution.py:327
  1.8 3.0 %collective-permute-start.1 = (bf16[256,384]{1,0:T(8,128)(2,1)S(1)}, bf16[256,384]{1,0:T(8,128)(2,1)S(1)}, u32[]{:S(2)}, u32[]{:S(2)}) collective-permute-start(bf16[256,384]{1,0:T(8,128)(2,1)S(1)} %get-tuple-element.35.refs_1_), channel_id=1, source_target_pairs={{0,1},{1,0},{2,3},{3,2},{4,5},{5,4},{6,7},{7,6},{8,9},{9,8},{10,11... | collective-permute-start | bytes 589832 | tf_op jit(solution)/shard_map/ppermute | solution.py:342
  4.8 1.5 %collective-permute-start.2 = (bf16[256,384]{1,0:T(8,128)(2,1)S(1)}, bf16[256,384]{1,0:T(8,128)(2,1)S(1)}, u32[]{:S(2)}, u32[]{:S(2)}) collective-permute-start(bf16[256,384]{1,0:T(8,128)(2,1)S(1)} %get-tuple-element.34.refs_0_), channel_id=1, source_target_pairs={{0,2},{1,3},{2,0},{3,1},{4,6},{5,7},{6,4},{7,5},{8,10},{9,11},{10,... | collective-permute-start | bytes 589832 | tf_op jit(solution)/shard_map/ppermute | solution.py:342
  6.3 0.5 collective-permute-start
  6.9 0.1 collective-permute-start.3
  6.9 2.6 %pick_kernel.1 = (bf16[1536,512]{1,0:T(8,128)(2,1)S(1)}, f32[8,512]{1,0:T(8,128)S(1)}, bf16[1024,512]{1,0:T(8,128)(2,1)S(1)}, s32[1,512]{1,0:T(1,128)S(1)}, f32[1,128]{1,0:T(1,128)S(1)}) custom-call(s32[1,512]{1,0:T(1,128)} %bitcast.8, f32[1,128]{1,0:T(1,128)} %bitcast.9, bf16[1536,1024]{1,0:T(8,128)(2,1)} %bitcast.4), custom_call_target="tpu_custom_call" | custom-call | bytes 1024 | tf_op jit(solution)/shard_map/pick_kernel/pallas_call | solution.py:327
  9.6 1.0 %collective-permute-done.1.refs_3_ = bf16[256,384]{1,0:T(8,128)(2,1)S(1)} collective-permute-done((bf16[256,384]{1,0:T(8,128)(2,1)S(1)}, bf16[256,384]{1,0:T(8,128)(2,1)S(1)}, u32[]{:S(2)}, u32[]{:S(2)}) %collective-permute-start.1) | collective-permute-done | bytes 196640 | tf_op jit(solution)/shard_map/ppermute | solution.py:342
  10.5 2.1 %collective-permute-done.2.refs_4_ = bf16[256,384]{1,0:T(8,128)(2,1)S(1)} collective-permute-done((bf16[256,384]{1,0:T(8,128)(2,1)S(1)}, bf16[256,384]{1,0:T(8,128)(2,1)S(1)}, u32[]{:S(2)}, u32[]{:S(2)}) %collective-permute-start.2) | collective-permute-done | bytes 196640 | tf_op jit(solution)/shard_map/ppermute | solution.py:342
  12.6 0.0 collective-permute-start.4
  12.7 2.0 %collective-permute-start.5 = (bf16[256,384]{1,0:T(8,128)(2,1)S(1)}, bf16[256,384]{1,0:T(8,128)(2,1)S(1)}, u32[]{:S(2)}, u32[]{:S(2)}) collective-permute-start(bf16[256,384]{1,0:T(8,128)(2,1)S(1)} %collective-permute-done.1.refs_3_), channel_id=1, source_target_pairs={{0,2},{1,3},{2,0},{3,1},{4,6},{5,7},{6,4},{7,5},{8,10},{9,11},{10,... | collective-permute-start | bytes 589832 | tf_op jit(solution)/shard_map/ppermute | solution.py:342
  14.7 2.3 %rest_kernel.1.chosen_ref = bf16[1536,512]{1,0:T(8,128)(2,1)S(1)} custom-call(bf16[1536,512]{1,0:T(8,128)(2,1)S(1)} %get-tuple-element.32.chosen_in, bf16[1024,512]{1,0:T(8,128)(2,1)S(1)} %get-tuple-element.33.one_ref, bf16[1536,1024]{1,0:T(8,128)(2,1)} %bitcast.5), custom_call_target="tpu_custom_call", output_to_operand_aliasing={{}: (0, {})} | custom-call | bytes 1024 | tf_op jit(solution)/shard_map/rest_kernel/pallas_call | solution.py:327
  17.0 0.0 collective-permute-done.refs_2_
  17.0 0.0 collective-permute-done.3.refs_5_
  17.0 1.1 %early_kernel.1 = (bf16[512,1536]{1,0:T(8,128)(2,1)S(1)}, f32[512,512]{1,0:T(8,128)S(1)}) custom-call(bf16[1536,512]{1,0:T(8,128)(2,1)S(1)} %rest_kernel.1.chosen_ref, bf16[256,384]{1,0:T(8,128)(2,1)S(1)} %get-tuple-element.34.refs_0_, bf16[256,384]{1,0:T(8,128)(2,1)S(1)} %get-tuple-element.35.refs_1_, bf16[256,384]{1,0:T(8,128)(2,1)S(1)} %collective-permute-done.refs_2_, ...), custom_call_target="tpu_custom_call" | custom-call | bytes 1024 | tf_op jit(solution)/shard_map/early_kernel/pallas_call | solution.py:327
  18.1 0.2 collective-permute-done.4.refs_0_
  18.3 1.3 %collective-permute-done.5.refs_1_ = bf16[256,384]{1,0:T(8,128)(2,1)S(1)} collective-permute-done((bf16[256,384]{1,0:T(8,128)(2,1)S(1)}, bf16[256,384]{1,0:T(8,128)(2,1)S(1)}, u32[]{:S(2)}, u32[]{:S(2)}) %collective-permute-start.5) | collective-permute-done | bytes 196640 | tf_op jit(solution)/shard_map/ppermute | solution.py:342
  19.6 0.3 send_kernel.1
  19.9 0.1 collective-permute-start.6
  20.0 0.0 copy-start
  20.0 0.4 keep_kernel.1
  20.4 1.5 %collective-permute-done.6.got_ref = f32[264,512]{1,0:T(8,128)S(1)} collective-permute-done((f32[264,512]{1,0:T(8,128)S(1)}, f32[264,512]{1,0:T(8,128)S(1)}, u32[]{:S(2)}, u32[]{:S(2)}) %collective-permute-start.6) | collective-permute-done | bytes 540704 | tf_op jit(solution)/shard_map/ppermute | solution.py:342
  21.9 0.2 pair_kernel.1
  22.1 1.8 %collective-permute-start.7 = (s16[72,512]{1,0:T(8,128)(2,1)S(1)}, s16[72,512]{1,0:T(8,128)(2,1)S(1)}, u32[]{:S(2)}, u32[]{:S(2)}) collective-permute-start(s16[72,512]{1,0:T(8,128)(2,1)S(1)} %get-tuple-element.49), channel_id=1, source_target_pairs={{0,3},{1,2},{2,1},{3,0},{4,7},{5,6},{6,5},{7,4},{8,11},{9,10},{10,... | collective-permute-start | bytes 221192 | tf_op jit(solution)/shard_map/ppermute | solution.py:342
  23.9 0.5 collective-permute-start.8
  24.4 1.3 %collective-permute-start.9 = (s16[72,512]{1,0:T(8,128)(2,1)S(1)}, s16[72,512]{1,0:T(8,128)(2,1)S(1)}, u32[]{:S(2)}, u32[]{:S(2)}) collective-permute-start(s16[72,512]{1,0:T(8,128)(2,1)S(1)} %get-tuple-element.51), channel_id=1, source_target_pairs={{0,1},{1,0},{2,3},{3,2},{4,5},{5,4},{6,7},{7,6},{8,9},{9,8},{10,11... | collective-permute-start | bytes 221192 | tf_op jit(solution)/shard_map/ppermute | solution.py:342
  25.6 0.0 copy-done
  25.7 1.8 %schur_kernel.1 = (f32[2048,128]{1,0:T(8,128)S(1)}, f32[2048,128]{1,0:T(8,128)S(1)}) custom-call(s32[1,512]{1,0:T(1,128)S(1)} %get-tuple-element.43.panel_ref, f32[1,128]{1,0:T(1,128)S(1)} %get-tuple-element.44.own_diagonal_ref, bf16[1536,1024]{1,0:T(8,128)(2,1)S(1)} %bitcast.6, bf16[512,1536]{1,0:T(8,128)(2,1)S(1)} %get-tuple-element.46.turned_ref), custom_call_target="tpu_custom_call" | custom-call | flops 2300000000 | bytes 1024 | tf_op jit(solution)/shard_map/schur_kernel/pallas_call | solution.py:327
  27.5 0.1 collective-permute-start.10
  27.5 0.0 collective-permute-done.7.refs_1_
  27.6 1.4 %collective-permute-done.8.refs_2_ = s16[72,512]{1,0:T(8,128)(2,1)S(1)} collective-permute-done((s16[72,512]{1,0:T(8,128)(2,1)S(1)}, s16[72,512]{1,0:T(8,128)(2,1)S(1)}, u32[]{:S(2)}, u32[]{:S(2)}) %collective-permute-start.8) | collective-permute-done | bytes 73760 | tf_op jit(solution)/shard_map/ppermute | solution.py:342
  28.9 0.1 collective-permute-done.9.refs_3_
  29.0 0.1 sum_kernel.2.refs_0_
  29.1 3.7 %collective-permute-start.13 = (s16[72,512]{1,0:T(8,128)(2,1)S(1)}, s16[72,512]{1,0:T(8,128)(2,1)S(1)}, u32[]{:S(2)}, u32[]{:S(2)}) collective-permute-start(s16[72,512]{1,0:T(8,128)(2,1)S(1)} %sum_kernel.2.refs_0_), channel_id=1, source_target_pairs={{0,24},{4,28},{8,16},{12,20},{16,8},{20,12},{24,0},{28,4},{1,25},{... | collective-permute-start | bytes 221192 | tf_op jit(solution)/shard_map/ppermute | solution.py:342
  32.8 0.0 collective-permute-start.12
  32.8 0.8 %collective-permute-start.11 = (s16[72,512]{1,0:T(8,128)(2,1)S(1)}, s16[72,512]{1,0:T(8,128)(2,1)S(1)}, u32[]{:S(2)}, u32[]{:S(2)}) collective-permute-start(s16[72,512]{1,0:T(8,128)(2,1)S(1)} %sum_kernel.2.refs_0_), channel_id=1, source_target_pairs={{0,8},{4,12},{8,0},{12,4},{16,24},{20,28},{24,16},{28,20},{1,9},{5... | collective-permute-start | bytes 221192 | tf_op jit(solution)/shard_map/ppermute | solution.py:342
  33.6 0.0 collective-permute-done.10.got_ref
  33.6 0.2 bulk_pair_kernel.1
  33.8 1.3 %collective-permute-start.14 = (s16[1056,128]{1,0:T(8,128)(2,1)S(1)}, s16[1056,128]{1,0:T(8,128)(2,1)S(1)}, u32[]{:S(2)}, u32[]{:S(2)}) collective-permute-start(s16[1056,128]{1,0:T(8,128)(2,1)S(1)} %get-tuple-element.54), channel_id=1, source_target_pairs={{0,8},{4,12},{8,0},{12,4},{16,24},{20,28},{24,16},{28,20},{1,9},{5... | collective-permute-start | bytes 811016 | tf_op jit(solution)/shard_map/ppermute | solution.py:342
  35.1 0.8 %collective-permute-done.13.refs_3_ = s16[72,512]{1,0:T(8,128)(2,1)S(1)} collective-permute-done((s16[72,512]{1,0:T(8,128)(2,1)S(1)}, s16[72,512]{1,0:T(8,128)(2,1)S(1)}, u32[]{:S(2)}, u32[]{:S(2)}) %collective-permute-start.13) | collective-permute-done | bytes 73760 | tf_op jit(solution)/shard_map/ppermute | solution.py:342
  35.9 3.4 %collective-permute-done.12.refs_2_ = s16[72,512]{1,0:T(8,128)(2,1)S(1)} collective-permute-done((s16[72,512]{1,0:T(8,128)(2,1)S(1)}, s16[72,512]{1,0:T(8,128)(2,1)S(1)}, u32[]{:S(2)}, u32[]{:S(2)}) %collective-permute-start.12) | collective-permute-done | bytes 73760 | tf_op jit(solution)/shard_map/ppermute | solution.py:342
  39.3 0.3 collective-permute-done.11.refs_1_
  39.5 0.1 sum_kernel.3.refs_0_
  39.7 2.1 %collective-permute-start.17 = (s16[72,512]{1,0:T(8,128)(2,1)S(1)}, s16[72,512]{1,0:T(8,128)(2,1)S(1)}, u32[]{:S(2)}, u32[]{:S(2)}) collective-permute-start(s16[72,512]{1,0:T(8,128)(2,1)S(1)} %sum_kernel.3.refs_0_), channel_id=1, source_target_pairs={{0,3},{1,2},{2,1},{3,0},{4,7},{5,6},{6,5},{7,4},{8,11},{9,10},{10,... | collective-permute-start | bytes 221192 | tf_op jit(solution)/shard_map/ppermute | solution.py:342
  41.8 0.4 collective-permute-start.16
  42.2 1.1 %collective-permute-start.15 = (s16[72,512]{1,0:T(8,128)(2,1)S(1)}, s16[72,512]{1,0:T(8,128)(2,1)S(1)}, u32[]{:S(2)}, u32[]{:S(2)}) collective-permute-start(s16[72,512]{1,0:T(8,128)(2,1)S(1)} %sum_kernel.3.refs_0_), channel_id=1, source_target_pairs={{0,1},{1,0},{2,3},{3,2},{4,5},{5,4},{6,7},{7,6},{8,9},{9,8},{10,11... | collective-permute-start | bytes 221192 | tf_op jit(solution)/shard_map/ppermute | solution.py:342
  43.2 1.2 %collective-permute-done.14.got_ref = s16[1056,128]{1,0:T(8,128)(2,1)S(1)} collective-permute-done((s16[1056,128]{1,0:T(8,128)(2,1)S(1)}, s16[1056,128]{1,0:T(8,128)(2,1)S(1)}, u32[]{:S(2)}, u32[]{:S(2)}) %collective-permute-start.14) | collective-permute-done | bytes 270368 | tf_op jit(solution)/shard_map/ppermute | solution.py:342
  44.4 0.2 bulk_sum_kernel.1
  44.6 0.9 %collective-permute-done.17.refs_3_ = s16[72,512]{1,0:T(8,128)(2,1)S(1)} collective-permute-done((s16[72,512]{1,0:T(8,128)(2,1)S(1)}, s16[72,512]{1,0:T(8,128)(2,1)S(1)}, u32[]{:S(2)}, u32[]{:S(2)}) %collective-permute-start.17) | collective-permute-done | bytes 73760 | tf_op jit(solution)/shard_map/ppermute | solution.py:342
  45.5 0.7 %collective-permute-done.16.refs_2_ = s16[72,512]{1,0:T(8,128)(2,1)S(1)} collective-permute-done((s16[72,512]{1,0:T(8,128)(2,1)S(1)}, s16[72,512]{1,0:T(8,128)(2,1)S(1)}, u32[]{:S(2)}, u32[]{:S(2)}) %collective-permute-start.16) | collective-permute-done | bytes 73760 | tf_op jit(solution)/shard_map/ppermute | solution.py:342
  46.2 0.3 collective-permute-done.15.refs_1_
  46.5 0.1 collective-permute-start.18
  46.6 1.5 %collective-permute-start.19 = (s16[528,128]{1,0:T(8,128)(2,1)S(1)}, s16[528,128]{1,0:T(8,128)(2,1)S(1)}, u32[]{:S(2)}, u32[]{:S(2)}) collective-permute-start(s16[528,128]{1,0:T(8,128)(2,1)S(1)} %get-tuple-element.57), channel_id=1, source_target_pairs={{0,16},{4,20},{8,24},{12,28},{16,0},{20,4},{24,8},{28,12},{1,17},{... | collective-permute-start | bytes 405512 | tf_op jit(solution)/shard_map/ppermute | solution.py:342
  48.1 0.2 own_kernel.1.half_ref
  48.3 0.0 collective-permute-done.18.other_ref
  48.3 7.0 %newton_kernel.1 = (f32[256,256]{1,0:T(8,128)S(1)}, f32[256,512]{1,0:T(8,128)S(1)}) custom-call(f32[256,512]{1,0:T(8,128)S(1)} %own_kernel.1.half_ref, s16[320,512]{1,0:T(8,128)(2,1)S(1)} %collective-permute-done.18.other_ref), custom_call_target="tpu_custom_call" | custom-call | bytes 1024 | tf_op jit(solution)/shard_map/newton_kernel/pallas_call | solution.py:327
  55.3 1.1 %collective-permute-done.19.refs_0_ = s16[528,128]{1,0:T(8,128)(2,1)S(1)} collective-permute-done((s16[528,128]{1,0:T(8,128)(2,1)S(1)}, s16[528,128]{1,0:T(8,128)(2,1)S(1)}, u32[]{:S(2)}, u32[]{:S(2)}) %collective-permute-start.19) | collective-permute-done | bytes 135200 | tf_op jit(solution)/shard_map/ppermute | solution.py:342
  56.4 1.2 %factor_kernel.1 = (f32[128,1,256]{2,1,0:T(1,128)}, f32[128,1,256]{2,1,0:T(1,128)}) custom-call(f32[256,256]{1,0:T(8,128)S(1)} %get-tuple-element.59.inverse_first_ref, f32[256,512]{1,0:T(8,128)S(1)} %get-tuple-element.60.inverse_second_ref, f32[512,128]{1,0:T(8,128)S(1)} %get-tuple-element.61.rows_ref, s16[528,128]{1,0:T(8,128)(2,1)S(1)} %collective-permute-done.19.refs_0_), custom_call_target="tpu_custom_call" | custom-call | bytes 1024 | tf_op jit(solution)/shard_map/factor_kernel/pallas_call | solution.py:327
  (1 shorter events, 0.0 us)
Async XLA Ops:
  1.8 8.7 %collective-permute-start.1 = (bf16[256,384]{1,0:T(8,128)(2,1)S(1)}, bf16[256,384]{1,0:T(8,128)(2,1)S(1)}, u32[]{:S(2)}, u32[]{:S(2)}) collective-permute-start(bf16[256,384]{1,0:T(8,128)(2,1)S(1)} %get-tuple-element.35.refs_1_), channel_id=1, source_target_pairs={{0,1},{1,0},{2,3},{3,2},{4,5},{5,4},{6,7},{7,6},{8,9},{9,8},{10,11... | collective-permute-start | bytes 589832 | tf_op jit(solution)/shard_map/ppermute | solution.py:342
  4.8 7.8 %collective-permute-start.2 = (bf16[256,384]{1,0:T(8,128)(2,1)S(1)}, bf16[256,384]{1,0:T(8,128)(2,1)S(1)}, u32[]{:S(2)}, u32[]{:S(2)}) collective-permute-start(bf16[256,384]{1,0:T(8,128)(2,1)S(1)} %get-tuple-element.34.refs_0_), channel_id=1, source_target_pairs={{0,2},{1,3},{2,0},{3,1},{4,6},{5,7},{6,4},{7,5},{8,10},{9,11},{10,... | collective-permute-start | bytes 589832 | tf_op jit(solution)/shard_map/ppermute | solution.py:342
  6.3 10.7 %collective-permute-start = (bf16[256,384]{1,0:T(8,128)(2,1)S(1)}, bf16[256,384]{1,0:T(8,128)(2,1)S(1)}, u32[]{:S(2)}, u32[]{:S(2)}) collective-permute-start(bf16[256,384]{1,0:T(8,128)(2,1)S(1)} %get-tuple-element.34.refs_0_), channel_id=1, source_target_pairs={{0,1},{1,0},{2,3},{3,2},{4,5},{5,4},{6,7},{7,6},{8,9},{9,8},{10,11... | collective-permute-start | bytes 589832 | tf_op jit(solution)/shard_map/ppermute | solution.py:342
  6.9 10.1 %collective-permute-start.3 = (bf16[256,384]{1,0:T(8,128)(2,1)S(1)}, bf16[256,384]{1,0:T(8,128)(2,1)S(1)}, u32[]{:S(2)}, u32[]{:S(2)}) collective-permute-start(bf16[256,384]{1,0:T(8,128)(2,1)S(1)} %get-tuple-element.35.refs_1_), channel_id=1, source_target_pairs={{0,2},{1,3},{2,0},{3,1},{4,6},{5,7},{6,4},{7,5},{8,10},{9,11},{10,... | collective-permute-start | bytes 589832 | tf_op jit(solution)/shard_map/ppermute | solution.py:342
  12.6 5.7 %collective-permute-start.4 = (bf16[256,384]{1,0:T(8,128)(2,1)S(1)}, bf16[256,384]{1,0:T(8,128)(2,1)S(1)}, u32[]{:S(2)}, u32[]{:S(2)}) collective-permute-start(bf16[256,384]{1,0:T(8,128)(2,1)S(1)} %collective-permute-done.2.refs_4_), channel_id=1, source_target_pairs={{0,1},{1,0},{2,3},{3,2},{4,5},{5,4},{6,7},{7,6},{8,9},{9,8},{10,11... | collective-permute-start | bytes 589832 | tf_op jit(solution)/shard_map/ppermute | solution.py:342
  12.7 6.9 %collective-permute-start.5 = (bf16[256,384]{1,0:T(8,128)(2,1)S(1)}, bf16[256,384]{1,0:T(8,128)(2,1)S(1)}, u32[]{:S(2)}, u32[]{:S(2)}) collective-permute-start(bf16[256,384]{1,0:T(8,128)(2,1)S(1)} %collective-permute-done.1.refs_3_), channel_id=1, source_target_pairs={{0,2},{1,3},{2,0},{3,1},{4,6},{5,7},{6,4},{7,5},{8,10},{9,11},{10,... | collective-permute-start | bytes 589832 | tf_op jit(solution)/shard_map/ppermute | solution.py:342
  19.9 2.0 %collective-permute-start.6 = (f32[264,512]{1,0:T(8,128)S(1)}, f32[264,512]{1,0:T(8,128)S(1)}, u32[]{:S(2)}, u32[]{:S(2)}) collective-permute-start(f32[264,512]{1,0:T(8,128)S(1)} %send_kernel.1), channel_id=1, source_target_pairs={{0,4},{4,0},{8,12},{12,8},{16,20},{20,16},{24,28},{28,24},{1,5},{5... | collective-permute-start | bytes 1622024 | tf_op jit(solution)/shard_map/ppermute | solution.py:342
  20.0 5.6 %copy-start = (bf16[1,1536,1024]{2,1,0:T(8,128)(2,1)S(1)}, bf16[1,1536,1024]{2,1,0:T(8,128)(2,1)}, u32[]{:S(2)}) copy-start(bf16[1,1536,1024]{2,1,0:T(8,128)(2,1)} %param.4) | copy-start | bytes 9437188
  22.1 5.5 %collective-permute-start.7 = (s16[72,512]{1,0:T(8,128)(2,1)S(1)}, s16[72,512]{1,0:T(8,128)(2,1)S(1)}, u32[]{:S(2)}, u32[]{:S(2)}) collective-permute-start(s16[72,512]{1,0:T(8,128)(2,1)S(1)} %get-tuple-element.49), channel_id=1, source_target_pairs={{0,3},{1,2},{2,1},{3,0},{4,7},{5,6},{6,5},{7,4},{8,11},{9,10},{10,... | collective-permute-start | bytes 221192 | tf_op jit(solution)/shard_map/ppermute | solution.py:342
  23.9 5.1 %collective-permute-start.8 = (s16[72,512]{1,0:T(8,128)(2,1)S(1)}, s16[72,512]{1,0:T(8,128)(2,1)S(1)}, u32[]{:S(2)}, u32[]{:S(2)}) collective-permute-start(s16[72,512]{1,0:T(8,128)(2,1)S(1)} %get-tuple-element.50), channel_id=1, source_target_pairs={{0,2},{1,3},{2,0},{3,1},{4,6},{5,7},{6,4},{7,5},{8,10},{9,11},{10,... | collective-permute-start | bytes 221192 | tf_op jit(solution)/shard_map/ppermute | solution.py:342
  24.4 4.7 %collective-permute-start.9 = (s16[72,512]{1,0:T(8,128)(2,1)S(1)}, s16[72,512]{1,0:T(8,128)(2,1)S(1)}, u32[]{:S(2)}, u32[]{:S(2)}) collective-permute-start(s16[72,512]{1,0:T(8,128)(2,1)S(1)} %get-tuple-element.51), channel_id=1, source_target_pairs={{0,1},{1,0},{2,3},{3,2},{4,5},{5,4},{6,7},{7,6},{8,9},{9,8},{10,11... | collective-permute-start | bytes 221192 | tf_op jit(solution)/shard_map/ppermute | solution.py:342
  27.5 6.1 %collective-permute-start.10 = (f32[2048,128]{1,0:T(8,128)S(1)}, f32[2048,128]{1,0:T(8,128)S(1)}, u32[]{:S(2)}, u32[]{:S(2)}) collective-permute-start(f32[2048,128]{1,0:T(8,128)S(1)} %get-tuple-element.53), channel_id=1, source_target_pairs={{0,4},{4,0},{8,12},{12,8},{16,20},{20,16},{24,28},{28,24},{1,5},{5... | collective-permute-start | bytes 3145736 | tf_op jit(solution)/shard_map/ppermute | solution.py:342
  29.1 6.7 %collective-permute-start.13 = (s16[72,512]{1,0:T(8,128)(2,1)S(1)}, s16[72,512]{1,0:T(8,128)(2,1)S(1)}, u32[]{:S(2)}, u32[]{:S(2)}) collective-permute-start(s16[72,512]{1,0:T(8,128)(2,1)S(1)} %sum_kernel.2.refs_0_), channel_id=1, source_target_pairs={{0,24},{4,28},{8,16},{12,20},{16,8},{20,12},{24,0},{28,4},{1,25},{... | collective-permute-start | bytes 221192 | tf_op jit(solution)/shard_map/ppermute | solution.py:342
  32.8 6.5 %collective-permute-start.12 = (s16[72,512]{1,0:T(8,128)(2,1)S(1)}, s16[72,512]{1,0:T(8,128)(2,1)S(1)}, u32[]{:S(2)}, u32[]{:S(2)}) collective-permute-start(s16[72,512]{1,0:T(8,128)(2,1)S(1)} %sum_kernel.2.refs_0_), channel_id=1, source_target_pairs={{0,16},{4,20},{8,24},{12,28},{16,0},{20,4},{24,8},{28,12},{1,17},{... | collective-permute-start | bytes 221192 | tf_op jit(solution)/shard_map/ppermute | solution.py:342
  32.8 6.7 %collective-permute-start.11 = (s16[72,512]{1,0:T(8,128)(2,1)S(1)}, s16[72,512]{1,0:T(8,128)(2,1)S(1)}, u32[]{:S(2)}, u32[]{:S(2)}) collective-permute-start(s16[72,512]{1,0:T(8,128)(2,1)S(1)} %sum_kernel.2.refs_0_), channel_id=1, source_target_pairs={{0,8},{4,12},{8,0},{12,4},{16,24},{20,28},{24,16},{28,20},{1,9},{5... | collective-permute-start | bytes 221192 | tf_op jit(solution)/shard_map/ppermute | solution.py:342
  33.8 10.6 %collective-permute-start.14 = (s16[1056,128]{1,0:T(8,128)(2,1)S(1)}, s16[1056,128]{1,0:T(8,128)(2,1)S(1)}, u32[]{:S(2)}, u32[]{:S(2)}) collective-permute-start(s16[1056,128]{1,0:T(8,128)(2,1)S(1)} %get-tuple-element.54), channel_id=1, source_target_pairs={{0,8},{4,12},{8,0},{12,4},{16,24},{20,28},{24,16},{28,20},{1,9},{5... | collective-permute-start | bytes 811016 | tf_op jit(solution)/shard_map/ppermute | solution.py:342
  39.7 5.9 %collective-permute-start.17 = (s16[72,512]{1,0:T(8,128)(2,1)S(1)}, s16[72,512]{1,0:T(8,128)(2,1)S(1)}, u32[]{:S(2)}, u32[]{:S(2)}) collective-permute-start(s16[72,512]{1,0:T(8,128)(2,1)S(1)} %sum_kernel.3.refs_0_), channel_id=1, source_target_pairs={{0,3},{1,2},{2,1},{3,0},{4,7},{5,6},{6,5},{7,4},{8,11},{9,10},{10,... | collective-permute-start | bytes 221192 | tf_op jit(solution)/shard_map/ppermute | solution.py:342
  41.8 4.5 %collective-permute-start.16 = (s16[72,512]{1,0:T(8,128)(2,1)S(1)}, s16[72,512]{1,0:T(8,128)(2,1)S(1)}, u32[]{:S(2)}, u32[]{:S(2)}) collective-permute-start(s16[72,512]{1,0:T(8,128)(2,1)S(1)} %sum_kernel.3.refs_0_), channel_id=1, source_target_pairs={{0,2},{1,3},{2,0},{3,1},{4,6},{5,7},{6,4},{7,5},{8,10},{9,11},{10,... | collective-permute-start | bytes 221192 | tf_op jit(solution)/shard_map/ppermute | solution.py:342
  42.2 4.4 %collective-permute-start.15 = (s16[72,512]{1,0:T(8,128)(2,1)S(1)}, s16[72,512]{1,0:T(8,128)(2,1)S(1)}, u32[]{:S(2)}, u32[]{:S(2)}) collective-permute-start(s16[72,512]{1,0:T(8,128)(2,1)S(1)} %sum_kernel.3.refs_0_), channel_id=1, source_target_pairs={{0,1},{1,0},{2,3},{3,2},{4,5},{5,4},{6,7},{7,6},{8,9},{9,8},{10,11... | collective-permute-start | bytes 221192 | tf_op jit(solution)/shard_map/ppermute | solution.py:342
  46.5 1.8 %collective-permute-start.18 = (s16[320,512]{1,0:T(8,128)(2,1)S(1)}, s16[320,512]{1,0:T(8,128)(2,1)S(1)}, u32[]{:S(2)}, u32[]{:S(2)}) collective-permute-start(s16[320,512]{1,0:T(8,128)(2,1)S(1)} %join_kernel.1.own_ref), channel_id=1, source_target_pairs={{0,4},{4,0},{8,12},{12,8},{16,20},{20,16},{24,28},{28,24},{1,5},{5... | collective-permute-start | bytes 983048 | tf_op jit(solution)/shard_map/ppermute | solution.py:342
  46.6 9.8 %collective-permute-start.19 = (s16[528,128]{1,0:T(8,128)(2,1)S(1)}, s16[528,128]{1,0:T(8,128)(2,1)S(1)}, u32[]{:S(2)}, u32[]{:S(2)}) collective-permute-start(s16[528,128]{1,0:T(8,128)(2,1)S(1)} %get-tuple-element.57), channel_id=1, source_target_pairs={{0,16},{4,20},{8,24},{12,28},{16,0},{20,4},{24,8},{28,12},{1,17},{... | collective-permute-start | bytes 405512 | tf_op jit(solution)/shard_map/ppermute | solution.py:342

commit v17 on v15

--- a/solution.py
+++ b/solution.py
@@ -113,27 +113,25 @@
         out_ref[...] = solves_copy[i].T
 
 
-def fetch(source_ref, target_ref, done, first):
-    rows = target_ref.shape[1]
+def order_of(rows):
+    row = lax.axis_index("row")
+    return [row ^ 3, row, row ^ 1, row ^ 2] if rows == 4 else list(range(CHUNKS))
+
+
+def fetch(source_ref, target_ref, done, blocks):
+    size = target_ref.shape[1]
     copies = [
-        pltpu.make_async_copy(source_ref.at[pl.ds((first + i) * rows, rows), :], target_ref.at[i], done.at[i])
-        for i in range(target_ref.shape[0])
+        pltpu.make_async_copy(source_ref.at[pl.ds(aligned(block, size), size), :], target_ref.at[i], done.at[i])
+        for i, block in enumerate(blocks)
     ]
     for copy in copies:
         copy.start()
     return copies
 
 
-def choose(copies, coupling_copy, one_ref, chosen_ref, first):
-    rows = coupling_copy.shape[1]
-    for i, copy in enumerate(copies):
-        copy.wait()
-        chosen_ref[(first + i) * rows:(first + i + 1) * rows, :] = dot(coupling_copy[i], one_ref[...]).astype(BF16)
-
-
 def pick_kernel(
-    panel_ref, own_diagonal_ref, coupling_ref,
-    chosen_ref, entry_ref, one_ref, panel_out, diagonal_out, coupling_copy, small_done, done,
+    rows, panel_ref, own_diagonal_ref, coupling_ref,
+    chosen_ref, far_ref, entry_ref, one_ref, panel_out, diagonal_out, coupling_copy, small_done, done,
 ):
     small = [
         pltpu.make_async_copy(panel_ref, panel_out, small_done.at[0]),
@@ -141,7 +139,8 @@
     ]
     for copy in small:
         copy.start()
-    copies = fetch(coupling_ref, coupling_copy, done, 0)
+    block = order_of(rows)[0]
+    copies = fetch(coupling_ref, coupling_copy, done, [block])
     for copy in small:
         copy.wait()
     columns, panel = one_ref.shape
@@ -154,18 +153,23 @@
     own = jnp.broadcast_to(diagonal_out[...], (8, share)).T[:, :1]
     entry = jnp.sum(jnp.where(owned, own, F32(0.0)), axis=0, keepdims=True)
     entry_ref[...] = jnp.broadcast_to(entry, entry_ref.shape)
-    choose(copies, coupling_copy, one_ref, chosen_ref, 0)
-
-
-def rest_kernel(chosen_in, one_ref, coupling_ref, chosen_ref, coupling_copy, done):
-    first = coupling_copy.shape[0]
-    copies = fetch(coupling_ref, coupling_copy, done, first)
-    choose(copies, coupling_copy, one_ref, chosen_ref, first)
-
-
-def early_kernel(chosen_ref, *refs):
-    *pieces, turned_ref, terms_ref = refs
-    row, _, _ = whereabouts()
+    copies[0].wait()
+    size = far_ref.shape[0]
+    far_ref[...] = dot(coupling_copy[0], one_ref[...]).astype(BF16)
+    chosen_ref[pl.ds(aligned(block, size), size), :] = far_ref[...]
+
+
+def rest_kernel(rows, chosen_in, one_ref, coupling_ref, chosen_ref, coupling_copy, done):
+    blocks = order_of(rows)[1:]
+    size = coupling_copy.shape[1]
+    for i, copy in enumerate(fetch(coupling_ref, coupling_copy, done, blocks)):
+        copy.wait()
+        chosen_ref[pl.ds(aligned(blocks[i], size), size), :] = dot(coupling_copy[i], one_ref[...]).astype(BF16)
+
+
+def early_kernel(rows, chosen_ref, entry_ref, *refs):
+    *pieces, turned_ref, own_ref, send_ref, terms_ref = refs
+    row, core, _ = whereabouts()
     if len(pieces) == 1:
         turned_ref[...] = pieces[0][...]
     else:
@@ -176,44 +180,50 @@
         start = aligned(row ^ (len(pieces) // 2), width)
         turned_ref[:, pl.ds(start, width)] = jnp.zeros((2 * half, width), BF16)
     terms_ref[...] = dot(turned_ref[...], chosen_ref[...])
-
-
-def half_terms(rows, row, chosen_ref, terms_ref, far, whose, out_ref, all_ref):
-    half = all_ref.shape[0]
+    size = own_ref.shape[0] // rows
+    for out_ref, whose in ((own_ref, core), (send_ref, 1 - core)):
+        for k in range(rows):
+            out_ref[k * size:(k + 1) * size, :] = terms_ref[pl.ds(aligned(whose * rows + (row ^ k), size), size), :]
+    send_ref[rows * size:, :] = entry_ref[...]
+
+
+def select_kernel(upper_ref, lower_ref, out_ref):
+    out_ref[...] = jnp.where(whereabouts()[1] == 0, lower_ref[...], upper_ref[...])
+
+
+def add_far(rows, block, chosen, far_ref):
+    row = lax.axis_index("row")
+    size = far_ref.shape[0] // rows
+    far_ref[...] = dot(block, chosen)
+    return [far_ref[pl.ds(aligned(row ^ k, size), size), :] for k in range(rows)]
+
+
+def keep_kernel(rows, turned_in, own_ref, got_ref, entry_ref, *refs):
+    *far, turned_ref, keep_ref, both_ref, far_ref = refs
+    row, core, _ = whereabouts()
+    half = keep_ref.shape[0]
     size = half // rows
-    total = terms_ref[pl.ds(aligned(whose, half), half), :]
+    both_ref[...] = jnp.broadcast_to(entry_ref[:1, :] + got_ref[half:half + 1, :], both_ref.shape)
+    keep_ref[...] = own_ref[...] + got_ref[:half, :]
     if far:
-        width = far[0].shape[1]
-        block = jnp.where(whose == 0, far[0][...], far[1][...])
-        total = total + dot(block, chosen_ref[pl.ds(aligned(row ^ (rows - 1), width), width), :])
-    all_ref[...] = total
-    for k in range(rows):
-        out_ref[k * size:(k + 1) * size, :] = all_ref[pl.ds(aligned(row ^ k, size), size), :]
-
-
-def send_kernel(rows, chosen_ref, entry_ref, terms_ref, *refs):
-    *far, send_ref, all_ref = refs
-    row, core, _ = whereabouts()
-    half_terms(rows, row, chosen_ref, terms_ref, far, 1 - core, send_ref, all_ref)
-    send_ref[all_ref.shape[0]:, :] = entry_ref[...]
-
-
-def keep_kernel(rows, turned_in, chosen_ref, terms_ref, *refs):
-    *far, turned_ref, keep_ref, all_ref = refs
-    row, core, _ = whereabouts()
-    half_terms(rows, row, chosen_ref, terms_ref, far, core, keep_ref, all_ref)
-    for i, piece in enumerate(far):
-        half, width = piece.shape
+        upper_ref, lower_ref, chosen_ref = far
+        width = upper_ref.shape[1]
         start = aligned(row ^ (rows - 1), width)
-        turned_ref[i * half:(i + 1) * half, pl.ds(start, width)] = piece[...]
-
-
-def pair_kernel(rows, keep_ref, got_ref, entry_ref, *out_refs):
+        turned_ref[:half, pl.ds(start, width)] = upper_ref[...]
+        turned_ref[half:, pl.ds(start, width)] = lower_ref[...]
+        block = jnp.where(core == 0, upper_ref[...], lower_ref[...])
+        for k, piece in enumerate(add_far(rows, block, chosen_ref[...], far_ref)):
+            keep_ref[k * size:(k + 1) * size, :] += piece
+
+
+def pair_kernel(rows, keep_ref, entry_ref, *refs):
+    *far, far_ref = refs
+    far, out_refs = far[:-rows], far[-rows:]
     size = keep_ref.shape[0] // rows
-    entry = entry_ref[:1, :] + got_ref[rows * size:rows * size + 1, :]
+    pieces = add_far(rows, far[0][...], far[1][...], far_ref) if far else None
     for k, out_ref in enumerate(out_refs):
-        part = slice(k * size, (k + 1) * size)
-        encode(keep_ref[part, :] + got_ref[part, :], out_ref, 0, SHORT, entry)
+        value = keep_ref[k * size:(k + 1) * size, :]
+        encode(value + pieces[k] if far else value, out_ref, 0, SHORT, entry_ref[:1, :])
 
 
 def sum_kernel(*refs):
@@ -226,7 +236,7 @@
 def join_kernel(*refs):
     *in_refs, out_ref = refs
     size = in_refs[0].shape[0] - SHORT
-    for k, ref in enumerate(in_refs):
+    for k, ref in enumerate(in_refs[:1] + in_refs[:0:-1]):
         start = k * (size + TAIL)
         out_ref[start:start + size, :] = ref[:size, :]
         tail = ref[size:, :].astype(jnp.int32)
@@ -347,15 +357,20 @@
     return [int(f"{p:0{width}b}"[::-1], 2) for p in range(count)]
 
 
-def gather_pieces(solves, rows, ready):
+def turn(solves, rows):
     block, panel = solves.shape
     if rows != 4:
-        return [lax.all_gather(solves.T, "row", axis=1, tiled=True)]
+        return None, None
     half = pltpu.VMEM((panel // 2, block), BF16)
-    upper, lower = call(
+    return call(
         turn_kernel, (half, half), solves, remain=1,
         scratch=[pltpu.VMEM((2, block, panel // 2), BF16), pltpu.SemaphoreType.DMA((2,))],
     )
+
+
+def gather_pieces(solves, upper, lower, ready):
+    if upper is None:
+        return [lax.all_gather(solves.T, "row", axis=1, tiled=True)]
     lower_x, upper_y = swap(lower, "row", 1), swap(upper, "row", 2)
     upper_x, lower_y = swap(upper, "row", 1), swap(lower, "row", 2)
     upper_far, lower_far = swap(after(upper_y, *ready), "row", 1), swap(after(lower_x, *ready), "row", 2)
@@ -375,42 +390,50 @@
     shape = pltpu.VMEM
     panel_row, diagonal_row = panel_rows[None, :], border_diagonal.T
     first_row = row * row_count + place * share
-    picked = shape((local, panel), BF16)
-    chunk_room = [
-        pltpu.VMEM((CHUNKS // 2, local // CHUNKS, row_count), BF16), pltpu.SemaphoreType.DMA((CHUNKS // 2,))
+    picked, part_picked = shape((local, panel), BF16), shape((local // CHUNKS, panel), BF16)
+    chunk_room = lambda count: [
+        pltpu.VMEM((count, local // CHUNKS, row_count), BF16), pltpu.SemaphoreType.DMA((count,))
     ]
-    chosen, entry, one, panel_row, diagonal_row = call(
-        pick_kernel,
+    room, done = chunk_room(1)
+    upper, lower = turn(solves, rows)
+    chosen, far_chosen, entry, one, panel_row, diagonal_row = call(
+        functools.partial(pick_kernel, rows),
         (
-            picked, shape((8, panel), F32), shape((row_count, panel), BF16),
+            picked, part_picked, shape((8, panel), F32), shape((row_count, panel), BF16),
             shape((1, panel), jnp.int32), shape((1, share), F32),
         ),
-        panel_row, diagonal_row, coupling, remain=3,
-        scratch=[chunk_room[0], pltpu.SemaphoreType.DMA((2,)), chunk_room[1]],
-    )
-    pieces = gather_pieces(solves, rows, (entry,))
+        panel_row, diagonal_row, coupling, remain=3, scratch=[room, pltpu.SemaphoreType.DMA((2,)), done],
+    )
+    pieces = gather_pieces(solves, upper, lower, (entry,))
     near, far = pieces[:6], pieces[6:]
-    chosen = call(rest_kernel, picked, chosen, one, coupling, remain=1, scratch=chunk_room, aliases={0: 0})
-    room = [pltpu.VMEM((panel // 2, panel), F32)]
-    turned, terms = call(
-        early_kernel, (shape((panel, local), BF16), shape((panel, panel), F32)), chosen, *near
-    )
-    send = call(
-        functools.partial(send_kernel, rows), shape((panel // 2 + 8, panel), F32),
-        chosen, entry, terms, *far, scratch=room,
-    )
-    turned, keep = call(
-        functools.partial(keep_kernel, rows), (shape((panel, local), BF16), shape((panel // 2, panel), F32)),
-        turned, chosen, terms, *far, scratch=room, aliases={0: 0},
+    split = rows == 4 and share % 128 == 0
+    chosen = call(
+        functools.partial(rest_kernel, rows), picked, chosen, one, coupling, remain=1,
+        scratch=chunk_room(CHUNKS - 1), aliases={0: 0},
+    )
+    other_chosen = swap(after(far_chosen, near[2], near[5]), "scen", 1) if split else None
+    half_shape, room = shape((panel // 2, panel), F32), [pltpu.VMEM((panel // 2, panel), F32)]
+    turned, own_near, send_near = call(
+        functools.partial(early_kernel, rows),
+        (shape((panel, local), BF16), half_shape, shape((panel // 2 + 8, panel), F32)),
+        chosen, entry, *near, scratch=[pltpu.VMEM((panel, panel), F32)],
+    )
+    got_near = swap(send_near, "scen", 1)
+    if split:
+        far_send = call(select_kernel, shape(far[0].shape, BF16), far[0], far[1], micros=3.0)
+        other_far = [swap(far_send, "scen", 1), other_chosen]
+        own_far = [*far, far_chosen]
+    else:
+        other_far = own_far = []
+    turned, keep, entry = call(
+        functools.partial(keep_kernel, rows), (shape((panel, local), BF16), half_shape, shape((8, panel), F32)),
+        turned, own_near, got_near, entry, *own_far, scratch=room, aliases={0: 0},
     )
     coded = shape((size + SHORT, panel), I16)
-    codes = call(
-        functools.partial(pair_kernel, rows), (coded,) * rows, keep, swap(send, "scen", 1), entry
-    )
-    arrived = [swap(codes[k], "row", k) for k in range(rows - 1, 0, -1)]
+    codes = call(functools.partial(pair_kernel, rows), (coded,) * rows, keep, entry, *other_far, scratch=room)
+    arrived = [swap(codes[k], "row", k) for k in [1, *range(rows - 1, 1, -1)]]
     part = codes[0]
     steps = bits_of(layers)
-    split = share % 128 == 0
     if split:
         count = layers // 2
         bulk = shape((layers * panel, share), F32)
@@ -426,7 +449,7 @@
         own = own + jnp.where(panel_rows[:, None] == mine[None, :], border_diagonal[:, 0][None, :], F32(0.0))
         part = call(sum_kernel, coded, part, *arrived)
     if split:
-        others = [swap(part, "scen", 2 * k) for k in range(1, layers)]
+        others = [swap(part, "scen", 2 * k) for k in range(layers - 1, 0, -1)]
         own, bulk_codes = call(functools.partial(bulk_pair_kernel, panel), halved(count), after(own, part), got)
         part = call(sum_kernel, coded, after(part, bulk_codes), *others, micros=5.0)
     else:
@@ -441,7 +464,7 @@
         got = [swap(bulk_codes, "scen", layers)]
     if split:
         part = after(part, bulk_codes)
-    joined = call(join_kernel, shape((rows * (size + TAIL), panel), I16), part, *shared)
+    joined = call(join_kernel, shape((rows * (size + TAIL), panel), I16), part, *shared[::-1])
     other = swap(joined, "scen", 1)
     own_half = call(
         functools.partial(own_kernel, rows), shape((panel // 2, panel), F32), joined

time: 57.8 us -> 57.5 us (level)
  waiting for transfers between devices: 16.1 us -> 14.1 us
  starting transfers between devices: 21.8 us -> 23.7 us
    ppermute x20 -> x22, waiting for transfers between devices: 16.1 us -> 14.1 us  [swap(): return lax.ppermute(x, axis, [(i, i ^ bit) for i in range(count)])]
    ppermute x20 -> x22, starting transfers between devices: 21.8 us -> 23.7 us  [swap(): return lax.ppermute(x, axis, [(i, i ^ bit) for i in range(count)])]
  transfers between devices with their start and end apart: 20 -> 22, of which waited for: 15 -> 16; matrix products, arithmetic and copies ran while one was open for 0% -> 0% of each run, Pallas kernels for 28% -> 28%
where the time goes in v17:
time: 57.5 us; the launch traced here: 57.3 us
  starting transfers between devices  23.7 us (41%)
  Pallas kernels  18.7 us (33%)
  waiting for transfers between devices  14.1 us (25%)
  between operations  0.8 us (1%)
    ppermute x22, starting transfers between devices, swap(): return lax.ppermute(x, axis, [(i, i ^ bit) for i in range(count)])  23.7 us
    pallas_call x16, Pallas kernels, call(): pl.pallas_call(kernel, name=getattr(kernel, 'func', kernel).__name__, out...  18.7 us
    ppermute x22, waiting for transfers between devices, swap(): return lax.ppermute(x, axis, [(i, i ^ bit) for i in range(count)])  14.1 us
  transfers between devices with their start and end apart: 22, of which 16 were waited for; matrix products, arithmetic and copies ran while one was open for 0% of the time, Pallas kernels for 28%

profile of v17, /device:TPU:0, one launch (start us, length us, event | category | flops | bytes accessed | tf_op | source)
XLA Modules:
  0.0 57.3 jit_solution(7379227110653072387)
XLA Ops:
  0.6 1.2 %turn_kernel.1 = (bf16[256,384]{1,0:T(8,128)(2,1)S(1)}, bf16[256,384]{1,0:T(8,128)(2,1)S(1)}) custom-call(bf16[384,512]{1,0:T(8,128)(2,1)} %bitcast.7), custom_call_target="tpu_custom_call" | custom-call | bytes 1024 | tf_op jit(solution)/shard_map/turn_kernel/pallas_call | solution.py:329
  1.8 3.0 %collective-permute-start.2 = (bf16[256,384]{1,0:T(8,128)(2,1)S(1)}, bf16[256,384]{1,0:T(8,128)(2,1)S(1)}, u32[]{:S(2)}, u32[]{:S(2)}) collective-permute-start(bf16[256,384]{1,0:T(8,128)(2,1)S(1)} %get-tuple-element.39.refs_0_), channel_id=1, source_target_pairs={{0,2},{1,3},{2,0},{3,1},{4,6},{5,7},{6,4},{7,5},{8,10},{9,11},{10,... | collective-permute-start | bytes 589832 | tf_op jit(solution)/shard_map/ppermute | solution.py:344
  4.8 1.5 %collective-permute-start.1 = (bf16[256,384]{1,0:T(8,128)(2,1)S(1)}, bf16[256,384]{1,0:T(8,128)(2,1)S(1)}, u32[]{:S(2)}, u32[]{:S(2)}) collective-permute-start(bf16[256,384]{1,0:T(8,128)(2,1)S(1)} %get-tuple-element.40.refs_1_), channel_id=1, source_target_pairs={{0,1},{1,0},{2,3},{3,2},{4,5},{5,4},{6,7},{7,6},{8,9},{9,8},{10,11... | collective-permute-start | bytes 589832 | tf_op jit(solution)/shard_map/ppermute | solution.py:344
  6.3 0.5 collective-permute-start
  6.9 0.1 collective-permute-start.3
  6.9 1.8 %pick_kernel.1 = (bf16[1536,512]{1,0:T(8,128)(2,1)S(1)}, bf16[384,512]{1,0:T(8,128)(2,1)S(1)}, f32[8,512]{1,0:T(8,128)S(1)}, bf16[1024,512]{1,0:T(8,128)(2,1)S(1...) custom-call(s32[1,512]{1,0:T(1,128)} %bitcast.8, f32[1,128]{1,0:T(1,128)} %bitcast.9, bf16[1536,1024]{1,0:T(8,128)(2,1)} %bitcast.4), custom_call_target="tpu_custom_call" | custom-call | bytes 1024 | tf_op jit(solution)/shard_map/pick_kernel/pallas_call | solution.py:329
  8.8 1.8 %collective-permute-done.2.refs_4_ = bf16[256,384]{1,0:T(8,128)(2,1)S(1)} collective-permute-done((bf16[256,384]{1,0:T(8,128)(2,1)S(1)}, bf16[256,384]{1,0:T(8,128)(2,1)S(1)}, u32[]{:S(2)}, u32[]{:S(2)}) %collective-permute-start.2) | collective-permute-done | bytes 196640 | tf_op jit(solution)/shard_map/ppermute | solution.py:344
  10.6 2.0 %collective-permute-start.5 = (bf16[256,384]{1,0:T(8,128)(2,1)S(1)}, bf16[256,384]{1,0:T(8,128)(2,1)S(1)}, u32[]{:S(2)}, u32[]{:S(2)}) collective-permute-start(bf16[256,384]{1,0:T(8,128)(2,1)S(1)} %collective-permute-done.2.refs_4_), channel_id=1, source_target_pairs={{0,1},{1,0},{2,3},{3,2},{4,5},{5,4},{6,7},{7,6},{8,9},{9,8},{10,11... | collective-permute-start | bytes 589832 | tf_op jit(solution)/shard_map/ppermute | solution.py:344
  12.6 0.1 collective-permute-done.1.refs_3_
  12.7 1.5 %collective-permute-start.6 = (bf16[256,384]{1,0:T(8,128)(2,1)S(1)}, bf16[256,384]{1,0:T(8,128)(2,1)S(1)}, u32[]{:S(2)}, u32[]{:S(2)}) collective-permute-start(bf16[256,384]{1,0:T(8,128)(2,1)S(1)} %collective-permute-done.1.refs_3_), channel_id=1, source_target_pairs={{0,2},{1,3},{2,0},{3,1},{4,6},{5,7},{6,4},{7,5},{8,10},{9,11},{10,... | collective-permute-start | bytes 589832 | tf_op jit(solution)/shard_map/ppermute | solution.py:344
  14.1 2.9 %rest_kernel.1.chosen_ref = bf16[1536,512]{1,0:T(8,128)(2,1)S(1)} custom-call(bf16[1536,512]{1,0:T(8,128)(2,1)S(1)} %get-tuple-element.36.chosen_in, bf16[1024,512]{1,0:T(8,128)(2,1)S(1)} %get-tuple-element.37.one_ref, bf16[1536,1024]{1,0:T(8,128)(2,1)} %bitcast.5), custom_call_target="tpu_custom_call", output_to_operand_aliasing={{}: (0, {})} | custom-call | bytes 1024 | tf_op jit(solution)/shard_map/rest_kernel/pallas_call | solution.py:329
  17.0 0.0 collective-permute-done.refs_2_
  17.0 0.0 collective-permute-done.3.refs_5_
  17.0 1.2 %early_kernel.1 = (bf16[512,1536]{1,0:T(8,128)(2,1)S(1)}, f32[256,512]{1,0:T(8,128)S(1)}, f32[264,512]{1,0:T(8,128)S(1)}) custom-call(bf16[1536,512]{1,0:T(8,128)(2,1)S(1)} %rest_kernel.1.chosen_ref, f32[8,512]{1,0:T(8,128)S(1)} %get-tuple-element.38.entry_ref, bf16[256,384]{1,0:T(8,128)(2,1)S(1)} %get-tuple-element.39.refs_0_, ...), custom_call_target="tpu_custom_call" | custom-call | bytes 1024 | tf_op jit(solution)/shard_map/early_kernel/pallas_call | solution.py:329
  18.2 0.1 collective-permute-start.4
  18.3 0.5 collective-permute-start.8
  18.8 0.8 %collective-permute-done.5.refs_0_.upper_ref = bf16[256,384]{1,0:T(8,128)(2,1)S(1)} collective-permute-done((bf16[256,384]{1,0:T(8,128)(2,1)S(1)}, bf16[256,384]{1,0:T(8,128)(2,1)S(1)}, u32[]{:S(2)}, u32[]{:S(2)}) %collective-permute-start.5) | collective-permute-done | bytes 196640 | tf_op jit(solution)/shard_map/ppermute | solution.py:344
  19.6 0.0 collective-permute-done.6.refs_1_.lower_ref
  19.7 0.1 collective-permute-start.7
  19.7 0.5 collective-permute-done.4.got_ref
  20.2 0.0 copy-start
  20.2 0.4 keep_kernel.1
  20.6 0.6 %collective-permute-done.7.refs_0_ = bf16[256,384]{1,0:T(8,128)(2,1)S(1)} collective-permute-done((bf16[256,384]{1,0:T(8,128)(2,1)S(1)}, bf16[256,384]{1,0:T(8,128)(2,1)S(1)}, u32[]{:S(2)}, u32[]{:S(2)}) %collective-permute-start.7) | collective-permute-done | bytes 196640 | tf_op jit(solution)/shard_map/ppermute | solution.py:344
  21.2 0.0 collective-permute-done.8.refs_1_
  21.2 0.5 pair_kernel.1
  21.6 1.5 %collective-permute-start.10 = (s16[72,512]{1,0:T(8,128)(2,1)S(1)}, s16[72,512]{1,0:T(8,128)(2,1)S(1)}, u32[]{:S(2)}, u32[]{:S(2)}) collective-permute-start(s16[72,512]{1,0:T(8,128)(2,1)S(1)} %get-tuple-element.58), channel_id=1, source_target_pairs={{0,3},{1,2},{2,1},{3,0},{4,7},{5,6},{6,5},{7,4},{8,11},{9,10},{10,... | collective-permute-start | bytes 221192 | tf_op jit(solution)/shard_map/ppermute | solution.py:344
  23.1 1.5 %collective-permute-start.11 = (s16[72,512]{1,0:T(8,128)(2,1)S(1)}, s16[72,512]{1,0:T(8,128)(2,1)S(1)}, u32[]{:S(2)}, u32[]{:S(2)}) collective-permute-start(s16[72,512]{1,0:T(8,128)(2,1)S(1)} %get-tuple-element.59), channel_id=1, source_target_pairs={{0,2},{1,3},{2,0},{3,1},{4,6},{5,7},{6,4},{7,5},{8,10},{9,11},{10,... | collective-permute-start | bytes 221192 | tf_op jit(solution)/shard_map/ppermute | solution.py:344
  24.6 0.5 collective-permute-start.9
  25.2 0.0 copy-done
  25.2 1.8 %schur_kernel.1 = (f32[2048,128]{1,0:T(8,128)S(1)}, f32[2048,128]{1,0:T(8,128)S(1)}) custom-call(s32[1,512]{1,0:T(1,128)S(1)} %get-tuple-element.51.panel_ref, f32[1,128]{1,0:T(1,128)S(1)} %get-tuple-element.52.own_diagonal_ref, bf16[1536,1024]{1,0:T(8,128)(2,1)S(1)} %bitcast.6, bf16[512,1536]{1,0:T(8,128)(2,1)S(1)} %get-tuple-element.54.turned_ref), custom_call_target="tpu_custom_call" | custom-call | flops 2300000000 | bytes 1024 | tf_op jit(solution)/shard_map/schur_kernel/pallas_call | solution.py:329
  27.0 0.1 collective-permute-start.12
  27.1 0.1 collective-permute-done.10.refs_2_
  27.2 1.3 %collective-permute-done.11.refs_3_ = s16[72,512]{1,0:T(8,128)(2,1)S(1)} collective-permute-done((s16[72,512]{1,0:T(8,128)(2,1)S(1)}, s16[72,512]{1,0:T(8,128)(2,1)S(1)}, u32[]{:S(2)}, u32[]{:S(2)}) %collective-permute-start.11) | collective-permute-done | bytes 73760 | tf_op jit(solution)/shard_map/ppermute | solution.py:344
  28.5 0.5 collective-permute-done.9.refs_1_
  29.0 0.1 sum_kernel.2.refs_0_
  29.1 3.7 %collective-permute-start.13 = (s16[72,512]{1,0:T(8,128)(2,1)S(1)}, s16[72,512]{1,0:T(8,128)(2,1)S(1)}, u32[]{:S(2)}, u32[]{:S(2)}) collective-permute-start(s16[72,512]{1,0:T(8,128)(2,1)S(1)} %sum_kernel.2.refs_0_), channel_id=1, source_target_pairs={{0,24},{4,28},{8,16},{12,20},{16,8},{20,12},{24,0},{28,4},{1,25},{... | collective-permute-start | bytes 221192 | tf_op jit(solution)/shard_map/ppermute | solution.py:344
  32.8 0.0 collective-permute-start.14
  32.8 0.8 %collective-permute-start.15 = (s16[72,512]{1,0:T(8,128)(2,1)S(1)}, s16[72,512]{1,0:T(8,128)(2,1)S(1)}, u32[]{:S(2)}, u32[]{:S(2)}) collective-permute-start(s16[72,512]{1,0:T(8,128)(2,1)S(1)} %sum_kernel.2.refs_0_), channel_id=1, source_target_pairs={{0,8},{4,12},{8,0},{12,4},{16,24},{20,28},{24,16},{28,20},{1,9},{5... | collective-permute-start | bytes 221192 | tf_op jit(solution)/shard_map/ppermute | solution.py:344
  33.6 0.0 collective-permute-done.12.got_ref
  33.6 0.2 bulk_pair_kernel.1
  33.8 1.3 %collective-permute-start.16 = (s16[1056,128]{1,0:T(8,128)(2,1)S(1)}, s16[1056,128]{1,0:T(8,128)(2,1)S(1)}, u32[]{:S(2)}, u32[]{:S(2)}) collective-permute-start(s16[1056,128]{1,0:T(8,128)(2,1)S(1)} %get-tuple-element.62), channel_id=1, source_target_pairs={{0,8},{4,12},{8,0},{12,4},{16,24},{20,28},{24,16},{28,20},{1,9},{5... | collective-permute-start | bytes 811016 | tf_op jit(solution)/shard_map/ppermute | solution.py:344
  35.1 1.2 %collective-permute-done.13.refs_1_ = s16[72,512]{1,0:T(8,128)(2,1)S(1)} collective-permute-done((s16[72,512]{1,0:T(8,128)(2,1)S(1)}, s16[72,512]{1,0:T(8,128)(2,1)S(1)}, u32[]{:S(2)}, u32[]{:S(2)}) %collective-permute-start.13) | collective-permute-done | bytes 73760 | tf_op jit(solution)/shard_map/ppermute | solution.py:344
  36.3 2.5 %collective-permute-done.14.refs_2_ = s16[72,512]{1,0:T(8,128)(2,1)S(1)} collective-permute-done((s16[72,512]{1,0:T(8,128)(2,1)S(1)}, s16[72,512]{1,0:T(8,128)(2,1)S(1)}, u32[]{:S(2)}, u32[]{:S(2)}) %collective-permute-start.14) | collective-permute-done | bytes 73760 | tf_op jit(solution)/shard_map/ppermute | solution.py:344
  38.8 0.8 %collective-permute-done.15.refs_3_ = s16[72,512]{1,0:T(8,128)(2,1)S(1)} collective-permute-done((s16[72,512]{1,0:T(8,128)(2,1)S(1)}, s16[72,512]{1,0:T(8,128)(2,1)S(1)}, u32[]{:S(2)}, u32[]{:S(2)}) %collective-permute-start.15) | collective-permute-done | bytes 73760 | tf_op jit(solution)/shard_map/ppermute | solution.py:344
  39.6 0.1 sum_kernel.3.refs_0_
  39.7 1.0 %collective-permute-start.17 = (s16[72,512]{1,0:T(8,128)(2,1)S(1)}, s16[72,512]{1,0:T(8,128)(2,1)S(1)}, u32[]{:S(2)}, u32[]{:S(2)}) collective-permute-start(s16[72,512]{1,0:T(8,128)(2,1)S(1)} %sum_kernel.3.refs_0_), channel_id=1, source_target_pairs={{0,3},{1,2},{2,1},{3,0},{4,7},{5,6},{6,5},{7,4},{8,11},{9,10},{10,... | collective-permute-start | bytes 221192 | tf_op jit(solution)/shard_map/ppermute | solution.py:344
  40.7 1.1 %collective-permute-start.18 = (s16[72,512]{1,0:T(8,128)(2,1)S(1)}, s16[72,512]{1,0:T(8,128)(2,1)S(1)}, u32[]{:S(2)}, u32[]{:S(2)}) collective-permute-start(s16[72,512]{1,0:T(8,128)(2,1)S(1)} %sum_kernel.3.refs_0_), channel_id=1, source_target_pairs={{0,2},{1,3},{2,0},{3,1},{4,6},{5,7},{6,4},{7,5},{8,10},{9,11},{10,... | collective-permute-start | bytes 221192 | tf_op jit(solution)/shard_map/ppermute | solution.py:344
  41.8 1.5 %collective-permute-start.19 = (s16[72,512]{1,0:T(8,128)(2,1)S(1)}, s16[72,512]{1,0:T(8,128)(2,1)S(1)}, u32[]{:S(2)}, u32[]{:S(2)}) collective-permute-start(s16[72,512]{1,0:T(8,128)(2,1)S(1)} %sum_kernel.3.refs_0_), channel_id=1, source_target_pairs={{0,1},{1,0},{2,3},{3,2},{4,5},{5,4},{6,7},{7,6},{8,9},{9,8},{10,11... | collective-permute-start | bytes 221192 | tf_op jit(solution)/shard_map/ppermute | solution.py:344
  43.3 1.1 %collective-permute-done.16.got_ref = s16[1056,128]{1,0:T(8,128)(2,1)S(1)} collective-permute-done((s16[1056,128]{1,0:T(8,128)(2,1)S(1)}, s16[1056,128]{1,0:T(8,128)(2,1)S(1)}, u32[]{:S(2)}, u32[]{:S(2)}) %collective-permute-start.16) | collective-permute-done | bytes 270368 | tf_op jit(solution)/shard_map/ppermute | solution.py:344
  44.4 0.2 bulk_sum_kernel.1
  44.5 0.6 %collective-permute-done.17.refs_1_ = s16[72,512]{1,0:T(8,128)(2,1)S(1)} collective-permute-done((s16[72,512]{1,0:T(8,128)(2,1)S(1)}, s16[72,512]{1,0:T(8,128)(2,1)S(1)}, u32[]{:S(2)}, u32[]{:S(2)}) %collective-permute-start.17) | collective-permute-done | bytes 73760 | tf_op jit(solution)/shard_map/ppermute | solution.py:344
  45.1 0.7 %collective-permute-done.18.refs_2_ = s16[72,512]{1,0:T(8,128)(2,1)S(1)} collective-permute-done((s16[72,512]{1,0:T(8,128)(2,1)S(1)}, s16[72,512]{1,0:T(8,128)(2,1)S(1)}, u32[]{:S(2)}, u32[]{:S(2)}) %collective-permute-start.18) | collective-permute-done | bytes 73760 | tf_op jit(solution)/shard_map/ppermute | solution.py:344
  45.9 0.3 collective-permute-done.19.refs_3_
  46.2 0.1 collective-permute-start.20
  46.3 1.4 %collective-permute-start.21 = (s16[528,128]{1,0:T(8,128)(2,1)S(1)}, s16[528,128]{1,0:T(8,128)(2,1)S(1)}, u32[]{:S(2)}, u32[]{:S(2)}) collective-permute-start(s16[528,128]{1,0:T(8,128)(2,1)S(1)} %get-tuple-element.65), channel_id=1, source_target_pairs={{0,16},{4,20},{8,24},{12,28},{16,0},{20,4},{24,8},{28,12},{1,17},{... | collective-permute-start | bytes 405512 | tf_op jit(solution)/shard_map/ppermute | solution.py:344
  47.7 0.2 own_kernel.1.half_ref
  47.9 0.0 collective-permute-done.20.other_ref
  47.9 7.0 %newton_kernel.1 = (f32[256,256]{1,0:T(8,128)S(1)}, f32[256,512]{1,0:T(8,128)S(1)}) custom-call(f32[256,512]{1,0:T(8,128)S(1)} %own_kernel.1.half_ref, s16[320,512]{1,0:T(8,128)(2,1)S(1)} %collective-permute-done.20.other_ref), custom_call_target="tpu_custom_call" | custom-call | bytes 1024 | tf_op jit(solution)/shard_map/newton_kernel/pallas_call | solution.py:329
  54.9 1.2 %collective-permute-done.21.refs_0_ = s16[528,128]{1,0:T(8,128)(2,1)S(1)} collective-permute-done((s16[528,128]{1,0:T(8,128)(2,1)S(1)}, s16[528,128]{1,0:T(8,128)(2,1)S(1)}, u32[]{:S(2)}, u32[]{:S(2)}) %collective-permute-start.21) | collective-permute-done | bytes 135200 | tf_op jit(solution)/shard_map/ppermute | solution.py:344
  56.1 1.2 %factor_kernel.1 = (f32[128,1,256]{2,1,0:T(1,128)}, f32[128,1,256]{2,1,0:T(1,128)}) custom-call(f32[256,256]{1,0:T(8,128)S(1)} %get-tuple-element.67.inverse_first_ref, f32[256,512]{1,0:T(8,128)S(1)} %get-tuple-element.68.inverse_second_ref, f32[512,128]{1,0:T(8,128)S(1)} %get-tuple-element.69.rows_ref, s16[528,128]{1,0:T(8,128)(2,1)S(1)} %collective-permute-done.21.refs_0_), custom_call_target="tpu_custom_call" | custom-call | bytes 1024 | tf_op jit(solution)/shard_map/factor_kernel/pallas_call | solution.py:329
  (2 shorter events, 0.1 us)
Async XLA Ops:
  1.8 8.8 %collective-permute-start.2 = (bf16[256,384]{1,0:T(8,128)(2,1)S(1)}, bf16[256,384]{1,0:T(8,128)(2,1)S(1)}, u32[]{:S(2)}, u32[]{:S(2)}) collective-permute-start(bf16[256,384]{1,0:T(8,128)(2,1)S(1)} %get-tuple-element.39.refs_0_), channel_id=1, source_target_pairs={{0,2},{1,3},{2,0},{3,1},{4,6},{5,7},{6,4},{7,5},{8,10},{9,11},{10,... | collective-permute-start | bytes 589832 | tf_op jit(solution)/shard_map/ppermute | solution.py:344
  4.8 7.8 %collective-permute-start.1 = (bf16[256,384]{1,0:T(8,128)(2,1)S(1)}, bf16[256,384]{1,0:T(8,128)(2,1)S(1)}, u32[]{:S(2)}, u32[]{:S(2)}) collective-permute-start(bf16[256,384]{1,0:T(8,128)(2,1)S(1)} %get-tuple-element.40.refs_1_), channel_id=1, source_target_pairs={{0,1},{1,0},{2,3},{3,2},{4,5},{5,4},{6,7},{7,6},{8,9},{9,8},{10,11... | collective-permute-start | bytes 589832 | tf_op jit(solution)/shard_map/ppermute | solution.py:344
  6.3 10.7 %collective-permute-start = (bf16[256,384]{1,0:T(8,128)(2,1)S(1)}, bf16[256,384]{1,0:T(8,128)(2,1)S(1)}, u32[]{:S(2)}, u32[]{:S(2)}) collective-permute-start(bf16[256,384]{1,0:T(8,128)(2,1)S(1)} %get-tuple-element.39.refs_0_), channel_id=1, source_target_pairs={{0,1},{1,0},{2,3},{3,2},{4,5},{5,4},{6,7},{7,6},{8,9},{9,8},{10,11... | collective-permute-start | bytes 589832 | tf_op jit(solution)/shard_map/ppermute | solution.py:344
  6.9 10.2 %collective-permute-start.3 = (bf16[256,384]{1,0:T(8,128)(2,1)S(1)}, bf16[256,384]{1,0:T(8,128)(2,1)S(1)}, u32[]{:S(2)}, u32[]{:S(2)}) collective-permute-start(bf16[256,384]{1,0:T(8,128)(2,1)S(1)} %get-tuple-element.40.refs_1_), channel_id=1, source_target_pairs={{0,2},{1,3},{2,0},{3,1},{4,6},{5,7},{6,4},{7,5},{8,10},{9,11},{10,... | collective-permute-start | bytes 589832 | tf_op jit(solution)/shard_map/ppermute | solution.py:344
  10.6 9.1 %collective-permute-start.5 = (bf16[256,384]{1,0:T(8,128)(2,1)S(1)}, bf16[256,384]{1,0:T(8,128)(2,1)S(1)}, u32[]{:S(2)}, u32[]{:S(2)}) collective-permute-start(bf16[256,384]{1,0:T(8,128)(2,1)S(1)} %collective-permute-done.2.refs_4_), channel_id=1, source_target_pairs={{0,1},{1,0},{2,3},{3,2},{4,5},{5,4},{6,7},{7,6},{8,9},{9,8},{10,11... | collective-permute-start | bytes 589832 | tf_op jit(solution)/shard_map/ppermute | solution.py:344
  12.7 7.0 %collective-permute-start.6 = (bf16[256,384]{1,0:T(8,128)(2,1)S(1)}, bf16[256,384]{1,0:T(8,128)(2,1)S(1)}, u32[]{:S(2)}, u32[]{:S(2)}) collective-permute-start(bf16[256,384]{1,0:T(8,128)(2,1)S(1)} %collective-permute-done.1.refs_3_), channel_id=1, source_target_pairs={{0,2},{1,3},{2,0},{3,1},{4,6},{5,7},{6,4},{7,5},{8,10},{9,11},{10,... | collective-permute-start | bytes 589832 | tf_op jit(solution)/shard_map/ppermute | solution.py:344
  18.2 2.0 %collective-permute-start.4 = (f32[264,512]{1,0:T(8,128)S(1)}, f32[264,512]{1,0:T(8,128)S(1)}, u32[]{:S(2)}, u32[]{:S(2)}) collective-permute-start(f32[264,512]{1,0:T(8,128)S(1)} %get-tuple-element.43), channel_id=1, source_target_pairs={{0,4},{4,0},{8,12},{12,8},{16,20},{20,16},{24,28},{28,24},{1,5},{5... | collective-permute-start | bytes 1622024 | tf_op jit(solution)/shard_map/ppermute | solution.py:344
  18.3 2.9 %collective-permute-start.8 = (bf16[384,512]{1,0:T(8,128)(2,1)S(1)}, bf16[384,512]{1,0:T(8,128)(2,1)S(1)}, u32[]{:S(2)}, u32[]{:S(2)}) collective-permute-start(bf16[384,512]{1,0:T(8,128)(2,1)S(1)} %get-tuple-element.49.refs_2_), channel_id=1, source_target_pairs={{0,4},{4,0},{8,12},{12,8},{16,20},{20,16},{24,28},{28,24},{1,5},{5... | collective-permute-start | bytes 1179656 | tf_op jit(solution)/shard_map/ppermute | solution.py:344
  19.7 1.5 %collective-permute-start.7 = (bf16[256,384]{1,0:T(8,128)(2,1)S(1)}, bf16[256,384]{1,0:T(8,128)(2,1)S(1)}, u32[]{:S(2)}, u32[]{:S(2)}) collective-permute-start(bf16[256,384]{1,0:T(8,128)(2,1)S(1)} %select_kernel.1), channel_id=1, source_target_pairs={{0,4},{4,0},{8,12},{12,8},{16,20},{20,16},{24,28},{28,24},{1,5},{5... | collective-permute-start | bytes 589832 | tf_op jit(solution)/shard_map/ppermute | solution.py:344
  20.2 5.0 %copy-start = (bf16[1,1536,1024]{2,1,0:T(8,128)(2,1)S(1)}, bf16[1,1536,1024]{2,1,0:T(8,128)(2,1)}, u32[]{:S(2)}) copy-start(bf16[1,1536,1024]{2,1,0:T(8,128)(2,1)} %param.4) | copy-start | bytes 9437188
  21.6 5.6 %collective-permute-start.10 = (s16[72,512]{1,0:T(8,128)(2,1)S(1)}, s16[72,512]{1,0:T(8,128)(2,1)S(1)}, u32[]{:S(2)}, u32[]{:S(2)}) collective-permute-start(s16[72,512]{1,0:T(8,128)(2,1)S(1)} %get-tuple-element.58), channel_id=1, source_target_pairs={{0,3},{1,2},{2,1},{3,0},{4,7},{5,6},{6,5},{7,4},{8,11},{9,10},{10,... | collective-permute-start | bytes 221192 | tf_op jit(solution)/shard_map/ppermute | solution.py:344
  23.1 5.4 %collective-permute-start.11 = (s16[72,512]{1,0:T(8,128)(2,1)S(1)}, s16[72,512]{1,0:T(8,128)(2,1)S(1)}, u32[]{:S(2)}, u32[]{:S(2)}) collective-permute-start(s16[72,512]{1,0:T(8,128)(2,1)S(1)} %get-tuple-element.59), channel_id=1, source_target_pairs={{0,2},{1,3},{2,0},{3,1},{4,6},{5,7},{6,4},{7,5},{8,10},{9,11},{10,... | collective-permute-start | bytes 221192 | tf_op jit(solution)/shard_map/ppermute | solution.py:344
  24.6 4.4 %collective-permute-start.9 = (s16[72,512]{1,0:T(8,128)(2,1)S(1)}, s16[72,512]{1,0:T(8,128)(2,1)S(1)}, u32[]{:S(2)}, u32[]{:S(2)}) collective-permute-start(s16[72,512]{1,0:T(8,128)(2,1)S(1)} %get-tuple-element.57), channel_id=1, source_target_pairs={{0,1},{1,0},{2,3},{3,2},{4,5},{5,4},{6,7},{7,6},{8,9},{9,8},{10,11... | collective-permute-start | bytes 221192 | tf_op jit(solution)/shard_map/ppermute | solution.py:344
  27.0 6.6 %collective-permute-start.12 = (f32[2048,128]{1,0:T(8,128)S(1)}, f32[2048,128]{1,0:T(8,128)S(1)}, u32[]{:S(2)}, u32[]{:S(2)}) collective-permute-start(f32[2048,128]{1,0:T(8,128)S(1)} %get-tuple-element.61), channel_id=1, source_target_pairs={{0,4},{4,0},{8,12},{12,8},{16,20},{20,16},{24,28},{28,24},{1,5},{5... | collective-permute-start | bytes 3145736 | tf_op jit(solution)/shard_map/ppermute | solution.py:344
  29.1 7.2 %collective-permute-start.13 = (s16[72,512]{1,0:T(8,128)(2,1)S(1)}, s16[72,512]{1,0:T(8,128)(2,1)S(1)}, u32[]{:S(2)}, u32[]{:S(2)}) collective-permute-start(s16[72,512]{1,0:T(8,128)(2,1)S(1)} %sum_kernel.2.refs_0_), channel_id=1, source_target_pairs={{0,24},{4,28},{8,16},{12,20},{16,8},{20,12},{24,0},{28,4},{1,25},{... | collective-permute-start | bytes 221192 | tf_op jit(solution)/shard_map/ppermute | solution.py:344
  32.8 5.9 %collective-permute-start.14 = (s16[72,512]{1,0:T(8,128)(2,1)S(1)}, s16[72,512]{1,0:T(8,128)(2,1)S(1)}, u32[]{:S(2)}, u32[]{:S(2)}) collective-permute-start(s16[72,512]{1,0:T(8,128)(2,1)S(1)} %sum_kernel.2.refs_0_), channel_id=1, source_target_pairs={{0,16},{4,20},{8,24},{12,28},{16,0},{20,4},{24,8},{28,12},{1,17},{... | collective-permute-start | bytes 221192 | tf_op jit(solution)/shard_map/ppermute | solution.py:344
  32.8 6.8 %collective-permute-start.15 = (s16[72,512]{1,0:T(8,128)(2,1)S(1)}, s16[72,512]{1,0:T(8,128)(2,1)S(1)}, u32[]{:S(2)}, u32[]{:S(2)}) collective-permute-start(s16[72,512]{1,0:T(8,128)(2,1)S(1)} %sum_kernel.2.refs_0_), channel_id=1, source_target_pairs={{0,8},{4,12},{8,0},{12,4},{16,24},{20,28},{24,16},{28,20},{1,9},{5... | collective-permute-start | bytes 221192 | tf_op jit(solution)/shard_map/ppermute | solution.py:344
  33.8 10.6 %collective-permute-start.16 = (s16[1056,128]{1,0:T(8,128)(2,1)S(1)}, s16[1056,128]{1,0:T(8,128)(2,1)S(1)}, u32[]{:S(2)}, u32[]{:S(2)}) collective-permute-start(s16[1056,128]{1,0:T(8,128)(2,1)S(1)} %get-tuple-element.62), channel_id=1, source_target_pairs={{0,8},{4,12},{8,0},{12,4},{16,24},{20,28},{24,16},{28,20},{1,9},{5... | collective-permute-start | bytes 811016 | tf_op jit(solution)/shard_map/ppermute | solution.py:344
  39.7 5.4 %collective-permute-start.17 = (s16[72,512]{1,0:T(8,128)(2,1)S(1)}, s16[72,512]{1,0:T(8,128)(2,1)S(1)}, u32[]{:S(2)}, u32[]{:S(2)}) collective-permute-start(s16[72,512]{1,0:T(8,128)(2,1)S(1)} %sum_kernel.3.refs_0_), channel_id=1, source_target_pairs={{0,3},{1,2},{2,1},{3,0},{4,7},{5,6},{6,5},{7,4},{8,11},{9,10},{10,... | collective-permute-start | bytes 221192 | tf_op jit(solution)/shard_map/ppermute | solution.py:344
  40.7 5.1 %collective-permute-start.18 = (s16[72,512]{1,0:T(8,128)(2,1)S(1)}, s16[72,512]{1,0:T(8,128)(2,1)S(1)}, u32[]{:S(2)}, u32[]{:S(2)}) collective-permute-start(s16[72,512]{1,0:T(8,128)(2,1)S(1)} %sum_kernel.3.refs_0_), channel_id=1, source_target_pairs={{0,2},{1,3},{2,0},{3,1},{4,6},{5,7},{6,4},{7,5},{8,10},{9,11},{10,... | collective-permute-start | bytes 221192 | tf_op jit(solution)/shard_map/ppermute | solution.py:344
  41.8 4.4 %collective-permute-start.19 = (s16[72,512]{1,0:T(8,128)(2,1)S(1)}, s16[72,512]{1,0:T(8,128)(2,1)S(1)}, u32[]{:S(2)}, u32[]{:S(2)}) collective-permute-start(s16[72,512]{1,0:T(8,128)(2,1)S(1)} %sum_kernel.3.refs_0_), channel_id=1, source_target_pairs={{0,1},{1,0},{2,3},{3,2},{4,5},{5,4},{6,7},{7,6},{8,9},{9,8},{10,11... | collective-permute-start | bytes 221192 | tf_op jit(solution)/shard_map/ppermute | solution.py:344
  46.2 1.7 %collective-permute-start.20 = (s16[320,512]{1,0:T(8,128)(2,1)S(1)}, s16[320,512]{1,0:T(8,128)(2,1)S(1)}, u32[]{:S(2)}, u32[]{:S(2)}) collective-permute-start(s16[320,512]{1,0:T(8,128)(2,1)S(1)} %join_kernel.1.own_ref), channel_id=1, source_target_pairs={{0,4},{4,0},{8,12},{12,8},{16,20},{20,16},{24,28},{28,24},{1,5},{5... | collective-permute-start | bytes 983048 | tf_op jit(solution)/shard_map/ppermute | solution.py:344
  46.3 9.8 %collective-permute-start.21 = (s16[528,128]{1,0:T(8,128)(2,1)S(1)}, s16[528,128]{1,0:T(8,128)(2,1)S(1)}, u32[]{:S(2)}, u32[]{:S(2)}) collective-permute-start(s16[528,128]{1,0:T(8,128)(2,1)S(1)} %get-tuple-element.65), channel_id=1, source_target_pairs={{0,16},{4,20},{8,24},{12,28},{16,0},{20,4},{24,8},{28,12},{1,17},{... | collective-permute-start | bytes 405512 | tf_op jit(solution)/shard_map/ppermute | solution.py:344

commit v18 on v17

--- a/solution.py
+++ b/solution.py
@@ -12,6 +12,7 @@
 TAIL = 16
 SHORT = 8
 CHUNKS = 4
+FIRST = 2
 LEVELS = 32000.0
 F32 = jnp.float32
 BF16 = jnp.bfloat16
@@ -139,8 +140,8 @@
     ]
     for copy in small:
         copy.start()
-    block = order_of(rows)[0]
-    copies = fetch(coupling_ref, coupling_copy, done, [block])
+    blocks = order_of(rows)[:FIRST]
+    copies = fetch(coupling_ref, coupling_copy, done, blocks)
     for copy in small:
         copy.wait()
     columns, panel = one_ref.shape
@@ -156,11 +157,14 @@
     copies[0].wait()
     size = far_ref.shape[0]
     far_ref[...] = dot(coupling_copy[0], one_ref[...]).astype(BF16)
-    chosen_ref[pl.ds(aligned(block, size), size), :] = far_ref[...]
+    chosen_ref[pl.ds(aligned(blocks[0], size), size), :] = far_ref[...]
+    for i in range(1, FIRST):
+        copies[i].wait()
+        chosen_ref[pl.ds(aligned(blocks[i], size), size), :] = dot(coupling_copy[i], one_ref[...]).astype(BF16)
 
 
 def rest_kernel(rows, chosen_in, one_ref, coupling_ref, chosen_ref, coupling_copy, done):
-    blocks = order_of(rows)[1:]
+    blocks = order_of(rows)[FIRST:]
     size = coupling_copy.shape[1]
     for i, copy in enumerate(fetch(coupling_ref, coupling_copy, done, blocks)):
         copy.wait()
@@ -394,7 +398,7 @@
     chunk_room = lambda count: [
         pltpu.VMEM((count, local // CHUNKS, row_count), BF16), pltpu.SemaphoreType.DMA((count,))
     ]
-    room, done = chunk_room(1)
+    room, done = chunk_room(FIRST)
     upper, lower = turn(solves, rows)
     chosen, far_chosen, entry, one, panel_row, diagonal_row = call(
         functools.partial(pick_kernel, rows),
@@ -409,7 +413,7 @@
     split = rows == 4 and share % 128 == 0
     chosen = call(
         functools.partial(rest_kernel, rows), picked, chosen, one, coupling, remain=1,
-        scratch=chunk_room(CHUNKS - 1), aliases={0: 0},
+        scratch=chunk_room(CHUNKS - FIRST), aliases={0: 0},
     )
     other_chosen = swap(after(far_chosen, near[2], near[5]), "scen", 1) if split else None
     half_shape, room = shape((panel // 2, panel), F32), [pltpu.VMEM((panel // 2, panel), F32)]

time: 57.5 us -> 57.5 us (level)
  transfers between devices with their start and end apart: 22 -> 22, of which waited for: 16 -> 17; matrix products, arithmetic and copies ran while one was open for 0% -> 0% of each run, Pallas kernels for 28% -> 28%
where the time goes in v18:
time: 57.5 us; the launch traced here: 57.3 us
  starting transfers between devices  23.7 us (41%)
  Pallas kernels  18.7 us (33%)
  waiting for transfers between devices  14.1 us (25%)
  between operations  0.78 us (1%)
    ppermute x22, starting transfers between devices, swap(): return lax.ppermute(x, axis, [(i, i ^ bit) for i in range(count)])  23.7 us
    pallas_call x16, Pallas kernels, call(): pl.pallas_call(kernel, name=getattr(kernel, 'func', kernel).__name__, out...  18.7 us
    ppermute x22, waiting for transfers between devices, swap(): return lax.ppermute(x, axis, [(i, i ^ bit) for i in range(count)])  14.1 us
  transfers between devices with their start and end apart: 22, of which 17 were waited for; matrix products, arithmetic and copies ran while one was open for 0% of the time, Pallas kernels for 28%

profile of v18, /device:TPU:0, one launch (start us, length us, event | category | flops | bytes accessed | tf_op | source)
XLA Modules:
  0.0 57.3 jit_solution(12975803818462439458)
XLA Ops:
  0.6 1.2 %turn_kernel.1 = (bf16[256,384]{1,0:T(8,128)(2,1)S(1)}, bf16[256,384]{1,0:T(8,128)(2,1)S(1)}) custom-call(bf16[384,512]{1,0:T(8,128)(2,1)} %bitcast.7), custom_call_target="tpu_custom_call" | custom-call | bytes 1024 | tf_op jit(solution)/shard_map/turn_kernel/pallas_call | solution.py:333
  1.8 3.0 %collective-permute-start.2 = (bf16[256,384]{1,0:T(8,128)(2,1)S(1)}, bf16[256,384]{1,0:T(8,128)(2,1)S(1)}, u32[]{:S(2)}, u32[]{:S(2)}) collective-permute-start(bf16[256,384]{1,0:T(8,128)(2,1)S(1)} %get-tuple-element.39.refs_0_), channel_id=1, source_target_pairs={{0,2},{1,3},{2,0},{3,1},{4,6},{5,7},{6,4},{7,5},{8,10},{9,11},{10,... | collective-permute-start | bytes 589832 | tf_op jit(solution)/shard_map/ppermute | solution.py:348
  4.8 1.5 %collective-permute-start.1 = (bf16[256,384]{1,0:T(8,128)(2,1)S(1)}, bf16[256,384]{1,0:T(8,128)(2,1)S(1)}, u32[]{:S(2)}, u32[]{:S(2)}) collective-permute-start(bf16[256,384]{1,0:T(8,128)(2,1)S(1)} %get-tuple-element.40.refs_1_), channel_id=1, source_target_pairs={{0,1},{1,0},{2,3},{3,2},{4,5},{5,4},{6,7},{7,6},{8,9},{9,8},{10,11... | collective-permute-start | bytes 589832 | tf_op jit(solution)/shard_map/ppermute | solution.py:348
  6.3 0.5 collective-permute-start
  6.9 0.1 collective-permute-start.3
  6.9 2.4 %pick_kernel.1 = (bf16[1536,512]{1,0:T(8,128)(2,1)S(1)}, bf16[384,512]{1,0:T(8,128)(2,1)S(1)}, f32[8,512]{1,0:T(8,128)S(1)}, bf16[1024,512]{1,0:T(8,128)(2,1)S(1...) custom-call(s32[1,512]{1,0:T(1,128)} %bitcast.8, f32[1,128]{1,0:T(1,128)} %bitcast.9, bf16[1536,1024]{1,0:T(8,128)(2,1)} %bitcast.4), custom_call_target="tpu_custom_call" | custom-call | bytes 1024 | tf_op jit(solution)/shard_map/pick_kernel/pallas_call | solution.py:333
  9.4 1.2 %collective-permute-done.2.refs_4_ = bf16[256,384]{1,0:T(8,128)(2,1)S(1)} collective-permute-done((bf16[256,384]{1,0:T(8,128)(2,1)S(1)}, bf16[256,384]{1,0:T(8,128)(2,1)S(1)}, u32[]{:S(2)}, u32[]{:S(2)}) %collective-permute-start.2) | collective-permute-done | bytes 196640 | tf_op jit(solution)/shard_map/ppermute | solution.py:348
  10.6 2.0 %collective-permute-start.5 = (bf16[256,384]{1,0:T(8,128)(2,1)S(1)}, bf16[256,384]{1,0:T(8,128)(2,1)S(1)}, u32[]{:S(2)}, u32[]{:S(2)}) collective-permute-start(bf16[256,384]{1,0:T(8,128)(2,1)S(1)} %collective-permute-done.2.refs_4_), channel_id=1, source_target_pairs={{0,1},{1,0},{2,3},{3,2},{4,5},{5,4},{6,7},{7,6},{8,9},{9,8},{10,11... | collective-permute-start | bytes 589832 | tf_op jit(solution)/shard_map/ppermute | solution.py:348
  12.6 0.1 collective-permute-done.1.refs_3_
  12.7 1.5 %collective-permute-start.6 = (bf16[256,384]{1,0:T(8,128)(2,1)S(1)}, bf16[256,384]{1,0:T(8,128)(2,1)S(1)}, u32[]{:S(2)}, u32[]{:S(2)}) collective-permute-start(bf16[256,384]{1,0:T(8,128)(2,1)S(1)} %collective-permute-done.1.refs_3_), channel_id=1, source_target_pairs={{0,2},{1,3},{2,0},{3,1},{4,6},{5,7},{6,4},{7,5},{8,10},{9,11},{10,... | collective-permute-start | bytes 589832 | tf_op jit(solution)/shard_map/ppermute | solution.py:348
  14.1 2.3 %rest_kernel.1.chosen_ref = bf16[1536,512]{1,0:T(8,128)(2,1)S(1)} custom-call(bf16[1536,512]{1,0:T(8,128)(2,1)S(1)} %get-tuple-element.36.chosen_in, bf16[1024,512]{1,0:T(8,128)(2,1)S(1)} %get-tuple-element.37.one_ref, bf16[1536,1024]{1,0:T(8,128)(2,1)} %bitcast.5), custom_call_target="tpu_custom_call", output_to_operand_aliasing={{}: (0, {})} | custom-call | bytes 1024 | tf_op jit(solution)/shard_map/rest_kernel/pallas_call | solution.py:333
  16.4 0.5 collective-permute-done.refs_2_
  16.9 0.0 collective-permute-done.3.refs_5_
  16.9 1.2 %early_kernel.1 = (bf16[512,1536]{1,0:T(8,128)(2,1)S(1)}, f32[256,512]{1,0:T(8,128)S(1)}, f32[264,512]{1,0:T(8,128)S(1)}) custom-call(bf16[1536,512]{1,0:T(8,128)(2,1)S(1)} %rest_kernel.1.chosen_ref, f32[8,512]{1,0:T(8,128)S(1)} %get-tuple-element.38.entry_ref, bf16[256,384]{1,0:T(8,128)(2,1)S(1)} %get-tuple-element.39.refs_0_, ...), custom_call_target="tpu_custom_call" | custom-call | bytes 1024 | tf_op jit(solution)/shard_map/early_kernel/pallas_call | solution.py:333
  18.0 0.1 collective-permute-start.4
  18.1 0.5 collective-permute-start.8
  18.6 1.0 %collective-permute-done.5.refs_0_.upper_ref = bf16[256,384]{1,0:T(8,128)(2,1)S(1)} collective-permute-done((bf16[256,384]{1,0:T(8,128)(2,1)S(1)}, bf16[256,384]{1,0:T(8,128)(2,1)S(1)}, u32[]{:S(2)}, u32[]{:S(2)}) %collective-permute-start.5) | collective-permute-done | bytes 196640 | tf_op jit(solution)/shard_map/ppermute | solution.py:348
  19.6 0.0 collective-permute-done.6.refs_1_.lower_ref
  19.7 0.1 collective-permute-start.7
  19.7 0.3 collective-permute-done.4.got_ref
  20.0 0.0 copy-start
  20.0 0.4 keep_kernel.1
  20.4 0.7 %collective-permute-done.7.refs_0_ = bf16[256,384]{1,0:T(8,128)(2,1)S(1)} collective-permute-done((bf16[256,384]{1,0:T(8,128)(2,1)S(1)}, bf16[256,384]{1,0:T(8,128)(2,1)S(1)}, u32[]{:S(2)}, u32[]{:S(2)}) %collective-permute-start.7) | collective-permute-done | bytes 196640 | tf_op jit(solution)/shard_map/ppermute | solution.py:348
  21.2 0.0 collective-permute-done.8.refs_1_
  21.2 0.5 pair_kernel.1
  21.6 1.5 %collective-permute-start.10 = (s16[72,512]{1,0:T(8,128)(2,1)S(1)}, s16[72,512]{1,0:T(8,128)(2,1)S(1)}, u32[]{:S(2)}, u32[]{:S(2)}) collective-permute-start(s16[72,512]{1,0:T(8,128)(2,1)S(1)} %get-tuple-element.58), channel_id=1, source_target_pairs={{0,3},{1,2},{2,1},{3,0},{4,7},{5,6},{6,5},{7,4},{8,11},{9,10},{10,... | collective-permute-start | bytes 221192 | tf_op jit(solution)/shard_map/ppermute | solution.py:348
  23.1 1.5 %collective-permute-start.11 = (s16[72,512]{1,0:T(8,128)(2,1)S(1)}, s16[72,512]{1,0:T(8,128)(2,1)S(1)}, u32[]{:S(2)}, u32[]{:S(2)}) collective-permute-start(s16[72,512]{1,0:T(8,128)(2,1)S(1)} %get-tuple-element.59), channel_id=1, source_target_pairs={{0,2},{1,3},{2,0},{3,1},{4,6},{5,7},{6,4},{7,5},{8,10},{9,11},{10,... | collective-permute-start | bytes 221192 | tf_op jit(solution)/shard_map/ppermute | solution.py:348
  24.6 0.5 collective-permute-start.9
  25.2 0.0 copy-done
  25.2 1.8 %schur_kernel.1 = (f32[2048,128]{1,0:T(8,128)S(1)}, f32[2048,128]{1,0:T(8,128)S(1)}) custom-call(s32[1,512]{1,0:T(1,128)S(1)} %get-tuple-element.51.panel_ref, f32[1,128]{1,0:T(1,128)S(1)} %get-tuple-element.52.own_diagonal_ref, bf16[1536,1024]{1,0:T(8,128)(2,1)S(1)} %bitcast.6, bf16[512,1536]{1,0:T(8,128)(2,1)S(1)} %get-tuple-element.54.turned_ref), custom_call_target="tpu_custom_call" | custom-call | flops 2300000000 | bytes 1024 | tf_op jit(solution)/shard_map/schur_kernel/pallas_call | solution.py:333
  27.0 0.1 collective-permute-start.12
  27.1 0.1 collective-permute-done.10.refs_2_
  27.2 1.3 %collective-permute-done.11.refs_3_ = s16[72,512]{1,0:T(8,128)(2,1)S(1)} collective-permute-done((s16[72,512]{1,0:T(8,128)(2,1)S(1)}, s16[72,512]{1,0:T(8,128)(2,1)S(1)}, u32[]{:S(2)}, u32[]{:S(2)}) %collective-permute-start.11) | collective-permute-done | bytes 73760 | tf_op jit(solution)/shard_map/ppermute | solution.py:348
  28.5 0.5 collective-permute-done.9.refs_1_
  29.0 0.1 sum_kernel.2.refs_0_
  29.1 3.7 %collective-permute-start.13 = (s16[72,512]{1,0:T(8,128)(2,1)S(1)}, s16[72,512]{1,0:T(8,128)(2,1)S(1)}, u32[]{:S(2)}, u32[]{:S(2)}) collective-permute-start(s16[72,512]{1,0:T(8,128)(2,1)S(1)} %sum_kernel.2.refs_0_), channel_id=1, source_target_pairs={{0,24},{4,28},{8,16},{12,20},{16,8},{20,12},{24,0},{28,4},{1,25},{... | collective-permute-start | bytes 221192 | tf_op jit(solution)/shard_map/ppermute | solution.py:348
  32.8 0.0 collective-permute-start.14
  32.8 0.8 %collective-permute-start.15 = (s16[72,512]{1,0:T(8,128)(2,1)S(1)}, s16[72,512]{1,0:T(8,128)(2,1)S(1)}, u32[]{:S(2)}, u32[]{:S(2)}) collective-permute-start(s16[72,512]{1,0:T(8,128)(2,1)S(1)} %sum_kernel.2.refs_0_), channel_id=1, source_target_pairs={{0,8},{4,12},{8,0},{12,4},{16,24},{20,28},{24,16},{28,20},{1,9},{5... | collective-permute-start | bytes 221192 | tf_op jit(solution)/shard_map/ppermute | solution.py:348
  33.6 0.0 collective-permute-done.12.got_ref
  33.6 0.2 bulk_pair_kernel.1
  33.8 1.3 %collective-permute-start.16 = (s16[1056,128]{1,0:T(8,128)(2,1)S(1)}, s16[1056,128]{1,0:T(8,128)(2,1)S(1)}, u32[]{:S(2)}, u32[]{:S(2)}) collective-permute-start(s16[1056,128]{1,0:T(8,128)(2,1)S(1)} %get-tuple-element.62), channel_id=1, source_target_pairs={{0,8},{4,12},{8,0},{12,4},{16,24},{20,28},{24,16},{28,20},{1,9},{5... | collective-permute-start | bytes 811016 | tf_op jit(solution)/shard_map/ppermute | solution.py:348
  35.1 1.2 %collective-permute-done.13.refs_1_ = s16[72,512]{1,0:T(8,128)(2,1)S(1)} collective-permute-done((s16[72,512]{1,0:T(8,128)(2,1)S(1)}, s16[72,512]{1,0:T(8,128)(2,1)S(1)}, u32[]{:S(2)}, u32[]{:S(2)}) %collective-permute-start.13) | collective-permute-done | bytes 73760 | tf_op jit(solution)/shard_map/ppermute | solution.py:348
  36.3 2.5 %collective-permute-done.14.refs_2_ = s16[72,512]{1,0:T(8,128)(2,1)S(1)} collective-permute-done((s16[72,512]{1,0:T(8,128)(2,1)S(1)}, s16[72,512]{1,0:T(8,128)(2,1)S(1)}, u32[]{:S(2)}, u32[]{:S(2)}) %collective-permute-start.14) | collective-permute-done | bytes 73760 | tf_op jit(solution)/shard_map/ppermute | solution.py:348
  38.8 0.8 %collective-permute-done.15.refs_3_ = s16[72,512]{1,0:T(8,128)(2,1)S(1)} collective-permute-done((s16[72,512]{1,0:T(8,128)(2,1)S(1)}, s16[72,512]{1,0:T(8,128)(2,1)S(1)}, u32[]{:S(2)}, u32[]{:S(2)}) %collective-permute-start.15) | collective-permute-done | bytes 73760 | tf_op jit(solution)/shard_map/ppermute | solution.py:348
  39.6 0.1 sum_kernel.3.refs_0_
  39.7 1.0 %collective-permute-start.17 = (s16[72,512]{1,0:T(8,128)(2,1)S(1)}, s16[72,512]{1,0:T(8,128)(2,1)S(1)}, u32[]{:S(2)}, u32[]{:S(2)}) collective-permute-start(s16[72,512]{1,0:T(8,128)(2,1)S(1)} %sum_kernel.3.refs_0_), channel_id=1, source_target_pairs={{0,3},{1,2},{2,1},{3,0},{4,7},{5,6},{6,5},{7,4},{8,11},{9,10},{10,... | collective-permute-start | bytes 221192 | tf_op jit(solution)/shard_map/ppermute | solution.py:348
  40.7 1.1 %collective-permute-start.18 = (s16[72,512]{1,0:T(8,128)(2,1)S(1)}, s16[72,512]{1,0:T(8,128)(2,1)S(1)}, u32[]{:S(2)}, u32[]{:S(2)}) collective-permute-start(s16[72,512]{1,0:T(8,128)(2,1)S(1)} %sum_kernel.3.refs_0_), channel_id=1, source_target_pairs={{0,2},{1,3},{2,0},{3,1},{4,6},{5,7},{6,4},{7,5},{8,10},{9,11},{10,... | collective-permute-start | bytes 221192 | tf_op jit(solution)/shard_map/ppermute | solution.py:348
  41.8 1.5 %collective-permute-start.19 = (s16[72,512]{1,0:T(8,128)(2,1)S(1)}, s16[72,512]{1,0:T(8,128)(2,1)S(1)}, u32[]{:S(2)}, u32[]{:S(2)}) collective-permute-start(s16[72,512]{1,0:T(8,128)(2,1)S(1)} %sum_kernel.3.refs_0_), channel_id=1, source_target_pairs={{0,1},{1,0},{2,3},{3,2},{4,5},{5,4},{6,7},{7,6},{8,9},{9,8},{10,11... | collective-permute-start | bytes 221192 | tf_op jit(solution)/shard_map/ppermute | solution.py:348
  43.3 1.1 %collective-permute-done.16.got_ref = s16[1056,128]{1,0:T(8,128)(2,1)S(1)} collective-permute-done((s16[1056,128]{1,0:T(8,128)(2,1)S(1)}, s16[1056,128]{1,0:T(8,128)(2,1)S(1)}, u32[]{:S(2)}, u32[]{:S(2)}) %collective-permute-start.16) | collective-permute-done | bytes 270368 | tf_op jit(solution)/shard_map/ppermute | solution.py:348
  44.4 0.2 bulk_sum_kernel.1
  44.5 0.6 %collective-permute-done.17.refs_1_ = s16[72,512]{1,0:T(8,128)(2,1)S(1)} collective-permute-done((s16[72,512]{1,0:T(8,128)(2,1)S(1)}, s16[72,512]{1,0:T(8,128)(2,1)S(1)}, u32[]{:S(2)}, u32[]{:S(2)}) %collective-permute-start.17) | collective-permute-done | bytes 73760 | tf_op jit(solution)/shard_map/ppermute | solution.py:348
  45.1 0.7 %collective-permute-done.18.refs_2_ = s16[72,512]{1,0:T(8,128)(2,1)S(1)} collective-permute-done((s16[72,512]{1,0:T(8,128)(2,1)S(1)}, s16[72,512]{1,0:T(8,128)(2,1)S(1)}, u32[]{:S(2)}, u32[]{:S(2)}) %collective-permute-start.18) | collective-permute-done | bytes 73760 | tf_op jit(solution)/shard_map/ppermute | solution.py:348
  45.9 0.3 collective-permute-done.19.refs_3_
  46.2 0.1 collective-permute-start.20
  46.3 1.4 %collective-permute-start.21 = (s16[528,128]{1,0:T(8,128)(2,1)S(1)}, s16[528,128]{1,0:T(8,128)(2,1)S(1)}, u32[]{:S(2)}, u32[]{:S(2)}) collective-permute-start(s16[528,128]{1,0:T(8,128)(2,1)S(1)} %get-tuple-element.65), channel_id=1, source_target_pairs={{0,16},{4,20},{8,24},{12,28},{16,0},{20,4},{24,8},{28,12},{1,17},{... | collective-permute-start | bytes 405512 | tf_op jit(solution)/shard_map/ppermute | solution.py:348
  47.7 0.2 own_kernel.1.half_ref
  47.9 0.0 collective-permute-done.20.other_ref
  47.9 7.0 %newton_kernel.1 = (f32[256,256]{1,0:T(8,128)S(1)}, f32[256,512]{1,0:T(8,128)S(1)}) custom-call(f32[256,512]{1,0:T(8,128)S(1)} %own_kernel.1.half_ref, s16[320,512]{1,0:T(8,128)(2,1)S(1)} %collective-permute-done.20.other_ref), custom_call_target="tpu_custom_call" | custom-call | bytes 1024 | tf_op jit(solution)/shard_map/newton_kernel/pallas_call | solution.py:333
  54.9 1.2 %collective-permute-done.21.refs_0_ = s16[528,128]{1,0:T(8,128)(2,1)S(1)} collective-permute-done((s16[528,128]{1,0:T(8,128)(2,1)S(1)}, s16[528,128]{1,0:T(8,128)(2,1)S(1)}, u32[]{:S(2)}, u32[]{:S(2)}) %collective-permute-start.21) | collective-permute-done | bytes 135200 | tf_op jit(solution)/shard_map/ppermute | solution.py:348
  56.1 1.2 %factor_kernel.1 = (f32[128,1,256]{2,1,0:T(1,128)}, f32[128,1,256]{2,1,0:T(1,128)}) custom-call(f32[256,256]{1,0:T(8,128)S(1)} %get-tuple-element.67.inverse_first_ref, f32[256,512]{1,0:T(8,128)S(1)} %get-tuple-element.68.inverse_second_ref, f32[512,128]{1,0:T(8,128)S(1)} %get-tuple-element.69.rows_ref, s16[528,128]{1,0:T(8,128)(2,1)S(1)} %collective-permute-done.21.refs_0_), custom_call_target="tpu_custom_call" | custom-call | bytes 1024 | tf_op jit(solution)/shard_map/factor_kernel/pallas_call | solution.py:333
  (2 shorter events, 0.1 us)
Async XLA Ops:
  1.8 8.8 %collective-permute-start.2 = (bf16[256,384]{1,0:T(8,128)(2,1)S(1)}, bf16[256,384]{1,0:T(8,128)(2,1)S(1)}, u32[]{:S(2)}, u32[]{:S(2)}) collective-permute-start(bf16[256,384]{1,0:T(8,128)(2,1)S(1)} %get-tuple-element.39.refs_0_), channel_id=1, source_target_pairs={{0,2},{1,3},{2,0},{3,1},{4,6},{5,7},{6,4},{7,5},{8,10},{9,11},{10,... | collective-permute-start | bytes 589832 | tf_op jit(solution)/shard_map/ppermute | solution.py:348
  4.8 7.8 %collective-permute-start.1 = (bf16[256,384]{1,0:T(8,128)(2,1)S(1)}, bf16[256,384]{1,0:T(8,128)(2,1)S(1)}, u32[]{:S(2)}, u32[]{:S(2)}) collective-permute-start(bf16[256,384]{1,0:T(8,128)(2,1)S(1)} %get-tuple-element.40.refs_1_), channel_id=1, source_target_pairs={{0,1},{1,0},{2,3},{3,2},{4,5},{5,4},{6,7},{7,6},{8,9},{9,8},{10,11... | collective-permute-start | bytes 589832 | tf_op jit(solution)/shard_map/ppermute | solution.py:348
  6.3 10.5 %collective-permute-start = (bf16[256,384]{1,0:T(8,128)(2,1)S(1)}, bf16[256,384]{1,0:T(8,128)(2,1)S(1)}, u32[]{:S(2)}, u32[]{:S(2)}) collective-permute-start(bf16[256,384]{1,0:T(8,128)(2,1)S(1)} %get-tuple-element.39.refs_0_), channel_id=1, source_target_pairs={{0,1},{1,0},{2,3},{3,2},{4,5},{5,4},{6,7},{7,6},{8,9},{9,8},{10,11... | collective-permute-start | bytes 589832 | tf_op jit(solution)/shard_map/ppermute | solution.py:348
  6.9 10.0 %collective-permute-start.3 = (bf16[256,384]{1,0:T(8,128)(2,1)S(1)}, bf16[256,384]{1,0:T(8,128)(2,1)S(1)}, u32[]{:S(2)}, u32[]{:S(2)}) collective-permute-start(bf16[256,384]{1,0:T(8,128)(2,1)S(1)} %get-tuple-element.40.refs_1_), channel_id=1, source_target_pairs={{0,2},{1,3},{2,0},{3,1},{4,6},{5,7},{6,4},{7,5},{8,10},{9,11},{10,... | collective-permute-start | bytes 589832 | tf_op jit(solution)/shard_map/ppermute | solution.py:348
  10.6 9.1 %collective-permute-start.5 = (bf16[256,384]{1,0:T(8,128)(2,1)S(1)}, bf16[256,384]{1,0:T(8,128)(2,1)S(1)}, u32[]{:S(2)}, u32[]{:S(2)}) collective-permute-start(bf16[256,384]{1,0:T(8,128)(2,1)S(1)} %collective-permute-done.2.refs_4_), channel_id=1, source_target_pairs={{0,1},{1,0},{2,3},{3,2},{4,5},{5,4},{6,7},{7,6},{8,9},{9,8},{10,11... | collective-permute-start | bytes 589832 | tf_op jit(solution)/shard_map/ppermute | solution.py:348
  12.7 7.0 %collective-permute-start.6 = (bf16[256,384]{1,0:T(8,128)(2,1)S(1)}, bf16[256,384]{1,0:T(8,128)(2,1)S(1)}, u32[]{:S(2)}, u32[]{:S(2)}) collective-permute-start(bf16[256,384]{1,0:T(8,128)(2,1)S(1)} %collective-permute-done.1.refs_3_), channel_id=1, source_target_pairs={{0,2},{1,3},{2,0},{3,1},{4,6},{5,7},{6,4},{7,5},{8,10},{9,11},{10,... | collective-permute-start | bytes 589832 | tf_op jit(solution)/shard_map/ppermute | solution.py:348
  18.0 2.0 %collective-permute-start.4 = (f32[264,512]{1,0:T(8,128)S(1)}, f32[264,512]{1,0:T(8,128)S(1)}, u32[]{:S(2)}, u32[]{:S(2)}) collective-permute-start(f32[264,512]{1,0:T(8,128)S(1)} %get-tuple-element.43), channel_id=1, source_target_pairs={{0,4},{4,0},{8,12},{12,8},{16,20},{20,16},{24,28},{28,24},{1,5},{5... | collective-permute-start | bytes 1622024 | tf_op jit(solution)/shard_map/ppermute | solution.py:348
  18.1 3.0 %collective-permute-start.8 = (bf16[384,512]{1,0:T(8,128)(2,1)S(1)}, bf16[384,512]{1,0:T(8,128)(2,1)S(1)}, u32[]{:S(2)}, u32[]{:S(2)}) collective-permute-start(bf16[384,512]{1,0:T(8,128)(2,1)S(1)} %get-tuple-element.49.refs_2_), channel_id=1, source_target_pairs={{0,4},{4,0},{8,12},{12,8},{16,20},{20,16},{24,28},{28,24},{1,5},{5... | collective-permute-start | bytes 1179656 | tf_op jit(solution)/shard_map/ppermute | solution.py:348
  19.7 1.5 %collective-permute-start.7 = (bf16[256,384]{1,0:T(8,128)(2,1)S(1)}, bf16[256,384]{1,0:T(8,128)(2,1)S(1)}, u32[]{:S(2)}, u32[]{:S(2)}) collective-permute-start(bf16[256,384]{1,0:T(8,128)(2,1)S(1)} %select_kernel.1), channel_id=1, source_target_pairs={{0,4},{4,0},{8,12},{12,8},{16,20},{20,16},{24,28},{28,24},{1,5},{5... | collective-permute-start | bytes 589832 | tf_op jit(solution)/shard_map/ppermute | solution.py:348
  20.0 5.1 %copy-start = (bf16[1,1536,1024]{2,1,0:T(8,128)(2,1)S(1)}, bf16[1,1536,1024]{2,1,0:T(8,128)(2,1)}, u32[]{:S(2)}) copy-start(bf16[1,1536,1024]{2,1,0:T(8,128)(2,1)} %param.4) | copy-start | bytes 9437188
  21.6 5.6 %collective-permute-start.10 = (s16[72,512]{1,0:T(8,128)(2,1)S(1)}, s16[72,512]{1,0:T(8,128)(2,1)S(1)}, u32[]{:S(2)}, u32[]{:S(2)}) collective-permute-start(s16[72,512]{1,0:T(8,128)(2,1)S(1)} %get-tuple-element.58), channel_id=1, source_target_pairs={{0,3},{1,2},{2,1},{3,0},{4,7},{5,6},{6,5},{7,4},{8,11},{9,10},{10,... | collective-permute-start | bytes 221192 | tf_op jit(solution)/shard_map/ppermute | solution.py:348
  23.1 5.4 %collective-permute-start.11 = (s16[72,512]{1,0:T(8,128)(2,1)S(1)}, s16[72,512]{1,0:T(8,128)(2,1)S(1)}, u32[]{:S(2)}, u32[]{:S(2)}) collective-permute-start(s16[72,512]{1,0:T(8,128)(2,1)S(1)} %get-tuple-element.59), channel_id=1, source_target_pairs={{0,2},{1,3},{2,0},{3,1},{4,6},{5,7},{6,4},{7,5},{8,10},{9,11},{10,... | collective-permute-start | bytes 221192 | tf_op jit(solution)/shard_map/ppermute | solution.py:348
  24.6 4.4 %collective-permute-start.9 = (s16[72,512]{1,0:T(8,128)(2,1)S(1)}, s16[72,512]{1,0:T(8,128)(2,1)S(1)}, u32[]{:S(2)}, u32[]{:S(2)}) collective-permute-start(s16[72,512]{1,0:T(8,128)(2,1)S(1)} %get-tuple-element.57), channel_id=1, source_target_pairs={{0,1},{1,0},{2,3},{3,2},{4,5},{5,4},{6,7},{7,6},{8,9},{9,8},{10,11... | collective-permute-start | bytes 221192 | tf_op jit(solution)/shard_map/ppermute | solution.py:348
  27.0 6.6 %collective-permute-start.12 = (f32[2048,128]{1,0:T(8,128)S(1)}, f32[2048,128]{1,0:T(8,128)S(1)}, u32[]{:S(2)}, u32[]{:S(2)}) collective-permute-start(f32[2048,128]{1,0:T(8,128)S(1)} %get-tuple-element.61), channel_id=1, source_target_pairs={{0,4},{4,0},{8,12},{12,8},{16,20},{20,16},{24,28},{28,24},{1,5},{5... | collective-permute-start | bytes 3145736 | tf_op jit(solution)/shard_map/ppermute | solution.py:348
  29.1 7.2 %collective-permute-start.13 = (s16[72,512]{1,0:T(8,128)(2,1)S(1)}, s16[72,512]{1,0:T(8,128)(2,1)S(1)}, u32[]{:S(2)}, u32[]{:S(2)}) collective-permute-start(s16[72,512]{1,0:T(8,128)(2,1)S(1)} %sum_kernel.2.refs_0_), channel_id=1, source_target_pairs={{0,24},{4,28},{8,16},{12,20},{16,8},{20,12},{24,0},{28,4},{1,25},{... | collective-permute-start | bytes 221192 | tf_op jit(solution)/shard_map/ppermute | solution.py:348
  32.8 5.9 %collective-permute-start.14 = (s16[72,512]{1,0:T(8,128)(2,1)S(1)}, s16[72,512]{1,0:T(8,128)(2,1)S(1)}, u32[]{:S(2)}, u32[]{:S(2)}) collective-permute-start(s16[72,512]{1,0:T(8,128)(2,1)S(1)} %sum_kernel.2.refs_0_), channel_id=1, source_target_pairs={{0,16},{4,20},{8,24},{12,28},{16,0},{20,4},{24,8},{28,12},{1,17},{... | collective-permute-start | bytes 221192 | tf_op jit(solution)/shard_map/ppermute | solution.py:348
  32.8 6.8 %collective-permute-start.15 = (s16[72,512]{1,0:T(8,128)(2,1)S(1)}, s16[72,512]{1,0:T(8,128)(2,1)S(1)}, u32[]{:S(2)}, u32[]{:S(2)}) collective-permute-start(s16[72,512]{1,0:T(8,128)(2,1)S(1)} %sum_kernel.2.refs_0_), channel_id=1, source_target_pairs={{0,8},{4,12},{8,0},{12,4},{16,24},{20,28},{24,16},{28,20},{1,9},{5... | collective-permute-start | bytes 221192 | tf_op jit(solution)/shard_map/ppermute | solution.py:348
  33.8 10.6 %collective-permute-start.16 = (s16[1056,128]{1,0:T(8,128)(2,1)S(1)}, s16[1056,128]{1,0:T(8,128)(2,1)S(1)}, u32[]{:S(2)}, u32[]{:S(2)}) collective-permute-start(s16[1056,128]{1,0:T(8,128)(2,1)S(1)} %get-tuple-element.62), channel_id=1, source_target_pairs={{0,8},{4,12},{8,0},{12,4},{16,24},{20,28},{24,16},{28,20},{1,9},{5... | collective-permute-start | bytes 811016 | tf_op jit(solution)/shard_map/ppermute | solution.py:348
  39.7 5.4 %collective-permute-start.17 = (s16[72,512]{1,0:T(8,128)(2,1)S(1)}, s16[72,512]{1,0:T(8,128)(2,1)S(1)}, u32[]{:S(2)}, u32[]{:S(2)}) collective-permute-start(s16[72,512]{1,0:T(8,128)(2,1)S(1)} %sum_kernel.3.refs_0_), channel_id=1, source_target_pairs={{0,3},{1,2},{2,1},{3,0},{4,7},{5,6},{6,5},{7,4},{8,11},{9,10},{10,... | collective-permute-start | bytes 221192 | tf_op jit(solution)/shard_map/ppermute | solution.py:348
  40.7 5.1 %collective-permute-start.18 = (s16[72,512]{1,0:T(8,128)(2,1)S(1)}, s16[72,512]{1,0:T(8,128)(2,1)S(1)}, u32[]{:S(2)}, u32[]{:S(2)}) collective-permute-start(s16[72,512]{1,0:T(8,128)(2,1)S(1)} %sum_kernel.3.refs_0_), channel_id=1, source_target_pairs={{0,2},{1,3},{2,0},{3,1},{4,6},{5,7},{6,4},{7,5},{8,10},{9,11},{10,... | collective-permute-start | bytes 221192 | tf_op jit(solution)/shard_map/ppermute | solution.py:348
  41.8 4.4 %collective-permute-start.19 = (s16[72,512]{1,0:T(8,128)(2,1)S(1)}, s16[72,512]{1,0:T(8,128)(2,1)S(1)}, u32[]{:S(2)}, u32[]{:S(2)}) collective-permute-start(s16[72,512]{1,0:T(8,128)(2,1)S(1)} %sum_kernel.3.refs_0_), channel_id=1, source_target_pairs={{0,1},{1,0},{2,3},{3,2},{4,5},{5,4},{6,7},{7,6},{8,9},{9,8},{10,11... | collective-permute-start | bytes 221192 | tf_op jit(solution)/shard_map/ppermute | solution.py:348
  46.2 1.7 %collective-permute-start.20 = (s16[320,512]{1,0:T(8,128)(2,1)S(1)}, s16[320,512]{1,0:T(8,128)(2,1)S(1)}, u32[]{:S(2)}, u32[]{:S(2)}) collective-permute-start(s16[320,512]{1,0:T(8,128)(2,1)S(1)} %join_kernel.1.own_ref), channel_id=1, source_target_pairs={{0,4},{4,0},{8,12},{12,8},{16,20},{20,16},{24,28},{28,24},{1,5},{5... | collective-permute-start | bytes 983048 | tf_op jit(solution)/shard_map/ppermute | solution.py:348
  46.3 9.8 %collective-permute-start.21 = (s16[528,128]{1,0:T(8,128)(2,1)S(1)}, s16[528,128]{1,0:T(8,128)(2,1)S(1)}, u32[]{:S(2)}, u32[]{:S(2)}) collective-permute-start(s16[528,128]{1,0:T(8,128)(2,1)S(1)} %get-tuple-element.65), channel_id=1, source_target_pairs={{0,16},{4,20},{8,24},{12,28},{16,0},{20,4},{24,8},{28,12},{1,17},{... | collective-permute-start | bytes 405512 | tf_op jit(solution)/shard_map/ppermute | solution.py:348

commit v19 on v17

--- a/solution.py
+++ b/solution.py
@@ -36,6 +36,10 @@
 
 def dot(a, b):
     return jnp.dot(a, b, preferred_element_type=F32)
+
+
+def contract(a, b, dims):
+    return lax.dot_general(a, b, (dims, ((), ())), preferred_element_type=F32)
 
 
 def product(a, b):
@@ -108,9 +112,11 @@
     ]
     for copy in copies:
         copy.start()
+    same = lax.broadcasted_iota(jnp.int32, (half, half), 0) == lax.broadcasted_iota(jnp.int32, (half, half), 1)
+    one = jnp.where(same, F32(1.0), F32(0.0)).astype(BF16)
     for i, out_ref in enumerate((upper_ref, lower_ref)):
         copies[i].wait()
-        out_ref[...] = solves_copy[i].T
+        out_ref[...] = contract(one, solves_copy[i], ((1,), (1,))).astype(BF16)
 
 
 def order_of(rows):

time: 57.5 us -> 57.8 us (level)
  no operation moved by 1% of the time
where the time goes in v19:
time: 57.8 us; the launch traced here: 57.6 us
  starting transfers between devices  23.7 us (41%)
  Pallas kernels  19.1 us (33%)
  waiting for transfers between devices  14 us (24%)
  between operations  0.8 us (1%)
    ppermute x22, starting transfers between devices, swap(): return lax.ppermute(x, axis, [(i, i ^ bit) for i in range(count)])  23.7 us
    pallas_call x16, Pallas kernels, call(): pl.pallas_call(kernel, name=getattr(kernel, 'func', kernel).__name__, out...  19.1 us
    ppermute x22, waiting for transfers between devices, swap(): return lax.ppermute(x, axis, [(i, i ^ bit) for i in range(count)])  14 us
  transfers between devices with their start and end apart: 22, of which 16 were waited for; matrix products, arithmetic and copies ran while one was open for 0% of the time, Pallas kernels for 28%

profile of v19, /device:TPU:0, one launch (start us, length us, event | category | flops | bytes accessed | tf_op | source)
XLA Modules:
  0.0 57.6 jit_solution(14139603477542872923)
XLA Ops:
  0.6 1.5 %turn_kernel.1 = (bf16[256,384]{1,0:T(8,128)(2,1)S(1)}, bf16[256,384]{1,0:T(8,128)(2,1)S(1)}) custom-call(bf16[384,512]{1,0:T(8,128)(2,1)} %bitcast.7), custom_call_target="tpu_custom_call" | custom-call | bytes 1024 | tf_op jit(solution)/shard_map/turn_kernel/pallas_call | solution.py:335
  2.1 3.0 %collective-permute-start.2 = (bf16[256,384]{1,0:T(8,128)(2,1)S(1)}, bf16[256,384]{1,0:T(8,128)(2,1)S(1)}, u32[]{:S(2)}, u32[]{:S(2)}) collective-permute-start(bf16[256,384]{1,0:T(8,128)(2,1)S(1)} %get-tuple-element.39.refs_0_), channel_id=1, source_target_pairs={{0,2},{1,3},{2,0},{3,1},{4,6},{5,7},{6,4},{7,5},{8,10},{9,11},{10,... | collective-permute-start | bytes 589832 | tf_op jit(solution)/shard_map/ppermute | solution.py:350
  5.1 1.5 %collective-permute-start.1 = (bf16[256,384]{1,0:T(8,128)(2,1)S(1)}, bf16[256,384]{1,0:T(8,128)(2,1)S(1)}, u32[]{:S(2)}, u32[]{:S(2)}) collective-permute-start(bf16[256,384]{1,0:T(8,128)(2,1)S(1)} %get-tuple-element.40.refs_1_), channel_id=1, source_target_pairs={{0,1},{1,0},{2,3},{3,2},{4,5},{5,4},{6,7},{7,6},{8,9},{9,8},{10,11... | collective-permute-start | bytes 589832 | tf_op jit(solution)/shard_map/ppermute | solution.py:350
  6.6 0.5 collective-permute-start
  7.2 0.1 collective-permute-start.3
  7.2 1.8 %pick_kernel.1 = (bf16[1536,512]{1,0:T(8,128)(2,1)S(1)}, bf16[384,512]{1,0:T(8,128)(2,1)S(1)}, f32[8,512]{1,0:T(8,128)S(1)}, bf16[1024,512]{1,0:T(8,128)(2,1)S(1...) custom-call(s32[1,512]{1,0:T(1,128)} %bitcast.8, f32[1,128]{1,0:T(1,128)} %bitcast.9, bf16[1536,1024]{1,0:T(8,128)(2,1)} %bitcast.4), custom_call_target="tpu_custom_call" | custom-call | bytes 1024 | tf_op jit(solution)/shard_map/pick_kernel/pallas_call | solution.py:335
  9.1 1.8 %collective-permute-done.2.refs_4_ = bf16[256,384]{1,0:T(8,128)(2,1)S(1)} collective-permute-done((bf16[256,384]{1,0:T(8,128)(2,1)S(1)}, bf16[256,384]{1,0:T(8,128)(2,1)S(1)}, u32[]{:S(2)}, u32[]{:S(2)}) %collective-permute-start.2) | collective-permute-done | bytes 196640 | tf_op jit(solution)/shard_map/ppermute | solution.py:350
  10.9 2.0 %collective-permute-start.5 = (bf16[256,384]{1,0:T(8,128)(2,1)S(1)}, bf16[256,384]{1,0:T(8,128)(2,1)S(1)}, u32[]{:S(2)}, u32[]{:S(2)}) collective-permute-start(bf16[256,384]{1,0:T(8,128)(2,1)S(1)} %collective-permute-done.2.refs_4_), channel_id=1, source_target_pairs={{0,1},{1,0},{2,3},{3,2},{4,5},{5,4},{6,7},{7,6},{8,9},{9,8},{10,11... | collective-permute-start | bytes 589832 | tf_op jit(solution)/shard_map/ppermute | solution.py:350
  12.9 0.1 collective-permute-done.1.refs_3_
  13.0 1.5 %collective-permute-start.6 = (bf16[256,384]{1,0:T(8,128)(2,1)S(1)}, bf16[256,384]{1,0:T(8,128)(2,1)S(1)}, u32[]{:S(2)}, u32[]{:S(2)}) collective-permute-start(bf16[256,384]{1,0:T(8,128)(2,1)S(1)} %collective-permute-done.1.refs_3_), channel_id=1, source_target_pairs={{0,2},{1,3},{2,0},{3,1},{4,6},{5,7},{6,4},{7,5},{8,10},{9,11},{10,... | collective-permute-start | bytes 589832 | tf_op jit(solution)/shard_map/ppermute | solution.py:350
  14.4 2.9 %rest_kernel.1.chosen_ref = bf16[1536,512]{1,0:T(8,128)(2,1)S(1)} custom-call(bf16[1536,512]{1,0:T(8,128)(2,1)S(1)} %get-tuple-element.36.chosen_in, bf16[1024,512]{1,0:T(8,128)(2,1)S(1)} %get-tuple-element.37.one_ref, bf16[1536,1024]{1,0:T(8,128)(2,1)} %bitcast.5), custom_call_target="tpu_custom_call", output_to_operand_aliasing={{}: (0, {})} | custom-call | bytes 1024 | tf_op jit(solution)/shard_map/rest_kernel/pallas_call | solution.py:335
  17.3 0.0 collective-permute-done.refs_2_
  17.3 0.0 collective-permute-done.3.refs_5_
  17.3 1.2 %early_kernel.1 = (bf16[512,1536]{1,0:T(8,128)(2,1)S(1)}, f32[256,512]{1,0:T(8,128)S(1)}, f32[264,512]{1,0:T(8,128)S(1)}) custom-call(bf16[1536,512]{1,0:T(8,128)(2,1)S(1)} %rest_kernel.1.chosen_ref, f32[8,512]{1,0:T(8,128)S(1)} %get-tuple-element.38.entry_ref, bf16[256,384]{1,0:T(8,128)(2,1)S(1)} %get-tuple-element.39.refs_0_, ...), custom_call_target="tpu_custom_call" | custom-call | bytes 1024 | tf_op jit(solution)/shard_map/early_kernel/pallas_call | solution.py:335
  18.5 0.1 collective-permute-start.4
  18.6 0.5 collective-permute-start.8
  19.1 0.8 %collective-permute-done.5.refs_0_.upper_ref = bf16[256,384]{1,0:T(8,128)(2,1)S(1)} collective-permute-done((bf16[256,384]{1,0:T(8,128)(2,1)S(1)}, bf16[256,384]{1,0:T(8,128)(2,1)S(1)}, u32[]{:S(2)}, u32[]{:S(2)}) %collective-permute-start.5) | collective-permute-done | bytes 196640 | tf_op jit(solution)/shard_map/ppermute | solution.py:350
  19.9 0.0 collective-permute-done.6.refs_1_.lower_ref
  20.0 0.1 collective-permute-start.7
  20.1 0.5 collective-permute-done.4.got_ref
  20.5 0.0 copy-start
  20.5 0.4 keep_kernel.1
  20.9 0.6 collective-permute-done.7.refs_0_
  21.5 0.0 collective-permute-done.8.refs_1_
  21.5 0.5 pair_kernel.1
  22.0 1.5 %collective-permute-start.10 = (s16[72,512]{1,0:T(8,128)(2,1)S(1)}, s16[72,512]{1,0:T(8,128)(2,1)S(1)}, u32[]{:S(2)}, u32[]{:S(2)}) collective-permute-start(s16[72,512]{1,0:T(8,128)(2,1)S(1)} %get-tuple-element.58), channel_id=1, source_target_pairs={{0,3},{1,2},{2,1},{3,0},{4,7},{5,6},{6,5},{7,4},{8,11},{9,10},{10,... | collective-permute-start | bytes 221192 | tf_op jit(solution)/shard_map/ppermute | solution.py:350
  23.5 1.5 %collective-permute-start.11 = (s16[72,512]{1,0:T(8,128)(2,1)S(1)}, s16[72,512]{1,0:T(8,128)(2,1)S(1)}, u32[]{:S(2)}, u32[]{:S(2)}) collective-permute-start(s16[72,512]{1,0:T(8,128)(2,1)S(1)} %get-tuple-element.59), channel_id=1, source_target_pairs={{0,2},{1,3},{2,0},{3,1},{4,6},{5,7},{6,4},{7,5},{8,10},{9,11},{10,... | collective-permute-start | bytes 221192 | tf_op jit(solution)/shard_map/ppermute | solution.py:350
  25.0 0.5 collective-permute-start.9
  25.5 0.0 copy-done
  25.5 1.8 %schur_kernel.1 = (f32[2048,128]{1,0:T(8,128)S(1)}, f32[2048,128]{1,0:T(8,128)S(1)}) custom-call(s32[1,512]{1,0:T(1,128)S(1)} %get-tuple-element.51.panel_ref, f32[1,128]{1,0:T(1,128)S(1)} %get-tuple-element.52.own_diagonal_ref, bf16[1536,1024]{1,0:T(8,128)(2,1)S(1)} %bitcast.6, bf16[512,1536]{1,0:T(8,128)(2,1)S(1)} %get-tuple-element.54.turned_ref), custom_call_target="tpu_custom_call" | custom-call | flops 2300000000 | bytes 1024 | tf_op jit(solution)/shard_map/schur_kernel/pallas_call | solution.py:335
  27.3 0.1 collective-permute-start.12
  27.4 0.1 collective-permute-done.10.refs_2_
  27.5 1.3 %collective-permute-done.11.refs_3_ = s16[72,512]{1,0:T(8,128)(2,1)S(1)} collective-permute-done((s16[72,512]{1,0:T(8,128)(2,1)S(1)}, s16[72,512]{1,0:T(8,128)(2,1)S(1)}, u32[]{:S(2)}, u32[]{:S(2)}) %collective-permute-start.11) | collective-permute-done | bytes 73760 | tf_op jit(solution)/shard_map/ppermute | solution.py:350
  28.8 0.5 collective-permute-done.9.refs_1_
  29.3 0.1 sum_kernel.2.refs_0_
  29.5 3.7 %collective-permute-start.13 = (s16[72,512]{1,0:T(8,128)(2,1)S(1)}, s16[72,512]{1,0:T(8,128)(2,1)S(1)}, u32[]{:S(2)}, u32[]{:S(2)}) collective-permute-start(s16[72,512]{1,0:T(8,128)(2,1)S(1)} %sum_kernel.2.refs_0_), channel_id=1, source_target_pairs={{0,24},{4,28},{8,16},{12,20},{16,8},{20,12},{24,0},{28,4},{1,25},{... | collective-permute-start | bytes 221192 | tf_op jit(solution)/shard_map/ppermute | solution.py:350
  33.1 0.0 collective-permute-start.14
  33.1 0.8 %collective-permute-start.15 = (s16[72,512]{1,0:T(8,128)(2,1)S(1)}, s16[72,512]{1,0:T(8,128)(2,1)S(1)}, u32[]{:S(2)}, u32[]{:S(2)}) collective-permute-start(s16[72,512]{1,0:T(8,128)(2,1)S(1)} %sum_kernel.2.refs_0_), channel_id=1, source_target_pairs={{0,8},{4,12},{8,0},{12,4},{16,24},{20,28},{24,16},{28,20},{1,9},{5... | collective-permute-start | bytes 221192 | tf_op jit(solution)/shard_map/ppermute | solution.py:350
  33.9 0.0 collective-permute-done.12.got_ref
  33.9 0.2 bulk_pair_kernel.1
  34.1 1.3 %collective-permute-start.16 = (s16[1056,128]{1,0:T(8,128)(2,1)S(1)}, s16[1056,128]{1,0:T(8,128)(2,1)S(1)}, u32[]{:S(2)}, u32[]{:S(2)}) collective-permute-start(s16[1056,128]{1,0:T(8,128)(2,1)S(1)} %get-tuple-element.62), channel_id=1, source_target_pairs={{0,8},{4,12},{8,0},{12,4},{16,24},{20,28},{24,16},{28,20},{1,9},{5... | collective-permute-start | bytes 811016 | tf_op jit(solution)/shard_map/ppermute | solution.py:350
  35.4 1.2 %collective-permute-done.13.refs_1_ = s16[72,512]{1,0:T(8,128)(2,1)S(1)} collective-permute-done((s16[72,512]{1,0:T(8,128)(2,1)S(1)}, s16[72,512]{1,0:T(8,128)(2,1)S(1)}, u32[]{:S(2)}, u32[]{:S(2)}) %collective-permute-start.13) | collective-permute-done | bytes 73760 | tf_op jit(solution)/shard_map/ppermute | solution.py:350
  36.6 2.5 %collective-permute-done.14.refs_2_ = s16[72,512]{1,0:T(8,128)(2,1)S(1)} collective-permute-done((s16[72,512]{1,0:T(8,128)(2,1)S(1)}, s16[72,512]{1,0:T(8,128)(2,1)S(1)}, u32[]{:S(2)}, u32[]{:S(2)}) %collective-permute-start.14) | collective-permute-done | bytes 73760 | tf_op jit(solution)/shard_map/ppermute | solution.py:350
  39.1 0.8 %collective-permute-done.15.refs_3_ = s16[72,512]{1,0:T(8,128)(2,1)S(1)} collective-permute-done((s16[72,512]{1,0:T(8,128)(2,1)S(1)}, s16[72,512]{1,0:T(8,128)(2,1)S(1)}, u32[]{:S(2)}, u32[]{:S(2)}) %collective-permute-start.15) | collective-permute-done | bytes 73760 | tf_op jit(solution)/shard_map/ppermute | solution.py:350
  39.9 0.1 sum_kernel.3.refs_0_
  40.1 1.0 %collective-permute-start.17 = (s16[72,512]{1,0:T(8,128)(2,1)S(1)}, s16[72,512]{1,0:T(8,128)(2,1)S(1)}, u32[]{:S(2)}, u32[]{:S(2)}) collective-permute-start(s16[72,512]{1,0:T(8,128)(2,1)S(1)} %sum_kernel.3.refs_0_), channel_id=1, source_target_pairs={{0,3},{1,2},{2,1},{3,0},{4,7},{5,6},{6,5},{7,4},{8,11},{9,10},{10,... | collective-permute-start | bytes 221192 | tf_op jit(solution)/shard_map/ppermute | solution.py:350
  41.0 1.1 %collective-permute-start.18 = (s16[72,512]{1,0:T(8,128)(2,1)S(1)}, s16[72,512]{1,0:T(8,128)(2,1)S(1)}, u32[]{:S(2)}, u32[]{:S(2)}) collective-permute-start(s16[72,512]{1,0:T(8,128)(2,1)S(1)} %sum_kernel.3.refs_0_), channel_id=1, source_target_pairs={{0,2},{1,3},{2,0},{3,1},{4,6},{5,7},{6,4},{7,5},{8,10},{9,11},{10,... | collective-permute-start | bytes 221192 | tf_op jit(solution)/shard_map/ppermute | solution.py:350
  42.1 1.5 %collective-permute-start.19 = (s16[72,512]{1,0:T(8,128)(2,1)S(1)}, s16[72,512]{1,0:T(8,128)(2,1)S(1)}, u32[]{:S(2)}, u32[]{:S(2)}) collective-permute-start(s16[72,512]{1,0:T(8,128)(2,1)S(1)} %sum_kernel.3.refs_0_), channel_id=1, source_target_pairs={{0,1},{1,0},{2,3},{3,2},{4,5},{5,4},{6,7},{7,6},{8,9},{9,8},{10,11... | collective-permute-start | bytes 221192 | tf_op jit(solution)/shard_map/ppermute | solution.py:350
  43.6 1.1 %collective-permute-done.16.got_ref = s16[1056,128]{1,0:T(8,128)(2,1)S(1)} collective-permute-done((s16[1056,128]{1,0:T(8,128)(2,1)S(1)}, s16[1056,128]{1,0:T(8,128)(2,1)S(1)}, u32[]{:S(2)}, u32[]{:S(2)}) %collective-permute-start.16) | collective-permute-done | bytes 270368 | tf_op jit(solution)/shard_map/ppermute | solution.py:350
  44.7 0.2 bulk_sum_kernel.1
  44.9 0.6 %collective-permute-done.17.refs_1_ = s16[72,512]{1,0:T(8,128)(2,1)S(1)} collective-permute-done((s16[72,512]{1,0:T(8,128)(2,1)S(1)}, s16[72,512]{1,0:T(8,128)(2,1)S(1)}, u32[]{:S(2)}, u32[]{:S(2)}) %collective-permute-start.17) | collective-permute-done | bytes 73760 | tf_op jit(solution)/shard_map/ppermute | solution.py:350
  45.5 0.7 %collective-permute-done.18.refs_2_ = s16[72,512]{1,0:T(8,128)(2,1)S(1)} collective-permute-done((s16[72,512]{1,0:T(8,128)(2,1)S(1)}, s16[72,512]{1,0:T(8,128)(2,1)S(1)}, u32[]{:S(2)}, u32[]{:S(2)}) %collective-permute-start.18) | collective-permute-done | bytes 73760 | tf_op jit(solution)/shard_map/ppermute | solution.py:350
  46.2 0.3 collective-permute-done.19.refs_3_
  46.5 0.1 collective-permute-start.20
  46.6 1.4 %collective-permute-start.21 = (s16[528,128]{1,0:T(8,128)(2,1)S(1)}, s16[528,128]{1,0:T(8,128)(2,1)S(1)}, u32[]{:S(2)}, u32[]{:S(2)}) collective-permute-start(s16[528,128]{1,0:T(8,128)(2,1)S(1)} %get-tuple-element.65), channel_id=1, source_target_pairs={{0,16},{4,20},{8,24},{12,28},{16,0},{20,4},{24,8},{28,12},{1,17},{... | collective-permute-start | bytes 405512 | tf_op jit(solution)/shard_map/ppermute | solution.py:350
  48.0 0.2 own_kernel.1.half_ref
  48.2 0.0 collective-permute-done.20.other_ref
  48.2 7.0 %newton_kernel.1 = (f32[256,256]{1,0:T(8,128)S(1)}, f32[256,512]{1,0:T(8,128)S(1)}) custom-call(f32[256,512]{1,0:T(8,128)S(1)} %own_kernel.1.half_ref, s16[320,512]{1,0:T(8,128)(2,1)S(1)} %collective-permute-done.20.other_ref), custom_call_target="tpu_custom_call" | custom-call | bytes 1024 | tf_op jit(solution)/shard_map/newton_kernel/pallas_call | solution.py:335
  55.2 1.2 %collective-permute-done.21.refs_0_ = s16[528,128]{1,0:T(8,128)(2,1)S(1)} collective-permute-done((s16[528,128]{1,0:T(8,128)(2,1)S(1)}, s16[528,128]{1,0:T(8,128)(2,1)S(1)}, u32[]{:S(2)}, u32[]{:S(2)}) %collective-permute-start.21) | collective-permute-done | bytes 135200 | tf_op jit(solution)/shard_map/ppermute | solution.py:350
  56.4 1.2 %factor_kernel.1 = (f32[128,1,256]{2,1,0:T(1,128)}, f32[128,1,256]{2,1,0:T(1,128)}) custom-call(f32[256,256]{1,0:T(8,128)S(1)} %get-tuple-element.67.inverse_first_ref, f32[256,512]{1,0:T(8,128)S(1)} %get-tuple-element.68.inverse_second_ref, f32[512,128]{1,0:T(8,128)S(1)} %get-tuple-element.69.rows_ref, s16[528,128]{1,0:T(8,128)(2,1)S(1)} %collective-permute-done.21.refs_0_), custom_call_target="tpu_custom_call" | custom-call | bytes 1024 | tf_op jit(solution)/shard_map/factor_kernel/pallas_call | solution.py:335
  (2 shorter events, 0.1 us)
Async XLA Ops:
  2.1 8.8 %collective-permute-start.2 = (bf16[256,384]{1,0:T(8,128)(2,1)S(1)}, bf16[256,384]{1,0:T(8,128)(2,1)S(1)}, u32[]{:S(2)}, u32[]{:S(2)}) collective-permute-start(bf16[256,384]{1,0:T(8,128)(2,1)S(1)} %get-tuple-element.39.refs_0_), channel_id=1, source_target_pairs={{0,2},{1,3},{2,0},{3,1},{4,6},{5,7},{6,4},{7,5},{8,10},{9,11},{10,... | collective-permute-start | bytes 589832 | tf_op jit(solution)/shard_map/ppermute | solution.py:350
  5.1 7.8 %collective-permute-start.1 = (bf16[256,384]{1,0:T(8,128)(2,1)S(1)}, bf16[256,384]{1,0:T(8,128)(2,1)S(1)}, u32[]{:S(2)}, u32[]{:S(2)}) collective-permute-start(bf16[256,384]{1,0:T(8,128)(2,1)S(1)} %get-tuple-element.40.refs_1_), channel_id=1, source_target_pairs={{0,1},{1,0},{2,3},{3,2},{4,5},{5,4},{6,7},{7,6},{8,9},{9,8},{10,11... | collective-permute-start | bytes 589832 | tf_op jit(solution)/shard_map/ppermute | solution.py:350
  6.6 10.7 %collective-permute-start = (bf16[256,384]{1,0:T(8,128)(2,1)S(1)}, bf16[256,384]{1,0:T(8,128)(2,1)S(1)}, u32[]{:S(2)}, u32[]{:S(2)}) collective-permute-start(bf16[256,384]{1,0:T(8,128)(2,1)S(1)} %get-tuple-element.39.refs_0_), channel_id=1, source_target_pairs={{0,1},{1,0},{2,3},{3,2},{4,5},{5,4},{6,7},{7,6},{8,9},{9,8},{10,11... | collective-permute-start | bytes 589832 | tf_op jit(solution)/shard_map/ppermute | solution.py:350
  7.2 10.2 %collective-permute-start.3 = (bf16[256,384]{1,0:T(8,128)(2,1)S(1)}, bf16[256,384]{1,0:T(8,128)(2,1)S(1)}, u32[]{:S(2)}, u32[]{:S(2)}) collective-permute-start(bf16[256,384]{1,0:T(8,128)(2,1)S(1)} %get-tuple-element.40.refs_1_), channel_id=1, source_target_pairs={{0,2},{1,3},{2,0},{3,1},{4,6},{5,7},{6,4},{7,5},{8,10},{9,11},{10,... | collective-permute-start | bytes 589832 | tf_op jit(solution)/shard_map/ppermute | solution.py:350
  10.9 9.1 %collective-permute-start.5 = (bf16[256,384]{1,0:T(8,128)(2,1)S(1)}, bf16[256,384]{1,0:T(8,128)(2,1)S(1)}, u32[]{:S(2)}, u32[]{:S(2)}) collective-permute-start(bf16[256,384]{1,0:T(8,128)(2,1)S(1)} %collective-permute-done.2.refs_4_), channel_id=1, source_target_pairs={{0,1},{1,0},{2,3},{3,2},{4,5},{5,4},{6,7},{7,6},{8,9},{9,8},{10,11... | collective-permute-start | bytes 589832 | tf_op jit(solution)/shard_map/ppermute | solution.py:350
  13.0 7.0 %collective-permute-start.6 = (bf16[256,384]{1,0:T(8,128)(2,1)S(1)}, bf16[256,384]{1,0:T(8,128)(2,1)S(1)}, u32[]{:S(2)}, u32[]{:S(2)}) collective-permute-start(bf16[256,384]{1,0:T(8,128)(2,1)S(1)} %collective-permute-done.1.refs_3_), channel_id=1, source_target_pairs={{0,2},{1,3},{2,0},{3,1},{4,6},{5,7},{6,4},{7,5},{8,10},{9,11},{10,... | collective-permute-start | bytes 589832 | tf_op jit(solution)/shard_map/ppermute | solution.py:350
  18.5 2.0 %collective-permute-start.4 = (f32[264,512]{1,0:T(8,128)S(1)}, f32[264,512]{1,0:T(8,128)S(1)}, u32[]{:S(2)}, u32[]{:S(2)}) collective-permute-start(f32[264,512]{1,0:T(8,128)S(1)} %get-tuple-element.43), channel_id=1, source_target_pairs={{0,4},{4,0},{8,12},{12,8},{16,20},{20,16},{24,28},{28,24},{1,5},{5... | collective-permute-start | bytes 1622024 | tf_op jit(solution)/shard_map/ppermute | solution.py:350
  18.6 2.9 %collective-permute-start.8 = (bf16[384,512]{1,0:T(8,128)(2,1)S(1)}, bf16[384,512]{1,0:T(8,128)(2,1)S(1)}, u32[]{:S(2)}, u32[]{:S(2)}) collective-permute-start(bf16[384,512]{1,0:T(8,128)(2,1)S(1)} %get-tuple-element.49.refs_2_), channel_id=1, source_target_pairs={{0,4},{4,0},{8,12},{12,8},{16,20},{20,16},{24,28},{28,24},{1,5},{5... | collective-permute-start | bytes 1179656 | tf_op jit(solution)/shard_map/ppermute | solution.py:350
  20.0 1.5 %collective-permute-start.7 = (bf16[256,384]{1,0:T(8,128)(2,1)S(1)}, bf16[256,384]{1,0:T(8,128)(2,1)S(1)}, u32[]{:S(2)}, u32[]{:S(2)}) collective-permute-start(bf16[256,384]{1,0:T(8,128)(2,1)S(1)} %select_kernel.1), channel_id=1, source_target_pairs={{0,4},{4,0},{8,12},{12,8},{16,20},{20,16},{24,28},{28,24},{1,5},{5... | collective-permute-start | bytes 589832 | tf_op jit(solution)/shard_map/ppermute | solution.py:350
  20.5 5.0 %copy-start = (bf16[1,1536,1024]{2,1,0:T(8,128)(2,1)S(1)}, bf16[1,1536,1024]{2,1,0:T(8,128)(2,1)}, u32[]{:S(2)}) copy-start(bf16[1,1536,1024]{2,1,0:T(8,128)(2,1)} %param.4) | copy-start | bytes 9437188
  22.0 5.6 %collective-permute-start.10 = (s16[72,512]{1,0:T(8,128)(2,1)S(1)}, s16[72,512]{1,0:T(8,128)(2,1)S(1)}, u32[]{:S(2)}, u32[]{:S(2)}) collective-permute-start(s16[72,512]{1,0:T(8,128)(2,1)S(1)} %get-tuple-element.58), channel_id=1, source_target_pairs={{0,3},{1,2},{2,1},{3,0},{4,7},{5,6},{6,5},{7,4},{8,11},{9,10},{10,... | collective-permute-start | bytes 221192 | tf_op jit(solution)/shard_map/ppermute | solution.py:350
  23.5 5.3 %collective-permute-start.11 = (s16[72,512]{1,0:T(8,128)(2,1)S(1)}, s16[72,512]{1,0:T(8,128)(2,1)S(1)}, u32[]{:S(2)}, u32[]{:S(2)}) collective-permute-start(s16[72,512]{1,0:T(8,128)(2,1)S(1)} %get-tuple-element.59), channel_id=1, source_target_pairs={{0,2},{1,3},{2,0},{3,1},{4,6},{5,7},{6,4},{7,5},{8,10},{9,11},{10,... | collective-permute-start | bytes 221192 | tf_op jit(solution)/shard_map/ppermute | solution.py:350
  25.0 4.4 %collective-permute-start.9 = (s16[72,512]{1,0:T(8,128)(2,1)S(1)}, s16[72,512]{1,0:T(8,128)(2,1)S(1)}, u32[]{:S(2)}, u32[]{:S(2)}) collective-permute-start(s16[72,512]{1,0:T(8,128)(2,1)S(1)} %get-tuple-element.57), channel_id=1, source_target_pairs={{0,1},{1,0},{2,3},{3,2},{4,5},{5,4},{6,7},{7,6},{8,9},{9,8},{10,11... | collective-permute-start | bytes 221192 | tf_op jit(solution)/shard_map/ppermute | solution.py:350
  27.3 6.6 %collective-permute-start.12 = (f32[2048,128]{1,0:T(8,128)S(1)}, f32[2048,128]{1,0:T(8,128)S(1)}, u32[]{:S(2)}, u32[]{:S(2)}) collective-permute-start(f32[2048,128]{1,0:T(8,128)S(1)} %get-tuple-element.61), channel_id=1, source_target_pairs={{0,4},{4,0},{8,12},{12,8},{16,20},{20,16},{24,28},{28,24},{1,5},{5... | collective-permute-start | bytes 3145736 | tf_op jit(solution)/shard_map/ppermute | solution.py:350
  29.5 7.2 %collective-permute-start.13 = (s16[72,512]{1,0:T(8,128)(2,1)S(1)}, s16[72,512]{1,0:T(8,128)(2,1)S(1)}, u32[]{:S(2)}, u32[]{:S(2)}) collective-permute-start(s16[72,512]{1,0:T(8,128)(2,1)S(1)} %sum_kernel.2.refs_0_), channel_id=1, source_target_pairs={{0,24},{4,28},{8,16},{12,20},{16,8},{20,12},{24,0},{28,4},{1,25},{... | collective-permute-start | bytes 221192 | tf_op jit(solution)/shard_map/ppermute | solution.py:350
  33.1 5.9 %collective-permute-start.14 = (s16[72,512]{1,0:T(8,128)(2,1)S(1)}, s16[72,512]{1,0:T(8,128)(2,1)S(1)}, u32[]{:S(2)}, u32[]{:S(2)}) collective-permute-start(s16[72,512]{1,0:T(8,128)(2,1)S(1)} %sum_kernel.2.refs_0_), channel_id=1, source_target_pairs={{0,16},{4,20},{8,24},{12,28},{16,0},{20,4},{24,8},{28,12},{1,17},{... | collective-permute-start | bytes 221192 | tf_op jit(solution)/shard_map/ppermute | solution.py:350
  33.1 6.8 %collective-permute-start.15 = (s16[72,512]{1,0:T(8,128)(2,1)S(1)}, s16[72,512]{1,0:T(8,128)(2,1)S(1)}, u32[]{:S(2)}, u32[]{:S(2)}) collective-permute-start(s16[72,512]{1,0:T(8,128)(2,1)S(1)} %sum_kernel.2.refs_0_), channel_id=1, source_target_pairs={{0,8},{4,12},{8,0},{12,4},{16,24},{20,28},{24,16},{28,20},{1,9},{5... | collective-permute-start | bytes 221192 | tf_op jit(solution)/shard_map/ppermute | solution.py:350
  34.1 10.6 %collective-permute-start.16 = (s16[1056,128]{1,0:T(8,128)(2,1)S(1)}, s16[1056,128]{1,0:T(8,128)(2,1)S(1)}, u32[]{:S(2)}, u32[]{:S(2)}) collective-permute-start(s16[1056,128]{1,0:T(8,128)(2,1)S(1)} %get-tuple-element.62), channel_id=1, source_target_pairs={{0,8},{4,12},{8,0},{12,4},{16,24},{20,28},{24,16},{28,20},{1,9},{5... | collective-permute-start | bytes 811016 | tf_op jit(solution)/shard_map/ppermute | solution.py:350
  40.1 5.4 %collective-permute-start.17 = (s16[72,512]{1,0:T(8,128)(2,1)S(1)}, s16[72,512]{1,0:T(8,128)(2,1)S(1)}, u32[]{:S(2)}, u32[]{:S(2)}) collective-permute-start(s16[72,512]{1,0:T(8,128)(2,1)S(1)} %sum_kernel.3.refs_0_), channel_id=1, source_target_pairs={{0,3},{1,2},{2,1},{3,0},{4,7},{5,6},{6,5},{7,4},{8,11},{9,10},{10,... | collective-permute-start | bytes 221192 | tf_op jit(solution)/shard_map/ppermute | solution.py:350
  41.0 5.1 %collective-permute-start.18 = (s16[72,512]{1,0:T(8,128)(2,1)S(1)}, s16[72,512]{1,0:T(8,128)(2,1)S(1)}, u32[]{:S(2)}, u32[]{:S(2)}) collective-permute-start(s16[72,512]{1,0:T(8,128)(2,1)S(1)} %sum_kernel.3.refs_0_), channel_id=1, source_target_pairs={{0,2},{1,3},{2,0},{3,1},{4,6},{5,7},{6,4},{7,5},{8,10},{9,11},{10,... | collective-permute-start | bytes 221192 | tf_op jit(solution)/shard_map/ppermute | solution.py:350
  42.1 4.4 %collective-permute-start.19 = (s16[72,512]{1,0:T(8,128)(2,1)S(1)}, s16[72,512]{1,0:T(8,128)(2,1)S(1)}, u32[]{:S(2)}, u32[]{:S(2)}) collective-permute-start(s16[72,512]{1,0:T(8,128)(2,1)S(1)} %sum_kernel.3.refs_0_), channel_id=1, source_target_pairs={{0,1},{1,0},{2,3},{3,2},{4,5},{5,4},{6,7},{7,6},{8,9},{9,8},{10,11... | collective-permute-start | bytes 221192 | tf_op jit(solution)/shard_map/ppermute | solution.py:350
  46.5 1.7 %collective-permute-start.20 = (s16[320,512]{1,0:T(8,128)(2,1)S(1)}, s16[320,512]{1,0:T(8,128)(2,1)S(1)}, u32[]{:S(2)}, u32[]{:S(2)}) collective-permute-start(s16[320,512]{1,0:T(8,128)(2,1)S(1)} %join_kernel.1.own_ref), channel_id=1, source_target_pairs={{0,4},{4,0},{8,12},{12,8},{16,20},{20,16},{24,28},{28,24},{1,5},{5... | collective-permute-start | bytes 983048 | tf_op jit(solution)/shard_map/ppermute | solution.py:350
  46.6 9.8 %collective-permute-start.21 = (s16[528,128]{1,0:T(8,128)(2,1)S(1)}, s16[528,128]{1,0:T(8,128)(2,1)S(1)}, u32[]{:S(2)}, u32[]{:S(2)}) collective-permute-start(s16[528,128]{1,0:T(8,128)(2,1)S(1)} %get-tuple-element.65), channel_id=1, source_target_pairs={{0,16},{4,20},{8,24},{12,28},{16,0},{20,4},{24,8},{28,12},{1,17},{... | collective-permute-start | bytes 405512 | tf_op jit(solution)/shard_map/ppermute | solution.py:350

commit v20 on v17

--- a/solution.py
+++ b/solution.py
@@ -266,10 +266,10 @@
     place_pieces(row, 1 - core, other_ref, pivots_ref, rows, 0)
     both = newton_beside(pivots_ref[:half, :half], pivots_ref[:half, half:])
     inverse_first = both[:, :half]
-    inverse_ref[...] = inverse_first
+    inverse_ref[...] = left_of(inverse_first)
     corner = pivots_ref[half:, :half]
     pivot = pivots_ref[half:, half:] - product(corner, both[:, half:])
-    second_ref[...] = newton_beside(pivot, -product(corner, inverse_first))
+    second_ref[...] = left_of(newton_beside(pivot, -product(corner, inverse_first)))
 
 
 def schur_kernel(panel_ref, own_diagonal_ref, coupling_ref, turned_ref, keep_ref, send_ref):
@@ -317,8 +317,8 @@
     for ref in got:
         rows = rows + decode(ref, 0, panel, TAIL)[0]
     first, second = rows[:half], rows[half:]
-    first_out[...] = product(inverse_first_ref[...], first).T[:, None, :]
-    second_out[...] = product(inverse_second_ref[...], jnp.concatenate([second, first], axis=0)).T[:, None, :]
+    first_out[...] = dot(inverse_first_ref[...], right_of(first)).T[:, None, :]
+    second_out[...] = dot(inverse_second_ref[...], right_of(jnp.concatenate([second, first], axis=0))).T[:, None, :]
 
 
 def call(kernel, out_shape, *args, scratch=(), remain=0, micros=0.0, aliases=None):
@@ -470,7 +470,7 @@
         functools.partial(own_kernel, rows), shape((panel // 2, panel), F32), joined
     )
     inverse_first, inverse_second = call(
-        functools.partial(newton_kernel, rows), (shape((half, half), F32), shape((half, panel), F32)),
+        functools.partial(newton_kernel, rows), (shape((half, 3 * half), BF16), shape((half, 3 * panel), BF16)),
         own_half, other, scratch=[pltpu.VMEM((panel, panel), F32)],
     )
     out = jax.ShapeDtypeStruct((share, 1, half), F32)

time: 57.5 us -> 57.5 us (level)
  no operation moved by 1% of the time
where the time goes in v20:
time: 57.5 us; the launch traced here: 57.3 us
  starting transfers between devices  23.7 us (41%)
  Pallas kernels  18.7 us (33%)
  waiting for transfers between devices  14.1 us (25%)
  between operations  0.8 us (1%)
    ppermute x22, starting transfers between devices, swap(): return lax.ppermute(x, axis, [(i, i ^ bit) for i in range(count)])  23.7 us
    pallas_call x16, Pallas kernels, call(): pl.pallas_call(kernel, name=getattr(kernel, 'func', kernel).__name__, out...  18.7 us
    ppermute x22, waiting for transfers between devices, swap(): return lax.ppermute(x, axis, [(i, i ^ bit) for i in range(count)])  14.1 us
  transfers between devices with their start and end apart: 22, of which 16 were waited for; matrix products, arithmetic and copies ran while one was open for 0% of the time, Pallas kernels for 28%

profile of v20, /device:TPU:0, one launch (start us, length us, event | category | flops | bytes accessed | tf_op | source)
XLA Modules:
  0.0 57.3 jit_solution(12061787533632622311)
XLA Ops:
  0.6 1.2 %turn_kernel.1 = (bf16[256,384]{1,0:T(8,128)(2,1)S(1)}, bf16[256,384]{1,0:T(8,128)(2,1)S(1)}) custom-call(bf16[384,512]{1,0:T(8,128)(2,1)} %bitcast.7), custom_call_target="tpu_custom_call" | custom-call | bytes 1024 | tf_op jit(solution)/shard_map/turn_kernel/pallas_call | solution.py:329
  1.8 3.0 %collective-permute-start.2 = (bf16[256,384]{1,0:T(8,128)(2,1)S(1)}, bf16[256,384]{1,0:T(8,128)(2,1)S(1)}, u32[]{:S(2)}, u32[]{:S(2)}) collective-permute-start(bf16[256,384]{1,0:T(8,128)(2,1)S(1)} %get-tuple-element.39.refs_0_), channel_id=1, source_target_pairs={{0,2},{1,3},{2,0},{3,1},{4,6},{5,7},{6,4},{7,5},{8,10},{9,11},{10,... | collective-permute-start | bytes 589832 | tf_op jit(solution)/shard_map/ppermute | solution.py:344
  4.8 1.5 %collective-permute-start.1 = (bf16[256,384]{1,0:T(8,128)(2,1)S(1)}, bf16[256,384]{1,0:T(8,128)(2,1)S(1)}, u32[]{:S(2)}, u32[]{:S(2)}) collective-permute-start(bf16[256,384]{1,0:T(8,128)(2,1)S(1)} %get-tuple-element.40.refs_1_), channel_id=1, source_target_pairs={{0,1},{1,0},{2,3},{3,2},{4,5},{5,4},{6,7},{7,6},{8,9},{9,8},{10,11... | collective-permute-start | bytes 589832 | tf_op jit(solution)/shard_map/ppermute | solution.py:344
  6.3 0.5 collective-permute-start
  6.9 0.1 collective-permute-start.3
  6.9 1.8 %pick_kernel.1 = (bf16[1536,512]{1,0:T(8,128)(2,1)S(1)}, bf16[384,512]{1,0:T(8,128)(2,1)S(1)}, f32[8,512]{1,0:T(8,128)S(1)}, bf16[1024,512]{1,0:T(8,128)(2,1)S(1...) custom-call(s32[1,512]{1,0:T(1,128)} %bitcast.8, f32[1,128]{1,0:T(1,128)} %bitcast.9, bf16[1536,1024]{1,0:T(8,128)(2,1)} %bitcast.4), custom_call_target="tpu_custom_call" | custom-call | bytes 1024 | tf_op jit(solution)/shard_map/pick_kernel/pallas_call | solution.py:329
  8.8 1.8 %collective-permute-done.2.refs_4_ = bf16[256,384]{1,0:T(8,128)(2,1)S(1)} collective-permute-done((bf16[256,384]{1,0:T(8,128)(2,1)S(1)}, bf16[256,384]{1,0:T(8,128)(2,1)S(1)}, u32[]{:S(2)}, u32[]{:S(2)}) %collective-permute-start.2) | collective-permute-done | bytes 196640 | tf_op jit(solution)/shard_map/ppermute | solution.py:344
  10.6 2.0 %collective-permute-start.5 = (bf16[256,384]{1,0:T(8,128)(2,1)S(1)}, bf16[256,384]{1,0:T(8,128)(2,1)S(1)}, u32[]{:S(2)}, u32[]{:S(2)}) collective-permute-start(bf16[256,384]{1,0:T(8,128)(2,1)S(1)} %collective-permute-done.2.refs_4_), channel_id=1, source_target_pairs={{0,1},{1,0},{2,3},{3,2},{4,5},{5,4},{6,7},{7,6},{8,9},{9,8},{10,11... | collective-permute-start | bytes 589832 | tf_op jit(solution)/shard_map/ppermute | solution.py:344
  12.6 0.1 collective-permute-done.1.refs_3_
  12.7 1.5 %collective-permute-start.6 = (bf16[256,384]{1,0:T(8,128)(2,1)S(1)}, bf16[256,384]{1,0:T(8,128)(2,1)S(1)}, u32[]{:S(2)}, u32[]{:S(2)}) collective-permute-start(bf16[256,384]{1,0:T(8,128)(2,1)S(1)} %collective-permute-done.1.refs_3_), channel_id=1, source_target_pairs={{0,2},{1,3},{2,0},{3,1},{4,6},{5,7},{6,4},{7,5},{8,10},{9,11},{10,... | collective-permute-start | bytes 589832 | tf_op jit(solution)/shard_map/ppermute | solution.py:344
  14.1 2.9 %rest_kernel.1.chosen_ref = bf16[1536,512]{1,0:T(8,128)(2,1)S(1)} custom-call(bf16[1536,512]{1,0:T(8,128)(2,1)S(1)} %get-tuple-element.36.chosen_in, bf16[1024,512]{1,0:T(8,128)(2,1)S(1)} %get-tuple-element.37.one_ref, bf16[1536,1024]{1,0:T(8,128)(2,1)} %bitcast.5), custom_call_target="tpu_custom_call", output_to_operand_aliasing={{}: (0, {})} | custom-call | bytes 1024 | tf_op jit(solution)/shard_map/rest_kernel/pallas_call | solution.py:329
  17.0 0.0 collective-permute-done.refs_2_
  17.0 0.0 collective-permute-done.3.refs_5_
  17.0 1.2 %early_kernel.1 = (bf16[512,1536]{1,0:T(8,128)(2,1)S(1)}, f32[256,512]{1,0:T(8,128)S(1)}, f32[264,512]{1,0:T(8,128)S(1)}) custom-call(bf16[1536,512]{1,0:T(8,128)(2,1)S(1)} %rest_kernel.1.chosen_ref, f32[8,512]{1,0:T(8,128)S(1)} %get-tuple-element.38.entry_ref, bf16[256,384]{1,0:T(8,128)(2,1)S(1)} %get-tuple-element.39.refs_0_, ...), custom_call_target="tpu_custom_call" | custom-call | bytes 1024 | tf_op jit(solution)/shard_map/early_kernel/pallas_call | solution.py:329
  18.2 0.1 collective-permute-start.4
  18.3 0.5 collective-permute-start.8
  18.8 0.8 %collective-permute-done.5.refs_0_.upper_ref = bf16[256,384]{1,0:T(8,128)(2,1)S(1)} collective-permute-done((bf16[256,384]{1,0:T(8,128)(2,1)S(1)}, bf16[256,384]{1,0:T(8,128)(2,1)S(1)}, u32[]{:S(2)}, u32[]{:S(2)}) %collective-permute-start.5) | collective-permute-done | bytes 196640 | tf_op jit(solution)/shard_map/ppermute | solution.py:344
  19.6 0.0 collective-permute-done.6.refs_1_.lower_ref
  19.7 0.1 collective-permute-start.7
  19.7 0.5 collective-permute-done.4.got_ref
  20.2 0.0 copy-start
  20.2 0.4 keep_kernel.1
  20.6 0.6 %collective-permute-done.7.refs_0_ = bf16[256,384]{1,0:T(8,128)(2,1)S(1)} collective-permute-done((bf16[256,384]{1,0:T(8,128)(2,1)S(1)}, bf16[256,384]{1,0:T(8,128)(2,1)S(1)}, u32[]{:S(2)}, u32[]{:S(2)}) %collective-permute-start.7) | collective-permute-done | bytes 196640 | tf_op jit(solution)/shard_map/ppermute | solution.py:344
  21.2 0.0 collective-permute-done.8.refs_1_
  21.2 0.5 pair_kernel.1
  21.6 1.5 %collective-permute-start.10 = (s16[72,512]{1,0:T(8,128)(2,1)S(1)}, s16[72,512]{1,0:T(8,128)(2,1)S(1)}, u32[]{:S(2)}, u32[]{:S(2)}) collective-permute-start(s16[72,512]{1,0:T(8,128)(2,1)S(1)} %get-tuple-element.58), channel_id=1, source_target_pairs={{0,3},{1,2},{2,1},{3,0},{4,7},{5,6},{6,5},{7,4},{8,11},{9,10},{10,... | collective-permute-start | bytes 221192 | tf_op jit(solution)/shard_map/ppermute | solution.py:344
  23.1 1.5 %collective-permute-start.11 = (s16[72,512]{1,0:T(8,128)(2,1)S(1)}, s16[72,512]{1,0:T(8,128)(2,1)S(1)}, u32[]{:S(2)}, u32[]{:S(2)}) collective-permute-start(s16[72,512]{1,0:T(8,128)(2,1)S(1)} %get-tuple-element.59), channel_id=1, source_target_pairs={{0,2},{1,3},{2,0},{3,1},{4,6},{5,7},{6,4},{7,5},{8,10},{9,11},{10,... | collective-permute-start | bytes 221192 | tf_op jit(solution)/shard_map/ppermute | solution.py:344
  24.6 0.5 collective-permute-start.9
  25.2 0.0 copy-done
  25.2 1.8 %schur_kernel.1 = (f32[2048,128]{1,0:T(8,128)S(1)}, f32[2048,128]{1,0:T(8,128)S(1)}) custom-call(s32[1,512]{1,0:T(1,128)S(1)} %get-tuple-element.51.panel_ref, f32[1,128]{1,0:T(1,128)S(1)} %get-tuple-element.52.own_diagonal_ref, bf16[1536,1024]{1,0:T(8,128)(2,1)S(1)} %bitcast.6, bf16[512,1536]{1,0:T(8,128)(2,1)S(1)} %get-tuple-element.54.turned_ref), custom_call_target="tpu_custom_call" | custom-call | flops 2300000000 | bytes 1024 | tf_op jit(solution)/shard_map/schur_kernel/pallas_call | solution.py:329
  27.0 0.1 collective-permute-start.12
  27.1 0.1 collective-permute-done.10.refs_2_
  27.2 1.3 %collective-permute-done.11.refs_3_ = s16[72,512]{1,0:T(8,128)(2,1)S(1)} collective-permute-done((s16[72,512]{1,0:T(8,128)(2,1)S(1)}, s16[72,512]{1,0:T(8,128)(2,1)S(1)}, u32[]{:S(2)}, u32[]{:S(2)}) %collective-permute-start.11) | collective-permute-done | bytes 73760 | tf_op jit(solution)/shard_map/ppermute | solution.py:344
  28.5 0.5 collective-permute-done.9.refs_1_
  29.0 0.1 sum_kernel.2.refs_0_
  29.1 3.7 %collective-permute-start.13 = (s16[72,512]{1,0:T(8,128)(2,1)S(1)}, s16[72,512]{1,0:T(8,128)(2,1)S(1)}, u32[]{:S(2)}, u32[]{:S(2)}) collective-permute-start(s16[72,512]{1,0:T(8,128)(2,1)S(1)} %sum_kernel.2.refs_0_), channel_id=1, source_target_pairs={{0,24},{4,28},{8,16},{12,20},{16,8},{20,12},{24,0},{28,4},{1,25},{... | collective-permute-start | bytes 221192 | tf_op jit(solution)/shard_map/ppermute | solution.py:344
  32.8 0.0 collective-permute-start.14
  32.8 0.8 %collective-permute-start.15 = (s16[72,512]{1,0:T(8,128)(2,1)S(1)}, s16[72,512]{1,0:T(8,128)(2,1)S(1)}, u32[]{:S(2)}, u32[]{:S(2)}) collective-permute-start(s16[72,512]{1,0:T(8,128)(2,1)S(1)} %sum_kernel.2.refs_0_), channel_id=1, source_target_pairs={{0,8},{4,12},{8,0},{12,4},{16,24},{20,28},{24,16},{28,20},{1,9},{5... | collective-permute-start | bytes 221192 | tf_op jit(solution)/shard_map/ppermute | solution.py:344
  33.6 0.0 collective-permute-done.12.got_ref
  33.6 0.2 bulk_pair_kernel.1
  33.8 1.3 %collective-permute-start.16 = (s16[1056,128]{1,0:T(8,128)(2,1)S(1)}, s16[1056,128]{1,0:T(8,128)(2,1)S(1)}, u32[]{:S(2)}, u32[]{:S(2)}) collective-permute-start(s16[1056,128]{1,0:T(8,128)(2,1)S(1)} %get-tuple-element.62), channel_id=1, source_target_pairs={{0,8},{4,12},{8,0},{12,4},{16,24},{20,28},{24,16},{28,20},{1,9},{5... | collective-permute-start | bytes 811016 | tf_op jit(solution)/shard_map/ppermute | solution.py:344
  35.1 1.2 %collective-permute-done.13.refs_1_ = s16[72,512]{1,0:T(8,128)(2,1)S(1)} collective-permute-done((s16[72,512]{1,0:T(8,128)(2,1)S(1)}, s16[72,512]{1,0:T(8,128)(2,1)S(1)}, u32[]{:S(2)}, u32[]{:S(2)}) %collective-permute-start.13) | collective-permute-done | bytes 73760 | tf_op jit(solution)/shard_map/ppermute | solution.py:344
  36.3 2.5 %collective-permute-done.14.refs_2_ = s16[72,512]{1,0:T(8,128)(2,1)S(1)} collective-permute-done((s16[72,512]{1,0:T(8,128)(2,1)S(1)}, s16[72,512]{1,0:T(8,128)(2,1)S(1)}, u32[]{:S(2)}, u32[]{:S(2)}) %collective-permute-start.14) | collective-permute-done | bytes 73760 | tf_op jit(solution)/shard_map/ppermute | solution.py:344
  38.8 0.8 %collective-permute-done.15.refs_3_ = s16[72,512]{1,0:T(8,128)(2,1)S(1)} collective-permute-done((s16[72,512]{1,0:T(8,128)(2,1)S(1)}, s16[72,512]{1,0:T(8,128)(2,1)S(1)}, u32[]{:S(2)}, u32[]{:S(2)}) %collective-permute-start.15) | collective-permute-done | bytes 73760 | tf_op jit(solution)/shard_map/ppermute | solution.py:344
  39.6 0.1 sum_kernel.3.refs_0_
  39.7 1.0 %collective-permute-start.17 = (s16[72,512]{1,0:T(8,128)(2,1)S(1)}, s16[72,512]{1,0:T(8,128)(2,1)S(1)}, u32[]{:S(2)}, u32[]{:S(2)}) collective-permute-start(s16[72,512]{1,0:T(8,128)(2,1)S(1)} %sum_kernel.3.refs_0_), channel_id=1, source_target_pairs={{0,3},{1,2},{2,1},{3,0},{4,7},{5,6},{6,5},{7,4},{8,11},{9,10},{10,... | collective-permute-start | bytes 221192 | tf_op jit(solution)/shard_map/ppermute | solution.py:344
  40.7 1.1 %collective-permute-start.18 = (s16[72,512]{1,0:T(8,128)(2,1)S(1)}, s16[72,512]{1,0:T(8,128)(2,1)S(1)}, u32[]{:S(2)}, u32[]{:S(2)}) collective-permute-start(s16[72,512]{1,0:T(8,128)(2,1)S(1)} %sum_kernel.3.refs_0_), channel_id=1, source_target_pairs={{0,2},{1,3},{2,0},{3,1},{4,6},{5,7},{6,4},{7,5},{8,10},{9,11},{10,... | collective-permute-start | bytes 221192 | tf_op jit(solution)/shard_map/ppermute | solution.py:344
  41.8 1.5 %collective-permute-start.19 = (s16[72,512]{1,0:T(8,128)(2,1)S(1)}, s16[72,512]{1,0:T(8,128)(2,1)S(1)}, u32[]{:S(2)}, u32[]{:S(2)}) collective-permute-start(s16[72,512]{1,0:T(8,128)(2,1)S(1)} %sum_kernel.3.refs_0_), channel_id=1, source_target_pairs={{0,1},{1,0},{2,3},{3,2},{4,5},{5,4},{6,7},{7,6},{8,9},{9,8},{10,11... | collective-permute-start | bytes 221192 | tf_op jit(solution)/shard_map/ppermute | solution.py:344
  43.3 1.1 %collective-permute-done.16.got_ref = s16[1056,128]{1,0:T(8,128)(2,1)S(1)} collective-permute-done((s16[1056,128]{1,0:T(8,128)(2,1)S(1)}, s16[1056,128]{1,0:T(8,128)(2,1)S(1)}, u32[]{:S(2)}, u32[]{:S(2)}) %collective-permute-start.16) | collective-permute-done | bytes 270368 | tf_op jit(solution)/shard_map/ppermute | solution.py:344
  44.4 0.2 bulk_sum_kernel.1
  44.5 0.6 %collective-permute-done.17.refs_1_ = s16[72,512]{1,0:T(8,128)(2,1)S(1)} collective-permute-done((s16[72,512]{1,0:T(8,128)(2,1)S(1)}, s16[72,512]{1,0:T(8,128)(2,1)S(1)}, u32[]{:S(2)}, u32[]{:S(2)}) %collective-permute-start.17) | collective-permute-done | bytes 73760 | tf_op jit(solution)/shard_map/ppermute | solution.py:344
  45.1 0.7 %collective-permute-done.18.refs_2_ = s16[72,512]{1,0:T(8,128)(2,1)S(1)} collective-permute-done((s16[72,512]{1,0:T(8,128)(2,1)S(1)}, s16[72,512]{1,0:T(8,128)(2,1)S(1)}, u32[]{:S(2)}, u32[]{:S(2)}) %collective-permute-start.18) | collective-permute-done | bytes 73760 | tf_op jit(solution)/shard_map/ppermute | solution.py:344
  45.9 0.3 collective-permute-done.19.refs_3_
  46.2 0.1 collective-permute-start.20
  46.3 1.4 %collective-permute-start.21 = (s16[528,128]{1,0:T(8,128)(2,1)S(1)}, s16[528,128]{1,0:T(8,128)(2,1)S(1)}, u32[]{:S(2)}, u32[]{:S(2)}) collective-permute-start(s16[528,128]{1,0:T(8,128)(2,1)S(1)} %get-tuple-element.65), channel_id=1, source_target_pairs={{0,16},{4,20},{8,24},{12,28},{16,0},{20,4},{24,8},{28,12},{1,17},{... | collective-permute-start | bytes 405512 | tf_op jit(solution)/shard_map/ppermute | solution.py:344
  47.7 0.2 own_kernel.1.half_ref
  47.9 0.0 collective-permute-done.20.other_ref
  47.9 7.0 %newton_kernel.1 = (bf16[256,768]{1,0:T(8,128)(2,1)S(1)}, bf16[256,1536]{1,0:T(8,128)(2,1)S(1)}) custom-call(f32[256,512]{1,0:T(8,128)S(1)} %own_kernel.1.half_ref, s16[320,512]{1,0:T(8,128)(2,1)S(1)} %collective-permute-done.20.other_ref), custom_call_target="tpu_custom_call" | custom-call | bytes 1024 | tf_op jit(solution)/shard_map/newton_kernel/pallas_call | solution.py:329
  54.9 1.2 %collective-permute-done.21.refs_0_ = s16[528,128]{1,0:T(8,128)(2,1)S(1)} collective-permute-done((s16[528,128]{1,0:T(8,128)(2,1)S(1)}, s16[528,128]{1,0:T(8,128)(2,1)S(1)}, u32[]{:S(2)}, u32[]{:S(2)}) %collective-permute-start.21) | collective-permute-done | bytes 135200 | tf_op jit(solution)/shard_map/ppermute | solution.py:344
  56.1 1.2 %factor_kernel.1 = (f32[128,1,256]{2,1,0:T(1,128)}, f32[128,1,256]{2,1,0:T(1,128)}) custom-call(bf16[256,768]{1,0:T(8,128)(2,1)S(1)} %get-tuple-element.67.inverse_first_ref, bf16[256,1536]{1,0:T(8,128)(2,1)S(1)} %get-tuple-element.68.inverse_second_ref, f32[512,128]{1,0:T(8,128)S(1)} %get-tuple-element.69.rows_ref, ...), custom_call_target="tpu_custom_call" | custom-call | bytes 1024 | tf_op jit(solution)/shard_map/factor_kernel/pallas_call | solution.py:329
  (2 shorter events, 0.1 us)
Async XLA Ops:
  1.8 8.8 %collective-permute-start.2 = (bf16[256,384]{1,0:T(8,128)(2,1)S(1)}, bf16[256,384]{1,0:T(8,128)(2,1)S(1)}, u32[]{:S(2)}, u32[]{:S(2)}) collective-permute-start(bf16[256,384]{1,0:T(8,128)(2,1)S(1)} %get-tuple-element.39.refs_0_), channel_id=1, source_target_pairs={{0,2},{1,3},{2,0},{3,1},{4,6},{5,7},{6,4},{7,5},{8,10},{9,11},{10,... | collective-permute-start | bytes 589832 | tf_op jit(solution)/shard_map/ppermute | solution.py:344
  4.8 7.8 %collective-permute-start.1 = (bf16[256,384]{1,0:T(8,128)(2,1)S(1)}, bf16[256,384]{1,0:T(8,128)(2,1)S(1)}, u32[]{:S(2)}, u32[]{:S(2)}) collective-permute-start(bf16[256,384]{1,0:T(8,128)(2,1)S(1)} %get-tuple-element.40.refs_1_), channel_id=1, source_target_pairs={{0,1},{1,0},{2,3},{3,2},{4,5},{5,4},{6,7},{7,6},{8,9},{9,8},{10,11... | collective-permute-start | bytes 589832 | tf_op jit(solution)/shard_map/ppermute | solution.py:344
  6.3 10.7 %collective-permute-start = (bf16[256,384]{1,0:T(8,128)(2,1)S(1)}, bf16[256,384]{1,0:T(8,128)(2,1)S(1)}, u32[]{:S(2)}, u32[]{:S(2)}) collective-permute-start(bf16[256,384]{1,0:T(8,128)(2,1)S(1)} %get-tuple-element.39.refs_0_), channel_id=1, source_target_pairs={{0,1},{1,0},{2,3},{3,2},{4,5},{5,4},{6,7},{7,6},{8,9},{9,8},{10,11... | collective-permute-start | bytes 589832 | tf_op jit(solution)/shard_map/ppermute | solution.py:344
  6.9 10.2 %collective-permute-start.3 = (bf16[256,384]{1,0:T(8,128)(2,1)S(1)}, bf16[256,384]{1,0:T(8,128)(2,1)S(1)}, u32[]{:S(2)}, u32[]{:S(2)}) collective-permute-start(bf16[256,384]{1,0:T(8,128)(2,1)S(1)} %get-tuple-element.40.refs_1_), channel_id=1, source_target_pairs={{0,2},{1,3},{2,0},{3,1},{4,6},{5,7},{6,4},{7,5},{8,10},{9,11},{10,... | collective-permute-start | bytes 589832 | tf_op jit(solution)/shard_map/ppermute | solution.py:344
  10.6 9.1 %collective-permute-start.5 = (bf16[256,384]{1,0:T(8,128)(2,1)S(1)}, bf16[256,384]{1,0:T(8,128)(2,1)S(1)}, u32[]{:S(2)}, u32[]{:S(2)}) collective-permute-start(bf16[256,384]{1,0:T(8,128)(2,1)S(1)} %collective-permute-done.2.refs_4_), channel_id=1, source_target_pairs={{0,1},{1,0},{2,3},{3,2},{4,5},{5,4},{6,7},{7,6},{8,9},{9,8},{10,11... | collective-permute-start | bytes 589832 | tf_op jit(solution)/shard_map/ppermute | solution.py:344
  12.7 7.0 %collective-permute-start.6 = (bf16[256,384]{1,0:T(8,128)(2,1)S(1)}, bf16[256,384]{1,0:T(8,128)(2,1)S(1)}, u32[]{:S(2)}, u32[]{:S(2)}) collective-permute-start(bf16[256,384]{1,0:T(8,128)(2,1)S(1)} %collective-permute-done.1.refs_3_), channel_id=1, source_target_pairs={{0,2},{1,3},{2,0},{3,1},{4,6},{5,7},{6,4},{7,5},{8,10},{9,11},{10,... | collective-permute-start | bytes 589832 | tf_op jit(solution)/shard_map/ppermute | solution.py:344
  18.2 2.0 %collective-permute-start.4 = (f32[264,512]{1,0:T(8,128)S(1)}, f32[264,512]{1,0:T(8,128)S(1)}, u32[]{:S(2)}, u32[]{:S(2)}) collective-permute-start(f32[264,512]{1,0:T(8,128)S(1)} %get-tuple-element.43), channel_id=1, source_target_pairs={{0,4},{4,0},{8,12},{12,8},{16,20},{20,16},{24,28},{28,24},{1,5},{5... | collective-permute-start | bytes 1622024 | tf_op jit(solution)/shard_map/ppermute | solution.py:344
  18.3 2.9 %collective-permute-start.8 = (bf16[384,512]{1,0:T(8,128)(2,1)S(1)}, bf16[384,512]{1,0:T(8,128)(2,1)S(1)}, u32[]{:S(2)}, u32[]{:S(2)}) collective-permute-start(bf16[384,512]{1,0:T(8,128)(2,1)S(1)} %get-tuple-element.49.refs_2_), channel_id=1, source_target_pairs={{0,4},{4,0},{8,12},{12,8},{16,20},{20,16},{24,28},{28,24},{1,5},{5... | collective-permute-start | bytes 1179656 | tf_op jit(solution)/shard_map/ppermute | solution.py:344
  19.7 1.5 %collective-permute-start.7 = (bf16[256,384]{1,0:T(8,128)(2,1)S(1)}, bf16[256,384]{1,0:T(8,128)(2,1)S(1)}, u32[]{:S(2)}, u32[]{:S(2)}) collective-permute-start(bf16[256,384]{1,0:T(8,128)(2,1)S(1)} %select_kernel.1), channel_id=1, source_target_pairs={{0,4},{4,0},{8,12},{12,8},{16,20},{20,16},{24,28},{28,24},{1,5},{5... | collective-permute-start | bytes 589832 | tf_op jit(solution)/shard_map/ppermute | solution.py:344
  20.2 5.0 %copy-start = (bf16[1,1536,1024]{2,1,0:T(8,128)(2,1)S(1)}, bf16[1,1536,1024]{2,1,0:T(8,128)(2,1)}, u32[]{:S(2)}) copy-start(bf16[1,1536,1024]{2,1,0:T(8,128)(2,1)} %param.4) | copy-start | bytes 9437188
  21.6 5.6 %collective-permute-start.10 = (s16[72,512]{1,0:T(8,128)(2,1)S(1)}, s16[72,512]{1,0:T(8,128)(2,1)S(1)}, u32[]{:S(2)}, u32[]{:S(2)}) collective-permute-start(s16[72,512]{1,0:T(8,128)(2,1)S(1)} %get-tuple-element.58), channel_id=1, source_target_pairs={{0,3},{1,2},{2,1},{3,0},{4,7},{5,6},{6,5},{7,4},{8,11},{9,10},{10,... | collective-permute-start | bytes 221192 | tf_op jit(solution)/shard_map/ppermute | solution.py:344
  23.1 5.4 %collective-permute-start.11 = (s16[72,512]{1,0:T(8,128)(2,1)S(1)}, s16[72,512]{1,0:T(8,128)(2,1)S(1)}, u32[]{:S(2)}, u32[]{:S(2)}) collective-permute-start(s16[72,512]{1,0:T(8,128)(2,1)S(1)} %get-tuple-element.59), channel_id=1, source_target_pairs={{0,2},{1,3},{2,0},{3,1},{4,6},{5,7},{6,4},{7,5},{8,10},{9,11},{10,... | collective-permute-start | bytes 221192 | tf_op jit(solution)/shard_map/ppermute | solution.py:344
  24.6 4.4 %collective-permute-start.9 = (s16[72,512]{1,0:T(8,128)(2,1)S(1)}, s16[72,512]{1,0:T(8,128)(2,1)S(1)}, u32[]{:S(2)}, u32[]{:S(2)}) collective-permute-start(s16[72,512]{1,0:T(8,128)(2,1)S(1)} %get-tuple-element.57), channel_id=1, source_target_pairs={{0,1},{1,0},{2,3},{3,2},{4,5},{5,4},{6,7},{7,6},{8,9},{9,8},{10,11... | collective-permute-start | bytes 221192 | tf_op jit(solution)/shard_map/ppermute | solution.py:344
  27.0 6.6 %collective-permute-start.12 = (f32[2048,128]{1,0:T(8,128)S(1)}, f32[2048,128]{1,0:T(8,128)S(1)}, u32[]{:S(2)}, u32[]{:S(2)}) collective-permute-start(f32[2048,128]{1,0:T(8,128)S(1)} %get-tuple-element.61), channel_id=1, source_target_pairs={{0,4},{4,0},{8,12},{12,8},{16,20},{20,16},{24,28},{28,24},{1,5},{5... | collective-permute-start | bytes 3145736 | tf_op jit(solution)/shard_map/ppermute | solution.py:344
  29.1 7.2 %collective-permute-start.13 = (s16[72,512]{1,0:T(8,128)(2,1)S(1)}, s16[72,512]{1,0:T(8,128)(2,1)S(1)}, u32[]{:S(2)}, u32[]{:S(2)}) collective-permute-start(s16[72,512]{1,0:T(8,128)(2,1)S(1)} %sum_kernel.2.refs_0_), channel_id=1, source_target_pairs={{0,24},{4,28},{8,16},{12,20},{16,8},{20,12},{24,0},{28,4},{1,25},{... | collective-permute-start | bytes 221192 | tf_op jit(solution)/shard_map/ppermute | solution.py:344
  32.8 5.9 %collective-permute-start.14 = (s16[72,512]{1,0:T(8,128)(2,1)S(1)}, s16[72,512]{1,0:T(8,128)(2,1)S(1)}, u32[]{:S(2)}, u32[]{:S(2)}) collective-permute-start(s16[72,512]{1,0:T(8,128)(2,1)S(1)} %sum_kernel.2.refs_0_), channel_id=1, source_target_pairs={{0,16},{4,20},{8,24},{12,28},{16,0},{20,4},{24,8},{28,12},{1,17},{... | collective-permute-start | bytes 221192 | tf_op jit(solution)/shard_map/ppermute | solution.py:344
  32.8 6.8 %collective-permute-start.15 = (s16[72,512]{1,0:T(8,128)(2,1)S(1)}, s16[72,512]{1,0:T(8,128)(2,1)S(1)}, u32[]{:S(2)}, u32[]{:S(2)}) collective-permute-start(s16[72,512]{1,0:T(8,128)(2,1)S(1)} %sum_kernel.2.refs_0_), channel_id=1, source_target_pairs={{0,8},{4,12},{8,0},{12,4},{16,24},{20,28},{24,16},{28,20},{1,9},{5... | collective-permute-start | bytes 221192 | tf_op jit(solution)/shard_map/ppermute | solution.py:344
  33.8 10.6 %collective-permute-start.16 = (s16[1056,128]{1,0:T(8,128)(2,1)S(1)}, s16[1056,128]{1,0:T(8,128)(2,1)S(1)}, u32[]{:S(2)}, u32[]{:S(2)}) collective-permute-start(s16[1056,128]{1,0:T(8,128)(2,1)S(1)} %get-tuple-element.62), channel_id=1, source_target_pairs={{0,8},{4,12},{8,0},{12,4},{16,24},{20,28},{24,16},{28,20},{1,9},{5... | collective-permute-start | bytes 811016 | tf_op jit(solution)/shard_map/ppermute | solution.py:344
  39.7 5.4 %collective-permute-start.17 = (s16[72,512]{1,0:T(8,128)(2,1)S(1)}, s16[72,512]{1,0:T(8,128)(2,1)S(1)}, u32[]{:S(2)}, u32[]{:S(2)}) collective-permute-start(s16[72,512]{1,0:T(8,128)(2,1)S(1)} %sum_kernel.3.refs_0_), channel_id=1, source_target_pairs={{0,3},{1,2},{2,1},{3,0},{4,7},{5,6},{6,5},{7,4},{8,11},{9,10},{10,... | collective-permute-start | bytes 221192 | tf_op jit(solution)/shard_map/ppermute | solution.py:344
  40.7 5.1 %collective-permute-start.18 = (s16[72,512]{1,0:T(8,128)(2,1)S(1)}, s16[72,512]{1,0:T(8,128)(2,1)S(1)}, u32[]{:S(2)}, u32[]{:S(2)}) collective-permute-start(s16[72,512]{1,0:T(8,128)(2,1)S(1)} %sum_kernel.3.refs_0_), channel_id=1, source_target_pairs={{0,2},{1,3},{2,0},{3,1},{4,6},{5,7},{6,4},{7,5},{8,10},{9,11},{10,... | collective-permute-start | bytes 221192 | tf_op jit(solution)/shard_map/ppermute | solution.py:344
  41.8 4.4 %collective-permute-start.19 = (s16[72,512]{1,0:T(8,128)(2,1)S(1)}, s16[72,512]{1,0:T(8,128)(2,1)S(1)}, u32[]{:S(2)}, u32[]{:S(2)}) collective-permute-start(s16[72,512]{1,0:T(8,128)(2,1)S(1)} %sum_kernel.3.refs_0_), channel_id=1, source_target_pairs={{0,1},{1,0},{2,3},{3,2},{4,5},{5,4},{6,7},{7,6},{8,9},{9,8},{10,11... | collective-permute-start | bytes 221192 | tf_op jit(solution)/shard_map/ppermute | solution.py:344
  46.2 1.7 %collective-permute-start.20 = (s16[320,512]{1,0:T(8,128)(2,1)S(1)}, s16[320,512]{1,0:T(8,128)(2,1)S(1)}, u32[]{:S(2)}, u32[]{:S(2)}) collective-permute-start(s16[320,512]{1,0:T(8,128)(2,1)S(1)} %join_kernel.1.own_ref), channel_id=1, source_target_pairs={{0,4},{4,0},{8,12},{12,8},{16,20},{20,16},{24,28},{28,24},{1,5},{5... | collective-permute-start | bytes 983048 | tf_op jit(solution)/shard_map/ppermute | solution.py:344
  46.3 9.8 %collective-permute-start.21 = (s16[528,128]{1,0:T(8,128)(2,1)S(1)}, s16[528,128]{1,0:T(8,128)(2,1)S(1)}, u32[]{:S(2)}, u32[]{:S(2)}) collective-permute-start(s16[528,128]{1,0:T(8,128)(2,1)S(1)} %get-tuple-element.65), channel_id=1, source_target_pairs={{0,16},{4,20},{8,24},{12,28},{16,0},{20,4},{24,8},{28,12},{1,17},{... | collective-permute-start | bytes 405512 | tf_op jit(solution)/shard_map/ppermute | solution.py:344

commit v21 on v17

--- a/solution.py
+++ b/solution.py
@@ -309,6 +309,12 @@
             encode(value, coded_ref, (i - half // panel) * (panel + TAIL), TAIL)
 
 
+def product_turned(a, b):
+    high, low = halves(b)
+    right = jnp.concatenate([high, low, high], axis=1)
+    return lax.dot_general(left_of(a), right, (((1,), (1,)), ((), ())), preferred_element_type=F32)
+
+
 def factor_kernel(inverse_first_ref, inverse_second_ref, rows_ref, *refs):
     *got, first_out, second_out = refs
     panel = rows_ref.shape[0]
@@ -317,8 +323,8 @@
     for ref in got:
         rows = rows + decode(ref, 0, panel, TAIL)[0]
     first, second = rows[:half], rows[half:]
-    first_out[...] = product(inverse_first_ref[...], first).T[:, None, :]
-    second_out[...] = product(inverse_second_ref[...], jnp.concatenate([second, first], axis=0)).T[:, None, :]
+    first_out[...] = product_turned(first.T, inverse_first_ref[...])[:, None, :]
+    second_out[...] = product_turned(jnp.concatenate([second.T, first.T], axis=1), inverse_second_ref[...])[:, None, :]
 
 
 def call(kernel, out_shape, *args, scratch=(), remain=0, micros=0.0, aliases=None):

time: 57.5 us -> 57.5 us (level)
  no operation moved by 1% of the time
where the time goes in v21:
time: 57.5 us; the launch traced here: 57.3 us
  starting transfers between devices  23.7 us (41%)
  Pallas kernels  18.8 us (33%)
  waiting for transfers between devices  14.1 us (25%)
  between operations  0.8 us (1%)
    ppermute x22, starting transfers between devices, swap(): return lax.ppermute(x, axis, [(i, i ^ bit) for i in range(count)])  23.7 us
    pallas_call x16, Pallas kernels, call(): pl.pallas_call(kernel, name=getattr(kernel, 'func', kernel).__name__, out...  18.8 us
    ppermute x22, waiting for transfers between devices, swap(): return lax.ppermute(x, axis, [(i, i ^ bit) for i in range(count)])  14.1 us
  transfers between devices with their start and end apart: 22, of which 16 were waited for; matrix products, arithmetic and copies ran while one was open for 0% of the time, Pallas kernels for 28%

profile of v21, /device:TPU:0, one launch (start us, length us, event | category | flops | bytes accessed | tf_op | source)
XLA Modules:
  0.0 57.3 jit_solution(8224249216297368337)
XLA Ops:
  0.6 1.2 %turn_kernel.1 = (bf16[256,384]{1,0:T(8,128)(2,1)S(1)}, bf16[256,384]{1,0:T(8,128)(2,1)S(1)}) custom-call(bf16[384,512]{1,0:T(8,128)(2,1)} %bitcast.7), custom_call_target="tpu_custom_call" | custom-call | bytes 1024 | tf_op jit(solution)/shard_map/turn_kernel/pallas_call | solution.py:335
  1.8 3.0 %collective-permute-start.2 = (bf16[256,384]{1,0:T(8,128)(2,1)S(1)}, bf16[256,384]{1,0:T(8,128)(2,1)S(1)}, u32[]{:S(2)}, u32[]{:S(2)}) collective-permute-start(bf16[256,384]{1,0:T(8,128)(2,1)S(1)} %get-tuple-element.39.refs_0_), channel_id=1, source_target_pairs={{0,2},{1,3},{2,0},{3,1},{4,6},{5,7},{6,4},{7,5},{8,10},{9,11},{10,... | collective-permute-start | bytes 589832 | tf_op jit(solution)/shard_map/ppermute | solution.py:350
  4.8 1.5 %collective-permute-start.1 = (bf16[256,384]{1,0:T(8,128)(2,1)S(1)}, bf16[256,384]{1,0:T(8,128)(2,1)S(1)}, u32[]{:S(2)}, u32[]{:S(2)}) collective-permute-start(bf16[256,384]{1,0:T(8,128)(2,1)S(1)} %get-tuple-element.40.refs_1_), channel_id=1, source_target_pairs={{0,1},{1,0},{2,3},{3,2},{4,5},{5,4},{6,7},{7,6},{8,9},{9,8},{10,11... | collective-permute-start | bytes 589832 | tf_op jit(solution)/shard_map/ppermute | solution.py:350
  6.3 0.5 collective-permute-start
  6.9 0.1 collective-permute-start.3
  6.9 1.8 %pick_kernel.1 = (bf16[1536,512]{1,0:T(8,128)(2,1)S(1)}, bf16[384,512]{1,0:T(8,128)(2,1)S(1)}, f32[8,512]{1,0:T(8,128)S(1)}, bf16[1024,512]{1,0:T(8,128)(2,1)S(1...) custom-call(s32[1,512]{1,0:T(1,128)} %bitcast.8, f32[1,128]{1,0:T(1,128)} %bitcast.9, bf16[1536,1024]{1,0:T(8,128)(2,1)} %bitcast.4), custom_call_target="tpu_custom_call" | custom-call | bytes 1024 | tf_op jit(solution)/shard_map/pick_kernel/pallas_call | solution.py:335
  8.8 1.8 %collective-permute-done.2.refs_4_ = bf16[256,384]{1,0:T(8,128)(2,1)S(1)} collective-permute-done((bf16[256,384]{1,0:T(8,128)(2,1)S(1)}, bf16[256,384]{1,0:T(8,128)(2,1)S(1)}, u32[]{:S(2)}, u32[]{:S(2)}) %collective-permute-start.2) | collective-permute-done | bytes 196640 | tf_op jit(solution)/shard_map/ppermute | solution.py:350
  10.6 2.0 %collective-permute-start.5 = (bf16[256,384]{1,0:T(8,128)(2,1)S(1)}, bf16[256,384]{1,0:T(8,128)(2,1)S(1)}, u32[]{:S(2)}, u32[]{:S(2)}) collective-permute-start(bf16[256,384]{1,0:T(8,128)(2,1)S(1)} %collective-permute-done.2.refs_4_), channel_id=1, source_target_pairs={{0,1},{1,0},{2,3},{3,2},{4,5},{5,4},{6,7},{7,6},{8,9},{9,8},{10,11... | collective-permute-start | bytes 589832 | tf_op jit(solution)/shard_map/ppermute | solution.py:350
  12.6 0.1 collective-permute-done.1.refs_3_
  12.7 1.5 %collective-permute-start.6 = (bf16[256,384]{1,0:T(8,128)(2,1)S(1)}, bf16[256,384]{1,0:T(8,128)(2,1)S(1)}, u32[]{:S(2)}, u32[]{:S(2)}) collective-permute-start(bf16[256,384]{1,0:T(8,128)(2,1)S(1)} %collective-permute-done.1.refs_3_), channel_id=1, source_target_pairs={{0,2},{1,3},{2,0},{3,1},{4,6},{5,7},{6,4},{7,5},{8,10},{9,11},{10,... | collective-permute-start | bytes 589832 | tf_op jit(solution)/shard_map/ppermute | solution.py:350
  14.1 2.9 %rest_kernel.1.chosen_ref = bf16[1536,512]{1,0:T(8,128)(2,1)S(1)} custom-call(bf16[1536,512]{1,0:T(8,128)(2,1)S(1)} %get-tuple-element.36.chosen_in, bf16[1024,512]{1,0:T(8,128)(2,1)S(1)} %get-tuple-element.37.one_ref, bf16[1536,1024]{1,0:T(8,128)(2,1)} %bitcast.5), custom_call_target="tpu_custom_call", output_to_operand_aliasing={{}: (0, {})} | custom-call | bytes 1024 | tf_op jit(solution)/shard_map/rest_kernel/pallas_call | solution.py:335
  17.0 0.0 collective-permute-done.refs_2_
  17.0 0.0 collective-permute-done.3.refs_5_
  17.0 1.2 %early_kernel.1 = (bf16[512,1536]{1,0:T(8,128)(2,1)S(1)}, f32[256,512]{1,0:T(8,128)S(1)}, f32[264,512]{1,0:T(8,128)S(1)}) custom-call(bf16[1536,512]{1,0:T(8,128)(2,1)S(1)} %rest_kernel.1.chosen_ref, f32[8,512]{1,0:T(8,128)S(1)} %get-tuple-element.38.entry_ref, bf16[256,384]{1,0:T(8,128)(2,1)S(1)} %get-tuple-element.39.refs_0_, ...), custom_call_target="tpu_custom_call" | custom-call | bytes 1024 | tf_op jit(solution)/shard_map/early_kernel/pallas_call | solution.py:335
  18.2 0.1 collective-permute-start.4
  18.3 0.5 collective-permute-start.8
  18.8 0.8 %collective-permute-done.5.refs_0_.upper_ref = bf16[256,384]{1,0:T(8,128)(2,1)S(1)} collective-permute-done((bf16[256,384]{1,0:T(8,128)(2,1)S(1)}, bf16[256,384]{1,0:T(8,128)(2,1)S(1)}, u32[]{:S(2)}, u32[]{:S(2)}) %collective-permute-start.5) | collective-permute-done | bytes 196640 | tf_op jit(solution)/shard_map/ppermute | solution.py:350
  19.6 0.0 collective-permute-done.6.refs_1_.lower_ref
  19.7 0.1 collective-permute-start.7
  19.7 0.5 collective-permute-done.4.got_ref
  20.2 0.0 copy-start
  20.2 0.4 keep_kernel.1
  20.6 0.6 %collective-permute-done.7.refs_0_ = bf16[256,384]{1,0:T(8,128)(2,1)S(1)} collective-permute-done((bf16[256,384]{1,0:T(8,128)(2,1)S(1)}, bf16[256,384]{1,0:T(8,128)(2,1)S(1)}, u32[]{:S(2)}, u32[]{:S(2)}) %collective-permute-start.7) | collective-permute-done | bytes 196640 | tf_op jit(solution)/shard_map/ppermute | solution.py:350
  21.2 0.0 collective-permute-done.8.refs_1_
  21.2 0.5 pair_kernel.1
  21.6 1.5 %collective-permute-start.10 = (s16[72,512]{1,0:T(8,128)(2,1)S(1)}, s16[72,512]{1,0:T(8,128)(2,1)S(1)}, u32[]{:S(2)}, u32[]{:S(2)}) collective-permute-start(s16[72,512]{1,0:T(8,128)(2,1)S(1)} %get-tuple-element.58), channel_id=1, source_target_pairs={{0,3},{1,2},{2,1},{3,0},{4,7},{5,6},{6,5},{7,4},{8,11},{9,10},{10,... | collective-permute-start | bytes 221192 | tf_op jit(solution)/shard_map/ppermute | solution.py:350
  23.1 1.5 %collective-permute-start.11 = (s16[72,512]{1,0:T(8,128)(2,1)S(1)}, s16[72,512]{1,0:T(8,128)(2,1)S(1)}, u32[]{:S(2)}, u32[]{:S(2)}) collective-permute-start(s16[72,512]{1,0:T(8,128)(2,1)S(1)} %get-tuple-element.59), channel_id=1, source_target_pairs={{0,2},{1,3},{2,0},{3,1},{4,6},{5,7},{6,4},{7,5},{8,10},{9,11},{10,... | collective-permute-start | bytes 221192 | tf_op jit(solution)/shard_map/ppermute | solution.py:350
  24.6 0.5 collective-permute-start.9
  25.2 0.0 copy-done
  25.2 1.8 %schur_kernel.1 = (f32[2048,128]{1,0:T(8,128)S(1)}, f32[2048,128]{1,0:T(8,128)S(1)}) custom-call(s32[1,512]{1,0:T(1,128)S(1)} %get-tuple-element.51.panel_ref, f32[1,128]{1,0:T(1,128)S(1)} %get-tuple-element.52.own_diagonal_ref, bf16[1536,1024]{1,0:T(8,128)(2,1)S(1)} %bitcast.6, bf16[512,1536]{1,0:T(8,128)(2,1)S(1)} %get-tuple-element.54.turned_ref), custom_call_target="tpu_custom_call" | custom-call | flops 2300000000 | bytes 1024 | tf_op jit(solution)/shard_map/schur_kernel/pallas_call | solution.py:335
  27.0 0.1 collective-permute-start.12
  27.1 0.1 collective-permute-done.10.refs_2_
  27.2 1.3 %collective-permute-done.11.refs_3_ = s16[72,512]{1,0:T(8,128)(2,1)S(1)} collective-permute-done((s16[72,512]{1,0:T(8,128)(2,1)S(1)}, s16[72,512]{1,0:T(8,128)(2,1)S(1)}, u32[]{:S(2)}, u32[]{:S(2)}) %collective-permute-start.11) | collective-permute-done | bytes 73760 | tf_op jit(solution)/shard_map/ppermute | solution.py:350
  28.5 0.5 collective-permute-done.9.refs_1_
  29.0 0.1 sum_kernel.2.refs_0_
  29.1 3.7 %collective-permute-start.13 = (s16[72,512]{1,0:T(8,128)(2,1)S(1)}, s16[72,512]{1,0:T(8,128)(2,1)S(1)}, u32[]{:S(2)}, u32[]{:S(2)}) collective-permute-start(s16[72,512]{1,0:T(8,128)(2,1)S(1)} %sum_kernel.2.refs_0_), channel_id=1, source_target_pairs={{0,24},{4,28},{8,16},{12,20},{16,8},{20,12},{24,0},{28,4},{1,25},{... | collective-permute-start | bytes 221192 | tf_op jit(solution)/shard_map/ppermute | solution.py:350
  32.8 0.0 collective-permute-start.14
  32.8 0.8 %collective-permute-start.15 = (s16[72,512]{1,0:T(8,128)(2,1)S(1)}, s16[72,512]{1,0:T(8,128)(2,1)S(1)}, u32[]{:S(2)}, u32[]{:S(2)}) collective-permute-start(s16[72,512]{1,0:T(8,128)(2,1)S(1)} %sum_kernel.2.refs_0_), channel_id=1, source_target_pairs={{0,8},{4,12},{8,0},{12,4},{16,24},{20,28},{24,16},{28,20},{1,9},{5... | collective-permute-start | bytes 221192 | tf_op jit(solution)/shard_map/ppermute | solution.py:350
  33.6 0.0 collective-permute-done.12.got_ref
  33.6 0.2 bulk_pair_kernel.1
  33.8 1.3 %collective-permute-start.16 = (s16[1056,128]{1,0:T(8,128)(2,1)S(1)}, s16[1056,128]{1,0:T(8,128)(2,1)S(1)}, u32[]{:S(2)}, u32[]{:S(2)}) collective-permute-start(s16[1056,128]{1,0:T(8,128)(2,1)S(1)} %get-tuple-element.62), channel_id=1, source_target_pairs={{0,8},{4,12},{8,0},{12,4},{16,24},{20,28},{24,16},{28,20},{1,9},{5... | collective-permute-start | bytes 811016 | tf_op jit(solution)/shard_map/ppermute | solution.py:350
  35.1 1.2 %collective-permute-done.13.refs_1_ = s16[72,512]{1,0:T(8,128)(2,1)S(1)} collective-permute-done((s16[72,512]{1,0:T(8,128)(2,1)S(1)}, s16[72,512]{1,0:T(8,128)(2,1)S(1)}, u32[]{:S(2)}, u32[]{:S(2)}) %collective-permute-start.13) | collective-permute-done | bytes 73760 | tf_op jit(solution)/shard_map/ppermute | solution.py:350
  36.3 2.5 %collective-permute-done.14.refs_2_ = s16[72,512]{1,0:T(8,128)(2,1)S(1)} collective-permute-done((s16[72,512]{1,0:T(8,128)(2,1)S(1)}, s16[72,512]{1,0:T(8,128)(2,1)S(1)}, u32[]{:S(2)}, u32[]{:S(2)}) %collective-permute-start.14) | collective-permute-done | bytes 73760 | tf_op jit(solution)/shard_map/ppermute | solution.py:350
  38.8 0.8 %collective-permute-done.15.refs_3_ = s16[72,512]{1,0:T(8,128)(2,1)S(1)} collective-permute-done((s16[72,512]{1,0:T(8,128)(2,1)S(1)}, s16[72,512]{1,0:T(8,128)(2,1)S(1)}, u32[]{:S(2)}, u32[]{:S(2)}) %collective-permute-start.15) | collective-permute-done | bytes 73760 | tf_op jit(solution)/shard_map/ppermute | solution.py:350
  39.6 0.1 sum_kernel.3.refs_0_
  39.7 1.0 %collective-permute-start.17 = (s16[72,512]{1,0:T(8,128)(2,1)S(1)}, s16[72,512]{1,0:T(8,128)(2,1)S(1)}, u32[]{:S(2)}, u32[]{:S(2)}) collective-permute-start(s16[72,512]{1,0:T(8,128)(2,1)S(1)} %sum_kernel.3.refs_0_), channel_id=1, source_target_pairs={{0,3},{1,2},{2,1},{3,0},{4,7},{5,6},{6,5},{7,4},{8,11},{9,10},{10,... | collective-permute-start | bytes 221192 | tf_op jit(solution)/shard_map/ppermute | solution.py:350
  40.7 1.1 %collective-permute-start.18 = (s16[72,512]{1,0:T(8,128)(2,1)S(1)}, s16[72,512]{1,0:T(8,128)(2,1)S(1)}, u32[]{:S(2)}, u32[]{:S(2)}) collective-permute-start(s16[72,512]{1,0:T(8,128)(2,1)S(1)} %sum_kernel.3.refs_0_), channel_id=1, source_target_pairs={{0,2},{1,3},{2,0},{3,1},{4,6},{5,7},{6,4},{7,5},{8,10},{9,11},{10,... | collective-permute-start | bytes 221192 | tf_op jit(solution)/shard_map/ppermute | solution.py:350
  41.8 1.5 %collective-permute-start.19 = (s16[72,512]{1,0:T(8,128)(2,1)S(1)}, s16[72,512]{1,0:T(8,128)(2,1)S(1)}, u32[]{:S(2)}, u32[]{:S(2)}) collective-permute-start(s16[72,512]{1,0:T(8,128)(2,1)S(1)} %sum_kernel.3.refs_0_), channel_id=1, source_target_pairs={{0,1},{1,0},{2,3},{3,2},{4,5},{5,4},{6,7},{7,6},{8,9},{9,8},{10,11... | collective-permute-start | bytes 221192 | tf_op jit(solution)/shard_map/ppermute | solution.py:350
  43.3 1.1 %collective-permute-done.16.got_ref = s16[1056,128]{1,0:T(8,128)(2,1)S(1)} collective-permute-done((s16[1056,128]{1,0:T(8,128)(2,1)S(1)}, s16[1056,128]{1,0:T(8,128)(2,1)S(1)}, u32[]{:S(2)}, u32[]{:S(2)}) %collective-permute-start.16) | collective-permute-done | bytes 270368 | tf_op jit(solution)/shard_map/ppermute | solution.py:350
  44.4 0.2 bulk_sum_kernel.1
  44.5 0.6 %collective-permute-done.17.refs_1_ = s16[72,512]{1,0:T(8,128)(2,1)S(1)} collective-permute-done((s16[72,512]{1,0:T(8,128)(2,1)S(1)}, s16[72,512]{1,0:T(8,128)(2,1)S(1)}, u32[]{:S(2)}, u32[]{:S(2)}) %collective-permute-start.17) | collective-permute-done | bytes 73760 | tf_op jit(solution)/shard_map/ppermute | solution.py:350
  45.1 0.7 %collective-permute-done.18.refs_2_ = s16[72,512]{1,0:T(8,128)(2,1)S(1)} collective-permute-done((s16[72,512]{1,0:T(8,128)(2,1)S(1)}, s16[72,512]{1,0:T(8,128)(2,1)S(1)}, u32[]{:S(2)}, u32[]{:S(2)}) %collective-permute-start.18) | collective-permute-done | bytes 73760 | tf_op jit(solution)/shard_map/ppermute | solution.py:350
  45.9 0.3 collective-permute-done.19.refs_3_
  46.2 0.1 collective-permute-start.20
  46.3 1.4 %collective-permute-start.21 = (s16[528,128]{1,0:T(8,128)(2,1)S(1)}, s16[528,128]{1,0:T(8,128)(2,1)S(1)}, u32[]{:S(2)}, u32[]{:S(2)}) collective-permute-start(s16[528,128]{1,0:T(8,128)(2,1)S(1)} %get-tuple-element.65), channel_id=1, source_target_pairs={{0,16},{4,20},{8,24},{12,28},{16,0},{20,4},{24,8},{28,12},{1,17},{... | collective-permute-start | bytes 405512 | tf_op jit(solution)/shard_map/ppermute | solution.py:350
  47.7 0.2 own_kernel.1.half_ref
  47.9 0.0 collective-permute-done.20.other_ref
  47.9 7.0 %newton_kernel.1 = (f32[256,256]{1,0:T(8,128)S(1)}, f32[256,512]{1,0:T(8,128)S(1)}) custom-call(f32[256,512]{1,0:T(8,128)S(1)} %own_kernel.1.half_ref, s16[320,512]{1,0:T(8,128)(2,1)S(1)} %collective-permute-done.20.other_ref), custom_call_target="tpu_custom_call" | custom-call | bytes 1024 | tf_op jit(solution)/shard_map/newton_kernel/pallas_call | solution.py:335
  54.9 1.2 %collective-permute-done.21.refs_0_ = s16[528,128]{1,0:T(8,128)(2,1)S(1)} collective-permute-done((s16[528,128]{1,0:T(8,128)(2,1)S(1)}, s16[528,128]{1,0:T(8,128)(2,1)S(1)}, u32[]{:S(2)}, u32[]{:S(2)}) %collective-permute-start.21) | collective-permute-done | bytes 135200 | tf_op jit(solution)/shard_map/ppermute | solution.py:350
  56.1 1.3 %factor_kernel.1 = (f32[128,1,256]{2,1,0:T(1,128)}, f32[128,1,256]{2,1,0:T(1,128)}) custom-call(f32[256,256]{1,0:T(8,128)S(1)} %get-tuple-element.67.inverse_first_ref, f32[256,512]{1,0:T(8,128)S(1)} %get-tuple-element.68.inverse_second_ref, f32[512,128]{1,0:T(8,128)S(1)} %get-tuple-element.69.rows_ref, s16[528,128]{1,0:T(8,128)(2,1)S(1)} %collective-permute-done.21.refs_0_), custom_call_target="tpu_custom_call" | custom-call | bytes 1024 | tf_op jit(solution)/shard_map/factor_kernel/pallas_call | solution.py:335
  (2 shorter events, 0.1 us)
Async XLA Ops:
  1.8 8.8 %collective-permute-start.2 = (bf16[256,384]{1,0:T(8,128)(2,1)S(1)}, bf16[256,384]{1,0:T(8,128)(2,1)S(1)}, u32[]{:S(2)}, u32[]{:S(2)}) collective-permute-start(bf16[256,384]{1,0:T(8,128)(2,1)S(1)} %get-tuple-element.39.refs_0_), channel_id=1, source_target_pairs={{0,2},{1,3},{2,0},{3,1},{4,6},{5,7},{6,4},{7,5},{8,10},{9,11},{10,... | collective-permute-start | bytes 589832 | tf_op jit(solution)/shard_map/ppermute | solution.py:350
  4.8 7.8 %collective-permute-start.1 = (bf16[256,384]{1,0:T(8,128)(2,1)S(1)}, bf16[256,384]{1,0:T(8,128)(2,1)S(1)}, u32[]{:S(2)}, u32[]{:S(2)}) collective-permute-start(bf16[256,384]{1,0:T(8,128)(2,1)S(1)} %get-tuple-element.40.refs_1_), channel_id=1, source_target_pairs={{0,1},{1,0},{2,3},{3,2},{4,5},{5,4},{6,7},{7,6},{8,9},{9,8},{10,11... | collective-permute-start | bytes 589832 | tf_op jit(solution)/shard_map/ppermute | solution.py:350
  6.3 10.7 %collective-permute-start = (bf16[256,384]{1,0:T(8,128)(2,1)S(1)}, bf16[256,384]{1,0:T(8,128)(2,1)S(1)}, u32[]{:S(2)}, u32[]{:S(2)}) collective-permute-start(bf16[256,384]{1,0:T(8,128)(2,1)S(1)} %get-tuple-element.39.refs_0_), channel_id=1, source_target_pairs={{0,1},{1,0},{2,3},{3,2},{4,5},{5,4},{6,7},{7,6},{8,9},{9,8},{10,11... | collective-permute-start | bytes 589832 | tf_op jit(solution)/shard_map/ppermute | solution.py:350
  6.9 10.2 %collective-permute-start.3 = (bf16[256,384]{1,0:T(8,128)(2,1)S(1)}, bf16[256,384]{1,0:T(8,128)(2,1)S(1)}, u32[]{:S(2)}, u32[]{:S(2)}) collective-permute-start(bf16[256,384]{1,0:T(8,128)(2,1)S(1)} %get-tuple-element.40.refs_1_), channel_id=1, source_target_pairs={{0,2},{1,3},{2,0},{3,1},{4,6},{5,7},{6,4},{7,5},{8,10},{9,11},{10,... | collective-permute-start | bytes 589832 | tf_op jit(solution)/shard_map/ppermute | solution.py:350
  10.6 9.1 %collective-permute-start.5 = (bf16[256,384]{1,0:T(8,128)(2,1)S(1)}, bf16[256,384]{1,0:T(8,128)(2,1)S(1)}, u32[]{:S(2)}, u32[]{:S(2)}) collective-permute-start(bf16[256,384]{1,0:T(8,128)(2,1)S(1)} %collective-permute-done.2.refs_4_), channel_id=1, source_target_pairs={{0,1},{1,0},{2,3},{3,2},{4,5},{5,4},{6,7},{7,6},{8,9},{9,8},{10,11... | collective-permute-start | bytes 589832 | tf_op jit(solution)/shard_map/ppermute | solution.py:350
  12.7 7.0 %collective-permute-start.6 = (bf16[256,384]{1,0:T(8,128)(2,1)S(1)}, bf16[256,384]{1,0:T(8,128)(2,1)S(1)}, u32[]{:S(2)}, u32[]{:S(2)}) collective-permute-start(bf16[256,384]{1,0:T(8,128)(2,1)S(1)} %collective-permute-done.1.refs_3_), channel_id=1, source_target_pairs={{0,2},{1,3},{2,0},{3,1},{4,6},{5,7},{6,4},{7,5},{8,10},{9,11},{10,... | collective-permute-start | bytes 589832 | tf_op jit(solution)/shard_map/ppermute | solution.py:350
  18.2 2.0 %collective-permute-start.4 = (f32[264,512]{1,0:T(8,128)S(1)}, f32[264,512]{1,0:T(8,128)S(1)}, u32[]{:S(2)}, u32[]{:S(2)}) collective-permute-start(f32[264,512]{1,0:T(8,128)S(1)} %get-tuple-element.43), channel_id=1, source_target_pairs={{0,4},{4,0},{8,12},{12,8},{16,20},{20,16},{24,28},{28,24},{1,5},{5... | collective-permute-start | bytes 1622024 | tf_op jit(solution)/shard_map/ppermute | solution.py:350
  18.3 2.9 %collective-permute-start.8 = (bf16[384,512]{1,0:T(8,128)(2,1)S(1)}, bf16[384,512]{1,0:T(8,128)(2,1)S(1)}, u32[]{:S(2)}, u32[]{:S(2)}) collective-permute-start(bf16[384,512]{1,0:T(8,128)(2,1)S(1)} %get-tuple-element.49.refs_2_), channel_id=1, source_target_pairs={{0,4},{4,0},{8,12},{12,8},{16,20},{20,16},{24,28},{28,24},{1,5},{5... | collective-permute-start | bytes 1179656 | tf_op jit(solution)/shard_map/ppermute | solution.py:350
  19.7 1.5 %collective-permute-start.7 = (bf16[256,384]{1,0:T(8,128)(2,1)S(1)}, bf16[256,384]{1,0:T(8,128)(2,1)S(1)}, u32[]{:S(2)}, u32[]{:S(2)}) collective-permute-start(bf16[256,384]{1,0:T(8,128)(2,1)S(1)} %select_kernel.1), channel_id=1, source_target_pairs={{0,4},{4,0},{8,12},{12,8},{16,20},{20,16},{24,28},{28,24},{1,5},{5... | collective-permute-start | bytes 589832 | tf_op jit(solution)/shard_map/ppermute | solution.py:350
  20.2 5.0 %copy-start = (bf16[1,1536,1024]{2,1,0:T(8,128)(2,1)S(1)}, bf16[1,1536,1024]{2,1,0:T(8,128)(2,1)}, u32[]{:S(2)}) copy-start(bf16[1,1536,1024]{2,1,0:T(8,128)(2,1)} %param.4) | copy-start | bytes 9437188
  21.6 5.6 %collective-permute-start.10 = (s16[72,512]{1,0:T(8,128)(2,1)S(1)}, s16[72,512]{1,0:T(8,128)(2,1)S(1)}, u32[]{:S(2)}, u32[]{:S(2)}) collective-permute-start(s16[72,512]{1,0:T(8,128)(2,1)S(1)} %get-tuple-element.58), channel_id=1, source_target_pairs={{0,3},{1,2},{2,1},{3,0},{4,7},{5,6},{6,5},{7,4},{8,11},{9,10},{10,... | collective-permute-start | bytes 221192 | tf_op jit(solution)/shard_map/ppermute | solution.py:350
  23.1 5.4 %collective-permute-start.11 = (s16[72,512]{1,0:T(8,128)(2,1)S(1)}, s16[72,512]{1,0:T(8,128)(2,1)S(1)}, u32[]{:S(2)}, u32[]{:S(2)}) collective-permute-start(s16[72,512]{1,0:T(8,128)(2,1)S(1)} %get-tuple-element.59), channel_id=1, source_target_pairs={{0,2},{1,3},{2,0},{3,1},{4,6},{5,7},{6,4},{7,5},{8,10},{9,11},{10,... | collective-permute-start | bytes 221192 | tf_op jit(solution)/shard_map/ppermute | solution.py:350
  24.6 4.4 %collective-permute-start.9 = (s16[72,512]{1,0:T(8,128)(2,1)S(1)}, s16[72,512]{1,0:T(8,128)(2,1)S(1)}, u32[]{:S(2)}, u32[]{:S(2)}) collective-permute-start(s16[72,512]{1,0:T(8,128)(2,1)S(1)} %get-tuple-element.57), channel_id=1, source_target_pairs={{0,1},{1,0},{2,3},{3,2},{4,5},{5,4},{6,7},{7,6},{8,9},{9,8},{10,11... | collective-permute-start | bytes 221192 | tf_op jit(solution)/shard_map/ppermute | solution.py:350
  27.0 6.6 %collective-permute-start.12 = (f32[2048,128]{1,0:T(8,128)S(1)}, f32[2048,128]{1,0:T(8,128)S(1)}, u32[]{:S(2)}, u32[]{:S(2)}) collective-permute-start(f32[2048,128]{1,0:T(8,128)S(1)} %get-tuple-element.61), channel_id=1, source_target_pairs={{0,4},{4,0},{8,12},{12,8},{16,20},{20,16},{24,28},{28,24},{1,5},{5... | collective-permute-start | bytes 3145736 | tf_op jit(solution)/shard_map/ppermute | solution.py:350
  29.1 7.2 %collective-permute-start.13 = (s16[72,512]{1,0:T(8,128)(2,1)S(1)}, s16[72,512]{1,0:T(8,128)(2,1)S(1)}, u32[]{:S(2)}, u32[]{:S(2)}) collective-permute-start(s16[72,512]{1,0:T(8,128)(2,1)S(1)} %sum_kernel.2.refs_0_), channel_id=1, source_target_pairs={{0,24},{4,28},{8,16},{12,20},{16,8},{20,12},{24,0},{28,4},{1,25},{... | collective-permute-start | bytes 221192 | tf_op jit(solution)/shard_map/ppermute | solution.py:350
  32.8 5.9 %collective-permute-start.14 = (s16[72,512]{1,0:T(8,128)(2,1)S(1)}, s16[72,512]{1,0:T(8,128)(2,1)S(1)}, u32[]{:S(2)}, u32[]{:S(2)}) collective-permute-start(s16[72,512]{1,0:T(8,128)(2,1)S(1)} %sum_kernel.2.refs_0_), channel_id=1, source_target_pairs={{0,16},{4,20},{8,24},{12,28},{16,0},{20,4},{24,8},{28,12},{1,17},{... | collective-permute-start | bytes 221192 | tf_op jit(solution)/shard_map/ppermute | solution.py:350
  32.8 6.8 %collective-permute-start.15 = (s16[72,512]{1,0:T(8,128)(2,1)S(1)}, s16[72,512]{1,0:T(8,128)(2,1)S(1)}, u32[]{:S(2)}, u32[]{:S(2)}) collective-permute-start(s16[72,512]{1,0:T(8,128)(2,1)S(1)} %sum_kernel.2.refs_0_), channel_id=1, source_target_pairs={{0,8},{4,12},{8,0},{12,4},{16,24},{20,28},{24,16},{28,20},{1,9},{5... | collective-permute-start | bytes 221192 | tf_op jit(solution)/shard_map/ppermute | solution.py:350
  33.8 10.6 %collective-permute-start.16 = (s16[1056,128]{1,0:T(8,128)(2,1)S(1)}, s16[1056,128]{1,0:T(8,128)(2,1)S(1)}, u32[]{:S(2)}, u32[]{:S(2)}) collective-permute-start(s16[1056,128]{1,0:T(8,128)(2,1)S(1)} %get-tuple-element.62), channel_id=1, source_target_pairs={{0,8},{4,12},{8,0},{12,4},{16,24},{20,28},{24,16},{28,20},{1,9},{5... | collective-permute-start | bytes 811016 | tf_op jit(solution)/shard_map/ppermute | solution.py:350
  39.7 5.4 %collective-permute-start.17 = (s16[72,512]{1,0:T(8,128)(2,1)S(1)}, s16[72,512]{1,0:T(8,128)(2,1)S(1)}, u32[]{:S(2)}, u32[]{:S(2)}) collective-permute-start(s16[72,512]{1,0:T(8,128)(2,1)S(1)} %sum_kernel.3.refs_0_), channel_id=1, source_target_pairs={{0,3},{1,2},{2,1},{3,0},{4,7},{5,6},{6,5},{7,4},{8,11},{9,10},{10,... | collective-permute-start | bytes 221192 | tf_op jit(solution)/shard_map/ppermute | solution.py:350
  40.7 5.1 %collective-permute-start.18 = (s16[72,512]{1,0:T(8,128)(2,1)S(1)}, s16[72,512]{1,0:T(8,128)(2,1)S(1)}, u32[]{:S(2)}, u32[]{:S(2)}) collective-permute-start(s16[72,512]{1,0:T(8,128)(2,1)S(1)} %sum_kernel.3.refs_0_), channel_id=1, source_target_pairs={{0,2},{1,3},{2,0},{3,1},{4,6},{5,7},{6,4},{7,5},{8,10},{9,11},{10,... | collective-permute-start | bytes 221192 | tf_op jit(solution)/shard_map/ppermute | solution.py:350
  41.8 4.4 %collective-permute-start.19 = (s16[72,512]{1,0:T(8,128)(2,1)S(1)}, s16[72,512]{1,0:T(8,128)(2,1)S(1)}, u32[]{:S(2)}, u32[]{:S(2)}) collective-permute-start(s16[72,512]{1,0:T(8,128)(2,1)S(1)} %sum_kernel.3.refs_0_), channel_id=1, source_target_pairs={{0,1},{1,0},{2,3},{3,2},{4,5},{5,4},{6,7},{7,6},{8,9},{9,8},{10,11... | collective-permute-start | bytes 221192 | tf_op jit(solution)/shard_map/ppermute | solution.py:350
  46.2 1.7 %collective-permute-start.20 = (s16[320,512]{1,0:T(8,128)(2,1)S(1)}, s16[320,512]{1,0:T(8,128)(2,1)S(1)}, u32[]{:S(2)}, u32[]{:S(2)}) collective-permute-start(s16[320,512]{1,0:T(8,128)(2,1)S(1)} %join_kernel.1.own_ref), channel_id=1, source_target_pairs={{0,4},{4,0},{8,12},{12,8},{16,20},{20,16},{24,28},{28,24},{1,5},{5... | collective-permute-start | bytes 983048 | tf_op jit(solution)/shard_map/ppermute | solution.py:350
  46.3 9.8 %collective-permute-start.21 = (s16[528,128]{1,0:T(8,128)(2,1)S(1)}, s16[528,128]{1,0:T(8,128)(2,1)S(1)}, u32[]{:S(2)}, u32[]{:S(2)}) collective-permute-start(s16[528,128]{1,0:T(8,128)(2,1)S(1)} %get-tuple-element.65), channel_id=1, source_target_pairs={{0,16},{4,20},{8,24},{12,28},{16,0},{20,4},{24,8},{28,12},{1,17},{... | collective-permute-start | bytes 405512 | tf_op jit(solution)/shard_map/ppermute | solution.py:350
